TPU v7x, 32 devices: a whole 2x2x4 slice. The times are simulated.
32 devices in a mesh: dp: 8 (over z, x), shard: 4 (over y, core).
Axes of the slice: x: 2, y: 2, z: 4, core: 2. Of those that a mesh axis runs over, the one named last changes fastest.
Arguments:
- tokens: bfloat16 [16384, 256], P(('dp', 'shard')), may hold values from -6 to 6
- cotangent: bfloat16 [16384, 256], P(('dp', 'shard')), may hold values from -6 to 6
- lengths: int32 [128], replicated, may hold values from 0 to 512, as said below
- seq_owner: int32 [128], replicated, may hold values from 0 to 31, as said below
- qkv_weight: float32 [256, 768], P('shard'), may hold values from -0.375 to 0.375
- out_weight: float32 [256, 256], P('shard'), may hold values from -2 to 2
- up_weight: float32 [256, 1024], P('shard'), may hold values from -0.375 to 0.375
- down_weight: float32 [1024, 256], P('shard'), may hold values from -0.1875 to 0.1875
- gains_biases: float32 [3072], P('shard'), may hold values from -0.35 to 1.7
- qkv_first: float32 [256, 768], P('shard'), may hold values from -16 to 16
- qkv_second: float32 [256, 768], P('shard'), may hold values from 19.16928 to 309.6576
- out_first: float32 [256, 256], P('shard'), may hold values from -6 to 6
- out_second: float32 [256, 256], P('shard'), may hold values from 1.664 to 26.88
- up_first: float32 [256, 1024], P('shard'), may hold values from -32 to 32
- up_second: float32 [256, 1024], P('shard'), may hold values from 53.248 to 860.16
- down_first: float32 [1024, 256], P('shard'), may hold values from -32 to 32
- down_second: float32 [1024, 256], P('shard'), may hold values from 53.248 to 860.16
- small_first: float32 [3072], P('shard'), may hold values from -64 to 64
- small_second: float32 [3072], P('shard'), may hold values from 212.992 to 3440.64
Outputs:
- output: bfloat16 [16384, 256], P(('dp', 'shard'))
- input_grad: float32 [16384, 256], P(('dp', 'shard'))
- qkv_first_next: float32 [256, 768], P('shard')
- qkv_second_next: float32 [256, 768], P('shard')
- qkv_weight_next: float32 [256, 768], P('shard')
- out_first_next: float32 [256, 256], P('shard')
- out_second_next: float32 [256, 256], P('shard')
- out_weight_next: float32 [256, 256], P('shard')
- up_first_next: float32 [256, 1024], P('shard')
- up_second_next: float32 [256, 1024], P('shard')
- up_weight_next: float32 [256, 1024], P('shard')
- down_first_next: float32 [1024, 256], P('shard')
- down_second_next: float32 [1024, 256], P('shard')
- down_weight_next: float32 [1024, 256], P('shard')
- small_first_next: float32 [3072], P('shard')
- small_second_next: float32 [3072], P('shard')
- gains_biases_next: float32 [3072], P('shard')
Inputs may be any that keep to these rules, and one draw needn't show every extreme that they name: The sequences that one device owns have lengths adding up to 512 or less. In every draw one device owns a single sequence of 512 tokens and its other sequences have length 0. A length of 0 is an empty sequence. `seq_owner`: each device owns exactly 4 sequences.
All inputs are finite; a program needn't handle non-finite values.
Results may differ from a plain program's by a relative error of at most 0.012.
The roundings to bfloat16 on the way count: a program that leaves them out, or rounds other values in their place, can miss the bound.
Values may be sent and summed in bfloat16 or wider, within the bound.
No kernel may reach another device: no remote copies, remote signals or barrier semaphores. Data moves between devices by JAX's collectives and lax.ppermute only.
A program may use at most 64 MiB of HBM per device.

v0:
```python
import math

import jax
import jax.numpy as jnp
from jax import lax
from jax.sharding import PartitionSpec as P

HEAD = 32
STEP = 10


norm_eps = 1e-05
beta_one = 0.9
beta_two = 0.95
learn_rate = 0.1
adam_eps = 1e-08
matrix_decay = 0.1
masked_score = -1e30


def standardize(values):
    centered = values - jnp.mean(values, axis=-1, keepdims=True)
    root_inv = lax.rsqrt(jnp.mean(centered * centered, axis=-1, keepdims=True) + norm_eps)
    return (centered * root_inv, root_inv)


def norm_back(upstream, normed, root_inv, gain):
    scaled = upstream * gain
    inner_mean = jnp.mean(scaled, axis=-1, keepdims=True)
    cross_mean = jnp.mean(scaled * normed, axis=-1, keepdims=True)
    through = root_inv * (scaled - inner_mean - normed * cross_mean)
    return (through, jnp.sum(upstream * normed, axis=0), jnp.sum(upstream, axis=0))


def contract_rows(left, right):
    return lax.dot_general(
        left, right, (((0,), (0,)), ((), ())), preferred_element_type=jnp.float32
    )


def contract_cols(left, right):
    return lax.dot_general(
        left, right, (((1,), (1,)), ((), ())), preferred_element_type=jnp.float32
    )


def unpack_small(small, width):
    pieces = [small[part_index * width : (part_index + 1) * width] for part_index in range(8)]
    return pieces + [small[8 * width :]]


def gelu_tanh(values):
    return jax.nn.gelu(values, approximate=True)


def adam_step(weight, grad, first, second, decay_rate):
    first_next = beta_one * first + (1.0 - beta_one) * grad
    second_next = beta_two * second + (1.0 - beta_two) * grad * grad
    first_fix = 1.0 - beta_one**STEP
    second_fix = 1.0 - beta_two**STEP
    update = first_next / first_fix / (jnp.sqrt(second_next / second_fix) + adam_eps)
    return (first_next, second_next, weight - learn_rate * (update + decay_rate * weight))


def shards(
    tokens,
    cotangent,
    lengths,
    seq_owner,
    qkv_weight,
    out_weight,
    up_weight,
    down_weight,
    gains_biases,
    qkv_first,
    qkv_second,
    out_first,
    out_second,
    up_first,
    up_second,
    down_first,
    down_second,
    small_first,
    small_second,
):
    row_count, model_width = tokens.shape
    head_count = model_width // HEAD
    score_scale = 1.0 / math.sqrt(HEAD)
    block_rows = min(512, row_count)
    device = lax.axis_index(("dp", "shard"))
    own_lengths = jnp.where(seq_owner == device, lengths, 0)
    seq_ends = jnp.cumsum(own_lengths)
    position = jnp.arange(row_count, dtype=jnp.int32)
    segment = jnp.sum((seq_ends[None, :] <= position[:, None]).astype(jnp.int32), axis=1)
    live_rows = (position < seq_ends[-1]).astype(jnp.float32)
    weight_pieces = (
        qkv_weight.astype(jnp.bfloat16),
        out_weight.astype(jnp.bfloat16),
        up_weight.astype(jnp.bfloat16),
        down_weight.astype(jnp.bfloat16),
        gains_biases.astype(jnp.bfloat16),
    )
    gathered = (
        lax.all_gather(weight_pieces[0], "shard", axis=0, tiled=True),
        lax.all_gather(weight_pieces[1], "shard", axis=0, tiled=True),
        lax.all_gather(weight_pieces[2], "shard", axis=0, tiled=True),
        lax.all_gather(weight_pieces[3], "shard", axis=0, tiled=True),
        lax.all_gather(weight_pieces[4], "shard", axis=0, tiled=True),
    )
    qkv_full, out_full, up_full, down_full, small_full = gathered
    small_parts = unpack_small(small_full.astype(jnp.float32), model_width)
    gain_one, bias_one, gain_two, bias_two, bias_query, bias_value, bias_out, bias_down, bias_up = (
        small_parts
    )
    inputs = tokens.astype(jnp.float32)
    normed_one, root_one = standardize(inputs)
    hidden_one = (normed_one * gain_one + bias_one).astype(jnp.bfloat16)
    joined_bias = jnp.concatenate([bias_query, jnp.zeros_like(bias_query), bias_value])
    joined = (
        jnp.dot(hidden_one, qkv_full, preferred_element_type=jnp.float32) + joined_bias
    ).astype(jnp.bfloat16)
    queries = joined[:, :model_width].reshape(row_count, head_count, HEAD)
    key_rows = joined[:, model_width : 2 * model_width].reshape(row_count, head_count, HEAD)
    value_rows = joined[:, 2 * model_width :].reshape(row_count, head_count, HEAD)

    def block_scores(offset):
        limit = offset + block_rows
        raw_scores = (
            jnp.einsum("qhd,khd->hqk", queries, key_rows, preferred_element_type=jnp.float32)
            * score_scale
        )
        allowed = (segment[offset:limit, None] == segment[None, :limit]) & (
            position[None, :limit] <= position[offset:limit, None]
        )
        return (queries, jnp.where(allowed[None], raw_scores, masked_score))

    offset = 0
    limit = offset + block_rows
    query_block, scores = block_scores(offset)
    row_max = jnp.max(scores, axis=-1, keepdims=True)
    exponent = jnp.exp(scores - row_max)
    total = jnp.sum(exponent, axis=-1, keepdims=True)
    probs_low = (exponent / total).astype(jnp.bfloat16)
    attended_blocks = jnp.einsum(
        "hqk,khd->qhd", probs_low, value_rows, preferred_element_type=jnp.float32
    )
    log_sums = [row_max + jnp.log(total)]
    attended = attended_blocks.reshape(row_count, model_width).astype(jnp.bfloat16)
    middle = inputs + (jnp.dot(attended, out_full, preferred_element_type=jnp.float32) + bias_out)
    normed_two, root_two = standardize(middle)
    hidden_two = (normed_two * gain_two + bias_two).astype(jnp.bfloat16)
    pre_act = jnp.dot(hidden_two, up_full, preferred_element_type=jnp.float32) + bias_up
    activated_full, gelu_pull = jax.vjp(gelu_tanh, pre_act)
    activated = activated_full.astype(jnp.bfloat16)
    output = (
        middle + (jnp.dot(activated, down_full, preferred_element_type=jnp.float32) + bias_down)
    ).astype(jnp.bfloat16)
    qkv_back, out_back, up_back, down_back, small_back = (
        lax.all_gather(weight_pieces[0], "shard", axis=0, tiled=True),
        lax.all_gather(weight_pieces[1], "shard", axis=0, tiled=True),
        lax.all_gather(weight_pieces[2], "shard", axis=0, tiled=True),
        lax.all_gather(weight_pieces[3], "shard", axis=0, tiled=True),
        lax.all_gather(weight_pieces[4], "shard", axis=0, tiled=True),
    )
    back_parts = unpack_small(small_back.astype(jnp.float32), model_width)
    gain_one_back = back_parts[0]
    gain_two_back = back_parts[2]
    seed_grad = cotangent.astype(jnp.float32) * live_rows[:, None]
    down_in = seed_grad.astype(jnp.bfloat16)
    grad_down = contract_rows(activated, down_in)
    bias_down_grad = jnp.sum(down_in.astype(jnp.float32), axis=0)
    act_grad = contract_cols(down_in, down_back)
    up_in = gelu_pull(act_grad)[0].astype(jnp.bfloat16)
    grad_up = contract_rows(hidden_two, up_in)
    bias_up_grad = jnp.sum(up_in.astype(jnp.float32), axis=0)
    hidden_two_grad = contract_cols(up_in, up_back)
    through_two, gain_two_grad, bias_two_grad = norm_back(
        hidden_two_grad, normed_two, root_two, gain_two_back
    )
    middle_grad = seed_grad + through_two
    out_in = middle_grad.astype(jnp.bfloat16)
    grad_out = contract_rows(attended, out_in)
    bias_out_grad = jnp.sum(out_in.astype(jnp.float32), axis=0)
    attended_grad = (
        contract_cols(out_in, out_back).astype(jnp.bfloat16).reshape(row_count, head_count, HEAD)
    )
    key_grad = jnp.zeros((row_count, head_count, HEAD), jnp.float32)
    value_grad = jnp.zeros((row_count, head_count, HEAD), jnp.float32)
    query_grads = []
    for block_index, offset in enumerate(range(0, row_count, block_rows)):
        limit = offset + block_rows
        query_block, scores = block_scores(offset)
        probs = jnp.exp(scores - log_sums[block_index])
        probs_low = probs.astype(jnp.bfloat16)
        value_grad = value_grad.at[:limit].add(
            jnp.einsum("hqk,qhd->khd", probs_low, attended_grad, preferred_element_type=jnp.float32)
        )
        prob_grad = jnp.einsum(
            "qhd,khd->hqk", attended_grad, value_rows, preferred_element_type=jnp.float32
        )
        weighted = jnp.sum(probs * prob_grad, axis=-1, keepdims=True)
        score_grad = (probs * (prob_grad - weighted)).astype(jnp.bfloat16)
        query_grads.append(
            jnp.einsum("hqk,khd->qhd", score_grad, key_rows, preferred_element_type=jnp.float32)
            * score_scale
        )
        key_grad = key_grad.at[:limit].add(
            jnp.einsum("hqk,qhd->khd", score_grad, query_block, preferred_element_type=jnp.float32)
            * score_scale
        )
    query_grad = query_grads[0].reshape(row_count, model_width)
    joined_grad = jnp.concatenate(
        [
            query_grad,
            key_grad.reshape(row_count, model_width),
            value_grad.reshape(row_count, model_width),
        ],
        axis=1,
    ).astype(jnp.bfloat16)
    grad_qkv = contract_rows(hidden_one, joined_grad)
    joined_sum = jnp.sum(joined_grad.astype(jnp.float32), axis=0)
    bias_query_grad = joined_sum[:model_width]
    bias_value_grad = joined_sum[2 * model_width :]
    hidden_one_grad = contract_cols(joined_grad, qkv_back)
    through_one, gain_one_grad, bias_one_grad = norm_back(
        hidden_one_grad, normed_one, root_one, gain_one_back
    )
    input_grad = middle_grad + through_one
    small_grad = jnp.concatenate(
        [
            gain_one_grad,
            bias_one_grad,
            gain_two_grad,
            bias_two_grad,
            bias_query_grad,
            bias_value_grad,
            bias_out_grad,
            bias_down_grad,
            bias_up_grad,
        ]
    )
    local_sums = (
        lax.psum_scatter(grad_qkv, "shard", scatter_dimension=0, tiled=True),
        lax.psum_scatter(grad_out, "shard", scatter_dimension=0, tiled=True),
        lax.psum_scatter(grad_up, "shard", scatter_dimension=0, tiled=True),
        lax.psum_scatter(grad_down, "shard", scatter_dimension=0, tiled=True),
        lax.psum_scatter(small_grad, "shard", scatter_dimension=0, tiled=True),
    )
    owned = lax.psum(
        (local_sums[0], local_sums[1], local_sums[2], local_sums[3], local_sums[4]), "dp"
    )
    qkv_new = adam_step(qkv_weight, owned[0], qkv_first, qkv_second, matrix_decay)
    out_new = adam_step(out_weight, owned[1], out_first, out_second, matrix_decay)
    up_new = adam_step(up_weight, owned[2], up_first, up_second, matrix_decay)
    down_new = adam_step(down_weight, owned[3], down_first, down_second, matrix_decay)
    small_new = adam_step(gains_biases, owned[4], small_first, small_second, 0.0)
    return (
        output,
        input_grad,
        qkv_new[0],
        qkv_new[1],
        qkv_new[2],
        out_new[0],
        out_new[1],
        out_new[2],
        up_new[0],
        up_new[1],
        up_new[2],
        down_new[0],
        down_new[1],
        down_new[2],
        small_new[0],
        small_new[1],
        small_new[2],
    )


def solution(mesh):
    return jax.shard_map(
        shards,
        mesh=mesh,
        in_specs=(
            P(("dp", "shard"), None),
            P(("dp", "shard"), None),
            P(),
            P(),
            P("shard", None),
            P("shard", None),
            P("shard", None),
            P("shard", None),
            P("shard"),
            P("shard", None),
            P("shard", None),
            P("shard", None),
            P("shard", None),
            P("shard", None),
            P("shard", None),
            P("shard", None),
            P("shard", None),
            P("shard"),
            P("shard"),
        ),
        out_specs=(
            P(("dp", "shard"), None),
            P(("dp", "shard"), None),
            P("shard", None),
            P("shard", None),
            P("shard", None),
            P("shard", None),
            P("shard", None),
            P("shard", None),
            P("shard", None),
            P("shard", None),
            P("shard", None),
            P("shard", None),
            P("shard", None),
            P("shard", None),
            P("shard"),
            P("shard"),
            P("shard"),
        ),
        check_vma=False,
    )
```

profile of v0, /device:TPU:0, one launch (start us, length us, event | category | flops | bytes accessed | tf_op | source)
XLA Modules:
  0.0 264.6 jit_solution(10267367462271482335)
XLA Ops:
  8.0 6.2 %all-gather = bf16[4,1,768]{2,1,0:T(2,128)(2,1)S(1)} all-gather(bf16[1,1,768]{2,1,0:T(2,128)(2,1)S(1)} %reshape.246), channel_id=1, replica_groups=mesh['dp'=8,'shard'=4] {'shard'}, dimensions={0}, use_global_device_ids=true | all-gather | bytes 7680 | tf_op jit(solution)/shard_map/all_gather | solution.py:108
  17.8 1.2 fusion.46
  19.2 5.6 %all_gather.22 = bf16[256,256]{1,0:T(8,128)(2,1)S(1)} all-gather(bf16[64,256]{1,0:T(8,128)(2,1)S(1)} %convert_element_type.104), channel_id=1, replica_groups=mesh['dp'=8,'shard'=4] {'shard'}, dimensions={0}, use_global_device_ids=true | all-gather | bytes 163840 | tf_op jit(solution)/shard_map/all_gather | solution.py:105
  24.8 0.9 convert_element_type.97
  25.7 1.0 convert_element_type.106
  26.7 1.0 convert_element_type.108
  28.4 6.7 %all_gather.21 = bf16[256,768]{1,0:T(8,128)(2,1)S(1)} all-gather(bf16[64,768]{1,0:T(8,128)(2,1)S(1)} %convert_element_type.97), channel_id=1, replica_groups=mesh['dp'=8,'shard'=4] {'shard'}, dimensions={0}, use_global_device_ids=true | all-gather | bytes 491520 | tf_op jit(solution)/shard_map/all_gather | solution.py:104
  35.1 7.7 %all_gather.24 = bf16[1024,256]{1,0:T(8,128)(2,1)} all-gather(bf16[256,256]{1,0:T(8,128)(2,1)S(1)} %convert_element_type.108), channel_id=1, replica_groups=mesh['dp'=8,'shard'=4] {'shard'}, dimensions={0}, use_global_device_ids=true | all-gather | bytes 655360 | tf_op jit(solution)/shard_map/all_gather | solution.py:107
  42.9 7.3 %all_gather.23 = bf16[256,1024]{1,0:T(8,128)(2,1)S(1)} all-gather(bf16[64,1024]{1,0:T(8,128)(2,1)S(1)} %convert_element_type.106), channel_id=1, replica_groups=mesh['dp'=8,'shard'=4] {'shard'}, dimensions={0}, use_global_device_ids=true | all-gather | bytes 655360 | tf_op jit(solution)/shard_map/all_gather | solution.py:106
  51.3 1.6 fusion.64
  52.9 1.2 fusion
  54.1 2.1 copy-done
  56.2 1.5 fusion.21
  59.4 2.4 convert_reduce_fusion
  61.8 1.8 fusion.67
  63.7 1.2 copy.98
  64.9 1.5 multiply_reduce_fusion.1
  66.4 1.9 convert_reduce_fusion.4
  68.3 1.9 fusion.48
  71.5 4.9 %fusion.16 = bf16[8,32,512]{2,1,0:T(8,128)(2,1)S(1)} fusion(bf16[512,8,32]{0,2,1:T(8,128)(2,1)S(1)} %bitcast.45, f32[8,512,512]{1,2,0:T(8,128)} %copy-done, f32[8,512]{1,0:T(8,128)S(1)} %log_add_fusion), kind=kOutput, calls=%fused_computation.31 | convolution fusion | flops 138543104 | bytes 8929280 | tf_op jit(solution)/shard_map/hqk,qhd->khd/dot_general | solution.py:196
  76.4 5.5 %multiply_reduce_fusion = (f32[8,512]{1,0:T(8,128)S(1)}, f32[8,512,512]{1,2,0:T(8,128)S(1)}) fusion(f32[8,512,512]{1,2,0:T(8,128)} %copy-done, f32[8,512]{1,0:T(8,128)S(1)} %log_add_fusion, bf16[512,8,32]{0,2,1:T(8,128)(2,1)S(1)} %bitcast.46, bf16[512,8,32]{0,2,1:T(8,128)(2,1)S(1)} %bitcast.52), kind=kOutput, calls=%fused_computation.1 | convolution fusion | flops 140505088 | bytes 17334272 | tf_op jit(solution)/shard_map/qhd,khd->hqk/dot_general | solution.py:198
  82.0 2.6 multiply_convert_fusion
  84.5 1.3 fusion.20
  86.7 1.3 fusion.51
  88.2 3.5 %fusion.40 = f32[1024,256]{1,0:T(8,128)} fusion(bf16[512,256]{0,1:T(8,128)(2,1)S(1)} %copy-done.7, f32[512]{0:T(512)S(1)} %copy-done.40, f32[512,1024]{1,0:T(8,128)} %copy-done.1, f32[1024]{0:T(1024)S(1)} %copy-done.47), kind=kOutput, calls=%fused_computation.78 | convolution fusion | flops 274071552 | bytes 3414016 | tf_op jit(solution)/shard_map/dot_general | solution.py:36
  91.8 1.5 fusion.55
  93.5 2.7 %fusion.15 = bf16[512,256]{0,1:T(8,128)(2,1)S(1)} fusion(f32[512,256]{0,1:T(8,128)S(1)} %get-tuple-element.167, bf16[1024,256]{1,0:T(8,128)(2,1)} %all_gather.24, f32[256]{0:T(256)S(1)} %copy-done.49, f32[512,1024]{1,0:T(8,128)} %copy-done.1, f32[1024]{0:T(1024)S(1)} %copy-done.47), kind=kOutput, calls=%fused_computation.30 | convolution fusion | flops 274071552 | bytes 3412992 | tf_op jit(solution)/shard_map/dot_general | solution.py:156
  97.0 1.0 fusion.66
  99.3 1.0 copy.106
  100.3 1.2 dynamic-slice.10
  102.4 1.3 constant_dynamic-update-slice_fusion.8
  103.7 1.3 constant_dynamic-update-slice_fusion.7
  105.0 1.3 constant_dynamic-update-slice_fusion.6
  106.3 1.3 constant_dynamic-update-slice_fusion.5
  107.6 1.3 constant_dynamic-update-slice_fusion.4
  108.9 8.9 %reduce-scatter.5.cloned.1.call-done = f32[64,768]{1,0:T(8,128)} async-done(((f32[256,768]{1,0:T(8,128)}), f32[64,768]{1,0:T(8,128)}) %reduce-scatter.5.cloned.1.call-update) | async-done | bytes 196624 | tf_op jit(solution)/shard_map/reduce_scatter | solution.py:243
  117.8 27.5 %reduce-scatter.11.cloned.1.call-done = f32[256,256]{1,0:T(8,128)} async-done(((f32[1024,256]{1,0:T(8,128)}), f32[256,256]{1,0:T(8,128)}) %reduce-scatter.11.cloned.1.call-update) | async-done | bytes 262160 | tf_op jit(solution)/shard_map/reduce_scatter | solution.py:246
  145.3 27.5 %reduce-scatter.9.cloned.1.call-done = f32[64,1024]{1,0:T(8,128)} async-done(((f32[256,1024]{1,0:T(8,128)}), f32[64,1024]{1,0:T(8,128)}) %reduce-scatter.9.cloned.1.call-update) | async-done | bytes 262160 | tf_op jit(solution)/shard_map/reduce_scatter | solution.py:245
  172.8 1.4 constant_dynamic-update-slice_fusion.3
  174.2 1.3 constant_dynamic-update-slice_fusion.2
  175.5 1.3 constant_dynamic-update-slice_fusion.1
  177.4 11.1 %all-reduce = f32[3072]{0:T(1024)S(1)} all-reduce(f32[3072]{0:T(1024)} %constant_dynamic-update-slice_fusion), channel_id=6, replica_groups=mesh['dp'=8,'shard'=4] {'shard'}, use_global_device_ids=true, to_apply=%region_29.30.clone | all-reduce | flops 3072 | bytes 24576
  188.5 21.5 %psum.39 = f32[768]{0:T(1024)S(1)} all-reduce(f32[768]{0:T(1024)S(1)} %dynamic-slice.11), channel_id=1, replica_groups=mesh['dp'=8,'shard'=4] {'dp'}, use_global_device_ids=true, to_apply=%region_30.31 | all-reduce | flops 768 | bytes 6144 | tf_op jit(solution)/shard_map/psum | solution.py:249
  210.7 40.8 %all-reduce.4.cloned.1.call-done = (f32[64,768]{1,0:T(8,128)}, f32[64,256]{1,0:T(8,128)}, f32[64,1024]{1,0:T(8,128)}, f32[256,256]{1,0:T(8,128)}) async-done(((f32[64,768]{1,0:T(8,128)}, f32[64,256]{1,0:T(8,128)}, f32[64,1024]{1,0:T(8,128)}, f32[256,256]{1,0:T(8,128)}), (f32[64,768]{1,0:T(8,128)}, f32[64,256]{1,0:T(8,128)}, f32[64,1024]{1,0:T(8,128)}, f32[256,256]{1,0:T(8,128)})) %all-reduce.4.cloned.1.call-update) | async-done | bytes 786448 | tf_op jit(solution)/shard_map/psum | solution.py:249
  251.5 1.6 multiply_subtract_fusion.3
  253.1 2.0 multiply_subtract_fusion.2
  255.1 1.9 multiply_subtract_fusion.1
  257.0 1.0 multiply_subtract_fusion
  (165 shorter events, 13.6 us)
Async XLA Ops:
  7.2 20.7 %copy-start.19 = (bf16[512,256]{1,0:T(8,128)(2,1)S(1)}, bf16[512,256]{1,0:T(8,128)(2,1)}, u32[]{:S(2)}) copy-start(bf16[512,256]{1,0:T(8,128)(2,1)} %param.27) | copy-start | bytes 786436
  7.2 21.0 %copy-start.20 = (bf16[512,256]{1,0:T(8,128)(2,1)S(1)}, bf16[512,256]{1,0:T(8,128)(2,1)}, u32[]{:S(2)}) copy-start(bf16[512,256]{1,0:T(8,128)(2,1)} %param.28) | copy-start | bytes 786436
  7.2 101.7 %reduce-scatter.7.cloned.1.call-start = ((), (), s32[]{:S(2)}) async-start(), calls=%async_computation.5 | async-start | bytes 327680 | tf_op jit(solution)/shard_map/reduce_scatter | solution.py:244
  15.4 34.8 %copy-start.35 = (f32[256]{0:T(256)}, f32[256]{0:T(256)S(1)}, u32[]{:S(2)}) copy-start(f32[256]{0:T(256)S(1)} %get-tuple-element.163) | copy-start | bytes 3076
  15.4 34.8 %copy-start.50 = (f32[256]{0:T(256)}, f32[256]{0:T(256)S(1)}, u32[]{:S(2)}) copy-start(f32[256]{0:T(256)S(1)} %get-tuple-element.162) | copy-start | bytes 3076
  28.1 22.1 %copy-start.28 = (f32[512]{0:T(512)}, f32[512]{0:T(512)S(1)}, u32[]{:S(2)}) copy-start(f32[512]{0:T(512)S(1)} %broadcast_multiply_fusion.5) | copy-start | bytes 6148
  28.3 21.9 %copy-start.32 = (f32[512]{0:T(512)}, f32[512]{0:T(512)S(1)}, u32[]{:S(2)}) copy-start(f32[512]{0:T(512)S(1)} %add_rsqrt_fusion.1) | copy-start | bytes 6148
  28.4 30.9 %copy-start.6 = (bf16[512,256]{0,1:T(8,128)(2,1)}, bf16[512,256]{0,1:T(8,128)(2,1)S(1)}, u32[]{:S(2)}) copy-start(bf16[512,256]{0,1:T(8,128)(2,1)S(1)} %copy.97) | copy-start | bytes 786436
  35.1 15.7 %copy-start.11 = (bf16[256,768]{1,0:T(8,128)(2,1)}, bf16[256,768]{1,0:T(8,128)(2,1)S(1)}, u32[]{:S(2)}) copy-start(bf16[256,768]{1,0:T(8,128)(2,1)S(1)} %all_gather.21) | copy-start | bytes 1179652
  51.2 2.8 %copy-start.2 = (bf16[512,256]{0,1:T(8,128)(2,1)}, bf16[512,256]{0,1:T(8,128)(2,1)S(1)}, u32[]{:S(2)}) copy-start(bf16[512,256]{0,1:T(8,128)(2,1)S(1)} %copy.91) | copy-start | bytes 786436
  52.9 3.3 %copy-start = (f32[8,512,512]{1,2,0:T(8,128)}, f32[8,512,512]{1,2,0:T(8,128)S(1)}, u32[]{:S(2)}) copy-start(f32[8,512,512]{1,2,0:T(8,128)S(1)} %get-tuple-element.165) | copy-start | bytes 25165828
  54.1 3.6 %copy-start.23 = (f32[8,512]{1,0:T(8,128)}, f32[8,512]{1,0:T(8,128)S(1)}, u32[]{:S(2)}) copy-start(f32[8,512]{1,0:T(8,128)S(1)} %fusion) | copy-start | bytes 49156
  56.2 1.6 copy-start.48
  56.2 2.6 copy-start.30
  56.2 2.6 copy-start.37
  57.7 1.7 copy-start.8
  59.4 2.4 copy-start.1
  70.3 47.6 %reduce-scatter.5.cloned.1.call-start = ((), (), s32[]{:S(2)}) async-start(), calls=%async_computation.4 | async-start | bytes 983040 | tf_op jit(solution)/shard_map/reduce_scatter | solution.py:243
  71.5 4.9 %copy-start.3 = (bf16[512,256]{0,1:T(8,128)(2,1)S(1)}, bf16[512,256]{0,1:T(8,128)(2,1)}, u32[]{:S(2)}) copy-start(bf16[512,256]{0,1:T(8,128)(2,1)} %copy-done.2) | copy-start | bytes 786436
  71.5 10.4 %slice-start = ((s8[8388608]{0:T(1024)(128)(4,1)}), s8[4194304]{0:T(1024)(128)(4,1)S(1)}, s32[]{:S(2)}) async-start(s8[8388608]{0:T(1024)(128)(4,1)} %bitcast.43), calls=%async_computation.9 | async-start | bytes 8388608
  76.4 5.5 %slice-start.1 = ((s8[8388608]{0:T(1024)(128)(4,1)}), s8[4194304]{0:T(1024)(128)(4,1)S(1)}, s32[]{:S(2)}) async-start(s8[8388608]{0:T(1024)(128)(4,1)} %bitcast.43), calls=%async_computation.10 | async-start | bytes 8388608
  86.6 1.5 copy-start.40
  88.0 3.8 %copy-start.22 = (f32[512]{0:T(512)S(1)}, f32[512]{0:T(512)}, u32[]{:S(2)}) copy-start(f32[512]{0:T(512)} %copy-done.21) | copy-start | bytes 6148
  88.1 3.8 %copy-start.27 = (f32[512]{0:T(512)S(1)}, f32[512]{0:T(512)}, u32[]{:S(2)}) copy-start(f32[512]{0:T(512)} %copy-done.26) | copy-start | bytes 6148
  88.1 3.8 %copy-start.31 = (f32[256]{0:T(256)S(1)}, f32[256]{0:T(256)}, u32[]{:S(2)}) copy-start(f32[256]{0:T(256)} %get-tuple-element.156) | copy-start | bytes 3076
  88.1 3.7 %copy-start.38 = (f32[256]{0:T(256)S(1)}, f32[256]{0:T(256)}, u32[]{:S(2)}) copy-start(f32[256]{0:T(256)} %get-tuple-element.158) | copy-start | bytes 3076
  88.1 57.2 %reduce-scatter.11.cloned.1.call-start = ((), (), s32[]{:S(2)}) async-start(), calls=%async_computation.7 | async-start | bytes 1310720 | tf_op jit(solution)/shard_map/reduce_scatter | solution.py:246
  91.7 1.7 copy-start.49
  91.7 81.0 %reduce-scatter.9.cloned.1.call-start = ((), (), s32[]{:S(2)}) async-start(), calls=%async_computation.6 | async-start | bytes 1310720 | tf_op jit(solution)/shard_map/reduce_scatter | solution.py:245
  93.4 158.1 %all-reduce.4.cloned.1.call-start = ((), (), s32[]{:S(2)}) async-start(), calls=%async_computation.8 | async-start | bytes 1572864 | tf_op jit(solution)/shard_map/psum | solution.py:249
  93.5 3.6 %copy-start.12 = (bf16[256,768]{1,0:T(8,128)(2,1)S(1)}, bf16[256,768]{1,0:T(8,128)(2,1)}, u32[]{:S(2)}) copy-start(bf16[256,768]{1,0:T(8,128)(2,1)} %copy-done.11) | copy-start | bytes 1179652
  99.0 111.0 %copy-start.34 = (f32[768]{0:T(1024)S(1)}, f32[768]{0:T(1024)}, u32[]{:S(2)}) copy-start(f32[768]{0:T(1024)} %param.35) | copy-start | bytes 9220
  99.0 152.4 %copy-start.18 = (f32[64,256]{1,0:T(8,128)S(1)}, f32[64,256]{1,0:T(8,128)}, u32[]{:S(2)}) copy-start(f32[64,256]{1,0:T(8,128)} %param.32) | copy-start | bytes 196612
  99.0 152.4 %copy-start.24 = (f32[64,256]{1,0:T(8,128)S(1)}, f32[64,256]{1,0:T(8,128)}, u32[]{:S(2)}) copy-start(f32[64,256]{1,0:T(8,128)} %param.39) | copy-start | bytes 196612
  99.0 152.4 %copy-start.25 = (f32[64,256]{1,0:T(8,128)S(1)}, f32[64,256]{1,0:T(8,128)}, u32[]{:S(2)}) copy-start(f32[64,256]{1,0:T(8,128)} %param.38) | copy-start | bytes 196612
  99.1 154.0 %copy-start.9 = (f32[64,768]{1,0:T(8,128)S(1)}, f32[64,768]{1,0:T(8,128)}, u32[]{:S(2)}) copy-start(f32[64,768]{1,0:T(8,128)} %param.31) | copy-start | bytes 589828
  99.3 74.9 %copy-start.42 = (f32[256]{0:T(256)S(1)}, f32[256]{0:T(256)}, u32[]{:S(2)}) copy-start(f32[256]{0:T(256)} %get-tuple-element.138) | copy-start | bytes 3076
  99.3 76.2 %copy-start.41 = (f32[256]{0:T(256)S(1)}, f32[256]{0:T(256)}, u32[]{:S(2)}) copy-start(f32[256]{0:T(256)} %get-tuple-element.155) | copy-start | bytes 3076
  99.3 77.5 %copy-start.45 = (f32[1024]{0:T(1024)S(1)}, f32[1024]{0:T(1024)}, u32[]{:S(2)}) copy-start(f32[1024]{0:T(1024)} %get-tuple-element.174) | copy-start | bytes 12292
  99.3 110.7 %copy-start.43 = (f32[768]{0:T(1024)S(1)}, f32[768]{0:T(1024)}, u32[]{:S(2)}) copy-start(f32[768]{0:T(1024)} %param.45) | copy-start | bytes 9220
  99.3 110.7 %copy-start.44 = (f32[768]{0:T(1024)S(1)}, f32[768]{0:T(1024)}, u32[]{:S(2)}) copy-start(f32[768]{0:T(1024)} %param.44) | copy-start | bytes 9220
  99.3 155.8 %copy-start.4 = (f32[64,1024]{1,0:T(8,128)S(1)}, f32[64,1024]{1,0:T(8,128)}, u32[]{:S(2)}) copy-start(f32[64,1024]{1,0:T(8,128)} %param.33) | copy-start | bytes 786436
  99.3 155.7 %copy-start.13 = (f32[64,1024]{1,0:T(8,128)S(1)}, f32[64,1024]{1,0:T(8,128)}, u32[]{:S(2)}) copy-start(f32[64,1024]{1,0:T(8,128)} %param.41) | copy-start | bytes 786436
  99.3 155.7 %copy-start.14 = (f32[64,1024]{1,0:T(8,128)S(1)}, f32[64,1024]{1,0:T(8,128)}, u32[]{:S(2)}) copy-start(f32[64,1024]{1,0:T(8,128)} %param.40) | copy-start | bytes 786436
  172.8 84.3 %copy-start.5 = (f32[256,256]{1,0:T(8,128)S(1)}, f32[256,256]{1,0:T(8,128)}, u32[]{:S(2)}) copy-start(f32[256,256]{1,0:T(8,128)} %param.34) | copy-start | bytes 786436
  172.8 84.3 %copy-start.15 = (f32[256,256]{1,0:T(8,128)S(1)}, f32[256,256]{1,0:T(8,128)}, u32[]{:S(2)}) copy-start(f32[256,256]{1,0:T(8,128)} %param.43) | copy-start | bytes 786436
  172.8 84.3 %copy-start.16 = (f32[256,256]{1,0:T(8,128)S(1)}, f32[256,256]{1,0:T(8,128)}, u32[]{:S(2)}) copy-start(f32[256,256]{1,0:T(8,128)} %param.42) | copy-start | bytes 786436
  251.5 5.6 %copy-start.17 = (f32[256,256]{1,0:T(8,128)S(1)}, f32[256,256]{1,0:T(8,128)}, u32[]{:S(2)}) copy-start(f32[256,256]{1,0:T(8,128)} %get-tuple-element.134) | copy-start | bytes 786436
  (11 other events, 11.4 us)
Sparse Core Ops, SparseCore 0:
  70.4 21.3 reduce-scatter.6
  94.5 23.2 reduce-scatter.4
  120.4 24.8 reduce-scatter.10
  147.8 24.8 reduce-scatter.8
  176.3 75.0 all-reduce.3
where the time goes:
time: 266 us; the launch traced here: 265 us
  waiting for transfers between devices  105 us (39%)
  blocking collectives  66.1 us (25%)
  matrix products  33.5 us (13%)
  other arithmetic  23.5 us (9%)
  local copies, waits for them, and re-layouts  21.1 us (8%)
  between operations  15.3 us (6%)
    psum x1, waiting for transfers between devices, shards(): lax.psum((local_sums[0], local_sums[1], local_sums[2], local_sums[3], loc...  40.8 us
    reduce_scatter x1, waiting for transfers between devices, shards(): lax.psum_scatter(grad_down, 'shard', scatter_dimension=0, tiled=True)  27.5 us
    reduce_scatter x1, waiting for transfers between devices, shards(): lax.psum_scatter(grad_up, 'shard', scatter_dimension=0, tiled=True)  27.5 us
    psum x1, blocking collectives, shards(): lax.psum((local_sums[0], local_sums[1], local_sums[2], local_sums[3], loc...  21.5 us
    unnamed x123, local copies, waits for them, and re-layouts  16.8 us
    unnamed x1, blocking collectives  11.1 us
    reduce_scatter x1, waiting for transfers between devices, shards(): lax.psum_scatter(grad_qkv, 'shard', scatter_dimension=0, tiled=True)  8.92 us
    dot_general x4, matrix products, contract_rows(): lax.dot_general(left, right, (((0,), (0,)), ((), ())), preferred_element_...  8.28 us
  transfers between devices with their start and end apart: 5, of which 4 were waited for; matrix products, arithmetic and copies ran while one was open for 16% of the time, Pallas kernels for 0%

commit v1 on v0

--- a/solution.py
+++ b/solution.py
@@ -6,6 +6,7 @@
 from jax.sharding import PartitionSpec as P
 
 HEAD = 32
+PAD = 64
 STEP = 10
 
 
@@ -60,6 +61,45 @@
     second_fix = 1.0 - beta_two**STEP
     update = first_next / first_fix / (jnp.sqrt(second_next / second_fix) + adam_eps)
     return (first_next, second_next, weight - learn_rate * (update + decay_rate * weight))
+
+
+def split_cols(values, width):
+    return jnp.concatenate(
+        [values[..., at : at + width] for at in range(0, values.shape[-1], width)], axis=-2
+    )
+
+
+def join_cols(values, count):
+    shard_count, rows, width = values.shape
+    values = values.reshape(shard_count, count, rows // count, width)
+    return values.transpose(0, 2, 1, 3).reshape(shard_count * rows // count, count * width)
+
+
+def exchange(values, axis, mask):
+    count = lax.axis_size(axis)
+    return lax.ppermute(values, axis, [(index, index ^ mask) for index in range(count)])
+
+
+def reduce_all(parts):
+    low, wide = jnp.bfloat16, jnp.float32
+    me = lax.axis_index("shard")
+    hold = parts
+    mask = 1
+    size = parts.shape[0]
+    pair = hold.reshape(size // 2, 2, *hold.shape[1:])
+    side = me % 2
+    keep = lax.dynamic_index_in_dim(pair, side, 1, keepdims=False)
+    send = lax.dynamic_index_in_dim(pair, 1 - side, 1, keepdims=False).astype(low)
+    hold = keep + exchange(send, "shard", 1).astype(wide)
+    side = me // 2
+    keep = lax.dynamic_index_in_dim(hold, side, 0, keepdims=False)
+    send = lax.dynamic_index_in_dim(hold, 1 - side, 0, keepdims=False).astype(low)
+    hold = keep + exchange(send, "shard", 2).astype(wide)
+    replicas = lax.axis_size("dp")
+    pieces = hold.astype(low).reshape(replicas, -1, hold.shape[-1])
+    received = lax.all_to_all(pieces, "dp", 0, 0, tiled=False)
+    piece = jnp.sum(received.astype(wide), axis=0).astype(low)
+    return lax.all_gather(piece, "dp", axis=0, tiled=True).astype(wide)
 
 
 def shards(
@@ -93,21 +133,28 @@
     position = jnp.arange(row_count, dtype=jnp.int32)
     segment = jnp.sum((seq_ends[None, :] <= position[:, None]).astype(jnp.int32), axis=1)
     live_rows = (position < seq_ends[-1]).astype(jnp.float32)
-    weight_pieces = (
-        qkv_weight.astype(jnp.bfloat16),
-        out_weight.astype(jnp.bfloat16),
-        up_weight.astype(jnp.bfloat16),
-        down_weight.astype(jnp.bfloat16),
-        gains_biases.astype(jnp.bfloat16),
-    )
-    gathered = (
-        lax.all_gather(weight_pieces[0], "shard", axis=0, tiled=True),
-        lax.all_gather(weight_pieces[1], "shard", axis=0, tiled=True),
-        lax.all_gather(weight_pieces[2], "shard", axis=0, tiled=True),
-        lax.all_gather(weight_pieces[3], "shard", axis=0, tiled=True),
-        lax.all_gather(weight_pieces[4], "shard", axis=0, tiled=True),
-    )
-    qkv_full, out_full, up_full, down_full, small_full = gathered
+    packed = jnp.concatenate(
+        [
+            split_cols(qkv_weight.astype(jnp.bfloat16), model_width),
+            out_weight.astype(jnp.bfloat16),
+            split_cols(up_weight.astype(jnp.bfloat16), model_width),
+            down_weight.astype(jnp.bfloat16),
+            gains_biases.astype(jnp.bfloat16).reshape(-1, model_width),
+        ],
+        axis=0,
+    )
+    gathered = lax.all_gather(packed, "shard", axis=0)
+    qkv_rows = qkv_weight.shape[0] * 3
+    out_rows = out_weight.shape[0]
+    up_rows = up_weight.shape[0] * 4
+    down_rows = down_weight.shape[0]
+    ends = [0, qkv_rows, qkv_rows + out_rows, qkv_rows + out_rows + up_rows]
+    ends.append(ends[-1] + down_rows)
+    qkv_full = join_cols(gathered[:, ends[0] : ends[1]], 3)
+    out_full = gathered[:, ends[1] : ends[2]].reshape(-1, model_width)
+    up_full = join_cols(gathered[:, ends[2] : ends[3]], 4)
+    down_full = gathered[:, ends[3] : ends[4]].reshape(-1, model_width)
+    small_full = gathered[:, ends[4] :].reshape(-1)
     small_parts = unpack_small(small_full.astype(jnp.float32), model_width)
     gain_one, bias_one, gain_two, bias_two, bias_query, bias_value, bias_out, bias_down, bias_up = (
         small_parts
@@ -155,16 +202,9 @@
     output = (
         middle + (jnp.dot(activated, down_full, preferred_element_type=jnp.float32) + bias_down)
     ).astype(jnp.bfloat16)
-    qkv_back, out_back, up_back, down_back, small_back = (
-        lax.all_gather(weight_pieces[0], "shard", axis=0, tiled=True),
-        lax.all_gather(weight_pieces[1], "shard", axis=0, tiled=True),
-        lax.all_gather(weight_pieces[2], "shard", axis=0, tiled=True),
-        lax.all_gather(weight_pieces[3], "shard", axis=0, tiled=True),
-        lax.all_gather(weight_pieces[4], "shard", axis=0, tiled=True),
-    )
-    back_parts = unpack_small(small_back.astype(jnp.float32), model_width)
-    gain_one_back = back_parts[0]
-    gain_two_back = back_parts[2]
+    qkv_back, out_back, up_back, down_back = qkv_full, out_full, up_full, down_full
+    gain_one_back = gain_one
+    gain_two_back = gain_two
     seed_grad = cotangent.astype(jnp.float32) * live_rows[:, None]
     down_in = seed_grad.astype(jnp.bfloat16)
     grad_down = contract_rows(activated, down_in)
@@ -239,16 +279,30 @@
             bias_up_grad,
         ]
     )
-    local_sums = (
-        lax.psum_scatter(grad_qkv, "shard", scatter_dimension=0, tiled=True),
-        lax.psum_scatter(grad_out, "shard", scatter_dimension=0, tiled=True),
-        lax.psum_scatter(grad_up, "shard", scatter_dimension=0, tiled=True),
-        lax.psum_scatter(grad_down, "shard", scatter_dimension=0, tiled=True),
-        lax.psum_scatter(small_grad, "shard", scatter_dimension=0, tiled=True),
-    )
-    owned = lax.psum(
-        (local_sums[0], local_sums[1], local_sums[2], local_sums[3], local_sums[4]), "dp"
-    )
+    shard_count = gathered.shape[0]
+    by_shard = lambda grad: grad.reshape(shard_count, -1, grad.shape[-1])
+    ffn_parts = jnp.concatenate(
+        [by_shard(grad_down), split_cols(by_shard(grad_up), model_width)], axis=1
+    )
+    small_rows = small_grad.reshape(shard_count, -1, model_width)
+    pad_rows = PAD - small_rows.shape[1]
+    att_parts = jnp.concatenate(
+        [
+            by_shard(grad_out),
+            split_cols(by_shard(grad_qkv), model_width),
+            small_rows,
+            jnp.zeros((shard_count, pad_rows, model_width), jnp.float32),
+        ],
+        axis=1,
+    )
+    ffn_sum = reduce_all(ffn_parts)
+    att_sum = reduce_all(att_parts)
+    own_down = ffn_sum[:down_rows]
+    own_up = join_cols(ffn_sum[None, down_rows:], 4)
+    own_out = att_sum[:out_rows]
+    own_qkv = join_cols(att_sum[None, out_rows : out_rows + qkv_rows], 3)
+    own_small = att_sum[out_rows + qkv_rows :][: small_rows.shape[1]].reshape(-1)
+    owned = (own_qkv, own_out, own_up, own_down, own_small)
     qkv_new = adam_step(qkv_weight, owned[0], qkv_first, qkv_second, matrix_decay)
     out_new = adam_step(out_weight, owned[1], out_first, out_second, matrix_decay)
     up_new = adam_step(up_weight, owned[2], up_first, up_second, matrix_decay)

time: 266 us -> 196 us (0.74)
  waiting for transfers between devices: 105 us -> 37.1 us
  starting transfers between devices: 0.39 us -> 10.4 us
  matrix products: 33.5 us -> 27.6 us
  blocking collectives: 66.1 us -> 61.5 us
    reduce_scatter x4 -> x0, waiting for transfers between devices: 63.8 us -> none  [the longest x1 27.5 us: shards(): lax.psum_scatter(grad_down, 'shard', scatter_dimension=0, tiled=True)]
    psum x1 -> x0, waiting for transfers between devices: 40.8 us -> none  [shards(): lax.psum((local_sums[0], local_sums[1], local_sums[2], local_sums[3], loc...]
    all_gather x5 -> x2, blocking collectives: 33.5 us -> 61.5 us  [reduce_all(): return lax.all_gather(piece, 'dp', axis=0, tiled=True).astype(wide)]
    psum x1 -> x0, blocking collectives: 21.5 us -> none  [shards(): lax.psum((local_sums[0], local_sums[1], local_sums[2], local_sums[3], loc...]
    all_gather x0 -> x1, waiting for transfers between devices: none -> 20 us  [shards(): gathered = lax.all_gather(packed, 'shard', axis=0)]
    all_to_all x0 -> x2, waiting for transfers between devices: none -> 12.4 us  [reduce_all(): received = lax.all_to_all(pieces, 'dp', 0, 0, tiled=False)]
    unnamed x1 -> x0, blocking collectives: 11.1 us -> none
    all_to_all x0 -> x2, starting transfers between devices: none -> 8.92 us  [reduce_all(): received = lax.all_to_all(pieces, 'dp', 0, 0, tiled=False)]
  transfers between devices with their start and end apart: 5 -> 7, of which waited for: 4 -> 5; matrix products, arithmetic and copies ran while one was open for 16% -> 8% of each run, Pallas kernels for 0% -> 0%
where the time goes in v1:
time: 196 us
  blocking collectives  61.5 us (31%)
  waiting for transfers between devices  37.1 us (19%)
  matrix products  27.6 us (14%)
  other arithmetic  24.4 us (12%)
  local copies, waits for them, and re-layouts  19 us (10%)
  between operations  15.4 us (8%)
  starting transfers between devices  10.4 us (5%)
    all_gather x2, blocking collectives, reduce_all(): return lax.all_gather(piece, 'dp', axis=0, tiled=True).astype(wide)  61.5 us
    all_gather x1, waiting for transfers between devices, shards(): gathered = lax.all_gather(packed, 'shard', axis=0)  20 us
    all_to_all x2, waiting for transfers between devices, reduce_all(): received = lax.all_to_all(pieces, 'dp', 0, 0, tiled=False)  12.4 us
    unnamed x151, local copies, waits for them, and re-layouts  9.61 us
    all_to_all x2, starting transfers between devices, reduce_all(): received = lax.all_to_all(pieces, 'dp', 0, 0, tiled=False)  8.92 us
    dot_general x4, matrix products, contract_cols(): lax.dot_general(left, right, (((1,), (1,)), ((), ())), preferred_element_...  5.7 us
    dot_general x1, matrix products, shards(): jnp.einsum('qhd,khd->hqk', attended_grad, value_rows, preferred_element_t...  5.4 us
    sub x5, other arithmetic, adam_step(): weight - learn_rate * (update + decay_rate * weight)  5.04 us
  transfers between devices with their start and end apart: 7, of which 5 were waited for; matrix products, arithmetic and copies ran while one was open for 8% of the time, Pallas kernels for 0%

profile of v1, /device:TPU:0, one launch (start us, length us, event | category | flops | bytes accessed | tf_op | source)
XLA Modules:
  0.0 195.5 jit_solution(13959635374827758515)
XLA Ops:
  7.3 0.7 convert_element_type.154
  8.0 0.9 convert_element_type.150
  9.0 1.0 convert_element_type.152
  10.0 0.8 constant_dynamic-update-slice_fusion.5
  10.9 1.0 convert_dynamic-update-slice_fusion
  11.9 0.7 copy-done.21
  15.3 20.0 %all-gather.4.cloned.1.call-done = bf16[4,771,256]{2,1,0:T(8,128)(2,1)} async-done(((bf16[1,771,256]{2,1,0:T(8,128)(2,1)}), bf16[4,771,256]{2,1,0:T(8,128)(2,1)}) %all-gather.4.cloned.1.call-update) | async-done | bytes 1579024 | tf_op jit(solution)/shard_map/all_gather | solution.py:146
  35.2 0.7 slice_convert_fusion
  36.6 1.3 fusion.69
  40.7 1.6 fusion.74
  42.3 1.2 fusion
  43.5 2.0 %copy-done = f32[8,512,512]{1,2,0:T(8,128)} copy-done((f32[8,512,512]{1,2,0:T(8,128)}, f32[8,512,512]{1,2,0:T(8,128)S(1)}, u32[]{:S(2)}) %copy-start) | copy-done | bytes 8388632
  45.6 1.5 fusion.21
  48.2 2.0 %fusion.47 = f32[1024,256]{1,0:T(8,128)} fusion(bf16[512,256]{0,1:T(8,128)(2,1)S(1)} %copy.112, f32[512]{0:T(512)S(1)} %fusion.54, f32[512,1024]{1,0:T(8,128)S(1)} %fusion.63, f32[1024]{0:T(1024)S(1)} %slice.218), kind=kOutput, calls=%fused_computation.93 | convolution fusion | flops 274071552 | bytes 3414016 | tf_op jit(solution)/shard_map/dot_general | solution.py:37
  50.2 2.4 %convert_reduce_fusion = (f32[1024]{0:T(1024)}, bf16[512,1024]{1,0:T(8,128)(2,1)S(1)}) fusion(f32[512,1024]{1,0:T(8,128)S(1)} %fusion.63, f32[1024]{0:T(1024)S(1)} %slice.218, bf16[1024,256]{1,0:T(8,128)(2,1)S(1)} %bitcast.149, bf16[512,256]{0,1:T(8,128)(2,1)S(1)} %copy.112, f32[512]{0:T(512)S(1)} %fusion.54), kind=kOutput, calls=%fused_computation.20 | convolution fusion | flops 280886272 | bytes 3942400 | tf_op jit(solution)/shard_map/dot_general | solution.py:43
  52.6 1.8 fusion.77
  55.7 1.6 multiply_reduce_fusion.1
  57.3 1.9 convert_reduce_fusion.4
  59.5 4.9 %fusion.16 = bf16[8,32,512]{2,1,0:T(8,128)(2,1)S(1)} fusion(bf16[512,8,32]{0,2,1:T(8,128)(2,1)S(1)} %bitcast.109, f32[8,512,512]{1,2,0:T(8,128)} %copy-done, f32[8,512]{1,0:T(8,128)S(1)} %log_add_fusion), kind=kOutput, calls=%fused_computation.31 | convolution fusion | flops 138543104 | bytes 8929280 | tf_op jit(solution)/shard_map/hqk,qhd->khd/dot_general | solution.py:236
  64.4 5.4 %multiply_reduce_fusion = (f32[8,512]{1,0:T(8,128)S(1)}, f32[8,512,512]{1,2,0:T(8,128)S(1)}) fusion(f32[8,512,512]{1,2,0:T(8,128)} %copy-done, f32[8,512]{1,0:T(8,128)S(1)} %log_add_fusion, bf16[512,8,32]{0,2,1:T(8,128)(2,1)S(1)} %bitcast.110, bf16[512,8,32]{0,2,1:T(8,128)(2,1)S(1)} %bitcast.122), kind=kOutput, calls=%fused_computation.1 | convolution fusion | flops 140505088 | bytes 17334272 | tf_op jit(solution)/shard_map/qhd,khd->hqk/dot_general | solution.py:238
  69.9 2.6 %multiply_convert_fusion = bf16[8,512,512]{1,2,0:T(8,128)(2,1)S(1)} fusion(f32[8,512,512]{1,2,0:T(8,128)S(1)} %get-tuple-element.174, f32[8,512,512]{1,2,0:T(8,128)S(1)} %bitcast.105, f32[8,512]{1,0:T(8,128)S(1)} %get-tuple-element.173, f32[8,512]{1,0:T(8,128)S(1)} %log_add_fusion), kind=kLoop, calls=%fused_computation | loop fusion | flops 8388608 | bytes 21004288 | tf_op jit(solution)/shard_map/convert_element_type | solution.py:242
  72.4 1.3 fusion.20
  73.8 0.7 fusion.19
  74.8 1.2 fusion.76
  76.1 1.3 fusion.58
  78.0 1.0 fusion.15
  79.0 0.8 copy.123
  80.7 0.8 fusion.37
  81.8 0.9 fusion.71
  83.3 2.2 %concatenate.51 = f32[2,2,320,256]{3,2,1,0:T(8,128)S(1)} concatenate(f32[2,2,64,256]{3,2,1,0:T(8,128)S(1)} %fusion.45, f32[2,2,64,256]{3,2,1,0:T(8,128)} %bitcast.137, f32[2,2,64,256]{3,2,1,0:T(8,128)} %bitcast.136, f32[2,2,64,256]{3,2,1,0:T(8,128)S(1)} %bitcast.135, f32[2,2,3,256]{3,2,1,0:T(4,128)S(1)} %concatenate.50, f32[2,2,61,256]{3,2,1,0:T(8,128)S(1)} %broadcast_in_dim.28), dimensions={2} | concatenate | bytes 2621440 | tf_op jit(solution)/shard_map/concatenate | solution.py:289
  86.0 1.4 collective-permute-done
  87.4 0.8 copy-done.6
  89.3 1.0 fusion.34
  90.2 2.0 %copy.124 = f32[512,256]{1,0:T(8,128)} copy(f32[512,256]{0,1:T(8,128)} %fusion.34) | data formatting | bytes 1048576
  92.3 3.3 %collective-permute-done.1 = bf16[320,256]{1,0:T(8,128)(2,1)} collective-permute-done((bf16[320,256]{1,0:T(8,128)(2,1)}, bf16[320,256]{1,0:T(8,128)(2,1)}, u32[]{:S(2)}, u32[]{:S(2)}) %collective-permute-start.1) | collective-permute-done | bytes 163872 | tf_op jit(solution)/shard_map/ppermute | solution.py:80
  95.6 1.8 fusion.41
  97.4 5.5 %all-to-all-start = ((bf16[8,40,256]{2,1,0:T(8,128)(2,1)}), bf16[8,40,256]{2,1,0:T(8,128)(2,1)S(1)}, u32[]{:S(2)}, u32[]{:S(2)}) async-start(bf16[8,40,256]{2,1,0:T(8,128)(2,1)} %bitcast.33), calls=%async_computation | async-start | bytes 327680 | tf_op jit(solution)/shard_map/all_to_all | solution.py:100
  102.9 1.2 bitcast_add_fusion
  104.8 5.6 %all-to-all-done = bf16[8,40,256]{2,1,0:T(8,128)(2,1)S(1)} async-done(((bf16[8,40,256]{2,1,0:T(8,128)(2,1)}), bf16[8,40,256]{2,1,0:T(8,128)(2,1)S(1)}, u32[]{:S(2)}, u32[]{:S(2)}) %all-to-all-start) | async-done | bytes 163872 | tf_op jit(solution)/shard_map/all_to_all | solution.py:100
  110.5 30.6 %all_gather.14 = bf16[320,256]{1,0:T(8,128)(2,1)S(1)} all-gather(bf16[40,256]{1,0:T(8,128)(2,1)S(1)} %reduce_sum.214), channel_id=1, replica_groups=mesh['dp'=8,'shard'=4] {'dp'}, dimensions={0}, use_global_device_ids=true | all-gather | bytes 184320 | tf_op jit(solution)/shard_map/all_gather | solution.py:102
  141.3 1.5 multiply_subtract_fusion.3
  142.9 0.8 fusion.38
  143.6 3.4 %all-to-all-start.1 = ((bf16[8,64,256]{2,1,0:T(8,128)(2,1)}), bf16[8,64,256]{2,1,0:T(8,128)(2,1)S(1)}, u32[]{:S(2)}, u32[]{:S(2)}) async-start(bf16[8,64,256]{2,1,0:T(8,128)(2,1)} %bitcast.46), calls=%async_computation.1 | async-start | bytes 524288 | tf_op jit(solution)/shard_map/all_to_all | solution.py:100
  147.7 0.9 multiply_subtract_fusion.2
  148.6 6.7 %all-to-all-done.1 = bf16[8,64,256]{2,1,0:T(8,128)(2,1)S(1)} async-done(((bf16[8,64,256]{2,1,0:T(8,128)(2,1)}), bf16[8,64,256]{2,1,0:T(8,128)(2,1)S(1)}, u32[]{:S(2)}, u32[]{:S(2)}) %all-to-all-start.1) | async-done | bytes 262176 | tf_op jit(solution)/shard_map/all_to_all | solution.py:100
  155.4 30.9 %all_gather.15 = bf16[512,256]{1,0:T(8,128)(2,1)S(1)} all-gather(bf16[64,256]{1,0:T(8,128)(2,1)S(1)} %reduce_sum.215), channel_id=1, replica_groups=mesh['dp'=8,'shard'=4] {'dp'}, dimensions={0}, use_global_device_ids=true | all-gather | bytes 294912 | tf_op jit(solution)/shard_map/all_gather | solution.py:102
  186.7 1.0 multiply_subtract_fusion
  187.7 1.0 multiply_subtract_fusion.1
  (221 shorter events, 14.0 us)
Async XLA Ops:
  7.2 5.5 %copy-start.59 = (s32[128]{0:T(128)S(1)}, s32[128]{0:T(128)}, u32[]{:S(2)}) copy-start(s32[128]{0:T(128)} %param.30) | copy-start | bytes 1540
  7.2 5.5 %copy-start.58 = (s32[128]{0:T(128)S(1)}, s32[128]{0:T(128)}, u32[]{:S(2)}) copy-start(s32[128]{0:T(128)} %param.29) | copy-start | bytes 1540
  7.2 6.4 %copy-start.29 = (bf16[512,256]{1,0:T(8,128)(2,1)S(1)}, bf16[512,256]{1,0:T(8,128)(2,1)}, u32[]{:S(2)}) copy-start(bf16[512,256]{1,0:T(8,128)(2,1)} %param.27) | copy-start | bytes 786436
  7.2 6.6 %copy-start.30 = (bf16[512,256]{1,0:T(8,128)(2,1)S(1)}, bf16[512,256]{1,0:T(8,128)(2,1)}, u32[]{:S(2)}) copy-start(bf16[512,256]{1,0:T(8,128)(2,1)} %param.28) | copy-start | bytes 786436
  7.2 28.0 %all-gather.4.cloned.1.call-start = ((), (), s32[]{:S(2)}) async-start(), calls=%async_computation.2 | async-start | bytes 1986560 | tf_op jit(solution)/shard_map/all_gather | solution.py:146
  14.0 36.2 %copy-start.12 = (bf16[512,256]{0,1:T(8,128)(2,1)}, bf16[512,256]{0,1:T(8,128)(2,1)S(1)}, u32[]{:S(2)}) copy-start(bf16[512,256]{0,1:T(8,128)(2,1)S(1)} %copy.112) | copy-start | bytes 786436
  14.7 35.5 %copy-start.45 = (f32[512]{0:T(512)}, f32[512]{0:T(512)S(1)}, u32[]{:S(2)}) copy-start(f32[512]{0:T(512)S(1)} %fusion.54) | copy-start | bytes 6148
  14.9 24.0 %copy-start.36 = (f32[512]{0:T(512)}, f32[512]{0:T(512)S(1)}, u32[]{:S(2)}) copy-start(f32[512]{0:T(512)S(1)} %broadcast_multiply_fusion.5) | copy-start | bytes 6148
  15.0 23.9 %copy-start.39 = (f32[512]{0:T(512)}, f32[512]{0:T(512)S(1)}, u32[]{:S(2)}) copy-start(f32[512]{0:T(512)S(1)} %add_rsqrt_fusion.1) | copy-start | bytes 6148
  36.0 14.2 %copy-start.52 = (f32[1024]{0:T(1024)}, f32[1024]{0:T(1024)S(1)}, u32[]{:S(2)}) copy-start(f32[1024]{0:T(1024)S(1)} %slice.218) | copy-start | bytes 12292
  36.6 2.4 %copy-start.43 = (f32[256]{0:T(256)}, f32[256]{0:T(256)S(1)}, u32[]{:S(2)}) copy-start(f32[256]{0:T(256)S(1)} %get-tuple-element.168) | copy-start | bytes 3076
  36.6 2.4 %copy-start.56 = (f32[256]{0:T(256)}, f32[256]{0:T(256)S(1)}, u32[]{:S(2)}) copy-start(f32[256]{0:T(256)S(1)} %get-tuple-element.167) | copy-start | bytes 3076
  36.6 17.8 %copy-start.38 = (f32[256]{0:T(256)}, f32[256]{0:T(256)S(1)}, u32[]{:S(2)}) copy-start(f32[256]{0:T(256)S(1)} %get-tuple-element.161) | copy-start | bytes 3076
  37.9 12.2 %copy-start.19 = (bf16[4,256,256]{2,1,0:T(8,128)(2,1)}, bf16[4,256,256]{2,1,0:T(8,128)(2,1)S(1)}, u32[]{:S(2)}) copy-start(bf16[4,256,256]{2,1,0:T(8,128)(2,1)S(1)} %get-tuple-element.149) | copy-start | bytes 1572868
  40.7 2.9 %copy-start.8 = (bf16[512,256]{0,1:T(8,128)(2,1)}, bf16[512,256]{0,1:T(8,128)(2,1)S(1)}, u32[]{:S(2)}) copy-start(bf16[512,256]{0,1:T(8,128)(2,1)S(1)} %copy.105) | copy-start | bytes 786436
  42.3 3.3 %copy-start = (f32[8,512,512]{1,2,0:T(8,128)}, f32[8,512,512]{1,2,0:T(8,128)S(1)}, u32[]{:S(2)}) copy-start(f32[8,512,512]{1,2,0:T(8,128)S(1)} %get-tuple-element.170) | copy-start | bytes 25165828
  47.4 7.0 %copy-start.33 = (f32[512]{0:T(512)}, f32[512]{0:T(512)S(1)}, u32[]{:S(2)}) copy-start(f32[512]{0:T(512)S(1)} %broadcast_multiply_fusion.4) | copy-start | bytes 6148
  47.5 6.9 %copy-start.35 = (f32[512]{0:T(512)}, f32[512]{0:T(512)S(1)}, u32[]{:S(2)}) copy-start(f32[512]{0:T(512)S(1)} %add_rsqrt_fusion) | copy-start | bytes 6148
  48.2 2.0 %copy-start.3 = (f32[512,1024]{1,0:T(8,128)}, f32[512,1024]{1,0:T(8,128)S(1)}, u32[]{:S(2)}) copy-start(f32[512,1024]{1,0:T(8,128)S(1)} %fusion.63) | copy-start | bytes 6291460
  59.5 4.9 %copy-start.9 = (bf16[512,256]{0,1:T(8,128)(2,1)S(1)}, bf16[512,256]{0,1:T(8,128)(2,1)}, u32[]{:S(2)}) copy-start(bf16[512,256]{0,1:T(8,128)(2,1)} %copy-done.8) | copy-start | bytes 786436
  59.5 10.3 %slice-start = ((s8[8388608]{0:T(1024)(128)(4,1)}), s8[4194304]{0:T(1024)(128)(4,1)S(1)}, s32[]{:S(2)}) async-start(s8[8388608]{0:T(1024)(128)(4,1)} %bitcast.104), calls=%async_computation.3 | async-start | bytes 8388608
  64.4 5.4 %slice-start.1 = ((s8[8388608]{0:T(1024)(128)(4,1)}), s8[4194304]{0:T(1024)(128)(4,1)S(1)}, s32[]{:S(2)}) async-start(s8[8388608]{0:T(1024)(128)(4,1)} %bitcast.104), calls=%async_computation.4 | async-start | bytes 8388608
  80.5 2.2 %copy-start.18 = (f32[512,256]{1,0:T(8,128)S(1)}, f32[512,256]{1,0:T(8,128)}, u32[]{:S(2)}) copy-start(f32[512,256]{1,0:T(8,128)} %get-tuple-element.176) | copy-start | bytes 1572868
  80.6 2.1 %copy-start.1 = (f32[2,2,512,256]{3,2,1,0:T(8,128)}, f32[2,2,512,256]{3,2,1,0:T(8,128)S(1)}, u32[]{:S(2)}) copy-start(f32[2,2,512,256]{3,2,1,0:T(8,128)S(1)} %constant_dynamic-update-slice_fusion.10) | copy-start | bytes 6291460
  80.6 2.5 %copy-start.42 = (f32[3072]{0:T(1024)S(1)}, f32[3072]{0:T(1024)}, u32[]{:S(2)}) copy-start(f32[3072]{0:T(1024)} %custom-call.1) | copy-start | bytes 36868
  80.6 2.5 %copy-start.54 = (f32[256]{0:T(256)S(1)}, f32[256]{0:T(256)}, u32[]{:S(2)}) copy-start(f32[256]{0:T(256)} %get-tuple-element.125) | copy-start | bytes 3076
  80.7 2.5 %copy-start.46 = (f32[256]{0:T(256)S(1)}, f32[256]{0:T(256)}, u32[]{:S(2)}) copy-start(f32[256]{0:T(256)} %get-tuple-element.177) | copy-start | bytes 3076
  80.7 2.6 %copy-start.48 = (f32[256]{0:T(256)S(1)}, f32[256]{0:T(256)}, u32[]{:S(2)}) copy-start(f32[256]{0:T(256)} %get-tuple-element.146) | copy-start | bytes 3076
  80.7 2.6 %copy-start.47 = (f32[256]{0:T(256)S(1)}, f32[256]{0:T(256)}, u32[]{:S(2)}) copy-start(f32[256]{0:T(256)} %get-tuple-element.160) | copy-start | bytes 3076
  80.7 2.6 %copy-start.51 = (f32[1024]{0:T(1024)S(1)}, f32[1024]{0:T(1024)}, u32[]{:S(2)}) copy-start(f32[1024]{0:T(1024)} %get-tuple-element.179) | copy-start | bytes 12292
  81.5 21.3 %collective-permute-start.2 = (bf16[2,512,256]{2,1,0:T(8,128)(2,1)}, bf16[2,512,256]{2,1,0:T(8,128)(2,1)}, u32[]{:S(2)}, u32[]{:S(2)}) collective-permute-start(bf16[2,512,256]{2,1,0:T(8,128)(2,1)} %fusion.37), channel_id=1, source_target_pairs={{0,1},{1,0},{2,3},{3,2},{4,5},{5,4},{6,7},{7,6},{8,9},{9,8},{10,11... | collective-permute-start | bytes 1572872 | tf_op jit(solution)/shard_map/ppermute | solution.py:80
  85.6 1.7 collective-permute-start
  88.3 14.7 %copy-start.2 = (f32[2,2,512,256]{3,2,1,0:T(8,128)S(1)}, f32[2,2,512,256]{3,2,1,0:T(8,128)}, u32[]{:S(2)}) copy-start(f32[2,2,512,256]{3,2,1,0:T(8,128)} %copy-done.1) | copy-start | bytes 6291460
  88.9 6.7 %collective-permute-start.1 = (bf16[320,256]{1,0:T(8,128)(2,1)}, bf16[320,256]{1,0:T(8,128)(2,1)}, u32[]{:S(2)}, u32[]{:S(2)}) collective-permute-start(bf16[320,256]{1,0:T(8,128)(2,1)} %fusion.51), channel_id=1, source_target_pairs={{0,2},{1,3},{2,0},{3,1},{4,6},{5,7},{6,4},{7,5},{8,10},{9,11},{10,... | collective-permute-start | bytes 491528 | tf_op jit(solution)/shard_map/ppermute | solution.py:80
  97.4 13.1 %all-to-all-start = ((bf16[8,40,256]{2,1,0:T(8,128)(2,1)}), bf16[8,40,256]{2,1,0:T(8,128)(2,1)S(1)}, u32[]{:S(2)}, u32[]{:S(2)}) async-start(bf16[8,40,256]{2,1,0:T(8,128)(2,1)} %bitcast.33), calls=%async_computation | async-start | bytes 327680 | tf_op jit(solution)/shard_map/all_to_all | solution.py:100
  102.9 38.4 %copy-start.28 = (f32[64,256]{1,0:T(8,128)S(1)}, f32[64,256]{1,0:T(8,128)}, u32[]{:S(2)}) copy-start(f32[64,256]{1,0:T(8,128)} %param.32) | copy-start | bytes 196612
  102.9 38.4 %copy-start.34 = (f32[64,256]{1,0:T(8,128)S(1)}, f32[64,256]{1,0:T(8,128)}, u32[]{:S(2)}) copy-start(f32[64,256]{1,0:T(8,128)} %param.39) | copy-start | bytes 196612
  104.1 42.9 %copy-start.41 = (f32[768]{0:T(1024)S(1)}, f32[768]{0:T(1024)}, u32[]{:S(2)}) copy-start(f32[768]{0:T(1024)} %param.35) | copy-start | bytes 9220
  104.2 42.9 %copy-start.49 = (f32[768]{0:T(1024)S(1)}, f32[768]{0:T(1024)}, u32[]{:S(2)}) copy-start(f32[768]{0:T(1024)} %param.45) | copy-start | bytes 9220
  104.2 42.9 %copy-start.50 = (f32[768]{0:T(1024)S(1)}, f32[768]{0:T(1024)}, u32[]{:S(2)}) copy-start(f32[768]{0:T(1024)} %param.44) | copy-start | bytes 9220
  104.2 43.5 %copy-start.17 = (f32[64,768]{1,0:T(8,128)S(1)}, f32[64,768]{1,0:T(8,128)}, u32[]{:S(2)}) copy-start(f32[64,768]{1,0:T(8,128)} %param.31) | copy-start | bytes 589828
  104.2 43.5 %copy-start.31 = (f32[64,768]{1,0:T(8,128)S(1)}, f32[64,768]{1,0:T(8,128)}, u32[]{:S(2)}) copy-start(f32[64,768]{1,0:T(8,128)} %param.37) | copy-start | bytes 589828
  104.2 43.5 %copy-start.32 = (f32[64,768]{1,0:T(8,128)S(1)}, f32[64,768]{1,0:T(8,128)}, u32[]{:S(2)}) copy-start(f32[64,768]{1,0:T(8,128)} %param.36) | copy-start | bytes 589828
  104.2 38.7 %collective-permute-start.3 = (bf16[512,256]{1,0:T(8,128)(2,1)S(1)}, bf16[512,256]{1,0:T(8,128)(2,1)S(1)}, u32[]{:S(2)}, u32[]{:S(2)}) collective-permute-start(bf16[512,256]{1,0:T(8,128)(2,1)S(1)} %fusion.44), channel_id=1, source_target_pairs={{0,2},{1,3},{2,0},{3,1},{4,6},{5,7},{6,4},{7,5},{8,10},{9,11},{10,... | collective-permute-start | bytes 786440 | tf_op jit(solution)/shard_map/ppermute | solution.py:80
  143.6 11.8 %all-to-all-start.1 = ((bf16[8,64,256]{2,1,0:T(8,128)(2,1)}), bf16[8,64,256]{2,1,0:T(8,128)(2,1)S(1)}, u32[]{:S(2)}, u32[]{:S(2)}) async-start(bf16[8,64,256]{2,1,0:T(8,128)(2,1)} %bitcast.46), calls=%async_computation.1 | async-start | bytes 524288 | tf_op jit(solution)/shard_map/all_to_all | solution.py:100
  147.7 38.9 %copy-start.10 = (f32[256,256]{1,0:T(8,128)S(1)}, f32[256,256]{1,0:T(8,128)}, u32[]{:S(2)}) copy-start(f32[256,256]{1,0:T(8,128)} %param.34) | copy-start | bytes 786436
  147.7 38.9 %copy-start.24 = (f32[256,256]{1,0:T(8,128)S(1)}, f32[256,256]{1,0:T(8,128)}, u32[]{:S(2)}) copy-start(f32[256,256]{1,0:T(8,128)} %param.43) | copy-start | bytes 786436
  147.7 38.9 %copy-start.25 = (f32[256,256]{1,0:T(8,128)S(1)}, f32[256,256]{1,0:T(8,128)}, u32[]{:S(2)}) copy-start(f32[256,256]{1,0:T(8,128)} %param.42) | copy-start | bytes 786436
  (22 other events, 30.3 us)
Sparse Core Ops, SparseCore 0:
  12.8 22.4 all-gather.3

commit v2 on v0

v2 whole, which is shorter than its diff:
```python
import functools
import math

import jax
import jax.numpy as jnp
from jax import lax
from jax.experimental import pallas as pl
from jax.experimental.pallas import tpu as pltpu
from jax.sharding import PartitionSpec as P

HEAD = 32
STEP = 10
LANES = 128
GROUP = 8
SMALL_PAD = 16
TILE_ROWS = 8

norm_eps = 1e-05
beta_one = 0.9
beta_two = 0.95
learn_rate = 0.1
adam_eps = 1e-08
matrix_decay = 0.1
masked_score = -1e30
low = jnp.bfloat16
wide = jnp.float32
log2_e = math.log2(math.e)
score_scale = 1.0 / math.sqrt(HEAD)
tanh_scale = math.sqrt(2.0 / math.pi)
cubic = 0.044715


def dot_nn(left, right):
    return jnp.dot(left, right, preferred_element_type=wide)


def dot_nt(left, right):
    return lax.dot_general(left, right, (((1,), (1,)), ((), ())), preferred_element_type=wide)


def standardize(values):
    centered = values - jnp.mean(values, axis=-1, keepdims=True)
    root_inv = lax.rsqrt(jnp.mean(centered * centered, axis=-1, keepdims=True) + norm_eps)
    return centered * root_inv, root_inv


def norm_back(upstream, normed, root_inv, gain):
    scaled = upstream * gain
    inner_mean = jnp.mean(scaled, axis=-1, keepdims=True)
    cross_mean = jnp.mean(scaled * normed, axis=-1, keepdims=True)
    through = root_inv * (scaled - inner_mean - normed * cross_mean)
    return (
        through,
        jnp.sum(upstream * normed, axis=0, keepdims=True),
        jnp.sum(upstream, axis=0, keepdims=True),
    )


def iota(shape, dim):
    return lax.broadcasted_iota(jnp.int32, shape, dim)


def own_row(lengths, owners, device):
    return jnp.where(owners == device, lengths, 0)


def ends_both(own):
    count = own.shape[1]
    shape = (count, count)
    rows, cols = iota(shape, 0), iota(shape, 1)
    spread = jnp.broadcast_to(own, shape)
    ends_col = jnp.sum(jnp.where(cols <= rows, spread, 0), axis=1, keepdims=True)
    own_col = jnp.sum(jnp.where(cols == rows, spread, 0), axis=1, keepdims=True)
    ends_row = jnp.sum(
        jnp.where(rows <= cols, jnp.broadcast_to(own_col, shape), 0), axis=0, keepdims=True
    )
    return ends_col, ends_row


def fill_mask(bias_ref, own, rows):
    ends_col, ends_row = ends_both(own)
    count = own.shape[1]
    seg_row = jnp.sum(
        (ends_col <= iota((count, rows), 1)).astype(jnp.int32), axis=0, keepdims=True
    )
    seg_col = jnp.sum(
        (ends_row <= iota((rows, count), 0)).astype(jnp.int32), axis=1, keepdims=True
    )
    allowed = (seg_row == seg_col) & (iota((rows, rows), 0) <= iota((rows, rows), 1))
    bias_ref[...] = jnp.where(allowed, 0.0, masked_score)


def fill_small(small_ref, shard, pieces, first_row):
    for offset, piece in enumerate(pieces):
        small_ref[shard ^ offset] = piece[first_row:, :].astype(wide)


def fill_cols(full_ref, shard, pieces, first_row, rows, width):
    blocks = full_ref.shape[1] // width
    for offset, piece in enumerate(pieces):
        at = pl.multiple_of((shard ^ offset) * rows, rows)
        for block in range(blocks):
            start = first_row + block * rows
            full_ref[pl.ds(at, rows), block * width : (block + 1) * width] = piece[
                start : start + rows, :
            ]


def head_mask(head):
    lane = iota((1, LANES), 1)
    first = head * HEAD % LANES
    return ((lane >= first) & (lane < first + HEAD)).astype(wide).astype(low)


def head_tile(head):
    first = head * HEAD // LANES * LANES
    return slice(first, first + LANES)


def query_blocks(rows):
    size = min(256, rows)
    return [(at, at + size) for at in range(0, rows, size)]


def put_blocks(target, row, source, width):
    rows = source.shape[0]
    for block in range(source.shape[1] // width):
        cols = slice(block * width, (block + 1) * width)
        target[row : row + rows, :] = source[:, cols].astype(low)
        row += rows
    return row


def pack_first_kernel(qkv_ref, small_ref, first_ref):
    width = first_ref.shape[1]
    row = put_blocks(first_ref, 0, qkv_ref, width)
    parts = [
        small_ref[block * width : (block + 1) * width].reshape(1, width)
        for block in range(small_ref.shape[0] // width)
    ]
    parts.append(jnp.zeros((SMALL_PAD - len(parts), width), wide))
    first_ref[row:, :] = jnp.concatenate(parts, axis=0).astype(low)


def pack_second_kernel(out_ref, up_ref, down_ref, second_ref):
    width = second_ref.shape[1]
    row = put_blocks(second_ref, 0, out_ref, width)
    row = put_blocks(second_ref, row, up_ref, width)
    put_blocks(second_ref, row, down_ref, width)


def attend_kernel(shards, ids, *refs):
    x_ref, len_ref, owner_ref = refs[:3]
    pieces = refs[3 : 3 + shards]
    joined_ref, out_ref, log_ref, weight_ref, small_ref, bias_ref, att_ref = refs[3 + shards :]
    rows, width = x_ref.shape
    shard = ids[1]
    part = width // shards
    fill_cols(weight_ref, shard, pieces, 0, part, width)
    fill_small(small_ref, shard, pieces, 3 * part)
    gain, shift = small_ref[0, 0:1, :], small_ref[0, 1:2, :]
    bias_query, bias_value = small_ref[1, 1:2, :], small_ref[1, 2:3, :]
    fill_mask(bias_ref, own_row(len_ref[...], owner_ref[...], ids[0]), rows)
    normed, _ = standardize(x_ref[...].astype(wide))
    hidden = (normed * gain + shift).astype(low)
    for block, bias in enumerate((bias_query, None, bias_value)):
        cols = slice(block * width, (block + 1) * width)
        value = dot_nn(hidden, weight_ref[:, cols])
        if bias is not None:
            value = value + bias
        joined_ref[:, cols] = value.astype(low)
    values_t = joined_ref[:, 2 * width :].T
    for head in range(width // HEAD):
        tile = head_tile(head)
        key_tile = joined_ref[:, width + tile.start : width + tile.stop] * head_mask(head)
        feature = slice(head * HEAD, (head + 1) * HEAD)
        for start, stop in query_blocks(rows):
            scores = dot_nt(key_tile[:stop], joined_ref[start:stop, tile])
            scores = scores * (score_scale * log2_e) + bias_ref[:stop, start:stop]
            top = jnp.max(scores, axis=0, keepdims=True)
            exponent = jnp.exp2(scores - top)
            total = jnp.sum(exponent, axis=0, keepdims=True)
            probs = (exponent * (1.0 / total)).astype(low)
            att_ref[feature, start:stop] = dot_nn(values_t[feature, :stop], probs).astype(low)
            log_ref[head : head + 1, start:stop] = top + jnp.log2(total)
    out_ref[...] = att_ref[...].T


def feed_kernel(shards, ids, *refs):
    x_ref, att_ref, seed_ref, len_ref, owner_ref = refs[:5]
    firsts = refs[5 : 5 + shards]
    pieces = refs[5 + shards : 5 + 2 * shards]
    refs = refs[5 + 2 * shards :]
    out_ref, middle_ref, dattend_ref, sums_ref, keep_ref = refs[:5]
    sends = refs[5 : 4 + shards]
    small_ref, out_w, up_w, down_w, grads_ref = refs[4 + shards :]
    rows, width = x_ref.shape
    hidden_count = up_w.shape[1]
    shard = ids[1]
    part = width // shards
    blocks = hidden_count // width
    down_part = hidden_count // shards
    fill_small(small_ref, shard, firsts, 3 * part)
    fill_cols(out_w, shard, pieces, 0, part, width)
    fill_cols(up_w, shard, pieces, part, part, width)
    fill_cols(down_w, shard, pieces, part + blocks * part, down_part, width)
    gain, shift = small_ref[0, 2:3, :], small_ref[1, 0:1, :]
    bias_out, bias_down = small_ref[2, 0:1, :], small_ref[2, 1:2, :]
    bias_up = [small_ref[2, 2:3, :]] + [small_ref[3, row : row + 1, :] for row in range(3)]
    live = jnp.sum(own_row(len_ref[...], owner_ref[...], ids[0]), axis=1, keepdims=True)
    live_rows = (iota((rows, 1), 0) < live).astype(wide)
    seed = seed_ref[...].astype(wide) * live_rows
    seed_low = seed.astype(low)
    attended = att_ref[...]
    middle = x_ref[...].astype(wide) + (dot_nn(attended, out_w[...]) + bias_out)
    normed, root = standardize(middle)
    hidden = (normed * gain + shift).astype(low)
    hidden_t = hidden.T
    result = middle + bias_down
    dhidden = jnp.zeros((rows, width), wide)
    sums_ref[...] = jnp.zeros(sums_ref.shape, wide)
    for block in range(blocks):
        cols = slice(block * width, (block + 1) * width)
        pre = dot_nn(hidden, up_w[:, cols]) + bias_up[block]
        square = pre * pre
        bend = jnp.tanh(tanh_scale * (pre + cubic * (pre * square)))
        half = 0.5 * (1.0 + bend)
        act = (pre * half).astype(low)
        slope = half + (0.5 * tanh_scale) * pre * (1.0 - bend * bend) * (
            1.0 + (3.0 * cubic) * square
        )
        dpre = (dot_nt(seed_low, down_w[cols, :]) * slope).astype(low)
        result = result + dot_nn(act, down_w[cols, :])
        dhidden = dhidden + dot_nt(dpre, up_w[:, cols])
        grad_down = dot_nn(act.T, seed_low)
        grad_up = dot_nn(hidden_t, dpre)
        for piece in range(width // down_part):
            target = block * (width // down_part) + piece
            at = part + blocks * part
            grads_ref[target, at : at + down_part, :] = grad_down[
                piece * down_part : (piece + 1) * down_part, :
            ]
        for target in range(shards):
            at = part + block * part
            grads_ref[target, at : at + part, :] = grad_up[target * part : (target + 1) * part, :]
        sums_ref[4 + block : 5 + block, :] = jnp.sum(dpre.astype(wide), axis=0, keepdims=True)
    out_ref[...] = result.astype(low)
    through, gain_grad, shift_grad = norm_back(dhidden, normed, root, gain)
    dmiddle = seed + through
    middle_ref[...] = dmiddle
    dmiddle_low = dmiddle.astype(low)
    grad_out = dot_nn(attended.T, dmiddle_low)
    for target in range(shards):
        grads_ref[target, :part, :] = grad_out[target * part : (target + 1) * part, :]
    dattend_ref[...] = dot_nt(dmiddle_low, out_w[...]).astype(low)
    sums_ref[0:1, :] = gain_grad
    sums_ref[1:2, :] = shift_grad
    sums_ref[2:3, :] = jnp.sum(dmiddle_low.astype(wide), axis=0, keepdims=True)
    sums_ref[3:4, :] = jnp.sum(seed_low.astype(wide), axis=0, keepdims=True)
    keep_ref[...] = grads_ref[shard]
    for offset in range(1, shards):
        sends[offset - 1][...] = grads_ref[shard ^ offset].astype(low)


def attend_back_kernel(shards, ids, *refs):
    x_ref, joined_ref, dattend_ref, log_ref, middle_ref, sums_in, len_ref, owner_ref = refs[:8]
    pieces = refs[8 : 8 + shards]
    refs = refs[8 + shards :]
    dx_ref, keep_ref = refs[:2]
    sends = refs[2 : 1 + shards]
    weight_ref, small_ref, bias_ref, dquery_t, dkey, dvalue, djoined, grads_ref = refs[1 + shards :]
    rows, width = x_ref.shape
    shard = ids[1]
    part = width // shards
    fill_cols(weight_ref, shard, pieces, 0, part, width)
    fill_small(small_ref, shard, pieces, 3 * part)
    gain, shift = small_ref[0, 0:1, :], small_ref[0, 1:2, :]
    fill_mask(bias_ref, own_row(len_ref[...], owner_ref[...], ids[0]), rows)
    keys_t = joined_ref[:, width : 2 * width].T
    dkey[...] = jnp.zeros(dkey.shape, wide)
    dvalue[...] = jnp.zeros(dvalue.shape, wide)
    for head in range(width // HEAD):
        tile = head_tile(head)
        mask = head_mask(head)
        key_tile = joined_ref[:, width + tile.start : width + tile.stop] * mask
        value_tile = joined_ref[:, 2 * width + tile.start : 2 * width + tile.stop] * mask
        feature = slice(head * HEAD, (head + 1) * HEAD)
        for start, stop in query_blocks(rows):
            query = joined_ref[start:stop, tile]
            datt = dattend_ref[start:stop, tile]
            scores = dot_nt(key_tile[:stop], query)
            scores = scores * (score_scale * log2_e) + bias_ref[:stop, start:stop]
            probs = jnp.exp2(scores - log_ref[head : head + 1, start:stop])
            dprobs = dot_nt(value_tile[:stop], datt)
            weighted = jnp.sum(probs * dprobs, axis=0, keepdims=True)
            dscores = (probs * (dprobs - weighted)).astype(low)
            dquery_t[feature, start:stop] = (
                dot_nn(keys_t[feature, :stop], dscores) * score_scale
            ).astype(low)
            dvalue[:stop, tile] += dot_nn(probs.astype(low), datt * mask)
            dkey[:stop, tile] += dot_nn(dscores, query * mask)
    djoined[:, :width] = dquery_t[...].T
    djoined[:, width : 2 * width] = (dkey[...] * score_scale).astype(low)
    djoined[:, 2 * width :] = dvalue[...].astype(low)
    normed, root = standardize(x_ref[...].astype(wide))
    hidden_t = (normed * gain + shift).astype(low).T
    dhidden = jnp.zeros((rows, width), wide)
    bias_sums = []
    for block in range(3):
        cols = slice(block * width, (block + 1) * width)
        piece = djoined[:, cols]
        dhidden = dhidden + dot_nt(piece, weight_ref[:, cols])
        grad = dot_nn(hidden_t, piece)
        for target in range(shards):
            grads_ref[target, block * part : (block + 1) * part, :] = grad[
                target * part : (target + 1) * part, :
            ]
        if block != 1:
            bias_sums.append(jnp.sum(piece.astype(wide), axis=0, keepdims=True))
    through, gain_grad, shift_grad = norm_back(dhidden, normed, root, gain)
    dx_ref[...] = middle_ref[...] + through
    sums = [gain_grad, shift_grad, sums_in[0:1, :], sums_in[1:2, :]] + bias_sums
    sums += [sums_in[row : row + 1, :] for row in range(2, 8)]
    per_shard = len(sums) // shards
    for target in range(shards):
        at = 3 * part
        grads_ref[target, at:, :] = jnp.zeros((grads_ref.shape[1] - at, width), wide)
        for row in range(per_shard):
            grads_ref[target, at + row * TILE_ROWS : at + row * TILE_ROWS + 1, :] = sums[
                target * per_shard + row
            ]
    keep_ref[...] = grads_ref[shard]
    for offset in range(1, shards):
        sends[offset - 1][...] = grads_ref[shard ^ offset].astype(low)


def piece_spans(total, tail, group):
    spans = [((total - tail) // group, 0)]
    if tail:
        spans.append((tail // group, total - tail))
    return spans


def split_kernel(shards, tails, *refs):
    pieces_ref = refs[-1]
    group = pieces_ref.shape[0]
    column = 0
    for chunk, tail in enumerate(tails):
        arrived = refs[chunk * shards : (chunk + 1) * shards]
        count = arrived[0].shape[0]
        for rows, first in piece_spans(count, tail, group):
            for index in range(group):
                at = first + index * rows
                total = arrived[0][at : at + rows, :]
                for piece in arrived[1:]:
                    total = total + piece[at : at + rows, :].astype(wide)
                pieces_ref[index, column : column + rows, :] = total.astype(low)
            column += rows


def piece_kernel(arrived_ref, sent_ref):
    total = arrived_ref[0].astype(wide)
    for index in range(1, arrived_ref.shape[0]):
        total = total + arrived_ref[index].astype(wide)
    for index in range(sent_ref.shape[0]):
        sent_ref[index] = total.astype(low)


def add_kernel(mine_ref, other_ref, sent_ref):
    total = (mine_ref[0].astype(wide) + other_ref[...].astype(wide)).astype(low)
    for index in range(sent_ref.shape[0]):
        sent_ref[index] = total


def adam_values(weight, grad, first, second, decay_rate):
    first_next = beta_one * first + (1.0 - beta_one) * grad
    second_next = beta_two * second + (1.0 - beta_two) * grad * grad
    first_fix = 1.0 - beta_one**STEP
    second_fix = 1.0 - beta_two**STEP
    update = (first_next * (1.0 / first_fix)) / (
        jnp.sqrt(second_next * (1.0 / second_fix)) + adam_eps
    )
    return first_next, second_next, weight - learn_rate * (update + decay_rate * weight)


def adam_kernel(spans, layout, *refs):
    pieces_ref = refs[0]
    grad_ref = refs[-1]
    count = len(layout)
    states = refs[1 : 1 + 3 * count]
    results = refs[1 + 3 * count : -1]
    for index in range(pieces_ref.shape[0]):
        value = pieces_ref[index].astype(wide)
        for rows, first, row in spans:
            at = first + index * rows
            grad_ref[at : at + rows, :] = value[row : row + rows, :]
    width = grad_ref.shape[1]
    for array, (first_row, stride, decay) in enumerate(layout):
        weight, first, second = states[3 * array : 3 * array + 3]
        new = results[3 * array : 3 * array + 3]
        vector = len(weight.shape) == 1
        rows = 1 if vector else weight.shape[0]
        for block in range(weight.shape[-1] // width):
            cols = slice(block * width, (block + 1) * width)
            where = cols if vector else (slice(None), cols)
            at = first_row + block * stride
            values = adam_values(
                weight[where].reshape(rows, width),
                grad_ref[at : at + rows, :],
                first[where].reshape(rows, width),
                second[where].reshape(rows, width),
                decay,
            )
            for target, value in zip(new, values):
                target[where] = value.reshape(width) if vector else value


def local_call(kernel, outs, operands, scratch=(), ids=None, flops=0, name=None):
    specs = [pl.BlockSpec(memory_space=pltpu.VMEM)] * len(operands)
    if ids is not None:
        operands = [ids] + list(operands)
        specs = [pl.BlockSpec(memory_space=pltpu.SMEM)] + specs
    outs = [jax.ShapeDtypeStruct(*out) for out in outs]
    moved = sum(
        math.prod(item.shape) * item.dtype.itemsize for item in list(operands) + outs
    )
    return pl.pallas_call(
        kernel,
        out_shape=outs,
        in_specs=specs,
        out_specs=[pl.BlockSpec(memory_space=pltpu.VMEM)] * len(outs),
        scratch_shapes=[pltpu.VMEM(*item) for item in scratch],
        compiler_params=pltpu.CompilerParams(vmem_limit_bytes=40 * 1024 * 1024),
        cost_estimate=pl.CostEstimate(flops=flops, bytes_accessed=moved, transcendentals=0),
        name=name,
    )(*operands)


def exchange(values, axis, mask):
    count = lax.axis_size(axis)
    return lax.ppermute(values, axis, [(index, index ^ mask) for index in range(count)])


def gather_shards(value, shards):
    found = {0: value}
    far = shards // 2
    while far:
        for offset in sorted(found):
            found[offset ^ far] = exchange(found[offset], "shard", far)
        far //= 2
    return [found[offset] for offset in range(shards)]


def swap_all(values, axis):
    return [exchange(value, axis, offset + 1) for offset, value in enumerate(values)]


def swap_pieces(pieces, group):
    replicas = lax.axis_size("dp")
    groups = None
    if replicas > group:
        groups = [list(range(at, at + group)) for at in range(0, replicas, group)]
    return lax.all_to_all(pieces, "dp", 0, 0, axis_index_groups=groups, tiled=True)


def reduce_replicas(chunks, tails, shards):
    replicas = lax.axis_size("dp")
    group = min(GROUP, replicas)
    width = chunks[0][0].shape[1]
    rows = sum(chunk[0].shape[0] for chunk in chunks) // group
    shape = (group, rows, width)
    (pieces,) = local_call(
        functools.partial(split_kernel, shards, tails),
        [(shape, low)],
        [piece for chunk in chunks for piece in chunk],
        name="split_sum",
    )
    (copies,) = local_call(
        piece_kernel, [(shape, low)], [swap_pieces(pieces, group)], name="piece_sum"
    )
    mask = group
    while mask < replicas:
        other = exchange(copies[0], "dp", mask)
        (copies,) = local_call(add_kernel, [(shape, low)], [copies, other], name="far_sum")
        mask *= 2
    return swap_pieces(copies, group)


def adam_call(pieces, counts, tails, states, layout):
    group, _, width = pieces.shape
    spans = []
    first = row = 0
    for total, tail in zip(counts, tails):
        for rows, start in piece_spans(total, tail, group):
            spans.append((rows, first + start, row))
            row += rows
        first += total
    return local_call(
        functools.partial(adam_kernel, spans, layout),
        [(state[0].shape, wide) for state in states for _ in range(3)],
        [pieces] + [item for state in states for item in state],
        [((first, width), wide)],
        name="adam",
    )


def shards_program(
    tokens,
    cotangent,
    lengths,
    seq_owner,
    qkv_weight,
    out_weight,
    up_weight,
    down_weight,
    gains_biases,
    qkv_first,
    qkv_second,
    out_first,
    out_second,
    up_first,
    up_second,
    down_first,
    down_second,
    small_first,
    small_second,
):
    rows, width = tokens.shape
    shards = lax.axis_size("shard")
    heads = width // HEAD
    part = qkv_weight.shape[0]
    hidden_count = up_weight.shape[1]
    device = lax.axis_index(("dp", "shard"))
    ids = jnp.stack([device, lax.axis_index("shard")]).astype(jnp.int32)
    lengths = lengths.reshape(1, -1)
    seq_owner = seq_owner.reshape(1, -1)
    first_rows = 3 * part + SMALL_PAD
    second_rows = part + up_weight.size // width + down_weight.shape[0]
    (first_pack,) = local_call(
        pack_first_kernel,
        [((first_rows, width), low)],
        [qkv_weight, gains_biases],
        name="pack_first",
    )
    firsts = gather_shards(first_pack, shards)
    (second_pack,) = local_call(
        pack_second_kernel,
        [((second_rows, width), low)],
        [out_weight, up_weight, down_weight],
        name="pack_second",
    )
    firsts, second_pack = lax.optimization_barrier((firsts, second_pack))
    seconds = {0: second_pack}
    seconds[2] = exchange(second_pack, "shard", 2)
    seconds[1] = exchange(second_pack, "shard", 1)
    square = (rows, rows)
    joined, attended, log_sums = local_call(
        functools.partial(attend_kernel, shards),
        [((rows, 3 * width), low), ((rows, width), low), ((heads, rows), wide)],
        [tokens, lengths, seq_owner] + firsts,
        [
            ((width, 3 * width), low),
            ((shards, SMALL_PAD, width), wide),
            (square, wide),
            ((width, rows), low),
        ],
        ids,
        flops=heads * rows * rows * 256 * 4,
        name="attend",
    )
    attended, seconds[2] = lax.optimization_barrier((attended, seconds[2]))
    seconds[3] = exchange(seconds[2], "shard", 1)
    seconds = [seconds[offset] for offset in range(shards)]
    output, middle_grad, attended_grad, sums, keep_ffn, *sends_ffn = local_call(
        functools.partial(feed_kernel, shards),
        [
            ((rows, width), low),
            ((rows, width), wide),
            ((rows, width), low),
            ((SMALL_PAD, width), wide),
            ((second_rows, width), wide),
        ]
        + [((second_rows, width), low)] * (shards - 1),
        [tokens, attended, cotangent, lengths, seq_owner] + firsts + seconds,
        [
            ((shards, SMALL_PAD, width), wide),
            ((width, width), low),
            ((width, hidden_count), low),
            ((hidden_count, width), low),
            ((shards, second_rows, width), wide),
        ],
        ids,
        flops=rows * width * (hidden_count * 12 + width * 6),
        name="feed",
    )
    arrived_ffn = swap_all(sends_ffn, "shard")
    tail = GROUP * TILE_ROWS
    att_rows = 3 * part + tail
    input_grad, keep_att, *sends_att = local_call(
        functools.partial(attend_back_kernel, shards),
        [((rows, width), wide), ((att_rows, width), wide)]
        + [((att_rows, width), low)] * (shards - 1),
        [tokens, joined, attended_grad, log_sums, middle_grad, sums, lengths, seq_owner] + firsts,
        [
            ((width, 3 * width), low),
            ((shards, SMALL_PAD, width), wide),
            (square, wide),
            ((width, rows), low),
            ((rows, width), wide),
            ((rows, width), wide),
            ((rows, 3 * width), low),
            ((shards, att_rows, width), wide),
        ],
        ids,
        flops=heads * rows * rows * 256 * 10,
        name="attend_back",
    )
    arrived_att = swap_all(sends_att, "shard")
    tails = (0, tail)
    pieces = reduce_replicas(
        [[keep_ffn] + arrived_ffn, [keep_att] + arrived_att], tails, shards
    )
    blocks = hidden_count // width
    results = adam_call(
        pieces,
        (second_rows, att_rows),
        tails,
        [
            (qkv_weight, qkv_first, qkv_second),
            (out_weight, out_first, out_second),
            (up_weight, up_first, up_second),
            (down_weight, down_first, down_second),
            (gains_biases, small_first, small_second),
        ],
        [
            (second_rows, part, matrix_decay),
            (0, part, matrix_decay),
            (part, part, matrix_decay),
            (part + blocks * part, 0, matrix_decay),
            (second_rows + 3 * part, TILE_ROWS, 0.0),
        ],
    )
    return (output, input_grad, *results)


def solution(mesh):
    rows = P(("dp", "shard"), None)
    matrix = P("shard", None)
    vector = P("shard")
    return jax.shard_map(
        shards_program,
        mesh=mesh,
        in_specs=(rows, rows, P(), P())
        + (matrix,) * 4
        + (vector,)
        + (matrix,) * 8
        + (vector, vector),
        out_specs=(rows, rows) + (matrix,) * 12 + (vector,) * 3,
        check_vma=False,
    )
```

time: 266 us -> 84.6 us (0.32)
  waiting for transfers between devices: 105 us -> 11.7 us
  matrix products: 33.5 us -> 0 us
  blocking collectives: 66.1 us -> 35.1 us
  other arithmetic: 23.5 us -> 0.07 us
  Pallas kernels: 0 us -> 22.1 us
  local copies, waits for them, and re-layouts: 21.1 us -> 4.19 us
  between operations: 15.3 us -> 0.96 us
  starting transfers between devices: 0.39 us -> 10.1 us
    reduce_scatter x4 -> x0, waiting for transfers between devices: 63.8 us -> none  [the longest x1 27.5 us: shards(): lax.psum_scatter(grad_down, 'shard', scatter_dimension=0, tiled=True)]
    psum x1 -> x0, waiting for transfers between devices: 40.8 us -> none  [shards(): lax.psum((local_sums[0], local_sums[1], local_sums[2], local_sums[3], loc...]
    all_to_all x0 -> x2, blocking collectives: none -> 35.1 us  [swap_pieces(): lax.all_to_all(pieces, 'dp', 0, 0, axis_index_groups=groups, tiled=True)]
    all_gather x5 -> x0, blocking collectives: 33.5 us -> none  [the longest x1 7.72 us: shards(): lax.all_gather(weight_pieces[3], 'shard', axis=0, tiled=True)]
    dot_general x18 -> x0, matrix products: 33.5 us -> none  [the longest x4 8.28 us: contract_rows(): lax.dot_general(left, right, (((0,), (0,)), ((), ())), preferred_element_...]
    pallas_call x0 -> x8, Pallas kernels: none -> 22.1 us  [local_call(): pl.pallas_call(kernel, out_shape=outs, in_specs=specs, out_specs=[pl.Bloc...]
    psum x1 -> x0, blocking collectives: 21.5 us -> none  [shards(): lax.psum((local_sums[0], local_sums[1], local_sums[2], local_sums[3], loc...]
    unnamed x123 -> x46, local copies, waits for them, and re-layouts: 16.8 us -> 4.19 us
  transfers between devices with their start and end apart: 5 -> 12, of which waited for: 4 -> 5; matrix products, arithmetic and copies ran while one was open for 16% -> 0% of each run, Pallas kernels for 0% -> 18%
where the time goes in v2:
time: 84.6 us; the launch traced here: 84.3 us
  blocking collectives  35.1 us (41%)
  Pallas kernels  22.1 us (26%)
  waiting for transfers between devices  11.7 us (14%)
  starting transfers between devices  10.1 us (12%)
  local copies, waits for them, and re-layouts  4.19 us (5%)
  between operations  0.96 us (1%)
    all_to_all x2, blocking collectives, swap_pieces(): lax.all_to_all(pieces, 'dp', 0, 0, axis_index_groups=groups, tiled=True)  35.1 us
    pallas_call x8, Pallas kernels, local_call(): pl.pallas_call(kernel, out_shape=outs, in_specs=specs, out_specs=[pl.Bloc...  22.1 us
    ppermute x12, waiting for transfers between devices, exchange(): lax.ppermute(values, axis, [(index, index ^ mask) for index in range(coun...  11.7 us
    ppermute x12, starting transfers between devices, exchange(): lax.ppermute(values, axis, [(index, index ^ mask) for index in range(coun...  10.1 us
    unnamed x46, local copies, waits for them, and re-layouts  4.19 us
  transfers between devices with their start and end apart: 12, of which 5 were waited for; matrix products, arithmetic and copies ran while one was open for 0% of the time, Pallas kernels for 18%

profile of v2, /device:TPU:0, one launch (start us, length us, event | category | flops | bytes accessed | tf_op | source)
XLA Modules:
  0.0 84.3 jit_solution(66909221163953570)
XLA Ops:
  0.7 0.0 copy-start.3
  0.7 1.0 %copy-done.3 = f32[64,768]{1,0:T(8,128)S(1)} copy-done((f32[64,768]{1,0:T(8,128)S(1)}, f32[64,768]{1,0:T(8,128)}, u32[]{:S(2)}) %copy-start.3) | copy-done | bytes 196632
  1.6 0.7 copy-done.15
  2.3 3.0 %collective-permute-start.1 = (bf16[208,256]{1,0:T(8,128)(2,1)S(1)}, bf16[208,256]{1,0:T(8,128)(2,1)S(1)}, u32[]{:S(2)}, u32[]{:S(2)}) collective-permute-start(bf16[208,256]{1,0:T(8,128)(2,1)S(1)} %pack_first.1.refs_3_.refs_5_.refs_8_), channel_id=1, source_target_pairs={{0,2},{1,3},{2,0},{3,1},{4,6},{5,7},{6,4},{7,5},{8,10},{9,11},{10,... | collective-permute-start | bytes 319496 | tf_op jit(solution)/shard_map/ppermute | solution.py:441
  5.4 0.0 collective-permute-start
  5.4 3.0 %collective-permute-done.1.refs_5_.refs_7_.refs_10_ = bf16[208,256]{1,0:T(8,128)(2,1)S(1)} collective-permute-done((bf16[208,256]{1,0:T(8,128)(2,1)S(1)}, bf16[208,256]{1,0:T(8,128)(2,1)S(1)}, u32[]{:S(2)}, u32[]{:S(2)}) %collective-permute-start.1) | collective-permute-done | bytes 106528 | tf_op jit(solution)/shard_map/ppermute | solution.py:441
  8.3 0.0 collective-permute-start.2
  8.4 0.9 %copy-done.1 = f32[256,256]{1,0:T(8,128)S(1)} copy-done((f32[256,256]{1,0:T(8,128)S(1)}, f32[256,256]{1,0:T(8,128)}, u32[]{:S(2)}) %copy-start.1) | copy-done | bytes 262168
  9.3 0.8 copy-done.5
  10.2 0.0 collective-permute-done.refs_4_.refs_6_.refs_9_
  10.2 0.0 collective-permute-done.2.refs_6_.refs_8_.refs_11_
  10.2 1.8 %collective-permute-start.3 = (bf16[576,256]{1,0:T(8,128)(2,1)S(1)}, bf16[576,256]{1,0:T(8,128)(2,1)S(1)}, u32[]{:S(2)}, u32[]{:S(2)}) collective-permute-start(bf16[576,256]{1,0:T(8,128)(2,1)S(1)} %pack_second.1.refs_9_), channel_id=1, source_target_pairs={{0,2},{1,3},{2,0},{3,1},{4,6},{5,7},{6,4},{7,5},{8,10},{9,11},{10,... | collective-permute-start | bytes 884744 | tf_op jit(solution)/shard_map/ppermute | solution.py:441
  12.0 0.1 pad_add_fusion.ids
  12.1 0.2 collective-permute-start.4
  12.3 0.6 copy-done.21
  13.0 0.0 copy-done.22
  13.0 5.9 %attend.1 = (bf16[512,768]{1,0:T(8,128)(2,1)S(1)}, bf16[512,256]{1,0:T(8,128)(2,1)S(1)}, f32[8,512]{1,0:T(8,128)S(1)}) custom-call(s32[2]{0:T(128)S(1)} %pad_add_fusion.ids, bf16[512,256]{1,0:T(8,128)(2,1)S(1)} %copy-done.20, s32[1,128]{1,0:T(1,128)S(1)} %bitcast.4, s32[1,128]{1,0:T(1,128)S(1)} %bitcast.7, ...), custom_call_target="tpu_custom_call" | custom-call | flops 2147483648 | bytes 1754120 | tf_op jit(solution)/shard_map/attend/pallas_call | solution.py:427
  18.9 0.8 collective-permute-done.3.refs_11_
  19.7 0.0 collective-permute-start.5
  19.7 0.0 collective-permute-done.4.refs_10_
  19.7 1.6 %collective-permute-done.5.refs_12_ = bf16[576,256]{1,0:T(8,128)(2,1)S(1)} collective-permute-done((bf16[576,256]{1,0:T(8,128)(2,1)S(1)}, bf16[576,256]{1,0:T(8,128)(2,1)S(1)}, u32[]{:S(2)}, u32[]{:S(2)}) %collective-permute-start.5) | collective-permute-done | bytes 294944 | tf_op jit(solution)/shard_map/ppermute | solution.py:441
  21.3 4.7 %feed.1 = (bf16[512,256]{1,0:T(8,128)(2,1)}, f32[512,256]{1,0:T(8,128)S(1)}, bf16[512,256]{1,0:T(8,128)(2,1)S(1)}, f32[16,256]{1,0:T(8,128)S(1)}, f32[576,256]{1...) custom-call(s32[2]{0:T(128)S(1)} %pad_add_fusion.ids, ...), custom_call_target="tpu_custom_call" | custom-call | flops 1811939328 | bytes 4932616 | tf_op jit(solution)/shard_map/feed/pallas_call | solution.py:427
  26.0 0.1 collective-permute-start.6
  26.1 1.8 %collective-permute-start.7 = (bf16[576,256]{1,0:T(8,128)(2,1)S(1)}, bf16[576,256]{1,0:T(8,128)(2,1)S(1)}, u32[]{:S(2)}, u32[]{:S(2)}) collective-permute-start(bf16[576,256]{1,0:T(8,128)(2,1)S(1)} %get-tuple-element.72), channel_id=1, source_target_pairs={{0,2},{1,3},{2,0},{3,1},{4,6},{5,7},{6,4},{7,5},{8,10},{9,11},{10,... | collective-permute-start | bytes 884744 | tf_op jit(solution)/shard_map/ppermute | solution.py:441
  27.9 0.0 collective-permute-start.8
  27.9 9.4 %attend_back.1 = (f32[512,256]{1,0:T(8,128)}, f32[256,256]{1,0:T(8,128)S(1)}, bf16[256,256]{1,0:T(8,128)(2,1)S(1)}, bf16[256,256]{1,0:T(8,128)(2,1)S(1)}, bf16[256,256]{1,0:T(8,128)(2,1)S(1)}) custom-call(s32[2]{0:T(128)S(1)} %pad_add_fusion.ids, bf16[512,256]{1,0:T(8,128)(2,1)S(1)} %copy-done.20, bf16[512,768]{1,0:T(8,128)(2,1)S(1)} %get-tuple-element.64.refs_1_, ...), custom_call_target="tpu_custom_call" | custom-call | flops 5368709120 | bytes 3474440 | tf_op jit(solution)/shard_map/attend_back/pallas_call | solution.py:427
  37.3 0.4 collective-permute-start.9
  37.7 1.7 %collective-permute-start.10 = (bf16[256,256]{1,0:T(8,128)(2,1)S(1)}, bf16[256,256]{1,0:T(8,128)(2,1)S(1)}, u32[]{:S(2)}, u32[]{:S(2)}) collective-permute-start(bf16[256,256]{1,0:T(8,128)(2,1)S(1)} %get-tuple-element.76), channel_id=1, source_target_pairs={{0,2},{1,3},{2,0},{3,1},{4,6},{5,7},{6,4},{7,5},{8,10},{9,11},{10,... | collective-permute-start | bytes 393224 | tf_op jit(solution)/shard_map/ppermute | solution.py:441
  39.4 0.0 collective-permute-done.9.refs_5_
  39.4 0.9 %collective-permute-start.11 = (bf16[256,256]{1,0:T(8,128)(2,1)S(1)}, bf16[256,256]{1,0:T(8,128)(2,1)S(1)}, u32[]{:S(2)}, u32[]{:S(2)}) collective-permute-start(bf16[256,256]{1,0:T(8,128)(2,1)S(1)} %get-tuple-element.77), channel_id=1, source_target_pairs={{0,3},{1,2},{2,1},{3,0},{4,7},{5,6},{6,5},{7,4},{8,11},{9,10},{10,... | collective-permute-start | bytes 393224 | tf_op jit(solution)/shard_map/ppermute | solution.py:441
  40.4 4.7 %collective-permute-done.10.refs_6_ = bf16[256,256]{1,0:T(8,128)(2,1)S(1)} collective-permute-done((bf16[256,256]{1,0:T(8,128)(2,1)S(1)}, bf16[256,256]{1,0:T(8,128)(2,1)S(1)}, u32[]{:S(2)}, u32[]{:S(2)}) %collective-permute-start.10) | collective-permute-done | bytes 131104 | tf_op jit(solution)/shard_map/ppermute | solution.py:441
  45.1 1.7 %collective-permute-done.11.refs_7_ = bf16[256,256]{1,0:T(8,128)(2,1)S(1)} collective-permute-done((bf16[256,256]{1,0:T(8,128)(2,1)S(1)}, bf16[256,256]{1,0:T(8,128)(2,1)S(1)}, u32[]{:S(2)}, u32[]{:S(2)}) %collective-permute-start.11) | collective-permute-done | bytes 131104 | tf_op jit(solution)/shard_map/ppermute | solution.py:441
  46.8 0.0 collective-permute-done.8.refs_3_
  46.8 0.2 split_sum.1
  47.0 0.0 copy-start.11
  47.0 0.0 copy-start.12
  47.0 0.0 copy-start.16
  47.0 0.0 copy-start.17
  47.0 0.0 copy-start.18
  47.1 19.1 %all_to_all.10.arrived_ref = bf16[8,104,256]{2,1,0:T(8,128)(2,1)S(1)} all-to-all(bf16[8,104,256]{2,1,0:T(8,128)(2,1)S(1)} %split_sum.1), channel_id=1, replica_groups=mesh['dp'=8,'shard'=4] {'dp'}, dimensions={0} | all-to-all | bytes 851968 | tf_op jit(solution)/shard_map/all_to_all | solution.py:463
  66.2 0.1 piece_sum.1
  66.2 0.0 copy-start.2
  66.3 0.0 copy-start.4
  66.3 0.0 copy-start.6
  66.3 0.0 copy-start.7
  66.3 0.0 copy-start.13
  66.3 16.0 %all_to_all.11.refs_0_ = bf16[8,104,256]{2,1,0:T(8,128)(2,1)S(1)} all-to-all(bf16[8,104,256]{2,1,0:T(8,128)(2,1)S(1)} %piece_sum.1), channel_id=1, replica_groups=mesh['dp'=8,'shard'=4] {'dp'}, dimensions={0} | all-to-all | bytes 851968 | tf_op jit(solution)/shard_map/all_to_all | solution.py:463
  82.5 1.8 %adam.1 = (f32[64,768]{1,0:T(8,128)}, f32[64,768]{1,0:T(8,128)}, f32[64,768]{1,0:T(8,128)}, f32[64,256]{1,0:T(8,128)}, f32[64,256]{1,0:T(8,128)}, /*index=5*/f32...) custom-call(bf16[8,104,256]{2,1,0:T(8,128)(2,1)S(1)} %all_to_all.11., ...), custom_call_target="tpu_custom_call" | custom-call | bytes 5163008 | tf_op jit(solution)/shard_map/adam/pallas_call | solution.py:427
  (33 shorter events, 0.1 us)
Async XLA Ops:
  0.7 7.7 %copy-start = (f32[64,1024]{1,0:T(8,128)S(1)}, f32[64,1024]{1,0:T(8,128)}, u32[]{:S(2)}) copy-start(f32[64,1024]{1,0:T(8,128)} %refs_7_.1) | copy-start | bytes 786436
  0.7 1.0 %copy-start.3 = (f32[64,768]{1,0:T(8,128)S(1)}, f32[64,768]{1,0:T(8,128)}, u32[]{:S(2)}) copy-start(f32[64,768]{1,0:T(8,128)} %refs_1_.1) | copy-start | bytes 589828
  1.6 0.7 copy-start.15
  2.3 6.0 %collective-permute-start.1 = (bf16[208,256]{1,0:T(8,128)(2,1)S(1)}, bf16[208,256]{1,0:T(8,128)(2,1)S(1)}, u32[]{:S(2)}, u32[]{:S(2)}) collective-permute-start(bf16[208,256]{1,0:T(8,128)(2,1)S(1)} %pack_first.1.refs_3_.refs_5_.refs_8_), channel_id=1, source_target_pairs={{0,2},{1,3},{2,0},{3,1},{4,6},{5,7},{6,4},{7,5},{8,10},{9,11},{10,... | collective-permute-start | bytes 319496 | tf_op jit(solution)/shard_map/ppermute | solution.py:441
  5.4 4.8 %collective-permute-start = (bf16[208,256]{1,0:T(8,128)(2,1)S(1)}, bf16[208,256]{1,0:T(8,128)(2,1)S(1)}, u32[]{:S(2)}, u32[]{:S(2)}) collective-permute-start(bf16[208,256]{1,0:T(8,128)(2,1)S(1)} %pack_first.1.refs_3_.refs_5_.refs_8_), channel_id=1, source_target_pairs={{0,1},{1,0},{2,3},{3,2},{4,5},{5,4},{6,7},{7,6},{8,9},{9,8},{10,11... | collective-permute-start | bytes 319496 | tf_op jit(solution)/shard_map/ppermute | solution.py:441
  8.3 1.8 %collective-permute-start.2 = (bf16[208,256]{1,0:T(8,128)(2,1)S(1)}, bf16[208,256]{1,0:T(8,128)(2,1)S(1)}, u32[]{:S(2)}, u32[]{:S(2)}) collective-permute-start(bf16[208,256]{1,0:T(8,128)(2,1)S(1)} %collective-permute-done.1.refs_5_.refs_7_.refs_10_), channel_id=1, source_target_pairs={{0,1},{1,0},{2,3},{3,2},{4,5},{5,4},{6,7},{7,6},{8,9},{9,8},{10,11... | collective-permute-start | bytes 319496 | tf_op jit(solution)/shard_map/ppermute | solution.py:441
  8.3 1.0 %copy-start.1 = (f32[256,256]{1,0:T(8,128)S(1)}, f32[256,256]{1,0:T(8,128)}, u32[]{:S(2)}) copy-start(f32[256,256]{1,0:T(8,128)} %refs_10_.1) | copy-start | bytes 786436
  9.3 0.8 copy-start.5
  10.1 2.2 %copy-start.20 = (bf16[512,256]{1,0:T(8,128)(2,1)S(1)}, bf16[512,256]{1,0:T(8,128)(2,1)}, u32[]{:S(2)}) copy-start(bf16[512,256]{1,0:T(8,128)(2,1)} %refs_0_.5) | copy-start | bytes 786436
  10.2 9.5 %collective-permute-start.3 = (bf16[576,256]{1,0:T(8,128)(2,1)S(1)}, bf16[576,256]{1,0:T(8,128)(2,1)S(1)}, u32[]{:S(2)}, u32[]{:S(2)}) collective-permute-start(bf16[576,256]{1,0:T(8,128)(2,1)S(1)} %pack_second.1.refs_9_), channel_id=1, source_target_pairs={{0,2},{1,3},{2,0},{3,1},{4,6},{5,7},{6,4},{7,5},{8,10},{9,11},{10,... | collective-permute-start | bytes 884744 | tf_op jit(solution)/shard_map/ppermute | solution.py:441
  12.1 7.6 %collective-permute-start.4 = (bf16[576,256]{1,0:T(8,128)(2,1)S(1)}, bf16[576,256]{1,0:T(8,128)(2,1)S(1)}, u32[]{:S(2)}, u32[]{:S(2)}) collective-permute-start(bf16[576,256]{1,0:T(8,128)(2,1)S(1)} %pack_second.1.refs_9_), channel_id=1, source_target_pairs={{0,1},{1,0},{2,3},{3,2},{4,5},{5,4},{6,7},{7,6},{8,9},{9,8},{10,11... | collective-permute-start | bytes 884744 | tf_op jit(solution)/shard_map/ppermute | solution.py:441
  12.3 0.7 copy-start.21
  12.3 0.7 copy-start.22
  13.0 8.3 %copy-start.19 = (bf16[512,256]{1,0:T(8,128)(2,1)S(1)}, bf16[512,256]{1,0:T(8,128)(2,1)}, u32[]{:S(2)}) copy-start(bf16[512,256]{1,0:T(8,128)(2,1)} %refs_2_.2) | copy-start | bytes 786436
  19.7 1.6 %collective-permute-start.5 = (bf16[576,256]{1,0:T(8,128)(2,1)S(1)}, bf16[576,256]{1,0:T(8,128)(2,1)S(1)}, u32[]{:S(2)}, u32[]{:S(2)}) collective-permute-start(bf16[576,256]{1,0:T(8,128)(2,1)S(1)} %collective-permute-done.3.refs_11_), channel_id=1, source_target_pairs={{0,1},{1,0},{2,3},{3,2},{4,5},{5,4},{6,7},{7,6},{8,9},{9,8},{10,11... | collective-permute-start | bytes 884744 | tf_op jit(solution)/shard_map/ppermute | solution.py:441
  26.0 20.8 %collective-permute-start.6 = (bf16[576,256]{1,0:T(8,128)(2,1)S(1)}, bf16[576,256]{1,0:T(8,128)(2,1)S(1)}, u32[]{:S(2)}, u32[]{:S(2)}) collective-permute-start(bf16[576,256]{1,0:T(8,128)(2,1)S(1)} %get-tuple-element.71), channel_id=1, source_target_pairs={{0,1},{1,0},{2,3},{3,2},{4,5},{5,4},{6,7},{7,6},{8,9},{9,8},{10,11... | collective-permute-start | bytes 884744 | tf_op jit(solution)/shard_map/ppermute | solution.py:441
  26.1 20.7 %collective-permute-start.7 = (bf16[576,256]{1,0:T(8,128)(2,1)S(1)}, bf16[576,256]{1,0:T(8,128)(2,1)S(1)}, u32[]{:S(2)}, u32[]{:S(2)}) collective-permute-start(bf16[576,256]{1,0:T(8,128)(2,1)S(1)} %get-tuple-element.72), channel_id=1, source_target_pairs={{0,2},{1,3},{2,0},{3,1},{4,6},{5,7},{6,4},{7,5},{8,10},{9,11},{10,... | collective-permute-start | bytes 884744 | tf_op jit(solution)/shard_map/ppermute | solution.py:441
  27.9 18.9 %collective-permute-start.8 = (bf16[576,256]{1,0:T(8,128)(2,1)S(1)}, bf16[576,256]{1,0:T(8,128)(2,1)S(1)}, u32[]{:S(2)}, u32[]{:S(2)}) collective-permute-start(bf16[576,256]{1,0:T(8,128)(2,1)S(1)} %get-tuple-element.73), channel_id=1, source_target_pairs={{0,3},{1,2},{2,1},{3,0},{4,7},{5,6},{6,5},{7,4},{8,11},{9,10},{10,... | collective-permute-start | bytes 884744 | tf_op jit(solution)/shard_map/ppermute | solution.py:441
  37.3 2.1 %collective-permute-start.9 = (bf16[256,256]{1,0:T(8,128)(2,1)S(1)}, bf16[256,256]{1,0:T(8,128)(2,1)S(1)}, u32[]{:S(2)}, u32[]{:S(2)}) collective-permute-start(bf16[256,256]{1,0:T(8,128)(2,1)S(1)} %get-tuple-element.75), channel_id=1, source_target_pairs={{0,1},{1,0},{2,3},{3,2},{4,5},{5,4},{6,7},{7,6},{8,9},{9,8},{10,11... | collective-permute-start | bytes 393224 | tf_op jit(solution)/shard_map/ppermute | solution.py:441
  37.7 7.4 %collective-permute-start.10 = (bf16[256,256]{1,0:T(8,128)(2,1)S(1)}, bf16[256,256]{1,0:T(8,128)(2,1)S(1)}, u32[]{:S(2)}, u32[]{:S(2)}) collective-permute-start(bf16[256,256]{1,0:T(8,128)(2,1)S(1)} %get-tuple-element.76), channel_id=1, source_target_pairs={{0,2},{1,3},{2,0},{3,1},{4,6},{5,7},{6,4},{7,5},{8,10},{9,11},{10,... | collective-permute-start | bytes 393224 | tf_op jit(solution)/shard_map/ppermute | solution.py:441
  39.4 7.4 %collective-permute-start.11 = (bf16[256,256]{1,0:T(8,128)(2,1)S(1)}, bf16[256,256]{1,0:T(8,128)(2,1)S(1)}, u32[]{:S(2)}, u32[]{:S(2)}) collective-permute-start(bf16[256,256]{1,0:T(8,128)(2,1)S(1)} %get-tuple-element.77), channel_id=1, source_target_pairs={{0,3},{1,2},{2,1},{3,0},{4,7},{5,6},{6,5},{7,4},{8,11},{9,10},{10,... | collective-permute-start | bytes 393224 | tf_op jit(solution)/shard_map/ppermute | solution.py:441
  47.0 35.3 %copy-start.11 = (f32[64,768]{1,0:T(8,128)S(1)}, f32[64,768]{1,0:T(8,128)}, u32[]{:S(2)}) copy-start(f32[64,768]{1,0:T(8,128)} %refs_2_.3) | copy-start | bytes 589828
  47.0 35.3 %copy-start.12 = (f32[64,768]{1,0:T(8,128)S(1)}, f32[64,768]{1,0:T(8,128)}, u32[]{:S(2)}) copy-start(f32[64,768]{1,0:T(8,128)} %refs_3_.1) | copy-start | bytes 589828
  47.0 35.3 %copy-start.16 = (f32[768]{0:T(1024)S(1)}, f32[768]{0:T(1024)}, u32[]{:S(2)}) copy-start(f32[768]{0:T(1024)} %refs_13_.1) | copy-start | bytes 9220
  47.0 35.3 %copy-start.17 = (f32[768]{0:T(1024)S(1)}, f32[768]{0:T(1024)}, u32[]{:S(2)}) copy-start(f32[768]{0:T(1024)} %refs_14_.1) | copy-start | bytes 9220
  47.0 35.3 %copy-start.18 = (f32[768]{0:T(1024)S(1)}, f32[768]{0:T(1024)}, u32[]{:S(2)}) copy-start(f32[768]{0:T(1024)} %refs_15_.1) | copy-start | bytes 9220
  66.2 16.2 %copy-start.8 = (f32[64,1024]{1,0:T(8,128)S(1)}, f32[64,1024]{1,0:T(8,128)}, u32[]{:S(2)}) copy-start(f32[64,1024]{1,0:T(8,128)} %refs_9_.1) | copy-start | bytes 786436
  66.2 16.2 %copy-start.9 = (f32[256,256]{1,0:T(8,128)S(1)}, f32[256,256]{1,0:T(8,128)}, u32[]{:S(2)}) copy-start(f32[256,256]{1,0:T(8,128)} %refs_11_.1) | copy-start | bytes 786436
  66.2 16.2 %copy-start.10 = (f32[256,256]{1,0:T(8,128)S(1)}, f32[256,256]{1,0:T(8,128)}, u32[]{:S(2)}) copy-start(f32[256,256]{1,0:T(8,128)} %refs_12_.1) | copy-start | bytes 786436
  66.2 16.2 %copy-start.14 = (f32[64,256]{1,0:T(8,128)S(1)}, f32[64,256]{1,0:T(8,128)}, u32[]{:S(2)}) copy-start(f32[64,256]{1,0:T(8,128)} %refs_6_.1) | copy-start | bytes 196612
  66.2 16.2 %copy-start.2 = (f32[256,256]{1,0:T(8,128)S(1)}, f32[256,256]{1,0:T(8,128)}, u32[]{:S(2)}) copy-start(f32[256,256]{1,0:T(8,128)} %refs_10_.1) | copy-start | bytes 786436
  66.3 16.2 %copy-start.4 = (f32[64,768]{1,0:T(8,128)S(1)}, f32[64,768]{1,0:T(8,128)}, u32[]{:S(2)}) copy-start(f32[64,768]{1,0:T(8,128)} %refs_1_.1) | copy-start | bytes 589828
  66.3 16.2 %copy-start.6 = (f32[64,256]{1,0:T(8,128)S(1)}, f32[64,256]{1,0:T(8,128)}, u32[]{:S(2)}) copy-start(f32[64,256]{1,0:T(8,128)} %refs_4_.1) | copy-start | bytes 196612
  66.3 16.2 %copy-start.7 = (f32[64,1024]{1,0:T(8,128)S(1)}, f32[64,1024]{1,0:T(8,128)}, u32[]{:S(2)}) copy-start(f32[64,1024]{1,0:T(8,128)} %refs_8_.1) | copy-start | bytes 786436
  66.3 16.2 %copy-start.13 = (f32[64,256]{1,0:T(8,128)S(1)}, f32[64,256]{1,0:T(8,128)}, u32[]{:S(2)}) copy-start(f32[64,256]{1,0:T(8,128)} %refs_5_.1) | copy-start | bytes 196612

commit v3 on v2

--- a/solution.py
+++ b/solution.py
@@ -266,9 +266,8 @@
     x_ref, joined_ref, dattend_ref, log_ref, middle_ref, sums_in, len_ref, owner_ref = refs[:8]
     pieces = refs[8 : 8 + shards]
     refs = refs[8 + shards :]
-    dx_ref, keep_ref = refs[:2]
-    sends = refs[2 : 1 + shards]
-    weight_ref, small_ref, bias_ref, dquery_t, dkey, dvalue, djoined, grads_ref = refs[1 + shards :]
+    dx_ref, keep_ref, send_ref = refs[:3]
+    weight_ref, small_ref, bias_ref, dquery_t, dkey, dvalue, djoined, grads_ref = refs[3:]
     rows, width = x_ref.shape
     shard = ids[1]
     part = width // shards
@@ -329,9 +328,16 @@
             grads_ref[target, at + row * TILE_ROWS : at + row * TILE_ROWS + 1, :] = sums[
                 target * per_shard + row
             ]
-    keep_ref[...] = grads_ref[shard]
-    for offset in range(1, shards):
-        sends[offset - 1][...] = grads_ref[shard ^ offset].astype(low)
+    side = shard % 2
+    for pair in range(shards // 2):
+        keep_ref[pair] = grads_ref[2 * pair + side]
+        send_ref[pair] = grads_ref[2 * pair + 1 - side].astype(low)
+
+
+def halve_kernel(ids, kept_ref, arrived_ref, keep_ref, send_ref):
+    half = ids[1] // 2
+    keep_ref[...] = kept_ref[half] + arrived_ref[half].astype(wide)
+    send_ref[...] = (kept_ref[1 - half] + arrived_ref[1 - half].astype(wide)).astype(low)
 
 
 def piece_spans(total, tail, group):
@@ -341,29 +347,31 @@
     return spans
 
 
-def split_kernel(shards, tails, *refs):
-    pieces_ref = refs[-1]
+def split_kernel(tail, *refs):
+    arrived, pieces_ref = refs[:-1], refs[-1]
     group = pieces_ref.shape[0]
-    column = 0
-    for chunk, tail in enumerate(tails):
-        arrived = refs[chunk * shards : (chunk + 1) * shards]
-        count = arrived[0].shape[0]
-        for rows, first in piece_spans(count, tail, group):
-            for index in range(group):
-                at = first + index * rows
-                total = arrived[0][at : at + rows, :]
-                for piece in arrived[1:]:
-                    total = total + piece[at : at + rows, :].astype(wide)
-                pieces_ref[index, column : column + rows, :] = total.astype(low)
-            column += rows
-
-
-def piece_kernel(arrived_ref, sent_ref):
-    total = arrived_ref[0].astype(wide)
-    for index in range(1, arrived_ref.shape[0]):
-        total = total + arrived_ref[index].astype(wide)
+    total = arrived[0][...]
+    for piece in arrived[1:]:
+        total = total + piece[...].astype(wide)
+    for index in range(group):
+        parts = [
+            total[first + index * rows : first + (index + 1) * rows, :]
+            for rows, first in piece_spans(total.shape[0], tail, group)
+        ]
+        pieces_ref[index] = jnp.concatenate(parts, axis=0).astype(low)
+
+
+def piece_kernel(*refs):
+    sent_ref = refs[-1]
+    parts = []
+    for arrived_ref in refs[:-1]:
+        total = arrived_ref[0].astype(wide)
+        for index in range(1, arrived_ref.shape[0]):
+            total = total + arrived_ref[index].astype(wide)
+        parts.append(total)
+    result = jnp.concatenate(parts, axis=0).astype(low)
     for index in range(sent_ref.shape[0]):
-        sent_ref[index] = total.astype(low)
+        sent_ref[index] = result
 
 
 def add_kernel(mine_ref, other_ref, sent_ref):
@@ -463,21 +471,21 @@
     return lax.all_to_all(pieces, "dp", 0, 0, axis_index_groups=groups, tiled=True)
 
 
-def reduce_replicas(chunks, tails, shards):
+def reduce_replicas(chunks, tails):
     replicas = lax.axis_size("dp")
     group = min(GROUP, replicas)
     width = chunks[0][0].shape[1]
-    rows = sum(chunk[0].shape[0] for chunk in chunks) // group
-    shape = (group, rows, width)
-    (pieces,) = local_call(
-        functools.partial(split_kernel, shards, tails),
-        [(shape, low)],
-        [piece for chunk in chunks for piece in chunk],
-        name="split_sum",
-    )
-    (copies,) = local_call(
-        piece_kernel, [(shape, low)], [swap_pieces(pieces, group)], name="piece_sum"
-    )
+    arrived = []
+    for chunk, tail in zip(chunks, tails):
+        (pieces,) = local_call(
+            functools.partial(split_kernel, tail),
+            [((group, chunk[0].shape[0] // group, width), low)],
+            chunk,
+            name="split_sum",
+        )
+        arrived.append(swap_pieces(pieces, group))
+    shape = (group, sum(pieces.shape[1] for pieces in arrived), width)
+    (copies,) = local_call(piece_kernel, [(shape, low)], arrived, name="piece_sum")
     mask = group
     while mask < replicas:
         other = exchange(copies[0], "dp", mask)
@@ -549,7 +557,7 @@
         [out_weight, up_weight, down_weight],
         name="pack_second",
     )
-    firsts, second_pack = lax.optimization_barrier((firsts, second_pack))
+    firsts[2], second_pack = lax.optimization_barrier((firsts[2], second_pack))
     seconds = {0: second_pack}
     seconds[2] = exchange(second_pack, "shard", 2)
     seconds[1] = exchange(second_pack, "shard", 1)
@@ -596,10 +604,13 @@
     arrived_ffn = swap_all(sends_ffn, "shard")
     tail = GROUP * TILE_ROWS
     att_rows = 3 * part + tail
-    input_grad, keep_att, *sends_att = local_call(
+    input_grad, kept_att, send_att = local_call(
         functools.partial(attend_back_kernel, shards),
-        [((rows, width), wide), ((att_rows, width), wide)]
-        + [((att_rows, width), low)] * (shards - 1),
+        [
+            ((rows, width), wide),
+            ((shards // 2, att_rows, width), wide),
+            ((shards // 2, att_rows, width), low),
+        ],
         [tokens, joined, attended_grad, log_sums, middle_grad, sums, lengths, seq_owner] + firsts,
         [
             ((width, 3 * width), low),
@@ -615,11 +626,16 @@
         flops=heads * rows * rows * 256 * 10,
         name="attend_back",
     )
-    arrived_att = swap_all(sends_att, "shard")
+    keep_att, send_att = local_call(
+        halve_kernel,
+        [((att_rows, width), wide), ((att_rows, width), low)],
+        [kept_att, exchange(send_att, "shard", 1)],
+        ids=ids,
+        name="halve",
+    )
+    arrived_att = [exchange(send_att, "shard", 2)]
     tails = (0, tail)
-    pieces = reduce_replicas(
-        [[keep_ffn] + arrived_ffn, [keep_att] + arrived_att], tails, shards
-    )
+    pieces = reduce_replicas([[keep_ffn] + arrived_ffn, [keep_att] + arrived_att], tails)
     blocks = hidden_count // width
     results = adam_call(
         pieces,

time: 84.6 us -> 88.5 us (1.046)
  blocking collectives: 35.1 us -> 29.7 us
  waiting for transfers between devices: 11.7 us -> 16 us
  starting transfers between devices: 10.1 us -> 13.7 us
  Pallas kernels: 22.1 us -> 23.4 us
    all_to_all x0 -> x1, starting transfers between devices: none -> 5.81 us  [swap_pieces(): lax.all_to_all(pieces, 'dp', 0, 0, axis_index_groups=groups, tiled=True)]
    all_to_all x2, blocking collectives: 35.1 us -> 29.7 us  [swap_pieces(): lax.all_to_all(pieces, 'dp', 0, 0, axis_index_groups=groups, tiled=True)]
    all_to_all x0 -> x1, waiting for transfers between devices: none -> 2.64 us  [swap_pieces(): lax.all_to_all(pieces, 'dp', 0, 0, axis_index_groups=groups, tiled=True)]
    ppermute x12 -> x11, starting transfers between devices: 10.1 us -> 7.9 us  [exchange(): lax.ppermute(values, axis, [(index, index ^ mask) for index in range(coun...]
    ppermute x12 -> x11, waiting for transfers between devices: 11.7 us -> 13.4 us  [exchange(): lax.ppermute(values, axis, [(index, index ^ mask) for index in range(coun...]
    pallas_call x8 -> x10, Pallas kernels: 22.1 us -> 23.4 us  [local_call(): pl.pallas_call(kernel, out_shape=outs, in_specs=specs, out_specs=[pl.Bloc...]
  transfers between devices with their start and end apart: 12 -> 12, of which waited for: 5 -> 7; matrix products, arithmetic and copies ran while one was open for 0% -> 0% of each run, Pallas kernels for 18% -> 8%
where the time goes in v3:
time: 88.5 us; the launch traced here: 88.1 us
  blocking collectives  29.7 us (34%)
  Pallas kernels  23.4 us (26%)
  waiting for transfers between devices  16 us (18%)
  starting transfers between devices  13.7 us (15%)
  local copies, waits for them, and re-layouts  4.19 us (5%)
  between operations  0.93 us (1%)
    all_to_all x2, blocking collectives, swap_pieces(): lax.all_to_all(pieces, 'dp', 0, 0, axis_index_groups=groups, tiled=True)  29.7 us
    pallas_call x10, Pallas kernels, local_call(): pl.pallas_call(kernel, out_shape=outs, in_specs=specs, out_specs=[pl.Bloc...  23.4 us
    ppermute x11, waiting for transfers between devices, exchange(): lax.ppermute(values, axis, [(index, index ^ mask) for index in range(coun...  13.4 us
    ppermute x11, starting transfers between devices, exchange(): lax.ppermute(values, axis, [(index, index ^ mask) for index in range(coun...  7.9 us
    all_to_all x1, starting transfers between devices, swap_pieces(): lax.all_to_all(pieces, 'dp', 0, 0, axis_index_groups=groups, tiled=True)  5.81 us
    unnamed x46, local copies, waits for them, and re-layouts  4.19 us
    all_to_all x1, waiting for transfers between devices, swap_pieces(): lax.all_to_all(pieces, 'dp', 0, 0, axis_index_groups=groups, tiled=True)  2.64 us
  transfers between devices with their start and end apart: 12, of which 7 were waited for; matrix products, arithmetic and copies ran while one was open for 0% of the time, Pallas kernels for 8%

profile of v3, /device:TPU:0, one launch (start us, length us, event | category | flops | bytes accessed | tf_op | source)
XLA Modules:
  0.0 88.1 jit_solution(16946052582512016492)
XLA Ops:
  0.7 0.0 copy-start.3
  0.7 1.0 %copy-done.3 = f32[64,768]{1,0:T(8,128)S(1)} copy-done((f32[64,768]{1,0:T(8,128)S(1)}, f32[64,768]{1,0:T(8,128)}, u32[]{:S(2)}) %copy-start.3) | copy-done | bytes 196632
  1.6 0.7 copy-done.15
  2.3 3.0 %collective-permute-start.1 = (bf16[208,256]{1,0:T(8,128)(2,1)S(1)}, bf16[208,256]{1,0:T(8,128)(2,1)S(1)}, u32[]{:S(2)}, u32[]{:S(2)}) collective-permute-start(bf16[208,256]{1,0:T(8,128)(2,1)S(1)} %pack_first.1.refs_3_.refs_5_.refs_8_), channel_id=1, source_target_pairs={{0,2},{1,3},{2,0},{3,1},{4,6},{5,7},{6,4},{7,5},{8,10},{9,11},{10,... | collective-permute-start | bytes 319496 | tf_op jit(solution)/shard_map/ppermute | solution.py:449
  5.4 0.0 collective-permute-start
  5.4 0.9 %copy-done.1 = f32[256,256]{1,0:T(8,128)S(1)} copy-done((f32[256,256]{1,0:T(8,128)S(1)}, f32[256,256]{1,0:T(8,128)}, u32[]{:S(2)}) %copy-start.1) | copy-done | bytes 262168
  6.3 0.8 copy-done.5
  7.2 1.1 %collective-permute-done.1.refs_5_.refs_7_.refs_10_ = bf16[208,256]{1,0:T(8,128)(2,1)S(1)} collective-permute-done((bf16[208,256]{1,0:T(8,128)(2,1)S(1)}, bf16[208,256]{1,0:T(8,128)(2,1)S(1)}, u32[]{:S(2)}, u32[]{:S(2)}) %collective-permute-start.1) | collective-permute-done | bytes 106528 | tf_op jit(solution)/shard_map/ppermute | solution.py:449
  8.3 1.7 %collective-permute-start.3 = (bf16[576,256]{1,0:T(8,128)(2,1)S(1)}, bf16[576,256]{1,0:T(8,128)(2,1)S(1)}, u32[]{:S(2)}, u32[]{:S(2)}) collective-permute-start(bf16[576,256]{1,0:T(8,128)(2,1)S(1)} %pack_second.1.refs_9_), channel_id=1, source_target_pairs={{0,2},{1,3},{2,0},{3,1},{4,6},{5,7},{6,4},{7,5},{8,10},{9,11},{10,... | collective-permute-start | bytes 884744 | tf_op jit(solution)/shard_map/ppermute | solution.py:449
  10.1 0.0 collective-permute-start.2
  10.1 0.1 pad_add_fusion.ids
  10.2 0.5 collective-permute-start.4
  10.7 0.0 collective-permute-done.refs_4_.refs_6_.refs_9_
  10.7 0.7 collective-permute-done.2.refs_6_.refs_8_.refs_11_
  11.4 0.6 copy-done.21
  12.1 0.0 copy-done.22
  12.1 5.9 %attend.1 = (bf16[512,768]{1,0:T(8,128)(2,1)S(1)}, bf16[512,256]{1,0:T(8,128)(2,1)S(1)}, f32[8,512]{1,0:T(8,128)S(1)}) custom-call(s32[2]{0:T(128)S(1)} %pad_add_fusion.ids, bf16[512,256]{1,0:T(8,128)(2,1)S(1)} %copy-done.20, s32[1,128]{1,0:T(1,128)S(1)} %bitcast.4, s32[1,128]{1,0:T(1,128)S(1)} %bitcast.7, ...), custom_call_target="tpu_custom_call" | custom-call | flops 2147483648 | bytes 1754120 | tf_op jit(solution)/shard_map/attend/pallas_call | solution.py:435
  18.0 0.0 collective-permute-done.3.refs_11_
  18.0 0.2 collective-permute-start.5
  18.3 0.0 collective-permute-done.4.refs_10_
  18.3 1.4 %collective-permute-done.5.refs_12_ = bf16[576,256]{1,0:T(8,128)(2,1)S(1)} collective-permute-done((bf16[576,256]{1,0:T(8,128)(2,1)S(1)}, bf16[576,256]{1,0:T(8,128)(2,1)S(1)}, u32[]{:S(2)}, u32[]{:S(2)}) %collective-permute-start.5) | collective-permute-done | bytes 294944 | tf_op jit(solution)/shard_map/ppermute | solution.py:449
  19.7 4.7 %feed.1 = (bf16[512,256]{1,0:T(8,128)(2,1)}, f32[512,256]{1,0:T(8,128)S(1)}, bf16[512,256]{1,0:T(8,128)(2,1)S(1)}, f32[16,256]{1,0:T(8,128)S(1)}, f32[576,256]{1...) custom-call(s32[2]{0:T(128)S(1)} %pad_add_fusion.ids, ...), custom_call_target="tpu_custom_call" | custom-call | flops 1811939328 | bytes 4932616 | tf_op jit(solution)/shard_map/feed/pallas_call | solution.py:435
  24.4 9.5 %attend_back.1 = (f32[512,256]{1,0:T(8,128)}, f32[2,256,256]{2,1,0:T(8,128)S(1)}, bf16[2,256,256]{2,1,0:T(8,128)(2,1)S(1)}) custom-call(s32[2]{0:T(128)S(1)} %pad_add_fusion.ids, bf16[512,256]{1,0:T(8,128)(2,1)S(1)} %copy-done.20, bf16[512,768]{1,0:T(8,128)(2,1)S(1)} %get-tuple-element.58.refs_1_, bf16[512,256]{1,0:T(8,128)(2,1)S(1)} %get-tuple-element.59.refs_2_, ...), custom_call_target="tpu_custom_call" | custom-call | flops 5368709120 | bytes 3605512 | tf_op jit(solution)/shard_map/attend_back/pallas_call | solution.py:435
  33.9 0.2 collective-permute-start.9
  34.0 1.4 %collective-permute-done.9.arrived_ref = bf16[2,256,256]{2,1,0:T(8,128)(2,1)S(1)} collective-permute-done((bf16[2,256,256]{2,1,0:T(8,128)(2,1)S(1)}, bf16[2,256,256]{2,1,0:T(8,128)(2,1)S(1)}, u32[]{:S(2)}, u32[]{:S(2)}) %collective-permute-start.9) | collective-permute-done | bytes 262176 | tf_op jit(solution)/shard_map/ppermute | solution.py:449
  35.4 0.6 halve.1
  36.0 0.4 collective-permute-start.10
  36.4 0.0 collective-permute-start.6
  36.4 1.7 %collective-permute-start.7 = (bf16[576,256]{1,0:T(8,128)(2,1)S(1)}, bf16[576,256]{1,0:T(8,128)(2,1)S(1)}, u32[]{:S(2)}, u32[]{:S(2)}) collective-permute-start(bf16[576,256]{1,0:T(8,128)(2,1)S(1)} %get-tuple-element.66), channel_id=1, source_target_pairs={{0,2},{1,3},{2,0},{3,1},{4,6},{5,7},{6,4},{7,5},{8,10},{9,11},{10,... | collective-permute-start | bytes 884744 | tf_op jit(solution)/shard_map/ppermute | solution.py:449
  38.1 0.1 collective-permute-start.8
  38.3 4.2 %collective-permute-done.10.refs_1_ = bf16[256,256]{1,0:T(8,128)(2,1)S(1)} collective-permute-done((bf16[256,256]{1,0:T(8,128)(2,1)S(1)}, bf16[256,256]{1,0:T(8,128)(2,1)S(1)}, u32[]{:S(2)}, u32[]{:S(2)}) %collective-permute-start.10) | collective-permute-done | bytes 131104 | tf_op jit(solution)/shard_map/ppermute | solution.py:449
  42.4 0.7 split_sum.3
  43.1 5.8 %all-to-all-start.1 = ((bf16[8,32,256]{2,1,0:T(8,128)(2,1)}), bf16[8,32,256]{2,1,0:T(8,128)(2,1)S(1)}, u32[]{:S(2)}, u32[]{:S(2)}) async-start(bf16[8,32,256]{2,1,0:T(8,128)(2,1)} %split_sum.3), calls=%async_computation.1 | async-start | bytes 262144 | tf_op jit(solution)/shard_map/all_to_all | solution.py:471
  48.9 0.0 collective-permute-done.6.refs_1_
  48.9 0.0 collective-permute-done.7.refs_2_
  48.9 4.6 %collective-permute-done.8.refs_3_ = bf16[576,256]{1,0:T(8,128)(2,1)S(1)} collective-permute-done((bf16[576,256]{1,0:T(8,128)(2,1)S(1)}, bf16[576,256]{1,0:T(8,128)(2,1)S(1)}, u32[]{:S(2)}, u32[]{:S(2)}) %collective-permute-start.8) | collective-permute-done | bytes 294944 | tf_op jit(solution)/shard_map/ppermute | solution.py:449
  53.5 0.1 split_sum.2
  53.6 2.6 %all-to-all-done.1.refs_1_ = bf16[8,32,256]{2,1,0:T(8,128)(2,1)S(1)} async-done(((bf16[8,32,256]{2,1,0:T(8,128)(2,1)}), bf16[8,32,256]{2,1,0:T(8,128)(2,1)S(1)}, u32[]{:S(2)}, u32[]{:S(2)}) %all-to-all-start.1) | async-done | bytes 131104 | tf_op jit(solution)/shard_map/all_to_all | solution.py:471
  56.3 0.0 copy-start.18
  56.3 14.3 %all_to_all.15.refs_0_ = bf16[8,72,256]{2,1,0:T(8,128)(2,1)S(1)} all-to-all(bf16[8,72,256]{2,1,0:T(8,128)(2,1)S(1)} %split_sum.2), channel_id=1, replica_groups=mesh['dp'=8,'shard'=4] {'dp'}, dimensions={0} | all-to-all | bytes 589824 | tf_op jit(solution)/shard_map/all_to_all | solution.py:471
  70.6 0.1 piece_sum.1
  70.6 0.0 copy-start.2
  70.6 0.0 copy-start.4
  70.7 0.0 copy-start.6
  70.7 0.0 copy-start.7
  70.7 0.0 copy-start.13
  70.7 15.4 %all_to_all.16.refs_0_ = bf16[8,104,256]{2,1,0:T(8,128)(2,1)S(1)} all-to-all(bf16[8,104,256]{2,1,0:T(8,128)(2,1)S(1)} %piece_sum.1), channel_id=1, replica_groups=mesh['dp'=8,'shard'=4] {'dp'}, dimensions={0} | all-to-all | bytes 851968 | tf_op jit(solution)/shard_map/all_to_all | solution.py:471
  86.3 1.8 %adam.1 = (f32[64,768]{1,0:T(8,128)}, f32[64,768]{1,0:T(8,128)}, f32[64,768]{1,0:T(8,128)}, f32[64,256]{1,0:T(8,128)}, f32[64,256]{1,0:T(8,128)}, /*index=5*/f32...) custom-call(bf16[8,104,256]{2,1,0:T(8,128)(2,1)S(1)} %all_to_all.16., ...), custom_call_target="tpu_custom_call" | custom-call | bytes 5163008 | tf_op jit(solution)/shard_map/adam/pallas_call | solution.py:435
  (35 shorter events, 0.1 us)
Async XLA Ops:
  0.7 4.7 %copy-start = (f32[64,1024]{1,0:T(8,128)S(1)}, f32[64,1024]{1,0:T(8,128)}, u32[]{:S(2)}) copy-start(f32[64,1024]{1,0:T(8,128)} %refs_7_.1) | copy-start | bytes 786436
  0.7 1.0 %copy-start.3 = (f32[64,768]{1,0:T(8,128)S(1)}, f32[64,768]{1,0:T(8,128)}, u32[]{:S(2)}) copy-start(f32[64,768]{1,0:T(8,128)} %refs_1_.1) | copy-start | bytes 589828
  1.6 0.7 copy-start.15
  2.3 6.0 %collective-permute-start.1 = (bf16[208,256]{1,0:T(8,128)(2,1)S(1)}, bf16[208,256]{1,0:T(8,128)(2,1)S(1)}, u32[]{:S(2)}, u32[]{:S(2)}) collective-permute-start(bf16[208,256]{1,0:T(8,128)(2,1)S(1)} %pack_first.1.refs_3_.refs_5_.refs_8_), channel_id=1, source_target_pairs={{0,2},{1,3},{2,0},{3,1},{4,6},{5,7},{6,4},{7,5},{8,10},{9,11},{10,... | collective-permute-start | bytes 319496 | tf_op jit(solution)/shard_map/ppermute | solution.py:449
  5.4 5.3 %collective-permute-start = (bf16[208,256]{1,0:T(8,128)(2,1)S(1)}, bf16[208,256]{1,0:T(8,128)(2,1)S(1)}, u32[]{:S(2)}, u32[]{:S(2)}) collective-permute-start(bf16[208,256]{1,0:T(8,128)(2,1)S(1)} %pack_first.1.refs_3_.refs_5_.refs_8_), channel_id=1, source_target_pairs={{0,1},{1,0},{2,3},{3,2},{4,5},{5,4},{6,7},{7,6},{8,9},{9,8},{10,11... | collective-permute-start | bytes 319496 | tf_op jit(solution)/shard_map/ppermute | solution.py:449
  5.4 1.0 %copy-start.1 = (f32[256,256]{1,0:T(8,128)S(1)}, f32[256,256]{1,0:T(8,128)}, u32[]{:S(2)}) copy-start(f32[256,256]{1,0:T(8,128)} %refs_10_.1) | copy-start | bytes 786436
  6.3 0.8 copy-start.5
  7.2 4.2 %copy-start.20 = (bf16[512,256]{1,0:T(8,128)(2,1)S(1)}, bf16[512,256]{1,0:T(8,128)(2,1)}, u32[]{:S(2)}) copy-start(bf16[512,256]{1,0:T(8,128)(2,1)} %refs_0_.5) | copy-start | bytes 786436
  8.3 9.7 %collective-permute-start.3 = (bf16[576,256]{1,0:T(8,128)(2,1)S(1)}, bf16[576,256]{1,0:T(8,128)(2,1)S(1)}, u32[]{:S(2)}, u32[]{:S(2)}) collective-permute-start(bf16[576,256]{1,0:T(8,128)(2,1)S(1)} %pack_second.1.refs_9_), channel_id=1, source_target_pairs={{0,2},{1,3},{2,0},{3,1},{4,6},{5,7},{6,4},{7,5},{8,10},{9,11},{10,... | collective-permute-start | bytes 884744 | tf_op jit(solution)/shard_map/ppermute | solution.py:449
  10.1 1.3 %collective-permute-start.2 = (bf16[208,256]{1,0:T(8,128)(2,1)S(1)}, bf16[208,256]{1,0:T(8,128)(2,1)S(1)}, u32[]{:S(2)}, u32[]{:S(2)}) collective-permute-start(bf16[208,256]{1,0:T(8,128)(2,1)S(1)} %collective-permute-done.1.refs_5_.refs_7_.refs_10_), channel_id=1, source_target_pairs={{0,1},{1,0},{2,3},{3,2},{4,5},{5,4},{6,7},{7,6},{8,9},{9,8},{10,11... | collective-permute-start | bytes 319496 | tf_op jit(solution)/shard_map/ppermute | solution.py:449
  10.2 8.1 %collective-permute-start.4 = (bf16[576,256]{1,0:T(8,128)(2,1)S(1)}, bf16[576,256]{1,0:T(8,128)(2,1)S(1)}, u32[]{:S(2)}, u32[]{:S(2)}) collective-permute-start(bf16[576,256]{1,0:T(8,128)(2,1)S(1)} %pack_second.1.refs_9_), channel_id=1, source_target_pairs={{0,1},{1,0},{2,3},{3,2},{4,5},{5,4},{6,7},{7,6},{8,9},{9,8},{10,11... | collective-permute-start | bytes 884744 | tf_op jit(solution)/shard_map/ppermute | solution.py:449
  11.4 0.7 copy-start.21
  11.4 0.7 copy-start.22
  12.1 7.6 %copy-start.19 = (bf16[512,256]{1,0:T(8,128)(2,1)S(1)}, bf16[512,256]{1,0:T(8,128)(2,1)}, u32[]{:S(2)}) copy-start(bf16[512,256]{1,0:T(8,128)(2,1)} %refs_2_.2) | copy-start | bytes 786436
  18.0 1.6 %collective-permute-start.5 = (bf16[576,256]{1,0:T(8,128)(2,1)S(1)}, bf16[576,256]{1,0:T(8,128)(2,1)S(1)}, u32[]{:S(2)}, u32[]{:S(2)}) collective-permute-start(bf16[576,256]{1,0:T(8,128)(2,1)S(1)} %collective-permute-done.3.refs_11_), channel_id=1, source_target_pairs={{0,1},{1,0},{2,3},{3,2},{4,5},{5,4},{6,7},{7,6},{8,9},{9,8},{10,11... | collective-permute-start | bytes 884744 | tf_op jit(solution)/shard_map/ppermute | solution.py:449
  33.9 1.5 %collective-permute-start.9 = (bf16[2,256,256]{2,1,0:T(8,128)(2,1)S(1)}, bf16[2,256,256]{2,1,0:T(8,128)(2,1)S(1)}, u32[]{:S(2)}, u32[]{:S(2)}) collective-permute-start(bf16[2,256,256]{2,1,0:T(8,128)(2,1)S(1)} %get-tuple-element.69), channel_id=1, source_target_pairs={{0,1},{1,0},{2,3},{3,2},{4,5},{5,4},{6,7},{7,6},{8,9},{9,8},{10,11... | collective-permute-start | bytes 786440 | tf_op jit(solution)/shard_map/ppermute | solution.py:449
  36.0 6.4 %collective-permute-start.10 = (bf16[256,256]{1,0:T(8,128)(2,1)S(1)}, bf16[256,256]{1,0:T(8,128)(2,1)S(1)}, u32[]{:S(2)}, u32[]{:S(2)}) collective-permute-start(bf16[256,256]{1,0:T(8,128)(2,1)S(1)} %get-tuple-element.71), channel_id=1, source_target_pairs={{0,2},{1,3},{2,0},{3,1},{4,6},{5,7},{6,4},{7,5},{8,10},{9,11},{10,... | collective-permute-start | bytes 393224 | tf_op jit(solution)/shard_map/ppermute | solution.py:449
  36.4 12.5 %collective-permute-start.6 = (bf16[576,256]{1,0:T(8,128)(2,1)S(1)}, bf16[576,256]{1,0:T(8,128)(2,1)S(1)}, u32[]{:S(2)}, u32[]{:S(2)}) collective-permute-start(bf16[576,256]{1,0:T(8,128)(2,1)S(1)} %get-tuple-element.65), channel_id=1, source_target_pairs={{0,1},{1,0},{2,3},{3,2},{4,5},{5,4},{6,7},{7,6},{8,9},{9,8},{10,11... | collective-permute-start | bytes 884744 | tf_op jit(solution)/shard_map/ppermute | solution.py:449
  36.4 12.6 %collective-permute-start.7 = (bf16[576,256]{1,0:T(8,128)(2,1)S(1)}, bf16[576,256]{1,0:T(8,128)(2,1)S(1)}, u32[]{:S(2)}, u32[]{:S(2)}) collective-permute-start(bf16[576,256]{1,0:T(8,128)(2,1)S(1)} %get-tuple-element.66), channel_id=1, source_target_pairs={{0,2},{1,3},{2,0},{3,1},{4,6},{5,7},{6,4},{7,5},{8,10},{9,11},{10,... | collective-permute-start | bytes 884744 | tf_op jit(solution)/shard_map/ppermute | solution.py:449
  38.1 15.4 %collective-permute-start.8 = (bf16[576,256]{1,0:T(8,128)(2,1)S(1)}, bf16[576,256]{1,0:T(8,128)(2,1)S(1)}, u32[]{:S(2)}, u32[]{:S(2)}) collective-permute-start(bf16[576,256]{1,0:T(8,128)(2,1)S(1)} %get-tuple-element.67), channel_id=1, source_target_pairs={{0,3},{1,2},{2,1},{3,0},{4,7},{5,6},{6,5},{7,4},{8,11},{9,10},{10,... | collective-permute-start | bytes 884744 | tf_op jit(solution)/shard_map/ppermute | solution.py:449
  43.1 13.2 %all-to-all-start.1 = ((bf16[8,32,256]{2,1,0:T(8,128)(2,1)}), bf16[8,32,256]{2,1,0:T(8,128)(2,1)S(1)}, u32[]{:S(2)}, u32[]{:S(2)}) async-start(bf16[8,32,256]{2,1,0:T(8,128)(2,1)} %split_sum.3), calls=%async_computation.1 | async-start | bytes 262144 | tf_op jit(solution)/shard_map/all_to_all | solution.py:471
  56.3 29.9 %copy-start.11 = (f32[64,768]{1,0:T(8,128)S(1)}, f32[64,768]{1,0:T(8,128)}, u32[]{:S(2)}) copy-start(f32[64,768]{1,0:T(8,128)} %refs_2_.3) | copy-start | bytes 589828
  56.3 29.9 %copy-start.12 = (f32[64,768]{1,0:T(8,128)S(1)}, f32[64,768]{1,0:T(8,128)}, u32[]{:S(2)}) copy-start(f32[64,768]{1,0:T(8,128)} %refs_3_.1) | copy-start | bytes 589828
  56.3 29.9 %copy-start.16 = (f32[768]{0:T(1024)S(1)}, f32[768]{0:T(1024)}, u32[]{:S(2)}) copy-start(f32[768]{0:T(1024)} %refs_13_.1) | copy-start | bytes 9220
  56.3 29.9 %copy-start.17 = (f32[768]{0:T(1024)S(1)}, f32[768]{0:T(1024)}, u32[]{:S(2)}) copy-start(f32[768]{0:T(1024)} %refs_14_.1) | copy-start | bytes 9220
  56.3 29.9 %copy-start.18 = (f32[768]{0:T(1024)S(1)}, f32[768]{0:T(1024)}, u32[]{:S(2)}) copy-start(f32[768]{0:T(1024)} %refs_15_.1) | copy-start | bytes 9220
  70.5 15.6 %copy-start.8 = (f32[64,1024]{1,0:T(8,128)S(1)}, f32[64,1024]{1,0:T(8,128)}, u32[]{:S(2)}) copy-start(f32[64,1024]{1,0:T(8,128)} %refs_9_.1) | copy-start | bytes 786436
  70.5 15.6 %copy-start.9 = (f32[256,256]{1,0:T(8,128)S(1)}, f32[256,256]{1,0:T(8,128)}, u32[]{:S(2)}) copy-start(f32[256,256]{1,0:T(8,128)} %refs_11_.1) | copy-start | bytes 786436
  70.6 15.6 %copy-start.10 = (f32[256,256]{1,0:T(8,128)S(1)}, f32[256,256]{1,0:T(8,128)}, u32[]{:S(2)}) copy-start(f32[256,256]{1,0:T(8,128)} %refs_12_.1) | copy-start | bytes 786436
  70.6 15.6 %copy-start.14 = (f32[64,256]{1,0:T(8,128)S(1)}, f32[64,256]{1,0:T(8,128)}, u32[]{:S(2)}) copy-start(f32[64,256]{1,0:T(8,128)} %refs_6_.1) | copy-start | bytes 196612
  70.6 15.6 %copy-start.2 = (f32[256,256]{1,0:T(8,128)S(1)}, f32[256,256]{1,0:T(8,128)}, u32[]{:S(2)}) copy-start(f32[256,256]{1,0:T(8,128)} %refs_10_.1) | copy-start | bytes 786436
  70.6 15.6 %copy-start.4 = (f32[64,768]{1,0:T(8,128)S(1)}, f32[64,768]{1,0:T(8,128)}, u32[]{:S(2)}) copy-start(f32[64,768]{1,0:T(8,128)} %refs_1_.1) | copy-start | bytes 589828
  70.7 15.6 %copy-start.6 = (f32[64,256]{1,0:T(8,128)S(1)}, f32[64,256]{1,0:T(8,128)}, u32[]{:S(2)}) copy-start(f32[64,256]{1,0:T(8,128)} %refs_4_.1) | copy-start | bytes 196612
  70.7 15.6 %copy-start.7 = (f32[64,1024]{1,0:T(8,128)S(1)}, f32[64,1024]{1,0:T(8,128)}, u32[]{:S(2)}) copy-start(f32[64,1024]{1,0:T(8,128)} %refs_8_.1) | copy-start | bytes 786436
  70.7 15.6 %copy-start.13 = (f32[64,256]{1,0:T(8,128)S(1)}, f32[64,256]{1,0:T(8,128)}, u32[]{:S(2)}) copy-start(f32[64,256]{1,0:T(8,128)} %refs_5_.1) | copy-start | bytes 196612

commit v4 on v3

--- a/solution.py
+++ b/solution.py
@@ -334,10 +334,18 @@
         send_ref[pair] = grads_ref[2 * pair + 1 - side].astype(low)
 
 
-def halve_kernel(ids, kept_ref, arrived_ref, keep_ref, send_ref):
-    half = ids[1] // 2
-    keep_ref[...] = kept_ref[half] + arrived_ref[half].astype(wide)
-    send_ref[...] = (kept_ref[1 - half] + arrived_ref[1 - half].astype(wide)).astype(low)
+def halve_kernel(which, bit, ids, *refs):
+    count = (len(refs) - 2) // 2
+    keep_ref, send_ref = refs[-2:]
+    side = (ids[which] >> bit) & 1
+    for pair in range(keep_ref.shape[0]):
+        for target, index in ((keep_ref, 2 * pair + side), (send_ref, 2 * pair + 1 - side)):
+            parts = []
+            for chunk in range(count):
+                kept, arrived = refs[2 * chunk : 2 * chunk + 2]
+                parts.append(kept[index] + arrived[index].astype(wide))
+            value = parts[0] if count == 1 else jnp.concatenate(parts, axis=0)
+            target[pair] = value.astype(target.dtype)
 
 
 def piece_spans(total, tail, group):
@@ -347,37 +355,27 @@
     return spans
 
 
-def split_kernel(tail, *refs):
-    arrived, pieces_ref = refs[:-1], refs[-1]
-    group = pieces_ref.shape[0]
+def split_kernel(tail, ids, *refs):
+    arrived, keep_ref, send_ref, sum_ref = refs[:-3], *refs[-3:]
+    group = sum_ref.shape[0]
     total = arrived[0][...]
     for piece in arrived[1:]:
         total = total + piece[...].astype(wide)
     for index in range(group):
-        parts = [
-            total[first + index * rows : first + (index + 1) * rows, :]
-            for rows, first in piece_spans(total.shape[0], tail, group)
-        ]
-        pieces_ref[index] = jnp.concatenate(parts, axis=0).astype(low)
-
-
-def piece_kernel(*refs):
-    sent_ref = refs[-1]
-    parts = []
-    for arrived_ref in refs[:-1]:
-        total = arrived_ref[0].astype(wide)
-        for index in range(1, arrived_ref.shape[0]):
-            total = total + arrived_ref[index].astype(wide)
-        parts.append(total)
-    result = jnp.concatenate(parts, axis=0).astype(low)
-    for index in range(sent_ref.shape[0]):
-        sent_ref[index] = result
-
-
-def add_kernel(mine_ref, other_ref, sent_ref):
-    total = (mine_ref[0].astype(wide) + other_ref[...].astype(wide)).astype(low)
-    for index in range(sent_ref.shape[0]):
-        sent_ref[index] = total
+        row = 0
+        for rows, first in piece_spans(total.shape[0], tail, group):
+            at = first + index * rows
+            sum_ref[index, row : row + rows, :] = total[at : at + rows, :]
+            row += rows
+    side = ids[2] & 1
+    for pair in range(group // 2):
+        keep_ref[pair] = sum_ref[2 * pair + side]
+        send_ref[pair] = sum_ref[2 * pair + 1 - side].astype(low)
+
+
+def add_kernel(mine_ref, other_ref, sum_ref):
+    total = mine_ref[...].astype(wide) + other_ref[...].astype(wide)
+    sum_ref[...] = total.astype(low).reshape(sum_ref.shape)
 
 
 def adam_values(weight, grad, first, second, decay_rate):
@@ -391,17 +389,18 @@
     return first_next, second_next, weight - learn_rate * (update + decay_rate * weight)
 
 
-def adam_kernel(spans, layout, *refs):
-    pieces_ref = refs[0]
+def adam_kernel(group, spans, layout, ids, *refs):
+    pieces = refs[:group]
     grad_ref = refs[-1]
     count = len(layout)
-    states = refs[1 : 1 + 3 * count]
-    results = refs[1 + 3 * count : -1]
-    for index in range(pieces_ref.shape[0]):
-        value = pieces_ref[index].astype(wide)
+    states = refs[group : group + 3 * count]
+    results = refs[group + 3 * count : -1]
+    for offset, piece in enumerate(pieces):
+        value = piece[...].astype(wide)
+        index = ids[2] ^ offset
         for rows, first, row in spans:
-            at = first + index * rows
-            grad_ref[at : at + rows, :] = value[row : row + rows, :]
+            at = pl.multiple_of(first + index * rows, TILE_ROWS)
+            grad_ref[pl.ds(at, rows), :] = value[row : row + rows, :]
     width = grad_ref.shape[1]
     for array, (first_row, stride, decay) in enumerate(layout):
         weight, first, second = states[3 * array : 3 * array + 3]
@@ -449,53 +448,63 @@
     return lax.ppermute(values, axis, [(index, index ^ mask) for index in range(count)])
 
 
-def gather_shards(value, shards):
+def gather_near(value, axis, count):
     found = {0: value}
-    far = shards // 2
+    far = count // 2
     while far:
         for offset in sorted(found):
-            found[offset ^ far] = exchange(found[offset], "shard", far)
+            found[offset ^ far] = exchange(found[offset], axis, far)
         far //= 2
-    return [found[offset] for offset in range(shards)]
+    return [found[offset] for offset in range(count)]
 
 
 def swap_all(values, axis):
     return [exchange(value, axis, offset + 1) for offset, value in enumerate(values)]
 
 
-def swap_pieces(pieces, group):
+def split_chunk(chunk, tail, ids, group):
+    rows, width = chunk[0].shape
+    half = (group // 2, rows // group, width)
+    keep, send = local_call(
+        functools.partial(split_kernel, tail),
+        [(half, wide), (half, low)],
+        chunk,
+        [((group,) + half[1:], wide)],
+        ids,
+        name="split_sum",
+    )
+    return keep, exchange(send, "dp", 1)
+
+
+def finish_sum(chunks, ids, group):
     replicas = lax.axis_size("dp")
-    groups = None
-    if replicas > group:
-        groups = [list(range(at, at + group)) for at in range(0, replicas, group)]
-    return lax.all_to_all(pieces, "dp", 0, 0, axis_index_groups=groups, tiled=True)
-
-
-def reduce_replicas(chunks, tails):
-    replicas = lax.axis_size("dp")
-    group = min(GROUP, replicas)
-    width = chunks[0][0].shape[1]
-    arrived = []
-    for chunk, tail in zip(chunks, tails):
-        (pieces,) = local_call(
-            functools.partial(split_kernel, tail),
-            [((group, chunk[0].shape[0] // group, width), low)],
-            chunk,
-            name="split_sum",
+    half, _, width = chunks[0][0].shape
+    rows = sum(chunk[0].shape[1] for chunk in chunks)
+    flat = [item for chunk in chunks for item in chunk]
+    bit = 1
+    while half > 1:
+        half //= 2
+        keep, send = local_call(
+            functools.partial(halve_kernel, 2, bit),
+            [((half, rows, width), wide), ((half, rows, width), low)],
+            flat,
+            ids=ids,
+            name="halve_dp",
         )
-        arrived.append(swap_pieces(pieces, group))
-    shape = (group, sum(pieces.shape[1] for pieces in arrived), width)
-    (copies,) = local_call(piece_kernel, [(shape, low)], arrived, name="piece_sum")
+        flat = [keep, exchange(send, "dp", 1 << bit)]
+        bit += 1
     mask = group
+    (piece,) = local_call(add_kernel, [((rows, width), low)], flat, name="piece_sum")
     while mask < replicas:
-        other = exchange(copies[0], "dp", mask)
-        (copies,) = local_call(add_kernel, [(shape, low)], [copies, other], name="far_sum")
+        other = exchange(piece, "dp", mask)
+        (piece,) = local_call(add_kernel, [((rows, width), low)], [piece, other], name="far_sum")
         mask *= 2
-    return swap_pieces(copies, group)
-
-
-def adam_call(pieces, counts, tails, states, layout):
-    group, _, width = pieces.shape
+    return gather_near(piece, "dp", group)
+
+
+def adam_call(pieces, counts, tails, states, layout, ids):
+    group = len(pieces)
+    width = pieces[0].shape[1]
     spans = []
     first = row = 0
     for total, tail in zip(counts, tails):
@@ -504,10 +513,11 @@
             row += rows
         first += total
     return local_call(
-        functools.partial(adam_kernel, spans, layout),
+        functools.partial(adam_kernel, group, spans, layout),
         [(state[0].shape, wide) for state in states for _ in range(3)],
-        [pieces] + [item for state in states for item in state],
+        pieces + [item for state in states for item in state],
         [((first, width), wide)],
+        ids,
         name="adam",
     )
 
@@ -539,7 +549,9 @@
     part = qkv_weight.shape[0]
     hidden_count = up_weight.shape[1]
     device = lax.axis_index(("dp", "shard"))
-    ids = jnp.stack([device, lax.axis_index("shard")]).astype(jnp.int32)
+    group = min(GROUP, lax.axis_size("dp"))
+    ids = jnp.stack([device, lax.axis_index("shard"), lax.axis_index("dp") % group])
+    ids = ids.astype(jnp.int32)
     lengths = lengths.reshape(1, -1)
     seq_owner = seq_owner.reshape(1, -1)
     first_rows = 3 * part + SMALL_PAD
@@ -550,7 +562,7 @@
         [qkv_weight, gains_biases],
         name="pack_first",
     )
-    firsts = gather_shards(first_pack, shards)
+    firsts = gather_near(first_pack, "shard", shards)
     (second_pack,) = local_call(
         pack_second_kernel,
         [((second_rows, width), low)],
@@ -626,16 +638,20 @@
         flops=heads * rows * rows * 256 * 10,
         name="attend_back",
     )
+    arrived_pair = exchange(send_att, "shard", 1)
+    arrived_pair, arrived_ffn = lax.optimization_barrier((arrived_pair, arrived_ffn))
     keep_att, send_att = local_call(
-        halve_kernel,
-        [((att_rows, width), wide), ((att_rows, width), low)],
-        [kept_att, exchange(send_att, "shard", 1)],
+        functools.partial(halve_kernel, 1, 1),
+        [((1, att_rows, width), wide), ((1, att_rows, width), low)],
+        [kept_att, arrived_pair],
         ids=ids,
         name="halve",
     )
-    arrived_att = [exchange(send_att, "shard", 2)]
     tails = (0, tail)
-    pieces = reduce_replicas([[keep_ffn] + arrived_ffn, [keep_att] + arrived_att], tails)
+    arrived_att = exchange(send_att, "shard", 2)
+    chunk_ffn = split_chunk([keep_ffn] + arrived_ffn, 0, ids, group)
+    chunk_att = split_chunk([keep_att[0], arrived_att[0]], tail, ids, group)
+    pieces = finish_sum([chunk_ffn, chunk_att], ids, group)
     blocks = hidden_count // width
     results = adam_call(
         pieces,
@@ -655,6 +671,7 @@
             (part + blocks * part, 0, matrix_decay),
             (second_rows + 3 * part, TILE_ROWS, 0.0),
         ],
+        ids,
     )
     return (output, input_grad, *results)
 

time: 88.5 us -> 80.3 us (0.907)
  blocking collectives: 29.7 us -> 0 us
  starting transfers between devices: 13.7 us -> 27.4 us
  waiting for transfers between devices: 16 us -> 22.8 us
  Pallas kernels: 23.4 us -> 25.5 us
    all_to_all x2 -> x0, blocking collectives: 29.7 us -> none  [swap_pieces(): lax.all_to_all(pieces, 'dp', 0, 0, axis_index_groups=groups, tiled=True)]
    ppermute x11 -> x22, starting transfers between devices: 7.9 us -> 27.4 us  [exchange(): lax.ppermute(values, axis, [(index, index ^ mask) for index in range(coun...]
    ppermute x11 -> x22, waiting for transfers between devices: 13.4 us -> 22.8 us  [exchange(): lax.ppermute(values, axis, [(index, index ^ mask) for index in range(coun...]
    all_to_all x1 -> x0, starting transfers between devices: 5.81 us -> none  [swap_pieces(): lax.all_to_all(pieces, 'dp', 0, 0, axis_index_groups=groups, tiled=True)]
    all_to_all x1 -> x0, waiting for transfers between devices: 2.64 us -> none  [swap_pieces(): lax.all_to_all(pieces, 'dp', 0, 0, axis_index_groups=groups, tiled=True)]
    pallas_call x10 -> x12, Pallas kernels: 23.4 us -> 25.5 us  [local_call(): pl.pallas_call(kernel, out_shape=outs, in_specs=specs, out_specs=[pl.Bloc...]
    unnamed x46 -> x44, local copies, waits for them, and re-layouts: 4.19 us -> 3.33 us
  transfers between devices with their start and end apart: 12 -> 22, of which waited for: 7 -> 13; matrix products, arithmetic and copies ran while one was open for 0% -> 0% of each run, Pallas kernels for 8% -> 21%
where the time goes in v4:
time: 80.3 us; the launch traced here: 80.1 us
  starting transfers between devices  27.4 us (34%)
  Pallas kernels  25.5 us (32%)
  waiting for transfers between devices  22.8 us (28%)
  local copies, waits for them, and re-layouts  3.33 us (4%)
  between operations  0.97 us (1%)
    ppermute x22, starting transfers between devices, exchange(): lax.ppermute(values, axis, [(index, index ^ mask) for index in range(coun...  27.4 us
    pallas_call x12, Pallas kernels, local_call(): pl.pallas_call(kernel, out_shape=outs, in_specs=specs, out_specs=[pl.Bloc...  25.5 us
    ppermute x22, waiting for transfers between devices, exchange(): lax.ppermute(values, axis, [(index, index ^ mask) for index in range(coun...  22.8 us
    unnamed x44, local copies, waits for them, and re-layouts  3.33 us
  transfers between devices with their start and end apart: 22, of which 13 were waited for; matrix products, arithmetic and copies ran while one was open for 0% of the time, Pallas kernels for 21%

profile of v4, /device:TPU:0, one launch (start us, length us, event | category | flops | bytes accessed | tf_op | source)
XLA Modules:
  0.0 80.1 jit_solution(5606916261465968986)
XLA Ops:
  0.7 1.0 %copy-done.3 = f32[64,768]{1,0:T(8,128)S(1)} copy-done((f32[64,768]{1,0:T(8,128)S(1)}, f32[64,768]{1,0:T(8,128)}, u32[]{:S(2)}) %copy-start.3) | copy-done | bytes 196632
  1.6 0.7 copy-done.14
  2.3 3.0 %collective-permute-start.1 = (bf16[208,256]{1,0:T(8,128)(2,1)S(1)}, bf16[208,256]{1,0:T(8,128)(2,1)S(1)}, u32[]{:S(2)}, u32[]{:S(2)}) collective-permute-start(bf16[208,256]{1,0:T(8,128)(2,1)S(1)} %pack_first.1.refs_3_.refs_5_.refs_8_), channel_id=1, source_target_pairs={{0,2},{1,3},{2,0},{3,1},{4,6},{5,7},{6,4},{7,5},{8,10},{9,11},{10,... | collective-permute-start | bytes 319496 | tf_op jit(solution)/shard_map/ppermute | solution.py:448
  5.4 0.9 %copy-done.1 = f32[256,256]{1,0:T(8,128)S(1)} copy-done((f32[256,256]{1,0:T(8,128)S(1)}, f32[256,256]{1,0:T(8,128)}, u32[]{:S(2)}) %copy-start.1) | copy-done | bytes 262168
  6.4 2.0 %collective-permute-done.1.refs_5_.refs_7_.refs_10_ = bf16[208,256]{1,0:T(8,128)(2,1)S(1)} collective-permute-done((bf16[208,256]{1,0:T(8,128)(2,1)S(1)}, bf16[208,256]{1,0:T(8,128)(2,1)S(1)}, u32[]{:S(2)}, u32[]{:S(2)}) %collective-permute-start.1) | collective-permute-done | bytes 106528 | tf_op jit(solution)/shard_map/ppermute | solution.py:448
  8.3 1.7 %collective-permute-start.3 = (bf16[576,256]{1,0:T(8,128)(2,1)S(1)}, bf16[576,256]{1,0:T(8,128)(2,1)S(1)}, u32[]{:S(2)}, u32[]{:S(2)}) collective-permute-start(bf16[576,256]{1,0:T(8,128)(2,1)S(1)} %pack_second.1.refs_9_), channel_id=1, source_target_pairs={{0,2},{1,3},{2,0},{3,1},{4,6},{5,7},{6,4},{7,5},{8,10},{9,11},{10,... | collective-permute-start | bytes 884744 | tf_op jit(solution)/shard_map/ppermute | solution.py:448
  10.1 0.1 pad_add_fusion.ids
  10.2 0.5 collective-permute-start.4
  10.7 0.7 collective-permute-done.2.refs_6_.refs_8_.refs_11_
  11.4 0.6 copy-done.20
  12.1 0.0 copy-done.21
  12.1 5.9 %attend.1 = (bf16[512,768]{1,0:T(8,128)(2,1)S(1)}, bf16[512,256]{1,0:T(8,128)(2,1)S(1)}, f32[8,512]{1,0:T(8,128)S(1)}) custom-call(s32[3]{0:T(128)S(1)} %pad_add_fusion.ids, bf16[512,256]{1,0:T(8,128)(2,1)S(1)} %copy-done.19, s32[1,128]{1,0:T(1,128)S(1)} %bitcast.9, s32[1,128]{1,0:T(1,128)S(1)} %bitcast.12, ...), custom_call_target="tpu_custom_call" | custom-call | flops 2147483648 | bytes 1754124 | tf_op jit(solution)/shard_map/attend/pallas_call | solution.py:434
  18.0 0.2 collective-permute-start.5
  18.2 1.4 %collective-permute-done.5.refs_12_ = bf16[576,256]{1,0:T(8,128)(2,1)S(1)} collective-permute-done((bf16[576,256]{1,0:T(8,128)(2,1)S(1)}, bf16[576,256]{1,0:T(8,128)(2,1)S(1)}, u32[]{:S(2)}, u32[]{:S(2)}) %collective-permute-start.5) | collective-permute-done | bytes 294944 | tf_op jit(solution)/shard_map/ppermute | solution.py:448
  19.7 4.7 %feed.1 = (bf16[512,256]{1,0:T(8,128)(2,1)}, f32[512,256]{1,0:T(8,128)S(1)}, bf16[512,256]{1,0:T(8,128)(2,1)S(1)}, f32[16,256]{1,0:T(8,128)S(1)}, f32[576,256]{1...) custom-call(s32[3]{0:T(128)S(1)} %pad_add_fusion.ids, ...), custom_call_target="tpu_custom_call" | custom-call | flops 1811939328 | bytes 4932620 | tf_op jit(solution)/shard_map/feed/pallas_call | solution.py:434
  24.3 0.1 collective-permute-start.7
  24.5 0.3 collective-permute-start.8
  24.8 1.4 %collective-permute-start.9 = (bf16[576,256]{1,0:T(8,128)(2,1)S(1)}, bf16[576,256]{1,0:T(8,128)(2,1)S(1)}, u32[]{:S(2)}, u32[]{:S(2)}) collective-permute-start(bf16[576,256]{1,0:T(8,128)(2,1)S(1)} %get-tuple-element.80), channel_id=1, source_target_pairs={{0,3},{1,2},{2,1},{3,0},{4,7},{5,6},{6,5},{7,4},{8,11},{9,10},{10,... | collective-permute-start | bytes 884744 | tf_op jit(solution)/shard_map/ppermute | solution.py:448
  26.2 9.4 %attend_back.1 = (f32[512,256]{1,0:T(8,128)}, f32[2,256,256]{2,1,0:T(8,128)S(1)}, bf16[2,256,256]{2,1,0:T(8,128)(2,1)S(1)}) custom-call(s32[3]{0:T(128)S(1)} %pad_add_fusion.ids, bf16[512,256]{1,0:T(8,128)(2,1)S(1)} %copy-done.19, bf16[512,768]{1,0:T(8,128)(2,1)S(1)} %get-tuple-element.70.refs_1_, bf16[512,256]{1,0:T(8,128)(2,1)S(1)} %get-tuple-element.71.refs_2_, ...), custom_call_target="tpu_custom_call" | custom-call | flops 5368709120 | bytes 3605516 | tf_op jit(solution)/shard_map/attend_back/pallas_call | solution.py:434
  35.6 0.4 collective-permute-start.6
  36.0 1.2 %collective-permute-done.6.refs_1_ = bf16[2,256,256]{2,1,0:T(8,128)(2,1)S(1)} collective-permute-done((bf16[2,256,256]{2,1,0:T(8,128)(2,1)S(1)}, bf16[2,256,256]{2,1,0:T(8,128)(2,1)S(1)}, u32[]{:S(2)}, u32[]{:S(2)}) %collective-permute-start.6) | collective-permute-done | bytes 262176 | tf_op jit(solution)/shard_map/ppermute | solution.py:448
  37.2 2.3 %collective-permute-done.9.refs_3_ = bf16[576,256]{1,0:T(8,128)(2,1)S(1)} collective-permute-done((bf16[576,256]{1,0:T(8,128)(2,1)S(1)}, bf16[576,256]{1,0:T(8,128)(2,1)S(1)}, u32[]{:S(2)}, u32[]{:S(2)}) %collective-permute-start.9) | collective-permute-done | bytes 294944 | tf_op jit(solution)/shard_map/ppermute | solution.py:448
  39.5 0.6 halve.1
  40.1 0.4 collective-permute-start.11
  40.5 0.8 split_sum.2
  41.3 1.8 %collective-permute-start.10 = (bf16[4,72,256]{2,1,0:T(8,128)(2,1)S(1)}, bf16[4,72,256]{2,1,0:T(8,128)(2,1)S(1)}, u32[]{:S(2)}, u32[]{:S(2)}) collective-permute-start(bf16[4,72,256]{2,1,0:T(8,128)(2,1)S(1)} %get-tuple-element.85), channel_id=1, source_target_pairs={{0,4},{4,0},{8,12},{12,8},{16,20},{20,16},{24,28},{28,24},{1,5},{5... | collective-permute-start | bytes 442376 | tf_op jit(solution)/shard_map/ppermute | solution.py:448
  43.1 2.9 %collective-permute-done.11 = bf16[1,256,256]{2,1,0:T(8,128)(2,1)S(1)} collective-permute-done((bf16[1,256,256]{2,1,0:T(8,128)(2,1)S(1)}, bf16[1,256,256]{2,1,0:T(8,128)(2,1)S(1)}, u32[]{:S(2)}, u32[]{:S(2)}) %collective-permute-start.11) | collective-permute-done | bytes 131104 | tf_op jit(solution)/shard_map/ppermute | solution.py:448
  46.0 0.6 split_sum.3
  46.6 1.5 %collective-permute-start.12 = (bf16[4,32,256]{2,1,0:T(8,128)(2,1)S(1)}, bf16[4,32,256]{2,1,0:T(8,128)(2,1)S(1)}, u32[]{:S(2)}, u32[]{:S(2)}) collective-permute-start(bf16[4,32,256]{2,1,0:T(8,128)(2,1)S(1)} %get-tuple-element.91), channel_id=1, source_target_pairs={{0,4},{4,0},{8,12},{12,8},{16,20},{20,16},{24,28},{28,24},{1,5},{5... | collective-permute-start | bytes 196616 | tf_op jit(solution)/shard_map/ppermute | solution.py:448
  48.2 2.8 %collective-permute-done.12.refs_3_ = bf16[4,32,256]{2,1,0:T(8,128)(2,1)S(1)} collective-permute-done((bf16[4,32,256]{2,1,0:T(8,128)(2,1)S(1)}, bf16[4,32,256]{2,1,0:T(8,128)(2,1)S(1)}, u32[]{:S(2)}, u32[]{:S(2)}) %collective-permute-start.12) | collective-permute-done | bytes 65568 | tf_op jit(solution)/shard_map/ppermute | solution.py:448
  51.0 0.6 halve_dp.2
  51.6 1.6 %collective-permute-start.13 = (bf16[2,104,256]{2,1,0:T(8,128)(2,1)S(1)}, bf16[2,104,256]{2,1,0:T(8,128)(2,1)S(1)}, u32[]{:S(2)}, u32[]{:S(2)}) collective-permute-start(bf16[2,104,256]{2,1,0:T(8,128)(2,1)S(1)} %get-tuple-element.93), channel_id=1, source_target_pairs={{0,8},{4,12},{8,0},{12,4},{16,24},{20,28},{24,16},{28,20},{1,9},{5... | collective-permute-start | bytes 319496 | tf_op jit(solution)/shard_map/ppermute | solution.py:448
  53.2 3.2 %collective-permute-done.13.refs_1_ = bf16[2,104,256]{2,1,0:T(8,128)(2,1)S(1)} collective-permute-done((bf16[2,104,256]{2,1,0:T(8,128)(2,1)S(1)}, bf16[2,104,256]{2,1,0:T(8,128)(2,1)S(1)}, u32[]{:S(2)}, u32[]{:S(2)}) %collective-permute-start.13) | collective-permute-done | bytes 106528 | tf_op jit(solution)/shard_map/ppermute | solution.py:448
  56.3 0.6 halve_dp.3
  56.9 2.6 %collective-permute-start.14 = (bf16[1,104,256]{2,1,0:T(8,128)(2,1)S(1)}, bf16[1,104,256]{2,1,0:T(8,128)(2,1)S(1)}, u32[]{:S(2)}, u32[]{:S(2)}) collective-permute-start(bf16[1,104,256]{2,1,0:T(8,128)(2,1)S(1)} %get-tuple-element.95), channel_id=1, source_target_pairs={{0,16},{4,20},{8,24},{12,28},{16,0},{20,4},{24,8},{28,12},{1,17},{... | collective-permute-start | bytes 159752 | tf_op jit(solution)/shard_map/ppermute | solution.py:448
  59.5 2.7 %collective-permute-done.14.other_ref = bf16[1,104,256]{2,1,0:T(8,128)(2,1)S(1)} collective-permute-done((bf16[1,104,256]{2,1,0:T(8,128)(2,1)S(1)}, bf16[1,104,256]{2,1,0:T(8,128)(2,1)S(1)}, u32[]{:S(2)}, u32[]{:S(2)}) %collective-permute-start.14) | collective-permute-done | bytes 53280 | tf_op jit(solution)/shard_map/ppermute | solution.py:448
  62.3 2.7 %collective-permute-start.18 = (bf16[104,256]{1,0:T(8,128)(2,1)S(1)}, bf16[104,256]{1,0:T(8,128)(2,1)S(1)}, u32[]{:S(2)}, u32[]{:S(2)}) collective-permute-start(bf16[104,256]{1,0:T(8,128)(2,1)S(1)} %piece_sum.1.refs_0_), channel_id=1, source_target_pairs={{0,16},{4,20},{8,24},{12,28},{16,0},{20,4},{24,8},{28,12},{1,17},{... | collective-permute-start | bytes 159752 | tf_op jit(solution)/shard_map/ppermute | solution.py:448
  65.0 2.8 %collective-permute-start.16 = (bf16[104,256]{1,0:T(8,128)(2,1)S(1)}, bf16[104,256]{1,0:T(8,128)(2,1)S(1)}, u32[]{:S(2)}, u32[]{:S(2)}) collective-permute-start(bf16[104,256]{1,0:T(8,128)(2,1)S(1)} %piece_sum.1.refs_0_), channel_id=1, source_target_pairs={{0,8},{4,12},{8,0},{12,4},{16,24},{20,28},{24,16},{28,20},{1,9},{5... | collective-permute-start | bytes 159752 | tf_op jit(solution)/shard_map/ppermute | solution.py:448
  67.8 2.1 %collective-permute-start.20 = (bf16[104,256]{1,0:T(8,128)(2,1)S(1)}, bf16[104,256]{1,0:T(8,128)(2,1)S(1)}, u32[]{:S(2)}, u32[]{:S(2)}) collective-permute-start(bf16[104,256]{1,0:T(8,128)(2,1)S(1)} %collective-permute-done.18.refs_4_), channel_id=1, source_target_pairs={{0,8},{4,12},{8,0},{12,4},{16,24},{20,28},{24,16},{28,20},{1,9},{5... | collective-permute-start | bytes 159752 | tf_op jit(solution)/shard_map/ppermute | solution.py:448
  69.9 1.5 %collective-permute-start.15 = (bf16[104,256]{1,0:T(8,128)(2,1)S(1)}, bf16[104,256]{1,0:T(8,128)(2,1)S(1)}, u32[]{:S(2)}, u32[]{:S(2)}) collective-permute-start(bf16[104,256]{1,0:T(8,128)(2,1)S(1)} %piece_sum.1.refs_0_), channel_id=1, source_target_pairs={{0,4},{4,0},{8,12},{12,8},{16,20},{20,16},{24,28},{28,24},{1,5},{5... | collective-permute-start | bytes 159752 | tf_op jit(solution)/shard_map/ppermute | solution.py:448
  71.4 0.5 collective-permute-start.19
  71.9 1.5 %collective-permute-start.17 = (bf16[104,256]{1,0:T(8,128)(2,1)S(1)}, bf16[104,256]{1,0:T(8,128)(2,1)S(1)}, u32[]{:S(2)}, u32[]{:S(2)}) collective-permute-start(bf16[104,256]{1,0:T(8,128)(2,1)S(1)} %collective-permute-done.16.refs_2_), channel_id=1, source_target_pairs={{0,4},{4,0},{8,12},{12,8},{16,20},{20,16},{24,28},{28,24},{1,5},{5... | collective-permute-start | bytes 159752 | tf_op jit(solution)/shard_map/ppermute | solution.py:448
  73.4 0.5 collective-permute-start.21
  73.9 0.1 collective-permute-done.15.refs_1_
  74.0 1.5 %collective-permute-done.19.refs_5_ = bf16[104,256]{1,0:T(8,128)(2,1)S(1)} collective-permute-done((bf16[104,256]{1,0:T(8,128)(2,1)S(1)}, bf16[104,256]{1,0:T(8,128)(2,1)S(1)}, u32[]{:S(2)}, u32[]{:S(2)}) %collective-permute-start.19) | collective-permute-done | bytes 53280 | tf_op jit(solution)/shard_map/ppermute | solution.py:448
  75.5 0.6 collective-permute-done.17.refs_3_
  76.1 1.5 %collective-permute-done.21.refs_7_ = bf16[104,256]{1,0:T(8,128)(2,1)S(1)} collective-permute-done((bf16[104,256]{1,0:T(8,128)(2,1)S(1)}, bf16[104,256]{1,0:T(8,128)(2,1)S(1)}, u32[]{:S(2)}, u32[]{:S(2)}) %collective-permute-start.21) | collective-permute-done | bytes 53280 | tf_op jit(solution)/shard_map/ppermute | solution.py:448
  77.6 2.3 %adam.1 = (f32[64,768]{1,0:T(8,128)}, f32[64,768]{1,0:T(8,128)}, f32[64,768]{1,0:T(8,128)}, f32[64,256]{1,0:T(8,128)}, f32[64,256]{1,0:T(8,128)}, /*index=5*/f32...) custom-call(s32[3]{0:T(128)S(1)} %pad_add_fusion.ids, ...), custom_call_target="tpu_custom_call" | custom-call | bytes 5163020 | tf_op jit(solution)/shard_map/adam/pallas_call | solution.py:434
  (53 shorter events, 0.2 us)
Async XLA Ops:
  0.7 4.7 %copy-start = (f32[64,1024]{1,0:T(8,128)S(1)}, f32[64,1024]{1,0:T(8,128)}, u32[]{:S(2)}) copy-start(f32[64,1024]{1,0:T(8,128)} %refs_14_.1) | copy-start | bytes 786436
  0.7 1.0 %copy-start.3 = (f32[64,768]{1,0:T(8,128)S(1)}, f32[64,768]{1,0:T(8,128)}, u32[]{:S(2)}) copy-start(f32[64,768]{1,0:T(8,128)} %refs_8_.1) | copy-start | bytes 589828
  1.6 0.7 copy-start.14
  2.3 3.1 %copy-start.9 = (f32[64,256]{1,0:T(8,128)S(1)}, f32[64,256]{1,0:T(8,128)}, u32[]{:S(2)}) copy-start(f32[64,256]{1,0:T(8,128)} %refs_11_.1) | copy-start | bytes 196612
  2.3 6.0 %collective-permute-start.1 = (bf16[208,256]{1,0:T(8,128)(2,1)S(1)}, bf16[208,256]{1,0:T(8,128)(2,1)S(1)}, u32[]{:S(2)}, u32[]{:S(2)}) collective-permute-start(bf16[208,256]{1,0:T(8,128)(2,1)S(1)} %pack_first.1.refs_3_.refs_5_.refs_8_), channel_id=1, source_target_pairs={{0,2},{1,3},{2,0},{3,1},{4,6},{5,7},{6,4},{7,5},{8,10},{9,11},{10,... | collective-permute-start | bytes 319496 | tf_op jit(solution)/shard_map/ppermute | solution.py:448
  5.4 5.3 %collective-permute-start = (bf16[208,256]{1,0:T(8,128)(2,1)S(1)}, bf16[208,256]{1,0:T(8,128)(2,1)S(1)}, u32[]{:S(2)}, u32[]{:S(2)}) collective-permute-start(bf16[208,256]{1,0:T(8,128)(2,1)S(1)} %pack_first.1.refs_3_.refs_5_.refs_8_), channel_id=1, source_target_pairs={{0,1},{1,0},{2,3},{3,2},{4,5},{5,4},{6,7},{7,6},{8,9},{9,8},{10,11... | collective-permute-start | bytes 319496 | tf_op jit(solution)/shard_map/ppermute | solution.py:448
  5.4 1.0 %copy-start.1 = (f32[256,256]{1,0:T(8,128)S(1)}, f32[256,256]{1,0:T(8,128)}, u32[]{:S(2)}) copy-start(f32[256,256]{1,0:T(8,128)} %refs_17_.1) | copy-start | bytes 786436
  6.3 5.1 %copy-start.19 = (bf16[512,256]{1,0:T(8,128)(2,1)S(1)}, bf16[512,256]{1,0:T(8,128)(2,1)}, u32[]{:S(2)}) copy-start(bf16[512,256]{1,0:T(8,128)(2,1)} %refs_0_.5) | copy-start | bytes 786436
  8.3 9.7 %collective-permute-start.3 = (bf16[576,256]{1,0:T(8,128)(2,1)S(1)}, bf16[576,256]{1,0:T(8,128)(2,1)S(1)}, u32[]{:S(2)}, u32[]{:S(2)}) collective-permute-start(bf16[576,256]{1,0:T(8,128)(2,1)S(1)} %pack_second.1.refs_9_), channel_id=1, source_target_pairs={{0,2},{1,3},{2,0},{3,1},{4,6},{5,7},{6,4},{7,5},{8,10},{9,11},{10,... | collective-permute-start | bytes 884744 | tf_op jit(solution)/shard_map/ppermute | solution.py:448
  10.1 1.3 %collective-permute-start.2 = (bf16[208,256]{1,0:T(8,128)(2,1)S(1)}, bf16[208,256]{1,0:T(8,128)(2,1)S(1)}, u32[]{:S(2)}, u32[]{:S(2)}) collective-permute-start(bf16[208,256]{1,0:T(8,128)(2,1)S(1)} %collective-permute-done.1.refs_5_.refs_7_.refs_10_), channel_id=1, source_target_pairs={{0,1},{1,0},{2,3},{3,2},{4,5},{5,4},{6,7},{7,6},{8,9},{9,8},{10,11... | collective-permute-start | bytes 319496 | tf_op jit(solution)/shard_map/ppermute | solution.py:448
  10.2 8.1 %collective-permute-start.4 = (bf16[576,256]{1,0:T(8,128)(2,1)S(1)}, bf16[576,256]{1,0:T(8,128)(2,1)S(1)}, u32[]{:S(2)}, u32[]{:S(2)}) collective-permute-start(bf16[576,256]{1,0:T(8,128)(2,1)S(1)} %pack_second.1.refs_9_), channel_id=1, source_target_pairs={{0,1},{1,0},{2,3},{3,2},{4,5},{5,4},{6,7},{7,6},{8,9},{9,8},{10,11... | collective-permute-start | bytes 884744 | tf_op jit(solution)/shard_map/ppermute | solution.py:448
  11.4 0.7 copy-start.20
  11.4 0.7 copy-start.21
  12.1 7.6 %copy-start.18 = (bf16[512,256]{1,0:T(8,128)(2,1)S(1)}, bf16[512,256]{1,0:T(8,128)(2,1)}, u32[]{:S(2)}) copy-start(bf16[512,256]{1,0:T(8,128)(2,1)} %refs_2_.1) | copy-start | bytes 786436
  18.0 1.6 %collective-permute-start.5 = (bf16[576,256]{1,0:T(8,128)(2,1)S(1)}, bf16[576,256]{1,0:T(8,128)(2,1)S(1)}, u32[]{:S(2)}, u32[]{:S(2)}) collective-permute-start(bf16[576,256]{1,0:T(8,128)(2,1)S(1)} %collective-permute-done.3.refs_11_), channel_id=1, source_target_pairs={{0,1},{1,0},{2,3},{3,2},{4,5},{5,4},{6,7},{7,6},{8,9},{9,8},{10,11... | collective-permute-start | bytes 884744 | tf_op jit(solution)/shard_map/ppermute | solution.py:448
  24.3 12.9 %collective-permute-start.7 = (bf16[576,256]{1,0:T(8,128)(2,1)S(1)}, bf16[576,256]{1,0:T(8,128)(2,1)S(1)}, u32[]{:S(2)}, u32[]{:S(2)}) collective-permute-start(bf16[576,256]{1,0:T(8,128)(2,1)S(1)} %get-tuple-element.78), channel_id=1, source_target_pairs={{0,1},{1,0},{2,3},{3,2},{4,5},{5,4},{6,7},{7,6},{8,9},{9,8},{10,11... | collective-permute-start | bytes 884744 | tf_op jit(solution)/shard_map/ppermute | solution.py:448
  24.5 12.7 %collective-permute-start.8 = (bf16[576,256]{1,0:T(8,128)(2,1)S(1)}, bf16[576,256]{1,0:T(8,128)(2,1)S(1)}, u32[]{:S(2)}, u32[]{:S(2)}) collective-permute-start(bf16[576,256]{1,0:T(8,128)(2,1)S(1)} %get-tuple-element.79), channel_id=1, source_target_pairs={{0,2},{1,3},{2,0},{3,1},{4,6},{5,7},{6,4},{7,5},{8,10},{9,11},{10,... | collective-permute-start | bytes 884744 | tf_op jit(solution)/shard_map/ppermute | solution.py:448
  24.8 14.7 %collective-permute-start.9 = (bf16[576,256]{1,0:T(8,128)(2,1)S(1)}, bf16[576,256]{1,0:T(8,128)(2,1)S(1)}, u32[]{:S(2)}, u32[]{:S(2)}) collective-permute-start(bf16[576,256]{1,0:T(8,128)(2,1)S(1)} %get-tuple-element.80), channel_id=1, source_target_pairs={{0,3},{1,2},{2,1},{3,0},{4,7},{5,6},{6,5},{7,4},{8,11},{9,10},{10,... | collective-permute-start | bytes 884744 | tf_op jit(solution)/shard_map/ppermute | solution.py:448
  35.6 1.6 %collective-permute-start.6 = (bf16[2,256,256]{2,1,0:T(8,128)(2,1)S(1)}, bf16[2,256,256]{2,1,0:T(8,128)(2,1)S(1)}, u32[]{:S(2)}, u32[]{:S(2)}) collective-permute-start(bf16[2,256,256]{2,1,0:T(8,128)(2,1)S(1)} %get-tuple-element.77), channel_id=1, source_target_pairs={{0,1},{1,0},{2,3},{3,2},{4,5},{5,4},{6,7},{7,6},{8,9},{9,8},{10,11... | collective-permute-start | bytes 786440 | tf_op jit(solution)/shard_map/ppermute | solution.py:448
  40.1 5.9 %collective-permute-start.11 = (bf16[1,256,256]{2,1,0:T(8,128)(2,1)S(1)}, bf16[1,256,256]{2,1,0:T(8,128)(2,1)S(1)}, u32[]{:S(2)}, u32[]{:S(2)}) collective-permute-start(bf16[1,256,256]{2,1,0:T(8,128)(2,1)S(1)} %get-tuple-element.89), channel_id=1, source_target_pairs={{0,2},{1,3},{2,0},{3,1},{4,6},{5,7},{6,4},{7,5},{8,10},{9,11},{10,... | collective-permute-start | bytes 393224 | tf_op jit(solution)/shard_map/ppermute | solution.py:448
  40.5 37.0 %copy-start.10 = (f32[64,768]{1,0:T(8,128)S(1)}, f32[64,768]{1,0:T(8,128)}, u32[]{:S(2)}) copy-start(f32[64,768]{1,0:T(8,128)} %refs_9_.1) | copy-start | bytes 589828
  40.5 37.0 %copy-start.11 = (f32[64,768]{1,0:T(8,128)S(1)}, f32[64,768]{1,0:T(8,128)}, u32[]{:S(2)}) copy-start(f32[64,768]{1,0:T(8,128)} %refs_10_.1) | copy-start | bytes 589828
  40.5 37.0 %copy-start.13 = (f32[64,256]{1,0:T(8,128)S(1)}, f32[64,256]{1,0:T(8,128)}, u32[]{:S(2)}) copy-start(f32[64,256]{1,0:T(8,128)} %refs_13_.1) | copy-start | bytes 196612
  40.5 37.0 %copy-start.16 = (f32[768]{0:T(1024)S(1)}, f32[768]{0:T(1024)}, u32[]{:S(2)}) copy-start(f32[768]{0:T(1024)} %refs_21_.1) | copy-start | bytes 9220
  40.5 37.1 %copy-start.17 = (f32[768]{0:T(1024)S(1)}, f32[768]{0:T(1024)}, u32[]{:S(2)}) copy-start(f32[768]{0:T(1024)} %refs_22_.1) | copy-start | bytes 9220
  41.3 6.8 %collective-permute-start.10 = (bf16[4,72,256]{2,1,0:T(8,128)(2,1)S(1)}, bf16[4,72,256]{2,1,0:T(8,128)(2,1)S(1)}, u32[]{:S(2)}, u32[]{:S(2)}) collective-permute-start(bf16[4,72,256]{2,1,0:T(8,128)(2,1)S(1)} %get-tuple-element.85), channel_id=1, source_target_pairs={{0,4},{4,0},{8,12},{12,8},{16,20},{20,16},{24,28},{28,24},{1,5},{5... | collective-permute-start | bytes 442376 | tf_op jit(solution)/shard_map/ppermute | solution.py:448
  46.0 31.5 %copy-start.7 = (f32[256,256]{1,0:T(8,128)S(1)}, f32[256,256]{1,0:T(8,128)}, u32[]{:S(2)}) copy-start(f32[256,256]{1,0:T(8,128)} %refs_18_.1) | copy-start | bytes 786436
  46.0 31.5 %copy-start.8 = (f32[256,256]{1,0:T(8,128)S(1)}, f32[256,256]{1,0:T(8,128)}, u32[]{:S(2)}) copy-start(f32[256,256]{1,0:T(8,128)} %refs_19_.1) | copy-start | bytes 786436
  46.6 4.3 %collective-permute-start.12 = (bf16[4,32,256]{2,1,0:T(8,128)(2,1)S(1)}, bf16[4,32,256]{2,1,0:T(8,128)(2,1)S(1)}, u32[]{:S(2)}, u32[]{:S(2)}) collective-permute-start(bf16[4,32,256]{2,1,0:T(8,128)(2,1)S(1)} %get-tuple-element.91), channel_id=1, source_target_pairs={{0,4},{4,0},{8,12},{12,8},{16,20},{20,16},{24,28},{28,24},{1,5},{5... | collective-permute-start | bytes 196616 | tf_op jit(solution)/shard_map/ppermute | solution.py:448
  51.0 26.6 %copy-start.5 = (f32[64,1024]{1,0:T(8,128)S(1)}, f32[64,1024]{1,0:T(8,128)}, u32[]{:S(2)}) copy-start(f32[64,1024]{1,0:T(8,128)} %refs_15_.1) | copy-start | bytes 786436
  51.0 26.6 %copy-start.6 = (f32[64,1024]{1,0:T(8,128)S(1)}, f32[64,1024]{1,0:T(8,128)}, u32[]{:S(2)}) copy-start(f32[64,1024]{1,0:T(8,128)} %refs_16_.1) | copy-start | bytes 786436
  51.6 4.8 %collective-permute-start.13 = (bf16[2,104,256]{2,1,0:T(8,128)(2,1)S(1)}, bf16[2,104,256]{2,1,0:T(8,128)(2,1)S(1)}, u32[]{:S(2)}, u32[]{:S(2)}) collective-permute-start(bf16[2,104,256]{2,1,0:T(8,128)(2,1)S(1)} %get-tuple-element.93), channel_id=1, source_target_pairs={{0,8},{4,12},{8,0},{12,4},{16,24},{20,28},{24,16},{28,20},{1,9},{5... | collective-permute-start | bytes 319496 | tf_op jit(solution)/shard_map/ppermute | solution.py:448
  56.3 21.3 %copy-start.2 = (f32[256,256]{1,0:T(8,128)S(1)}, f32[256,256]{1,0:T(8,128)}, u32[]{:S(2)}) copy-start(f32[256,256]{1,0:T(8,128)} %refs_17_.1) | copy-start | bytes 786436
  56.3 21.3 %copy-start.4 = (f32[64,768]{1,0:T(8,128)S(1)}, f32[64,768]{1,0:T(8,128)}, u32[]{:S(2)}) copy-start(f32[64,768]{1,0:T(8,128)} %refs_8_.1) | copy-start | bytes 589828
  56.9 5.3 %collective-permute-start.14 = (bf16[1,104,256]{2,1,0:T(8,128)(2,1)S(1)}, bf16[1,104,256]{2,1,0:T(8,128)(2,1)S(1)}, u32[]{:S(2)}, u32[]{:S(2)}) collective-permute-start(bf16[1,104,256]{2,1,0:T(8,128)(2,1)S(1)} %get-tuple-element.95), channel_id=1, source_target_pairs={{0,16},{4,20},{8,24},{12,28},{16,0},{20,4},{24,8},{28,12},{1,17},{... | collective-permute-start | bytes 159752 | tf_op jit(solution)/shard_map/ppermute | solution.py:448
  62.2 15.4 %copy-start.12 = (f32[64,256]{1,0:T(8,128)S(1)}, f32[64,256]{1,0:T(8,128)}, u32[]{:S(2)}) copy-start(f32[64,256]{1,0:T(8,128)} %refs_12_.1) | copy-start | bytes 196612
  62.2 15.4 %copy-start.15 = (f32[768]{0:T(1024)S(1)}, f32[768]{0:T(1024)}, u32[]{:S(2)}) copy-start(f32[768]{0:T(1024)} %refs_20_.1) | copy-start | bytes 9220
  62.3 5.5 %collective-permute-start.18 = (bf16[104,256]{1,0:T(8,128)(2,1)S(1)}, bf16[104,256]{1,0:T(8,128)(2,1)S(1)}, u32[]{:S(2)}, u32[]{:S(2)}) collective-permute-start(bf16[104,256]{1,0:T(8,128)(2,1)S(1)} %piece_sum.1.refs_0_), channel_id=1, source_target_pairs={{0,16},{4,20},{8,24},{12,28},{16,0},{20,4},{24,8},{28,12},{1,17},{... | collective-permute-start | bytes 159752 | tf_op jit(solution)/shard_map/ppermute | solution.py:448
  65.0 6.9 %collective-permute-start.16 = (bf16[104,256]{1,0:T(8,128)(2,1)S(1)}, bf16[104,256]{1,0:T(8,128)(2,1)S(1)}, u32[]{:S(2)}, u32[]{:S(2)}) collective-permute-start(bf16[104,256]{1,0:T(8,128)(2,1)S(1)} %piece_sum.1.refs_0_), channel_id=1, source_target_pairs={{0,8},{4,12},{8,0},{12,4},{16,24},{20,28},{24,16},{28,20},{1,9},{5... | collective-permute-start | bytes 159752 | tf_op jit(solution)/shard_map/ppermute | solution.py:448
  67.8 5.6 %collective-permute-start.20 = (bf16[104,256]{1,0:T(8,128)(2,1)S(1)}, bf16[104,256]{1,0:T(8,128)(2,1)S(1)}, u32[]{:S(2)}, u32[]{:S(2)}) collective-permute-start(bf16[104,256]{1,0:T(8,128)(2,1)S(1)} %collective-permute-done.18.refs_4_), channel_id=1, source_target_pairs={{0,8},{4,12},{8,0},{12,4},{16,24},{20,28},{24,16},{28,20},{1,9},{5... | collective-permute-start | bytes 159752 | tf_op jit(solution)/shard_map/ppermute | solution.py:448
  69.9 4.1 %collective-permute-start.15 = (bf16[104,256]{1,0:T(8,128)(2,1)S(1)}, bf16[104,256]{1,0:T(8,128)(2,1)S(1)}, u32[]{:S(2)}, u32[]{:S(2)}) collective-permute-start(bf16[104,256]{1,0:T(8,128)(2,1)S(1)} %piece_sum.1.refs_0_), channel_id=1, source_target_pairs={{0,4},{4,0},{8,12},{12,8},{16,20},{20,16},{24,28},{28,24},{1,5},{5... | collective-permute-start | bytes 159752 | tf_op jit(solution)/shard_map/ppermute | solution.py:448
  71.4 4.1 %collective-permute-start.19 = (bf16[104,256]{1,0:T(8,128)(2,1)S(1)}, bf16[104,256]{1,0:T(8,128)(2,1)S(1)}, u32[]{:S(2)}, u32[]{:S(2)}) collective-permute-start(bf16[104,256]{1,0:T(8,128)(2,1)S(1)} %collective-permute-done.18.refs_4_), channel_id=1, source_target_pairs={{0,4},{4,0},{8,12},{12,8},{16,20},{20,16},{24,28},{28,24},{1,5},{5... | collective-permute-start | bytes 159752 | tf_op jit(solution)/shard_map/ppermute | solution.py:448
  71.9 4.2 %collective-permute-start.17 = (bf16[104,256]{1,0:T(8,128)(2,1)S(1)}, bf16[104,256]{1,0:T(8,128)(2,1)S(1)}, u32[]{:S(2)}, u32[]{:S(2)}) collective-permute-start(bf16[104,256]{1,0:T(8,128)(2,1)S(1)} %collective-permute-done.16.refs_2_), channel_id=1, source_target_pairs={{0,4},{4,0},{8,12},{12,8},{16,20},{20,16},{24,28},{28,24},{1,5},{5... | collective-permute-start | bytes 159752 | tf_op jit(solution)/shard_map/ppermute | solution.py:448
  73.4 4.1 %collective-permute-start.21 = (bf16[104,256]{1,0:T(8,128)(2,1)S(1)}, bf16[104,256]{1,0:T(8,128)(2,1)S(1)}, u32[]{:S(2)}, u32[]{:S(2)}) collective-permute-start(bf16[104,256]{1,0:T(8,128)(2,1)S(1)} %collective-permute-done.20.refs_6_), channel_id=1, source_target_pairs={{0,4},{4,0},{8,12},{12,8},{16,20},{20,16},{24,28},{28,24},{1,5},{5... | collective-permute-start | bytes 159752 | tf_op jit(solution)/shard_map/ppermute | solution.py:448

commit v5 on v4

--- a/solution.py
+++ b/solution.py
@@ -131,38 +131,65 @@
     return row
 
 
-def pack_first_kernel(qkv_ref, small_ref, first_ref):
+def fetch_all(sources, buffers, sems):
+    copies = [
+        pltpu.make_async_copy(source, buffer, sems.at[index])
+        for index, (source, buffer) in enumerate(zip(sources, buffers))
+    ]
+    for copy in copies:
+        copy.start()
+    return copies
+
+
+def pack_first_kernel(qkv_ref, small_ref, first_ref, qkv_buf, small_buf, sems):
     width = first_ref.shape[1]
-    row = put_blocks(first_ref, 0, qkv_ref, width)
+    small_copy, qkv_copy = fetch_all((small_ref, qkv_ref), (small_buf, qkv_buf), sems)
+    small_copy.wait()
     parts = [
-        small_ref[block * width : (block + 1) * width].reshape(1, width)
-        for block in range(small_ref.shape[0] // width)
+        small_buf[block * width : (block + 1) * width].reshape(1, width)
+        for block in range(small_buf.shape[0] // width)
     ]
     parts.append(jnp.zeros((SMALL_PAD - len(parts), width), wide))
-    first_ref[row:, :] = jnp.concatenate(parts, axis=0).astype(low)
-
-
-def pack_second_kernel(out_ref, up_ref, down_ref, second_ref):
+    first_ref[first_ref.shape[0] - SMALL_PAD :, :] = jnp.concatenate(parts, axis=0).astype(low)
+    qkv_copy.wait()
+    put_blocks(first_ref, 0, qkv_buf, width)
+
+
+def pack_second_kernel(out_ref, up_ref, down_ref, second_ref, out_buf, up_buf, down_buf, sems):
     width = second_ref.shape[1]
-    row = put_blocks(second_ref, 0, out_ref, width)
-    row = put_blocks(second_ref, row, up_ref, width)
-    put_blocks(second_ref, row, down_ref, width)
-
-
-def attend_kernel(shards, ids, *refs):
-    x_ref, len_ref, owner_ref = refs[:3]
-    pieces = refs[3 : 3 + shards]
-    joined_ref, out_ref, log_ref, weight_ref, small_ref, bias_ref, att_ref = refs[3 + shards :]
-    rows, width = x_ref.shape
-    shard = ids[1]
+    buffers = (out_buf, up_buf, down_buf)
+    copies = fetch_all((out_ref, up_ref, down_ref), buffers, sems)
+    row = 0
+    for copy, buffer in zip(copies, buffers):
+        copy.wait()
+        row = put_blocks(second_ref, row, buffer, width)
+
+
+def prepare_kernel(shards, x_ref, seed_ref, len_ref, owner_ref, bias_ref, norm_ref, root_ref, low_ref):
+    rows = x_ref.shape[0]
+    device = lax.axis_index("dp") * shards + lax.axis_index("shard")
+    own = own_row(len_ref[...], owner_ref[...], device)
+    fill_mask(bias_ref, own, rows)
+    normed, root = standardize(x_ref[...].astype(wide))
+    norm_ref[...] = normed
+    root_ref[...] = root
+    live = jnp.sum(own, axis=1, keepdims=True)
+    live_rows = (iota((rows, 1), 0) < live).astype(wide)
+    low_ref[...] = (seed_ref[...].astype(wide) * live_rows).astype(low)
+
+
+def attend_kernel(shards, *refs):
+    norm_ref, bias_ref = refs[:2]
+    pieces = refs[2 : 2 + shards]
+    joined_ref, out_ref, log_ref, weight_ref, small_ref, att_ref = refs[2 + shards :]
+    rows, width = norm_ref.shape
+    shard = lax.axis_index("shard")
     part = width // shards
     fill_cols(weight_ref, shard, pieces, 0, part, width)
     fill_small(small_ref, shard, pieces, 3 * part)
     gain, shift = small_ref[0, 0:1, :], small_ref[0, 1:2, :]
     bias_query, bias_value = small_ref[1, 1:2, :], small_ref[1, 2:3, :]
-    fill_mask(bias_ref, own_row(len_ref[...], owner_ref[...], ids[0]), rows)
-    normed, _ = standardize(x_ref[...].astype(wide))
-    hidden = (normed * gain + shift).astype(low)
+    hidden = (norm_ref[...] * gain + shift).astype(low)
     for block, bias in enumerate((bias_query, None, bias_value)):
         cols = slice(block * width, (block + 1) * width)
         value = dot_nn(hidden, weight_ref[:, cols])
@@ -186,17 +213,16 @@
     out_ref[...] = att_ref[...].T
 
 
-def feed_kernel(shards, ids, *refs):
-    x_ref, att_ref, seed_ref, len_ref, owner_ref = refs[:5]
-    firsts = refs[5 : 5 + shards]
-    pieces = refs[5 + shards : 5 + 2 * shards]
-    refs = refs[5 + 2 * shards :]
-    out_ref, middle_ref, dattend_ref, sums_ref, keep_ref = refs[:5]
-    sends = refs[5 : 4 + shards]
-    small_ref, out_w, up_w, down_w, grads_ref = refs[4 + shards :]
+def feed_kernel(shards, *refs):
+    x_ref, att_ref, seed_ref = refs[:3]
+    firsts = refs[3 : 3 + shards]
+    pieces = refs[3 + shards : 3 + 2 * shards]
+    refs = refs[3 + 2 * shards :]
+    out_ref, middle_ref, dattend_ref, sums_ref, keep_ref, send_ref = refs[:6]
+    small_ref, out_w, up_w, down_w, grads_ref = refs[6:]
     rows, width = x_ref.shape
     hidden_count = up_w.shape[1]
-    shard = ids[1]
+    shard = lax.axis_index("shard")
     part = width // shards
     blocks = hidden_count // width
     down_part = hidden_count // shards
@@ -207,10 +233,8 @@
     gain, shift = small_ref[0, 2:3, :], small_ref[1, 0:1, :]
     bias_out, bias_down = small_ref[2, 0:1, :], small_ref[2, 1:2, :]
     bias_up = [small_ref[2, 2:3, :]] + [small_ref[3, row : row + 1, :] for row in range(3)]
-    live = jnp.sum(own_row(len_ref[...], owner_ref[...], ids[0]), axis=1, keepdims=True)
-    live_rows = (iota((rows, 1), 0) < live).astype(wide)
-    seed = seed_ref[...].astype(wide) * live_rows
-    seed_low = seed.astype(low)
+    seed_low = seed_ref[...]
+    seed = seed_low.astype(wide)
     attended = att_ref[...]
     middle = x_ref[...].astype(wide) + (dot_nn(attended, out_w[...]) + bias_out)
     normed, root = standardize(middle)
@@ -256,34 +280,31 @@
     sums_ref[0:1, :] = gain_grad
     sums_ref[1:2, :] = shift_grad
     sums_ref[2:3, :] = jnp.sum(dmiddle_low.astype(wide), axis=0, keepdims=True)
-    sums_ref[3:4, :] = jnp.sum(seed_low.astype(wide), axis=0, keepdims=True)
-    keep_ref[...] = grads_ref[shard]
-    for offset in range(1, shards):
-        sends[offset - 1][...] = grads_ref[shard ^ offset].astype(low)
-
-
-def attend_back_kernel(shards, ids, *refs):
-    x_ref, joined_ref, dattend_ref, log_ref, middle_ref, sums_in, len_ref, owner_ref = refs[:8]
-    pieces = refs[8 : 8 + shards]
-    refs = refs[8 + shards :]
-    dx_ref, keep_ref, send_ref = refs[:3]
-    weight_ref, small_ref, bias_ref, dquery_t, dkey, dvalue, djoined, grads_ref = refs[3:]
-    rows, width = x_ref.shape
-    shard = ids[1]
-    part = width // shards
-    fill_cols(weight_ref, shard, pieces, 0, part, width)
-    fill_small(small_ref, shard, pieces, 3 * part)
-    gain, shift = small_ref[0, 0:1, :], small_ref[0, 1:2, :]
-    fill_mask(bias_ref, own_row(len_ref[...], owner_ref[...], ids[0]), rows)
-    keys_t = joined_ref[:, width : 2 * width].T
+    sums_ref[3:4, :] = jnp.sum(seed, axis=0, keepdims=True)
+    part_ways(grads_ref, keep_ref, send_ref, shard % 2)
+
+
+def part_ways(grads_ref, keep_ref, send_ref, side):
+    for pair in range(keep_ref.shape[0]):
+        keep_ref[pair] = grads_ref[2 * pair + side]
+        send_ref[pair] = grads_ref[2 * pair + 1 - side].astype(low)
+
+
+def back_tile(tile_index, joined_ref, dattend_ref, log_ref, bias_ref, dquery_t, dkey, dvalue):
+    rows = joined_ref.shape[0]
+    width = joined_ref.shape[1] // 3
+    first = tile_index * LANES
+    tile = slice(first, first + LANES)
+    keys_t = joined_ref[:, width + first : width + first + LANES].T
     dkey[...] = jnp.zeros(dkey.shape, wide)
     dvalue[...] = jnp.zeros(dvalue.shape, wide)
-    for head in range(width // HEAD):
-        tile = head_tile(head)
+    per_tile = LANES // HEAD
+    for local in range(per_tile):
+        head = tile_index * per_tile + local
         mask = head_mask(head)
-        key_tile = joined_ref[:, width + tile.start : width + tile.stop] * mask
-        value_tile = joined_ref[:, 2 * width + tile.start : 2 * width + tile.stop] * mask
-        feature = slice(head * HEAD, (head + 1) * HEAD)
+        key_tile = joined_ref[:, width + first : width + first + LANES] * mask
+        value_tile = joined_ref[:, 2 * width + first : 2 * width + first + LANES] * mask
+        feature = slice(local * HEAD, (local + 1) * HEAD)
         for start, stop in query_blocks(rows):
             query = joined_ref[start:stop, tile]
             datt = dattend_ref[start:stop, tile]
@@ -296,12 +317,38 @@
             dquery_t[feature, start:stop] = (
                 dot_nn(keys_t[feature, :stop], dscores) * score_scale
             ).astype(low)
-            dvalue[:stop, tile] += dot_nn(probs.astype(low), datt * mask)
-            dkey[:stop, tile] += dot_nn(dscores, query * mask)
-    djoined[:, :width] = dquery_t[...].T
-    djoined[:, width : 2 * width] = (dkey[...] * score_scale).astype(low)
-    djoined[:, 2 * width :] = dvalue[...].astype(low)
-    normed, root = standardize(x_ref[...].astype(wide))
+            dvalue[:stop, :] += dot_nn(probs.astype(low), datt * mask)
+            dkey[:stop, :] += dot_nn(dscores, query * mask)
+    return dquery_t[...].T, (dkey[...] * score_scale).astype(low), dvalue[...].astype(low)
+
+
+def back_first_kernel(joined_ref, dattend_ref, log_ref, bias_ref, *refs):
+    results, scratch = refs[:3], refs[3:]
+    values = back_tile(0, joined_ref, dattend_ref, log_ref, bias_ref, *scratch)
+    for target, value in zip(results, values):
+        target[...] = value
+
+
+def back_last_kernel(shards, *refs):
+    joined_ref, dattend_ref, log_ref, bias_ref = refs[:4]
+    earlier = refs[4:7]
+    norm_ref, root_ref, middle_ref, sums_in = refs[7:11]
+    pieces = refs[11 : 11 + shards]
+    refs = refs[11 + shards :]
+    dx_ref, keep_ref, send_ref = refs[:3]
+    weight_ref, small_ref, dquery_t, dkey, dvalue, djoined, grads_ref = refs[3:]
+    rows, width = norm_ref.shape
+    shard = lax.axis_index("shard")
+    part = width // shards
+    fill_cols(weight_ref, shard, pieces, 0, part, width)
+    fill_small(small_ref, shard, pieces, 3 * part)
+    gain, shift = small_ref[0, 0:1, :], small_ref[0, 1:2, :]
+    values = back_tile(1, joined_ref, dattend_ref, log_ref, bias_ref, dquery_t, dkey, dvalue)
+    for block in range(3):
+        at = block * width
+        djoined[:, at : at + LANES] = earlier[block][...]
+        djoined[:, at + LANES : at + 2 * LANES] = values[block]
+    normed, root = norm_ref[...], root_ref[...]
     hidden_t = (normed * gain + shift).astype(low).T
     dhidden = jnp.zeros((rows, width), wide)
     bias_sums = []
@@ -328,16 +375,13 @@
             grads_ref[target, at + row * TILE_ROWS : at + row * TILE_ROWS + 1, :] = sums[
                 target * per_shard + row
             ]
-    side = shard % 2
-    for pair in range(shards // 2):
-        keep_ref[pair] = grads_ref[2 * pair + side]
-        send_ref[pair] = grads_ref[2 * pair + 1 - side].astype(low)
-
-
-def halve_kernel(which, bit, ids, *refs):
+    part_ways(grads_ref, keep_ref, send_ref, shard % 2)
+
+
+def halve_kernel(axis, bit, *refs):
     count = (len(refs) - 2) // 2
     keep_ref, send_ref = refs[-2:]
-    side = (ids[which] >> bit) & 1
+    side = (lax.axis_index(axis) >> bit) & 1
     for pair in range(keep_ref.shape[0]):
         for target, index in ((keep_ref, 2 * pair + side), (send_ref, 2 * pair + 1 - side)):
             parts = []
@@ -355,7 +399,7 @@
     return spans
 
 
-def split_kernel(tail, ids, *refs):
+def split_kernel(tail, *refs):
     arrived, keep_ref, send_ref, sum_ref = refs[:-3], *refs[-3:]
     group = sum_ref.shape[0]
     total = arrived[0][...]
@@ -367,7 +411,7 @@
             at = first + index * rows
             sum_ref[index, row : row + rows, :] = total[at : at + rows, :]
             row += rows
-    side = ids[2] & 1
+    side = lax.axis_index("dp") & 1
     for pair in range(group // 2):
         keep_ref[pair] = sum_ref[2 * pair + side]
         send_ref[pair] = sum_ref[2 * pair + 1 - side].astype(low)
@@ -389,7 +433,7 @@
     return first_next, second_next, weight - learn_rate * (update + decay_rate * weight)
 
 
-def adam_kernel(group, spans, layout, ids, *refs):
+def adam_kernel(group, spans, layout, *refs):
     pieces = refs[:group]
     grad_ref = refs[-1]
     count = len(layout)
@@ -397,7 +441,7 @@
     results = refs[group + 3 * count : -1]
     for offset, piece in enumerate(pieces):
         value = piece[...].astype(wide)
-        index = ids[2] ^ offset
+        index = (lax.axis_index("dp") & (group - 1)) ^ offset
         for rows, first, row in spans:
             at = pl.multiple_of(first + index * rows, TILE_ROWS)
             grad_ref[pl.ds(at, rows), :] = value[row : row + rows, :]
@@ -422,21 +466,21 @@
                 target[where] = value.reshape(width) if vector else value
 
 
-def local_call(kernel, outs, operands, scratch=(), ids=None, flops=0, name=None):
-    specs = [pl.BlockSpec(memory_space=pltpu.VMEM)] * len(operands)
-    if ids is not None:
-        operands = [ids] + list(operands)
-        specs = [pl.BlockSpec(memory_space=pltpu.SMEM)] + specs
+def local_call(kernel, outs, operands, scratch=(), flops=0, name=None, fetch=False):
+    space = pl.ANY if fetch else pltpu.VMEM
     outs = [jax.ShapeDtypeStruct(*out) for out in outs]
     moved = sum(
         math.prod(item.shape) * item.dtype.itemsize for item in list(operands) + outs
     )
+    scratch_shapes = [pltpu.VMEM(*item) for item in scratch]
+    if fetch:
+        scratch_shapes.append(pltpu.SemaphoreType.DMA((len(operands),)))
     return pl.pallas_call(
         kernel,
         out_shape=outs,
-        in_specs=specs,
+        in_specs=[pl.BlockSpec(memory_space=space)] * len(operands),
         out_specs=[pl.BlockSpec(memory_space=pltpu.VMEM)] * len(outs),
-        scratch_shapes=[pltpu.VMEM(*item) for item in scratch],
+        scratch_shapes=scratch_shapes,
         compiler_params=pltpu.CompilerParams(vmem_limit_bytes=40 * 1024 * 1024),
         cost_estimate=pl.CostEstimate(flops=flops, bytes_accessed=moved, transcendentals=0),
         name=name,
@@ -458,11 +502,15 @@
     return [found[offset] for offset in range(count)]
 
 
-def swap_all(values, axis):
-    return [exchange(value, axis, offset + 1) for offset, value in enumerate(values)]
-
-
-def split_chunk(chunk, tail, ids, group):
+def halve_call(axis, bit, flat, name):
+    half, _, width = flat[0].shape
+    shape = (half // 2, sum(item.shape[1] for item in flat[::2]), width)
+    return local_call(
+        functools.partial(halve_kernel, axis, bit), [(shape, wide), (shape, low)], flat, name=name
+    )
+
+
+def split_chunk(chunk, tail, group):
     rows, width = chunk[0].shape
     half = (group // 2, rows // group, width)
     keep, send = local_call(
@@ -470,13 +518,12 @@
         [(half, wide), (half, low)],
         chunk,
         [((group,) + half[1:], wide)],
-        ids,
         name="split_sum",
     )
     return keep, exchange(send, "dp", 1)
 
 
-def finish_sum(chunks, ids, group):
+def finish_sum(chunks, group):
     replicas = lax.axis_size("dp")
     half, _, width = chunks[0][0].shape
     rows = sum(chunk[0].shape[1] for chunk in chunks)
@@ -484,13 +531,7 @@
     bit = 1
     while half > 1:
         half //= 2
-        keep, send = local_call(
-            functools.partial(halve_kernel, 2, bit),
-            [((half, rows, width), wide), ((half, rows, width), low)],
-            flat,
-            ids=ids,
-            name="halve_dp",
-        )
+        keep, send = halve_call("dp", bit, flat, "halve_dp")
         flat = [keep, exchange(send, "dp", 1 << bit)]
         bit += 1
     mask = group
@@ -502,7 +543,7 @@
     return gather_near(piece, "dp", group)
 
 
-def adam_call(pieces, counts, tails, states, layout, ids):
+def adam_call(pieces, counts, tails, states, layout):
     group = len(pieces)
     width = pieces[0].shape[1]
     spans = []
@@ -517,7 +558,6 @@
         [(state[0].shape, wide) for state in states for _ in range(3)],
         pieces + [item for state in states for item in state],
         [((first, width), wide)],
-        ids,
         name="adam",
     )
 
@@ -548,10 +588,7 @@
     heads = width // HEAD
     part = qkv_weight.shape[0]
     hidden_count = up_weight.shape[1]
-    device = lax.axis_index(("dp", "shard"))
     group = min(GROUP, lax.axis_size("dp"))
-    ids = jnp.stack([device, lax.axis_index("shard"), lax.axis_index("dp") % group])
-    ids = ids.astype(jnp.int32)
     lengths = lengths.reshape(1, -1)
     seq_owner = seq_owner.reshape(1, -1)
     first_rows = 3 * part + SMALL_PAD
@@ -560,48 +597,58 @@
         pack_first_kernel,
         [((first_rows, width), low)],
         [qkv_weight, gains_biases],
+        [(qkv_weight.shape, wide), (gains_biases.shape, wide)],
         name="pack_first",
+        fetch=True,
     )
     firsts = gather_near(first_pack, "shard", shards)
+    square = (rows, rows)
+    bias, normed, root, seed = local_call(
+        functools.partial(prepare_kernel, shards),
+        [(square, wide), ((rows, width), wide), ((rows, 1), wide), ((rows, width), low)],
+        [tokens, cotangent, lengths, seq_owner],
+        name="prepare",
+    )
+    matrices = [out_weight, up_weight, down_weight]
     (second_pack,) = local_call(
         pack_second_kernel,
         [((second_rows, width), low)],
-        [out_weight, up_weight, down_weight],
+        matrices,
+        [(item.shape, wide) for item in matrices],
         name="pack_second",
+        fetch=True,
     )
     firsts[2], second_pack = lax.optimization_barrier((firsts[2], second_pack))
     seconds = {0: second_pack}
     seconds[2] = exchange(second_pack, "shard", 2)
     seconds[1] = exchange(second_pack, "shard", 1)
-    square = (rows, rows)
     joined, attended, log_sums = local_call(
         functools.partial(attend_kernel, shards),
         [((rows, 3 * width), low), ((rows, width), low), ((heads, rows), wide)],
-        [tokens, lengths, seq_owner] + firsts,
+        [normed, bias] + firsts,
         [
             ((width, 3 * width), low),
             ((shards, SMALL_PAD, width), wide),
-            (square, wide),
             ((width, rows), low),
         ],
-        ids,
         flops=heads * rows * rows * 256 * 4,
         name="attend",
     )
     attended, seconds[2] = lax.optimization_barrier((attended, seconds[2]))
     seconds[3] = exchange(seconds[2], "shard", 1)
     seconds = [seconds[offset] for offset in range(shards)]
-    output, middle_grad, attended_grad, sums, keep_ffn, *sends_ffn = local_call(
+    pair = (shards // 2, second_rows, width)
+    output, middle_grad, attended_grad, sums, kept_ffn, send_ffn = local_call(
         functools.partial(feed_kernel, shards),
         [
             ((rows, width), low),
             ((rows, width), wide),
             ((rows, width), low),
             ((SMALL_PAD, width), wide),
-            ((second_rows, width), wide),
-        ]
-        + [((second_rows, width), low)] * (shards - 1),
-        [tokens, attended, cotangent, lengths, seq_owner] + firsts + seconds,
+            (pair, wide),
+            (pair, low),
+        ],
+        [tokens, attended, seed] + firsts + seconds,
         [
             ((shards, SMALL_PAD, width), wide),
             ((width, width), low),
@@ -609,49 +656,45 @@
             ((hidden_count, width), low),
             ((shards, second_rows, width), wide),
         ],
-        ids,
         flops=rows * width * (hidden_count * 12 + width * 6),
         name="feed",
     )
-    arrived_ffn = swap_all(sends_ffn, "shard")
+    arrived_ffn = exchange(send_ffn, "shard", 1)
+    shared = [joined, attended_grad, log_sums, bias]
+    tile_scratch = [((LANES, rows), low), ((rows, LANES), wide), ((rows, LANES), wide)]
+    first_query, first_key, first_value = local_call(
+        back_first_kernel,
+        [((rows, LANES), low)] * 3,
+        shared,
+        tile_scratch,
+        flops=heads * rows * rows * 256 * 5,
+        name="back_first",
+    )
+    first_query, arrived_ffn = lax.optimization_barrier((first_query, arrived_ffn))
+    keep_ffn, send_ffn = halve_call("shard", 1, [kept_ffn, arrived_ffn], "halve_ffn")
+    first_query, send_ffn = lax.optimization_barrier((first_query, send_ffn))
+    arrived_ffn = exchange(send_ffn, "shard", 2)
     tail = GROUP * TILE_ROWS
     att_rows = 3 * part + tail
+    pair = (shards // 2, att_rows, width)
     input_grad, kept_att, send_att = local_call(
-        functools.partial(attend_back_kernel, shards),
-        [
-            ((rows, width), wide),
-            ((shards // 2, att_rows, width), wide),
-            ((shards // 2, att_rows, width), low),
-        ],
-        [tokens, joined, attended_grad, log_sums, middle_grad, sums, lengths, seq_owner] + firsts,
-        [
-            ((width, 3 * width), low),
-            ((shards, SMALL_PAD, width), wide),
-            (square, wide),
-            ((width, rows), low),
-            ((rows, width), wide),
-            ((rows, width), wide),
-            ((rows, 3 * width), low),
-            ((shards, att_rows, width), wide),
-        ],
-        ids,
-        flops=heads * rows * rows * 256 * 10,
-        name="attend_back",
-    )
-    arrived_pair = exchange(send_att, "shard", 1)
-    arrived_pair, arrived_ffn = lax.optimization_barrier((arrived_pair, arrived_ffn))
-    keep_att, send_att = local_call(
-        functools.partial(halve_kernel, 1, 1),
-        [((1, att_rows, width), wide), ((1, att_rows, width), low)],
-        [kept_att, arrived_pair],
-        ids=ids,
-        name="halve",
-    )
+        functools.partial(back_last_kernel, shards),
+        [((rows, width), wide), (pair, wide), (pair, low)],
+        shared + [first_query, first_key, first_value, normed, root, middle_grad, sums] + firsts,
+        [((width, 3 * width), low), ((shards, SMALL_PAD, width), wide)]
+        + tile_scratch
+        + [((rows, 3 * width), low), ((shards, att_rows, width), wide)],
+        flops=heads * rows * rows * 256 * 6,
+        name="back_last",
+    )
+    arrived_att = exchange(send_att, "shard", 1)
+    keep_att, send_att = halve_call("shard", 1, [kept_att, arrived_att], "halve_att")
+    send_att, arrived_ffn = lax.optimization_barrier((send_att, arrived_ffn))
     tails = (0, tail)
     arrived_att = exchange(send_att, "shard", 2)
-    chunk_ffn = split_chunk([keep_ffn] + arrived_ffn, 0, ids, group)
-    chunk_att = split_chunk([keep_att[0], arrived_att[0]], tail, ids, group)
-    pieces = finish_sum([chunk_ffn, chunk_att], ids, group)
+    chunk_ffn = split_chunk([keep_ffn[0], arrived_ffn[0]], 0, group)
+    chunk_att = split_chunk([keep_att[0], arrived_att[0]], tail, group)
+    pieces = finish_sum([chunk_ffn, chunk_att], group)
     blocks = hidden_count // width
     results = adam_call(
         pieces,
@@ -671,7 +714,6 @@
             (part + blocks * part, 0, matrix_decay),
             (second_rows + 3 * part, TILE_ROWS, 0.0),
         ],
-        ids,
     )
     return (output, input_grad, *results)
 

time: 80.3 us -> 77.4 us (0.964)
  Pallas kernels: 25.5 us -> 21.6 us
  waiting for transfers between devices: 22.8 us -> 19.9 us
  local copies, waits for them, and re-layouts: 3.33 us -> 5.39 us
  starting transfers between devices: 27.4 us -> 29.2 us
    pallas_call x12 -> x15, Pallas kernels: 25.5 us -> 21.6 us  [local_call(): pl.pallas_call(kernel, out_shape=outs, in_specs=[pl.BlockSpec(memory_spac...]
    ppermute x22 -> x21, waiting for transfers between devices: 22.8 us -> 19.9 us  [exchange(): lax.ppermute(values, axis, [(index, index ^ mask) for index in range(coun...]
    unnamed x44 -> x50, local copies, waits for them, and re-layouts: 3.33 us -> 5.39 us
    ppermute x22 -> x21, starting transfers between devices: 27.4 us -> 29.2 us  [exchange(): lax.ppermute(values, axis, [(index, index ^ mask) for index in range(coun...]
  transfers between devices with their start and end apart: 22 -> 21, of which waited for: 13 -> 13; matrix products, arithmetic and copies ran while one was open for 0% -> 0% of each run, Pallas kernels for 21% -> 20%
where the time goes in v5:
time: 77.4 us; the launch traced here: 77.1 us
  starting transfers between devices  29.2 us (38%)
  Pallas kernels  21.6 us (28%)
  waiting for transfers between devices  19.9 us (26%)
  local copies, waits for them, and re-layouts  5.39 us (7%)
  between operations  1 us (1%)
    ppermute x21, starting transfers between devices, exchange(): lax.ppermute(values, axis, [(index, index ^ mask) for index in range(coun...  29.2 us
    pallas_call x15, Pallas kernels, local_call(): pl.pallas_call(kernel, out_shape=outs, in_specs=[pl.BlockSpec(memory_spac...  21.6 us
    ppermute x21, waiting for transfers between devices, exchange(): lax.ppermute(values, axis, [(index, index ^ mask) for index in range(coun...  19.9 us
    unnamed x50, local copies, waits for them, and re-layouts  5.39 us
  transfers between devices with their start and end apart: 21, of which 13 were waited for; matrix products, arithmetic and copies ran while one was open for 0% of the time, Pallas kernels for 20%

profile of v5, /device:TPU:0, one launch (start us, length us, event | category | flops | bytes accessed | tf_op | source)
XLA Modules:
  0.0 77.1 jit_solution(15516821042235992911)
XLA Ops:
  0.7 0.9 %copy-done.4 = f32[64,768]{1,0:T(8,128)S(1)} copy-done((f32[64,768]{1,0:T(8,128)S(1)}, f32[64,768]{1,0:T(8,128)}, u32[]{:S(2)}) %copy-start.4) | copy-done | bytes 196632
  1.6 0.7 copy-done.19
  2.3 0.3 pack_first.1.refs_2_.refs_3_.refs_11_
  2.6 3.0 %collective-permute-start.1 = (bf16[208,256]{1,0:T(8,128)(2,1)S(1)}, bf16[208,256]{1,0:T(8,128)(2,1)S(1)}, u32[]{:S(2)}, u32[]{:S(2)}) collective-permute-start(bf16[208,256]{1,0:T(8,128)(2,1)S(1)} %pack_first.1.refs_2_.refs_3_.refs_11_), channel_id=1, source_target_pairs={{0,2},{1,3},{2,0},{3,1},{4,6},{5,7},{6,4},{7,5},{8,10},{9,11},{10,... | collective-permute-start | bytes 319496 | tf_op jit(solution)/shard_map/ppermute | solution.py:492
  5.6 3.0 %collective-permute-done.1.refs_4_.refs_5_.refs_13_ = bf16[208,256]{1,0:T(8,128)(2,1)S(1)} collective-permute-done((bf16[208,256]{1,0:T(8,128)(2,1)S(1)}, bf16[208,256]{1,0:T(8,128)(2,1)S(1)}, u32[]{:S(2)}, u32[]{:S(2)}) %collective-permute-start.1) | collective-permute-done | bytes 106528 | tf_op jit(solution)/shard_map/ppermute | solution.py:492
  8.6 0.9 %copy-done = f32[64,1024]{1,0:T(8,128)S(1)} copy-done((f32[64,1024]{1,0:T(8,128)S(1)}, f32[64,1024]{1,0:T(8,128)}, u32[]{:S(2)}) %copy-start) | copy-done | bytes 262168
  9.5 0.9 %copy-done.2 = f32[256,256]{1,0:T(8,128)S(1)} copy-done((f32[256,256]{1,0:T(8,128)S(1)}, f32[256,256]{1,0:T(8,128)}, u32[]{:S(2)}) %copy-start.2) | copy-done | bytes 262168
  10.5 0.8 %copy-done.6 = f32[64,256]{1,0:T(8,128)S(1)} copy-done((f32[64,256]{1,0:T(8,128)S(1)}, f32[64,256]{1,0:T(8,128)}, u32[]{:S(2)}) %copy-start.6) | copy-done | bytes 65560
  11.3 0.1 pack_second.1.refs_7_
  11.5 1.8 %collective-permute-start.3 = (bf16[576,256]{1,0:T(8,128)(2,1)S(1)}, bf16[576,256]{1,0:T(8,128)(2,1)S(1)}, u32[]{:S(2)}, u32[]{:S(2)}) collective-permute-start(bf16[576,256]{1,0:T(8,128)(2,1)S(1)} %pack_second.1.refs_7_), channel_id=1, source_target_pairs={{0,2},{1,3},{2,0},{3,1},{4,6},{5,7},{6,4},{7,5},{8,10},{9,11},{10,... | collective-permute-start | bytes 884744 | tf_op jit(solution)/shard_map/ppermute | solution.py:492
  13.3 0.9 %copy-done.9 = bf16[512,256]{1,0:T(8,128)(2,1)S(1)} copy-done((bf16[512,256]{1,0:T(8,128)(2,1)S(1)}, bf16[512,256]{1,0:T(8,128)(2,1)}, u32[]{:S(2)}) %copy-start.9) | copy-done | bytes 262168
  14.2 0.6 prepare.1
  14.9 0.3 collective-permute-start.4
  15.2 5.2 %attend.1 = (bf16[512,768]{1,0:T(8,128)(2,1)S(1)}, bf16[512,256]{1,0:T(8,128)(2,1)S(1)}, f32[8,512]{1,0:T(8,128)S(1)}) custom-call(f32[512,256]{1,0:T(8,128)S(1)} %get-tuple-element.73.refs_0_.refs_7_, f32[512,512]{1,0:T(8,128)S(1)} %get-tuple-element.74.refs_1_.bias_ref.refs_3_, bf16[208,256]{1,0:T(8,128)(2,1)S(1)} %pack_first.1.refs_2_.refs_3_.refs_11_, ...), custom_call_target="tpu_custom_call" | custom-call | flops 2147483648 | bytes 3063808 | tf_op jit(solution)/shard_map/attend/pallas_call | solution.py:478
  20.4 0.6 collective-permute-done.3.refs_9_
  21.0 1.6 %collective-permute-done.5.refs_10_ = bf16[576,256]{1,0:T(8,128)(2,1)S(1)} collective-permute-done((bf16[576,256]{1,0:T(8,128)(2,1)S(1)}, bf16[576,256]{1,0:T(8,128)(2,1)S(1)}, u32[]{:S(2)}, u32[]{:S(2)}) %collective-permute-start.5) | collective-permute-done | bytes 294944 | tf_op jit(solution)/shard_map/ppermute | solution.py:492
  22.5 4.1 %feed.1 = (bf16[512,256]{1,0:T(8,128)(2,1)}, f32[512,256]{1,0:T(8,128)S(1)}, bf16[512,256]{1,0:T(8,128)(2,1)S(1)}, f32[16,256]{1,0:T(8,128)S(1)}, f32[2,576,256]...) custom-call(bf16[512,256]{1,0:T(8,128)(2,1)S(1)} %copy-done.10, bf16[512,256]{1,0:T(8,128)(2,1)S(1)} %get-tuple-element.78.refs_1_, ...), custom_call_target="tpu_custom_call" | custom-call | flops 1811939328 | bytes 5226496 | tf_op jit(solution)/shard_map/feed/pallas_call | solution.py:478
  26.7 0.2 collective-permute-start.6
  26.8 3.7 %back_first.1 = (bf16[512,128]{1,0:T(8,128)(2,1)S(1)}, bf16[512,128]{1,0:T(8,128)(2,1)S(1)}, bf16[512,128]{1,0:T(8,128)(2,1)S(1)}) custom-call(bf16[512,768]{1,0:T(8,128)(2,1)S(1)} %get-tuple-element.82.joined_ref.refs_0_, bf16[512,256]{1,0:T(8,128)(2,1)S(1)} %get-tuple-element.83.dattend_ref.refs_1_, f32[8,512]{1,0:T(8,128)S(1)} %get-tuple-element.84.log_ref.refs_2_, ...), custom_call_target="tpu_custom_call" | custom-call | flops 2684354560 | bytes 2506752 | tf_op jit(solution)/shard_map/back_first/pallas_call | solution.py:478
  30.5 0.1 halve_ffn.1
  30.6 1.8 %collective-permute-start.8 = (bf16[1,576,256]{2,1,0:T(8,128)(2,1)S(1)}, bf16[1,576,256]{2,1,0:T(8,128)(2,1)S(1)}, u32[]{:S(2)}, u32[]{:S(2)}) collective-permute-start(bf16[1,576,256]{2,1,0:T(8,128)(2,1)S(1)} %get-tuple-element.102), channel_id=1, source_target_pairs={{0,2},{1,3},{2,0},{3,1},{4,6},{5,7},{6,4},{7,5},{8,10},{9,11},{10,... | collective-permute-start | bytes 884744 | tf_op jit(solution)/shard_map/ppermute | solution.py:492
  32.4 5.4 %back_last.1 = (f32[512,256]{1,0:T(8,128)}, f32[2,256,256]{2,1,0:T(8,128)S(1)}, bf16[2,256,256]{2,1,0:T(8,128)(2,1)S(1)}) custom-call(bf16[512,768]{1,0:T(8,128)(2,1)S(1)} %get-tuple-element.82.joined_ref.refs_0_, bf16[512,256]{1,0:T(8,128)(2,1)S(1)} %get-tuple-element.83.dattend_ref.refs_1_, f32[8,512]{1,0:T(8,128)S(1)} %get-tuple-element.84.log_ref.refs_2_, ...), custom_call_target="tpu_custom_call" | custom-call | flops 3221225472 | bytes 5310464 | tf_op jit(solution)/shard_map/back_last/pallas_call | solution.py:478
  37.8 0.1 collective-permute-start.7
  37.9 1.5 %collective-permute-done.7.refs_1_ = bf16[2,256,256]{2,1,0:T(8,128)(2,1)S(1)} collective-permute-done((bf16[2,256,256]{2,1,0:T(8,128)(2,1)S(1)}, bf16[2,256,256]{2,1,0:T(8,128)(2,1)S(1)}, u32[]{:S(2)}, u32[]{:S(2)}) %collective-permute-start.7) | collective-permute-done | bytes 262176 | tf_op jit(solution)/shard_map/ppermute | solution.py:492
  39.4 0.6 collective-permute-done.8
  40.0 1.7 %collective-permute-start.10 = (bf16[1,256,256]{2,1,0:T(8,128)(2,1)S(1)}, bf16[1,256,256]{2,1,0:T(8,128)(2,1)S(1)}, u32[]{:S(2)}, u32[]{:S(2)}) collective-permute-start(bf16[1,256,256]{2,1,0:T(8,128)(2,1)S(1)} %get-tuple-element.107), channel_id=1, source_target_pairs={{0,2},{1,3},{2,0},{3,1},{4,6},{5,7},{6,4},{7,5},{8,10},{9,11},{10,... | collective-permute-start | bytes 393224 | tf_op jit(solution)/shard_map/ppermute | solution.py:492
  41.8 0.1 split_sum.2
  42.0 1.6 %collective-permute-start.9 = (bf16[4,72,256]{2,1,0:T(8,128)(2,1)S(1)}, bf16[4,72,256]{2,1,0:T(8,128)(2,1)S(1)}, u32[]{:S(2)}, u32[]{:S(2)}) collective-permute-start(bf16[4,72,256]{2,1,0:T(8,128)(2,1)S(1)} %get-tuple-element.105), channel_id=1, source_target_pairs={{0,4},{4,0},{8,12},{12,8},{16,20},{20,16},{24,28},{28,24},{1,5},{5... | collective-permute-start | bytes 442376 | tf_op jit(solution)/shard_map/ppermute | solution.py:492
  43.5 1.5 %collective-permute-done.10 = bf16[1,256,256]{2,1,0:T(8,128)(2,1)S(1)} collective-permute-done((bf16[1,256,256]{2,1,0:T(8,128)(2,1)S(1)}, bf16[1,256,256]{2,1,0:T(8,128)(2,1)S(1)}, u32[]{:S(2)}, u32[]{:S(2)}) %collective-permute-start.10) | collective-permute-done | bytes 131104 | tf_op jit(solution)/shard_map/ppermute | solution.py:492
  45.0 0.1 split_sum.3
  45.1 1.7 %collective-permute-start.11 = (bf16[4,32,256]{2,1,0:T(8,128)(2,1)S(1)}, bf16[4,32,256]{2,1,0:T(8,128)(2,1)S(1)}, u32[]{:S(2)}, u32[]{:S(2)}) collective-permute-start(bf16[4,32,256]{2,1,0:T(8,128)(2,1)S(1)} %get-tuple-element.109), channel_id=1, source_target_pairs={{0,4},{4,0},{8,12},{12,8},{16,20},{20,16},{24,28},{28,24},{1,5},{5... | collective-permute-start | bytes 196616 | tf_op jit(solution)/shard_map/ppermute | solution.py:492
  46.8 1.1 %collective-permute-done.9.refs_1_ = bf16[4,72,256]{2,1,0:T(8,128)(2,1)S(1)} collective-permute-done((bf16[4,72,256]{2,1,0:T(8,128)(2,1)S(1)}, bf16[4,72,256]{2,1,0:T(8,128)(2,1)S(1)}, u32[]{:S(2)}, u32[]{:S(2)}) %collective-permute-start.9) | collective-permute-done | bytes 147488 | tf_op jit(solution)/shard_map/ppermute | solution.py:492
  47.9 1.5 %collective-permute-done.11.refs_3_ = bf16[4,32,256]{2,1,0:T(8,128)(2,1)S(1)} collective-permute-done((bf16[4,32,256]{2,1,0:T(8,128)(2,1)S(1)}, bf16[4,32,256]{2,1,0:T(8,128)(2,1)S(1)}, u32[]{:S(2)}, u32[]{:S(2)}) %collective-permute-start.11) | collective-permute-done | bytes 65568 | tf_op jit(solution)/shard_map/ppermute | solution.py:492
  49.4 1.8 %collective-permute-start.12 = (bf16[2,104,256]{2,1,0:T(8,128)(2,1)S(1)}, bf16[2,104,256]{2,1,0:T(8,128)(2,1)S(1)}, u32[]{:S(2)}, u32[]{:S(2)}) collective-permute-start(bf16[2,104,256]{2,1,0:T(8,128)(2,1)S(1)} %get-tuple-element.111), channel_id=1, source_target_pairs={{0,8},{4,12},{8,0},{12,4},{16,24},{20,28},{24,16},{28,20},{1,9},{5... | collective-permute-start | bytes 319496 | tf_op jit(solution)/shard_map/ppermute | solution.py:492
  51.2 3.0 %collective-permute-done.12.refs_1_ = bf16[2,104,256]{2,1,0:T(8,128)(2,1)S(1)} collective-permute-done((bf16[2,104,256]{2,1,0:T(8,128)(2,1)S(1)}, bf16[2,104,256]{2,1,0:T(8,128)(2,1)S(1)}, u32[]{:S(2)}, u32[]{:S(2)}) %collective-permute-start.12) | collective-permute-done | bytes 106528 | tf_op jit(solution)/shard_map/ppermute | solution.py:492
  54.2 3.2 %collective-permute-start.13 = (bf16[1,104,256]{2,1,0:T(8,128)(2,1)S(1)}, bf16[1,104,256]{2,1,0:T(8,128)(2,1)S(1)}, u32[]{:S(2)}, u32[]{:S(2)}) collective-permute-start(bf16[1,104,256]{2,1,0:T(8,128)(2,1)S(1)} %get-tuple-element.113), channel_id=1, source_target_pairs={{0,16},{4,20},{8,24},{12,28},{16,0},{20,4},{24,8},{28,12},{1,17},{... | collective-permute-start | bytes 159752 | tf_op jit(solution)/shard_map/ppermute | solution.py:492
  57.4 2.5 %collective-permute-done.13.other_ref = bf16[1,104,256]{2,1,0:T(8,128)(2,1)S(1)} collective-permute-done((bf16[1,104,256]{2,1,0:T(8,128)(2,1)S(1)}, bf16[1,104,256]{2,1,0:T(8,128)(2,1)S(1)}, u32[]{:S(2)}, u32[]{:S(2)}) %collective-permute-start.13) | collective-permute-done | bytes 53280 | tf_op jit(solution)/shard_map/ppermute | solution.py:492
  60.0 2.9 %collective-permute-start.17 = (bf16[104,256]{1,0:T(8,128)(2,1)S(1)}, bf16[104,256]{1,0:T(8,128)(2,1)S(1)}, u32[]{:S(2)}, u32[]{:S(2)}) collective-permute-start(bf16[104,256]{1,0:T(8,128)(2,1)S(1)} %piece_sum.1.refs_0_), channel_id=1, source_target_pairs={{0,16},{4,20},{8,24},{12,28},{16,0},{20,4},{24,8},{28,12},{1,17},{... | collective-permute-start | bytes 159752 | tf_op jit(solution)/shard_map/ppermute | solution.py:492
  62.9 2.5 %collective-permute-start.15 = (bf16[104,256]{1,0:T(8,128)(2,1)S(1)}, bf16[104,256]{1,0:T(8,128)(2,1)S(1)}, u32[]{:S(2)}, u32[]{:S(2)}) collective-permute-start(bf16[104,256]{1,0:T(8,128)(2,1)S(1)} %piece_sum.1.refs_0_), channel_id=1, source_target_pairs={{0,8},{4,12},{8,0},{12,4},{16,24},{20,28},{24,16},{28,20},{1,9},{5... | collective-permute-start | bytes 159752 | tf_op jit(solution)/shard_map/ppermute | solution.py:492
  65.4 2.1 %collective-permute-start.19 = (bf16[104,256]{1,0:T(8,128)(2,1)S(1)}, bf16[104,256]{1,0:T(8,128)(2,1)S(1)}, u32[]{:S(2)}, u32[]{:S(2)}) collective-permute-start(bf16[104,256]{1,0:T(8,128)(2,1)S(1)} %collective-permute-done.17.refs_4_), channel_id=1, source_target_pairs={{0,8},{4,12},{8,0},{12,4},{16,24},{20,28},{24,16},{28,20},{1,9},{5... | collective-permute-start | bytes 159752 | tf_op jit(solution)/shard_map/ppermute | solution.py:492
  67.5 1.5 %collective-permute-start.14 = (bf16[104,256]{1,0:T(8,128)(2,1)S(1)}, bf16[104,256]{1,0:T(8,128)(2,1)S(1)}, u32[]{:S(2)}, u32[]{:S(2)}) collective-permute-start(bf16[104,256]{1,0:T(8,128)(2,1)S(1)} %piece_sum.1.refs_0_), channel_id=1, source_target_pairs={{0,4},{4,0},{8,12},{12,8},{16,20},{20,16},{24,28},{28,24},{1,5},{5... | collective-permute-start | bytes 159752 | tf_op jit(solution)/shard_map/ppermute | solution.py:492
  69.0 0.5 collective-permute-start.18
  69.5 1.5 %collective-permute-start.16 = (bf16[104,256]{1,0:T(8,128)(2,1)S(1)}, bf16[104,256]{1,0:T(8,128)(2,1)S(1)}, u32[]{:S(2)}, u32[]{:S(2)}) collective-permute-start(bf16[104,256]{1,0:T(8,128)(2,1)S(1)} %collective-permute-done.15.refs_2_), channel_id=1, source_target_pairs={{0,4},{4,0},{8,12},{12,8},{16,20},{20,16},{24,28},{28,24},{1,5},{5... | collective-permute-start | bytes 159752 | tf_op jit(solution)/shard_map/ppermute | solution.py:492
  71.0 1.0 %collective-permute-start.20 = (bf16[104,256]{1,0:T(8,128)(2,1)S(1)}, bf16[104,256]{1,0:T(8,128)(2,1)S(1)}, u32[]{:S(2)}, u32[]{:S(2)}) collective-permute-start(bf16[104,256]{1,0:T(8,128)(2,1)S(1)} %collective-permute-done.19.refs_6_), channel_id=1, source_target_pairs={{0,4},{4,0},{8,12},{12,8},{16,20},{20,16},{24,28},{28,24},{1,5},{5... | collective-permute-start | bytes 159752 | tf_op jit(solution)/shard_map/ppermute | solution.py:492
  72.0 1.1 %collective-permute-done.18.refs_5_ = bf16[104,256]{1,0:T(8,128)(2,1)S(1)} collective-permute-done((bf16[104,256]{1,0:T(8,128)(2,1)S(1)}, bf16[104,256]{1,0:T(8,128)(2,1)S(1)}, u32[]{:S(2)}, u32[]{:S(2)}) %collective-permute-start.18) | collective-permute-done | bytes 53280 | tf_op jit(solution)/shard_map/ppermute | solution.py:492
  73.1 0.6 collective-permute-done.16.refs_3_
  73.7 1.5 %collective-permute-done.20.refs_7_ = bf16[104,256]{1,0:T(8,128)(2,1)S(1)} collective-permute-done((bf16[104,256]{1,0:T(8,128)(2,1)S(1)}, bf16[104,256]{1,0:T(8,128)(2,1)S(1)}, u32[]{:S(2)}, u32[]{:S(2)}) %collective-permute-start.20) | collective-permute-done | bytes 53280 | tf_op jit(solution)/shard_map/ppermute | solution.py:492
  75.3 1.8 %adam.1 = (f32[64,768]{1,0:T(8,128)}, f32[64,768]{1,0:T(8,128)}, f32[64,768]{1,0:T(8,128)}, f32[64,256]{1,0:T(8,128)}, f32[64,256]{1,0:T(8,128)}, /*index=5*/f32...) custom-call(bf16[104,256]{1,0:T(8,128)(2,1)S(1)} %piece_sum.1.refs_0, ...), custom_call_target="tpu_custom_call" | custom-call | bytes 5163008 | tf_op jit(solution)/shard_map/adam/pallas_call | solution.py:478
  (59 shorter events, 0.3 us)
Async XLA Ops:
  0.7 0.9 %copy-start.4 = (f32[64,768]{1,0:T(8,128)S(1)}, f32[64,768]{1,0:T(8,128)}, u32[]{:S(2)}) copy-start(f32[64,768]{1,0:T(8,128)} %refs_8_.1) | copy-start | bytes 589828
  1.6 0.7 copy-start.19
  2.3 11.0 %copy-start.8 = (bf16[512,256]{1,0:T(8,128)(2,1)S(1)}, bf16[512,256]{1,0:T(8,128)(2,1)}, u32[]{:S(2)}) copy-start(bf16[512,256]{1,0:T(8,128)(2,1)} %seed_ref.1) | copy-start | bytes 786436
  2.3 11.0 %copy-start.23 = (s32[128]{0:T(128)S(1)}, s32[128]{0:T(128)}, u32[]{:S(2)}) copy-start(s32[128]{0:T(128)} %param.21) | copy-start | bytes 1540
  2.3 11.0 %copy-start.24 = (s32[128]{0:T(128)S(1)}, s32[128]{0:T(128)}, u32[]{:S(2)}) copy-start(s32[128]{0:T(128)} %param.22) | copy-start | bytes 1540
  2.6 6.0 %collective-permute-start.1 = (bf16[208,256]{1,0:T(8,128)(2,1)S(1)}, bf16[208,256]{1,0:T(8,128)(2,1)S(1)}, u32[]{:S(2)}, u32[]{:S(2)}) collective-permute-start(bf16[208,256]{1,0:T(8,128)(2,1)S(1)} %pack_first.1.refs_2_.refs_3_.refs_11_), channel_id=1, source_target_pairs={{0,2},{1,3},{2,0},{3,1},{4,6},{5,7},{6,4},{7,5},{8,10},{9,11},{10,... | collective-permute-start | bytes 319496 | tf_op jit(solution)/shard_map/ppermute | solution.py:492
  5.6 9.6 %collective-permute-start = (bf16[208,256]{1,0:T(8,128)(2,1)S(1)}, bf16[208,256]{1,0:T(8,128)(2,1)S(1)}, u32[]{:S(2)}, u32[]{:S(2)}) collective-permute-start(bf16[208,256]{1,0:T(8,128)(2,1)S(1)} %pack_first.1.refs_2_.refs_3_.refs_11_), channel_id=1, source_target_pairs={{0,1},{1,0},{2,3},{3,2},{4,5},{5,4},{6,7},{7,6},{8,9},{9,8},{10,11... | collective-permute-start | bytes 319496 | tf_op jit(solution)/shard_map/ppermute | solution.py:492
  8.6 6.6 %collective-permute-start.2 = (bf16[208,256]{1,0:T(8,128)(2,1)S(1)}, bf16[208,256]{1,0:T(8,128)(2,1)S(1)}, u32[]{:S(2)}, u32[]{:S(2)}) collective-permute-start(bf16[208,256]{1,0:T(8,128)(2,1)S(1)} %collective-permute-done.1.refs_4_.refs_5_.refs_13_), channel_id=1, source_target_pairs={{0,1},{1,0},{2,3},{3,2},{4,5},{5,4},{6,7},{7,6},{8,9},{9,8},{10,11... | collective-permute-start | bytes 319496 | tf_op jit(solution)/shard_map/ppermute | solution.py:492
  8.6 1.0 %copy-start = (f32[64,1024]{1,0:T(8,128)S(1)}, f32[64,1024]{1,0:T(8,128)}, u32[]{:S(2)}) copy-start(f32[64,1024]{1,0:T(8,128)} %refs_14_.1) | copy-start | bytes 786436
  9.5 0.9 %copy-start.2 = (f32[256,256]{1,0:T(8,128)S(1)}, f32[256,256]{1,0:T(8,128)}, u32[]{:S(2)}) copy-start(f32[256,256]{1,0:T(8,128)} %refs_17_.1) | copy-start | bytes 786436
  10.5 0.8 %copy-start.6 = (f32[64,256]{1,0:T(8,128)S(1)}, f32[64,256]{1,0:T(8,128)}, u32[]{:S(2)}) copy-start(f32[64,256]{1,0:T(8,128)} %refs_11_.1) | copy-start | bytes 196612
  11.5 9.5 %collective-permute-start.3 = (bf16[576,256]{1,0:T(8,128)(2,1)S(1)}, bf16[576,256]{1,0:T(8,128)(2,1)S(1)}, u32[]{:S(2)}, u32[]{:S(2)}) collective-permute-start(bf16[576,256]{1,0:T(8,128)(2,1)S(1)} %pack_second.1.refs_7_), channel_id=1, source_target_pairs={{0,2},{1,3},{2,0},{3,1},{4,6},{5,7},{6,4},{7,5},{8,10},{9,11},{10,... | collective-permute-start | bytes 884744 | tf_op jit(solution)/shard_map/ppermute | solution.py:492
  13.3 1.0 %copy-start.9 = (bf16[512,256]{1,0:T(8,128)(2,1)S(1)}, bf16[512,256]{1,0:T(8,128)(2,1)}, u32[]{:S(2)}) copy-start(bf16[512,256]{1,0:T(8,128)(2,1)} %refs_0_.1) | copy-start | bytes 786436
  14.9 6.1 %collective-permute-start.4 = (bf16[576,256]{1,0:T(8,128)(2,1)S(1)}, bf16[576,256]{1,0:T(8,128)(2,1)S(1)}, u32[]{:S(2)}, u32[]{:S(2)}) collective-permute-start(bf16[576,256]{1,0:T(8,128)(2,1)S(1)} %pack_second.1.refs_7_), channel_id=1, source_target_pairs={{0,1},{1,0},{2,3},{3,2},{4,5},{5,4},{6,7},{7,6},{8,9},{9,8},{10,11... | collective-permute-start | bytes 884744 | tf_op jit(solution)/shard_map/ppermute | solution.py:492
  15.2 7.4 %copy-start.10 = (bf16[512,256]{1,0:T(8,128)(2,1)S(1)}, bf16[512,256]{1,0:T(8,128)(2,1)}, u32[]{:S(2)}) copy-start(bf16[512,256]{1,0:T(8,128)(2,1)} %refs_0_.1) | copy-start | bytes 786436
  21.0 1.6 %collective-permute-start.5 = (bf16[576,256]{1,0:T(8,128)(2,1)S(1)}, bf16[576,256]{1,0:T(8,128)(2,1)S(1)}, u32[]{:S(2)}, u32[]{:S(2)}) collective-permute-start(bf16[576,256]{1,0:T(8,128)(2,1)S(1)} %collective-permute-done.3.refs_9_), channel_id=1, source_target_pairs={{0,1},{1,0},{2,3},{3,2},{4,5},{5,4},{6,7},{7,6},{8,9},{9,8},{10,11... | collective-permute-start | bytes 884744 | tf_op jit(solution)/shard_map/ppermute | solution.py:492
  26.7 3.8 %collective-permute-start.6 = (bf16[2,576,256]{2,1,0:T(8,128)(2,1)S(1)}, bf16[2,576,256]{2,1,0:T(8,128)(2,1)S(1)}, u32[]{:S(2)}, u32[]{:S(2)}) collective-permute-start(bf16[2,576,256]{2,1,0:T(8,128)(2,1)S(1)} %get-tuple-element.86), channel_id=1, source_target_pairs={{0,1},{1,0},{2,3},{3,2},{4,5},{5,4},{6,7},{7,6},{8,9},{9,8},{10,11... | collective-permute-start | bytes 1769480 | tf_op jit(solution)/shard_map/ppermute | solution.py:492
  30.6 9.3 %collective-permute-start.8 = (bf16[1,576,256]{2,1,0:T(8,128)(2,1)S(1)}, bf16[1,576,256]{2,1,0:T(8,128)(2,1)S(1)}, u32[]{:S(2)}, u32[]{:S(2)}) collective-permute-start(bf16[1,576,256]{2,1,0:T(8,128)(2,1)S(1)} %get-tuple-element.102), channel_id=1, source_target_pairs={{0,2},{1,3},{2,0},{3,1},{4,6},{5,7},{6,4},{7,5},{8,10},{9,11},{10,... | collective-permute-start | bytes 884744 | tf_op jit(solution)/shard_map/ppermute | solution.py:492
  37.8 1.5 %collective-permute-start.7 = (bf16[2,256,256]{2,1,0:T(8,128)(2,1)S(1)}, bf16[2,256,256]{2,1,0:T(8,128)(2,1)S(1)}, u32[]{:S(2)}, u32[]{:S(2)}) collective-permute-start(bf16[2,256,256]{2,1,0:T(8,128)(2,1)S(1)} %get-tuple-element.100), channel_id=1, source_target_pairs={{0,1},{1,0},{2,3},{3,2},{4,5},{5,4},{6,7},{7,6},{8,9},{9,8},{10,11... | collective-permute-start | bytes 786440 | tf_op jit(solution)/shard_map/ppermute | solution.py:492
  40.0 5.1 %collective-permute-start.10 = (bf16[1,256,256]{2,1,0:T(8,128)(2,1)S(1)}, bf16[1,256,256]{2,1,0:T(8,128)(2,1)S(1)}, u32[]{:S(2)}, u32[]{:S(2)}) collective-permute-start(bf16[1,256,256]{2,1,0:T(8,128)(2,1)S(1)} %get-tuple-element.107), channel_id=1, source_target_pairs={{0,2},{1,3},{2,0},{3,1},{4,6},{5,7},{6,4},{7,5},{8,10},{9,11},{10,... | collective-permute-start | bytes 393224 | tf_op jit(solution)/shard_map/ppermute | solution.py:492
  41.7 33.5 %copy-start.1 = (f32[64,1024]{1,0:T(8,128)S(1)}, f32[64,1024]{1,0:T(8,128)}, u32[]{:S(2)}) copy-start(f32[64,1024]{1,0:T(8,128)} %refs_14_.1) | copy-start | bytes 786436
  41.7 33.5 %copy-start.3 = (f32[256,256]{1,0:T(8,128)S(1)}, f32[256,256]{1,0:T(8,128)}, u32[]{:S(2)}) copy-start(f32[256,256]{1,0:T(8,128)} %refs_17_.1) | copy-start | bytes 786436
  41.7 33.5 %copy-start.5 = (f32[64,768]{1,0:T(8,128)S(1)}, f32[64,768]{1,0:T(8,128)}, u32[]{:S(2)}) copy-start(f32[64,768]{1,0:T(8,128)} %refs_8_.1) | copy-start | bytes 589828
  41.7 33.5 %copy-start.7 = (f32[64,256]{1,0:T(8,128)S(1)}, f32[64,256]{1,0:T(8,128)}, u32[]{:S(2)}) copy-start(f32[64,256]{1,0:T(8,128)} %refs_11_.1) | copy-start | bytes 196612
  41.7 33.5 %copy-start.11 = (f32[64,1024]{1,0:T(8,128)S(1)}, f32[64,1024]{1,0:T(8,128)}, u32[]{:S(2)}) copy-start(f32[64,1024]{1,0:T(8,128)} %refs_15_.1) | copy-start | bytes 786436
  41.7 33.5 %copy-start.12 = (f32[64,1024]{1,0:T(8,128)S(1)}, f32[64,1024]{1,0:T(8,128)}, u32[]{:S(2)}) copy-start(f32[64,1024]{1,0:T(8,128)} %refs_16_.1) | copy-start | bytes 786436
  41.7 33.5 %copy-start.13 = (f32[256,256]{1,0:T(8,128)S(1)}, f32[256,256]{1,0:T(8,128)}, u32[]{:S(2)}) copy-start(f32[256,256]{1,0:T(8,128)} %refs_18_.1) | copy-start | bytes 786436
  41.7 33.5 %copy-start.14 = (f32[256,256]{1,0:T(8,128)S(1)}, f32[256,256]{1,0:T(8,128)}, u32[]{:S(2)}) copy-start(f32[256,256]{1,0:T(8,128)} %refs_19_.1) | copy-start | bytes 786436
  41.8 33.5 %copy-start.15 = (f32[64,768]{1,0:T(8,128)S(1)}, f32[64,768]{1,0:T(8,128)}, u32[]{:S(2)}) copy-start(f32[64,768]{1,0:T(8,128)} %refs_9_.1) | copy-start | bytes 589828
  41.8 33.5 %copy-start.16 = (f32[64,768]{1,0:T(8,128)S(1)}, f32[64,768]{1,0:T(8,128)}, u32[]{:S(2)}) copy-start(f32[64,768]{1,0:T(8,128)} %refs_10_.1) | copy-start | bytes 589828
  41.8 33.5 %copy-start.17 = (f32[64,256]{1,0:T(8,128)S(1)}, f32[64,256]{1,0:T(8,128)}, u32[]{:S(2)}) copy-start(f32[64,256]{1,0:T(8,128)} %refs_12_.1) | copy-start | bytes 196612
  41.8 33.5 %copy-start.18 = (f32[64,256]{1,0:T(8,128)S(1)}, f32[64,256]{1,0:T(8,128)}, u32[]{:S(2)}) copy-start(f32[64,256]{1,0:T(8,128)} %refs_13_.1) | copy-start | bytes 196612
  41.8 33.5 %copy-start.20 = (f32[768]{0:T(1024)S(1)}, f32[768]{0:T(1024)}, u32[]{:S(2)}) copy-start(f32[768]{0:T(1024)} %refs_20_.1) | copy-start | bytes 9220
  41.8 33.5 %copy-start.21 = (f32[768]{0:T(1024)S(1)}, f32[768]{0:T(1024)}, u32[]{:S(2)}) copy-start(f32[768]{0:T(1024)} %refs_21_.1) | copy-start | bytes 9220
  41.8 33.5 %copy-start.22 = (f32[768]{0:T(1024)S(1)}, f32[768]{0:T(1024)}, u32[]{:S(2)}) copy-start(f32[768]{0:T(1024)} %refs_22_.1) | copy-start | bytes 9220
  42.0 5.9 %collective-permute-start.9 = (bf16[4,72,256]{2,1,0:T(8,128)(2,1)S(1)}, bf16[4,72,256]{2,1,0:T(8,128)(2,1)S(1)}, u32[]{:S(2)}, u32[]{:S(2)}) collective-permute-start(bf16[4,72,256]{2,1,0:T(8,128)(2,1)S(1)} %get-tuple-element.105), channel_id=1, source_target_pairs={{0,4},{4,0},{8,12},{12,8},{16,20},{20,16},{24,28},{28,24},{1,5},{5... | collective-permute-start | bytes 442376 | tf_op jit(solution)/shard_map/ppermute | solution.py:492
  45.1 4.3 %collective-permute-start.11 = (bf16[4,32,256]{2,1,0:T(8,128)(2,1)S(1)}, bf16[4,32,256]{2,1,0:T(8,128)(2,1)S(1)}, u32[]{:S(2)}, u32[]{:S(2)}) collective-permute-start(bf16[4,32,256]{2,1,0:T(8,128)(2,1)S(1)} %get-tuple-element.109), channel_id=1, source_target_pairs={{0,4},{4,0},{8,12},{12,8},{16,20},{20,16},{24,28},{28,24},{1,5},{5... | collective-permute-start | bytes 196616 | tf_op jit(solution)/shard_map/ppermute | solution.py:492
  49.4 4.8 %collective-permute-start.12 = (bf16[2,104,256]{2,1,0:T(8,128)(2,1)S(1)}, bf16[2,104,256]{2,1,0:T(8,128)(2,1)S(1)}, u32[]{:S(2)}, u32[]{:S(2)}) collective-permute-start(bf16[2,104,256]{2,1,0:T(8,128)(2,1)S(1)} %get-tuple-element.111), channel_id=1, source_target_pairs={{0,8},{4,12},{8,0},{12,4},{16,24},{20,28},{24,16},{28,20},{1,9},{5... | collective-permute-start | bytes 319496 | tf_op jit(solution)/shard_map/ppermute | solution.py:492
  54.2 5.7 %collective-permute-start.13 = (bf16[1,104,256]{2,1,0:T(8,128)(2,1)S(1)}, bf16[1,104,256]{2,1,0:T(8,128)(2,1)S(1)}, u32[]{:S(2)}, u32[]{:S(2)}) collective-permute-start(bf16[1,104,256]{2,1,0:T(8,128)(2,1)S(1)} %get-tuple-element.113), channel_id=1, source_target_pairs={{0,16},{4,20},{8,24},{12,28},{16,0},{20,4},{24,8},{28,12},{1,17},{... | collective-permute-start | bytes 159752 | tf_op jit(solution)/shard_map/ppermute | solution.py:492
  60.0 5.4 %collective-permute-start.17 = (bf16[104,256]{1,0:T(8,128)(2,1)S(1)}, bf16[104,256]{1,0:T(8,128)(2,1)S(1)}, u32[]{:S(2)}, u32[]{:S(2)}) collective-permute-start(bf16[104,256]{1,0:T(8,128)(2,1)S(1)} %piece_sum.1.refs_0_), channel_id=1, source_target_pairs={{0,16},{4,20},{8,24},{12,28},{16,0},{20,4},{24,8},{28,12},{1,17},{... | collective-permute-start | bytes 159752 | tf_op jit(solution)/shard_map/ppermute | solution.py:492
  62.9 6.6 %collective-permute-start.15 = (bf16[104,256]{1,0:T(8,128)(2,1)S(1)}, bf16[104,256]{1,0:T(8,128)(2,1)S(1)}, u32[]{:S(2)}, u32[]{:S(2)}) collective-permute-start(bf16[104,256]{1,0:T(8,128)(2,1)S(1)} %piece_sum.1.refs_0_), channel_id=1, source_target_pairs={{0,8},{4,12},{8,0},{12,4},{16,24},{20,28},{24,16},{28,20},{1,9},{5... | collective-permute-start | bytes 159752 | tf_op jit(solution)/shard_map/ppermute | solution.py:492
  65.4 5.7 %collective-permute-start.19 = (bf16[104,256]{1,0:T(8,128)(2,1)S(1)}, bf16[104,256]{1,0:T(8,128)(2,1)S(1)}, u32[]{:S(2)}, u32[]{:S(2)}) collective-permute-start(bf16[104,256]{1,0:T(8,128)(2,1)S(1)} %collective-permute-done.17.refs_4_), channel_id=1, source_target_pairs={{0,8},{4,12},{8,0},{12,4},{16,24},{20,28},{24,16},{28,20},{1,9},{5... | collective-permute-start | bytes 159752 | tf_op jit(solution)/shard_map/ppermute | solution.py:492
  67.5 4.6 %collective-permute-start.14 = (bf16[104,256]{1,0:T(8,128)(2,1)S(1)}, bf16[104,256]{1,0:T(8,128)(2,1)S(1)}, u32[]{:S(2)}, u32[]{:S(2)}) collective-permute-start(bf16[104,256]{1,0:T(8,128)(2,1)S(1)} %piece_sum.1.refs_0_), channel_id=1, source_target_pairs={{0,4},{4,0},{8,12},{12,8},{16,20},{20,16},{24,28},{28,24},{1,5},{5... | collective-permute-start | bytes 159752 | tf_op jit(solution)/shard_map/ppermute | solution.py:492
  69.0 4.1 %collective-permute-start.18 = (bf16[104,256]{1,0:T(8,128)(2,1)S(1)}, bf16[104,256]{1,0:T(8,128)(2,1)S(1)}, u32[]{:S(2)}, u32[]{:S(2)}) collective-permute-start(bf16[104,256]{1,0:T(8,128)(2,1)S(1)} %collective-permute-done.17.refs_4_), channel_id=1, source_target_pairs={{0,4},{4,0},{8,12},{12,8},{16,20},{20,16},{24,28},{28,24},{1,5},{5... | collective-permute-start | bytes 159752 | tf_op jit(solution)/shard_map/ppermute | solution.py:492
  69.5 4.2 %collective-permute-start.16 = (bf16[104,256]{1,0:T(8,128)(2,1)S(1)}, bf16[104,256]{1,0:T(8,128)(2,1)S(1)}, u32[]{:S(2)}, u32[]{:S(2)}) collective-permute-start(bf16[104,256]{1,0:T(8,128)(2,1)S(1)} %collective-permute-done.15.refs_2_), channel_id=1, source_target_pairs={{0,4},{4,0},{8,12},{12,8},{16,20},{20,16},{24,28},{28,24},{1,5},{5... | collective-permute-start | bytes 159752 | tf_op jit(solution)/shard_map/ppermute | solution.py:492
  71.0 4.1 %collective-permute-start.20 = (bf16[104,256]{1,0:T(8,128)(2,1)S(1)}, bf16[104,256]{1,0:T(8,128)(2,1)S(1)}, u32[]{:S(2)}, u32[]{:S(2)}) collective-permute-start(bf16[104,256]{1,0:T(8,128)(2,1)S(1)} %collective-permute-done.19.refs_6_), channel_id=1, source_target_pairs={{0,4},{4,0},{8,12},{12,8},{16,20},{20,16},{24,28},{28,24},{1,5},{5... | collective-permute-start | bytes 159752 | tf_op jit(solution)/shard_map/ppermute | solution.py:492

commit v6 on v5

--- a/solution.py
+++ b/solution.py
@@ -14,6 +14,7 @@
 GROUP = 8
 SMALL_PAD = 16
 TILE_ROWS = 8
+CHUNK = 64
 
 norm_eps = 1e-05
 beta_one = 0.9
@@ -181,7 +182,7 @@
 def attend_kernel(shards, *refs):
     norm_ref, bias_ref = refs[:2]
     pieces = refs[2 : 2 + shards]
-    joined_ref, out_ref, log_ref, weight_ref, small_ref, att_ref = refs[2 + shards :]
+    joined_ref, out_ref, log_ref, att_ref, weight_ref, small_ref = refs[2 + shards :]
     rows, width = norm_ref.shape
     shard = lax.axis_index("shard")
     part = width // shards
@@ -202,15 +203,26 @@
         key_tile = joined_ref[:, width + tile.start : width + tile.stop] * head_mask(head)
         feature = slice(head * HEAD, (head + 1) * HEAD)
         for start, stop in query_blocks(rows):
-            scores = dot_nt(key_tile[:stop], joined_ref[start:stop, tile])
-            scores = scores * (score_scale * log2_e) + bias_ref[:stop, start:stop]
-            top = jnp.max(scores, axis=0, keepdims=True)
-            exponent = jnp.exp2(scores - top)
-            total = jnp.sum(exponent, axis=0, keepdims=True)
-            probs = (exponent * (1.0 / total)).astype(low)
-            att_ref[feature, start:stop] = dot_nn(values_t[feature, :stop], probs).astype(low)
+            raw = dot_nt(key_tile[:stop], joined_ref[start:stop, tile])
+            scores = []
+            top = None
+            for at in range(0, stop, CHUNK):
+                piece = raw[at : at + CHUNK] * (score_scale * log2_e)
+                piece = piece + bias_ref[at : at + CHUNK, start:stop]
+                scores.append(piece)
+                top = piece if top is None else jnp.maximum(top, piece)
+            top = jnp.max(top, axis=0, keepdims=True)
+            exponents = []
+            total = None
+            for piece in scores:
+                piece = jnp.exp2(piece - top)
+                total = piece if total is None else total + piece
+                exponents.append(piece.astype(low))
+            total = jnp.sum(total, axis=0, keepdims=True)
+            mixed = dot_nn(values_t[feature, :stop], jnp.concatenate(exponents, axis=0))
+            att_ref[feature, start:stop] = mixed * (1.0 / total)
             log_ref[head : head + 1, start:stop] = top + jnp.log2(total)
-    out_ref[...] = att_ref[...].T
+    out_ref[...] = att_ref[...].astype(low).T
 
 
 def feed_kernel(shards, *refs):
@@ -245,15 +257,20 @@
     sums_ref[...] = jnp.zeros(sums_ref.shape, wide)
     for block in range(blocks):
         cols = slice(block * width, (block + 1) * width)
-        pre = dot_nn(hidden, up_w[:, cols]) + bias_up[block]
-        square = pre * pre
-        bend = jnp.tanh(tanh_scale * (pre + cubic * (pre * square)))
-        half = 0.5 * (1.0 + bend)
-        act = (pre * half).astype(low)
-        slope = half + (0.5 * tanh_scale) * pre * (1.0 - bend * bend) * (
-            1.0 + (3.0 * cubic) * square
-        )
-        dpre = (dot_nt(seed_low, down_w[cols, :]) * slope).astype(low)
+        raw = dot_nn(hidden, up_w[:, cols])
+        dact = dot_nt(seed_low, down_w[cols, :])
+        act, dpre = [], []
+        for at in range(0, rows, CHUNK):
+            pre = raw[at : at + CHUNK] + bias_up[block]
+            square = pre * pre
+            bend = jnp.tanh(pre * (tanh_scale + (tanh_scale * cubic) * square))
+            half = 0.5 + 0.5 * bend
+            act.append((pre * half).astype(low))
+            slope = 0.5 * tanh_scale + (1.5 * tanh_scale * cubic) * square
+            slope = half + (pre * slope) * (1.0 - bend * bend)
+            dpre.append((dact[at : at + CHUNK] * slope).astype(low))
+        act = jnp.concatenate(act, axis=0)
+        dpre = jnp.concatenate(dpre, axis=0)
         result = result + dot_nn(act, down_w[cols, :])
         dhidden = dhidden + dot_nt(dpre, up_w[:, cols])
         grad_down = dot_nn(act.T, seed_low)
@@ -290,7 +307,9 @@
         send_ref[pair] = grads_ref[2 * pair + 1 - side].astype(low)
 
 
-def back_tile(tile_index, joined_ref, dattend_ref, log_ref, bias_ref, dquery_t, dkey, dvalue):
+def back_tile(
+    tile_index, joined_ref, dattend_ref, log_ref, bias_ref, mixed_ref, dquery_t, dkey, dvalue
+):
     rows = joined_ref.shape[0]
     width = joined_ref.shape[1] // 3
     first = tile_index * LANES
@@ -299,42 +318,50 @@
     dkey[...] = jnp.zeros(dkey.shape, wide)
     dvalue[...] = jnp.zeros(dvalue.shape, wide)
     per_tile = LANES // HEAD
+    inner = dattend_ref[:, tile].T.astype(wide) * mixed_ref[first : first + LANES, :]
     for local in range(per_tile):
         head = tile_index * per_tile + local
         mask = head_mask(head)
         key_tile = joined_ref[:, width + first : width + first + LANES] * mask
         value_tile = joined_ref[:, 2 * width + first : 2 * width + first + LANES] * mask
         feature = slice(local * HEAD, (local + 1) * HEAD)
+        weighted = jnp.sum(inner[feature, :], axis=0, keepdims=True)
         for start, stop in query_blocks(rows):
             query = joined_ref[start:stop, tile]
             datt = dattend_ref[start:stop, tile]
-            scores = dot_nt(key_tile[:stop], query)
-            scores = scores * (score_scale * log2_e) + bias_ref[:stop, start:stop]
-            probs = jnp.exp2(scores - log_ref[head : head + 1, start:stop])
+            raw = dot_nt(key_tile[:stop], query)
             dprobs = dot_nt(value_tile[:stop], datt)
-            weighted = jnp.sum(probs * dprobs, axis=0, keepdims=True)
-            dscores = (probs * (dprobs - weighted)).astype(low)
+            logs = log_ref[head : head + 1, start:stop]
+            probs, dscores = [], []
+            for at in range(0, stop, CHUNK):
+                piece = raw[at : at + CHUNK] * (score_scale * log2_e)
+                piece = jnp.exp2(piece + bias_ref[at : at + CHUNK, start:stop] - logs)
+                probs.append(piece.astype(low))
+                piece = piece * (dprobs[at : at + CHUNK] - weighted[:, start:stop])
+                dscores.append(piece.astype(low))
+            probs = jnp.concatenate(probs, axis=0)
+            dscores = jnp.concatenate(dscores, axis=0)
             dquery_t[feature, start:stop] = (
                 dot_nn(keys_t[feature, :stop], dscores) * score_scale
             ).astype(low)
-            dvalue[:stop, :] += dot_nn(probs.astype(low), datt * mask)
+            dvalue[:stop, :] += dot_nn(probs, datt * mask)
             dkey[:stop, :] += dot_nn(dscores, query * mask)
     return dquery_t[...].T, (dkey[...] * score_scale).astype(low), dvalue[...].astype(low)
 
 
-def back_first_kernel(joined_ref, dattend_ref, log_ref, bias_ref, *refs):
-    results, scratch = refs[:3], refs[3:]
-    values = back_tile(0, joined_ref, dattend_ref, log_ref, bias_ref, *scratch)
+def back_first_kernel(*refs):
+    results, scratch = refs[5:8], refs[8:]
+    values = back_tile(0, *refs[:5], *scratch)
     for target, value in zip(results, values):
         target[...] = value
 
 
 def back_last_kernel(shards, *refs):
-    joined_ref, dattend_ref, log_ref, bias_ref = refs[:4]
-    earlier = refs[4:7]
-    norm_ref, root_ref, middle_ref, sums_in = refs[7:11]
-    pieces = refs[11 : 11 + shards]
-    refs = refs[11 + shards :]
+    shared = refs[:5]
+    earlier = refs[5:8]
+    norm_ref, root_ref, middle_ref, sums_in = refs[8:12]
+    pieces = refs[12 : 12 + shards]
+    refs = refs[12 + shards :]
     dx_ref, keep_ref, send_ref = refs[:3]
     weight_ref, small_ref, dquery_t, dkey, dvalue, djoined, grads_ref = refs[3:]
     rows, width = norm_ref.shape
@@ -343,7 +370,7 @@
     fill_cols(weight_ref, shard, pieces, 0, part, width)
     fill_small(small_ref, shard, pieces, 3 * part)
     gain, shift = small_ref[0, 0:1, :], small_ref[0, 1:2, :]
-    values = back_tile(1, joined_ref, dattend_ref, log_ref, bias_ref, dquery_t, dkey, dvalue)
+    values = back_tile(1, *shared, dquery_t, dkey, dvalue)
     for block in range(3):
         at = block * width
         djoined[:, at : at + LANES] = earlier[block][...]
@@ -467,7 +494,7 @@
 
 
 def local_call(kernel, outs, operands, scratch=(), flops=0, name=None, fetch=False):
-    space = pl.ANY if fetch else pltpu.VMEM
+    space = pltpu.HBM if fetch else pltpu.VMEM
     outs = [jax.ShapeDtypeStruct(*out) for out in outs]
     moved = sum(
         math.prod(item.shape) * item.dtype.itemsize for item in list(operands) + outs
@@ -481,7 +508,7 @@
         in_specs=[pl.BlockSpec(memory_space=space)] * len(operands),
         out_specs=[pl.BlockSpec(memory_space=pltpu.VMEM)] * len(outs),
         scratch_shapes=scratch_shapes,
-        compiler_params=pltpu.CompilerParams(vmem_limit_bytes=40 * 1024 * 1024),
+        compiler_params=pltpu.CompilerParams(vmem_limit_bytes=(56 if fetch else 40) * 1024 * 1024),
         cost_estimate=pl.CostEstimate(flops=flops, bytes_accessed=moved, transcendentals=0),
         name=name,
     )(*operands)
@@ -601,7 +628,9 @@
         name="pack_first",
         fetch=True,
     )
-    firsts = gather_near(first_pack, "shard", shards)
+    firsts = {0: first_pack}
+    firsts[2] = exchange(first_pack, "shard", 2)
+    firsts[1] = exchange(first_pack, "shard", 1)
     square = (rows, rows)
     bias, normed, root, seed = local_call(
         functools.partial(prepare_kernel, shards),
@@ -618,19 +647,24 @@
         name="pack_second",
         fetch=True,
     )
-    firsts[2], second_pack = lax.optimization_barrier((firsts[2], second_pack))
+    firsts[2], second_pack, bias, normed, root, seed = lax.optimization_barrier(
+        (firsts[2], second_pack, bias, normed, root, seed)
+    )
+    firsts[3] = exchange(firsts[2], "shard", 1)
+    firsts = [firsts[offset] for offset in range(shards)]
     seconds = {0: second_pack}
     seconds[2] = exchange(second_pack, "shard", 2)
     seconds[1] = exchange(second_pack, "shard", 1)
-    joined, attended, log_sums = local_call(
+    joined, attended, log_sums, mixed = local_call(
         functools.partial(attend_kernel, shards),
-        [((rows, 3 * width), low), ((rows, width), low), ((heads, rows), wide)],
+        [
+            ((rows, 3 * width), low),
+            ((rows, width), low),
+            ((heads, rows), wide),
+            ((width, rows), wide),
+        ],
         [normed, bias] + firsts,
-        [
-            ((width, 3 * width), low),
-            ((shards, SMALL_PAD, width), wide),
-            ((width, rows), low),
-        ],
+        [((width, 3 * width), low), ((shards, SMALL_PAD, width), wide)],
         flops=heads * rows * rows * 256 * 4,
         name="attend",
     )
@@ -660,7 +694,7 @@
         name="feed",
     )
     arrived_ffn = exchange(send_ffn, "shard", 1)
-    shared = [joined, attended_grad, log_sums, bias]
+    shared = [joined, attended_grad, log_sums, bias, mixed]
     tile_scratch = [((LANES, rows), low), ((rows, LANES), wide), ((rows, LANES), wide)]
     first_query, first_key, first_value = local_call(
         back_first_kernel,

time: 77.4 us -> 73.8 us (0.953)
  local copies, waits for them, and re-layouts: 5.39 us -> 0.11 us
  waiting for transfers between devices: 19.9 us -> 23.1 us
  starting transfers between devices: 29.2 us -> 26.9 us
  Pallas kernels: 21.6 us -> 22.4 us
    unnamed x50 -> x42, local copies, waits for them, and re-layouts: 5.39 us -> 0.11 us
    ppermute x21, waiting for transfers between devices: 19.9 us -> 23.1 us  [exchange(): lax.ppermute(values, axis, [(index, index ^ mask) for index in range(coun...]
    ppermute x21, starting transfers between devices: 29.2 us -> 26.9 us  [exchange(): lax.ppermute(values, axis, [(index, index ^ mask) for index in range(coun...]
  transfers between devices with their start and end apart: 21 -> 21, of which waited for: 13 -> 14; matrix products, arithmetic and copies ran while one was open for 0% -> 0% of each run, Pallas kernels for 20% -> 20%
where the time goes in v6:
time: 73.8 us; the launch traced here: 73.6 us
  starting transfers between devices  26.9 us (36%)
  waiting for transfers between devices  23.1 us (31%)
  Pallas kernels  22.4 us (30%)
  between operations  1.06 us (1%)
    ppermute x21, starting transfers between devices, exchange(): lax.ppermute(values, axis, [(index, index ^ mask) for index in range(coun...  26.9 us
    ppermute x21, waiting for transfers between devices, exchange(): lax.ppermute(values, axis, [(index, index ^ mask) for index in range(coun...  23.1 us
    pallas_call x15, Pallas kernels, local_call(): pl.pallas_call(kernel, out_shape=outs, in_specs=[pl.BlockSpec(memory_spac...  22.4 us
  transfers between devices with their start and end apart: 21, of which 14 were waited for; matrix products, arithmetic and copies ran while one was open for 0% of the time, Pallas kernels for 20%

profile of v6, /device:TPU:0, one launch (start us, length us, event | category | flops | bytes accessed | tf_op | source)
XLA Modules:
  0.0 73.6 jit_solution(3319586675798627893)
XLA Ops:
  0.7 1.7 %pack_first.1.refs_2_.refs_3_.refs_12_ = bf16[208,256]{1,0:T(8,128)(2,1)} custom-call(f32[64,768]{1,0:T(8,128)} %refs_8_.1, f32[768]{0:T(1024)} %refs_20_.1), custom_call_target="tpu_custom_call" | custom-call | bytes 306176 | tf_op jit(solution)/shard_map/pack_first/pallas_call | solution.py:505
  2.4 0.0 copy-start.13
  2.4 3.0 %collective-permute-start = (bf16[208,256]{1,0:T(8,128)(2,1)}, bf16[208,256]{1,0:T(8,128)(2,1)S(1)}, u32[]{:S(2)}, u32[]{:S(2)}) collective-permute-start(bf16[208,256]{1,0:T(8,128)(2,1)} %pack_first.1.refs_2_.refs_3_.refs_12_), channel_id=1, source_target_pairs={{0,2},{1,3},{2,0},{3,1},{4,6},{5,7},{6,4},{7,5},{8,10},{9,11},{10,... | collective-permute-start | bytes 319496 | tf_op jit(solution)/shard_map/ppermute | solution.py:519
  5.4 1.8 %pack_second.1.refs_7_ = bf16[576,256]{1,0:T(8,128)(2,1)} custom-call(f32[64,256]{1,0:T(8,128)} %refs_11_.1, f32[64,1024]{1,0:T(8,128)} %refs_14_.1, f32[256,256]{1,0:T(8,128)} %refs_17_.1), custom_call_target="tpu_custom_call" | custom-call | bytes 884736 | tf_op jit(solution)/shard_map/pack_second/pallas_call | solution.py:505
  7.3 0.6 prepare.1
  7.9 0.7 collective-permute-done.refs_4_.refs_5_.refs_14_
  8.6 1.7 %collective-permute-start.3 = (bf16[576,256]{1,0:T(8,128)(2,1)}, bf16[576,256]{1,0:T(8,128)(2,1)S(1)}, u32[]{:S(2)}, u32[]{:S(2)}) collective-permute-start(bf16[576,256]{1,0:T(8,128)(2,1)} %pack_second.1.refs_7_), channel_id=1, source_target_pairs={{0,2},{1,3},{2,0},{3,1},{4,6},{5,7},{6,4},{7,5},{8,10},{9,11},{10,... | collective-permute-start | bytes 884744 | tf_op jit(solution)/shard_map/ppermute | solution.py:519
  10.3 0.2 collective-permute-start.4
  10.6 4.4 %attend.1 = (bf16[512,768]{1,0:T(8,128)(2,1)S(1)}, bf16[512,256]{1,0:T(8,128)(2,1)S(1)}, f32[8,512]{1,0:T(8,128)S(1)}, f32[256,512]{1,0:T(8,128)S(1)}) custom-call(f32[512,256]{1,0:T(8,128)S(1)} %get-tuple-element.82.refs_0_.refs_8_, f32[512,512]{1,0:T(8,128)S(1)} %get-tuple-element.83.refs_1_.refs_3_, bf16[208,256]{1,0:T(8,128)(2,1)S(1)} %copy-done.13, ...), custom_call_target="tpu_custom_call" | custom-call | flops 2147483648 | bytes 3588096 | tf_op jit(solution)/shard_map/attend/pallas_call | solution.py:505
  15.0 3.2 %collective-permute-done.3.refs_9_ = bf16[576,256]{1,0:T(8,128)(2,1)S(1)} collective-permute-done((bf16[576,256]{1,0:T(8,128)(2,1)}, bf16[576,256]{1,0:T(8,128)(2,1)S(1)}, u32[]{:S(2)}, u32[]{:S(2)}) %collective-permute-start.3) | collective-permute-done | bytes 294944 | tf_op jit(solution)/shard_map/ppermute | solution.py:519
  18.2 1.6 %collective-permute-done.5.refs_10_ = bf16[576,256]{1,0:T(8,128)(2,1)S(1)} collective-permute-done((bf16[576,256]{1,0:T(8,128)(2,1)S(1)}, bf16[576,256]{1,0:T(8,128)(2,1)S(1)}, u32[]{:S(2)}, u32[]{:S(2)}) %collective-permute-start.5) | collective-permute-done | bytes 294944 | tf_op jit(solution)/shard_map/ppermute | solution.py:519
  19.8 4.0 %feed.1 = (bf16[512,256]{1,0:T(8,128)(2,1)}, f32[512,256]{1,0:T(8,128)S(1)}, bf16[512,256]{1,0:T(8,128)(2,1)S(1)}, f32[16,256]{1,0:T(8,128)S(1)}, f32[2,576,256]...) custom-call(bf16[512,256]{1,0:T(8,128)(2,1)S(1)} %copy-done.6, bf16[512,256]{1,0:T(8,128)(2,1)S(1)} %get-tuple-element.87.refs_1_, ...), custom_call_target="tpu_custom_call" | custom-call | flops 1811939328 | bytes 5226496 | tf_op jit(solution)/shard_map/feed/pallas_call | solution.py:505
  23.8 0.1 collective-permute-start.6
  23.9 3.0 %back_first.1 = (bf16[512,128]{1,0:T(8,128)(2,1)S(1)}, bf16[512,128]{1,0:T(8,128)(2,1)S(1)}, bf16[512,128]{1,0:T(8,128)(2,1)S(1)}) custom-call(bf16[512,768]{1,0:T(8,128)(2,1)S(1)} %get-tuple-element.91.refs_0_, bf16[512,256]{1,0:T(8,128)(2,1)S(1)} %get-tuple-element.92.refs_1_, f32[8,512]{1,0:T(8,128)S(1)} %get-tuple-element.93.refs_2_, ...), custom_call_target="tpu_custom_call" | custom-call | flops 2684354560 | bytes 3031040 | tf_op jit(solution)/shard_map/back_first/pallas_call | solution.py:505
  26.9 0.1 halve_ffn.1
  27.1 1.8 %collective-permute-start.8 = (bf16[1,576,256]{2,1,0:T(8,128)(2,1)S(1)}, bf16[1,576,256]{2,1,0:T(8,128)(2,1)S(1)}, u32[]{:S(2)}, u32[]{:S(2)}) collective-permute-start(bf16[1,576,256]{2,1,0:T(8,128)(2,1)S(1)} %get-tuple-element.112), channel_id=1, source_target_pairs={{0,2},{1,3},{2,0},{3,1},{4,6},{5,7},{6,4},{7,5},{8,10},{9,11},{10,... | collective-permute-start | bytes 884744 | tf_op jit(solution)/shard_map/ppermute | solution.py:519
  28.9 4.7 %back_last.1 = (f32[512,256]{1,0:T(8,128)}, f32[2,256,256]{2,1,0:T(8,128)S(1)}, bf16[2,256,256]{2,1,0:T(8,128)(2,1)S(1)}) custom-call(bf16[512,768]{1,0:T(8,128)(2,1)S(1)} %get-tuple-element.91.refs_0_, bf16[512,256]{1,0:T(8,128)(2,1)S(1)} %get-tuple-element.92.refs_1_, f32[8,512]{1,0:T(8,128)S(1)} %get-tuple-element.93.refs_2_, ...), custom_call_target="tpu_custom_call" | custom-call | flops 3221225472 | bytes 5834752 | tf_op jit(solution)/shard_map/back_last/pallas_call | solution.py:505
  33.6 0.1 collective-permute-start.7
  33.6 1.5 %collective-permute-done.7.refs_1_ = bf16[2,256,256]{2,1,0:T(8,128)(2,1)S(1)} collective-permute-done((bf16[2,256,256]{2,1,0:T(8,128)(2,1)S(1)}, bf16[2,256,256]{2,1,0:T(8,128)(2,1)S(1)}, u32[]{:S(2)}, u32[]{:S(2)}) %collective-permute-start.7) | collective-permute-done | bytes 262176 | tf_op jit(solution)/shard_map/ppermute | solution.py:519
  35.2 1.2 %collective-permute-done.8 = bf16[1,576,256]{2,1,0:T(8,128)(2,1)S(1)} collective-permute-done((bf16[1,576,256]{2,1,0:T(8,128)(2,1)S(1)}, bf16[1,576,256]{2,1,0:T(8,128)(2,1)S(1)}, u32[]{:S(2)}, u32[]{:S(2)}) %collective-permute-start.8) | collective-permute-done | bytes 294944 | tf_op jit(solution)/shard_map/ppermute | solution.py:519
  36.4 1.7 %collective-permute-start.10 = (bf16[1,256,256]{2,1,0:T(8,128)(2,1)S(1)}, bf16[1,256,256]{2,1,0:T(8,128)(2,1)S(1)}, u32[]{:S(2)}, u32[]{:S(2)}) collective-permute-start(bf16[1,256,256]{2,1,0:T(8,128)(2,1)S(1)} %get-tuple-element.117), channel_id=1, source_target_pairs={{0,2},{1,3},{2,0},{3,1},{4,6},{5,7},{6,4},{7,5},{8,10},{9,11},{10,... | collective-permute-start | bytes 393224 | tf_op jit(solution)/shard_map/ppermute | solution.py:519
  38.2 0.0 copy-start.7
  38.2 0.0 copy-start.8
  38.2 0.0 copy-start.11
  38.2 0.0 copy-start.12
  38.3 0.1 split_sum.2
  38.4 1.6 %collective-permute-start.9 = (bf16[4,72,256]{2,1,0:T(8,128)(2,1)S(1)}, bf16[4,72,256]{2,1,0:T(8,128)(2,1)S(1)}, u32[]{:S(2)}, u32[]{:S(2)}) collective-permute-start(bf16[4,72,256]{2,1,0:T(8,128)(2,1)S(1)} %get-tuple-element.115), channel_id=1, source_target_pairs={{0,4},{4,0},{8,12},{12,8},{16,20},{20,16},{24,28},{28,24},{1,5},{5... | collective-permute-start | bytes 442376 | tf_op jit(solution)/shard_map/ppermute | solution.py:519
  40.0 1.4 %collective-permute-done.10 = bf16[1,256,256]{2,1,0:T(8,128)(2,1)S(1)} collective-permute-done((bf16[1,256,256]{2,1,0:T(8,128)(2,1)S(1)}, bf16[1,256,256]{2,1,0:T(8,128)(2,1)S(1)}, u32[]{:S(2)}, u32[]{:S(2)}) %collective-permute-start.10) | collective-permute-done | bytes 131104 | tf_op jit(solution)/shard_map/ppermute | solution.py:519
  41.4 0.1 split_sum.3
  41.4 1.8 %collective-permute-start.11 = (bf16[4,32,256]{2,1,0:T(8,128)(2,1)S(1)}, bf16[4,32,256]{2,1,0:T(8,128)(2,1)S(1)}, u32[]{:S(2)}, u32[]{:S(2)}) collective-permute-start(bf16[4,32,256]{2,1,0:T(8,128)(2,1)S(1)} %get-tuple-element.119), channel_id=1, source_target_pairs={{0,4},{4,0},{8,12},{12,8},{16,20},{20,16},{24,28},{28,24},{1,5},{5... | collective-permute-start | bytes 196616 | tf_op jit(solution)/shard_map/ppermute | solution.py:519
  43.2 1.1 %collective-permute-done.9.refs_1_ = bf16[4,72,256]{2,1,0:T(8,128)(2,1)S(1)} collective-permute-done((bf16[4,72,256]{2,1,0:T(8,128)(2,1)S(1)}, bf16[4,72,256]{2,1,0:T(8,128)(2,1)S(1)}, u32[]{:S(2)}, u32[]{:S(2)}) %collective-permute-start.9) | collective-permute-done | bytes 147488 | tf_op jit(solution)/shard_map/ppermute | solution.py:519
  44.3 1.4 %collective-permute-done.11.refs_3_ = bf16[4,32,256]{2,1,0:T(8,128)(2,1)S(1)} collective-permute-done((bf16[4,32,256]{2,1,0:T(8,128)(2,1)S(1)}, bf16[4,32,256]{2,1,0:T(8,128)(2,1)S(1)}, u32[]{:S(2)}, u32[]{:S(2)}) %collective-permute-start.11) | collective-permute-done | bytes 65568 | tf_op jit(solution)/shard_map/ppermute | solution.py:519
  45.8 1.9 %collective-permute-start.12 = (bf16[2,104,256]{2,1,0:T(8,128)(2,1)S(1)}, bf16[2,104,256]{2,1,0:T(8,128)(2,1)S(1)}, u32[]{:S(2)}, u32[]{:S(2)}) collective-permute-start(bf16[2,104,256]{2,1,0:T(8,128)(2,1)S(1)} %get-tuple-element.121), channel_id=1, source_target_pairs={{0,8},{4,12},{8,0},{12,4},{16,24},{20,28},{24,16},{28,20},{1,9},{5... | collective-permute-start | bytes 319496 | tf_op jit(solution)/shard_map/ppermute | solution.py:519
  47.7 2.9 %collective-permute-done.12.refs_1_ = bf16[2,104,256]{2,1,0:T(8,128)(2,1)S(1)} collective-permute-done((bf16[2,104,256]{2,1,0:T(8,128)(2,1)S(1)}, bf16[2,104,256]{2,1,0:T(8,128)(2,1)S(1)}, u32[]{:S(2)}, u32[]{:S(2)}) %collective-permute-start.12) | collective-permute-done | bytes 106528 | tf_op jit(solution)/shard_map/ppermute | solution.py:519
  50.6 3.3 %collective-permute-start.13 = (bf16[1,104,256]{2,1,0:T(8,128)(2,1)S(1)}, bf16[1,104,256]{2,1,0:T(8,128)(2,1)S(1)}, u32[]{:S(2)}, u32[]{:S(2)}) collective-permute-start(bf16[1,104,256]{2,1,0:T(8,128)(2,1)S(1)} %get-tuple-element.123), channel_id=1, source_target_pairs={{0,16},{4,20},{8,24},{12,28},{16,0},{20,4},{24,8},{28,12},{1,17},{... | collective-permute-start | bytes 159752 | tf_op jit(solution)/shard_map/ppermute | solution.py:519
  53.9 3.9 %collective-permute-done.13.other_ref = bf16[1,104,256]{2,1,0:T(8,128)(2,1)S(1)} collective-permute-done((bf16[1,104,256]{2,1,0:T(8,128)(2,1)S(1)}, bf16[1,104,256]{2,1,0:T(8,128)(2,1)S(1)}, u32[]{:S(2)}, u32[]{:S(2)}) %collective-permute-start.13) | collective-permute-done | bytes 53280 | tf_op jit(solution)/shard_map/ppermute | solution.py:519
  57.8 1.6 %collective-permute-start.17 = (bf16[104,256]{1,0:T(8,128)(2,1)S(1)}, bf16[104,256]{1,0:T(8,128)(2,1)S(1)}, u32[]{:S(2)}, u32[]{:S(2)}) collective-permute-start(bf16[104,256]{1,0:T(8,128)(2,1)S(1)} %piece_sum.1.refs_0_), channel_id=1, source_target_pairs={{0,16},{4,20},{8,24},{12,28},{16,0},{20,4},{24,8},{28,12},{1,17},{... | collective-permute-start | bytes 159752 | tf_op jit(solution)/shard_map/ppermute | solution.py:519
  59.4 2.5 %collective-permute-start.15 = (bf16[104,256]{1,0:T(8,128)(2,1)S(1)}, bf16[104,256]{1,0:T(8,128)(2,1)S(1)}, u32[]{:S(2)}, u32[]{:S(2)}) collective-permute-start(bf16[104,256]{1,0:T(8,128)(2,1)S(1)} %piece_sum.1.refs_0_), channel_id=1, source_target_pairs={{0,8},{4,12},{8,0},{12,4},{16,24},{20,28},{24,16},{28,20},{1,9},{5... | collective-permute-start | bytes 159752 | tf_op jit(solution)/shard_map/ppermute | solution.py:519
  61.8 1.1 %collective-permute-done.17.refs_4_ = bf16[104,256]{1,0:T(8,128)(2,1)S(1)} collective-permute-done((bf16[104,256]{1,0:T(8,128)(2,1)S(1)}, bf16[104,256]{1,0:T(8,128)(2,1)S(1)}, u32[]{:S(2)}, u32[]{:S(2)}) %collective-permute-start.17) | collective-permute-done | bytes 53280 | tf_op jit(solution)/shard_map/ppermute | solution.py:519
  62.9 1.1 %collective-permute-start.19 = (bf16[104,256]{1,0:T(8,128)(2,1)S(1)}, bf16[104,256]{1,0:T(8,128)(2,1)S(1)}, u32[]{:S(2)}, u32[]{:S(2)}) collective-permute-start(bf16[104,256]{1,0:T(8,128)(2,1)S(1)} %collective-permute-done.17.refs_4_), channel_id=1, source_target_pairs={{0,8},{4,12},{8,0},{12,4},{16,24},{20,28},{24,16},{28,20},{1,9},{5... | collective-permute-start | bytes 159752 | tf_op jit(solution)/shard_map/ppermute | solution.py:519
  64.0 1.5 %collective-permute-start.14 = (bf16[104,256]{1,0:T(8,128)(2,1)S(1)}, bf16[104,256]{1,0:T(8,128)(2,1)S(1)}, u32[]{:S(2)}, u32[]{:S(2)}) collective-permute-start(bf16[104,256]{1,0:T(8,128)(2,1)S(1)} %piece_sum.1.refs_0_), channel_id=1, source_target_pairs={{0,4},{4,0},{8,12},{12,8},{16,20},{20,16},{24,28},{28,24},{1,5},{5... | collective-permute-start | bytes 159752 | tf_op jit(solution)/shard_map/ppermute | solution.py:519
  65.5 0.5 collective-permute-start.18
  66.0 1.5 %collective-permute-start.16 = (bf16[104,256]{1,0:T(8,128)(2,1)S(1)}, bf16[104,256]{1,0:T(8,128)(2,1)S(1)}, u32[]{:S(2)}, u32[]{:S(2)}) collective-permute-start(bf16[104,256]{1,0:T(8,128)(2,1)S(1)} %collective-permute-done.15.refs_2_), channel_id=1, source_target_pairs={{0,4},{4,0},{8,12},{12,8},{16,20},{20,16},{24,28},{28,24},{1,5},{5... | collective-permute-start | bytes 159752 | tf_op jit(solution)/shard_map/ppermute | solution.py:519
  67.5 1.0 %collective-permute-start.20 = (bf16[104,256]{1,0:T(8,128)(2,1)S(1)}, bf16[104,256]{1,0:T(8,128)(2,1)S(1)}, u32[]{:S(2)}, u32[]{:S(2)}) collective-permute-start(bf16[104,256]{1,0:T(8,128)(2,1)S(1)} %collective-permute-done.19.refs_6_), channel_id=1, source_target_pairs={{0,4},{4,0},{8,12},{12,8},{16,20},{20,16},{24,28},{28,24},{1,5},{5... | collective-permute-start | bytes 159752 | tf_op jit(solution)/shard_map/ppermute | solution.py:519
  68.5 1.1 %collective-permute-done.18.refs_5_ = bf16[104,256]{1,0:T(8,128)(2,1)S(1)} collective-permute-done((bf16[104,256]{1,0:T(8,128)(2,1)S(1)}, bf16[104,256]{1,0:T(8,128)(2,1)S(1)}, u32[]{:S(2)}, u32[]{:S(2)}) %collective-permute-start.18) | collective-permute-done | bytes 53280 | tf_op jit(solution)/shard_map/ppermute | solution.py:519
  69.6 0.6 collective-permute-done.16.refs_3_
  70.2 1.5 %collective-permute-done.20.refs_7_ = bf16[104,256]{1,0:T(8,128)(2,1)S(1)} collective-permute-done((bf16[104,256]{1,0:T(8,128)(2,1)S(1)}, bf16[104,256]{1,0:T(8,128)(2,1)S(1)}, u32[]{:S(2)}, u32[]{:S(2)}) %collective-permute-start.20) | collective-permute-done | bytes 53280 | tf_op jit(solution)/shard_map/ppermute | solution.py:519
  71.8 1.8 %adam.1 = (f32[64,768]{1,0:T(8,128)}, f32[64,768]{1,0:T(8,128)}, f32[64,768]{1,0:T(8,128)}, f32[64,256]{1,0:T(8,128)}, f32[64,256]{1,0:T(8,128)}, /*index=5*/f32...) custom-call(bf16[104,256]{1,0:T(8,128)(2,1)S(1)} %piece_sum.1.refs_0, ...), custom_call_target="tpu_custom_call" | custom-call | bytes 5163008 | tf_op jit(solution)/shard_map/adam/pallas_call | solution.py:505
  (51 shorter events, 0.2 us)
Async XLA Ops:
  0.7 6.6 %copy-start.6 = (bf16[512,256]{1,0:T(8,128)(2,1)S(1)}, bf16[512,256]{1,0:T(8,128)(2,1)}, u32[]{:S(2)}) copy-start(bf16[512,256]{1,0:T(8,128)(2,1)} %refs_0_.1) | copy-start | bytes 786436
  0.7 6.6 %copy-start.20 = (s32[128]{0:T(128)S(1)}, s32[128]{0:T(128)}, u32[]{:S(2)}) copy-start(s32[128]{0:T(128)} %param.22) | copy-start | bytes 1540
  0.7 6.6 %copy-start.19 = (s32[128]{0:T(128)S(1)}, s32[128]{0:T(128)}, u32[]{:S(2)}) copy-start(s32[128]{0:T(128)} %param.21) | copy-start | bytes 1540
  0.7 6.6 %copy-start.5 = (bf16[512,256]{1,0:T(8,128)(2,1)S(1)}, bf16[512,256]{1,0:T(8,128)(2,1)}, u32[]{:S(2)}) copy-start(bf16[512,256]{1,0:T(8,128)(2,1)} %seed_ref.1) | copy-start | bytes 786436
  2.4 8.2 %copy-start.13 = (bf16[208,256]{1,0:T(8,128)(2,1)S(1)}, bf16[208,256]{1,0:T(8,128)(2,1)}, u32[]{:S(2)}) copy-start(bf16[208,256]{1,0:T(8,128)(2,1)} %pack_first.1.refs_2_.refs_3_.refs_12_) | copy-start | bytes 319492
  2.4 6.2 %collective-permute-start = (bf16[208,256]{1,0:T(8,128)(2,1)}, bf16[208,256]{1,0:T(8,128)(2,1)S(1)}, u32[]{:S(2)}, u32[]{:S(2)}) collective-permute-start(bf16[208,256]{1,0:T(8,128)(2,1)} %pack_first.1.refs_2_.refs_3_.refs_12_), channel_id=1, source_target_pairs={{0,2},{1,3},{2,0},{3,1},{4,6},{5,7},{6,4},{7,5},{8,10},{9,11},{10,... | collective-permute-start | bytes 319496 | tf_op jit(solution)/shard_map/ppermute | solution.py:519
  5.4 5.2 %collective-permute-start.1 = (bf16[208,256]{1,0:T(8,128)(2,1)}, bf16[208,256]{1,0:T(8,128)(2,1)S(1)}, u32[]{:S(2)}, u32[]{:S(2)}) collective-permute-start(bf16[208,256]{1,0:T(8,128)(2,1)} %pack_first.1.refs_2_.refs_3_.refs_12_), channel_id=1, source_target_pairs={{0,1},{1,0},{2,3},{3,2},{4,5},{5,4},{6,7},{7,6},{8,9},{9,8},{10,11... | collective-permute-start | bytes 319496 | tf_op jit(solution)/shard_map/ppermute | solution.py:519
  8.6 11.2 %copy-start.3 = (bf16[576,256]{1,0:T(8,128)(2,1)S(1)}, bf16[576,256]{1,0:T(8,128)(2,1)}, u32[]{:S(2)}) copy-start(bf16[576,256]{1,0:T(8,128)(2,1)} %pack_second.1.refs_7_) | copy-start | bytes 884740
  8.6 2.0 %collective-permute-start.2 = (bf16[208,256]{1,0:T(8,128)(2,1)S(1)}, bf16[208,256]{1,0:T(8,128)(2,1)S(1)}, u32[]{:S(2)}, u32[]{:S(2)}) collective-permute-start(bf16[208,256]{1,0:T(8,128)(2,1)S(1)} %collective-permute-done.refs_4_.refs_5_.refs_14_), channel_id=1, source_target_pairs={{0,1},{1,0},{2,3},{3,2},{4,5},{5,4},{6,7},{7,6},{8,9},{9,8},{10,11... | collective-permute-start | bytes 319496 | tf_op jit(solution)/shard_map/ppermute | solution.py:519
  8.6 9.6 %collective-permute-start.3 = (bf16[576,256]{1,0:T(8,128)(2,1)}, bf16[576,256]{1,0:T(8,128)(2,1)S(1)}, u32[]{:S(2)}, u32[]{:S(2)}) collective-permute-start(bf16[576,256]{1,0:T(8,128)(2,1)} %pack_second.1.refs_7_), channel_id=1, source_target_pairs={{0,2},{1,3},{2,0},{3,1},{4,6},{5,7},{6,4},{7,5},{8,10},{9,11},{10,... | collective-permute-start | bytes 884744 | tf_op jit(solution)/shard_map/ppermute | solution.py:519
  10.3 7.9 %collective-permute-start.4 = (bf16[576,256]{1,0:T(8,128)(2,1)}, bf16[576,256]{1,0:T(8,128)(2,1)S(1)}, u32[]{:S(2)}, u32[]{:S(2)}) collective-permute-start(bf16[576,256]{1,0:T(8,128)(2,1)} %pack_second.1.refs_7_), channel_id=1, source_target_pairs={{0,1},{1,0},{2,3},{3,2},{4,5},{5,4},{6,7},{7,6},{8,9},{9,8},{10,11... | collective-permute-start | bytes 884744 | tf_op jit(solution)/shard_map/ppermute | solution.py:519
  18.2 1.6 %collective-permute-start.5 = (bf16[576,256]{1,0:T(8,128)(2,1)S(1)}, bf16[576,256]{1,0:T(8,128)(2,1)S(1)}, u32[]{:S(2)}, u32[]{:S(2)}) collective-permute-start(bf16[576,256]{1,0:T(8,128)(2,1)S(1)} %collective-permute-done.3.refs_9_), channel_id=1, source_target_pairs={{0,1},{1,0},{2,3},{3,2},{4,5},{5,4},{6,7},{7,6},{8,9},{9,8},{10,11... | collective-permute-start | bytes 884744 | tf_op jit(solution)/shard_map/ppermute | solution.py:519
  23.8 3.1 %collective-permute-start.6 = (bf16[2,576,256]{2,1,0:T(8,128)(2,1)S(1)}, bf16[2,576,256]{2,1,0:T(8,128)(2,1)S(1)}, u32[]{:S(2)}, u32[]{:S(2)}) collective-permute-start(bf16[2,576,256]{2,1,0:T(8,128)(2,1)S(1)} %get-tuple-element.96), channel_id=1, source_target_pairs={{0,1},{1,0},{2,3},{3,2},{4,5},{5,4},{6,7},{7,6},{8,9},{9,8},{10,11... | collective-permute-start | bytes 1769480 | tf_op jit(solution)/shard_map/ppermute | solution.py:519
  27.1 9.4 %collective-permute-start.8 = (bf16[1,576,256]{2,1,0:T(8,128)(2,1)S(1)}, bf16[1,576,256]{2,1,0:T(8,128)(2,1)S(1)}, u32[]{:S(2)}, u32[]{:S(2)}) collective-permute-start(bf16[1,576,256]{2,1,0:T(8,128)(2,1)S(1)} %get-tuple-element.112), channel_id=1, source_target_pairs={{0,2},{1,3},{2,0},{3,1},{4,6},{5,7},{6,4},{7,5},{8,10},{9,11},{10,... | collective-permute-start | bytes 884744 | tf_op jit(solution)/shard_map/ppermute | solution.py:519
  33.6 1.5 %collective-permute-start.7 = (bf16[2,256,256]{2,1,0:T(8,128)(2,1)S(1)}, bf16[2,256,256]{2,1,0:T(8,128)(2,1)S(1)}, u32[]{:S(2)}, u32[]{:S(2)}) collective-permute-start(bf16[2,256,256]{2,1,0:T(8,128)(2,1)S(1)} %get-tuple-element.110), channel_id=1, source_target_pairs={{0,1},{1,0},{2,3},{3,2},{4,5},{5,4},{6,7},{7,6},{8,9},{9,8},{10,11... | collective-permute-start | bytes 786440 | tf_op jit(solution)/shard_map/ppermute | solution.py:519
  36.4 5.0 %collective-permute-start.10 = (bf16[1,256,256]{2,1,0:T(8,128)(2,1)S(1)}, bf16[1,256,256]{2,1,0:T(8,128)(2,1)S(1)}, u32[]{:S(2)}, u32[]{:S(2)}) collective-permute-start(bf16[1,256,256]{2,1,0:T(8,128)(2,1)S(1)} %get-tuple-element.117), channel_id=1, source_target_pairs={{0,2},{1,3},{2,0},{3,1},{4,6},{5,7},{6,4},{7,5},{8,10},{9,11},{10,... | collective-permute-start | bytes 393224 | tf_op jit(solution)/shard_map/ppermute | solution.py:519
  38.1 33.5 %copy-start = (f32[64,1024]{1,0:T(8,128)S(1)}, f32[64,1024]{1,0:T(8,128)}, u32[]{:S(2)}) copy-start(f32[64,1024]{1,0:T(8,128)} %refs_14_.1) | copy-start | bytes 786436
  38.1 33.5 %copy-start.1 = (f32[256,256]{1,0:T(8,128)S(1)}, f32[256,256]{1,0:T(8,128)}, u32[]{:S(2)}) copy-start(f32[256,256]{1,0:T(8,128)} %refs_17_.1) | copy-start | bytes 786436
  38.1 33.5 %copy-start.2 = (f32[64,768]{1,0:T(8,128)S(1)}, f32[64,768]{1,0:T(8,128)}, u32[]{:S(2)}) copy-start(f32[64,768]{1,0:T(8,128)} %refs_8_.1) | copy-start | bytes 589828
  38.2 33.5 %copy-start.4 = (f32[64,256]{1,0:T(8,128)S(1)}, f32[64,256]{1,0:T(8,128)}, u32[]{:S(2)}) copy-start(f32[64,256]{1,0:T(8,128)} %refs_11_.1) | copy-start | bytes 196612
  38.2 33.5 %copy-start.7 = (f32[64,1024]{1,0:T(8,128)S(1)}, f32[64,1024]{1,0:T(8,128)}, u32[]{:S(2)}) copy-start(f32[64,1024]{1,0:T(8,128)} %refs_15_.1) | copy-start | bytes 786436
  38.2 33.5 %copy-start.8 = (f32[64,1024]{1,0:T(8,128)S(1)}, f32[64,1024]{1,0:T(8,128)}, u32[]{:S(2)}) copy-start(f32[64,1024]{1,0:T(8,128)} %refs_16_.1) | copy-start | bytes 786436
  38.2 33.5 %copy-start.9 = (f32[256,256]{1,0:T(8,128)S(1)}, f32[256,256]{1,0:T(8,128)}, u32[]{:S(2)}) copy-start(f32[256,256]{1,0:T(8,128)} %refs_18_.1) | copy-start | bytes 786436
  38.2 33.5 %copy-start.10 = (f32[256,256]{1,0:T(8,128)S(1)}, f32[256,256]{1,0:T(8,128)}, u32[]{:S(2)}) copy-start(f32[256,256]{1,0:T(8,128)} %refs_19_.1) | copy-start | bytes 786436
  38.2 33.5 %copy-start.11 = (f32[64,768]{1,0:T(8,128)S(1)}, f32[64,768]{1,0:T(8,128)}, u32[]{:S(2)}) copy-start(f32[64,768]{1,0:T(8,128)} %refs_9_.1) | copy-start | bytes 589828
  38.2 33.5 %copy-start.12 = (f32[64,768]{1,0:T(8,128)S(1)}, f32[64,768]{1,0:T(8,128)}, u32[]{:S(2)}) copy-start(f32[64,768]{1,0:T(8,128)} %refs_10_.1) | copy-start | bytes 589828
  38.2 33.5 %copy-start.14 = (f32[64,256]{1,0:T(8,128)S(1)}, f32[64,256]{1,0:T(8,128)}, u32[]{:S(2)}) copy-start(f32[64,256]{1,0:T(8,128)} %refs_12_.1) | copy-start | bytes 196612
  38.2 33.5 %copy-start.15 = (f32[64,256]{1,0:T(8,128)S(1)}, f32[64,256]{1,0:T(8,128)}, u32[]{:S(2)}) copy-start(f32[64,256]{1,0:T(8,128)} %refs_13_.1) | copy-start | bytes 196612
  38.3 33.5 %copy-start.16 = (f32[768]{0:T(1024)S(1)}, f32[768]{0:T(1024)}, u32[]{:S(2)}) copy-start(f32[768]{0:T(1024)} %refs_20_.1) | copy-start | bytes 9220
  38.3 33.5 %copy-start.17 = (f32[768]{0:T(1024)S(1)}, f32[768]{0:T(1024)}, u32[]{:S(2)}) copy-start(f32[768]{0:T(1024)} %refs_21_.1) | copy-start | bytes 9220
  38.3 33.5 %copy-start.18 = (f32[768]{0:T(1024)S(1)}, f32[768]{0:T(1024)}, u32[]{:S(2)}) copy-start(f32[768]{0:T(1024)} %refs_22_.1) | copy-start | bytes 9220
  38.4 5.9 %collective-permute-start.9 = (bf16[4,72,256]{2,1,0:T(8,128)(2,1)S(1)}, bf16[4,72,256]{2,1,0:T(8,128)(2,1)S(1)}, u32[]{:S(2)}, u32[]{:S(2)}) collective-permute-start(bf16[4,72,256]{2,1,0:T(8,128)(2,1)S(1)} %get-tuple-element.115), channel_id=1, source_target_pairs={{0,4},{4,0},{8,12},{12,8},{16,20},{20,16},{24,28},{28,24},{1,5},{5... | collective-permute-start | bytes 442376 | tf_op jit(solution)/shard_map/ppermute | solution.py:519
  41.4 4.3 %collective-permute-start.11 = (bf16[4,32,256]{2,1,0:T(8,128)(2,1)S(1)}, bf16[4,32,256]{2,1,0:T(8,128)(2,1)S(1)}, u32[]{:S(2)}, u32[]{:S(2)}) collective-permute-start(bf16[4,32,256]{2,1,0:T(8,128)(2,1)S(1)} %get-tuple-element.119), channel_id=1, source_target_pairs={{0,4},{4,0},{8,12},{12,8},{16,20},{20,16},{24,28},{28,24},{1,5},{5... | collective-permute-start | bytes 196616 | tf_op jit(solution)/shard_map/ppermute | solution.py:519
  45.8 4.8 %collective-permute-start.12 = (bf16[2,104,256]{2,1,0:T(8,128)(2,1)S(1)}, bf16[2,104,256]{2,1,0:T(8,128)(2,1)S(1)}, u32[]{:S(2)}, u32[]{:S(2)}) collective-permute-start(bf16[2,104,256]{2,1,0:T(8,128)(2,1)S(1)} %get-tuple-element.121), channel_id=1, source_target_pairs={{0,8},{4,12},{8,0},{12,4},{16,24},{20,28},{24,16},{28,20},{1,9},{5... | collective-permute-start | bytes 319496 | tf_op jit(solution)/shard_map/ppermute | solution.py:519
  50.6 7.2 %collective-permute-start.13 = (bf16[1,104,256]{2,1,0:T(8,128)(2,1)S(1)}, bf16[1,104,256]{2,1,0:T(8,128)(2,1)S(1)}, u32[]{:S(2)}, u32[]{:S(2)}) collective-permute-start(bf16[1,104,256]{2,1,0:T(8,128)(2,1)S(1)} %get-tuple-element.123), channel_id=1, source_target_pairs={{0,16},{4,20},{8,24},{12,28},{16,0},{20,4},{24,8},{28,12},{1,17},{... | collective-permute-start | bytes 159752 | tf_op jit(solution)/shard_map/ppermute | solution.py:519
  57.8 5.1 %collective-permute-start.17 = (bf16[104,256]{1,0:T(8,128)(2,1)S(1)}, bf16[104,256]{1,0:T(8,128)(2,1)S(1)}, u32[]{:S(2)}, u32[]{:S(2)}) collective-permute-start(bf16[104,256]{1,0:T(8,128)(2,1)S(1)} %piece_sum.1.refs_0_), channel_id=1, source_target_pairs={{0,16},{4,20},{8,24},{12,28},{16,0},{20,4},{24,8},{28,12},{1,17},{... | collective-permute-start | bytes 159752 | tf_op jit(solution)/shard_map/ppermute | solution.py:519
  59.4 6.7 %collective-permute-start.15 = (bf16[104,256]{1,0:T(8,128)(2,1)S(1)}, bf16[104,256]{1,0:T(8,128)(2,1)S(1)}, u32[]{:S(2)}, u32[]{:S(2)}) collective-permute-start(bf16[104,256]{1,0:T(8,128)(2,1)S(1)} %piece_sum.1.refs_0_), channel_id=1, source_target_pairs={{0,8},{4,12},{8,0},{12,4},{16,24},{20,28},{24,16},{28,20},{1,9},{5... | collective-permute-start | bytes 159752 | tf_op jit(solution)/shard_map/ppermute | solution.py:519
  62.9 4.6 %collective-permute-start.19 = (bf16[104,256]{1,0:T(8,128)(2,1)S(1)}, bf16[104,256]{1,0:T(8,128)(2,1)S(1)}, u32[]{:S(2)}, u32[]{:S(2)}) collective-permute-start(bf16[104,256]{1,0:T(8,128)(2,1)S(1)} %collective-permute-done.17.refs_4_), channel_id=1, source_target_pairs={{0,8},{4,12},{8,0},{12,4},{16,24},{20,28},{24,16},{28,20},{1,9},{5... | collective-permute-start | bytes 159752 | tf_op jit(solution)/shard_map/ppermute | solution.py:519
  64.0 4.5 %collective-permute-start.14 = (bf16[104,256]{1,0:T(8,128)(2,1)S(1)}, bf16[104,256]{1,0:T(8,128)(2,1)S(1)}, u32[]{:S(2)}, u32[]{:S(2)}) collective-permute-start(bf16[104,256]{1,0:T(8,128)(2,1)S(1)} %piece_sum.1.refs_0_), channel_id=1, source_target_pairs={{0,4},{4,0},{8,12},{12,8},{16,20},{20,16},{24,28},{28,24},{1,5},{5... | collective-permute-start | bytes 159752 | tf_op jit(solution)/shard_map/ppermute | solution.py:519
  65.5 4.1 %collective-permute-start.18 = (bf16[104,256]{1,0:T(8,128)(2,1)S(1)}, bf16[104,256]{1,0:T(8,128)(2,1)S(1)}, u32[]{:S(2)}, u32[]{:S(2)}) collective-permute-start(bf16[104,256]{1,0:T(8,128)(2,1)S(1)} %collective-permute-done.17.refs_4_), channel_id=1, source_target_pairs={{0,4},{4,0},{8,12},{12,8},{16,20},{20,16},{24,28},{28,24},{1,5},{5... | collective-permute-start | bytes 159752 | tf_op jit(solution)/shard_map/ppermute | solution.py:519
  66.0 4.2 %collective-permute-start.16 = (bf16[104,256]{1,0:T(8,128)(2,1)S(1)}, bf16[104,256]{1,0:T(8,128)(2,1)S(1)}, u32[]{:S(2)}, u32[]{:S(2)}) collective-permute-start(bf16[104,256]{1,0:T(8,128)(2,1)S(1)} %collective-permute-done.15.refs_2_), channel_id=1, source_target_pairs={{0,4},{4,0},{8,12},{12,8},{16,20},{20,16},{24,28},{28,24},{1,5},{5... | collective-permute-start | bytes 159752 | tf_op jit(solution)/shard_map/ppermute | solution.py:519
  67.5 4.1 %collective-permute-start.20 = (bf16[104,256]{1,0:T(8,128)(2,1)S(1)}, bf16[104,256]{1,0:T(8,128)(2,1)S(1)}, u32[]{:S(2)}, u32[]{:S(2)}) collective-permute-start(bf16[104,256]{1,0:T(8,128)(2,1)S(1)} %collective-permute-done.19.refs_6_), channel_id=1, source_target_pairs={{0,4},{4,0},{8,12},{12,8},{16,20},{20,16},{24,28},{28,24},{1,5},{5... | collective-permute-start | bytes 159752 | tf_op jit(solution)/shard_map/ppermute | solution.py:519

commit v7 on v6

--- a/solution.py
+++ b/solution.py
@@ -198,30 +198,39 @@
             value = value + bias
         joined_ref[:, cols] = value.astype(low)
     values_t = joined_ref[:, 2 * width :].T
-    for head in range(width // HEAD):
+    units = [
+        (head, start, stop) for head in range(width // HEAD) for start, stop in query_blocks(rows)
+    ]
+
+    def raw_scores(head, start, stop):
         tile = head_tile(head)
-        key_tile = joined_ref[:, width + tile.start : width + tile.stop] * head_mask(head)
+        key_tile = joined_ref[:stop, width + tile.start : width + tile.stop] * head_mask(head)
+        return dot_nt(key_tile, joined_ref[start:stop, tile])
+
+    ahead = raw_scores(*units[0])
+    for index, (head, start, stop) in enumerate(units):
+        raw = ahead
+        if index + 1 < len(units):
+            ahead = raw_scores(*units[index + 1])
         feature = slice(head * HEAD, (head + 1) * HEAD)
-        for start, stop in query_blocks(rows):
-            raw = dot_nt(key_tile[:stop], joined_ref[start:stop, tile])
-            scores = []
-            top = None
-            for at in range(0, stop, CHUNK):
-                piece = raw[at : at + CHUNK] * (score_scale * log2_e)
-                piece = piece + bias_ref[at : at + CHUNK, start:stop]
-                scores.append(piece)
-                top = piece if top is None else jnp.maximum(top, piece)
-            top = jnp.max(top, axis=0, keepdims=True)
-            exponents = []
-            total = None
-            for piece in scores:
-                piece = jnp.exp2(piece - top)
-                total = piece if total is None else total + piece
-                exponents.append(piece.astype(low))
-            total = jnp.sum(total, axis=0, keepdims=True)
-            mixed = dot_nn(values_t[feature, :stop], jnp.concatenate(exponents, axis=0))
-            att_ref[feature, start:stop] = mixed * (1.0 / total)
-            log_ref[head : head + 1, start:stop] = top + jnp.log2(total)
+        scores = []
+        top = None
+        for at in range(0, stop, CHUNK):
+            piece = raw[at : at + CHUNK] * (score_scale * log2_e)
+            piece = piece + bias_ref[at : at + CHUNK, start:stop]
+            scores.append(piece)
+            top = piece if top is None else jnp.maximum(top, piece)
+        top = jnp.max(top, axis=0, keepdims=True)
+        exponents = []
+        total = None
+        for piece in scores:
+            piece = jnp.exp2(piece - top)
+            total = piece if total is None else total + piece
+            exponents.append(piece.astype(low))
+        total = jnp.sum(total, axis=0, keepdims=True)
+        mixed = dot_nn(values_t[feature, :stop], jnp.concatenate(exponents, axis=0))
+        att_ref[feature, start:stop] = mixed * (1.0 / total)
+        log_ref[head : head + 1, start:stop] = top + jnp.log2(total)
     out_ref[...] = att_ref[...].astype(low).T
 
 
@@ -255,10 +264,17 @@
     result = middle + bias_down
     dhidden = jnp.zeros((rows, width), wide)
     sums_ref[...] = jnp.zeros(sums_ref.shape, wide)
+
+    def raw_products(block):
+        cols = slice(block * width, (block + 1) * width)
+        return dot_nn(hidden, up_w[:, cols]), dot_nt(seed_low, down_w[cols, :])
+
+    ahead = raw_products(0)
     for block in range(blocks):
         cols = slice(block * width, (block + 1) * width)
-        raw = dot_nn(hidden, up_w[:, cols])
-        dact = dot_nt(seed_low, down_w[cols, :])
+        raw, dact = ahead
+        if block + 1 < blocks:
+            ahead = raw_products(block + 1)
         act, dpre = [], []
         for at in range(0, rows, CHUNK):
             pre = raw[at : at + CHUNK] + bias_up[block]
@@ -307,56 +323,64 @@
         send_ref[pair] = grads_ref[2 * pair + 1 - side].astype(low)
 
 
-def back_tile(
-    tile_index, joined_ref, dattend_ref, log_ref, bias_ref, mixed_ref, dquery_t, dkey, dvalue
+def back_heads(
+    heads, joined_ref, dattend_ref, log_ref, bias_ref, mixed_ref, dquery_t, dkey, dvalue
 ):
     rows = joined_ref.shape[0]
     width = joined_ref.shape[1] // 3
-    first = tile_index * LANES
-    tile = slice(first, first + LANES)
-    keys_t = joined_ref[:, width + first : width + first + LANES].T
+    first = heads[0] * HEAD
+    count = len(heads) * HEAD
+    base = first // LANES * LANES
+    tile = slice(base, base + LANES)
+    inside = slice(first - base, first - base + count)
+    keys_t = joined_ref[:, width + base : width + base + LANES].T
+    datt_t = dattend_ref[:, tile].T[inside]
+    inner = datt_t.astype(wide) * mixed_ref[first : first + count, :]
+    units = [(head, start, stop) for head in heads for start, stop in query_blocks(rows)]
+
+    def raw_products(head, start, stop):
+        mask = head_mask(head)
+        key_tile = joined_ref[:stop, width + base : width + base + LANES] * mask
+        value_tile = joined_ref[:stop, 2 * width + base : 2 * width + base + LANES] * mask
+        query = joined_ref[start:stop, tile]
+        datt = dattend_ref[start:stop, tile]
+        return dot_nt(key_tile, query), dot_nt(value_tile, datt), query * mask, datt * mask
+
+    ahead = raw_products(*units[0])
+    for index, (head, start, stop) in enumerate(units):
+        raw, dprobs, query, datt = ahead
+        if index + 1 < len(units):
+            ahead = raw_products(*units[index + 1])
+        local = head * HEAD - first
+        feature = slice(local, local + HEAD)
+        weighted = jnp.sum(inner[feature, start:stop], axis=0, keepdims=True)
+        logs = log_ref[head : head + 1, start:stop]
+        probs, dscores = [], []
+        for at in range(0, stop, CHUNK):
+            piece = raw[at : at + CHUNK] * (score_scale * log2_e)
+            piece = jnp.exp2(piece + bias_ref[at : at + CHUNK, start:stop] - logs)
+            probs.append(piece.astype(low))
+            piece = piece * (dprobs[at : at + CHUNK] - weighted)
+            dscores.append(piece.astype(low))
+        probs = jnp.concatenate(probs, axis=0)
+        dscores = jnp.concatenate(dscores, axis=0)
+        depth = slice(head * HEAD - base, head * HEAD - base + HEAD)
+        dquery_t[depth, start:stop] = (
+            dot_nn(keys_t[depth, :stop], dscores) * score_scale
+        ).astype(low)
+        dvalue[:stop, :] += dot_nn(probs, datt)
+        dkey[:stop, :] += dot_nn(dscores, query)
+
+
+def back_first_kernel(heads, *refs):
+    dquery_t, dkey, dvalue = refs[5:8]
     dkey[...] = jnp.zeros(dkey.shape, wide)
     dvalue[...] = jnp.zeros(dvalue.shape, wide)
-    per_tile = LANES // HEAD
-    inner = dattend_ref[:, tile].T.astype(wide) * mixed_ref[first : first + LANES, :]
-    for local in range(per_tile):
-        head = tile_index * per_tile + local
-        mask = head_mask(head)
-        key_tile = joined_ref[:, width + first : width + first + LANES] * mask
-        value_tile = joined_ref[:, 2 * width + first : 2 * width + first + LANES] * mask
-        feature = slice(local * HEAD, (local + 1) * HEAD)
-        weighted = jnp.sum(inner[feature, :], axis=0, keepdims=True)
-        for start, stop in query_blocks(rows):
-            query = joined_ref[start:stop, tile]
-            datt = dattend_ref[start:stop, tile]
-            raw = dot_nt(key_tile[:stop], query)
-            dprobs = dot_nt(value_tile[:stop], datt)
-            logs = log_ref[head : head + 1, start:stop]
-            probs, dscores = [], []
-            for at in range(0, stop, CHUNK):
-                piece = raw[at : at + CHUNK] * (score_scale * log2_e)
-                piece = jnp.exp2(piece + bias_ref[at : at + CHUNK, start:stop] - logs)
-                probs.append(piece.astype(low))
-                piece = piece * (dprobs[at : at + CHUNK] - weighted[:, start:stop])
-                dscores.append(piece.astype(low))
-            probs = jnp.concatenate(probs, axis=0)
-            dscores = jnp.concatenate(dscores, axis=0)
-            dquery_t[feature, start:stop] = (
-                dot_nn(keys_t[feature, :stop], dscores) * score_scale
-            ).astype(low)
-            dvalue[:stop, :] += dot_nn(probs, datt * mask)
-            dkey[:stop, :] += dot_nn(dscores, query * mask)
-    return dquery_t[...].T, (dkey[...] * score_scale).astype(low), dvalue[...].astype(low)
-
-
-def back_first_kernel(*refs):
-    results, scratch = refs[5:8], refs[8:]
-    values = back_tile(0, *refs[:5], *scratch)
-    for target, value in zip(results, values):
-        target[...] = value
-
-
-def back_last_kernel(shards, *refs):
+    dquery_t[...] = jnp.zeros(dquery_t.shape, low)
+    back_heads(heads, *refs)
+
+
+def back_last_kernel(shards, groups, *refs):
     shared = refs[:5]
     earlier = refs[5:8]
     norm_ref, root_ref, middle_ref, sums_in = refs[8:12]
@@ -370,11 +394,18 @@
     fill_cols(weight_ref, shard, pieces, 0, part, width)
     fill_small(small_ref, shard, pieces, 3 * part)
     gain, shift = small_ref[0, 0:1, :], small_ref[0, 1:2, :]
-    values = back_tile(1, *shared, dquery_t, dkey, dvalue)
-    for block in range(3):
-        at = block * width
-        djoined[:, at : at + LANES] = earlier[block][...]
-        djoined[:, at + LANES : at + 2 * LANES] = values[block]
+    for target, value in zip((dquery_t, dkey, dvalue), earlier):
+        target[...] = value[...]
+    for index, heads in enumerate(groups):
+        back_heads(heads, *shared, dquery_t, dkey, dvalue)
+        if (heads[-1] + 1) * HEAD % LANES == 0:
+            first = (heads[-1] + 1) * HEAD - LANES
+            values = (dquery_t[...].T, dkey[...] * score_scale, dvalue[...])
+            for block, value in enumerate(values):
+                at = block * width + first
+                djoined[:, at : at + LANES] = value.astype(low)
+            dkey[...] = jnp.zeros(dkey.shape, wide)
+            dvalue[...] = jnp.zeros(dvalue.shape, wide)
     normed, root = norm_ref[...], root_ref[...]
     hidden_t = (normed * gain + shift).astype(low).T
     dhidden = jnp.zeros((rows, width), wide)
@@ -462,10 +493,12 @@
 
 def adam_kernel(group, spans, layout, *refs):
     pieces = refs[:group]
-    grad_ref = refs[-1]
     count = len(layout)
     states = refs[group : group + 3 * count]
-    results = refs[group + 3 * count : -1]
+    results = refs[group + 3 * count : group + 6 * count]
+    buffers = refs[group + 6 * count : group + 9 * count]
+    grad_ref, sems = refs[-2:]
+    copies = []
     for offset, piece in enumerate(pieces):
         value = piece[...].astype(wide)
         index = (lax.axis_index("dp") & (group - 1)) ^ offset
@@ -475,7 +508,7 @@
     width = grad_ref.shape[1]
     for array, (first_row, stride, decay) in enumerate(layout):
         weight, first, second = states[3 * array : 3 * array + 3]
-        new = results[3 * array : 3 * array + 3]
+        new = buffers[3 * array : 3 * array + 3]
         vector = len(weight.shape) == 1
         rows = 1 if vector else weight.shape[0]
         for block in range(weight.shape[-1] // width):
@@ -491,24 +524,33 @@
             )
             for target, value in zip(new, values):
                 target[where] = value.reshape(width) if vector else value
-
-
-def local_call(kernel, outs, operands, scratch=(), flops=0, name=None, fetch=False):
-    space = pltpu.HBM if fetch else pltpu.VMEM
+        for index in range(3 * array, 3 * array + 3):
+            copies.append(
+                pltpu.make_async_copy(buffers[index], results[index], sems.at[index])
+            )
+            copies[-1].start()
+    for copy in copies:
+        copy.wait()
+
+
+def local_call(kernel, outs, operands, scratch=(), flops=0, name=None, fetch=False, sems=0):
+    in_space = pltpu.HBM if fetch else pltpu.VMEM
+    out_space = pltpu.HBM if sems else pltpu.VMEM
     outs = [jax.ShapeDtypeStruct(*out) for out in outs]
     moved = sum(
         math.prod(item.shape) * item.dtype.itemsize for item in list(operands) + outs
     )
     scratch_shapes = [pltpu.VMEM(*item) for item in scratch]
-    if fetch:
-        scratch_shapes.append(pltpu.SemaphoreType.DMA((len(operands),)))
+    if fetch or sems:
+        scratch_shapes.append(pltpu.SemaphoreType.DMA((sems or len(operands),)))
+    limit = 56 if fetch else 40
     return pl.pallas_call(
         kernel,
         out_shape=outs,
-        in_specs=[pl.BlockSpec(memory_space=space)] * len(operands),
-        out_specs=[pl.BlockSpec(memory_space=pltpu.VMEM)] * len(outs),
+        in_specs=[pl.BlockSpec(memory_space=in_space)] * len(operands),
+        out_specs=[pl.BlockSpec(memory_space=out_space)] * len(outs),
         scratch_shapes=scratch_shapes,
-        compiler_params=pltpu.CompilerParams(vmem_limit_bytes=(56 if fetch else 40) * 1024 * 1024),
+        compiler_params=pltpu.CompilerParams(vmem_limit_bytes=limit * 1024 * 1024),
         cost_estimate=pl.CostEstimate(flops=flops, bytes_accessed=moved, transcendentals=0),
         name=name,
     )(*operands)
@@ -580,12 +622,14 @@
             spans.append((rows, first + start, row))
             row += rows
         first += total
+    outs = [(state[0].shape, wide) for state in states for _ in range(3)]
     return local_call(
         functools.partial(adam_kernel, group, spans, layout),
-        [(state[0].shape, wide) for state in states for _ in range(3)],
+        outs,
         pieces + [item for state in states for item in state],
-        [((first, width), wide)],
+        outs + [((first, width), wide)],
         name="adam",
+        sems=len(outs),
     )
 
 
@@ -631,14 +675,9 @@
     firsts = {0: first_pack}
     firsts[2] = exchange(first_pack, "shard", 2)
     firsts[1] = exchange(first_pack, "shard", 1)
-    square = (rows, rows)
-    bias, normed, root, seed = local_call(
-        functools.partial(prepare_kernel, shards),
-        [(square, wide), ((rows, width), wide), ((rows, 1), wide), ((rows, width), low)],
-        [tokens, cotangent, lengths, seq_owner],
-        name="prepare",
-    )
-    matrices = [out_weight, up_weight, down_weight]
+    first_pack, matrices = lax.optimization_barrier(
+        (first_pack, [out_weight, up_weight, down_weight])
+    )
     (second_pack,) = local_call(
         pack_second_kernel,
         [((second_rows, width), low)],
@@ -647,14 +686,22 @@
         name="pack_second",
         fetch=True,
     )
-    firsts[2], second_pack, bias, normed, root, seed = lax.optimization_barrier(
-        (firsts[2], second_pack, bias, normed, root, seed)
-    )
-    firsts[3] = exchange(firsts[2], "shard", 1)
-    firsts = [firsts[offset] for offset in range(shards)]
+    early_tokens, second_pack = lax.optimization_barrier((tokens, second_pack))
+    square = (rows, rows)
+    bias, normed, root, seed = local_call(
+        functools.partial(prepare_kernel, shards),
+        [(square, wide), ((rows, width), wide), ((rows, 1), wide), ((rows, width), low)],
+        [early_tokens, cotangent, lengths, seq_owner],
+        name="prepare",
+    )
     seconds = {0: second_pack}
     seconds[2] = exchange(second_pack, "shard", 2)
     seconds[1] = exchange(second_pack, "shard", 1)
+    firsts[2], bias, normed, root, seed = lax.optimization_barrier(
+        (firsts[2], bias, normed, root, seed)
+    )
+    firsts[3] = exchange(firsts[2], "shard", 1)
+    firsts = [firsts[offset] for offset in range(shards)]
     joined, attended, log_sums, mixed = local_call(
         functools.partial(attend_kernel, shards),
         [
@@ -665,7 +712,7 @@
         ],
         [normed, bias] + firsts,
         [((width, 3 * width), low), ((shards, SMALL_PAD, width), wide)],
-        flops=heads * rows * rows * 256 * 4,
+        flops=heads * rows * rows * 640,
         name="attend",
     )
     attended, seconds[2] = lax.optimization_barrier((attended, seconds[2]))
@@ -696,12 +743,14 @@
     arrived_ffn = exchange(send_ffn, "shard", 1)
     shared = [joined, attended_grad, log_sums, bias, mixed]
     tile_scratch = [((LANES, rows), low), ((rows, LANES), wide), ((rows, LANES), wide)]
+    per_tile = LANES // HEAD
+    groups = [list(range(at, at + per_tile)) for at in range(0, heads, per_tile)]
+    groups = [groups[0][:2], groups[0][2:]] + groups[1:]
     first_query, first_key, first_value = local_call(
-        back_first_kernel,
-        [((rows, LANES), low)] * 3,
+        functools.partial(back_first_kernel, groups[0]),
+        tile_scratch,
         shared,
-        tile_scratch,
-        flops=heads * rows * rows * 256 * 5,
+        flops=heads * rows * rows * 256 * 5 // 2,
         name="back_first",
     )
     first_query, arrived_ffn = lax.optimization_barrier((first_query, arrived_ffn))
@@ -712,7 +761,7 @@
     att_rows = 3 * part + tail
     pair = (shards // 2, att_rows, width)
     input_grad, kept_att, send_att = local_call(
-        functools.partial(back_last_kernel, shards),
+        functools.partial(back_last_kernel, shards, groups[1:]),
         [((rows, width), wide), (pair, wide), (pair, low)],
         shared + [first_query, first_key, first_value, normed, root, middle_grad, sums] + firsts,
         [((width, 3 * width), low), ((shards, SMALL_PAD, width), wide)]

time: 73.8 us -> 69.9 us (0.947)
  starting transfers between devices: 26.9 us -> 21.1 us
  waiting for transfers between devices: 23.1 us -> 28.2 us
  Pallas kernels: 22.4 us -> 19.1 us
    ppermute x21, starting transfers between devices: 26.9 us -> 21.1 us  [exchange(): lax.ppermute(values, axis, [(index, index ^ mask) for index in range(coun...]
    ppermute x21, waiting for transfers between devices: 23.1 us -> 28.2 us  [exchange(): lax.ppermute(values, axis, [(index, index ^ mask) for index in range(coun...]
    pallas_call x15, Pallas kernels: 22.4 us -> 19.1 us  [local_call(): pl.pallas_call(kernel, out_shape=outs, in_specs=[pl.BlockSpec(memory_spac...]
  transfers between devices with their start and end apart: 21 -> 21, of which waited for: 14 -> 15; matrix products, arithmetic and copies ran while one was open for 0% -> 0% of each run, Pallas kernels for 20% -> 17%
where the time goes in v7:
time: 69.9 us; the launch traced here: 69.7 us
  waiting for transfers between devices  28.2 us (40%)
  starting transfers between devices  21.1 us (30%)
  Pallas kernels  19.1 us (27%)
  between operations  1.17 us (2%)
    ppermute x21, waiting for transfers between devices, exchange(): lax.ppermute(values, axis, [(index, index ^ mask) for index in range(coun...  28.2 us
    ppermute x21, starting transfers between devices, exchange(): lax.ppermute(values, axis, [(index, index ^ mask) for index in range(coun...  21.1 us
    pallas_call x15, Pallas kernels, local_call(): pl.pallas_call(kernel, out_shape=outs, in_specs=[pl.BlockSpec(memory_spac...  19.1 us
  transfers between devices with their start and end apart: 21, of which 15 were waited for; matrix products, arithmetic and copies ran while one was open for 0% of the time, Pallas kernels for 17%

profile of v7, /device:TPU:0, one launch (start us, length us, event | category | flops | bytes accessed | tf_op | source)
XLA Modules:
  0.0 69.7 jit_solution(12670436872377061229)
XLA Ops:
  0.7 1.7 %pack_first.1.refs_2_.refs_3_.refs_12_ = bf16[208,256]{1,0:T(8,128)(2,1)} custom-call(f32[64,768]{1,0:T(8,128)} %refs_8_.1, f32[768]{0:T(1024)} %refs_20_.1), custom_call_target="tpu_custom_call" | custom-call | bytes 306176 | tf_op jit(solution)/shard_map/pack_first/pallas_call | solution.py:547
  2.4 0.0 copy-start.13
  2.4 3.0 %collective-permute-start = (bf16[208,256]{1,0:T(8,128)(2,1)}, bf16[208,256]{1,0:T(8,128)(2,1)S(1)}, u32[]{:S(2)}, u32[]{:S(2)}) collective-permute-start(bf16[208,256]{1,0:T(8,128)(2,1)} %pack_first.1.refs_2_.refs_3_.refs_12_), channel_id=1, source_target_pairs={{0,2},{1,3},{2,0},{3,1},{4,6},{5,7},{6,4},{7,5},{8,10},{9,11},{10,... | collective-permute-start | bytes 319496 | tf_op jit(solution)/shard_map/ppermute | solution.py:561
  5.4 1.8 %pack_second.1.refs_7_ = bf16[576,256]{1,0:T(8,128)(2,1)} custom-call(f32[64,256]{1,0:T(8,128)} %refs_11_.1, f32[64,1024]{1,0:T(8,128)} %refs_14_.1, f32[256,256]{1,0:T(8,128)} %refs_17_.1), custom_call_target="tpu_custom_call" | custom-call | bytes 884736 | tf_op jit(solution)/shard_map/pack_second/pallas_call | solution.py:547
  7.2 0.1 collective-permute-start.3
  7.3 0.1 collective-permute-start.1
  7.4 0.6 prepare.1
  8.1 0.5 collective-permute-done.refs_4_.refs_5_.refs_14_
  8.6 0.1 collective-permute-start.2
  8.7 0.5 collective-permute-start.4
  9.1 0.8 %collective-permute-done.2.refs_5_.refs_6_.refs_15_ = bf16[208,256]{1,0:T(8,128)(2,1)S(1)} collective-permute-done((bf16[208,256]{1,0:T(8,128)(2,1)S(1)}, bf16[208,256]{1,0:T(8,128)(2,1)S(1)}, u32[]{:S(2)}, u32[]{:S(2)}) %collective-permute-start.2) | collective-permute-done | bytes 106528 | tf_op jit(solution)/shard_map/ppermute | solution.py:561
  9.9 2.9 %attend.1 = (bf16[512,768]{1,0:T(8,128)(2,1)S(1)}, bf16[512,256]{1,0:T(8,128)(2,1)S(1)}, f32[8,512]{1,0:T(8,128)S(1)}, f32[256,512]{1,0:T(8,128)S(1)}) custom-call(f32[512,256]{1,0:T(8,128)S(1)} %get-tuple-element.90.refs_0_.refs_8_, f32[512,512]{1,0:T(8,128)S(1)} %get-tuple-element.91.refs_1_.refs_3_, bf16[208,256]{1,0:T(8,128)(2,1)S(1)} %copy-done.13, ...), custom_call_target="tpu_custom_call" | custom-call | flops 1342177280 | bytes 3588096 | tf_op jit(solution)/shard_map/attend/pallas_call | solution.py:547
  12.9 3.1 %collective-permute-done.3.refs_9_ = bf16[576,256]{1,0:T(8,128)(2,1)S(1)} collective-permute-done((bf16[576,256]{1,0:T(8,128)(2,1)}, bf16[576,256]{1,0:T(8,128)(2,1)S(1)}, u32[]{:S(2)}, u32[]{:S(2)}) %collective-permute-start.3) | collective-permute-done | bytes 294944 | tf_op jit(solution)/shard_map/ppermute | solution.py:561
  16.0 1.6 %collective-permute-done.5.refs_10_ = bf16[576,256]{1,0:T(8,128)(2,1)S(1)} collective-permute-done((bf16[576,256]{1,0:T(8,128)(2,1)S(1)}, bf16[576,256]{1,0:T(8,128)(2,1)S(1)}, u32[]{:S(2)}, u32[]{:S(2)}) %collective-permute-start.5) | collective-permute-done | bytes 294944 | tf_op jit(solution)/shard_map/ppermute | solution.py:561
  17.6 3.8 %feed.1 = (bf16[512,256]{1,0:T(8,128)(2,1)}, f32[512,256]{1,0:T(8,128)S(1)}, bf16[512,256]{1,0:T(8,128)(2,1)S(1)}, f32[16,256]{1,0:T(8,128)S(1)}, f32[2,576,256]...) custom-call(bf16[512,256]{1,0:T(8,128)(2,1)S(1)} %copy-done.6, bf16[512,256]{1,0:T(8,128)(2,1)S(1)} %get-tuple-element.95.refs_1_, ...), custom_call_target="tpu_custom_call" | custom-call | flops 1811939328 | bytes 5226496 | tf_op jit(solution)/shard_map/feed/pallas_call | solution.py:547
  21.3 0.1 collective-permute-start.6
  21.5 1.2 %back_first.1 = (bf16[128,512]{1,0:T(8,128)(2,1)S(1)}, f32[512,128]{1,0:T(8,128)S(1)}, f32[512,128]{1,0:T(8,128)S(1)}) custom-call(bf16[512,768]{1,0:T(8,128)(2,1)S(1)} %get-tuple-element.99.refs_0_, bf16[512,256]{1,0:T(8,128)(2,1)S(1)} %get-tuple-element.100.refs_1_, f32[8,512]{1,0:T(8,128)S(1)} %get-tuple-element.101.refs_2_, ...), custom_call_target="tpu_custom_call" | custom-call | flops 1342177280 | bytes 3293184 | tf_op jit(solution)/shard_map/back_first/pallas_call | solution.py:547
  22.7 0.7 collective-permute-done.6.refs_1_
  23.3 0.1 halve_ffn.1
  23.4 0.7 %collective-permute-start.8 = (bf16[1,576,256]{2,1,0:T(8,128)(2,1)S(1)}, bf16[1,576,256]{2,1,0:T(8,128)(2,1)S(1)}, u32[]{:S(2)}, u32[]{:S(2)}) collective-permute-start(bf16[1,576,256]{2,1,0:T(8,128)(2,1)S(1)} %get-tuple-element.120), channel_id=1, source_target_pairs={{0,2},{1,3},{2,0},{3,1},{4,6},{5,7},{6,4},{7,5},{8,10},{9,11},{10,... | collective-permute-start | bytes 884744 | tf_op jit(solution)/shard_map/ppermute | solution.py:561
  24.2 4.9 %back_last.1 = (f32[512,256]{1,0:T(8,128)}, f32[2,256,256]{2,1,0:T(8,128)S(1)}, bf16[2,256,256]{2,1,0:T(8,128)(2,1)S(1)}) custom-call(bf16[512,768]{1,0:T(8,128)(2,1)S(1)} %get-tuple-element.99.refs_0_, bf16[512,256]{1,0:T(8,128)(2,1)S(1)} %get-tuple-element.100.refs_1_, f32[8,512]{1,0:T(8,128)S(1)} %get-tuple-element.101.refs_2_, ...), custom_call_target="tpu_custom_call" | custom-call | flops 3221225472 | bytes 6096896 | tf_op jit(solution)/shard_map/back_last/pallas_call | solution.py:547
  29.0 1.5 %collective-permute-done.7.refs_1_ = bf16[2,256,256]{2,1,0:T(8,128)(2,1)S(1)} collective-permute-done((bf16[2,256,256]{2,1,0:T(8,128)(2,1)S(1)}, bf16[2,256,256]{2,1,0:T(8,128)(2,1)S(1)}, u32[]{:S(2)}, u32[]{:S(2)}) %collective-permute-start.7) | collective-permute-done | bytes 262176 | tf_op jit(solution)/shard_map/ppermute | solution.py:561
  30.6 1.9 %collective-permute-done.8 = bf16[1,576,256]{2,1,0:T(8,128)(2,1)S(1)} collective-permute-done((bf16[1,576,256]{2,1,0:T(8,128)(2,1)S(1)}, bf16[1,576,256]{2,1,0:T(8,128)(2,1)S(1)}, u32[]{:S(2)}, u32[]{:S(2)}) %collective-permute-start.8) | collective-permute-done | bytes 294944 | tf_op jit(solution)/shard_map/ppermute | solution.py:561
  32.6 0.7 collective-permute-start.10
  33.3 0.0 copy-start.9
  33.3 0.0 copy-start.10
  33.3 0.0 copy-start.14
  33.4 0.1 split_sum.2
  33.5 1.6 %collective-permute-start.9 = (bf16[4,72,256]{2,1,0:T(8,128)(2,1)S(1)}, bf16[4,72,256]{2,1,0:T(8,128)(2,1)S(1)}, u32[]{:S(2)}, u32[]{:S(2)}) collective-permute-start(bf16[4,72,256]{2,1,0:T(8,128)(2,1)S(1)} %get-tuple-element.123), channel_id=1, source_target_pairs={{0,4},{4,0},{8,12},{12,8},{16,20},{20,16},{24,28},{28,24},{1,5},{5... | collective-permute-start | bytes 442376 | tf_op jit(solution)/shard_map/ppermute | solution.py:561
  35.1 2.5 %collective-permute-done.10 = bf16[1,256,256]{2,1,0:T(8,128)(2,1)S(1)} collective-permute-done((bf16[1,256,256]{2,1,0:T(8,128)(2,1)S(1)}, bf16[1,256,256]{2,1,0:T(8,128)(2,1)S(1)}, u32[]{:S(2)}, u32[]{:S(2)}) %collective-permute-start.10) | collective-permute-done | bytes 131104 | tf_op jit(solution)/shard_map/ppermute | solution.py:561
  37.5 0.1 split_sum.3
  37.6 1.6 %collective-permute-start.11 = (bf16[4,32,256]{2,1,0:T(8,128)(2,1)S(1)}, bf16[4,32,256]{2,1,0:T(8,128)(2,1)S(1)}, u32[]{:S(2)}, u32[]{:S(2)}) collective-permute-start(bf16[4,32,256]{2,1,0:T(8,128)(2,1)S(1)} %get-tuple-element.127), channel_id=1, source_target_pairs={{0,4},{4,0},{8,12},{12,8},{16,20},{20,16},{24,28},{28,24},{1,5},{5... | collective-permute-start | bytes 196616 | tf_op jit(solution)/shard_map/ppermute | solution.py:561
  39.2 2.8 %collective-permute-done.11.refs_3_ = bf16[4,32,256]{2,1,0:T(8,128)(2,1)S(1)} collective-permute-done((bf16[4,32,256]{2,1,0:T(8,128)(2,1)S(1)}, bf16[4,32,256]{2,1,0:T(8,128)(2,1)S(1)}, u32[]{:S(2)}, u32[]{:S(2)}) %collective-permute-start.11) | collective-permute-done | bytes 65568 | tf_op jit(solution)/shard_map/ppermute | solution.py:561
  42.0 1.6 %collective-permute-start.12 = (bf16[2,104,256]{2,1,0:T(8,128)(2,1)S(1)}, bf16[2,104,256]{2,1,0:T(8,128)(2,1)S(1)}, u32[]{:S(2)}, u32[]{:S(2)}) collective-permute-start(bf16[2,104,256]{2,1,0:T(8,128)(2,1)S(1)} %get-tuple-element.129), channel_id=1, source_target_pairs={{0,8},{4,12},{8,0},{12,4},{16,24},{20,28},{24,16},{28,20},{1,9},{5... | collective-permute-start | bytes 319496 | tf_op jit(solution)/shard_map/ppermute | solution.py:561
  43.6 3.7 %collective-permute-done.12.refs_1_ = bf16[2,104,256]{2,1,0:T(8,128)(2,1)S(1)} collective-permute-done((bf16[2,104,256]{2,1,0:T(8,128)(2,1)S(1)}, bf16[2,104,256]{2,1,0:T(8,128)(2,1)S(1)}, u32[]{:S(2)}, u32[]{:S(2)}) %collective-permute-start.12) | collective-permute-done | bytes 106528 | tf_op jit(solution)/shard_map/ppermute | solution.py:561
  47.3 2.6 %collective-permute-start.13 = (bf16[1,104,256]{2,1,0:T(8,128)(2,1)S(1)}, bf16[1,104,256]{2,1,0:T(8,128)(2,1)S(1)}, u32[]{:S(2)}, u32[]{:S(2)}) collective-permute-start(bf16[1,104,256]{2,1,0:T(8,128)(2,1)S(1)} %get-tuple-element.131), channel_id=1, source_target_pairs={{0,16},{4,20},{8,24},{12,28},{16,0},{20,4},{24,8},{28,12},{1,17},{... | collective-permute-start | bytes 159752 | tf_op jit(solution)/shard_map/ppermute | solution.py:561
  49.9 3.7 %collective-permute-done.13.other_ref = bf16[1,104,256]{2,1,0:T(8,128)(2,1)S(1)} collective-permute-done((bf16[1,104,256]{2,1,0:T(8,128)(2,1)S(1)}, bf16[1,104,256]{2,1,0:T(8,128)(2,1)S(1)}, u32[]{:S(2)}, u32[]{:S(2)}) %collective-permute-start.13) | collective-permute-done | bytes 53280 | tf_op jit(solution)/shard_map/ppermute | solution.py:561
  53.6 1.5 %collective-permute-start.17 = (bf16[104,256]{1,0:T(8,128)(2,1)S(1)}, bf16[104,256]{1,0:T(8,128)(2,1)S(1)}, u32[]{:S(2)}, u32[]{:S(2)}) collective-permute-start(bf16[104,256]{1,0:T(8,128)(2,1)S(1)} %piece_sum.1.refs_0_), channel_id=1, source_target_pairs={{0,16},{4,20},{8,24},{12,28},{16,0},{20,4},{24,8},{28,12},{1,17},{... | collective-permute-start | bytes 159752 | tf_op jit(solution)/shard_map/ppermute | solution.py:561
  55.1 2.0 %collective-permute-start.15 = (bf16[104,256]{1,0:T(8,128)(2,1)S(1)}, bf16[104,256]{1,0:T(8,128)(2,1)S(1)}, u32[]{:S(2)}, u32[]{:S(2)}) collective-permute-start(bf16[104,256]{1,0:T(8,128)(2,1)S(1)} %piece_sum.1.refs_0_), channel_id=1, source_target_pairs={{0,8},{4,12},{8,0},{12,4},{16,24},{20,28},{24,16},{28,20},{1,9},{5... | collective-permute-start | bytes 159752 | tf_op jit(solution)/shard_map/ppermute | solution.py:561
  57.1 2.2 %collective-permute-done.17.refs_4_ = bf16[104,256]{1,0:T(8,128)(2,1)S(1)} collective-permute-done((bf16[104,256]{1,0:T(8,128)(2,1)S(1)}, bf16[104,256]{1,0:T(8,128)(2,1)S(1)}, u32[]{:S(2)}, u32[]{:S(2)}) %collective-permute-start.17) | collective-permute-done | bytes 53280 | tf_op jit(solution)/shard_map/ppermute | solution.py:561
  59.3 1.5 %collective-permute-start.14 = (bf16[104,256]{1,0:T(8,128)(2,1)S(1)}, bf16[104,256]{1,0:T(8,128)(2,1)S(1)}, u32[]{:S(2)}, u32[]{:S(2)}) collective-permute-start(bf16[104,256]{1,0:T(8,128)(2,1)S(1)} %piece_sum.1.refs_0_), channel_id=1, source_target_pairs={{0,4},{4,0},{8,12},{12,8},{16,20},{20,16},{24,28},{28,24},{1,5},{5... | collective-permute-start | bytes 159752 | tf_op jit(solution)/shard_map/ppermute | solution.py:561
  60.8 0.5 collective-permute-start.18
  61.4 1.5 %collective-permute-start.16 = (bf16[104,256]{1,0:T(8,128)(2,1)S(1)}, bf16[104,256]{1,0:T(8,128)(2,1)S(1)}, u32[]{:S(2)}, u32[]{:S(2)}) collective-permute-start(bf16[104,256]{1,0:T(8,128)(2,1)S(1)} %collective-permute-done.15.refs_2_), channel_id=1, source_target_pairs={{0,4},{4,0},{8,12},{12,8},{16,20},{20,16},{24,28},{28,24},{1,5},{5... | collective-permute-start | bytes 159752 | tf_op jit(solution)/shard_map/ppermute | solution.py:561
  62.9 0.6 collective-permute-done.19.refs_6_
  63.5 1.5 %collective-permute-start.20 = (bf16[104,256]{1,0:T(8,128)(2,1)S(1)}, bf16[104,256]{1,0:T(8,128)(2,1)S(1)}, u32[]{:S(2)}, u32[]{:S(2)}) collective-permute-start(bf16[104,256]{1,0:T(8,128)(2,1)S(1)} %collective-permute-done.19.refs_6_), channel_id=1, source_target_pairs={{0,4},{4,0},{8,12},{12,8},{16,20},{20,16},{24,28},{28,24},{1,5},{5... | collective-permute-start | bytes 159752 | tf_op jit(solution)/shard_map/ppermute | solution.py:561
  65.0 0.6 collective-permute-done.16.refs_3_
  65.5 2.1 %collective-permute-done.20.refs_7_ = bf16[104,256]{1,0:T(8,128)(2,1)S(1)} collective-permute-done((bf16[104,256]{1,0:T(8,128)(2,1)S(1)}, bf16[104,256]{1,0:T(8,128)(2,1)S(1)}, u32[]{:S(2)}, u32[]{:S(2)}) %collective-permute-start.20) | collective-permute-done | bytes 53280 | tf_op jit(solution)/shard_map/ppermute | solution.py:561
  67.7 1.8 %adam.1 = (f32[64,768]{1,0:T(8,128)}, f32[64,768]{1,0:T(8,128)}, f32[64,768]{1,0:T(8,128)}, f32[64,256]{1,0:T(8,128)}, f32[64,256]{1,0:T(8,128)}, /*index=5*/f32...) custom-call(bf16[104,256]{1,0:T(8,128)(2,1)S(1)} %piece_sum.1.refs_0, ...), custom_call_target="tpu_custom_call" | custom-call | bytes 5163008 | tf_op jit(solution)/shard_map/adam/pallas_call | solution.py:547
  (51 shorter events, 0.2 us)
Async XLA Ops:
  0.7 6.7 %copy-start.6 = (bf16[512,256]{1,0:T(8,128)(2,1)S(1)}, bf16[512,256]{1,0:T(8,128)(2,1)}, u32[]{:S(2)}) copy-start(bf16[512,256]{1,0:T(8,128)(2,1)} %refs_0_.1) | copy-start | bytes 786436
  0.7 6.7 %copy-start.20 = (s32[128]{0:T(128)S(1)}, s32[128]{0:T(128)}, u32[]{:S(2)}) copy-start(s32[128]{0:T(128)} %param.22) | copy-start | bytes 1540
  0.7 6.7 %copy-start.19 = (s32[128]{0:T(128)S(1)}, s32[128]{0:T(128)}, u32[]{:S(2)}) copy-start(s32[128]{0:T(128)} %param.21) | copy-start | bytes 1540
  0.7 6.7 %copy-start.5 = (bf16[512,256]{1,0:T(8,128)(2,1)S(1)}, bf16[512,256]{1,0:T(8,128)(2,1)}, u32[]{:S(2)}) copy-start(bf16[512,256]{1,0:T(8,128)(2,1)} %seed_ref.1) | copy-start | bytes 786436
  2.4 7.5 %copy-start.13 = (bf16[208,256]{1,0:T(8,128)(2,1)S(1)}, bf16[208,256]{1,0:T(8,128)(2,1)}, u32[]{:S(2)}) copy-start(bf16[208,256]{1,0:T(8,128)(2,1)} %pack_first.1.refs_2_.refs_3_.refs_12_) | copy-start | bytes 319492
  2.4 6.2 %collective-permute-start = (bf16[208,256]{1,0:T(8,128)(2,1)}, bf16[208,256]{1,0:T(8,128)(2,1)S(1)}, u32[]{:S(2)}, u32[]{:S(2)}) collective-permute-start(bf16[208,256]{1,0:T(8,128)(2,1)} %pack_first.1.refs_2_.refs_3_.refs_12_), channel_id=1, source_target_pairs={{0,2},{1,3},{2,0},{3,1},{4,6},{5,7},{6,4},{7,5},{8,10},{9,11},{10,... | collective-permute-start | bytes 319496 | tf_op jit(solution)/shard_map/ppermute | solution.py:561
  7.2 8.7 %collective-permute-start.3 = (bf16[576,256]{1,0:T(8,128)(2,1)}, bf16[576,256]{1,0:T(8,128)(2,1)S(1)}, u32[]{:S(2)}, u32[]{:S(2)}) collective-permute-start(bf16[576,256]{1,0:T(8,128)(2,1)} %pack_second.1.refs_7_), channel_id=1, source_target_pairs={{0,2},{1,3},{2,0},{3,1},{4,6},{5,7},{6,4},{7,5},{8,10},{9,11},{10,... | collective-permute-start | bytes 884744 | tf_op jit(solution)/shard_map/ppermute | solution.py:561
  7.3 1.8 %collective-permute-start.1 = (bf16[208,256]{1,0:T(8,128)(2,1)}, bf16[208,256]{1,0:T(8,128)(2,1)S(1)}, u32[]{:S(2)}, u32[]{:S(2)}) collective-permute-start(bf16[208,256]{1,0:T(8,128)(2,1)} %pack_first.1.refs_2_.refs_3_.refs_12_), channel_id=1, source_target_pairs={{0,1},{1,0},{2,3},{3,2},{4,5},{5,4},{6,7},{7,6},{8,9},{9,8},{10,11... | collective-permute-start | bytes 319496 | tf_op jit(solution)/shard_map/ppermute | solution.py:561
  8.6 9.0 %copy-start.3 = (bf16[576,256]{1,0:T(8,128)(2,1)S(1)}, bf16[576,256]{1,0:T(8,128)(2,1)}, u32[]{:S(2)}) copy-start(bf16[576,256]{1,0:T(8,128)(2,1)} %pack_second.1.refs_7_) | copy-start | bytes 884740
  8.6 1.3 %collective-permute-start.2 = (bf16[208,256]{1,0:T(8,128)(2,1)S(1)}, bf16[208,256]{1,0:T(8,128)(2,1)S(1)}, u32[]{:S(2)}, u32[]{:S(2)}) collective-permute-start(bf16[208,256]{1,0:T(8,128)(2,1)S(1)} %collective-permute-done.refs_4_.refs_5_.refs_14_), channel_id=1, source_target_pairs={{0,1},{1,0},{2,3},{3,2},{4,5},{5,4},{6,7},{7,6},{8,9},{9,8},{10,11... | collective-permute-start | bytes 319496 | tf_op jit(solution)/shard_map/ppermute | solution.py:561
  8.7 7.3 %collective-permute-start.4 = (bf16[576,256]{1,0:T(8,128)(2,1)}, bf16[576,256]{1,0:T(8,128)(2,1)S(1)}, u32[]{:S(2)}, u32[]{:S(2)}) collective-permute-start(bf16[576,256]{1,0:T(8,128)(2,1)} %pack_second.1.refs_7_), channel_id=1, source_target_pairs={{0,1},{1,0},{2,3},{3,2},{4,5},{5,4},{6,7},{7,6},{8,9},{9,8},{10,11... | collective-permute-start | bytes 884744 | tf_op jit(solution)/shard_map/ppermute | solution.py:561
  16.0 1.6 %collective-permute-start.5 = (bf16[576,256]{1,0:T(8,128)(2,1)S(1)}, bf16[576,256]{1,0:T(8,128)(2,1)S(1)}, u32[]{:S(2)}, u32[]{:S(2)}) collective-permute-start(bf16[576,256]{1,0:T(8,128)(2,1)S(1)} %collective-permute-done.3.refs_9_), channel_id=1, source_target_pairs={{0,1},{1,0},{2,3},{3,2},{4,5},{5,4},{6,7},{7,6},{8,9},{9,8},{10,11... | collective-permute-start | bytes 884744 | tf_op jit(solution)/shard_map/ppermute | solution.py:561
  21.3 2.0 %collective-permute-start.6 = (bf16[2,576,256]{2,1,0:T(8,128)(2,1)S(1)}, bf16[2,576,256]{2,1,0:T(8,128)(2,1)S(1)}, u32[]{:S(2)}, u32[]{:S(2)}) collective-permute-start(bf16[2,576,256]{2,1,0:T(8,128)(2,1)S(1)} %get-tuple-element.104), channel_id=1, source_target_pairs={{0,1},{1,0},{2,3},{3,2},{4,5},{5,4},{6,7},{7,6},{8,9},{9,8},{10,11... | collective-permute-start | bytes 1769480 | tf_op jit(solution)/shard_map/ppermute | solution.py:561
  23.4 9.1 %collective-permute-start.8 = (bf16[1,576,256]{2,1,0:T(8,128)(2,1)S(1)}, bf16[1,576,256]{2,1,0:T(8,128)(2,1)S(1)}, u32[]{:S(2)}, u32[]{:S(2)}) collective-permute-start(bf16[1,576,256]{2,1,0:T(8,128)(2,1)S(1)} %get-tuple-element.120), channel_id=1, source_target_pairs={{0,2},{1,3},{2,0},{3,1},{4,6},{5,7},{6,4},{7,5},{8,10},{9,11},{10,... | collective-permute-start | bytes 884744 | tf_op jit(solution)/shard_map/ppermute | solution.py:561
  29.0 1.5 %collective-permute-start.7 = (bf16[2,256,256]{2,1,0:T(8,128)(2,1)S(1)}, bf16[2,256,256]{2,1,0:T(8,128)(2,1)S(1)}, u32[]{:S(2)}, u32[]{:S(2)}) collective-permute-start(bf16[2,256,256]{2,1,0:T(8,128)(2,1)S(1)} %get-tuple-element.118), channel_id=1, source_target_pairs={{0,1},{1,0},{2,3},{3,2},{4,5},{5,4},{6,7},{7,6},{8,9},{9,8},{10,11... | collective-permute-start | bytes 786440 | tf_op jit(solution)/shard_map/ppermute | solution.py:561
  32.6 5.0 %collective-permute-start.10 = (bf16[1,256,256]{2,1,0:T(8,128)(2,1)S(1)}, bf16[1,256,256]{2,1,0:T(8,128)(2,1)S(1)}, u32[]{:S(2)}, u32[]{:S(2)}) collective-permute-start(bf16[1,256,256]{2,1,0:T(8,128)(2,1)S(1)} %get-tuple-element.125), channel_id=1, source_target_pairs={{0,2},{1,3},{2,0},{3,1},{4,6},{5,7},{6,4},{7,5},{8,10},{9,11},{10,... | collective-permute-start | bytes 393224 | tf_op jit(solution)/shard_map/ppermute | solution.py:561
  33.2 34.4 %copy-start = (f32[64,1024]{1,0:T(8,128)S(1)}, f32[64,1024]{1,0:T(8,128)}, u32[]{:S(2)}) copy-start(f32[64,1024]{1,0:T(8,128)} %refs_14_.1) | copy-start | bytes 786436
  33.2 34.4 %copy-start.1 = (f32[256,256]{1,0:T(8,128)S(1)}, f32[256,256]{1,0:T(8,128)}, u32[]{:S(2)}) copy-start(f32[256,256]{1,0:T(8,128)} %refs_17_.1) | copy-start | bytes 786436
  33.2 34.4 %copy-start.2 = (f32[64,768]{1,0:T(8,128)S(1)}, f32[64,768]{1,0:T(8,128)}, u32[]{:S(2)}) copy-start(f32[64,768]{1,0:T(8,128)} %refs_8_.1) | copy-start | bytes 589828
  33.2 34.4 %copy-start.4 = (f32[64,256]{1,0:T(8,128)S(1)}, f32[64,256]{1,0:T(8,128)}, u32[]{:S(2)}) copy-start(f32[64,256]{1,0:T(8,128)} %refs_11_.1) | copy-start | bytes 196612
  33.2 34.4 %copy-start.7 = (f32[64,1024]{1,0:T(8,128)S(1)}, f32[64,1024]{1,0:T(8,128)}, u32[]{:S(2)}) copy-start(f32[64,1024]{1,0:T(8,128)} %refs_15_.1) | copy-start | bytes 786436
  33.3 34.4 %copy-start.8 = (f32[64,1024]{1,0:T(8,128)S(1)}, f32[64,1024]{1,0:T(8,128)}, u32[]{:S(2)}) copy-start(f32[64,1024]{1,0:T(8,128)} %refs_16_.1) | copy-start | bytes 786436
  33.3 34.4 %copy-start.9 = (f32[256,256]{1,0:T(8,128)S(1)}, f32[256,256]{1,0:T(8,128)}, u32[]{:S(2)}) copy-start(f32[256,256]{1,0:T(8,128)} %refs_18_.1) | copy-start | bytes 786436
  33.3 34.4 %copy-start.10 = (f32[256,256]{1,0:T(8,128)S(1)}, f32[256,256]{1,0:T(8,128)}, u32[]{:S(2)}) copy-start(f32[256,256]{1,0:T(8,128)} %refs_19_.1) | copy-start | bytes 786436
  33.3 34.4 %copy-start.11 = (f32[64,768]{1,0:T(8,128)S(1)}, f32[64,768]{1,0:T(8,128)}, u32[]{:S(2)}) copy-start(f32[64,768]{1,0:T(8,128)} %refs_9_.1) | copy-start | bytes 589828
  33.3 34.4 %copy-start.12 = (f32[64,768]{1,0:T(8,128)S(1)}, f32[64,768]{1,0:T(8,128)}, u32[]{:S(2)}) copy-start(f32[64,768]{1,0:T(8,128)} %refs_10_.1) | copy-start | bytes 589828
  33.3 34.4 %copy-start.14 = (f32[64,256]{1,0:T(8,128)S(1)}, f32[64,256]{1,0:T(8,128)}, u32[]{:S(2)}) copy-start(f32[64,256]{1,0:T(8,128)} %refs_12_.1) | copy-start | bytes 196612
  33.3 34.4 %copy-start.15 = (f32[64,256]{1,0:T(8,128)S(1)}, f32[64,256]{1,0:T(8,128)}, u32[]{:S(2)}) copy-start(f32[64,256]{1,0:T(8,128)} %refs_13_.1) | copy-start | bytes 196612
  33.3 34.4 %copy-start.16 = (f32[768]{0:T(1024)S(1)}, f32[768]{0:T(1024)}, u32[]{:S(2)}) copy-start(f32[768]{0:T(1024)} %refs_20_.1) | copy-start | bytes 9220
  33.4 34.4 %copy-start.17 = (f32[768]{0:T(1024)S(1)}, f32[768]{0:T(1024)}, u32[]{:S(2)}) copy-start(f32[768]{0:T(1024)} %refs_21_.1) | copy-start | bytes 9220
  33.4 34.4 %copy-start.18 = (f32[768]{0:T(1024)S(1)}, f32[768]{0:T(1024)}, u32[]{:S(2)}) copy-start(f32[768]{0:T(1024)} %refs_22_.1) | copy-start | bytes 9220
  33.5 5.6 %collective-permute-start.9 = (bf16[4,72,256]{2,1,0:T(8,128)(2,1)S(1)}, bf16[4,72,256]{2,1,0:T(8,128)(2,1)S(1)}, u32[]{:S(2)}, u32[]{:S(2)}) collective-permute-start(bf16[4,72,256]{2,1,0:T(8,128)(2,1)S(1)} %get-tuple-element.123), channel_id=1, source_target_pairs={{0,4},{4,0},{8,12},{12,8},{16,20},{20,16},{24,28},{28,24},{1,5},{5... | collective-permute-start | bytes 442376 | tf_op jit(solution)/shard_map/ppermute | solution.py:561
  37.6 4.3 %collective-permute-start.11 = (bf16[4,32,256]{2,1,0:T(8,128)(2,1)S(1)}, bf16[4,32,256]{2,1,0:T(8,128)(2,1)S(1)}, u32[]{:S(2)}, u32[]{:S(2)}) collective-permute-start(bf16[4,32,256]{2,1,0:T(8,128)(2,1)S(1)} %get-tuple-element.127), channel_id=1, source_target_pairs={{0,4},{4,0},{8,12},{12,8},{16,20},{20,16},{24,28},{28,24},{1,5},{5... | collective-permute-start | bytes 196616 | tf_op jit(solution)/shard_map/ppermute | solution.py:561
  42.0 5.3 %collective-permute-start.12 = (bf16[2,104,256]{2,1,0:T(8,128)(2,1)S(1)}, bf16[2,104,256]{2,1,0:T(8,128)(2,1)S(1)}, u32[]{:S(2)}, u32[]{:S(2)}) collective-permute-start(bf16[2,104,256]{2,1,0:T(8,128)(2,1)S(1)} %get-tuple-element.129), channel_id=1, source_target_pairs={{0,8},{4,12},{8,0},{12,4},{16,24},{20,28},{24,16},{28,20},{1,9},{5... | collective-permute-start | bytes 319496 | tf_op jit(solution)/shard_map/ppermute | solution.py:561
  47.3 6.2 %collective-permute-start.13 = (bf16[1,104,256]{2,1,0:T(8,128)(2,1)S(1)}, bf16[1,104,256]{2,1,0:T(8,128)(2,1)S(1)}, u32[]{:S(2)}, u32[]{:S(2)}) collective-permute-start(bf16[1,104,256]{2,1,0:T(8,128)(2,1)S(1)} %get-tuple-element.131), channel_id=1, source_target_pairs={{0,16},{4,20},{8,24},{12,28},{16,0},{20,4},{24,8},{28,12},{1,17},{... | collective-permute-start | bytes 159752 | tf_op jit(solution)/shard_map/ppermute | solution.py:561
  53.6 5.7 %collective-permute-start.17 = (bf16[104,256]{1,0:T(8,128)(2,1)S(1)}, bf16[104,256]{1,0:T(8,128)(2,1)S(1)}, u32[]{:S(2)}, u32[]{:S(2)}) collective-permute-start(bf16[104,256]{1,0:T(8,128)(2,1)S(1)} %piece_sum.1.refs_0_), channel_id=1, source_target_pairs={{0,16},{4,20},{8,24},{12,28},{16,0},{20,4},{24,8},{28,12},{1,17},{... | collective-permute-start | bytes 159752 | tf_op jit(solution)/shard_map/ppermute | solution.py:561
  55.1 6.2 %collective-permute-start.15 = (bf16[104,256]{1,0:T(8,128)(2,1)S(1)}, bf16[104,256]{1,0:T(8,128)(2,1)S(1)}, u32[]{:S(2)}, u32[]{:S(2)}) collective-permute-start(bf16[104,256]{1,0:T(8,128)(2,1)S(1)} %piece_sum.1.refs_0_), channel_id=1, source_target_pairs={{0,8},{4,12},{8,0},{12,4},{16,24},{20,28},{24,16},{28,20},{1,9},{5... | collective-permute-start | bytes 159752 | tf_op jit(solution)/shard_map/ppermute | solution.py:561
  59.3 4.1 %collective-permute-start.19 = (bf16[104,256]{1,0:T(8,128)(2,1)S(1)}, bf16[104,256]{1,0:T(8,128)(2,1)S(1)}, u32[]{:S(2)}, u32[]{:S(2)}) collective-permute-start(bf16[104,256]{1,0:T(8,128)(2,1)S(1)} %collective-permute-done.17.refs_4_), channel_id=1, source_target_pairs={{0,8},{4,12},{8,0},{12,4},{16,24},{20,28},{24,16},{28,20},{1,9},{5... | collective-permute-start | bytes 159752 | tf_op jit(solution)/shard_map/ppermute | solution.py:561
  59.3 5.6 %collective-permute-start.14 = (bf16[104,256]{1,0:T(8,128)(2,1)S(1)}, bf16[104,256]{1,0:T(8,128)(2,1)S(1)}, u32[]{:S(2)}, u32[]{:S(2)}) collective-permute-start(bf16[104,256]{1,0:T(8,128)(2,1)S(1)} %piece_sum.1.refs_0_), channel_id=1, source_target_pairs={{0,4},{4,0},{8,12},{12,8},{16,20},{20,16},{24,28},{28,24},{1,5},{5... | collective-permute-start | bytes 159752 | tf_op jit(solution)/shard_map/ppermute | solution.py:561
  60.8 4.1 %collective-permute-start.18 = (bf16[104,256]{1,0:T(8,128)(2,1)S(1)}, bf16[104,256]{1,0:T(8,128)(2,1)S(1)}, u32[]{:S(2)}, u32[]{:S(2)}) collective-permute-start(bf16[104,256]{1,0:T(8,128)(2,1)S(1)} %collective-permute-done.17.refs_4_), channel_id=1, source_target_pairs={{0,4},{4,0},{8,12},{12,8},{16,20},{20,16},{24,28},{28,24},{1,5},{5... | collective-permute-start | bytes 159752 | tf_op jit(solution)/shard_map/ppermute | solution.py:561
  61.4 4.2 %collective-permute-start.16 = (bf16[104,256]{1,0:T(8,128)(2,1)S(1)}, bf16[104,256]{1,0:T(8,128)(2,1)S(1)}, u32[]{:S(2)}, u32[]{:S(2)}) collective-permute-start(bf16[104,256]{1,0:T(8,128)(2,1)S(1)} %collective-permute-done.15.refs_2_), channel_id=1, source_target_pairs={{0,4},{4,0},{8,12},{12,8},{16,20},{20,16},{24,28},{28,24},{1,5},{5... | collective-permute-start | bytes 159752 | tf_op jit(solution)/shard_map/ppermute | solution.py:561
  63.5 4.1 %collective-permute-start.20 = (bf16[104,256]{1,0:T(8,128)(2,1)S(1)}, bf16[104,256]{1,0:T(8,128)(2,1)S(1)}, u32[]{:S(2)}, u32[]{:S(2)}) collective-permute-start(bf16[104,256]{1,0:T(8,128)(2,1)S(1)} %collective-permute-done.19.refs_6_), channel_id=1, source_target_pairs={{0,4},{4,0},{8,12},{12,8},{16,20},{20,16},{24,28},{28,24},{1,5},{5... | collective-permute-start | bytes 159752 | tf_op jit(solution)/shard_map/ppermute | solution.py:561

commit v8 on v7

--- a/solution.py
+++ b/solution.py
@@ -234,7 +234,7 @@
     out_ref[...] = att_ref[...].astype(low).T
 
 
-def feed_kernel(shards, *refs):
+def feed_kernel(shards, group, *refs):
     x_ref, att_ref, seed_ref = refs[:3]
     firsts = refs[3 : 3 + shards]
     pieces = refs[3 + shards : 3 + 2 * shards]
@@ -314,7 +314,8 @@
     sums_ref[1:2, :] = shift_grad
     sums_ref[2:3, :] = jnp.sum(dmiddle_low.astype(wide), axis=0, keepdims=True)
     sums_ref[3:4, :] = jnp.sum(seed, axis=0, keepdims=True)
-    part_ways(grads_ref, keep_ref, send_ref, shard % 2)
+    side = (shard ^ parity(lax.axis_index("dp"), group)) & 1
+    part_ways(grads_ref, keep_ref, send_ref, side)
 
 
 def part_ways(grads_ref, keep_ref, send_ref, side):
@@ -380,7 +381,7 @@
     back_heads(heads, *refs)
 
 
-def back_last_kernel(shards, groups, *refs):
+def back_last_kernel(shards, group, head_groups, *refs):
     shared = refs[:5]
     earlier = refs[5:8]
     norm_ref, root_ref, middle_ref, sums_in = refs[8:12]
@@ -396,7 +397,7 @@
     gain, shift = small_ref[0, 0:1, :], small_ref[0, 1:2, :]
     for target, value in zip((dquery_t, dkey, dvalue), earlier):
         target[...] = value[...]
-    for index, heads in enumerate(groups):
+    for heads in head_groups:
         back_heads(heads, *shared, dquery_t, dkey, dvalue)
         if (heads[-1] + 1) * HEAD % LANES == 0:
             first = (heads[-1] + 1) * HEAD - LANES
@@ -426,14 +427,12 @@
     sums = [gain_grad, shift_grad, sums_in[0:1, :], sums_in[1:2, :]] + bias_sums
     sums += [sums_in[row : row + 1, :] for row in range(2, 8)]
     per_shard = len(sums) // shards
+    empty = [jnp.zeros((grads_ref.shape[1] - 3 * part - per_shard, width), wide)]
     for target in range(shards):
-        at = 3 * part
-        grads_ref[target, at:, :] = jnp.zeros((grads_ref.shape[1] - at, width), wide)
-        for row in range(per_shard):
-            grads_ref[target, at + row * TILE_ROWS : at + row * TILE_ROWS + 1, :] = sums[
-                target * per_shard + row
-            ]
-    part_ways(grads_ref, keep_ref, send_ref, shard % 2)
+        rows_here = sums[target * per_shard : (target + 1) * per_shard]
+        grads_ref[target, 3 * part :, :] = jnp.concatenate(rows_here + empty, axis=0)
+    side = (shard ^ parity(lax.axis_index("dp"), group)) & 1
+    part_ways(grads_ref, keep_ref, send_ref, side)
 
 
 def halve_kernel(axis, bit, *refs):
@@ -451,9 +450,9 @@
 
 
 def piece_spans(total, tail, group):
-    spans = [((total - tail) // group, 0)]
+    spans = [((total - tail) // group, 0, True)]
     if tail:
-        spans.append((tail // group, total - tail))
+        spans.append((tail, total - tail, False))
     return spans
 
 
@@ -465,8 +464,8 @@
         total = total + piece[...].astype(wide)
     for index in range(group):
         row = 0
-        for rows, first in piece_spans(total.shape[0], tail, group):
-            at = first + index * rows
+        for rows, first, moves in piece_spans(total.shape[0], tail, group):
+            at = first + index * rows if moves else first
             sum_ref[index, row : row + rows, :] = total[at : at + rows, :]
             row += rows
     side = lax.axis_index("dp") & 1
@@ -561,14 +560,38 @@
     return lax.ppermute(values, axis, [(index, index ^ mask) for index in range(count)])
 
 
-def gather_near(value, axis, count):
-    found = {0: value}
-    far = count // 2
-    while far:
-        for offset in sorted(found):
-            found[offset ^ far] = exchange(found[offset], axis, far)
+def parity(index, group):
+    result = index & 1
+    bit = 1
+    while (1 << bit) < group:
+        result = result ^ ((index >> bit) & 1)
+        bit += 1
+    return result
+
+
+def cross(values, mask, group, settle=False):
+    replicas, shards = lax.axis_size("dp"), lax.axis_size("shard")
+    pairs = []
+    for replica in range(replicas):
+        flip = parity(replica, group) if settle else 1
+        for shard in range(shards):
+            target = (replica ^ mask) * shards + (shard ^ flip)
+            pairs.append((replica * shards + shard, target))
+    return lax.ppermute(values, ("dp", "shard"), pairs)
+
+
+def gather_pieces(value, group):
+    held = {0: value}
+    far = group // 2
+    while far > 1:
+        for offset in sorted(held):
+            held[offset ^ far] = cross(held[offset], far, group)
         far //= 2
-    return [found[offset] for offset in range(count)]
+    found = {}
+    for offset in sorted(held):
+        found[offset ^ 1] = cross(held[offset], 1, group, settle=True)
+        found[offset] = cross(held[offset], 0, group, settle=True)
+    return [found[offset] for offset in range(group)]
 
 
 def halve_call(axis, bit, flat, name):
@@ -581,7 +604,7 @@
 
 def split_chunk(chunk, tail, group):
     rows, width = chunk[0].shape
-    half = (group // 2, rows // group, width)
+    half = (group // 2, (rows - tail) // group + tail, width)
     keep, send = local_call(
         functools.partial(split_kernel, tail),
         [(half, wide), (half, low)],
@@ -589,7 +612,7 @@
         [((group,) + half[1:], wide)],
         name="split_sum",
     )
-    return keep, exchange(send, "dp", 1)
+    return keep, cross(send, 1, group)
 
 
 def finish_sum(chunks, group):
@@ -601,7 +624,7 @@
     while half > 1:
         half //= 2
         keep, send = halve_call("dp", bit, flat, "halve_dp")
-        flat = [keep, exchange(send, "dp", 1 << bit)]
+        flat = [keep, cross(send, 1 << bit, group)]
         bit += 1
     mask = group
     (piece,) = local_call(add_kernel, [((rows, width), low)], flat, name="piece_sum")
@@ -609,7 +632,7 @@
         other = exchange(piece, "dp", mask)
         (piece,) = local_call(add_kernel, [((rows, width), low)], [piece, other], name="far_sum")
         mask *= 2
-    return gather_near(piece, "dp", group)
+    return gather_pieces(piece, group)
 
 
 def adam_call(pieces, counts, tails, states, layout):
@@ -618,9 +641,10 @@
     spans = []
     first = row = 0
     for total, tail in zip(counts, tails):
-        for rows, start in piece_spans(total, tail, group):
+        for rows, start, moves in piece_spans(total, tail, group):
             spans.append((rows, first + start, row))
             row += rows
+            first += rows * (group - 1) * (not moves)
         first += total
     outs = [(state[0].shape, wide) for state in states for _ in range(3)]
     return local_call(
@@ -720,7 +744,7 @@
     seconds = [seconds[offset] for offset in range(shards)]
     pair = (shards // 2, second_rows, width)
     output, middle_grad, attended_grad, sums, kept_ffn, send_ffn = local_call(
-        functools.partial(feed_kernel, shards),
+        functools.partial(feed_kernel, shards, group),
         [
             ((rows, width), low),
             ((rows, width), wide),
@@ -757,11 +781,11 @@
     keep_ffn, send_ffn = halve_call("shard", 1, [kept_ffn, arrived_ffn], "halve_ffn")
     first_query, send_ffn = lax.optimization_barrier((first_query, send_ffn))
     arrived_ffn = exchange(send_ffn, "shard", 2)
-    tail = GROUP * TILE_ROWS
+    tail = TILE_ROWS
     att_rows = 3 * part + tail
     pair = (shards // 2, att_rows, width)
     input_grad, kept_att, send_att = local_call(
-        functools.partial(back_last_kernel, shards, groups[1:]),
+        functools.partial(back_last_kernel, shards, group, groups[1:]),
         [((rows, width), wide), (pair, wide), (pair, low)],
         shared + [first_query, first_key, first_value, normed, root, middle_grad, sums] + firsts,
         [((width, 3 * width), low), ((shards, SMALL_PAD, width), wide)]
@@ -795,7 +819,7 @@
             (0, part, matrix_decay),
             (part, part, matrix_decay),
             (part + blocks * part, 0, matrix_decay),
-            (second_rows + 3 * part, TILE_ROWS, 0.0),
+            (second_rows + 3 * part, 1, 0.0),
         ],
     )
     return (output, input_grad, *results)

time: 69.9 us -> 70.8 us (1.013)
  waiting for transfers between devices: 28.2 us -> 25 us
  starting transfers between devices: 21.1 us -> 24.1 us
    ppermute x0 -> x15, starting transfers between devices: none -> 18.9 us  [cross(): return lax.ppermute(values, ('dp', 'shard'), pairs)]
    ppermute x21 -> x10, starting transfers between devices: 21.1 us -> 5.24 us  [exchange(): lax.ppermute(values, axis, [(index, index ^ mask) for index in range(coun...]
    ppermute x21 -> x10, waiting for transfers between devices: 28.2 us -> 13.4 us  [exchange(): lax.ppermute(values, axis, [(index, index ^ mask) for index in range(coun...]
    ppermute x0 -> x15, waiting for transfers between devices: none -> 11.6 us  [cross(): return lax.ppermute(values, ('dp', 'shard'), pairs)]
  transfers between devices with their start and end apart: 21 -> 25, of which waited for: 15 -> 13; matrix products, arithmetic and copies ran while one was open for 0% -> 0% of each run, Pallas kernels for 17% -> 17%
where the time goes in v8:
time: 70.8 us; the launch traced here: 70 us
  waiting for transfers between devices  25 us (35%)
  starting transfers between devices  24.1 us (34%)
  Pallas kernels  19.5 us (28%)
  between operations  1.26 us (2%)
    pallas_call x15, Pallas kernels, local_call(): pl.pallas_call(kernel, out_shape=outs, in_specs=[pl.BlockSpec(memory_spac...  19.5 us
    ppermute x15, starting transfers between devices, cross(): return lax.ppermute(values, ('dp', 'shard'), pairs)  18.9 us
    ppermute x10, waiting for transfers between devices, exchange(): lax.ppermute(values, axis, [(index, index ^ mask) for index in range(coun...  13.4 us
    ppermute x15, waiting for transfers between devices, cross(): return lax.ppermute(values, ('dp', 'shard'), pairs)  11.6 us
    ppermute x10, starting transfers between devices, exchange(): lax.ppermute(values, axis, [(index, index ^ mask) for index in range(coun...  5.24 us
  transfers between devices with their start and end apart: 25, of which 13 were waited for; matrix products, arithmetic and copies ran while one was open for 0% of the time, Pallas kernels for 17%

profile of v8, /device:TPU:0, one launch (start us, length us, event | category | flops | bytes accessed | tf_op | source)
XLA Modules:
  0.0 70.0 jit_solution(12850387419929739031)
XLA Ops:
  0.7 1.7 %pack_first.1.refs_2_.refs_3_.refs_12_ = bf16[208,256]{1,0:T(8,128)(2,1)} custom-call(f32[64,768]{1,0:T(8,128)} %refs_8_.1, f32[768]{0:T(1024)} %refs_20_.1), custom_call_target="tpu_custom_call" | custom-call | bytes 306176 | tf_op jit(solution)/shard_map/pack_first/pallas_call | solution.py:546
  2.4 0.0 copy-start.13
  2.4 3.0 %collective-permute-start = (bf16[208,256]{1,0:T(8,128)(2,1)}, bf16[208,256]{1,0:T(8,128)(2,1)S(1)}, u32[]{:S(2)}, u32[]{:S(2)}) collective-permute-start(bf16[208,256]{1,0:T(8,128)(2,1)} %pack_first.1.refs_2_.refs_3_.refs_12_), channel_id=1, source_target_pairs={{0,2},{1,3},{2,0},{3,1},{4,6},{5,7},{6,4},{7,5},{8,10},{9,11},{10,... | collective-permute-start | bytes 319496 | tf_op jit(solution)/shard_map/ppermute | solution.py:560
  5.4 1.8 %pack_second.1.refs_7_ = bf16[576,256]{1,0:T(8,128)(2,1)} custom-call(f32[64,256]{1,0:T(8,128)} %refs_11_.1, f32[64,1024]{1,0:T(8,128)} %refs_14_.1, f32[256,256]{1,0:T(8,128)} %refs_17_.1), custom_call_target="tpu_custom_call" | custom-call | bytes 884736 | tf_op jit(solution)/shard_map/pack_second/pallas_call | solution.py:546
  7.2 0.1 collective-permute-start.3
  7.3 0.1 collective-permute-start.1
  7.4 0.6 prepare.1
  8.1 0.5 collective-permute-done.refs_4_.refs_5_.refs_14_
  8.6 0.1 collective-permute-start.2
  8.7 0.5 collective-permute-start.4
  9.1 0.8 %collective-permute-done.2.refs_5_.refs_6_.refs_15_ = bf16[208,256]{1,0:T(8,128)(2,1)S(1)} collective-permute-done((bf16[208,256]{1,0:T(8,128)(2,1)S(1)}, bf16[208,256]{1,0:T(8,128)(2,1)S(1)}, u32[]{:S(2)}, u32[]{:S(2)}) %collective-permute-start.2) | collective-permute-done | bytes 106528 | tf_op jit(solution)/shard_map/ppermute | solution.py:560
  9.9 3.0 %attend.1 = (bf16[512,768]{1,0:T(8,128)(2,1)S(1)}, bf16[512,256]{1,0:T(8,128)(2,1)S(1)}, f32[8,512]{1,0:T(8,128)S(1)}, f32[256,512]{1,0:T(8,128)S(1)}) custom-call(f32[512,256]{1,0:T(8,128)S(1)} %get-tuple-element.90.refs_0_.refs_8_, f32[512,512]{1,0:T(8,128)S(1)} %get-tuple-element.91.refs_1_.refs_3_, bf16[208,256]{1,0:T(8,128)(2,1)S(1)} %copy-done.13, ...), custom_call_target="tpu_custom_call" | custom-call | flops 1342177280 | bytes 3588096 | tf_op jit(solution)/shard_map/attend/pallas_call | solution.py:546
  12.9 3.0 %collective-permute-done.3.refs_9_ = bf16[576,256]{1,0:T(8,128)(2,1)S(1)} collective-permute-done((bf16[576,256]{1,0:T(8,128)(2,1)}, bf16[576,256]{1,0:T(8,128)(2,1)S(1)}, u32[]{:S(2)}, u32[]{:S(2)}) %collective-permute-start.3) | collective-permute-done | bytes 294944 | tf_op jit(solution)/shard_map/ppermute | solution.py:560
  16.0 1.6 %collective-permute-done.5.refs_10_ = bf16[576,256]{1,0:T(8,128)(2,1)S(1)} collective-permute-done((bf16[576,256]{1,0:T(8,128)(2,1)S(1)}, bf16[576,256]{1,0:T(8,128)(2,1)S(1)}, u32[]{:S(2)}, u32[]{:S(2)}) %collective-permute-start.5) | collective-permute-done | bytes 294944 | tf_op jit(solution)/shard_map/ppermute | solution.py:560
  17.6 3.9 %feed.1 = (bf16[512,256]{1,0:T(8,128)(2,1)}, f32[512,256]{1,0:T(8,128)S(1)}, bf16[512,256]{1,0:T(8,128)(2,1)S(1)}, f32[16,256]{1,0:T(8,128)S(1)}, f32[2,576,256]...) custom-call(bf16[512,256]{1,0:T(8,128)(2,1)S(1)} %copy-done.6, bf16[512,256]{1,0:T(8,128)(2,1)S(1)} %get-tuple-element.95.refs_1_, ...), custom_call_target="tpu_custom_call" | custom-call | flops 1811939328 | bytes 5226496 | tf_op jit(solution)/shard_map/feed/pallas_call | solution.py:546
  21.4 0.1 collective-permute-start.6
  21.6 1.2 %back_first.1 = (bf16[128,512]{1,0:T(8,128)(2,1)S(1)}, f32[512,128]{1,0:T(8,128)S(1)}, f32[512,128]{1,0:T(8,128)S(1)}) custom-call(bf16[512,768]{1,0:T(8,128)(2,1)S(1)} %get-tuple-element.99.refs_0_, bf16[512,256]{1,0:T(8,128)(2,1)S(1)} %get-tuple-element.100.refs_1_, f32[8,512]{1,0:T(8,128)S(1)} %get-tuple-element.101.refs_2_, ...), custom_call_target="tpu_custom_call" | custom-call | flops 1342177280 | bytes 3293184 | tf_op jit(solution)/shard_map/back_first/pallas_call | solution.py:546
  22.8 0.7 collective-permute-done.6.refs_1_
  23.4 0.1 halve_ffn.1
  23.6 0.7 %collective-permute-start.8 = (bf16[1,576,256]{2,1,0:T(8,128)(2,1)S(1)}, bf16[1,576,256]{2,1,0:T(8,128)(2,1)S(1)}, u32[]{:S(2)}, u32[]{:S(2)}) collective-permute-start(bf16[1,576,256]{2,1,0:T(8,128)(2,1)S(1)} %get-tuple-element.120), channel_id=1, source_target_pairs={{0,2},{1,3},{2,0},{3,1},{4,6},{5,7},{6,4},{7,5},{8,10},{9,11},{10,... | collective-permute-start | bytes 884744 | tf_op jit(solution)/shard_map/ppermute | solution.py:560
  24.3 5.0 %back_last.1 = (f32[512,256]{1,0:T(8,128)}, f32[2,200,256]{2,1,0:T(8,128)S(1)}, bf16[2,200,256]{2,1,0:T(8,128)(2,1)S(1)}) custom-call(bf16[512,768]{1,0:T(8,128)(2,1)S(1)} %get-tuple-element.99.refs_0_, bf16[512,256]{1,0:T(8,128)(2,1)S(1)} %get-tuple-element.100.refs_1_, f32[8,512]{1,0:T(8,128)S(1)} %get-tuple-element.101.refs_2_, ...), custom_call_target="tpu_custom_call" | custom-call | flops 3221225472 | bytes 5924864 | tf_op jit(solution)/shard_map/back_last/pallas_call | solution.py:546
  29.3 1.5 %collective-permute-done.7.refs_1_ = bf16[2,200,256]{2,1,0:T(8,128)(2,1)S(1)} collective-permute-done((bf16[2,200,256]{2,1,0:T(8,128)(2,1)S(1)}, bf16[2,200,256]{2,1,0:T(8,128)(2,1)S(1)}, u32[]{:S(2)}, u32[]{:S(2)}) %collective-permute-start.7) | collective-permute-done | bytes 204832 | tf_op jit(solution)/shard_map/ppermute | solution.py:560
  30.8 1.8 %collective-permute-done.8 = bf16[1,576,256]{2,1,0:T(8,128)(2,1)S(1)} collective-permute-done((bf16[1,576,256]{2,1,0:T(8,128)(2,1)S(1)}, bf16[1,576,256]{2,1,0:T(8,128)(2,1)S(1)}, u32[]{:S(2)}, u32[]{:S(2)}) %collective-permute-start.8) | collective-permute-done | bytes 294944 | tf_op jit(solution)/shard_map/ppermute | solution.py:560
  32.7 0.7 collective-permute-start.10
  33.4 0.0 copy-start.9
  33.4 0.0 copy-start.10
  33.5 0.1 split_sum.2
  33.6 0.2 collective-permute-start.9
  33.8 3.5 %collective-permute-done.10 = bf16[1,200,256]{2,1,0:T(8,128)(2,1)S(1)} collective-permute-done((bf16[1,200,256]{2,1,0:T(8,128)(2,1)S(1)}, bf16[1,200,256]{2,1,0:T(8,128)(2,1)S(1)}, u32[]{:S(2)}, u32[]{:S(2)}) %collective-permute-start.10) | collective-permute-done | bytes 102432 | tf_op jit(solution)/shard_map/ppermute | solution.py:560
  37.4 0.1 collective-permute-start.11
  37.5 2.3 %collective-permute-done.9.refs_1_ = bf16[4,72,256]{2,1,0:T(8,128)(2,1)S(1)} collective-permute-done((bf16[4,72,256]{2,1,0:T(8,128)(2,1)S(1)}, bf16[4,72,256]{2,1,0:T(8,128)(2,1)S(1)}, u32[]{:S(2)}, u32[]{:S(2)}) %collective-permute-start.9) | collective-permute-done | bytes 147488 | tf_op jit(solution)/shard_map/ppermute | solution.py:580
  39.8 2.0 %collective-permute-done.11.refs_3_ = bf16[4,32,256]{2,1,0:T(8,128)(2,1)S(1)} collective-permute-done((bf16[4,32,256]{2,1,0:T(8,128)(2,1)S(1)}, bf16[4,32,256]{2,1,0:T(8,128)(2,1)S(1)}, u32[]{:S(2)}, u32[]{:S(2)}) %collective-permute-start.11) | collective-permute-done | bytes 65568 | tf_op jit(solution)/shard_map/ppermute | solution.py:580
  41.8 1.4 %collective-permute-start.12 = (bf16[2,104,256]{2,1,0:T(8,128)(2,1)S(1)}, bf16[2,104,256]{2,1,0:T(8,128)(2,1)S(1)}, u32[]{:S(2)}, u32[]{:S(2)}) collective-permute-start(bf16[2,104,256]{2,1,0:T(8,128)(2,1)S(1)} %get-tuple-element.129), channel_id=1, source_target_pairs={{0,9},{1,8},{2,11},{3,10},{4,13},{5,12},{6,15},{7,14},{8,1},{9,0},... | collective-permute-start | bytes 319496 | tf_op jit(solution)/shard_map/ppermute | solution.py:580
  43.2 3.7 %collective-permute-done.12.refs_1_ = bf16[2,104,256]{2,1,0:T(8,128)(2,1)S(1)} collective-permute-done((bf16[2,104,256]{2,1,0:T(8,128)(2,1)S(1)}, bf16[2,104,256]{2,1,0:T(8,128)(2,1)S(1)}, u32[]{:S(2)}, u32[]{:S(2)}) %collective-permute-start.12) | collective-permute-done | bytes 106528 | tf_op jit(solution)/shard_map/ppermute | solution.py:580
  46.9 2.4 %collective-permute-start.13 = (bf16[1,104,256]{2,1,0:T(8,128)(2,1)S(1)}, bf16[1,104,256]{2,1,0:T(8,128)(2,1)S(1)}, u32[]{:S(2)}, u32[]{:S(2)}) collective-permute-start(bf16[1,104,256]{2,1,0:T(8,128)(2,1)S(1)} %get-tuple-element.131), channel_id=1, source_target_pairs={{0,17},{1,16},{2,19},{3,18},{4,21},{5,20},{6,23},{7,22},{8,25},{9,... | collective-permute-start | bytes 159752 | tf_op jit(solution)/shard_map/ppermute | solution.py:580
  49.3 2.4 %collective-permute-done.13.other_ref = bf16[1,104,256]{2,1,0:T(8,128)(2,1)S(1)} collective-permute-done((bf16[1,104,256]{2,1,0:T(8,128)(2,1)S(1)}, bf16[1,104,256]{2,1,0:T(8,128)(2,1)S(1)}, u32[]{:S(2)}, u32[]{:S(2)}) %collective-permute-start.13) | collective-permute-done | bytes 53280 | tf_op jit(solution)/shard_map/ppermute | solution.py:580
  51.7 2.5 %collective-permute-start.19 = (bf16[104,256]{1,0:T(8,128)(2,1)S(1)}, bf16[104,256]{1,0:T(8,128)(2,1)S(1)}, u32[]{:S(2)}, u32[]{:S(2)}) collective-permute-start(bf16[104,256]{1,0:T(8,128)(2,1)S(1)} %piece_sum.1), channel_id=1, source_target_pairs={{0,17},{1,16},{2,19},{3,18},{4,21},{5,20},{6,23},{7,22},{8,25},{9,... | collective-permute-start | bytes 159752 | tf_op jit(solution)/shard_map/ppermute | solution.py:580
  54.2 2.8 %collective-permute-start.16 = (bf16[104,256]{1,0:T(8,128)(2,1)S(1)}, bf16[104,256]{1,0:T(8,128)(2,1)S(1)}, u32[]{:S(2)}, u32[]{:S(2)}) collective-permute-start(bf16[104,256]{1,0:T(8,128)(2,1)S(1)} %piece_sum.1), channel_id=1, source_target_pairs={{0,9},{1,8},{2,11},{3,10},{4,13},{5,12},{6,15},{7,14},{8,1},{9,0},... | collective-permute-start | bytes 159752 | tf_op jit(solution)/shard_map/ppermute | solution.py:580
  57.0 0.7 collective-permute-start.14
  57.7 1.6 %collective-permute-start.22 = (bf16[104,256]{1,0:T(8,128)(2,1)S(1)}, bf16[104,256]{1,0:T(8,128)(2,1)S(1)}, u32[]{:S(2)}, u32[]{:S(2)}) collective-permute-start(bf16[104,256]{1,0:T(8,128)(2,1)S(1)} %collective-permute-done.19), channel_id=1, source_target_pairs={{0,9},{1,8},{2,11},{3,10},{4,13},{5,12},{6,15},{7,14},{8,1},{9,0},... | collective-permute-start | bytes 159752 | tf_op jit(solution)/shard_map/ppermute | solution.py:580
  59.3 1.9 %collective-permute-start.21 = (bf16[104,256]{1,0:T(8,128)(2,1)S(1)}, bf16[104,256]{1,0:T(8,128)(2,1)S(1)}, u32[]{:S(2)}, u32[]{:S(2)}) collective-permute-start(bf16[104,256]{1,0:T(8,128)(2,1)S(1)} %collective-permute-done.19), channel_id=1, source_target_pairs={{0,4},{1,5},{2,6},{3,7},{4,1},{5,0},{6,3},{7,2},{8,13},{9,12},{10,... | collective-permute-start | bytes 159752 | tf_op jit(solution)/shard_map/ppermute | solution.py:580
  61.2 0.7 collective-permute-start.20
  61.8 1.5 %collective-permute-start.18 = (bf16[104,256]{1,0:T(8,128)(2,1)S(1)}, bf16[104,256]{1,0:T(8,128)(2,1)S(1)}, u32[]{:S(2)}, u32[]{:S(2)}) collective-permute-start(bf16[104,256]{1,0:T(8,128)(2,1)S(1)} %collective-permute-done.16), channel_id=1, source_target_pairs={{0,4},{1,5},{2,6},{3,7},{4,1},{5,0},{6,3},{7,2},{8,13},{9,12},{10,... | collective-permute-start | bytes 159752 | tf_op jit(solution)/shard_map/ppermute | solution.py:580
  63.4 0.7 collective-permute-start.17
  64.1 1.9 %collective-permute-start.24 = (bf16[104,256]{1,0:T(8,128)(2,1)S(1)}, bf16[104,256]{1,0:T(8,128)(2,1)S(1)}, u32[]{:S(2)}, u32[]{:S(2)}) collective-permute-start(bf16[104,256]{1,0:T(8,128)(2,1)S(1)} %collective-permute-done.22), channel_id=1, source_target_pairs={{0,4},{1,5},{2,6},{3,7},{4,1},{5,0},{6,3},{7,2},{8,13},{9,12},{10,... | collective-permute-start | bytes 159752 | tf_op jit(solution)/shard_map/ppermute | solution.py:580
  66.0 0.7 collective-permute-start.23
  66.7 1.2 %collective-permute-done.24.refs_7_ = bf16[104,256]{1,0:T(8,128)(2,1)S(1)} collective-permute-done((bf16[104,256]{1,0:T(8,128)(2,1)S(1)}, bf16[104,256]{1,0:T(8,128)(2,1)S(1)}, u32[]{:S(2)}, u32[]{:S(2)}) %collective-permute-start.24) | collective-permute-done | bytes 53280 | tf_op jit(solution)/shard_map/ppermute | solution.py:580
  68.0 1.8 %adam.1 = (f32[64,768]{1,0:T(8,128)}, f32[64,768]{1,0:T(8,128)}, f32[64,768]{1,0:T(8,128)}, f32[64,256]{1,0:T(8,128)}, f32[64,256]{1,0:T(8,128)}, /*index=5*/f32...) custom-call(bf16[104,256]{1,0:T(8,128)(2,1)S(1)} %collective-permute, ...), custom_call_target="tpu_custom_call" | custom-call | bytes 5163008 | tf_op jit(solution)/shard_map/adam/pallas_call | solution.py:546
  (59 shorter events, 0.3 us)
Async XLA Ops:
  0.7 6.7 %copy-start.6 = (bf16[512,256]{1,0:T(8,128)(2,1)S(1)}, bf16[512,256]{1,0:T(8,128)(2,1)}, u32[]{:S(2)}) copy-start(bf16[512,256]{1,0:T(8,128)(2,1)} %refs_0_.1) | copy-start | bytes 786436
  0.7 6.7 %copy-start.20 = (s32[128]{0:T(128)S(1)}, s32[128]{0:T(128)}, u32[]{:S(2)}) copy-start(s32[128]{0:T(128)} %param.22) | copy-start | bytes 1540
  0.7 6.7 %copy-start.19 = (s32[128]{0:T(128)S(1)}, s32[128]{0:T(128)}, u32[]{:S(2)}) copy-start(s32[128]{0:T(128)} %param.21) | copy-start | bytes 1540
  0.7 6.7 %copy-start.5 = (bf16[512,256]{1,0:T(8,128)(2,1)S(1)}, bf16[512,256]{1,0:T(8,128)(2,1)}, u32[]{:S(2)}) copy-start(bf16[512,256]{1,0:T(8,128)(2,1)} %seed_ref.1) | copy-start | bytes 786436
  2.4 7.5 %copy-start.13 = (bf16[208,256]{1,0:T(8,128)(2,1)S(1)}, bf16[208,256]{1,0:T(8,128)(2,1)}, u32[]{:S(2)}) copy-start(bf16[208,256]{1,0:T(8,128)(2,1)} %pack_first.1.refs_2_.refs_3_.refs_12_) | copy-start | bytes 319492
  2.4 6.2 %collective-permute-start = (bf16[208,256]{1,0:T(8,128)(2,1)}, bf16[208,256]{1,0:T(8,128)(2,1)S(1)}, u32[]{:S(2)}, u32[]{:S(2)}) collective-permute-start(bf16[208,256]{1,0:T(8,128)(2,1)} %pack_first.1.refs_2_.refs_3_.refs_12_), channel_id=1, source_target_pairs={{0,2},{1,3},{2,0},{3,1},{4,6},{5,7},{6,4},{7,5},{8,10},{9,11},{10,... | collective-permute-start | bytes 319496 | tf_op jit(solution)/shard_map/ppermute | solution.py:560
  7.2 8.7 %collective-permute-start.3 = (bf16[576,256]{1,0:T(8,128)(2,1)}, bf16[576,256]{1,0:T(8,128)(2,1)S(1)}, u32[]{:S(2)}, u32[]{:S(2)}) collective-permute-start(bf16[576,256]{1,0:T(8,128)(2,1)} %pack_second.1.refs_7_), channel_id=1, source_target_pairs={{0,2},{1,3},{2,0},{3,1},{4,6},{5,7},{6,4},{7,5},{8,10},{9,11},{10,... | collective-permute-start | bytes 884744 | tf_op jit(solution)/shard_map/ppermute | solution.py:560
  7.3 1.8 %collective-permute-start.1 = (bf16[208,256]{1,0:T(8,128)(2,1)}, bf16[208,256]{1,0:T(8,128)(2,1)S(1)}, u32[]{:S(2)}, u32[]{:S(2)}) collective-permute-start(bf16[208,256]{1,0:T(8,128)(2,1)} %pack_first.1.refs_2_.refs_3_.refs_12_), channel_id=1, source_target_pairs={{0,1},{1,0},{2,3},{3,2},{4,5},{5,4},{6,7},{7,6},{8,9},{9,8},{10,11... | collective-permute-start | bytes 319496 | tf_op jit(solution)/shard_map/ppermute | solution.py:560
  8.6 9.0 %copy-start.3 = (bf16[576,256]{1,0:T(8,128)(2,1)S(1)}, bf16[576,256]{1,0:T(8,128)(2,1)}, u32[]{:S(2)}) copy-start(bf16[576,256]{1,0:T(8,128)(2,1)} %pack_second.1.refs_7_) | copy-start | bytes 884740
  8.6 1.3 %collective-permute-start.2 = (bf16[208,256]{1,0:T(8,128)(2,1)S(1)}, bf16[208,256]{1,0:T(8,128)(2,1)S(1)}, u32[]{:S(2)}, u32[]{:S(2)}) collective-permute-start(bf16[208,256]{1,0:T(8,128)(2,1)S(1)} %collective-permute-done.refs_4_.refs_5_.refs_14_), channel_id=1, source_target_pairs={{0,1},{1,0},{2,3},{3,2},{4,5},{5,4},{6,7},{7,6},{8,9},{9,8},{10,11... | collective-permute-start | bytes 319496 | tf_op jit(solution)/shard_map/ppermute | solution.py:560
  8.7 7.3 %collective-permute-start.4 = (bf16[576,256]{1,0:T(8,128)(2,1)}, bf16[576,256]{1,0:T(8,128)(2,1)S(1)}, u32[]{:S(2)}, u32[]{:S(2)}) collective-permute-start(bf16[576,256]{1,0:T(8,128)(2,1)} %pack_second.1.refs_7_), channel_id=1, source_target_pairs={{0,1},{1,0},{2,3},{3,2},{4,5},{5,4},{6,7},{7,6},{8,9},{9,8},{10,11... | collective-permute-start | bytes 884744 | tf_op jit(solution)/shard_map/ppermute | solution.py:560
  16.0 1.6 %collective-permute-start.5 = (bf16[576,256]{1,0:T(8,128)(2,1)S(1)}, bf16[576,256]{1,0:T(8,128)(2,1)S(1)}, u32[]{:S(2)}, u32[]{:S(2)}) collective-permute-start(bf16[576,256]{1,0:T(8,128)(2,1)S(1)} %collective-permute-done.3.refs_9_), channel_id=1, source_target_pairs={{0,1},{1,0},{2,3},{3,2},{4,5},{5,4},{6,7},{7,6},{8,9},{9,8},{10,11... | collective-permute-start | bytes 884744 | tf_op jit(solution)/shard_map/ppermute | solution.py:560
  21.4 2.0 %collective-permute-start.6 = (bf16[2,576,256]{2,1,0:T(8,128)(2,1)S(1)}, bf16[2,576,256]{2,1,0:T(8,128)(2,1)S(1)}, u32[]{:S(2)}, u32[]{:S(2)}) collective-permute-start(bf16[2,576,256]{2,1,0:T(8,128)(2,1)S(1)} %get-tuple-element.104), channel_id=1, source_target_pairs={{0,1},{1,0},{2,3},{3,2},{4,5},{5,4},{6,7},{7,6},{8,9},{9,8},{10,11... | collective-permute-start | bytes 1769480 | tf_op jit(solution)/shard_map/ppermute | solution.py:560
  23.6 9.1 %collective-permute-start.8 = (bf16[1,576,256]{2,1,0:T(8,128)(2,1)S(1)}, bf16[1,576,256]{2,1,0:T(8,128)(2,1)S(1)}, u32[]{:S(2)}, u32[]{:S(2)}) collective-permute-start(bf16[1,576,256]{2,1,0:T(8,128)(2,1)S(1)} %get-tuple-element.120), channel_id=1, source_target_pairs={{0,2},{1,3},{2,0},{3,1},{4,6},{5,7},{6,4},{7,5},{8,10},{9,11},{10,... | collective-permute-start | bytes 884744 | tf_op jit(solution)/shard_map/ppermute | solution.py:560
  29.3 1.5 %collective-permute-start.7 = (bf16[2,200,256]{2,1,0:T(8,128)(2,1)S(1)}, bf16[2,200,256]{2,1,0:T(8,128)(2,1)S(1)}, u32[]{:S(2)}, u32[]{:S(2)}) collective-permute-start(bf16[2,200,256]{2,1,0:T(8,128)(2,1)S(1)} %get-tuple-element.118), channel_id=1, source_target_pairs={{0,1},{1,0},{2,3},{3,2},{4,5},{5,4},{6,7},{7,6},{8,9},{9,8},{10,11... | collective-permute-start | bytes 614408 | tf_op jit(solution)/shard_map/ppermute | solution.py:560
  32.7 4.7 %collective-permute-start.10 = (bf16[1,200,256]{2,1,0:T(8,128)(2,1)S(1)}, bf16[1,200,256]{2,1,0:T(8,128)(2,1)S(1)}, u32[]{:S(2)}, u32[]{:S(2)}) collective-permute-start(bf16[1,200,256]{2,1,0:T(8,128)(2,1)S(1)} %get-tuple-element.125), channel_id=1, source_target_pairs={{0,2},{1,3},{2,0},{3,1},{4,6},{5,7},{6,4},{7,5},{8,10},{9,11},{10,... | collective-permute-start | bytes 307208 | tf_op jit(solution)/shard_map/ppermute | solution.py:560
  33.3 34.5 %copy-start = (f32[64,1024]{1,0:T(8,128)S(1)}, f32[64,1024]{1,0:T(8,128)}, u32[]{:S(2)}) copy-start(f32[64,1024]{1,0:T(8,128)} %refs_14_.1) | copy-start | bytes 786436
  33.4 34.5 %copy-start.1 = (f32[256,256]{1,0:T(8,128)S(1)}, f32[256,256]{1,0:T(8,128)}, u32[]{:S(2)}) copy-start(f32[256,256]{1,0:T(8,128)} %refs_17_.1) | copy-start | bytes 786436
  33.4 34.5 %copy-start.2 = (f32[64,768]{1,0:T(8,128)S(1)}, f32[64,768]{1,0:T(8,128)}, u32[]{:S(2)}) copy-start(f32[64,768]{1,0:T(8,128)} %refs_8_.1) | copy-start | bytes 589828
  33.4 34.5 %copy-start.4 = (f32[64,256]{1,0:T(8,128)S(1)}, f32[64,256]{1,0:T(8,128)}, u32[]{:S(2)}) copy-start(f32[64,256]{1,0:T(8,128)} %refs_11_.1) | copy-start | bytes 196612
  33.4 34.5 %copy-start.7 = (f32[64,1024]{1,0:T(8,128)S(1)}, f32[64,1024]{1,0:T(8,128)}, u32[]{:S(2)}) copy-start(f32[64,1024]{1,0:T(8,128)} %refs_15_.1) | copy-start | bytes 786436
  33.4 34.5 %copy-start.8 = (f32[64,1024]{1,0:T(8,128)S(1)}, f32[64,1024]{1,0:T(8,128)}, u32[]{:S(2)}) copy-start(f32[64,1024]{1,0:T(8,128)} %refs_16_.1) | copy-start | bytes 786436
  33.4 34.5 %copy-start.9 = (f32[256,256]{1,0:T(8,128)S(1)}, f32[256,256]{1,0:T(8,128)}, u32[]{:S(2)}) copy-start(f32[256,256]{1,0:T(8,128)} %refs_18_.1) | copy-start | bytes 786436
  33.4 34.5 %copy-start.10 = (f32[256,256]{1,0:T(8,128)S(1)}, f32[256,256]{1,0:T(8,128)}, u32[]{:S(2)}) copy-start(f32[256,256]{1,0:T(8,128)} %refs_19_.1) | copy-start | bytes 786436
  33.4 34.5 %copy-start.11 = (f32[64,768]{1,0:T(8,128)S(1)}, f32[64,768]{1,0:T(8,128)}, u32[]{:S(2)}) copy-start(f32[64,768]{1,0:T(8,128)} %refs_9_.1) | copy-start | bytes 589828
  33.4 34.5 %copy-start.12 = (f32[64,768]{1,0:T(8,128)S(1)}, f32[64,768]{1,0:T(8,128)}, u32[]{:S(2)}) copy-start(f32[64,768]{1,0:T(8,128)} %refs_10_.1) | copy-start | bytes 589828
  33.4 34.5 %copy-start.14 = (f32[64,256]{1,0:T(8,128)S(1)}, f32[64,256]{1,0:T(8,128)}, u32[]{:S(2)}) copy-start(f32[64,256]{1,0:T(8,128)} %refs_12_.1) | copy-start | bytes 196612
  33.4 34.5 %copy-start.15 = (f32[64,256]{1,0:T(8,128)S(1)}, f32[64,256]{1,0:T(8,128)}, u32[]{:S(2)}) copy-start(f32[64,256]{1,0:T(8,128)} %refs_13_.1) | copy-start | bytes 196612
  33.5 34.5 %copy-start.16 = (f32[768]{0:T(1024)S(1)}, f32[768]{0:T(1024)}, u32[]{:S(2)}) copy-start(f32[768]{0:T(1024)} %refs_20_.1) | copy-start | bytes 9220
  33.5 34.5 %copy-start.17 = (f32[768]{0:T(1024)S(1)}, f32[768]{0:T(1024)}, u32[]{:S(2)}) copy-start(f32[768]{0:T(1024)} %refs_21_.1) | copy-start | bytes 9220
  33.5 34.5 %copy-start.18 = (f32[768]{0:T(1024)S(1)}, f32[768]{0:T(1024)}, u32[]{:S(2)}) copy-start(f32[768]{0:T(1024)} %refs_22_.1) | copy-start | bytes 9220
  33.6 6.2 %collective-permute-start.9 = (bf16[4,72,256]{2,1,0:T(8,128)(2,1)S(1)}, bf16[4,72,256]{2,1,0:T(8,128)(2,1)S(1)}, u32[]{:S(2)}, u32[]{:S(2)}) collective-permute-start(bf16[4,72,256]{2,1,0:T(8,128)(2,1)S(1)} %get-tuple-element.123), channel_id=1, source_target_pairs={{0,5},{1,4},{2,7},{3,6},{4,1},{5,0},{6,3},{7,2},{8,13},{9,12},{10,... | collective-permute-start | bytes 442376 | tf_op jit(solution)/shard_map/ppermute | solution.py:580
  37.4 4.4 %collective-permute-start.11 = (bf16[4,32,256]{2,1,0:T(8,128)(2,1)S(1)}, bf16[4,32,256]{2,1,0:T(8,128)(2,1)S(1)}, u32[]{:S(2)}, u32[]{:S(2)}) collective-permute-start(bf16[4,32,256]{2,1,0:T(8,128)(2,1)S(1)} %get-tuple-element.127), channel_id=1, source_target_pairs={{0,5},{1,4},{2,7},{3,6},{4,1},{5,0},{6,3},{7,2},{8,13},{9,12},{10,... | collective-permute-start | bytes 196616 | tf_op jit(solution)/shard_map/ppermute | solution.py:580
  41.8 5.0 %collective-permute-start.12 = (bf16[2,104,256]{2,1,0:T(8,128)(2,1)S(1)}, bf16[2,104,256]{2,1,0:T(8,128)(2,1)S(1)}, u32[]{:S(2)}, u32[]{:S(2)}) collective-permute-start(bf16[2,104,256]{2,1,0:T(8,128)(2,1)S(1)} %get-tuple-element.129), channel_id=1, source_target_pairs={{0,9},{1,8},{2,11},{3,10},{4,13},{5,12},{6,15},{7,14},{8,1},{9,0},... | collective-permute-start | bytes 319496 | tf_op jit(solution)/shard_map/ppermute | solution.py:580
  46.9 4.8 %collective-permute-start.13 = (bf16[1,104,256]{2,1,0:T(8,128)(2,1)S(1)}, bf16[1,104,256]{2,1,0:T(8,128)(2,1)S(1)}, u32[]{:S(2)}, u32[]{:S(2)}) collective-permute-start(bf16[1,104,256]{2,1,0:T(8,128)(2,1)S(1)} %get-tuple-element.131), channel_id=1, source_target_pairs={{0,17},{1,16},{2,19},{3,18},{4,21},{5,20},{6,23},{7,22},{8,25},{9,... | collective-permute-start | bytes 159752 | tf_op jit(solution)/shard_map/ppermute | solution.py:580
  51.7 5.9 %collective-permute-start.19 = (bf16[104,256]{1,0:T(8,128)(2,1)S(1)}, bf16[104,256]{1,0:T(8,128)(2,1)S(1)}, u32[]{:S(2)}, u32[]{:S(2)}) collective-permute-start(bf16[104,256]{1,0:T(8,128)(2,1)S(1)} %piece_sum.1), channel_id=1, source_target_pairs={{0,17},{1,16},{2,19},{3,18},{4,21},{5,20},{6,23},{7,22},{8,25},{9,... | collective-permute-start | bytes 159752 | tf_op jit(solution)/shard_map/ppermute | solution.py:580
  54.2 7.0 %collective-permute-start.16 = (bf16[104,256]{1,0:T(8,128)(2,1)S(1)}, bf16[104,256]{1,0:T(8,128)(2,1)S(1)}, u32[]{:S(2)}, u32[]{:S(2)}) collective-permute-start(bf16[104,256]{1,0:T(8,128)(2,1)S(1)} %piece_sum.1), channel_id=1, source_target_pairs={{0,9},{1,8},{2,11},{3,10},{4,13},{5,12},{6,15},{7,14},{8,1},{9,0},... | collective-permute-start | bytes 159752 | tf_op jit(solution)/shard_map/ppermute | solution.py:580
  57.0 4.9 %collective-permute-start.15 = (bf16[104,256]{1,0:T(8,128)(2,1)S(1)}, bf16[104,256]{1,0:T(8,128)(2,1)S(1)}, u32[]{:S(2)}, u32[]{:S(2)}) collective-permute-start(bf16[104,256]{1,0:T(8,128)(2,1)S(1)} %piece_sum.1), channel_id=1, source_target_pairs={{0,4},{1,5},{2,6},{3,7},{4,1},{5,0},{6,3},{7,2},{8,13},{9,12},{10,... | collective-permute-start | bytes 159752 | tf_op jit(solution)/shard_map/ppermute | solution.py:580
  57.0 6.4 %collective-permute-start.14 = (bf16[104,256]{1,0:T(8,128)(2,1)S(1)}, bf16[104,256]{1,0:T(8,128)(2,1)S(1)}, u32[]{:S(2)}, u32[]{:S(2)}) collective-permute-start(bf16[104,256]{1,0:T(8,128)(2,1)S(1)} %piece_sum.1), channel_id=1, source_target_pairs={{0,0},{1,1},{2,2},{3,3},{4,5},{5,4},{6,7},{7,6},{8,9},{9,8},{10,11... | collective-permute-start | bytes 159752 | tf_op jit(solution)/shard_map/ppermute | solution.py:580
  57.7 6.4 %collective-permute-start.22 = (bf16[104,256]{1,0:T(8,128)(2,1)S(1)}, bf16[104,256]{1,0:T(8,128)(2,1)S(1)}, u32[]{:S(2)}, u32[]{:S(2)}) collective-permute-start(bf16[104,256]{1,0:T(8,128)(2,1)S(1)} %collective-permute-done.19), channel_id=1, source_target_pairs={{0,9},{1,8},{2,11},{3,10},{4,13},{5,12},{6,15},{7,14},{8,1},{9,0},... | collective-permute-start | bytes 159752 | tf_op jit(solution)/shard_map/ppermute | solution.py:580
  59.3 6.7 %collective-permute-start.21 = (bf16[104,256]{1,0:T(8,128)(2,1)S(1)}, bf16[104,256]{1,0:T(8,128)(2,1)S(1)}, u32[]{:S(2)}, u32[]{:S(2)}) collective-permute-start(bf16[104,256]{1,0:T(8,128)(2,1)S(1)} %collective-permute-done.19), channel_id=1, source_target_pairs={{0,4},{1,5},{2,6},{3,7},{4,1},{5,0},{6,3},{7,2},{8,13},{9,12},{10,... | collective-permute-start | bytes 159752 | tf_op jit(solution)/shard_map/ppermute | solution.py:580
  61.2 5.5 %collective-permute-start.20 = (bf16[104,256]{1,0:T(8,128)(2,1)S(1)}, bf16[104,256]{1,0:T(8,128)(2,1)S(1)}, u32[]{:S(2)}, u32[]{:S(2)}) collective-permute-start(bf16[104,256]{1,0:T(8,128)(2,1)S(1)} %collective-permute-done.19), channel_id=1, source_target_pairs={{0,0},{1,1},{2,2},{3,3},{4,5},{5,4},{6,7},{7,6},{8,9},{9,8},{10,11... | collective-permute-start | bytes 159752 | tf_op jit(solution)/shard_map/ppermute | solution.py:580
  61.8 4.8 %collective-permute-start.18 = (bf16[104,256]{1,0:T(8,128)(2,1)S(1)}, bf16[104,256]{1,0:T(8,128)(2,1)S(1)}, u32[]{:S(2)}, u32[]{:S(2)}) collective-permute-start(bf16[104,256]{1,0:T(8,128)(2,1)S(1)} %collective-permute-done.16), channel_id=1, source_target_pairs={{0,4},{1,5},{2,6},{3,7},{4,1},{5,0},{6,3},{7,2},{8,13},{9,12},{10,... | collective-permute-start | bytes 159752 | tf_op jit(solution)/shard_map/ppermute | solution.py:580
  63.4 3.3 %collective-permute-start.17 = (bf16[104,256]{1,0:T(8,128)(2,1)S(1)}, bf16[104,256]{1,0:T(8,128)(2,1)S(1)}, u32[]{:S(2)}, u32[]{:S(2)}) collective-permute-start(bf16[104,256]{1,0:T(8,128)(2,1)S(1)} %collective-permute-done.16), channel_id=1, source_target_pairs={{0,0},{1,1},{2,2},{3,3},{4,5},{5,4},{6,7},{7,6},{8,9},{9,8},{10,11... | collective-permute-start | bytes 159752 | tf_op jit(solution)/shard_map/ppermute | solution.py:580
  64.1 3.8 %collective-permute-start.24 = (bf16[104,256]{1,0:T(8,128)(2,1)S(1)}, bf16[104,256]{1,0:T(8,128)(2,1)S(1)}, u32[]{:S(2)}, u32[]{:S(2)}) collective-permute-start(bf16[104,256]{1,0:T(8,128)(2,1)S(1)} %collective-permute-done.22), channel_id=1, source_target_pairs={{0,4},{1,5},{2,6},{3,7},{4,1},{5,0},{6,3},{7,2},{8,13},{9,12},{10,... | collective-permute-start | bytes 159752 | tf_op jit(solution)/shard_map/ppermute | solution.py:580
  66.0 1.9 %collective-permute-start.23 = (bf16[104,256]{1,0:T(8,128)(2,1)S(1)}, bf16[104,256]{1,0:T(8,128)(2,1)S(1)}, u32[]{:S(2)}, u32[]{:S(2)}) collective-permute-start(bf16[104,256]{1,0:T(8,128)(2,1)S(1)} %collective-permute-done.22), channel_id=1, source_target_pairs={{0,0},{1,1},{2,2},{3,3},{4,5},{5,4},{6,7},{7,6},{8,9},{9,8},{10,11... | collective-permute-start | bytes 159752 | tf_op jit(solution)/shard_map/ppermute | solution.py:580

commit v9 on v7

--- a/solution.py
+++ b/solution.py
@@ -314,7 +314,7 @@
     sums_ref[1:2, :] = shift_grad
     sums_ref[2:3, :] = jnp.sum(dmiddle_low.astype(wide), axis=0, keepdims=True)
     sums_ref[3:4, :] = jnp.sum(seed, axis=0, keepdims=True)
-    part_ways(grads_ref, keep_ref, send_ref, shard % 2)
+    part_ways(grads_ref, keep_ref, send_ref, shard & 1)
 
 
 def part_ways(grads_ref, keep_ref, send_ref, side):
@@ -380,7 +380,7 @@
     back_heads(heads, *refs)
 
 
-def back_last_kernel(shards, groups, *refs):
+def back_last_kernel(shards, head_groups, *refs):
     shared = refs[:5]
     earlier = refs[5:8]
     norm_ref, root_ref, middle_ref, sums_in = refs[8:12]
@@ -396,7 +396,7 @@
     gain, shift = small_ref[0, 0:1, :], small_ref[0, 1:2, :]
     for target, value in zip((dquery_t, dkey, dvalue), earlier):
         target[...] = value[...]
-    for index, heads in enumerate(groups):
+    for heads in head_groups:
         back_heads(heads, *shared, dquery_t, dkey, dvalue)
         if (heads[-1] + 1) * HEAD % LANES == 0:
             first = (heads[-1] + 1) * HEAD - LANES
@@ -426,14 +426,11 @@
     sums = [gain_grad, shift_grad, sums_in[0:1, :], sums_in[1:2, :]] + bias_sums
     sums += [sums_in[row : row + 1, :] for row in range(2, 8)]
     per_shard = len(sums) // shards
+    empty = [jnp.zeros((grads_ref.shape[1] - 3 * part - per_shard, width), wide)]
     for target in range(shards):
-        at = 3 * part
-        grads_ref[target, at:, :] = jnp.zeros((grads_ref.shape[1] - at, width), wide)
-        for row in range(per_shard):
-            grads_ref[target, at + row * TILE_ROWS : at + row * TILE_ROWS + 1, :] = sums[
-                target * per_shard + row
-            ]
-    part_ways(grads_ref, keep_ref, send_ref, shard % 2)
+        rows_here = sums[target * per_shard : (target + 1) * per_shard]
+        grads_ref[target, 3 * part :, :] = jnp.concatenate(rows_here + empty, axis=0)
+    part_ways(grads_ref, keep_ref, send_ref, shard & 1)
 
 
 def halve_kernel(axis, bit, *refs):
@@ -451,9 +448,9 @@
 
 
 def piece_spans(total, tail, group):
-    spans = [((total - tail) // group, 0)]
+    spans = [((total - tail) // group, 0, True)]
     if tail:
-        spans.append((tail // group, total - tail))
+        spans.append((tail, total - tail, False))
     return spans
 
 
@@ -465,8 +462,8 @@
         total = total + piece[...].astype(wide)
     for index in range(group):
         row = 0
-        for rows, first in piece_spans(total.shape[0], tail, group):
-            at = first + index * rows
+        for rows, first, moves in piece_spans(total.shape[0], tail, group):
+            at = first + index * rows if moves else first
             sum_ref[index, row : row + rows, :] = total[at : at + rows, :]
             row += rows
     side = lax.axis_index("dp") & 1
@@ -475,9 +472,13 @@
         send_ref[pair] = sum_ref[2 * pair + 1 - side].astype(low)
 
 
-def add_kernel(mine_ref, other_ref, sum_ref):
-    total = mine_ref[...].astype(wide) + other_ref[...].astype(wide)
-    sum_ref[...] = total.astype(low).reshape(sum_ref.shape)
+def piece_kernel(*refs):
+    parts = [
+        mine[...].reshape(mine.shape[-2:]).astype(wide)
+        + other[...].reshape(other.shape[-2:]).astype(wide)
+        for mine, other in zip(refs[:-1:2], refs[1:-1:2])
+    ]
+    refs[-1][...] = jnp.concatenate(parts, axis=0).astype(low)
 
 
 def adam_values(weight, grad, first, second, decay_rate):
@@ -561,14 +562,20 @@
     return lax.ppermute(values, axis, [(index, index ^ mask) for index in range(count)])
 
 
-def gather_near(value, axis, count):
+def gather_pieces(value, group):
     found = {0: value}
-    far = count // 2
-    while far:
+    found[1] = exchange(value, "dp", 1)
+    far = group // 2
+    while far > 1:
         for offset in sorted(found):
-            found[offset ^ far] = exchange(found[offset], axis, far)
+            if offset & 1 == 0:
+                found[offset ^ far] = exchange(found[offset], "dp", far)
+        if far == group // 2:
+            found[far], found[1] = lax.optimization_barrier((found[far], found[1]))
         far //= 2
-    return [found[offset] for offset in range(count)]
+    for offset in range(2, group, 2):
+        found[offset ^ 1] = exchange(found[offset], "dp", 1)
+    return [found[offset] for offset in range(group)]
 
 
 def halve_call(axis, bit, flat, name):
@@ -581,7 +588,7 @@
 
 def split_chunk(chunk, tail, group):
     rows, width = chunk[0].shape
-    half = (group // 2, rows // group, width)
+    half = (group // 2, (rows - tail) // group + tail, width)
     keep, send = local_call(
         functools.partial(split_kernel, tail),
         [(half, wide), (half, low)],
@@ -592,24 +599,29 @@
     return keep, exchange(send, "dp", 1)
 
 
-def finish_sum(chunks, group):
-    replicas = lax.axis_size("dp")
-    half, _, width = chunks[0][0].shape
-    rows = sum(chunk[0].shape[1] for chunk in chunks)
-    flat = [item for chunk in chunks for item in chunk]
+def near_sum(flat):
+    half = flat[0].shape[0]
     bit = 1
     while half > 1:
         half //= 2
         keep, send = halve_call("dp", bit, flat, "halve_dp")
         flat = [keep, exchange(send, "dp", 1 << bit)]
         bit += 1
+    return flat
+
+
+def finish_sum(chunks, group):
+    replicas = lax.axis_size("dp")
+    flat = [item for chunk in chunks for item in near_sum(chunk)]
+    width = flat[0].shape[-1]
+    rows = sum(item.shape[1] for item in flat[::2])
+    (piece,) = local_call(piece_kernel, [((rows, width), low)], flat, name="piece_sum")
     mask = group
-    (piece,) = local_call(add_kernel, [((rows, width), low)], flat, name="piece_sum")
     while mask < replicas:
         other = exchange(piece, "dp", mask)
-        (piece,) = local_call(add_kernel, [((rows, width), low)], [piece, other], name="far_sum")
+        (piece,) = local_call(piece_kernel, [((rows, width), low)], [piece, other], name="far_sum")
         mask *= 2
-    return gather_near(piece, "dp", group)
+    return gather_pieces(piece, group)
 
 
 def adam_call(pieces, counts, tails, states, layout):
@@ -618,9 +630,10 @@
     spans = []
     first = row = 0
     for total, tail in zip(counts, tails):
-        for rows, start in piece_spans(total, tail, group):
+        for rows, start, moves in piece_spans(total, tail, group):
             spans.append((rows, first + start, row))
             row += rows
+            first += rows * (group - 1) * (not moves)
         first += total
     outs = [(state[0].shape, wide) for state in states for _ in range(3)]
     return local_call(
@@ -745,7 +758,7 @@
     tile_scratch = [((LANES, rows), low), ((rows, LANES), wide), ((rows, LANES), wide)]
     per_tile = LANES // HEAD
     groups = [list(range(at, at + per_tile)) for at in range(0, heads, per_tile)]
-    groups = [groups[0][:2], groups[0][2:]] + groups[1:]
+    groups = [groups[0][:3], groups[0][3:]] + groups[1:]
     first_query, first_key, first_value = local_call(
         functools.partial(back_first_kernel, groups[0]),
         tile_scratch,
@@ -757,7 +770,7 @@
     keep_ffn, send_ffn = halve_call("shard", 1, [kept_ffn, arrived_ffn], "halve_ffn")
     first_query, send_ffn = lax.optimization_barrier((first_query, send_ffn))
     arrived_ffn = exchange(send_ffn, "shard", 2)
-    tail = GROUP * TILE_ROWS
+    tail = TILE_ROWS
     att_rows = 3 * part + tail
     pair = (shards // 2, att_rows, width)
     input_grad, kept_att, send_att = local_call(
@@ -795,7 +808,7 @@
             (0, part, matrix_decay),
             (part, part, matrix_decay),
             (part + blocks * part, 0, matrix_decay),
-            (second_rows + 3 * part, TILE_ROWS, 0.0),
+            (second_rows + 3 * part, 1, 0.0),
         ],
     )
     return (output, input_grad, *results)

time: 69.9 us -> 69.5 us (level)
  waiting for transfers between devices: 28.2 us -> 24.1 us
  starting transfers between devices: 21.1 us -> 24.4 us
    ppermute x21 -> x23, waiting for transfers between devices: 28.2 us -> 24.1 us  [exchange(): lax.ppermute(values, axis, [(index, index ^ mask) for index in range(coun...]
    ppermute x21 -> x23, starting transfers between devices: 21.1 us -> 24.4 us  [exchange(): lax.ppermute(values, axis, [(index, index ^ mask) for index in range(coun...]
    pallas_call x15 -> x17, Pallas kernels: 19.1 us -> 19.5 us  [local_call(): pl.pallas_call(kernel, out_shape=outs, in_specs=[pl.BlockSpec(memory_spac...]
  transfers between devices with their start and end apart: 21 -> 23, of which waited for: 15 -> 15; matrix products, arithmetic and copies ran while one was open for 0% -> 0% of each run, Pallas kernels for 17% -> 17%
where the time goes in v9:
time: 69.5 us; the launch traced here: 69.4 us
  starting transfers between devices  24.4 us (35%)
  waiting for transfers between devices  24.1 us (35%)
  Pallas kernels  19.5 us (28%)
  between operations  1.18 us (2%)
    ppermute x23, starting transfers between devices, exchange(): lax.ppermute(values, axis, [(index, index ^ mask) for index in range(coun...  24.4 us
    ppermute x23, waiting for transfers between devices, exchange(): lax.ppermute(values, axis, [(index, index ^ mask) for index in range(coun...  24.1 us
    pallas_call x17, Pallas kernels, local_call(): pl.pallas_call(kernel, out_shape=outs, in_specs=[pl.BlockSpec(memory_spac...  19.5 us
  transfers between devices with their start and end apart: 23, of which 15 were waited for; matrix products, arithmetic and copies ran while one was open for 0% of the time, Pallas kernels for 17%

profile of v9, /device:TPU:0, one launch (start us, length us, event | category | flops | bytes accessed | tf_op | source)
XLA Modules:
  0.0 69.4 jit_solution(12118129672040335264)
XLA Ops:
  0.7 1.7 %pack_first.1.refs_2_.refs_3_.refs_12_ = bf16[208,256]{1,0:T(8,128)(2,1)} custom-call(f32[64,768]{1,0:T(8,128)} %refs_8_.1, f32[768]{0:T(1024)} %refs_20_.1), custom_call_target="tpu_custom_call" | custom-call | bytes 306176 | tf_op jit(solution)/shard_map/pack_first/pallas_call | solution.py:548
  2.4 3.0 %collective-permute-start = (bf16[208,256]{1,0:T(8,128)(2,1)}, bf16[208,256]{1,0:T(8,128)(2,1)S(1)}, u32[]{:S(2)}, u32[]{:S(2)}) collective-permute-start(bf16[208,256]{1,0:T(8,128)(2,1)} %pack_first.1.refs_2_.refs_3_.refs_12_), channel_id=1, source_target_pairs={{0,2},{1,3},{2,0},{3,1},{4,6},{5,7},{6,4},{7,5},{8,10},{9,11},{10,... | collective-permute-start | bytes 319496 | tf_op jit(solution)/shard_map/ppermute | solution.py:562
  5.4 1.8 %pack_second.1.refs_7_ = bf16[576,256]{1,0:T(8,128)(2,1)} custom-call(f32[64,256]{1,0:T(8,128)} %refs_11_.1, f32[64,1024]{1,0:T(8,128)} %refs_14_.1, f32[256,256]{1,0:T(8,128)} %refs_17_.1), custom_call_target="tpu_custom_call" | custom-call | bytes 884736 | tf_op jit(solution)/shard_map/pack_second/pallas_call | solution.py:548
  7.2 0.1 collective-permute-start.3
  7.3 0.1 collective-permute-start.1
  7.4 0.6 prepare.1
  8.1 0.5 collective-permute-done.refs_4_.refs_5_.refs_14_
  8.6 0.1 collective-permute-start.2
  8.7 0.5 collective-permute-start.4
  9.1 0.8 %collective-permute-done.2.refs_5_.refs_6_.refs_15_ = bf16[208,256]{1,0:T(8,128)(2,1)S(1)} collective-permute-done((bf16[208,256]{1,0:T(8,128)(2,1)S(1)}, bf16[208,256]{1,0:T(8,128)(2,1)S(1)}, u32[]{:S(2)}, u32[]{:S(2)}) %collective-permute-start.2) | collective-permute-done | bytes 106528 | tf_op jit(solution)/shard_map/ppermute | solution.py:562
  9.9 3.0 %attend.1 = (bf16[512,768]{1,0:T(8,128)(2,1)S(1)}, bf16[512,256]{1,0:T(8,128)(2,1)S(1)}, f32[8,512]{1,0:T(8,128)S(1)}, f32[256,512]{1,0:T(8,128)S(1)}) custom-call(f32[512,256]{1,0:T(8,128)S(1)} %get-tuple-element.96.refs_0_.refs_8_, f32[512,512]{1,0:T(8,128)S(1)} %get-tuple-element.97.refs_1_.refs_3_, bf16[208,256]{1,0:T(8,128)(2,1)S(1)} %copy-done.13, ...), custom_call_target="tpu_custom_call" | custom-call | flops 1342177280 | bytes 3588096 | tf_op jit(solution)/shard_map/attend/pallas_call | solution.py:548
  12.9 3.0 %collective-permute-done.3.refs_9_ = bf16[576,256]{1,0:T(8,128)(2,1)S(1)} collective-permute-done((bf16[576,256]{1,0:T(8,128)(2,1)}, bf16[576,256]{1,0:T(8,128)(2,1)S(1)}, u32[]{:S(2)}, u32[]{:S(2)}) %collective-permute-start.3) | collective-permute-done | bytes 294944 | tf_op jit(solution)/shard_map/ppermute | solution.py:562
  16.0 1.6 %collective-permute-done.5.refs_10_ = bf16[576,256]{1,0:T(8,128)(2,1)S(1)} collective-permute-done((bf16[576,256]{1,0:T(8,128)(2,1)S(1)}, bf16[576,256]{1,0:T(8,128)(2,1)S(1)}, u32[]{:S(2)}, u32[]{:S(2)}) %collective-permute-start.5) | collective-permute-done | bytes 294944 | tf_op jit(solution)/shard_map/ppermute | solution.py:562
  17.6 3.9 %feed.1 = (bf16[512,256]{1,0:T(8,128)(2,1)}, f32[512,256]{1,0:T(8,128)S(1)}, bf16[512,256]{1,0:T(8,128)(2,1)S(1)}, f32[16,256]{1,0:T(8,128)S(1)}, f32[2,576,256]...) custom-call(bf16[512,256]{1,0:T(8,128)(2,1)S(1)} %copy-done.6, bf16[512,256]{1,0:T(8,128)(2,1)S(1)} %get-tuple-element.101.refs_1_, ...), custom_call_target="tpu_custom_call" | custom-call | flops 1811939328 | bytes 5226496 | tf_op jit(solution)/shard_map/feed/pallas_call | solution.py:548
  21.5 0.1 collective-permute-start.6
  21.6 1.7 %back_first.1 = (bf16[128,512]{1,0:T(8,128)(2,1)S(1)}, f32[512,128]{1,0:T(8,128)S(1)}, f32[512,128]{1,0:T(8,128)S(1)}) custom-call(bf16[512,768]{1,0:T(8,128)(2,1)S(1)} %get-tuple-element.105.refs_0_, bf16[512,256]{1,0:T(8,128)(2,1)S(1)} %get-tuple-element.106.refs_1_, f32[8,512]{1,0:T(8,128)S(1)} %get-tuple-element.107.refs_2_, ...), custom_call_target="tpu_custom_call" | custom-call | flops 1342177280 | bytes 3293184 | tf_op jit(solution)/shard_map/back_first/pallas_call | solution.py:548
  23.3 0.1 collective-permute-done.6.refs_1_
  23.5 0.1 halve_ffn.1
  23.6 0.7 %collective-permute-start.8 = (bf16[1,576,256]{2,1,0:T(8,128)(2,1)S(1)}, bf16[1,576,256]{2,1,0:T(8,128)(2,1)S(1)}, u32[]{:S(2)}, u32[]{:S(2)}) collective-permute-start(bf16[1,576,256]{2,1,0:T(8,128)(2,1)S(1)} %get-tuple-element.126), channel_id=1, source_target_pairs={{0,2},{1,3},{2,0},{3,1},{4,6},{5,7},{6,4},{7,5},{8,10},{9,11},{10,... | collective-permute-start | bytes 884744 | tf_op jit(solution)/shard_map/ppermute | solution.py:562
  24.3 4.5 %back_last.1 = (f32[512,256]{1,0:T(8,128)}, f32[2,200,256]{2,1,0:T(8,128)S(1)}, bf16[2,200,256]{2,1,0:T(8,128)(2,1)S(1)}) custom-call(bf16[512,768]{1,0:T(8,128)(2,1)S(1)} %get-tuple-element.105.refs_0_, bf16[512,256]{1,0:T(8,128)(2,1)S(1)} %get-tuple-element.106.refs_1_, f32[8,512]{1,0:T(8,128)S(1)} %get-tuple-element.107.refs_2_, ...), custom_call_target="tpu_custom_call" | custom-call | flops 3221225472 | bytes 5924864 | tf_op jit(solution)/shard_map/back_last/pallas_call | solution.py:548
  28.8 1.5 %collective-permute-done.7.refs_1_ = bf16[2,200,256]{2,1,0:T(8,128)(2,1)S(1)} collective-permute-done((bf16[2,200,256]{2,1,0:T(8,128)(2,1)S(1)}, bf16[2,200,256]{2,1,0:T(8,128)(2,1)S(1)}, u32[]{:S(2)}, u32[]{:S(2)}) %collective-permute-start.7) | collective-permute-done | bytes 204832 | tf_op jit(solution)/shard_map/ppermute | solution.py:562
  30.3 2.5 %collective-permute-done.8 = bf16[1,576,256]{2,1,0:T(8,128)(2,1)S(1)} collective-permute-done((bf16[1,576,256]{2,1,0:T(8,128)(2,1)S(1)}, bf16[1,576,256]{2,1,0:T(8,128)(2,1)S(1)}, u32[]{:S(2)}, u32[]{:S(2)}) %collective-permute-start.8) | collective-permute-done | bytes 294944 | tf_op jit(solution)/shard_map/ppermute | solution.py:562
  32.8 0.0 copy-start.7
  32.8 0.0 copy-start.8
  33.0 0.1 split_sum.2
  33.1 1.6 %collective-permute-start.9 = (bf16[4,72,256]{2,1,0:T(8,128)(2,1)S(1)}, bf16[4,72,256]{2,1,0:T(8,128)(2,1)S(1)}, u32[]{:S(2)}, u32[]{:S(2)}) collective-permute-start(bf16[4,72,256]{2,1,0:T(8,128)(2,1)S(1)} %get-tuple-element.129), channel_id=1, source_target_pairs={{0,4},{4,0},{8,12},{12,8},{16,20},{20,16},{24,28},{28,24},{1,5},{5... | collective-permute-start | bytes 442376 | tf_op jit(solution)/shard_map/ppermute | solution.py:562
  34.7 0.7 collective-permute-start.12
  35.3 4.0 %collective-permute-done.12 = bf16[1,200,256]{2,1,0:T(8,128)(2,1)S(1)} collective-permute-done((bf16[1,200,256]{2,1,0:T(8,128)(2,1)S(1)}, bf16[1,200,256]{2,1,0:T(8,128)(2,1)S(1)}, u32[]{:S(2)}, u32[]{:S(2)}) %collective-permute-start.12) | collective-permute-done | bytes 102432 | tf_op jit(solution)/shard_map/ppermute | solution.py:562
  39.4 0.6 collective-permute-start.13
  40.0 1.6 %collective-permute-start.10 = (bf16[2,72,256]{2,1,0:T(8,128)(2,1)S(1)}, bf16[2,72,256]{2,1,0:T(8,128)(2,1)S(1)}, u32[]{:S(2)}, u32[]{:S(2)}) collective-permute-start(bf16[2,72,256]{2,1,0:T(8,128)(2,1)S(1)} %get-tuple-element.131), channel_id=1, source_target_pairs={{0,8},{4,12},{8,0},{12,4},{16,24},{20,28},{24,16},{28,20},{1,9},{5... | collective-permute-start | bytes 221192 | tf_op jit(solution)/shard_map/ppermute | solution.py:562
  41.6 2.0 %collective-permute-done.13.refs_1_ = bf16[4,32,256]{2,1,0:T(8,128)(2,1)S(1)} collective-permute-done((bf16[4,32,256]{2,1,0:T(8,128)(2,1)S(1)}, bf16[4,32,256]{2,1,0:T(8,128)(2,1)S(1)}, u32[]{:S(2)}, u32[]{:S(2)}) %collective-permute-start.13) | collective-permute-done | bytes 65568 | tf_op jit(solution)/shard_map/ppermute | solution.py:562
  43.7 1.6 %collective-permute-start.14 = (bf16[2,32,256]{2,1,0:T(8,128)(2,1)S(1)}, bf16[2,32,256]{2,1,0:T(8,128)(2,1)S(1)}, u32[]{:S(2)}, u32[]{:S(2)}) collective-permute-start(bf16[2,32,256]{2,1,0:T(8,128)(2,1)S(1)} %get-tuple-element.139), channel_id=1, source_target_pairs={{0,8},{4,12},{8,0},{12,4},{16,24},{20,28},{24,16},{28,20},{1,9},{5... | collective-permute-start | bytes 98312 | tf_op jit(solution)/shard_map/ppermute | solution.py:562
  45.4 2.7 %collective-permute-start.11 = (bf16[1,72,256]{2,1,0:T(8,128)(2,1)S(1)}, bf16[1,72,256]{2,1,0:T(8,128)(2,1)S(1)}, u32[]{:S(2)}, u32[]{:S(2)}) collective-permute-start(bf16[1,72,256]{2,1,0:T(8,128)(2,1)S(1)} %get-tuple-element.133), channel_id=1, source_target_pairs={{0,16},{4,20},{8,24},{12,28},{16,0},{20,4},{24,8},{28,12},{1,17},{... | collective-permute-start | bytes 110600 | tf_op jit(solution)/shard_map/ppermute | solution.py:562
  48.1 2.3 %collective-permute-start.15 = (bf16[1,32,256]{2,1,0:T(8,128)(2,1)S(1)}, bf16[1,32,256]{2,1,0:T(8,128)(2,1)S(1)}, u32[]{:S(2)}, u32[]{:S(2)}) collective-permute-start(bf16[1,32,256]{2,1,0:T(8,128)(2,1)S(1)} %get-tuple-element.141), channel_id=1, source_target_pairs={{0,16},{4,20},{8,24},{12,28},{16,0},{20,4},{24,8},{28,12},{1,17},{... | collective-permute-start | bytes 49160 | tf_op jit(solution)/shard_map/ppermute | solution.py:562
  50.4 2.5 %collective-permute-done.15.refs_3_ = bf16[1,32,256]{2,1,0:T(8,128)(2,1)S(1)} collective-permute-done((bf16[1,32,256]{2,1,0:T(8,128)(2,1)S(1)}, bf16[1,32,256]{2,1,0:T(8,128)(2,1)S(1)}, u32[]{:S(2)}, u32[]{:S(2)}) %collective-permute-start.15) | collective-permute-done | bytes 16416 | tf_op jit(solution)/shard_map/ppermute | solution.py:562
  52.8 1.1 %collective-permute-start.17 = (bf16[104,256]{1,0:T(8,128)(2,1)S(1)}, bf16[104,256]{1,0:T(8,128)(2,1)S(1)}, u32[]{:S(2)}, u32[]{:S(2)}) collective-permute-start(bf16[104,256]{1,0:T(8,128)(2,1)S(1)} %piece_sum.1.refs_0_), channel_id=1, source_target_pairs={{0,4},{4,0},{8,12},{12,8},{16,20},{20,16},{24,28},{28,24},{1,5},{5... | collective-permute-start | bytes 159752 | tf_op jit(solution)/shard_map/ppermute | solution.py:562
  54.0 1.7 %collective-permute-start.16 = (bf16[104,256]{1,0:T(8,128)(2,1)S(1)}, bf16[104,256]{1,0:T(8,128)(2,1)S(1)}, u32[]{:S(2)}, u32[]{:S(2)}) collective-permute-start(bf16[104,256]{1,0:T(8,128)(2,1)S(1)} %piece_sum.1.refs_0_), channel_id=1, source_target_pairs={{0,16},{4,20},{8,24},{12,28},{16,0},{20,4},{24,8},{28,12},{1,17},{... | collective-permute-start | bytes 159752 | tf_op jit(solution)/shard_map/ppermute | solution.py:562
  55.7 1.7 %collective-permute-start.18 = (bf16[104,256]{1,0:T(8,128)(2,1)S(1)}, bf16[104,256]{1,0:T(8,128)(2,1)S(1)}, u32[]{:S(2)}, u32[]{:S(2)}) collective-permute-start(bf16[104,256]{1,0:T(8,128)(2,1)S(1)} %piece_sum.1.refs_0_), channel_id=1, source_target_pairs={{0,8},{4,12},{8,0},{12,4},{16,24},{20,28},{24,16},{28,20},{1,9},{5... | collective-permute-start | bytes 159752 | tf_op jit(solution)/shard_map/ppermute | solution.py:562
  57.4 0.1 collective-permute-done.17.refs_1_
  57.5 1.5 %collective-permute-done.16.refs_4_ = bf16[104,256]{1,0:T(8,128)(2,1)S(1)} collective-permute-done((bf16[104,256]{1,0:T(8,128)(2,1)S(1)}, bf16[104,256]{1,0:T(8,128)(2,1)S(1)}, u32[]{:S(2)}, u32[]{:S(2)}) %collective-permute-start.16) | collective-permute-done | bytes 53280 | tf_op jit(solution)/shard_map/ppermute | solution.py:562
  59.0 1.3 %collective-permute-start.21 = (bf16[104,256]{1,0:T(8,128)(2,1)S(1)}, bf16[104,256]{1,0:T(8,128)(2,1)S(1)}, u32[]{:S(2)}, u32[]{:S(2)}) collective-permute-start(bf16[104,256]{1,0:T(8,128)(2,1)S(1)} %collective-permute-done.16.refs_4_), channel_id=1, source_target_pairs={{0,8},{4,12},{8,0},{12,4},{16,24},{20,28},{24,16},{28,20},{1,9},{5... | collective-permute-start | bytes 159752 | tf_op jit(solution)/shard_map/ppermute | solution.py:562
  60.3 1.1 %collective-permute-start.20 = (bf16[104,256]{1,0:T(8,128)(2,1)S(1)}, bf16[104,256]{1,0:T(8,128)(2,1)S(1)}, u32[]{:S(2)}, u32[]{:S(2)}) collective-permute-start(bf16[104,256]{1,0:T(8,128)(2,1)S(1)} %collective-permute-done.16.refs_4_), channel_id=1, source_target_pairs={{0,4},{4,0},{8,12},{12,8},{16,20},{20,16},{24,28},{28,24},{1,5},{5... | collective-permute-start | bytes 159752 | tf_op jit(solution)/shard_map/ppermute | solution.py:562
  61.3 1.0 %collective-permute-start.19 = (bf16[104,256]{1,0:T(8,128)(2,1)S(1)}, bf16[104,256]{1,0:T(8,128)(2,1)S(1)}, u32[]{:S(2)}, u32[]{:S(2)}) collective-permute-start(bf16[104,256]{1,0:T(8,128)(2,1)S(1)} %collective-permute-done.18.refs_2_), channel_id=1, source_target_pairs={{0,4},{4,0},{8,12},{12,8},{16,20},{20,16},{24,28},{28,24},{1,5},{5... | collective-permute-start | bytes 159752 | tf_op jit(solution)/shard_map/ppermute | solution.py:562
  62.3 0.8 %collective-permute-done.21.refs_6_ = bf16[104,256]{1,0:T(8,128)(2,1)S(1)} collective-permute-done((bf16[104,256]{1,0:T(8,128)(2,1)S(1)}, bf16[104,256]{1,0:T(8,128)(2,1)S(1)}, u32[]{:S(2)}, u32[]{:S(2)}) %collective-permute-start.21) | collective-permute-done | bytes 53280 | tf_op jit(solution)/shard_map/ppermute | solution.py:562
  63.1 1.0 %collective-permute-start.22 = (bf16[104,256]{1,0:T(8,128)(2,1)S(1)}, bf16[104,256]{1,0:T(8,128)(2,1)S(1)}, u32[]{:S(2)}, u32[]{:S(2)}) collective-permute-start(bf16[104,256]{1,0:T(8,128)(2,1)S(1)} %collective-permute-done.21.refs_6_), channel_id=1, source_target_pairs={{0,4},{4,0},{8,12},{12,8},{16,20},{20,16},{24,28},{28,24},{1,5},{5... | collective-permute-start | bytes 159752 | tf_op jit(solution)/shard_map/ppermute | solution.py:562
  64.1 1.4 %collective-permute-done.19.refs_3_ = bf16[104,256]{1,0:T(8,128)(2,1)S(1)} collective-permute-done((bf16[104,256]{1,0:T(8,128)(2,1)S(1)}, bf16[104,256]{1,0:T(8,128)(2,1)S(1)}, u32[]{:S(2)}, u32[]{:S(2)}) %collective-permute-start.19) | collective-permute-done | bytes 53280 | tf_op jit(solution)/shard_map/ppermute | solution.py:562
  65.5 1.8 %collective-permute-done.22.refs_7_ = bf16[104,256]{1,0:T(8,128)(2,1)S(1)} collective-permute-done((bf16[104,256]{1,0:T(8,128)(2,1)S(1)}, bf16[104,256]{1,0:T(8,128)(2,1)S(1)}, u32[]{:S(2)}, u32[]{:S(2)}) %collective-permute-start.22) | collective-permute-done | bytes 53280 | tf_op jit(solution)/shard_map/ppermute | solution.py:562
  67.4 1.8 %adam.1 = (f32[64,768]{1,0:T(8,128)}, f32[64,768]{1,0:T(8,128)}, f32[64,768]{1,0:T(8,128)}, f32[64,256]{1,0:T(8,128)}, f32[64,256]{1,0:T(8,128)}, /*index=5*/f32...) custom-call(bf16[104,256]{1,0:T(8,128)(2,1)S(1)} %piece_sum.1.refs_0, ...), custom_call_target="tpu_custom_call" | custom-call | bytes 5163008 | tf_op jit(solution)/shard_map/adam/pallas_call | solution.py:548
  (57 shorter events, 0.3 us)
Async XLA Ops:
  0.7 6.7 %copy-start.6 = (bf16[512,256]{1,0:T(8,128)(2,1)S(1)}, bf16[512,256]{1,0:T(8,128)(2,1)}, u32[]{:S(2)}) copy-start(bf16[512,256]{1,0:T(8,128)(2,1)} %refs_0_.1) | copy-start | bytes 786436
  0.7 6.7 %copy-start.20 = (s32[128]{0:T(128)S(1)}, s32[128]{0:T(128)}, u32[]{:S(2)}) copy-start(s32[128]{0:T(128)} %param.22) | copy-start | bytes 1540
  0.7 6.7 %copy-start.19 = (s32[128]{0:T(128)S(1)}, s32[128]{0:T(128)}, u32[]{:S(2)}) copy-start(s32[128]{0:T(128)} %param.21) | copy-start | bytes 1540
  0.7 6.7 %copy-start.5 = (bf16[512,256]{1,0:T(8,128)(2,1)S(1)}, bf16[512,256]{1,0:T(8,128)(2,1)}, u32[]{:S(2)}) copy-start(bf16[512,256]{1,0:T(8,128)(2,1)} %seed_ref.1) | copy-start | bytes 786436
  2.4 7.5 %copy-start.13 = (bf16[208,256]{1,0:T(8,128)(2,1)S(1)}, bf16[208,256]{1,0:T(8,128)(2,1)}, u32[]{:S(2)}) copy-start(bf16[208,256]{1,0:T(8,128)(2,1)} %pack_first.1.refs_2_.refs_3_.refs_12_) | copy-start | bytes 319492
  2.4 6.2 %collective-permute-start = (bf16[208,256]{1,0:T(8,128)(2,1)}, bf16[208,256]{1,0:T(8,128)(2,1)S(1)}, u32[]{:S(2)}, u32[]{:S(2)}) collective-permute-start(bf16[208,256]{1,0:T(8,128)(2,1)} %pack_first.1.refs_2_.refs_3_.refs_12_), channel_id=1, source_target_pairs={{0,2},{1,3},{2,0},{3,1},{4,6},{5,7},{6,4},{7,5},{8,10},{9,11},{10,... | collective-permute-start | bytes 319496 | tf_op jit(solution)/shard_map/ppermute | solution.py:562
  7.2 8.7 %collective-permute-start.3 = (bf16[576,256]{1,0:T(8,128)(2,1)}, bf16[576,256]{1,0:T(8,128)(2,1)S(1)}, u32[]{:S(2)}, u32[]{:S(2)}) collective-permute-start(bf16[576,256]{1,0:T(8,128)(2,1)} %pack_second.1.refs_7_), channel_id=1, source_target_pairs={{0,2},{1,3},{2,0},{3,1},{4,6},{5,7},{6,4},{7,5},{8,10},{9,11},{10,... | collective-permute-start | bytes 884744 | tf_op jit(solution)/shard_map/ppermute | solution.py:562
  7.3 1.8 %collective-permute-start.1 = (bf16[208,256]{1,0:T(8,128)(2,1)}, bf16[208,256]{1,0:T(8,128)(2,1)S(1)}, u32[]{:S(2)}, u32[]{:S(2)}) collective-permute-start(bf16[208,256]{1,0:T(8,128)(2,1)} %pack_first.1.refs_2_.refs_3_.refs_12_), channel_id=1, source_target_pairs={{0,1},{1,0},{2,3},{3,2},{4,5},{5,4},{6,7},{7,6},{8,9},{9,8},{10,11... | collective-permute-start | bytes 319496 | tf_op jit(solution)/shard_map/ppermute | solution.py:562
  8.6 9.0 %copy-start.3 = (bf16[576,256]{1,0:T(8,128)(2,1)S(1)}, bf16[576,256]{1,0:T(8,128)(2,1)}, u32[]{:S(2)}) copy-start(bf16[576,256]{1,0:T(8,128)(2,1)} %pack_second.1.refs_7_) | copy-start | bytes 884740
  8.6 1.3 %collective-permute-start.2 = (bf16[208,256]{1,0:T(8,128)(2,1)S(1)}, bf16[208,256]{1,0:T(8,128)(2,1)S(1)}, u32[]{:S(2)}, u32[]{:S(2)}) collective-permute-start(bf16[208,256]{1,0:T(8,128)(2,1)S(1)} %collective-permute-done.refs_4_.refs_5_.refs_14_), channel_id=1, source_target_pairs={{0,1},{1,0},{2,3},{3,2},{4,5},{5,4},{6,7},{7,6},{8,9},{9,8},{10,11... | collective-permute-start | bytes 319496 | tf_op jit(solution)/shard_map/ppermute | solution.py:562
  8.7 7.3 %collective-permute-start.4 = (bf16[576,256]{1,0:T(8,128)(2,1)}, bf16[576,256]{1,0:T(8,128)(2,1)S(1)}, u32[]{:S(2)}, u32[]{:S(2)}) collective-permute-start(bf16[576,256]{1,0:T(8,128)(2,1)} %pack_second.1.refs_7_), channel_id=1, source_target_pairs={{0,1},{1,0},{2,3},{3,2},{4,5},{5,4},{6,7},{7,6},{8,9},{9,8},{10,11... | collective-permute-start | bytes 884744 | tf_op jit(solution)/shard_map/ppermute | solution.py:562
  16.0 1.6 %collective-permute-start.5 = (bf16[576,256]{1,0:T(8,128)(2,1)S(1)}, bf16[576,256]{1,0:T(8,128)(2,1)S(1)}, u32[]{:S(2)}, u32[]{:S(2)}) collective-permute-start(bf16[576,256]{1,0:T(8,128)(2,1)S(1)} %collective-permute-done.3.refs_9_), channel_id=1, source_target_pairs={{0,1},{1,0},{2,3},{3,2},{4,5},{5,4},{6,7},{7,6},{8,9},{9,8},{10,11... | collective-permute-start | bytes 884744 | tf_op jit(solution)/shard_map/ppermute | solution.py:562
  21.5 2.0 %collective-permute-start.6 = (bf16[2,576,256]{2,1,0:T(8,128)(2,1)S(1)}, bf16[2,576,256]{2,1,0:T(8,128)(2,1)S(1)}, u32[]{:S(2)}, u32[]{:S(2)}) collective-permute-start(bf16[2,576,256]{2,1,0:T(8,128)(2,1)S(1)} %get-tuple-element.110), channel_id=1, source_target_pairs={{0,1},{1,0},{2,3},{3,2},{4,5},{5,4},{6,7},{7,6},{8,9},{9,8},{10,11... | collective-permute-start | bytes 1769480 | tf_op jit(solution)/shard_map/ppermute | solution.py:562
  23.6 9.2 %collective-permute-start.8 = (bf16[1,576,256]{2,1,0:T(8,128)(2,1)S(1)}, bf16[1,576,256]{2,1,0:T(8,128)(2,1)S(1)}, u32[]{:S(2)}, u32[]{:S(2)}) collective-permute-start(bf16[1,576,256]{2,1,0:T(8,128)(2,1)S(1)} %get-tuple-element.126), channel_id=1, source_target_pairs={{0,2},{1,3},{2,0},{3,1},{4,6},{5,7},{6,4},{7,5},{8,10},{9,11},{10,... | collective-permute-start | bytes 884744 | tf_op jit(solution)/shard_map/ppermute | solution.py:562
  28.8 1.5 %collective-permute-start.7 = (bf16[2,200,256]{2,1,0:T(8,128)(2,1)S(1)}, bf16[2,200,256]{2,1,0:T(8,128)(2,1)S(1)}, u32[]{:S(2)}, u32[]{:S(2)}) collective-permute-start(bf16[2,200,256]{2,1,0:T(8,128)(2,1)S(1)} %get-tuple-element.124), channel_id=1, source_target_pairs={{0,1},{1,0},{2,3},{3,2},{4,5},{5,4},{6,7},{7,6},{8,9},{9,8},{10,11... | collective-permute-start | bytes 614408 | tf_op jit(solution)/shard_map/ppermute | solution.py:562
  32.8 34.4 %copy-start = (f32[64,1024]{1,0:T(8,128)S(1)}, f32[64,1024]{1,0:T(8,128)}, u32[]{:S(2)}) copy-start(f32[64,1024]{1,0:T(8,128)} %refs_14_.1) | copy-start | bytes 786436
  32.8 34.4 %copy-start.1 = (f32[256,256]{1,0:T(8,128)S(1)}, f32[256,256]{1,0:T(8,128)}, u32[]{:S(2)}) copy-start(f32[256,256]{1,0:T(8,128)} %refs_17_.1) | copy-start | bytes 786436
  32.8 34.4 %copy-start.2 = (f32[64,768]{1,0:T(8,128)S(1)}, f32[64,768]{1,0:T(8,128)}, u32[]{:S(2)}) copy-start(f32[64,768]{1,0:T(8,128)} %refs_8_.1) | copy-start | bytes 589828
  32.8 34.4 %copy-start.4 = (f32[64,256]{1,0:T(8,128)S(1)}, f32[64,256]{1,0:T(8,128)}, u32[]{:S(2)}) copy-start(f32[64,256]{1,0:T(8,128)} %refs_11_.1) | copy-start | bytes 196612
  32.8 34.4 %copy-start.7 = (f32[64,1024]{1,0:T(8,128)S(1)}, f32[64,1024]{1,0:T(8,128)}, u32[]{:S(2)}) copy-start(f32[64,1024]{1,0:T(8,128)} %refs_15_.1) | copy-start | bytes 786436
  32.8 34.4 %copy-start.8 = (f32[64,1024]{1,0:T(8,128)S(1)}, f32[64,1024]{1,0:T(8,128)}, u32[]{:S(2)}) copy-start(f32[64,1024]{1,0:T(8,128)} %refs_16_.1) | copy-start | bytes 786436
  32.9 34.4 %copy-start.9 = (f32[256,256]{1,0:T(8,128)S(1)}, f32[256,256]{1,0:T(8,128)}, u32[]{:S(2)}) copy-start(f32[256,256]{1,0:T(8,128)} %refs_18_.1) | copy-start | bytes 786436
  32.9 34.4 %copy-start.10 = (f32[256,256]{1,0:T(8,128)S(1)}, f32[256,256]{1,0:T(8,128)}, u32[]{:S(2)}) copy-start(f32[256,256]{1,0:T(8,128)} %refs_19_.1) | copy-start | bytes 786436
  32.9 34.4 %copy-start.11 = (f32[64,768]{1,0:T(8,128)S(1)}, f32[64,768]{1,0:T(8,128)}, u32[]{:S(2)}) copy-start(f32[64,768]{1,0:T(8,128)} %refs_9_.1) | copy-start | bytes 589828
  32.9 34.4 %copy-start.12 = (f32[64,768]{1,0:T(8,128)S(1)}, f32[64,768]{1,0:T(8,128)}, u32[]{:S(2)}) copy-start(f32[64,768]{1,0:T(8,128)} %refs_10_.1) | copy-start | bytes 589828
  32.9 34.4 %copy-start.14 = (f32[64,256]{1,0:T(8,128)S(1)}, f32[64,256]{1,0:T(8,128)}, u32[]{:S(2)}) copy-start(f32[64,256]{1,0:T(8,128)} %refs_12_.1) | copy-start | bytes 196612
  32.9 34.4 %copy-start.15 = (f32[64,256]{1,0:T(8,128)S(1)}, f32[64,256]{1,0:T(8,128)}, u32[]{:S(2)}) copy-start(f32[64,256]{1,0:T(8,128)} %refs_13_.1) | copy-start | bytes 196612
  32.9 34.4 %copy-start.16 = (f32[768]{0:T(1024)S(1)}, f32[768]{0:T(1024)}, u32[]{:S(2)}) copy-start(f32[768]{0:T(1024)} %refs_20_.1) | copy-start | bytes 9220
  32.9 34.4 %copy-start.17 = (f32[768]{0:T(1024)S(1)}, f32[768]{0:T(1024)}, u32[]{:S(2)}) copy-start(f32[768]{0:T(1024)} %refs_21_.1) | copy-start | bytes 9220
  33.0 34.4 %copy-start.18 = (f32[768]{0:T(1024)S(1)}, f32[768]{0:T(1024)}, u32[]{:S(2)}) copy-start(f32[768]{0:T(1024)} %refs_22_.1) | copy-start | bytes 9220
  33.1 6.9 %collective-permute-start.9 = (bf16[4,72,256]{2,1,0:T(8,128)(2,1)S(1)}, bf16[4,72,256]{2,1,0:T(8,128)(2,1)S(1)}, u32[]{:S(2)}, u32[]{:S(2)}) collective-permute-start(bf16[4,72,256]{2,1,0:T(8,128)(2,1)S(1)} %get-tuple-element.129), channel_id=1, source_target_pairs={{0,4},{4,0},{8,12},{12,8},{16,20},{20,16},{24,28},{28,24},{1,5},{5... | collective-permute-start | bytes 442376 | tf_op jit(solution)/shard_map/ppermute | solution.py:562
  34.7 4.7 %collective-permute-start.12 = (bf16[1,200,256]{2,1,0:T(8,128)(2,1)S(1)}, bf16[1,200,256]{2,1,0:T(8,128)(2,1)S(1)}, u32[]{:S(2)}, u32[]{:S(2)}) collective-permute-start(bf16[1,200,256]{2,1,0:T(8,128)(2,1)S(1)} %get-tuple-element.135), channel_id=1, source_target_pairs={{0,2},{1,3},{2,0},{3,1},{4,6},{5,7},{6,4},{7,5},{8,10},{9,11},{10,... | collective-permute-start | bytes 307208 | tf_op jit(solution)/shard_map/ppermute | solution.py:562
  39.4 4.3 %collective-permute-start.13 = (bf16[4,32,256]{2,1,0:T(8,128)(2,1)S(1)}, bf16[4,32,256]{2,1,0:T(8,128)(2,1)S(1)}, u32[]{:S(2)}, u32[]{:S(2)}) collective-permute-start(bf16[4,32,256]{2,1,0:T(8,128)(2,1)S(1)} %get-tuple-element.137), channel_id=1, source_target_pairs={{0,4},{4,0},{8,12},{12,8},{16,20},{20,16},{24,28},{28,24},{1,5},{5... | collective-permute-start | bytes 196616 | tf_op jit(solution)/shard_map/ppermute | solution.py:562
  40.0 5.4 %collective-permute-start.10 = (bf16[2,72,256]{2,1,0:T(8,128)(2,1)S(1)}, bf16[2,72,256]{2,1,0:T(8,128)(2,1)S(1)}, u32[]{:S(2)}, u32[]{:S(2)}) collective-permute-start(bf16[2,72,256]{2,1,0:T(8,128)(2,1)S(1)} %get-tuple-element.131), channel_id=1, source_target_pairs={{0,8},{4,12},{8,0},{12,4},{16,24},{20,28},{24,16},{28,20},{1,9},{5... | collective-permute-start | bytes 221192 | tf_op jit(solution)/shard_map/ppermute | solution.py:562
  43.7 4.3 %collective-permute-start.14 = (bf16[2,32,256]{2,1,0:T(8,128)(2,1)S(1)}, bf16[2,32,256]{2,1,0:T(8,128)(2,1)S(1)}, u32[]{:S(2)}, u32[]{:S(2)}) collective-permute-start(bf16[2,32,256]{2,1,0:T(8,128)(2,1)S(1)} %get-tuple-element.139), channel_id=1, source_target_pairs={{0,8},{4,12},{8,0},{12,4},{16,24},{20,28},{24,16},{28,20},{1,9},{5... | collective-permute-start | bytes 98312 | tf_op jit(solution)/shard_map/ppermute | solution.py:562
  45.4 7.4 %collective-permute-start.11 = (bf16[1,72,256]{2,1,0:T(8,128)(2,1)S(1)}, bf16[1,72,256]{2,1,0:T(8,128)(2,1)S(1)}, u32[]{:S(2)}, u32[]{:S(2)}) collective-permute-start(bf16[1,72,256]{2,1,0:T(8,128)(2,1)S(1)} %get-tuple-element.133), channel_id=1, source_target_pairs={{0,16},{4,20},{8,24},{12,28},{16,0},{20,4},{24,8},{28,12},{1,17},{... | collective-permute-start | bytes 110600 | tf_op jit(solution)/shard_map/ppermute | solution.py:562
  48.1 4.8 %collective-permute-start.15 = (bf16[1,32,256]{2,1,0:T(8,128)(2,1)S(1)}, bf16[1,32,256]{2,1,0:T(8,128)(2,1)S(1)}, u32[]{:S(2)}, u32[]{:S(2)}) collective-permute-start(bf16[1,32,256]{2,1,0:T(8,128)(2,1)S(1)} %get-tuple-element.141), channel_id=1, source_target_pairs={{0,16},{4,20},{8,24},{12,28},{16,0},{20,4},{24,8},{28,12},{1,17},{... | collective-permute-start | bytes 49160 | tf_op jit(solution)/shard_map/ppermute | solution.py:562
  52.8 4.6 %collective-permute-start.17 = (bf16[104,256]{1,0:T(8,128)(2,1)S(1)}, bf16[104,256]{1,0:T(8,128)(2,1)S(1)}, u32[]{:S(2)}, u32[]{:S(2)}) collective-permute-start(bf16[104,256]{1,0:T(8,128)(2,1)S(1)} %piece_sum.1.refs_0_), channel_id=1, source_target_pairs={{0,4},{4,0},{8,12},{12,8},{16,20},{20,16},{24,28},{28,24},{1,5},{5... | collective-permute-start | bytes 159752 | tf_op jit(solution)/shard_map/ppermute | solution.py:562
  54.0 5.0 %collective-permute-start.16 = (bf16[104,256]{1,0:T(8,128)(2,1)S(1)}, bf16[104,256]{1,0:T(8,128)(2,1)S(1)}, u32[]{:S(2)}, u32[]{:S(2)}) collective-permute-start(bf16[104,256]{1,0:T(8,128)(2,1)S(1)} %piece_sum.1.refs_0_), channel_id=1, source_target_pairs={{0,16},{4,20},{8,24},{12,28},{16,0},{20,4},{24,8},{28,12},{1,17},{... | collective-permute-start | bytes 159752 | tf_op jit(solution)/shard_map/ppermute | solution.py:562
  55.7 5.6 %collective-permute-start.18 = (bf16[104,256]{1,0:T(8,128)(2,1)S(1)}, bf16[104,256]{1,0:T(8,128)(2,1)S(1)}, u32[]{:S(2)}, u32[]{:S(2)}) collective-permute-start(bf16[104,256]{1,0:T(8,128)(2,1)S(1)} %piece_sum.1.refs_0_), channel_id=1, source_target_pairs={{0,8},{4,12},{8,0},{12,4},{16,24},{20,28},{24,16},{28,20},{1,9},{5... | collective-permute-start | bytes 159752 | tf_op jit(solution)/shard_map/ppermute | solution.py:562
  59.0 4.1 %collective-permute-start.21 = (bf16[104,256]{1,0:T(8,128)(2,1)S(1)}, bf16[104,256]{1,0:T(8,128)(2,1)S(1)}, u32[]{:S(2)}, u32[]{:S(2)}) collective-permute-start(bf16[104,256]{1,0:T(8,128)(2,1)S(1)} %collective-permute-done.16.refs_4_), channel_id=1, source_target_pairs={{0,8},{4,12},{8,0},{12,4},{16,24},{20,28},{24,16},{28,20},{1,9},{5... | collective-permute-start | bytes 159752 | tf_op jit(solution)/shard_map/ppermute | solution.py:562
  60.3 5.2 %collective-permute-start.20 = (bf16[104,256]{1,0:T(8,128)(2,1)S(1)}, bf16[104,256]{1,0:T(8,128)(2,1)S(1)}, u32[]{:S(2)}, u32[]{:S(2)}) collective-permute-start(bf16[104,256]{1,0:T(8,128)(2,1)S(1)} %collective-permute-done.16.refs_4_), channel_id=1, source_target_pairs={{0,4},{4,0},{8,12},{12,8},{16,20},{20,16},{24,28},{28,24},{1,5},{5... | collective-permute-start | bytes 159752 | tf_op jit(solution)/shard_map/ppermute | solution.py:562
  61.3 4.1 %collective-permute-start.19 = (bf16[104,256]{1,0:T(8,128)(2,1)S(1)}, bf16[104,256]{1,0:T(8,128)(2,1)S(1)}, u32[]{:S(2)}, u32[]{:S(2)}) collective-permute-start(bf16[104,256]{1,0:T(8,128)(2,1)S(1)} %collective-permute-done.18.refs_2_), channel_id=1, source_target_pairs={{0,4},{4,0},{8,12},{12,8},{16,20},{20,16},{24,28},{28,24},{1,5},{5... | collective-permute-start | bytes 159752 | tf_op jit(solution)/shard_map/ppermute | solution.py:562
  63.1 4.1 %collective-permute-start.22 = (bf16[104,256]{1,0:T(8,128)(2,1)S(1)}, bf16[104,256]{1,0:T(8,128)(2,1)S(1)}, u32[]{:S(2)}, u32[]{:S(2)}) collective-permute-start(bf16[104,256]{1,0:T(8,128)(2,1)S(1)} %collective-permute-done.21.refs_6_), channel_id=1, source_target_pairs={{0,4},{4,0},{8,12},{12,8},{16,20},{20,16},{24,28},{28,24},{1,5},{5... | collective-permute-start | bytes 159752 | tf_op jit(solution)/shard_map/ppermute | solution.py:562

commit v10 on v9

--- a/solution.py
+++ b/solution.py
@@ -234,13 +234,13 @@
     out_ref[...] = att_ref[...].astype(low).T
 
 
-def feed_kernel(shards, *refs):
+def feed_first_kernel(shards, *refs):
     x_ref, att_ref, seed_ref = refs[:3]
     firsts = refs[3 : 3 + shards]
     pieces = refs[3 + shards : 3 + 2 * shards]
     refs = refs[3 + 2 * shards :]
-    out_ref, middle_ref, dattend_ref, sums_ref, keep_ref, send_ref = refs[:6]
-    small_ref, out_w, up_w, down_w, grads_ref = refs[6:]
+    act_ref, base_ref, dhidden_ref, norm_ref, root_ref, out_w, down_w, sums_ref = refs[:8]
+    keep_ref, send_ref, small_ref, up_w, grads_ref = refs[8:]
     rows, width = x_ref.shape
     hidden_count = up_w.shape[1]
     shard = lax.axis_index("shard")
@@ -255,13 +255,13 @@
     bias_out, bias_down = small_ref[2, 0:1, :], small_ref[2, 1:2, :]
     bias_up = [small_ref[2, 2:3, :]] + [small_ref[3, row : row + 1, :] for row in range(3)]
     seed_low = seed_ref[...]
-    seed = seed_low.astype(wide)
-    attended = att_ref[...]
-    middle = x_ref[...].astype(wide) + (dot_nn(attended, out_w[...]) + bias_out)
+    middle = x_ref[...].astype(wide) + (dot_nn(att_ref[...], out_w[...]) + bias_out)
+    base_ref[...] = middle + bias_down
     normed, root = standardize(middle)
+    norm_ref[...] = normed
+    root_ref[...] = root
     hidden = (normed * gain + shift).astype(low)
     hidden_t = hidden.T
-    result = middle + bias_down
     dhidden = jnp.zeros((rows, width), wide)
     sums_ref[...] = jnp.zeros(sums_ref.shape, wide)
 
@@ -287,34 +287,48 @@
             dpre.append((dact[at : at + CHUNK] * slope).astype(low))
         act = jnp.concatenate(act, axis=0)
         dpre = jnp.concatenate(dpre, axis=0)
-        result = result + dot_nn(act, down_w[cols, :])
+        act_ref[:, cols] = act
         dhidden = dhidden + dot_nt(dpre, up_w[:, cols])
         grad_down = dot_nn(act.T, seed_low)
         grad_up = dot_nn(hidden_t, dpre)
         for piece in range(width // down_part):
             target = block * (width // down_part) + piece
-            at = part + blocks * part
-            grads_ref[target, at : at + down_part, :] = grad_down[
+            grads_ref[target, :down_part, :] = grad_down[
                 piece * down_part : (piece + 1) * down_part, :
             ]
         for target in range(shards):
-            at = part + block * part
+            at = down_part + block * part
             grads_ref[target, at : at + part, :] = grad_up[target * part : (target + 1) * part, :]
         sums_ref[4 + block : 5 + block, :] = jnp.sum(dpre.astype(wide), axis=0, keepdims=True)
-    out_ref[...] = result.astype(low)
-    through, gain_grad, shift_grad = norm_back(dhidden, normed, root, gain)
+    dhidden_ref[...] = dhidden
+    part_ways(grads_ref, keep_ref, send_ref, shard & 1)
+
+
+def output_kernel(base_ref, act_ref, down_w, out_ref):
+    out_ref[...] = (base_ref[...] + dot_nn(act_ref[...], down_w[...])).astype(low)
+
+
+def feed_last_kernel(shards, *refs):
+    att_ref, seed_ref, dhidden_ref, norm_ref, root_ref, out_w, sums_in = refs[:7]
+    firsts = refs[7 : 7 + shards]
+    middle_ref, dattend_ref, grad_ref, sums_ref, small_ref = refs[7 + shards :]
+    rows, width = norm_ref.shape
+    shard = lax.axis_index("shard")
+    fill_small(small_ref, shard, firsts, 3 * (width // shards))
+    seed = seed_ref[...].astype(wide)
+    through, gain_grad, shift_grad = norm_back(
+        dhidden_ref[...], norm_ref[...], root_ref[...], small_ref[0, 2:3, :]
+    )
     dmiddle = seed + through
     middle_ref[...] = dmiddle
     dmiddle_low = dmiddle.astype(low)
-    grad_out = dot_nn(attended.T, dmiddle_low)
-    for target in range(shards):
-        grads_ref[target, :part, :] = grad_out[target * part : (target + 1) * part, :]
     dattend_ref[...] = dot_nt(dmiddle_low, out_w[...]).astype(low)
+    grad_ref[...] = dot_nn(att_ref[...].T, dmiddle_low)
+    sums_ref[...] = sums_in[...]
     sums_ref[0:1, :] = gain_grad
     sums_ref[1:2, :] = shift_grad
     sums_ref[2:3, :] = jnp.sum(dmiddle_low.astype(wide), axis=0, keepdims=True)
     sums_ref[3:4, :] = jnp.sum(seed, axis=0, keepdims=True)
-    part_ways(grads_ref, keep_ref, send_ref, shard & 1)
 
 
 def part_ways(grads_ref, keep_ref, send_ref, side):
@@ -372,20 +386,11 @@
         dkey[:stop, :] += dot_nn(dscores, query)
 
 
-def back_first_kernel(heads, *refs):
-    dquery_t, dkey, dvalue = refs[5:8]
-    dkey[...] = jnp.zeros(dkey.shape, wide)
-    dvalue[...] = jnp.zeros(dvalue.shape, wide)
-    dquery_t[...] = jnp.zeros(dquery_t.shape, low)
-    back_heads(heads, *refs)
-
-
-def back_last_kernel(shards, head_groups, *refs):
+def back_kernel(shards, *refs):
     shared = refs[:5]
-    earlier = refs[5:8]
-    norm_ref, root_ref, middle_ref, sums_in = refs[8:12]
-    pieces = refs[12 : 12 + shards]
-    refs = refs[12 + shards :]
+    norm_ref, root_ref, middle_ref, sums_in, grad_out = refs[5:10]
+    pieces = refs[10 : 10 + shards]
+    refs = refs[10 + shards :]
     dx_ref, keep_ref, send_ref = refs[:3]
     weight_ref, small_ref, dquery_t, dkey, dvalue, djoined, grads_ref = refs[3:]
     rows, width = norm_ref.shape
@@ -394,18 +399,16 @@
     fill_cols(weight_ref, shard, pieces, 0, part, width)
     fill_small(small_ref, shard, pieces, 3 * part)
     gain, shift = small_ref[0, 0:1, :], small_ref[0, 1:2, :]
-    for target, value in zip((dquery_t, dkey, dvalue), earlier):
-        target[...] = value[...]
-    for heads in head_groups:
+    per_tile = LANES // HEAD
+    for first in range(0, width, LANES):
+        dkey[...] = jnp.zeros(dkey.shape, wide)
+        dvalue[...] = jnp.zeros(dvalue.shape, wide)
+        heads = range(first // HEAD, first // HEAD + per_tile)
         back_heads(heads, *shared, dquery_t, dkey, dvalue)
-        if (heads[-1] + 1) * HEAD % LANES == 0:
-            first = (heads[-1] + 1) * HEAD - LANES
-            values = (dquery_t[...].T, dkey[...] * score_scale, dvalue[...])
-            for block, value in enumerate(values):
-                at = block * width + first
-                djoined[:, at : at + LANES] = value.astype(low)
-            dkey[...] = jnp.zeros(dkey.shape, wide)
-            dvalue[...] = jnp.zeros(dvalue.shape, wide)
+        values = (dquery_t[...].T, dkey[...] * score_scale, dvalue[...])
+        for block, value in enumerate(values):
+            at = block * width + first
+            djoined[:, at : at + LANES] = value.astype(low)
     normed, root = norm_ref[...], root_ref[...]
     hidden_t = (normed * gain + shift).astype(low).T
     dhidden = jnp.zeros((rows, width), wide)
@@ -426,25 +429,25 @@
     sums = [gain_grad, shift_grad, sums_in[0:1, :], sums_in[1:2, :]] + bias_sums
     sums += [sums_in[row : row + 1, :] for row in range(2, 8)]
     per_shard = len(sums) // shards
-    empty = [jnp.zeros((grads_ref.shape[1] - 3 * part - per_shard, width), wide)]
+    body = 4 * part
+    empty = [jnp.zeros((grads_ref.shape[1] - body - per_shard, width), wide)]
     for target in range(shards):
         rows_here = sums[target * per_shard : (target + 1) * per_shard]
-        grads_ref[target, 3 * part :, :] = jnp.concatenate(rows_here + empty, axis=0)
+        grads_ref[target, 3 * part : body, :] = grad_out[target * part : (target + 1) * part, :]
+        grads_ref[target, body:, :] = jnp.concatenate(rows_here + empty, axis=0)
     part_ways(grads_ref, keep_ref, send_ref, shard & 1)
 
 
-def halve_kernel(axis, bit, *refs):
-    count = (len(refs) - 2) // 2
-    keep_ref, send_ref = refs[-2:]
+def halve_kernel(axis, bit, counts, kept, arrived, *outs):
     side = (lax.axis_index(axis) >> bit) & 1
-    for pair in range(keep_ref.shape[0]):
-        for target, index in ((keep_ref, 2 * pair + side), (send_ref, 2 * pair + 1 - side)):
-            parts = []
-            for chunk in range(count):
-                kept, arrived = refs[2 * chunk : 2 * chunk + 2]
-                parts.append(kept[index] + arrived[index].astype(wide))
-            value = parts[0] if count == 1 else jnp.concatenate(parts, axis=0)
-            target[pair] = value.astype(target.dtype)
+    for pair in range(outs[0].shape[0]):
+        mine = kept[2 * pair + side] + arrived[2 * pair + side].astype(wide)
+        other = kept[2 * pair + 1 - side] + arrived[2 * pair + 1 - side].astype(wide)
+        row = 0
+        for chunk, count in enumerate(counts):
+            outs[2 * chunk][pair] = mine[row : row + count]
+            outs[2 * chunk + 1][pair] = other[row : row + count].astype(low)
+            row += count
 
 
 def piece_spans(total, tail, group):
@@ -578,12 +581,15 @@
     return [found[offset] for offset in range(group)]
 
 
-def halve_call(axis, bit, flat, name):
-    half, _, width = flat[0].shape
-    shape = (half // 2, sum(item.shape[1] for item in flat[::2]), width)
-    return local_call(
-        functools.partial(halve_kernel, axis, bit), [(shape, wide), (shape, low)], flat, name=name
-    )
+def halve_call(axis, bit, kept, arrived, name, counts=None):
+    half, rows, width = kept.shape
+    counts = counts or [rows]
+    outs = []
+    for count in counts:
+        shape = (half // 2, count, width)
+        outs += [(shape, wide), (shape, low)]
+    kernel = functools.partial(halve_kernel, axis, bit, counts)
+    return local_call(kernel, outs, [kept, arrived], name=name)
 
 
 def split_chunk(chunk, tail, group):
@@ -599,20 +605,28 @@
     return keep, exchange(send, "dp", 1)
 
 
-def near_sum(flat):
-    half = flat[0].shape[0]
+def after_arrivals(early, arrival):
+    ready, arrival = lax.optimization_barrier(([flat[1] for flat in early], arrival))
+    return [[flat[0], item] for flat, item in zip(early, ready)], arrival
+
+
+def next_sum(flat, bit):
+    keep, send = halve_call("dp", bit, *flat, "halve_dp")
+    return [keep, exchange(send, "dp", 1 << bit)]
+
+
+def finish_sum(early, late, group):
+    replicas = lax.axis_size("dp")
     bit = 1
-    while half > 1:
-        half //= 2
-        keep, send = halve_call("dp", bit, flat, "halve_dp")
-        flat = [keep, exchange(send, "dp", 1 << bit)]
+    while (1 << bit) < group:
+        early = [next_sum(flat, bit) for flat in early]
+        last = (2 << bit) >= group
+        waited, ready = after_arrivals(early[:1] if last else early, late[1])
+        early = waited + early[len(waited) :]
+        late = [late[0], ready]
+        late = next_sum(late, bit)
         bit += 1
-    return flat
-
-
-def finish_sum(chunks, group):
-    replicas = lax.axis_size("dp")
-    flat = [item for chunk in chunks for item in near_sum(chunk)]
+    flat = [item for chunk in early + [late] for item in chunk]
     width = flat[0].shape[-1]
     rows = sum(item.shape[1] for item in flat[::2])
     (piece,) = local_call(piece_kernel, [((rows, width), low)], flat, name="piece_sum")
@@ -731,71 +745,99 @@
     attended, seconds[2] = lax.optimization_barrier((attended, seconds[2]))
     seconds[3] = exchange(seconds[2], "shard", 1)
     seconds = [seconds[offset] for offset in range(shards)]
-    pair = (shards // 2, second_rows, width)
-    output, middle_grad, attended_grad, sums, kept_ffn, send_ffn = local_call(
-        functools.partial(feed_kernel, shards),
-        [
-            ((rows, width), low),
-            ((rows, width), wide),
-            ((rows, width), low),
-            ((SMALL_PAD, width), wide),
-            (pair, wide),
-            (pair, low),
-        ],
-        [tokens, attended, seed] + firsts + seconds,
-        [
-            ((shards, SMALL_PAD, width), wide),
-            ((width, width), low),
-            ((width, hidden_count), low),
-            ((hidden_count, width), low),
-            ((shards, second_rows, width), wide),
-        ],
-        flops=rows * width * (hidden_count * 12 + width * 6),
-        name="feed",
+    down_rows, up_rows = down_weight.shape[0], up_weight.size // width
+    blocks = hidden_count // width
+    square = (width, width)
+    pair = (shards // 2, down_rows + up_rows, width)
+    act, base, dhidden, norm_two, root_two, out_full, down_full, sums, kept_ffn, send_ffn = (
+        local_call(
+            functools.partial(feed_first_kernel, shards),
+            [
+                ((rows, hidden_count), low),
+                ((rows, width), wide),
+                ((rows, width), wide),
+                ((rows, width), wide),
+                ((rows, 1), wide),
+                (square, low),
+                ((hidden_count, width), low),
+                ((SMALL_PAD, width), wide),
+                (pair, wide),
+                (pair, low),
+            ],
+            [tokens, attended, seed] + firsts + seconds,
+            [
+                ((shards, SMALL_PAD, width), wide),
+                ((width, hidden_count), low),
+                ((shards, down_rows + up_rows, width), wide),
+            ],
+            flops=rows * width * hidden_count * 10,
+            name="feed_first",
+        )
     )
     arrived_ffn = exchange(send_ffn, "shard", 1)
-    shared = [joined, attended_grad, log_sums, bias, mixed]
-    tile_scratch = [((LANES, rows), low), ((rows, LANES), wide), ((rows, LANES), wide)]
-    per_tile = LANES // HEAD
-    groups = [list(range(at, at + per_tile)) for at in range(0, heads, per_tile)]
-    groups = [groups[0][:3], groups[0][3:]] + groups[1:]
-    first_query, first_key, first_value = local_call(
-        functools.partial(back_first_kernel, groups[0]),
-        tile_scratch,
-        shared,
-        flops=heads * rows * rows * 256 * 5 // 2,
-        name="back_first",
-    )
-    first_query, arrived_ffn = lax.optimization_barrier((first_query, arrived_ffn))
-    keep_ffn, send_ffn = halve_call("shard", 1, [kept_ffn, arrived_ffn], "halve_ffn")
-    first_query, send_ffn = lax.optimization_barrier((first_query, send_ffn))
-    arrived_ffn = exchange(send_ffn, "shard", 2)
+    (output,) = local_call(
+        output_kernel,
+        [((rows, width), low)],
+        [base, act, down_full],
+        flops=rows * width * hidden_count * 2,
+        name="output",
+    )
+    middle_grad, attended_grad, grad_out, sums = local_call(
+        functools.partial(feed_last_kernel, shards),
+        [((rows, width), wide), ((rows, width), low), (square, wide), ((SMALL_PAD, width), wide)],
+        [attended, seed, dhidden, norm_two, root_two, out_full, sums] + firsts,
+        [((shards, SMALL_PAD, width), wide)],
+        flops=rows * width * width * 4,
+        name="feed_last",
+    )
+    attended_grad, arrived_ffn = lax.optimization_barrier((attended_grad, arrived_ffn))
+    keep_down, send_down, keep_up, send_up = halve_call(
+        "shard", 1, kept_ffn, arrived_ffn, "halve_ffn", [down_rows, up_rows]
+    )
+    attended_grad, send_down, send_up = lax.optimization_barrier(
+        (attended_grad, send_down, send_up)
+    )
+    arrived_down = exchange(send_down, "shard", 2)
+    arrived_up = exchange(send_up, "shard", 2)
     tail = TILE_ROWS
-    att_rows = 3 * part + tail
+    att_rows = 4 * part + tail
     pair = (shards // 2, att_rows, width)
     input_grad, kept_att, send_att = local_call(
-        functools.partial(back_last_kernel, shards, groups[1:]),
+        functools.partial(back_kernel, shards),
         [((rows, width), wide), (pair, wide), (pair, low)],
-        shared + [first_query, first_key, first_value, normed, root, middle_grad, sums] + firsts,
-        [((width, 3 * width), low), ((shards, SMALL_PAD, width), wide)]
-        + tile_scratch
-        + [((rows, 3 * width), low), ((shards, att_rows, width), wide)],
-        flops=heads * rows * rows * 256 * 6,
-        name="back_last",
+        [joined, attended_grad, log_sums, bias, mixed]
+        + [normed, root, middle_grad, sums, grad_out]
+        + firsts,
+        [
+            ((width, 3 * width), low),
+            ((shards, SMALL_PAD, width), wide),
+            ((LANES, rows), low),
+            ((rows, LANES), wide),
+            ((rows, LANES), wide),
+            ((rows, 3 * width), low),
+            ((shards, att_rows, width), wide),
+        ],
+        flops=heads * rows * rows * 256 * 10,
+        name="back",
+    )
+    send_att, arrived_down, arrived_up = lax.optimization_barrier(
+        (send_att, arrived_down, arrived_up)
     )
     arrived_att = exchange(send_att, "shard", 1)
-    keep_att, send_att = halve_call("shard", 1, [kept_att, arrived_att], "halve_att")
-    send_att, arrived_ffn = lax.optimization_barrier((send_att, arrived_ffn))
-    tails = (0, tail)
+    keep_att, send_att = halve_call("shard", 1, kept_att, arrived_att, "halve_att")
     arrived_att = exchange(send_att, "shard", 2)
-    chunk_ffn = split_chunk([keep_ffn[0], arrived_ffn[0]], 0, group)
-    chunk_att = split_chunk([keep_att[0], arrived_att[0]], tail, group)
-    pieces = finish_sum([chunk_ffn, chunk_att], group)
-    blocks = hidden_count // width
+    early = [
+        split_chunk([keep_down[0], arrived_down[0]], 0, group),
+        split_chunk([keep_up[0], arrived_up[0]], 0, group),
+    ]
+    early, arrived_att = after_arrivals(early, arrived_att)
+    late = split_chunk([keep_att[0], arrived_att[0]], tail, group)
+    pieces = finish_sum(early, late, group)
+    second_at = down_rows + up_rows
     results = adam_call(
         pieces,
-        (second_rows, att_rows),
-        tails,
+        (down_rows, up_rows, att_rows),
+        (0, 0, tail),
         [
             (qkv_weight, qkv_first, qkv_second),
             (out_weight, out_first, out_second),
@@ -804,11 +846,11 @@
             (gains_biases, small_first, small_second),
         ],
         [
-            (second_rows, part, matrix_decay),
-            (0, part, matrix_decay),
-            (part, part, matrix_decay),
-            (part + blocks * part, 0, matrix_decay),
-            (second_rows + 3 * part, 1, 0.0),
+            (second_at, part, matrix_decay),
+            (second_at + 3 * part, part, matrix_decay),
+            (down_rows, part, matrix_decay),
+            (0, 0, matrix_decay),
+            (second_at + 4 * part, 1, 0.0),
         ],
     )
     return (output, input_grad, *results)

time: 69.5 us -> 76.1 us (1.095)
  waiting for transfers between devices: 24.1 us -> 28.3 us
  starting transfers between devices: 24.4 us -> 26.1 us
  Pallas kernels: 19.5 us -> 20.3 us
    ppermute x23 -> x27, waiting for transfers between devices: 24.1 us -> 28.3 us  [exchange(): lax.ppermute(values, axis, [(index, index ^ mask) for index in range(coun...]
    ppermute x23 -> x27, starting transfers between devices: 24.4 us -> 26.1 us  [exchange(): lax.ppermute(values, axis, [(index, index ^ mask) for index in range(coun...]
    pallas_call x17 -> x21, Pallas kernels: 19.5 us -> 20.3 us  [local_call(): pl.pallas_call(kernel, out_shape=outs, in_specs=[pl.BlockSpec(memory_spac...]
  transfers between devices with their start and end apart: 23 -> 27, of which waited for: 15 -> 18; matrix products, arithmetic and copies ran while one was open for 0% -> 0% of each run, Pallas kernels for 17% -> 18%
where the time goes in v10:
time: 76.1 us; the launch traced here: 75.9 us
  waiting for transfers between devices  28.3 us (37%)
  starting transfers between devices  26.1 us (34%)
  Pallas kernels  20.3 us (27%)
  between operations  1.16 us (2%)
    ppermute x27, waiting for transfers between devices, exchange(): lax.ppermute(values, axis, [(index, index ^ mask) for index in range(coun...  28.3 us
    ppermute x27, starting transfers between devices, exchange(): lax.ppermute(values, axis, [(index, index ^ mask) for index in range(coun...  26.1 us
    pallas_call x21, Pallas kernels, local_call(): pl.pallas_call(kernel, out_shape=outs, in_specs=[pl.BlockSpec(memory_spac...  20.3 us
  transfers between devices with their start and end apart: 27, of which 18 were waited for; matrix products, arithmetic and copies ran while one was open for 0% of the time, Pallas kernels for 18%

profile of v10, /device:TPU:0, one launch (start us, length us, event | category | flops | bytes accessed | tf_op | source)
XLA Modules:
  0.0 75.9 jit_solution(16990437491652001993)
XLA Ops:
  0.7 1.6 %pack_first.1.refs_2_.refs_3_.refs_7_.refs_10_ = bf16[208,256]{1,0:T(8,128)(2,1)} custom-call(f32[64,768]{1,0:T(8,128)} %refs_8_.1, f32[768]{0:T(1024)} %refs_20_.1), custom_call_target="tpu_custom_call" | custom-call | bytes 306176 | tf_op jit(solution)/shard_map/pack_first/pallas_call | solution.py:551
  2.3 3.0 %collective-permute-start = (bf16[208,256]{1,0:T(8,128)(2,1)}, bf16[208,256]{1,0:T(8,128)(2,1)S(1)}, u32[]{:S(2)}, u32[]{:S(2)}) collective-permute-start(bf16[208,256]{1,0:T(8,128)(2,1)} %pack_first.1.refs_2_.refs_3_.refs_7_.refs_10_), channel_id=1, source_target_pairs={{0,2},{1,3},{2,0},{3,1},{4,6},{5,7},{6,4},{7,5},{8,10},{9,11},{10,... | collective-permute-start | bytes 319496 | tf_op jit(solution)/shard_map/ppermute | solution.py:565
  5.3 1.8 %pack_second.1.refs_7_ = bf16[576,256]{1,0:T(8,128)(2,1)} custom-call(f32[64,256]{1,0:T(8,128)} %refs_11_.1, f32[64,1024]{1,0:T(8,128)} %refs_14_.1, f32[256,256]{1,0:T(8,128)} %refs_17_.1), custom_call_target="tpu_custom_call" | custom-call | bytes 884736 | tf_op jit(solution)/shard_map/pack_second/pallas_call | solution.py:551
  7.4 0.7 prepare.1
  8.1 0.4 collective-permute-done.refs_4_.refs_5_.refs_9_.refs_12_
  8.6 0.4 collective-permute-start.4
  9.0 0.8 %collective-permute-done.2.refs_5_.refs_6_.refs_10_.refs_13_ = bf16[208,256]{1,0:T(8,128)(2,1)S(1)} collective-permute-done((bf16[208,256]{1,0:T(8,128)(2,1)S(1)}, bf16[208,256]{1,0:T(8,128)(2,1)S(1)}, u32[]{:S(2)}, u32[]{:S(2)}) %collective-permute-start.2) | collective-permute-done | bytes 106528 | tf_op jit(solution)/shard_map/ppermute | solution.py:565
  9.8 3.0 %attend.1 = (bf16[512,768]{1,0:T(8,128)(2,1)S(1)}, bf16[512,256]{1,0:T(8,128)(2,1)S(1)}, f32[8,512]{1,0:T(8,128)S(1)}, f32[256,512]{1,0:T(8,128)S(1)}) custom-call(f32[512,256]{1,0:T(8,128)S(1)} %get-tuple-element.119.refs_0_.refs_5_, f32[512,512]{1,0:T(8,128)S(1)} %get-tuple-element.120.refs_1_.refs_3_, bf16[208,256]{1,0:T(8,128)(2,1)S(1)} %copy-done.3, ...), custom_call_target="tpu_custom_call" | custom-call | flops 1342177280 | bytes 3588096 | tf_op jit(solution)/shard_map/attend/pallas_call | solution.py:551
  12.9 3.1 %collective-permute-done.3.refs_9_ = bf16[576,256]{1,0:T(8,128)(2,1)S(1)} collective-permute-done((bf16[576,256]{1,0:T(8,128)(2,1)}, bf16[576,256]{1,0:T(8,128)(2,1)S(1)}, u32[]{:S(2)}, u32[]{:S(2)}) %collective-permute-start.3) | collective-permute-done | bytes 294944 | tf_op jit(solution)/shard_map/ppermute | solution.py:565
  16.0 1.6 %collective-permute-done.5.refs_10_ = bf16[576,256]{1,0:T(8,128)(2,1)S(1)} collective-permute-done((bf16[576,256]{1,0:T(8,128)(2,1)S(1)}, bf16[576,256]{1,0:T(8,128)(2,1)S(1)}, u32[]{:S(2)}, u32[]{:S(2)}) %collective-permute-start.5) | collective-permute-done | bytes 294944 | tf_op jit(solution)/shard_map/ppermute | solution.py:565
  17.5 3.0 %feed_first.1 = (bf16[512,1024]{1,0:T(8,128)(2,1)S(1)}, f32[512,256]{1,0:T(8,128)S(1)}, f32[512,256]{1,0:T(8,128)S(1)}, f32[512,256]{1,0:T(8,128)S(1)}, f32[512,...) custom-call(bf16[512,256]{1,0:T(8,128)(2,1)S(1)} %copy-done.7, ...), custom_call_target="tpu_custom_call" | custom-call | flops 1342177280 | bytes 7260160 | tf_op jit(solution)/shard_map/feed_first/pallas_call | solution.py:551
  20.5 0.2 collective-permute-start.6
  20.7 0.7 feed_last.1
  21.4 1.1 %collective-permute-done.6.arrived = bf16[2,512,256]{2,1,0:T(8,128)(2,1)S(1)} collective-permute-done((bf16[2,512,256]{2,1,0:T(8,128)(2,1)S(1)}, bf16[2,512,256]{2,1,0:T(8,128)(2,1)S(1)}, u32[]{:S(2)}, u32[]{:S(2)}) %collective-permute-start.6) | collective-permute-done | bytes 524320 | tf_op jit(solution)/shard_map/ppermute | solution.py:565
  22.6 0.7 collective-permute-start.7
  23.3 1.4 %collective-permute-start.8 = (bf16[1,256,256]{2,1,0:T(8,128)(2,1)S(1)}, bf16[1,256,256]{2,1,0:T(8,128)(2,1)S(1)}, u32[]{:S(2)}, u32[]{:S(2)}) collective-permute-start(bf16[1,256,256]{2,1,0:T(8,128)(2,1)S(1)} %get-tuple-element.154), channel_id=1, source_target_pairs={{0,2},{1,3},{2,0},{3,1},{4,6},{5,7},{6,4},{7,5},{8,10},{9,11},{10,... | collective-permute-start | bytes 393224 | tf_op jit(solution)/shard_map/ppermute | solution.py:565
  24.7 6.1 %back.1 = (f32[512,256]{1,0:T(8,128)}, f32[2,264,256]{2,1,0:T(8,128)S(1)}, bf16[2,264,256]{2,1,0:T(8,128)(2,1)S(1)}) custom-call(bf16[512,768]{1,0:T(8,128)(2,1)S(1)} %get-tuple-element.130.refs_0_, bf16[512,256]{1,0:T(8,128)(2,1)S(1)} %get-tuple-element.143.refs_1_, f32[8,512]{1,0:T(8,128)S(1)} %get-tuple-element.144.refs_2_, ...), custom_call_target="tpu_custom_call" | custom-call | flops 5368709120 | bytes 5728256 | tf_op jit(solution)/shard_map/back/pallas_call | solution.py:551
  30.8 0.2 collective-permute-done.8
  31.0 1.5 %collective-permute-done.11.arrived = bf16[2,264,256]{2,1,0:T(8,128)(2,1)S(1)} collective-permute-done((bf16[2,264,256]{2,1,0:T(8,128)(2,1)S(1)}, bf16[2,264,256]{2,1,0:T(8,128)(2,1)S(1)}, u32[]{:S(2)}, u32[]{:S(2)}) %collective-permute-start.11) | collective-permute-done | bytes 270368 | tf_op jit(solution)/shard_map/ppermute | solution.py:565
  32.6 0.7 collective-permute-start.12
  33.4 1.6 %collective-permute-start.10 = (bf16[4,32,256]{2,1,0:T(8,128)(2,1)S(1)}, bf16[4,32,256]{2,1,0:T(8,128)(2,1)S(1)}, u32[]{:S(2)}, u32[]{:S(2)}) collective-permute-start(bf16[4,32,256]{2,1,0:T(8,128)(2,1)S(1)} %get-tuple-element.160), channel_id=1, source_target_pairs={{0,4},{4,0},{8,12},{12,8},{16,20},{20,16},{24,28},{28,24},{1,5},{5... | collective-permute-start | bytes 196616 | tf_op jit(solution)/shard_map/ppermute | solution.py:565
  35.0 0.6 collective-permute-start.9
  35.6 2.6 %collective-permute-done.10.arrived = bf16[4,32,256]{2,1,0:T(8,128)(2,1)S(1)} collective-permute-done((bf16[4,32,256]{2,1,0:T(8,128)(2,1)S(1)}, bf16[4,32,256]{2,1,0:T(8,128)(2,1)S(1)}, u32[]{:S(2)}, u32[]{:S(2)}) %collective-permute-start.10) | collective-permute-done | bytes 65568 | tf_op jit(solution)/shard_map/ppermute | solution.py:565
  38.2 1.1 %collective-permute-done.9.arrived = bf16[4,32,256]{2,1,0:T(8,128)(2,1)S(1)} collective-permute-done((bf16[4,32,256]{2,1,0:T(8,128)(2,1)S(1)}, bf16[4,32,256]{2,1,0:T(8,128)(2,1)S(1)}, u32[]{:S(2)}, u32[]{:S(2)}) %collective-permute-start.9) | collective-permute-done | bytes 65568 | tf_op jit(solution)/shard_map/ppermute | solution.py:565
  39.4 0.9 %collective-permute-start.15 = (bf16[4,40,256]{2,1,0:T(8,128)(2,1)S(1)}, bf16[4,40,256]{2,1,0:T(8,128)(2,1)S(1)}, u32[]{:S(2)}, u32[]{:S(2)}) collective-permute-start(bf16[4,40,256]{2,1,0:T(8,128)(2,1)S(1)} %get-tuple-element.172), channel_id=1, source_target_pairs={{0,4},{4,0},{8,12},{12,8},{16,20},{20,16},{24,28},{28,24},{1,5},{5... | collective-permute-start | bytes 245768 | tf_op jit(solution)/shard_map/ppermute | solution.py:565
  40.3 1.6 %collective-permute-start.13 = (bf16[2,32,256]{2,1,0:T(8,128)(2,1)S(1)}, bf16[2,32,256]{2,1,0:T(8,128)(2,1)S(1)}, u32[]{:S(2)}, u32[]{:S(2)}) collective-permute-start(bf16[2,32,256]{2,1,0:T(8,128)(2,1)S(1)} %get-tuple-element.166), channel_id=1, source_target_pairs={{0,8},{4,12},{8,0},{12,4},{16,24},{20,28},{24,16},{28,20},{1,9},{5... | collective-permute-start | bytes 98312 | tf_op jit(solution)/shard_map/ppermute | solution.py:565
  42.0 0.5 collective-permute-start.14
  42.5 1.8 %collective-permute-done.13.arrived = bf16[2,32,256]{2,1,0:T(8,128)(2,1)S(1)} collective-permute-done((bf16[2,32,256]{2,1,0:T(8,128)(2,1)S(1)}, bf16[2,32,256]{2,1,0:T(8,128)(2,1)S(1)}, u32[]{:S(2)}, u32[]{:S(2)}) %collective-permute-start.13) | collective-permute-done | bytes 32800 | tf_op jit(solution)/shard_map/ppermute | solution.py:565
  44.3 1.7 %collective-permute-done.14.arrived = bf16[2,32,256]{2,1,0:T(8,128)(2,1)S(1)} collective-permute-done((bf16[2,32,256]{2,1,0:T(8,128)(2,1)S(1)}, bf16[2,32,256]{2,1,0:T(8,128)(2,1)S(1)}, u32[]{:S(2)}, u32[]{:S(2)}) %collective-permute-start.14) | collective-permute-done | bytes 32800 | tf_op jit(solution)/shard_map/ppermute | solution.py:565
  46.0 0.5 collective-permute-start.17
  46.5 2.7 %collective-permute-start.16 = (bf16[1,32,256]{2,1,0:T(8,128)(2,1)S(1)}, bf16[1,32,256]{2,1,0:T(8,128)(2,1)S(1)}, u32[]{:S(2)}, u32[]{:S(2)}) collective-permute-start(bf16[1,32,256]{2,1,0:T(8,128)(2,1)S(1)} %get-tuple-element.175), channel_id=1, source_target_pairs={{0,16},{4,20},{8,24},{12,28},{16,0},{20,4},{24,8},{28,12},{1,17},{... | collective-permute-start | bytes 49160 | tf_op jit(solution)/shard_map/ppermute | solution.py:565
  49.2 2.0 %collective-permute-done.16.refs_1_ = bf16[1,32,256]{2,1,0:T(8,128)(2,1)S(1)} collective-permute-done((bf16[1,32,256]{2,1,0:T(8,128)(2,1)S(1)}, bf16[1,32,256]{2,1,0:T(8,128)(2,1)S(1)}, u32[]{:S(2)}, u32[]{:S(2)}) %collective-permute-start.16) | collective-permute-done | bytes 16416 | tf_op jit(solution)/shard_map/ppermute | solution.py:565
  51.3 2.9 %collective-permute-start.19 = (bf16[1,40,256]{2,1,0:T(8,128)(2,1)S(1)}, bf16[1,40,256]{2,1,0:T(8,128)(2,1)S(1)}, u32[]{:S(2)}, u32[]{:S(2)}) collective-permute-start(bf16[1,40,256]{2,1,0:T(8,128)(2,1)S(1)} %get-tuple-element.187), channel_id=1, source_target_pairs={{0,16},{4,20},{8,24},{12,28},{16,0},{20,4},{24,8},{28,12},{1,17},{... | collective-permute-start | bytes 61448 | tf_op jit(solution)/shard_map/ppermute | solution.py:565
  54.1 0.2 collective-permute-start.18
  54.3 4.5 %collective-permute-done.18.refs_3_ = bf16[1,32,256]{2,1,0:T(8,128)(2,1)S(1)} collective-permute-done((bf16[1,32,256]{2,1,0:T(8,128)(2,1)S(1)}, bf16[1,32,256]{2,1,0:T(8,128)(2,1)S(1)}, u32[]{:S(2)}, u32[]{:S(2)}) %collective-permute-start.18) | collective-permute-done | bytes 16416 | tf_op jit(solution)/shard_map/ppermute | solution.py:565
  58.9 1.6 %collective-permute-start.21 = (bf16[104,256]{1,0:T(8,128)(2,1)S(1)}, bf16[104,256]{1,0:T(8,128)(2,1)S(1)}, u32[]{:S(2)}, u32[]{:S(2)}) collective-permute-start(bf16[104,256]{1,0:T(8,128)(2,1)S(1)} %piece_sum.1.refs_0_), channel_id=1, source_target_pairs={{0,4},{4,0},{8,12},{12,8},{16,20},{20,16},{24,28},{28,24},{1,5},{5... | collective-permute-start | bytes 159752 | tf_op jit(solution)/shard_map/ppermute | solution.py:565
  60.5 2.3 %collective-permute-start.22 = (bf16[104,256]{1,0:T(8,128)(2,1)S(1)}, bf16[104,256]{1,0:T(8,128)(2,1)S(1)}, u32[]{:S(2)}, u32[]{:S(2)}) collective-permute-start(bf16[104,256]{1,0:T(8,128)(2,1)S(1)} %piece_sum.1.refs_0_), channel_id=1, source_target_pairs={{0,8},{4,12},{8,0},{12,4},{16,24},{20,28},{24,16},{28,20},{1,9},{5... | collective-permute-start | bytes 159752 | tf_op jit(solution)/shard_map/ppermute | solution.py:565
  62.8 0.8 %collective-permute-done.21.refs_1_ = bf16[104,256]{1,0:T(8,128)(2,1)S(1)} collective-permute-done((bf16[104,256]{1,0:T(8,128)(2,1)S(1)}, bf16[104,256]{1,0:T(8,128)(2,1)S(1)}, u32[]{:S(2)}, u32[]{:S(2)}) %collective-permute-start.21) | collective-permute-done | bytes 53280 | tf_op jit(solution)/shard_map/ppermute | solution.py:565
  63.7 1.9 %collective-permute-done.20.refs_4_ = bf16[104,256]{1,0:T(8,128)(2,1)S(1)} collective-permute-done((bf16[104,256]{1,0:T(8,128)(2,1)S(1)}, bf16[104,256]{1,0:T(8,128)(2,1)S(1)}, u32[]{:S(2)}, u32[]{:S(2)}) %collective-permute-start.20) | collective-permute-done | bytes 53280 | tf_op jit(solution)/shard_map/ppermute | solution.py:565
  65.6 1.5 %collective-permute-start.25 = (bf16[104,256]{1,0:T(8,128)(2,1)S(1)}, bf16[104,256]{1,0:T(8,128)(2,1)S(1)}, u32[]{:S(2)}, u32[]{:S(2)}) collective-permute-start(bf16[104,256]{1,0:T(8,128)(2,1)S(1)} %collective-permute-done.20.refs_4_), channel_id=1, source_target_pairs={{0,8},{4,12},{8,0},{12,4},{16,24},{20,28},{24,16},{28,20},{1,9},{5... | collective-permute-start | bytes 159752 | tf_op jit(solution)/shard_map/ppermute | solution.py:565
  67.0 0.9 %collective-permute-start.24 = (bf16[104,256]{1,0:T(8,128)(2,1)S(1)}, bf16[104,256]{1,0:T(8,128)(2,1)S(1)}, u32[]{:S(2)}, u32[]{:S(2)}) collective-permute-start(bf16[104,256]{1,0:T(8,128)(2,1)S(1)} %collective-permute-done.20.refs_4_), channel_id=1, source_target_pairs={{0,4},{4,0},{8,12},{12,8},{16,20},{20,16},{24,28},{28,24},{1,5},{5... | collective-permute-start | bytes 159752 | tf_op jit(solution)/shard_map/ppermute | solution.py:565
  67.9 1.1 %collective-permute-start.23 = (bf16[104,256]{1,0:T(8,128)(2,1)S(1)}, bf16[104,256]{1,0:T(8,128)(2,1)S(1)}, u32[]{:S(2)}, u32[]{:S(2)}) collective-permute-start(bf16[104,256]{1,0:T(8,128)(2,1)S(1)} %collective-permute-done.22.refs_2_), channel_id=1, source_target_pairs={{0,4},{4,0},{8,12},{12,8},{16,20},{20,16},{24,28},{28,24},{1,5},{5... | collective-permute-start | bytes 159752 | tf_op jit(solution)/shard_map/ppermute | solution.py:565
  69.1 0.6 collective-permute-done.25.refs_6_
  69.7 0.5 collective-permute-start.26
  70.3 1.1 %output.1 = bf16[512,256]{1,0:T(8,128)(2,1)} custom-call(f32[512,256]{1,0:T(8,128)S(1)} %get-tuple-element.127.base_ref, bf16[512,1024]{1,0:T(8,128)(2,1)S(1)} %get-tuple-element.128.act_ref, bf16[1024,256]{1,0:T(8,128)(2,1)S(1)} %get-tuple-element.129.down_w), custom_call_target="tpu_custom_call" | custom-call | flops 268435456 | bytes 2359296 | tf_op jit(solution)/shard_map/output/pallas_call | solution.py:551
  71.5 0.6 collective-permute-done.23.refs_3_
  72.1 1.7 %collective-permute-done.26.refs_7_ = bf16[104,256]{1,0:T(8,128)(2,1)S(1)} collective-permute-done((bf16[104,256]{1,0:T(8,128)(2,1)S(1)}, bf16[104,256]{1,0:T(8,128)(2,1)S(1)}, u32[]{:S(2)}, u32[]{:S(2)}) %collective-permute-start.26) | collective-permute-done | bytes 53280 | tf_op jit(solution)/shard_map/ppermute | solution.py:565
  74.0 1.8 %adam.1 = (f32[64,768]{1,0:T(8,128)}, f32[64,768]{1,0:T(8,128)}, f32[64,768]{1,0:T(8,128)}, f32[64,256]{1,0:T(8,128)}, f32[64,256]{1,0:T(8,128)}, /*index=5*/f32...) custom-call(bf16[104,256]{1,0:T(8,128)(2,1)S(1)} %piece_sum.1.refs_0, ...), custom_call_target="tpu_custom_call" | custom-call | bytes 5163008 | tf_op jit(solution)/shard_map/adam/pallas_call | solution.py:551
  (69 shorter events, 0.9 us)
Async XLA Ops:
  2.3 5.1 %copy-start.3 = (bf16[208,256]{1,0:T(8,128)(2,1)S(1)}, bf16[208,256]{1,0:T(8,128)(2,1)}, u32[]{:S(2)}) copy-start(bf16[208,256]{1,0:T(8,128)(2,1)} %pack_first.1.refs_2_.refs_3_.refs_7_.refs_10_) | copy-start | bytes 319492
  2.3 5.1 %copy-start.6 = (bf16[512,256]{1,0:T(8,128)(2,1)S(1)}, bf16[512,256]{1,0:T(8,128)(2,1)}, u32[]{:S(2)}) copy-start(bf16[512,256]{1,0:T(8,128)(2,1)} %seed_ref.1) | copy-start | bytes 786436
  2.3 5.1 %copy-start.7 = (bf16[512,256]{1,0:T(8,128)(2,1)S(1)}, bf16[512,256]{1,0:T(8,128)(2,1)}, u32[]{:S(2)}) copy-start(bf16[512,256]{1,0:T(8,128)(2,1)} %refs_0_.1) | copy-start | bytes 786436
  2.3 6.2 %collective-permute-start = (bf16[208,256]{1,0:T(8,128)(2,1)}, bf16[208,256]{1,0:T(8,128)(2,1)S(1)}, u32[]{:S(2)}, u32[]{:S(2)}) collective-permute-start(bf16[208,256]{1,0:T(8,128)(2,1)} %pack_first.1.refs_2_.refs_3_.refs_7_.refs_10_), channel_id=1, source_target_pairs={{0,2},{1,3},{2,0},{3,1},{4,6},{5,7},{6,4},{7,5},{8,10},{9,11},{10,... | collective-permute-start | bytes 319496 | tf_op jit(solution)/shard_map/ppermute | solution.py:565
  5.3 2.1 %copy-start.19 = (s32[128]{0:T(128)S(1)}, s32[128]{0:T(128)}, u32[]{:S(2)}) copy-start(s32[128]{0:T(128)} %param.21) | copy-start | bytes 1540
  5.3 2.1 %copy-start.20 = (s32[128]{0:T(128)S(1)}, s32[128]{0:T(128)}, u32[]{:S(2)}) copy-start(s32[128]{0:T(128)} %param.22) | copy-start | bytes 1540
  7.2 1.4 %copy-start.4 = (bf16[576,256]{1,0:T(8,128)(2,1)S(1)}, bf16[576,256]{1,0:T(8,128)(2,1)}, u32[]{:S(2)}) copy-start(bf16[576,256]{1,0:T(8,128)(2,1)} %pack_second.1.refs_7_) | copy-start | bytes 884740
  7.2 8.7 %collective-permute-start.3 = (bf16[576,256]{1,0:T(8,128)(2,1)}, bf16[576,256]{1,0:T(8,128)(2,1)S(1)}, u32[]{:S(2)}, u32[]{:S(2)}) collective-permute-start(bf16[576,256]{1,0:T(8,128)(2,1)} %pack_second.1.refs_7_), channel_id=1, source_target_pairs={{0,2},{1,3},{2,0},{3,1},{4,6},{5,7},{6,4},{7,5},{8,10},{9,11},{10,... | collective-permute-start | bytes 884744 | tf_op jit(solution)/shard_map/ppermute | solution.py:565
  7.4 1.7 %collective-permute-start.1 = (bf16[208,256]{1,0:T(8,128)(2,1)S(1)}, bf16[208,256]{1,0:T(8,128)(2,1)S(1)}, u32[]{:S(2)}, u32[]{:S(2)}) collective-permute-start(bf16[208,256]{1,0:T(8,128)(2,1)S(1)} %copy-done.3), channel_id=1, source_target_pairs={{0,1},{1,0},{2,3},{3,2},{4,5},{5,4},{6,7},{7,6},{8,9},{9,8},{10,11... | collective-permute-start | bytes 319496 | tf_op jit(solution)/shard_map/ppermute | solution.py:565
  8.5 1.3 %collective-permute-start.2 = (bf16[208,256]{1,0:T(8,128)(2,1)S(1)}, bf16[208,256]{1,0:T(8,128)(2,1)S(1)}, u32[]{:S(2)}, u32[]{:S(2)}) collective-permute-start(bf16[208,256]{1,0:T(8,128)(2,1)S(1)} %collective-permute-done.refs_4_.refs_5_.refs_9_.refs_12_), channel_id=1, source_target_pairs={{0,1},{1,0},{2,3},{3,2},{4,5},{5,4},{6,7},{7,6},{8,9},{9,8},{10,11... | collective-permute-start | bytes 319496 | tf_op jit(solution)/shard_map/ppermute | solution.py:565
  8.6 7.3 %collective-permute-start.4 = (bf16[576,256]{1,0:T(8,128)(2,1)S(1)}, bf16[576,256]{1,0:T(8,128)(2,1)S(1)}, u32[]{:S(2)}, u32[]{:S(2)}) collective-permute-start(bf16[576,256]{1,0:T(8,128)(2,1)S(1)} %copy-done.4), channel_id=1, source_target_pairs={{0,1},{1,0},{2,3},{3,2},{4,5},{5,4},{6,7},{7,6},{8,9},{9,8},{10,11... | collective-permute-start | bytes 884744 | tf_op jit(solution)/shard_map/ppermute | solution.py:565
  16.0 1.6 %collective-permute-start.5 = (bf16[576,256]{1,0:T(8,128)(2,1)S(1)}, bf16[576,256]{1,0:T(8,128)(2,1)S(1)}, u32[]{:S(2)}, u32[]{:S(2)}) collective-permute-start(bf16[576,256]{1,0:T(8,128)(2,1)S(1)} %collective-permute-done.3.refs_9_), channel_id=1, source_target_pairs={{0,1},{1,0},{2,3},{3,2},{4,5},{5,4},{6,7},{7,6},{8,9},{9,8},{10,11... | collective-permute-start | bytes 884744 | tf_op jit(solution)/shard_map/ppermute | solution.py:565
  20.5 2.0 %collective-permute-start.6 = (bf16[2,512,256]{2,1,0:T(8,128)(2,1)S(1)}, bf16[2,512,256]{2,1,0:T(8,128)(2,1)S(1)}, u32[]{:S(2)}, u32[]{:S(2)}) collective-permute-start(bf16[2,512,256]{2,1,0:T(8,128)(2,1)S(1)} %get-tuple-element.137), channel_id=1, source_target_pairs={{0,1},{1,0},{2,3},{3,2},{4,5},{5,4},{6,7},{7,6},{8,9},{9,8},{10,11... | collective-permute-start | bytes 1572872 | tf_op jit(solution)/shard_map/ppermute | solution.py:565
  22.6 8.2 %collective-permute-start.7 = (bf16[1,256,256]{2,1,0:T(8,128)(2,1)S(1)}, bf16[1,256,256]{2,1,0:T(8,128)(2,1)S(1)}, u32[]{:S(2)}, u32[]{:S(2)}) collective-permute-start(bf16[1,256,256]{2,1,0:T(8,128)(2,1)S(1)} %get-tuple-element.153), channel_id=1, source_target_pairs={{0,2},{1,3},{2,0},{3,1},{4,6},{5,7},{6,4},{7,5},{8,10},{9,11},{10,... | collective-permute-start | bytes 393224 | tf_op jit(solution)/shard_map/ppermute | solution.py:565
  23.3 7.7 %collective-permute-start.8 = (bf16[1,256,256]{2,1,0:T(8,128)(2,1)S(1)}, bf16[1,256,256]{2,1,0:T(8,128)(2,1)S(1)}, u32[]{:S(2)}, u32[]{:S(2)}) collective-permute-start(bf16[1,256,256]{2,1,0:T(8,128)(2,1)S(1)} %get-tuple-element.154), channel_id=1, source_target_pairs={{0,2},{1,3},{2,0},{3,1},{4,6},{5,7},{6,4},{7,5},{8,10},{9,11},{10,... | collective-permute-start | bytes 393224 | tf_op jit(solution)/shard_map/ppermute | solution.py:565
  31.0 1.5 %collective-permute-start.11 = (bf16[2,264,256]{2,1,0:T(8,128)(2,1)S(1)}, bf16[2,264,256]{2,1,0:T(8,128)(2,1)S(1)}, u32[]{:S(2)}, u32[]{:S(2)}) collective-permute-start(bf16[2,264,256]{2,1,0:T(8,128)(2,1)S(1)} %get-tuple-element.162), channel_id=1, source_target_pairs={{0,1},{1,0},{2,3},{3,2},{4,5},{5,4},{6,7},{7,6},{8,9},{9,8},{10,11... | collective-permute-start | bytes 811016 | tf_op jit(solution)/shard_map/ppermute | solution.py:565
  32.6 6.7 %collective-permute-start.12 = (bf16[1,264,256]{2,1,0:T(8,128)(2,1)S(1)}, bf16[1,264,256]{2,1,0:T(8,128)(2,1)S(1)}, u32[]{:S(2)}, u32[]{:S(2)}) collective-permute-start(bf16[1,264,256]{2,1,0:T(8,128)(2,1)S(1)} %get-tuple-element.163), channel_id=1, source_target_pairs={{0,2},{1,3},{2,0},{3,1},{4,6},{5,7},{6,4},{7,5},{8,10},{9,11},{10,... | collective-permute-start | bytes 405512 | tf_op jit(solution)/shard_map/ppermute | solution.py:565
  33.4 4.8 %collective-permute-start.10 = (bf16[4,32,256]{2,1,0:T(8,128)(2,1)S(1)}, bf16[4,32,256]{2,1,0:T(8,128)(2,1)S(1)}, u32[]{:S(2)}, u32[]{:S(2)}) collective-permute-start(bf16[4,32,256]{2,1,0:T(8,128)(2,1)S(1)} %get-tuple-element.160), channel_id=1, source_target_pairs={{0,4},{4,0},{8,12},{12,8},{16,20},{20,16},{24,28},{28,24},{1,5},{5... | collective-permute-start | bytes 196616 | tf_op jit(solution)/shard_map/ppermute | solution.py:565
  35.0 4.3 %collective-permute-start.9 = (bf16[4,32,256]{2,1,0:T(8,128)(2,1)S(1)}, bf16[4,32,256]{2,1,0:T(8,128)(2,1)S(1)}, u32[]{:S(2)}, u32[]{:S(2)}) collective-permute-start(bf16[4,32,256]{2,1,0:T(8,128)(2,1)S(1)} %get-tuple-element.157), channel_id=1, source_target_pairs={{0,4},{4,0},{8,12},{12,8},{16,20},{20,16},{24,28},{28,24},{1,5},{5... | collective-permute-start | bytes 196616 | tf_op jit(solution)/shard_map/ppermute | solution.py:565
  39.4 6.6 %collective-permute-start.15 = (bf16[4,40,256]{2,1,0:T(8,128)(2,1)S(1)}, bf16[4,40,256]{2,1,0:T(8,128)(2,1)S(1)}, u32[]{:S(2)}, u32[]{:S(2)}) collective-permute-start(bf16[4,40,256]{2,1,0:T(8,128)(2,1)S(1)} %get-tuple-element.172), channel_id=1, source_target_pairs={{0,4},{4,0},{8,12},{12,8},{16,20},{20,16},{24,28},{28,24},{1,5},{5... | collective-permute-start | bytes 245768 | tf_op jit(solution)/shard_map/ppermute | solution.py:565
  40.3 4.0 %collective-permute-start.13 = (bf16[2,32,256]{2,1,0:T(8,128)(2,1)S(1)}, bf16[2,32,256]{2,1,0:T(8,128)(2,1)S(1)}, u32[]{:S(2)}, u32[]{:S(2)}) collective-permute-start(bf16[2,32,256]{2,1,0:T(8,128)(2,1)S(1)} %get-tuple-element.166), channel_id=1, source_target_pairs={{0,8},{4,12},{8,0},{12,4},{16,24},{20,28},{24,16},{28,20},{1,9},{5... | collective-permute-start | bytes 98312 | tf_op jit(solution)/shard_map/ppermute | solution.py:565
  42.0 4.0 %collective-permute-start.14 = (bf16[2,32,256]{2,1,0:T(8,128)(2,1)S(1)}, bf16[2,32,256]{2,1,0:T(8,128)(2,1)S(1)}, u32[]{:S(2)}, u32[]{:S(2)}) collective-permute-start(bf16[2,32,256]{2,1,0:T(8,128)(2,1)S(1)} %get-tuple-element.169), channel_id=1, source_target_pairs={{0,8},{4,12},{8,0},{12,4},{16,24},{20,28},{24,16},{28,20},{1,9},{5... | collective-permute-start | bytes 98312 | tf_op jit(solution)/shard_map/ppermute | solution.py:565
  46.0 5.2 %collective-permute-start.17 = (bf16[2,40,256]{2,1,0:T(8,128)(2,1)S(1)}, bf16[2,40,256]{2,1,0:T(8,128)(2,1)S(1)}, u32[]{:S(2)}, u32[]{:S(2)}) collective-permute-start(bf16[2,40,256]{2,1,0:T(8,128)(2,1)S(1)} %get-tuple-element.178), channel_id=1, source_target_pairs={{0,8},{4,12},{8,0},{12,4},{16,24},{20,28},{24,16},{28,20},{1,9},{5... | collective-permute-start | bytes 122888 | tf_op jit(solution)/shard_map/ppermute | solution.py:565
  46.5 4.7 %collective-permute-start.16 = (bf16[1,32,256]{2,1,0:T(8,128)(2,1)S(1)}, bf16[1,32,256]{2,1,0:T(8,128)(2,1)S(1)}, u32[]{:S(2)}, u32[]{:S(2)}) collective-permute-start(bf16[1,32,256]{2,1,0:T(8,128)(2,1)S(1)} %get-tuple-element.175), channel_id=1, source_target_pairs={{0,16},{4,20},{8,24},{12,28},{16,0},{20,4},{24,8},{28,12},{1,17},{... | collective-permute-start | bytes 49160 | tf_op jit(solution)/shard_map/ppermute | solution.py:565
  51.2 22.6 %copy-start.16 = (f32[768]{0:T(1024)S(1)}, f32[768]{0:T(1024)}, u32[]{:S(2)}) copy-start(f32[768]{0:T(1024)} %refs_20_.1) | copy-start | bytes 9220
  51.2 22.6 %copy-start.17 = (f32[768]{0:T(1024)S(1)}, f32[768]{0:T(1024)}, u32[]{:S(2)}) copy-start(f32[768]{0:T(1024)} %refs_21_.1) | copy-start | bytes 9220
  51.2 22.6 %copy-start.18 = (f32[768]{0:T(1024)S(1)}, f32[768]{0:T(1024)}, u32[]{:S(2)}) copy-start(f32[768]{0:T(1024)} %refs_22_.1) | copy-start | bytes 9220
  51.3 7.6 %collective-permute-start.19 = (bf16[1,40,256]{2,1,0:T(8,128)(2,1)S(1)}, bf16[1,40,256]{2,1,0:T(8,128)(2,1)S(1)}, u32[]{:S(2)}, u32[]{:S(2)}) collective-permute-start(bf16[1,40,256]{2,1,0:T(8,128)(2,1)S(1)} %get-tuple-element.187), channel_id=1, source_target_pairs={{0,16},{4,20},{8,24},{12,28},{16,0},{20,4},{24,8},{28,12},{1,17},{... | collective-permute-start | bytes 61448 | tf_op jit(solution)/shard_map/ppermute | solution.py:565
  54.1 4.7 %collective-permute-start.18 = (bf16[1,32,256]{2,1,0:T(8,128)(2,1)S(1)}, bf16[1,32,256]{2,1,0:T(8,128)(2,1)S(1)}, u32[]{:S(2)}, u32[]{:S(2)}) collective-permute-start(bf16[1,32,256]{2,1,0:T(8,128)(2,1)S(1)} %get-tuple-element.183), channel_id=1, source_target_pairs={{0,16},{4,20},{8,24},{12,28},{16,0},{20,4},{24,8},{28,12},{1,17},{... | collective-permute-start | bytes 49160 | tf_op jit(solution)/shard_map/ppermute | solution.py:565
  58.9 4.8 %collective-permute-start.21 = (bf16[104,256]{1,0:T(8,128)(2,1)S(1)}, bf16[104,256]{1,0:T(8,128)(2,1)S(1)}, u32[]{:S(2)}, u32[]{:S(2)}) collective-permute-start(bf16[104,256]{1,0:T(8,128)(2,1)S(1)} %piece_sum.1.refs_0_), channel_id=1, source_target_pairs={{0,4},{4,0},{8,12},{12,8},{16,20},{20,16},{24,28},{28,24},{1,5},{5... | collective-permute-start | bytes 159752 | tf_op jit(solution)/shard_map/ppermute | solution.py:565
  60.5 5.0 %collective-permute-start.20 = (bf16[104,256]{1,0:T(8,128)(2,1)S(1)}, bf16[104,256]{1,0:T(8,128)(2,1)S(1)}, u32[]{:S(2)}, u32[]{:S(2)}) collective-permute-start(bf16[104,256]{1,0:T(8,128)(2,1)S(1)} %piece_sum.1.refs_0_), channel_id=1, source_target_pairs={{0,16},{4,20},{8,24},{12,28},{16,0},{20,4},{24,8},{28,12},{1,17},{... | collective-permute-start | bytes 159752 | tf_op jit(solution)/shard_map/ppermute | solution.py:565
  60.5 7.4 %collective-permute-start.22 = (bf16[104,256]{1,0:T(8,128)(2,1)S(1)}, bf16[104,256]{1,0:T(8,128)(2,1)S(1)}, u32[]{:S(2)}, u32[]{:S(2)}) collective-permute-start(bf16[104,256]{1,0:T(8,128)(2,1)S(1)} %piece_sum.1.refs_0_), channel_id=1, source_target_pairs={{0,8},{4,12},{8,0},{12,4},{16,24},{20,28},{24,16},{28,20},{1,9},{5... | collective-permute-start | bytes 159752 | tf_op jit(solution)/shard_map/ppermute | solution.py:565
  65.6 4.1 %collective-permute-start.25 = (bf16[104,256]{1,0:T(8,128)(2,1)S(1)}, bf16[104,256]{1,0:T(8,128)(2,1)S(1)}, u32[]{:S(2)}, u32[]{:S(2)}) collective-permute-start(bf16[104,256]{1,0:T(8,128)(2,1)S(1)} %collective-permute-done.20.refs_4_), channel_id=1, source_target_pairs={{0,8},{4,12},{8,0},{12,4},{16,24},{20,28},{24,16},{28,20},{1,9},{5... | collective-permute-start | bytes 159752 | tf_op jit(solution)/shard_map/ppermute | solution.py:565
  67.0 5.0 %collective-permute-start.24 = (bf16[104,256]{1,0:T(8,128)(2,1)S(1)}, bf16[104,256]{1,0:T(8,128)(2,1)S(1)}, u32[]{:S(2)}, u32[]{:S(2)}) collective-permute-start(bf16[104,256]{1,0:T(8,128)(2,1)S(1)} %collective-permute-done.20.refs_4_), channel_id=1, source_target_pairs={{0,4},{4,0},{8,12},{12,8},{16,20},{20,16},{24,28},{28,24},{1,5},{5... | collective-permute-start | bytes 159752 | tf_op jit(solution)/shard_map/ppermute | solution.py:565
  67.9 4.1 %collective-permute-start.23 = (bf16[104,256]{1,0:T(8,128)(2,1)S(1)}, bf16[104,256]{1,0:T(8,128)(2,1)S(1)}, u32[]{:S(2)}, u32[]{:S(2)}) collective-permute-start(bf16[104,256]{1,0:T(8,128)(2,1)S(1)} %collective-permute-done.22.refs_2_), channel_id=1, source_target_pairs={{0,4},{4,0},{8,12},{12,8},{16,20},{20,16},{24,28},{28,24},{1,5},{5... | collective-permute-start | bytes 159752 | tf_op jit(solution)/shard_map/ppermute | solution.py:565
  69.7 4.1 %collective-permute-start.26 = (bf16[104,256]{1,0:T(8,128)(2,1)S(1)}, bf16[104,256]{1,0:T(8,128)(2,1)S(1)}, u32[]{:S(2)}, u32[]{:S(2)}) collective-permute-start(bf16[104,256]{1,0:T(8,128)(2,1)S(1)} %collective-permute-done.25.refs_6_), channel_id=1, source_target_pairs={{0,4},{4,0},{8,12},{12,8},{16,20},{20,16},{24,28},{28,24},{1,5},{5... | collective-permute-start | bytes 159752 | tf_op jit(solution)/shard_map/ppermute | solution.py:565
  70.2 3.6 %copy-start = (f32[64,1024]{1,0:T(8,128)S(1)}, f32[64,1024]{1,0:T(8,128)}, u32[]{:S(2)}) copy-start(f32[64,1024]{1,0:T(8,128)} %refs_14_.1) | copy-start | bytes 786436
  70.2 3.6 %copy-start.1 = (f32[256,256]{1,0:T(8,128)S(1)}, f32[256,256]{1,0:T(8,128)}, u32[]{:S(2)}) copy-start(f32[256,256]{1,0:T(8,128)} %refs_17_.1) | copy-start | bytes 786436
  70.2 3.7 %copy-start.2 = (f32[64,768]{1,0:T(8,128)S(1)}, f32[64,768]{1,0:T(8,128)}, u32[]{:S(2)}) copy-start(f32[64,768]{1,0:T(8,128)} %refs_8_.1) | copy-start | bytes 589828
  70.2 3.7 %copy-start.5 = (f32[64,256]{1,0:T(8,128)S(1)}, f32[64,256]{1,0:T(8,128)}, u32[]{:S(2)}) copy-start(f32[64,256]{1,0:T(8,128)} %refs_11_.1) | copy-start | bytes 196612
  70.2 3.7 %copy-start.8 = (f32[64,1024]{1,0:T(8,128)S(1)}, f32[64,1024]{1,0:T(8,128)}, u32[]{:S(2)}) copy-start(f32[64,1024]{1,0:T(8,128)} %refs_15_.1) | copy-start | bytes 786436
  70.2 3.7 %copy-start.9 = (f32[64,1024]{1,0:T(8,128)S(1)}, f32[64,1024]{1,0:T(8,128)}, u32[]{:S(2)}) copy-start(f32[64,1024]{1,0:T(8,128)} %refs_16_.1) | copy-start | bytes 786436
  70.2 3.7 %copy-start.10 = (f32[256,256]{1,0:T(8,128)S(1)}, f32[256,256]{1,0:T(8,128)}, u32[]{:S(2)}) copy-start(f32[256,256]{1,0:T(8,128)} %refs_18_.1) | copy-start | bytes 786436
  70.3 3.7 %copy-start.11 = (f32[256,256]{1,0:T(8,128)S(1)}, f32[256,256]{1,0:T(8,128)}, u32[]{:S(2)}) copy-start(f32[256,256]{1,0:T(8,128)} %refs_19_.1) | copy-start | bytes 786436
  70.3 3.7 %copy-start.12 = (f32[64,768]{1,0:T(8,128)S(1)}, f32[64,768]{1,0:T(8,128)}, u32[]{:S(2)}) copy-start(f32[64,768]{1,0:T(8,128)} %refs_9_.1) | copy-start | bytes 589828
  70.3 3.7 %copy-start.13 = (f32[64,768]{1,0:T(8,128)S(1)}, f32[64,768]{1,0:T(8,128)}, u32[]{:S(2)}) copy-start(f32[64,768]{1,0:T(8,128)} %refs_10_.1) | copy-start | bytes 589828
  70.3 3.7 %copy-start.14 = (f32[64,256]{1,0:T(8,128)S(1)}, f32[64,256]{1,0:T(8,128)}, u32[]{:S(2)}) copy-start(f32[64,256]{1,0:T(8,128)} %refs_12_.1) | copy-start | bytes 196612
  70.3 3.7 %copy-start.15 = (f32[64,256]{1,0:T(8,128)S(1)}, f32[64,256]{1,0:T(8,128)}, u32[]{:S(2)}) copy-start(f32[64,256]{1,0:T(8,128)} %refs_13_.1) | copy-start | bytes 196612

commit v11 on v10

--- a/solution.py
+++ b/solution.py
@@ -475,13 +475,21 @@
         send_ref[pair] = sum_ref[2 * pair + 1 - side].astype(low)
 
 
-def piece_kernel(*refs):
-    parts = [
-        mine[...].reshape(mine.shape[-2:]).astype(wide)
-        + other[...].reshape(other.shape[-2:]).astype(wide)
-        for mine, other in zip(refs[:-1:2], refs[1:-1:2])
-    ]
-    refs[-1][...] = jnp.concatenate(parts, axis=0).astype(low)
+def merge_kernel(*refs):
+    target = refs[-1]
+    for index in range(target.shape[0]):
+        parts = [
+            kept[index] + arrived[index].astype(wide)
+            for kept, arrived in zip(refs[:-1:2], refs[1:-1:2])
+        ]
+        target[index] = jnp.concatenate(parts, axis=0).astype(low)
+
+
+def piece_kernel(arrived_ref, piece_ref):
+    total = arrived_ref[0].astype(wide)
+    for index in range(1, arrived_ref.shape[0]):
+        total = total + arrived_ref[index].astype(wide)
+    piece_ref[...] = total.astype(low)
 
 
 def adam_values(weight, grad, first, second, decay_rate):
@@ -605,35 +613,32 @@
     return keep, exchange(send, "dp", 1)
 
 
-def after_arrivals(early, arrival):
-    ready, arrival = lax.optimization_barrier(([flat[1] for flat in early], arrival))
-    return [[flat[0], item] for flat, item in zip(early, ready)], arrival
-
-
-def next_sum(flat, bit):
-    keep, send = halve_call("dp", bit, *flat, "halve_dp")
-    return [keep, exchange(send, "dp", 1 << bit)]
-
-
-def finish_sum(early, late, group):
+def swap_far(pieces, group):
     replicas = lax.axis_size("dp")
-    bit = 1
-    while (1 << bit) < group:
-        early = [next_sum(flat, bit) for flat in early]
-        last = (2 << bit) >= group
-        waited, ready = after_arrivals(early[:1] if last else early, late[1])
-        early = waited + early[len(waited) :]
-        late = [late[0], ready]
-        late = next_sum(late, bit)
-        bit += 1
-    flat = [item for chunk in early + [late] for item in chunk]
-    width = flat[0].shape[-1]
-    rows = sum(item.shape[1] for item in flat[::2])
-    (piece,) = local_call(piece_kernel, [((rows, width), low)], flat, name="piece_sum")
+    groups = [
+        list(range(base + side, base + group, 2))
+        for base in range(0, replicas, group)
+        for side in range(2)
+    ]
+    return lax.all_to_all(pieces, "dp", 0, 0, axis_index_groups=groups, tiled=True)
+
+
+def finish_sum(chunks, group):
+    replicas = lax.axis_size("dp")
+    width = chunks[0][0].shape[-1]
+    rows = sum(chunk[0].shape[1] for chunk in chunks)
+    flat = [item for chunk in chunks for item in chunk]
+    (pieces,) = local_call(
+        merge_kernel, [((group // 2, rows, width), low)], flat, name="merge_chunks"
+    )
+    arrived = swap_far(pieces, group)
+    (piece,) = local_call(piece_kernel, [((rows, width), low)], [arrived], name="piece_sum")
     mask = group
     while mask < replicas:
         other = exchange(piece, "dp", mask)
-        (piece,) = local_call(piece_kernel, [((rows, width), low)], [piece, other], name="far_sum")
+        (piece,) = local_call(
+            piece_kernel, [((rows, width), low)], [jnp.stack([piece, other])], name="far_sum"
+        )
         mask *= 2
     return gather_pieces(piece, group)
 
@@ -791,14 +796,9 @@
         name="feed_last",
     )
     attended_grad, arrived_ffn = lax.optimization_barrier((attended_grad, arrived_ffn))
-    keep_down, send_down, keep_up, send_up = halve_call(
-        "shard", 1, kept_ffn, arrived_ffn, "halve_ffn", [down_rows, up_rows]
-    )
-    attended_grad, send_down, send_up = lax.optimization_barrier(
-        (attended_grad, send_down, send_up)
-    )
-    arrived_down = exchange(send_down, "shard", 2)
-    arrived_up = exchange(send_up, "shard", 2)
+    keep_ffn, send_ffn = halve_call("shard", 1, kept_ffn, arrived_ffn, "halve_ffn")
+    attended_grad, send_ffn = lax.optimization_barrier((attended_grad, send_ffn))
+    arrived_ffn = exchange(send_ffn, "shard", 2)
     tail = TILE_ROWS
     att_rows = 4 * part + tail
     pair = (shards // 2, att_rows, width)
@@ -820,24 +820,21 @@
         flops=heads * rows * rows * 256 * 10,
         name="back",
     )
-    send_att, arrived_down, arrived_up = lax.optimization_barrier(
-        (send_att, arrived_down, arrived_up)
-    )
+    send_att, arrived_ffn = lax.optimization_barrier((send_att, arrived_ffn))
     arrived_att = exchange(send_att, "shard", 1)
     keep_att, send_att = halve_call("shard", 1, kept_att, arrived_att, "halve_att")
+    send_att, arrived_ffn = lax.optimization_barrier((send_att, arrived_ffn))
     arrived_att = exchange(send_att, "shard", 2)
-    early = [
-        split_chunk([keep_down[0], arrived_down[0]], 0, group),
-        split_chunk([keep_up[0], arrived_up[0]], 0, group),
+    chunks = [
+        split_chunk([keep_ffn[0], arrived_ffn[0]], 0, group),
+        split_chunk([keep_att[0], arrived_att[0]], tail, group),
     ]
-    early, arrived_att = after_arrivals(early, arrived_att)
-    late = split_chunk([keep_att[0], arrived_att[0]], tail, group)
-    pieces = finish_sum(early, late, group)
+    pieces = finish_sum(chunks, group)
     second_at = down_rows + up_rows
     results = adam_call(
         pieces,
-        (down_rows, up_rows, att_rows),
-        (0, 0, tail),
+        (second_at, att_rows),
+        (0, tail),
         [
             (qkv_weight, qkv_first, qkv_second),
             (out_weight, out_first, out_second),

time: 76.1 us -> 72.4 us (0.951)
  blocking collectives: 0 us -> 11.6 us
  starting transfers between devices: 26.1 us -> 15 us
  waiting for transfers between devices: 28.3 us -> 24.3 us
    all_to_all x0 -> x1, blocking collectives: none -> 11.6 us  [swap_far(): lax.all_to_all(pieces, 'dp', 0, 0, axis_index_groups=groups, tiled=True)]
    ppermute x27 -> x19, starting transfers between devices: 26.1 us -> 15 us  [exchange(): lax.ppermute(values, axis, [(index, index ^ mask) for index in range(coun...]
    ppermute x27 -> x19, waiting for transfers between devices: 28.3 us -> 24.3 us  [exchange(): lax.ppermute(values, axis, [(index, index ^ mask) for index in range(coun...]
    pallas_call x21 -> x15, Pallas kernels: 20.3 us -> 20 us  [local_call(): pl.pallas_call(kernel, out_shape=outs, in_specs=[pl.BlockSpec(memory_spac...]
  transfers between devices with their start and end apart: 27 -> 19, of which waited for: 18 -> 13; matrix products, arithmetic and copies ran while one was open for 0% -> 0% of each run, Pallas kernels for 18% -> 18%
where the time goes in v11:
time: 72.4 us; the launch traced here: 72.2 us
  waiting for transfers between devices  24.3 us (34%)
  Pallas kernels  20 us (28%)
  starting transfers between devices  15 us (21%)
  blocking collectives  11.6 us (16%)
  between operations  1.15 us (2%)
    ppermute x19, waiting for transfers between devices, exchange(): lax.ppermute(values, axis, [(index, index ^ mask) for index in range(coun...  24.3 us
    pallas_call x15, Pallas kernels, local_call(): pl.pallas_call(kernel, out_shape=outs, in_specs=[pl.BlockSpec(memory_spac...  20 us
    ppermute x19, starting transfers between devices, exchange(): lax.ppermute(values, axis, [(index, index ^ mask) for index in range(coun...  15 us
    all_to_all x1, blocking collectives, swap_far(): lax.all_to_all(pieces, 'dp', 0, 0, axis_index_groups=groups, tiled=True)  11.6 us
  transfers between devices with their start and end apart: 19, of which 13 were waited for; matrix products, arithmetic and copies ran while one was open for 0% of the time, Pallas kernels for 18%

profile of v11, /device:TPU:0, one launch (start us, length us, event | category | flops | bytes accessed | tf_op | source)
XLA Modules:
  0.0 72.2 jit_solution(1906843448704498968)
XLA Ops:
  0.7 1.6 %pack_first.1.refs_2_.refs_3_.refs_7_.refs_10_ = bf16[208,256]{1,0:T(8,128)(2,1)} custom-call(f32[64,768]{1,0:T(8,128)} %refs_8_.1, f32[768]{0:T(1024)} %refs_20_.1), custom_call_target="tpu_custom_call" | custom-call | bytes 306176 | tf_op jit(solution)/shard_map/pack_first/pallas_call | solution.py:559
  2.3 0.0 copy-start.6
  2.3 0.0 copy-start.7
  2.3 3.0 %collective-permute-start = (bf16[208,256]{1,0:T(8,128)(2,1)}, bf16[208,256]{1,0:T(8,128)(2,1)S(1)}, u32[]{:S(2)}, u32[]{:S(2)}) collective-permute-start(bf16[208,256]{1,0:T(8,128)(2,1)} %pack_first.1.refs_2_.refs_3_.refs_7_.refs_10_), channel_id=1, source_target_pairs={{0,2},{1,3},{2,0},{3,1},{4,6},{5,7},{6,4},{7,5},{8,10},{9,11},{10,... | collective-permute-start | bytes 319496 | tf_op jit(solution)/shard_map/ppermute | solution.py:573
  5.3 1.8 %pack_second.1.refs_7_ = bf16[576,256]{1,0:T(8,128)(2,1)} custom-call(f32[64,256]{1,0:T(8,128)} %refs_11_.1, f32[64,1024]{1,0:T(8,128)} %refs_14_.1, f32[256,256]{1,0:T(8,128)} %refs_17_.1), custom_call_target="tpu_custom_call" | custom-call | bytes 884736 | tf_op jit(solution)/shard_map/pack_second/pallas_call | solution.py:559
  7.2 0.2 collective-permute-start.3
  7.4 0.6 prepare.1
  8.1 0.4 collective-permute-done.refs_4_.refs_5_.refs_9_.refs_12_
  8.5 0.1 collective-permute-start.2
  8.6 0.4 collective-permute-start.4
  9.0 0.8 %collective-permute-done.2.refs_5_.refs_6_.refs_10_.refs_13_ = bf16[208,256]{1,0:T(8,128)(2,1)S(1)} collective-permute-done((bf16[208,256]{1,0:T(8,128)(2,1)S(1)}, bf16[208,256]{1,0:T(8,128)(2,1)S(1)}, u32[]{:S(2)}, u32[]{:S(2)}) %collective-permute-start.2) | collective-permute-done | bytes 106528 | tf_op jit(solution)/shard_map/ppermute | solution.py:573
  9.8 2.9 %attend.1 = (bf16[512,768]{1,0:T(8,128)(2,1)S(1)}, bf16[512,256]{1,0:T(8,128)(2,1)S(1)}, f32[8,512]{1,0:T(8,128)S(1)}, f32[256,512]{1,0:T(8,128)S(1)}) custom-call(f32[512,256]{1,0:T(8,128)S(1)} %get-tuple-element.95.refs_0_.refs_5_, f32[512,512]{1,0:T(8,128)S(1)} %get-tuple-element.96.refs_1_.refs_3_, bf16[208,256]{1,0:T(8,128)(2,1)S(1)} %copy-done.3, ...), custom_call_target="tpu_custom_call" | custom-call | flops 1342177280 | bytes 3588096 | tf_op jit(solution)/shard_map/attend/pallas_call | solution.py:559
  12.8 3.2 %collective-permute-done.3.refs_9_ = bf16[576,256]{1,0:T(8,128)(2,1)S(1)} collective-permute-done((bf16[576,256]{1,0:T(8,128)(2,1)}, bf16[576,256]{1,0:T(8,128)(2,1)S(1)}, u32[]{:S(2)}, u32[]{:S(2)}) %collective-permute-start.3) | collective-permute-done | bytes 294944 | tf_op jit(solution)/shard_map/ppermute | solution.py:573
  16.0 1.6 %collective-permute-done.5.refs_10_ = bf16[576,256]{1,0:T(8,128)(2,1)S(1)} collective-permute-done((bf16[576,256]{1,0:T(8,128)(2,1)S(1)}, bf16[576,256]{1,0:T(8,128)(2,1)S(1)}, u32[]{:S(2)}, u32[]{:S(2)}) %collective-permute-start.5) | collective-permute-done | bytes 294944 | tf_op jit(solution)/shard_map/ppermute | solution.py:573
  17.5 3.0 %feed_first.1 = (bf16[512,1024]{1,0:T(8,128)(2,1)S(1)}, f32[512,256]{1,0:T(8,128)S(1)}, f32[512,256]{1,0:T(8,128)S(1)}, f32[512,256]{1,0:T(8,128)S(1)}, f32[512,...) custom-call(bf16[512,256]{1,0:T(8,128)(2,1)S(1)} %copy-done.7, ...), custom_call_target="tpu_custom_call" | custom-call | flops 1342177280 | bytes 7260160 | tf_op jit(solution)/shard_map/feed_first/pallas_call | solution.py:559
  20.5 0.2 collective-permute-start.6
  20.7 0.7 feed_last.1
  21.4 1.1 %collective-permute-done.6.arrived = bf16[2,512,256]{2,1,0:T(8,128)(2,1)S(1)} collective-permute-done((bf16[2,512,256]{2,1,0:T(8,128)(2,1)S(1)}, bf16[2,512,256]{2,1,0:T(8,128)(2,1)S(1)}, u32[]{:S(2)}, u32[]{:S(2)}) %collective-permute-start.6) | collective-permute-done | bytes 524320 | tf_op jit(solution)/shard_map/ppermute | solution.py:573
  22.5 0.1 halve_ffn.1
  22.6 0.7 collective-permute-start.7
  23.3 5.9 %back.1 = (f32[512,256]{1,0:T(8,128)}, f32[2,264,256]{2,1,0:T(8,128)S(1)}, bf16[2,264,256]{2,1,0:T(8,128)(2,1)S(1)}) custom-call(bf16[512,768]{1,0:T(8,128)(2,1)S(1)} %get-tuple-element.106.refs_0_, bf16[512,256]{1,0:T(8,128)(2,1)S(1)} %get-tuple-element.118.refs_1_, f32[8,512]{1,0:T(8,128)S(1)} %get-tuple-element.119.refs_2_, ...), custom_call_target="tpu_custom_call" | custom-call | flops 5368709120 | bytes 5728256 | tf_op jit(solution)/shard_map/back/pallas_call | solution.py:559
  29.2 1.8 %collective-permute-done.7 = bf16[1,512,256]{2,1,0:T(8,128)(2,1)S(1)} collective-permute-done((bf16[1,512,256]{2,1,0:T(8,128)(2,1)S(1)}, bf16[1,512,256]{2,1,0:T(8,128)(2,1)S(1)}, u32[]{:S(2)}, u32[]{:S(2)}) %collective-permute-start.7) | collective-permute-done | bytes 262176 | tf_op jit(solution)/shard_map/ppermute | solution.py:573
  31.0 1.5 %collective-permute-done.8.arrived = bf16[2,264,256]{2,1,0:T(8,128)(2,1)S(1)} collective-permute-done((bf16[2,264,256]{2,1,0:T(8,128)(2,1)S(1)}, bf16[2,264,256]{2,1,0:T(8,128)(2,1)S(1)}, u32[]{:S(2)}, u32[]{:S(2)}) %collective-permute-start.8) | collective-permute-done | bytes 270368 | tf_op jit(solution)/shard_map/ppermute | solution.py:573
  32.6 0.1 halve_att.1
  32.6 0.7 collective-permute-start.10
  33.3 0.1 split_sum.2
  33.4 1.6 %collective-permute-start.9 = (bf16[4,64,256]{2,1,0:T(8,128)(2,1)S(1)}, bf16[4,64,256]{2,1,0:T(8,128)(2,1)S(1)}, u32[]{:S(2)}, u32[]{:S(2)}) collective-permute-start(bf16[4,64,256]{2,1,0:T(8,128)(2,1)S(1)} %get-tuple-element.135), channel_id=1, source_target_pairs={{0,4},{4,0},{8,12},{12,8},{16,20},{20,16},{24,28},{28,24},{1,5},{5... | collective-permute-start | bytes 393224 | tf_op jit(solution)/shard_map/ppermute | solution.py:573
  35.0 3.3 %collective-permute-done.10 = bf16[1,264,256]{2,1,0:T(8,128)(2,1)S(1)} collective-permute-done((bf16[1,264,256]{2,1,0:T(8,128)(2,1)S(1)}, bf16[1,264,256]{2,1,0:T(8,128)(2,1)S(1)}, u32[]{:S(2)}, u32[]{:S(2)}) %collective-permute-start.10) | collective-permute-done | bytes 135200 | tf_op jit(solution)/shard_map/ppermute | solution.py:573
  38.3 0.1 split_sum.3
  38.4 1.6 %collective-permute-start.11 = (bf16[4,40,256]{2,1,0:T(8,128)(2,1)S(1)}, bf16[4,40,256]{2,1,0:T(8,128)(2,1)S(1)}, u32[]{:S(2)}, u32[]{:S(2)}) collective-permute-start(bf16[4,40,256]{2,1,0:T(8,128)(2,1)S(1)} %get-tuple-element.139), channel_id=1, source_target_pairs={{0,4},{4,0},{8,12},{12,8},{16,20},{20,16},{24,28},{28,24},{1,5},{5... | collective-permute-start | bytes 245768 | tf_op jit(solution)/shard_map/ppermute | solution.py:573
  39.9 2.9 %collective-permute-done.11.refs_3_ = bf16[4,40,256]{2,1,0:T(8,128)(2,1)S(1)} collective-permute-done((bf16[4,40,256]{2,1,0:T(8,128)(2,1)S(1)}, bf16[4,40,256]{2,1,0:T(8,128)(2,1)S(1)}, u32[]{:S(2)}, u32[]{:S(2)}) %collective-permute-start.11) | collective-permute-done | bytes 81952 | tf_op jit(solution)/shard_map/ppermute | solution.py:573
  42.9 0.1 merge_chunks.1
  42.9 0.0 copy-start.16
  43.0 11.6 %all_to_all.5.arrived_ref = bf16[4,104,256]{2,1,0:T(8,128)(2,1)S(1)} all-to-all(bf16[4,104,256]{2,1,0:T(8,128)(2,1)S(1)} %merge_chunks.1), channel_id=1, replica_groups={{0,8,16,24},{4,12,20,28},{1,9,17,25},{5,13,21,29},{2,10,18,26},{6,14,22..., dimensions={0} | all-to-all | bytes 425984 | tf_op jit(solution)/shard_map/all_to_all | solution.py:623
  54.7 1.6 %collective-permute-start.13 = (bf16[104,256]{1,0:T(8,128)(2,1)S(1)}, bf16[104,256]{1,0:T(8,128)(2,1)S(1)}, u32[]{:S(2)}, u32[]{:S(2)}) collective-permute-start(bf16[104,256]{1,0:T(8,128)(2,1)S(1)} %piece_sum.1.refs_0_), channel_id=1, source_target_pairs={{0,4},{4,0},{8,12},{12,8},{16,20},{20,16},{24,28},{28,24},{1,5},{5... | collective-permute-start | bytes 159752 | tf_op jit(solution)/shard_map/ppermute | solution.py:573
  56.2 0.8 %collective-permute-start.12 = (bf16[104,256]{1,0:T(8,128)(2,1)S(1)}, bf16[104,256]{1,0:T(8,128)(2,1)S(1)}, u32[]{:S(2)}, u32[]{:S(2)}) collective-permute-start(bf16[104,256]{1,0:T(8,128)(2,1)S(1)} %piece_sum.1.refs_0_), channel_id=1, source_target_pairs={{0,16},{4,20},{8,24},{12,28},{16,0},{20,4},{24,8},{28,12},{1,17},{... | collective-permute-start | bytes 159752 | tf_op jit(solution)/shard_map/ppermute | solution.py:573
  57.0 1.1 %collective-permute-start.14 = (bf16[104,256]{1,0:T(8,128)(2,1)S(1)}, bf16[104,256]{1,0:T(8,128)(2,1)S(1)}, u32[]{:S(2)}, u32[]{:S(2)}) collective-permute-start(bf16[104,256]{1,0:T(8,128)(2,1)S(1)} %piece_sum.1.refs_0_), channel_id=1, source_target_pairs={{0,8},{4,12},{8,0},{12,4},{16,24},{20,28},{24,16},{28,20},{1,9},{5... | collective-permute-start | bytes 159752 | tf_op jit(solution)/shard_map/ppermute | solution.py:573
  58.1 0.7 collective-permute-done.13.refs_1_
  58.9 3.0 %collective-permute-done.12.refs_4_ = bf16[104,256]{1,0:T(8,128)(2,1)S(1)} collective-permute-done((bf16[104,256]{1,0:T(8,128)(2,1)S(1)}, bf16[104,256]{1,0:T(8,128)(2,1)S(1)}, u32[]{:S(2)}, u32[]{:S(2)}) %collective-permute-start.12) | collective-permute-done | bytes 53280 | tf_op jit(solution)/shard_map/ppermute | solution.py:573
  61.8 0.5 collective-permute-start.17
  62.3 0.5 collective-permute-start.16
  62.9 1.5 %collective-permute-start.15 = (bf16[104,256]{1,0:T(8,128)(2,1)S(1)}, bf16[104,256]{1,0:T(8,128)(2,1)S(1)}, u32[]{:S(2)}, u32[]{:S(2)}) collective-permute-start(bf16[104,256]{1,0:T(8,128)(2,1)S(1)} %collective-permute-done.14.refs_2_), channel_id=1, source_target_pairs={{0,4},{4,0},{8,12},{12,8},{16,20},{20,16},{24,28},{28,24},{1,5},{5... | collective-permute-start | bytes 159752 | tf_op jit(solution)/shard_map/ppermute | solution.py:573
  64.4 1.6 %collective-permute-done.17.refs_6_ = bf16[104,256]{1,0:T(8,128)(2,1)S(1)} collective-permute-done((bf16[104,256]{1,0:T(8,128)(2,1)S(1)}, bf16[104,256]{1,0:T(8,128)(2,1)S(1)}, u32[]{:S(2)}, u32[]{:S(2)}) %collective-permute-start.17) | collective-permute-done | bytes 53280 | tf_op jit(solution)/shard_map/ppermute | solution.py:573
  65.9 0.5 collective-permute-start.18
  66.5 0.0 copy-start.10
  66.6 1.1 %output.1 = bf16[512,256]{1,0:T(8,128)(2,1)} custom-call(f32[512,256]{1,0:T(8,128)S(1)} %get-tuple-element.103.base_ref, bf16[512,1024]{1,0:T(8,128)(2,1)S(1)} %get-tuple-element.104.act_ref, bf16[1024,256]{1,0:T(8,128)(2,1)S(1)} %get-tuple-element.105.down_w), custom_call_target="tpu_custom_call" | custom-call | flops 268435456 | bytes 2359296 | tf_op jit(solution)/shard_map/output/pallas_call | solution.py:559
  67.7 2.3 %collective-permute-done.18.refs_7_ = bf16[104,256]{1,0:T(8,128)(2,1)S(1)} collective-permute-done((bf16[104,256]{1,0:T(8,128)(2,1)S(1)}, bf16[104,256]{1,0:T(8,128)(2,1)S(1)}, u32[]{:S(2)}, u32[]{:S(2)}) %collective-permute-start.18) | collective-permute-done | bytes 53280 | tf_op jit(solution)/shard_map/ppermute | solution.py:573
  70.2 1.8 %adam.1 = (f32[64,768]{1,0:T(8,128)}, f32[64,768]{1,0:T(8,128)}, f32[64,768]{1,0:T(8,128)}, f32[64,256]{1,0:T(8,128)}, f32[64,256]{1,0:T(8,128)}, /*index=5*/f32...) custom-call(bf16[104,256]{1,0:T(8,128)(2,1)S(1)} %piece_sum.1.refs_0, ...), custom_call_target="tpu_custom_call" | custom-call | bytes 5163008 | tf_op jit(solution)/shard_map/adam/pallas_call | solution.py:559
  (48 shorter events, 0.2 us)
Async XLA Ops:
  2.3 5.1 %copy-start.3 = (bf16[208,256]{1,0:T(8,128)(2,1)S(1)}, bf16[208,256]{1,0:T(8,128)(2,1)}, u32[]{:S(2)}) copy-start(bf16[208,256]{1,0:T(8,128)(2,1)} %pack_first.1.refs_2_.refs_3_.refs_7_.refs_10_) | copy-start | bytes 319492
  2.3 5.1 %copy-start.6 = (bf16[512,256]{1,0:T(8,128)(2,1)S(1)}, bf16[512,256]{1,0:T(8,128)(2,1)}, u32[]{:S(2)}) copy-start(bf16[512,256]{1,0:T(8,128)(2,1)} %seed_ref.1) | copy-start | bytes 786436
  2.3 5.1 %copy-start.7 = (bf16[512,256]{1,0:T(8,128)(2,1)S(1)}, bf16[512,256]{1,0:T(8,128)(2,1)}, u32[]{:S(2)}) copy-start(bf16[512,256]{1,0:T(8,128)(2,1)} %refs_0_.1) | copy-start | bytes 786436
  2.3 6.2 %collective-permute-start = (bf16[208,256]{1,0:T(8,128)(2,1)}, bf16[208,256]{1,0:T(8,128)(2,1)S(1)}, u32[]{:S(2)}, u32[]{:S(2)}) collective-permute-start(bf16[208,256]{1,0:T(8,128)(2,1)} %pack_first.1.refs_2_.refs_3_.refs_7_.refs_10_), channel_id=1, source_target_pairs={{0,2},{1,3},{2,0},{3,1},{4,6},{5,7},{6,4},{7,5},{8,10},{9,11},{10,... | collective-permute-start | bytes 319496 | tf_op jit(solution)/shard_map/ppermute | solution.py:573
  5.3 2.1 %copy-start.19 = (s32[128]{0:T(128)S(1)}, s32[128]{0:T(128)}, u32[]{:S(2)}) copy-start(s32[128]{0:T(128)} %param.21) | copy-start | bytes 1540
  5.3 2.1 %copy-start.20 = (s32[128]{0:T(128)S(1)}, s32[128]{0:T(128)}, u32[]{:S(2)}) copy-start(s32[128]{0:T(128)} %param.22) | copy-start | bytes 1540
  7.2 1.4 %copy-start.4 = (bf16[576,256]{1,0:T(8,128)(2,1)S(1)}, bf16[576,256]{1,0:T(8,128)(2,1)}, u32[]{:S(2)}) copy-start(bf16[576,256]{1,0:T(8,128)(2,1)} %pack_second.1.refs_7_) | copy-start | bytes 884740
  7.2 8.7 %collective-permute-start.3 = (bf16[576,256]{1,0:T(8,128)(2,1)}, bf16[576,256]{1,0:T(8,128)(2,1)S(1)}, u32[]{:S(2)}, u32[]{:S(2)}) collective-permute-start(bf16[576,256]{1,0:T(8,128)(2,1)} %pack_second.1.refs_7_), channel_id=1, source_target_pairs={{0,2},{1,3},{2,0},{3,1},{4,6},{5,7},{6,4},{7,5},{8,10},{9,11},{10,... | collective-permute-start | bytes 884744 | tf_op jit(solution)/shard_map/ppermute | solution.py:573
  7.4 1.7 %collective-permute-start.1 = (bf16[208,256]{1,0:T(8,128)(2,1)S(1)}, bf16[208,256]{1,0:T(8,128)(2,1)S(1)}, u32[]{:S(2)}, u32[]{:S(2)}) collective-permute-start(bf16[208,256]{1,0:T(8,128)(2,1)S(1)} %copy-done.3), channel_id=1, source_target_pairs={{0,1},{1,0},{2,3},{3,2},{4,5},{5,4},{6,7},{7,6},{8,9},{9,8},{10,11... | collective-permute-start | bytes 319496 | tf_op jit(solution)/shard_map/ppermute | solution.py:573
  8.5 1.3 %collective-permute-start.2 = (bf16[208,256]{1,0:T(8,128)(2,1)S(1)}, bf16[208,256]{1,0:T(8,128)(2,1)S(1)}, u32[]{:S(2)}, u32[]{:S(2)}) collective-permute-start(bf16[208,256]{1,0:T(8,128)(2,1)S(1)} %collective-permute-done.refs_4_.refs_5_.refs_9_.refs_12_), channel_id=1, source_target_pairs={{0,1},{1,0},{2,3},{3,2},{4,5},{5,4},{6,7},{7,6},{8,9},{9,8},{10,11... | collective-permute-start | bytes 319496 | tf_op jit(solution)/shard_map/ppermute | solution.py:573
  8.6 7.3 %collective-permute-start.4 = (bf16[576,256]{1,0:T(8,128)(2,1)S(1)}, bf16[576,256]{1,0:T(8,128)(2,1)S(1)}, u32[]{:S(2)}, u32[]{:S(2)}) collective-permute-start(bf16[576,256]{1,0:T(8,128)(2,1)S(1)} %copy-done.4), channel_id=1, source_target_pairs={{0,1},{1,0},{2,3},{3,2},{4,5},{5,4},{6,7},{7,6},{8,9},{9,8},{10,11... | collective-permute-start | bytes 884744 | tf_op jit(solution)/shard_map/ppermute | solution.py:573
  16.0 1.6 %collective-permute-start.5 = (bf16[576,256]{1,0:T(8,128)(2,1)S(1)}, bf16[576,256]{1,0:T(8,128)(2,1)S(1)}, u32[]{:S(2)}, u32[]{:S(2)}) collective-permute-start(bf16[576,256]{1,0:T(8,128)(2,1)S(1)} %collective-permute-done.3.refs_9_), channel_id=1, source_target_pairs={{0,1},{1,0},{2,3},{3,2},{4,5},{5,4},{6,7},{7,6},{8,9},{9,8},{10,11... | collective-permute-start | bytes 884744 | tf_op jit(solution)/shard_map/ppermute | solution.py:573
  20.5 2.0 %collective-permute-start.6 = (bf16[2,512,256]{2,1,0:T(8,128)(2,1)S(1)}, bf16[2,512,256]{2,1,0:T(8,128)(2,1)S(1)}, u32[]{:S(2)}, u32[]{:S(2)}) collective-permute-start(bf16[2,512,256]{2,1,0:T(8,128)(2,1)S(1)} %get-tuple-element.113), channel_id=1, source_target_pairs={{0,1},{1,0},{2,3},{3,2},{4,5},{5,4},{6,7},{7,6},{8,9},{9,8},{10,11... | collective-permute-start | bytes 1572872 | tf_op jit(solution)/shard_map/ppermute | solution.py:573
  22.6 8.4 %collective-permute-start.7 = (bf16[1,512,256]{2,1,0:T(8,128)(2,1)S(1)}, bf16[1,512,256]{2,1,0:T(8,128)(2,1)S(1)}, u32[]{:S(2)}, u32[]{:S(2)}) collective-permute-start(bf16[1,512,256]{2,1,0:T(8,128)(2,1)S(1)} %get-tuple-element.129), channel_id=1, source_target_pairs={{0,2},{1,3},{2,0},{3,1},{4,6},{5,7},{6,4},{7,5},{8,10},{9,11},{10,... | collective-permute-start | bytes 786440 | tf_op jit(solution)/shard_map/ppermute | solution.py:573
  31.0 1.5 %collective-permute-start.8 = (bf16[2,264,256]{2,1,0:T(8,128)(2,1)S(1)}, bf16[2,264,256]{2,1,0:T(8,128)(2,1)S(1)}, u32[]{:S(2)}, u32[]{:S(2)}) collective-permute-start(bf16[2,264,256]{2,1,0:T(8,128)(2,1)S(1)} %get-tuple-element.130), channel_id=1, source_target_pairs={{0,1},{1,0},{2,3},{3,2},{4,5},{5,4},{6,7},{7,6},{8,9},{9,8},{10,11... | collective-permute-start | bytes 811016 | tf_op jit(solution)/shard_map/ppermute | solution.py:573
  32.6 5.7 %collective-permute-start.10 = (bf16[1,264,256]{2,1,0:T(8,128)(2,1)S(1)}, bf16[1,264,256]{2,1,0:T(8,128)(2,1)S(1)}, u32[]{:S(2)}, u32[]{:S(2)}) collective-permute-start(bf16[1,264,256]{2,1,0:T(8,128)(2,1)S(1)} %get-tuple-element.137), channel_id=1, source_target_pairs={{0,2},{1,3},{2,0},{3,1},{4,6},{5,7},{6,4},{7,5},{8,10},{9,11},{10,... | collective-permute-start | bytes 405512 | tf_op jit(solution)/shard_map/ppermute | solution.py:573
  33.4 6.5 %collective-permute-start.9 = (bf16[4,64,256]{2,1,0:T(8,128)(2,1)S(1)}, bf16[4,64,256]{2,1,0:T(8,128)(2,1)S(1)}, u32[]{:S(2)}, u32[]{:S(2)}) collective-permute-start(bf16[4,64,256]{2,1,0:T(8,128)(2,1)S(1)} %get-tuple-element.135), channel_id=1, source_target_pairs={{0,4},{4,0},{8,12},{12,8},{16,20},{20,16},{24,28},{28,24},{1,5},{5... | collective-permute-start | bytes 393224 | tf_op jit(solution)/shard_map/ppermute | solution.py:573
  38.4 4.5 %collective-permute-start.11 = (bf16[4,40,256]{2,1,0:T(8,128)(2,1)S(1)}, bf16[4,40,256]{2,1,0:T(8,128)(2,1)S(1)}, u32[]{:S(2)}, u32[]{:S(2)}) collective-permute-start(bf16[4,40,256]{2,1,0:T(8,128)(2,1)S(1)} %get-tuple-element.139), channel_id=1, source_target_pairs={{0,4},{4,0},{8,12},{12,8},{16,20},{20,16},{24,28},{28,24},{1,5},{5... | collective-permute-start | bytes 245768 | tf_op jit(solution)/shard_map/ppermute | solution.py:573
  42.9 27.1 %copy-start.16 = (f32[768]{0:T(1024)S(1)}, f32[768]{0:T(1024)}, u32[]{:S(2)}) copy-start(f32[768]{0:T(1024)} %refs_20_.1) | copy-start | bytes 9220
  42.9 27.1 %copy-start.17 = (f32[768]{0:T(1024)S(1)}, f32[768]{0:T(1024)}, u32[]{:S(2)}) copy-start(f32[768]{0:T(1024)} %refs_21_.1) | copy-start | bytes 9220
  43.0 27.1 %copy-start.18 = (f32[768]{0:T(1024)S(1)}, f32[768]{0:T(1024)}, u32[]{:S(2)}) copy-start(f32[768]{0:T(1024)} %refs_22_.1) | copy-start | bytes 9220
  54.7 4.2 %collective-permute-start.13 = (bf16[104,256]{1,0:T(8,128)(2,1)S(1)}, bf16[104,256]{1,0:T(8,128)(2,1)S(1)}, u32[]{:S(2)}, u32[]{:S(2)}) collective-permute-start(bf16[104,256]{1,0:T(8,128)(2,1)S(1)} %piece_sum.1.refs_0_), channel_id=1, source_target_pairs={{0,4},{4,0},{8,12},{12,8},{16,20},{20,16},{24,28},{28,24},{1,5},{5... | collective-permute-start | bytes 159752 | tf_op jit(solution)/shard_map/ppermute | solution.py:573
  56.2 5.6 %collective-permute-start.12 = (bf16[104,256]{1,0:T(8,128)(2,1)S(1)}, bf16[104,256]{1,0:T(8,128)(2,1)S(1)}, u32[]{:S(2)}, u32[]{:S(2)}) collective-permute-start(bf16[104,256]{1,0:T(8,128)(2,1)S(1)} %piece_sum.1.refs_0_), channel_id=1, source_target_pairs={{0,16},{4,20},{8,24},{12,28},{16,0},{20,4},{24,8},{28,12},{1,17},{... | collective-permute-start | bytes 159752 | tf_op jit(solution)/shard_map/ppermute | solution.py:573
  57.0 5.9 %collective-permute-start.14 = (bf16[104,256]{1,0:T(8,128)(2,1)S(1)}, bf16[104,256]{1,0:T(8,128)(2,1)S(1)}, u32[]{:S(2)}, u32[]{:S(2)}) collective-permute-start(bf16[104,256]{1,0:T(8,128)(2,1)S(1)} %piece_sum.1.refs_0_), channel_id=1, source_target_pairs={{0,8},{4,12},{8,0},{12,4},{16,24},{20,28},{24,16},{28,20},{1,9},{5... | collective-permute-start | bytes 159752 | tf_op jit(solution)/shard_map/ppermute | solution.py:573
  61.8 4.1 %collective-permute-start.17 = (bf16[104,256]{1,0:T(8,128)(2,1)S(1)}, bf16[104,256]{1,0:T(8,128)(2,1)S(1)}, u32[]{:S(2)}, u32[]{:S(2)}) collective-permute-start(bf16[104,256]{1,0:T(8,128)(2,1)S(1)} %collective-permute-done.12.refs_4_), channel_id=1, source_target_pairs={{0,8},{4,12},{8,0},{12,4},{16,24},{20,28},{24,16},{28,20},{1,9},{5... | collective-permute-start | bytes 159752 | tf_op jit(solution)/shard_map/ppermute | solution.py:573
  62.3 5.4 %collective-permute-start.16 = (bf16[104,256]{1,0:T(8,128)(2,1)S(1)}, bf16[104,256]{1,0:T(8,128)(2,1)S(1)}, u32[]{:S(2)}, u32[]{:S(2)}) collective-permute-start(bf16[104,256]{1,0:T(8,128)(2,1)S(1)} %collective-permute-done.12.refs_4_), channel_id=1, source_target_pairs={{0,4},{4,0},{8,12},{12,8},{16,20},{20,16},{24,28},{28,24},{1,5},{5... | collective-permute-start | bytes 159752 | tf_op jit(solution)/shard_map/ppermute | solution.py:573
  62.9 4.9 %collective-permute-start.15 = (bf16[104,256]{1,0:T(8,128)(2,1)S(1)}, bf16[104,256]{1,0:T(8,128)(2,1)S(1)}, u32[]{:S(2)}, u32[]{:S(2)}) collective-permute-start(bf16[104,256]{1,0:T(8,128)(2,1)S(1)} %collective-permute-done.14.refs_2_), channel_id=1, source_target_pairs={{0,4},{4,0},{8,12},{12,8},{16,20},{20,16},{24,28},{28,24},{1,5},{5... | collective-permute-start | bytes 159752 | tf_op jit(solution)/shard_map/ppermute | solution.py:573
  65.9 4.1 %collective-permute-start.18 = (bf16[104,256]{1,0:T(8,128)(2,1)S(1)}, bf16[104,256]{1,0:T(8,128)(2,1)S(1)}, u32[]{:S(2)}, u32[]{:S(2)}) collective-permute-start(bf16[104,256]{1,0:T(8,128)(2,1)S(1)} %collective-permute-done.17.refs_6_), channel_id=1, source_target_pairs={{0,4},{4,0},{8,12},{12,8},{16,20},{20,16},{24,28},{28,24},{1,5},{5... | collective-permute-start | bytes 159752 | tf_op jit(solution)/shard_map/ppermute | solution.py:573
  66.5 3.6 %copy-start = (f32[64,1024]{1,0:T(8,128)S(1)}, f32[64,1024]{1,0:T(8,128)}, u32[]{:S(2)}) copy-start(f32[64,1024]{1,0:T(8,128)} %refs_14_.1) | copy-start | bytes 786436
  66.5 3.6 %copy-start.1 = (f32[256,256]{1,0:T(8,128)S(1)}, f32[256,256]{1,0:T(8,128)}, u32[]{:S(2)}) copy-start(f32[256,256]{1,0:T(8,128)} %refs_17_.1) | copy-start | bytes 786436
  66.5 3.6 %copy-start.2 = (f32[64,768]{1,0:T(8,128)S(1)}, f32[64,768]{1,0:T(8,128)}, u32[]{:S(2)}) copy-start(f32[64,768]{1,0:T(8,128)} %refs_8_.1) | copy-start | bytes 589828
  66.5 3.6 %copy-start.5 = (f32[64,256]{1,0:T(8,128)S(1)}, f32[64,256]{1,0:T(8,128)}, u32[]{:S(2)}) copy-start(f32[64,256]{1,0:T(8,128)} %refs_11_.1) | copy-start | bytes 196612
  66.5 3.6 %copy-start.8 = (f32[64,1024]{1,0:T(8,128)S(1)}, f32[64,1024]{1,0:T(8,128)}, u32[]{:S(2)}) copy-start(f32[64,1024]{1,0:T(8,128)} %refs_15_.1) | copy-start | bytes 786436
  66.5 3.6 %copy-start.9 = (f32[64,1024]{1,0:T(8,128)S(1)}, f32[64,1024]{1,0:T(8,128)}, u32[]{:S(2)}) copy-start(f32[64,1024]{1,0:T(8,128)} %refs_16_.1) | copy-start | bytes 786436
  66.5 3.6 %copy-start.10 = (f32[256,256]{1,0:T(8,128)S(1)}, f32[256,256]{1,0:T(8,128)}, u32[]{:S(2)}) copy-start(f32[256,256]{1,0:T(8,128)} %refs_18_.1) | copy-start | bytes 786436
  66.5 3.6 %copy-start.11 = (f32[256,256]{1,0:T(8,128)S(1)}, f32[256,256]{1,0:T(8,128)}, u32[]{:S(2)}) copy-start(f32[256,256]{1,0:T(8,128)} %refs_19_.1) | copy-start | bytes 786436
  66.5 3.6 %copy-start.12 = (f32[64,768]{1,0:T(8,128)S(1)}, f32[64,768]{1,0:T(8,128)}, u32[]{:S(2)}) copy-start(f32[64,768]{1,0:T(8,128)} %refs_9_.1) | copy-start | bytes 589828
  66.6 3.6 %copy-start.13 = (f32[64,768]{1,0:T(8,128)S(1)}, f32[64,768]{1,0:T(8,128)}, u32[]{:S(2)}) copy-start(f32[64,768]{1,0:T(8,128)} %refs_10_.1) | copy-start | bytes 589828
  66.6 3.6 %copy-start.14 = (f32[64,256]{1,0:T(8,128)S(1)}, f32[64,256]{1,0:T(8,128)}, u32[]{:S(2)}) copy-start(f32[64,256]{1,0:T(8,128)} %refs_12_.1) | copy-start | bytes 196612
  66.6 3.6 %copy-start.15 = (f32[64,256]{1,0:T(8,128)S(1)}, f32[64,256]{1,0:T(8,128)}, u32[]{:S(2)}) copy-start(f32[64,256]{1,0:T(8,128)} %refs_13_.1) | copy-start | bytes 196612

commit v12 on v9

--- a/solution.py
+++ b/solution.py
@@ -433,18 +433,19 @@
     part_ways(grads_ref, keep_ref, send_ref, shard & 1)
 
 
-def halve_kernel(axis, bit, *refs):
-    count = (len(refs) - 2) // 2
-    keep_ref, send_ref = refs[-2:]
-    side = (lax.axis_index(axis) >> bit) & 1
+def halve_kernel(bit, kept, *refs):
+    arrived, (keep_ref, send_ref) = refs[:-2], refs[-2:]
+    side = (lax.axis_index("dp") >> bit) & 1
+
+    def total(index):
+        value = kept[index]
+        for piece in arrived:
+            value = value + piece[index].astype(wide)
+        return value
+
     for pair in range(keep_ref.shape[0]):
-        for target, index in ((keep_ref, 2 * pair + side), (send_ref, 2 * pair + 1 - side)):
-            parts = []
-            for chunk in range(count):
-                kept, arrived = refs[2 * chunk : 2 * chunk + 2]
-                parts.append(kept[index] + arrived[index].astype(wide))
-            value = parts[0] if count == 1 else jnp.concatenate(parts, axis=0)
-            target[pair] = value.astype(target.dtype)
+        keep_ref[pair] = total(2 * pair + side)
+        send_ref[pair] = total(2 * pair + 1 - side).astype(low)
 
 
 def piece_spans(total, tail, group):
@@ -454,22 +455,23 @@
     return spans
 
 
-def split_kernel(tail, *refs):
-    arrived, keep_ref, send_ref, sum_ref = refs[:-3], *refs[-3:]
-    group = sum_ref.shape[0]
-    total = arrived[0][...]
-    for piece in arrived[1:]:
-        total = total + piece[...].astype(wide)
-    for index in range(group):
-        row = 0
-        for rows, first, moves in piece_spans(total.shape[0], tail, group):
-            at = first + index * rows if moves else first
-            sum_ref[index, row : row + rows, :] = total[at : at + rows, :]
-            row += rows
+def quarter_kernel(tail, kept, arrived, keep_ref, beside_ref, across_ref, corner_ref, sum_ref):
+    group = sum_ref.shape[1]
+    for half in range(2):
+        total = kept[half] + arrived[half].astype(wide)
+        for index in range(group):
+            row = 0
+            for rows, first, moves in piece_spans(total.shape[0], tail, group):
+                at = first + index * rows if moves else first
+                sum_ref[half, index, row : row + rows, :] = total[at : at + rows, :]
+                row += rows
+    mine = (lax.axis_index("shard") >> 1) & 1
     side = lax.axis_index("dp") & 1
     for pair in range(group // 2):
-        keep_ref[pair] = sum_ref[2 * pair + side]
-        send_ref[pair] = sum_ref[2 * pair + 1 - side].astype(low)
+        keep_ref[pair] = sum_ref[mine, 2 * pair + side]
+        beside_ref[pair] = sum_ref[1 - mine, 2 * pair + side].astype(low)
+        across_ref[pair] = sum_ref[mine, 2 * pair + 1 - side].astype(low)
+        corner_ref[pair] = sum_ref[1 - mine, 2 * pair + 1 - side].astype(low)
 
 
 def piece_kernel(*refs):
@@ -578,25 +580,30 @@
     return [found[offset] for offset in range(group)]
 
 
-def halve_call(axis, bit, flat, name):
-    half, _, width = flat[0].shape
-    shape = (half // 2, sum(item.shape[1] for item in flat[::2]), width)
+def corner(values):
+    replicas, shards = lax.axis_size("dp"), lax.axis_size("shard")
+    pairs = [
+        (replica * shards + shard, (replica ^ 1) * shards + (shard ^ 2))
+        for replica in range(replicas)
+        for shard in range(shards)
+    ]
+    return lax.ppermute(values, ("dp", "shard"), pairs)
+
+
+def quarter_call(kept, arrived, tail, group, name):
+    _, rows, width = kept.shape
+    shape = (group // 2, (rows - tail) // group + tail, width)
     return local_call(
-        functools.partial(halve_kernel, axis, bit), [(shape, wide), (shape, low)], flat, name=name
-    )
-
-
-def split_chunk(chunk, tail, group):
-    rows, width = chunk[0].shape
-    half = (group // 2, (rows - tail) // group + tail, width)
-    keep, send = local_call(
-        functools.partial(split_kernel, tail),
-        [(half, wide), (half, low)],
-        chunk,
-        [((group,) + half[1:], wide)],
-        name="split_sum",
-    )
-    return keep, exchange(send, "dp", 1)
+        functools.partial(quarter_kernel, tail),
+        [(shape, wide)] + [(shape, low)] * 3,
+        [kept, arrived],
+        [((2, group) + shape[1:], wide)],
+        name=name,
+    )
+
+
+def spread(beside, across, far):
+    return [exchange(beside, "shard", 2), exchange(across, "dp", 1), corner(far)]
 
 
 def near_sum(flat):
@@ -604,7 +611,13 @@
     bit = 1
     while half > 1:
         half //= 2
-        keep, send = halve_call("dp", bit, flat, "halve_dp")
+        shape = (half,) + flat[0].shape[1:]
+        keep, send = local_call(
+            functools.partial(halve_kernel, bit),
+            [(shape, wide), (shape, low)],
+            flat,
+            name="halve_dp",
+        )
         flat = [keep, exchange(send, "dp", 1 << bit)]
         bit += 1
     return flat
@@ -767,10 +780,10 @@
         name="back_first",
     )
     first_query, arrived_ffn = lax.optimization_barrier((first_query, arrived_ffn))
-    keep_ffn, send_ffn = halve_call("shard", 1, [kept_ffn, arrived_ffn], "halve_ffn")
-    first_query, send_ffn = lax.optimization_barrier((first_query, send_ffn))
-    arrived_ffn = exchange(send_ffn, "shard", 2)
     tail = TILE_ROWS
+    keep_ffn, *sends_ffn = quarter_call(kept_ffn, arrived_ffn, 0, group, "quarter_ffn")
+    first_query, sends_ffn = lax.optimization_barrier((first_query, sends_ffn))
+    arrived_ffn = spread(*sends_ffn)
     att_rows = 3 * part + tail
     pair = (shards // 2, att_rows, width)
     input_grad, kept_att, send_att = local_call(
@@ -783,14 +796,14 @@
         flops=heads * rows * rows * 256 * 6,
         name="back_last",
     )
+    send_att, arrived_ffn[0], arrived_ffn[1] = lax.optimization_barrier(
+        (send_att, arrived_ffn[0], arrived_ffn[1])
+    )
     arrived_att = exchange(send_att, "shard", 1)
-    keep_att, send_att = halve_call("shard", 1, [kept_att, arrived_att], "halve_att")
-    send_att, arrived_ffn = lax.optimization_barrier((send_att, arrived_ffn))
+    keep_att, *sends_att = quarter_call(kept_att, arrived_att, tail, group, "quarter_att")
+    arrived_att = spread(*sends_att)
     tails = (0, tail)
-    arrived_att = exchange(send_att, "shard", 2)
-    chunk_ffn = split_chunk([keep_ffn[0], arrived_ffn[0]], 0, group)
-    chunk_att = split_chunk([keep_att[0], arrived_att[0]], tail, group)
-    pieces = finish_sum([chunk_ffn, chunk_att], group)
+    pieces = finish_sum([[keep_ffn] + arrived_ffn, [keep_att] + arrived_att], group)
     blocks = hidden_count // width
     results = adam_call(
         pieces,

time: 69.5 us -> 66.8 us (0.961)
  waiting for transfers between devices: 24.1 us -> 16.8 us
  starting transfers between devices: 24.4 us -> 29 us
    ppermute x23, waiting for transfers between devices: 24.1 us -> 13.9 us  [exchange(): lax.ppermute(values, axis, [(index, index ^ mask) for index in range(coun...]
    ppermute x0 -> x2, starting transfers between devices: none -> 3.25 us  [corner(): return lax.ppermute(values, ('dp', 'shard'), pairs)]
    ppermute x0 -> x2, waiting for transfers between devices: none -> 2.88 us  [corner(): return lax.ppermute(values, ('dp', 'shard'), pairs)]
    ppermute x23, starting transfers between devices: 24.4 us -> 25.8 us  [exchange(): lax.ppermute(values, axis, [(index, index ^ mask) for index in range(coun...]
    pallas_call x17 -> x15, Pallas kernels: 19.5 us -> 19.6 us  [local_call(): pl.pallas_call(kernel, out_shape=outs, in_specs=[pl.BlockSpec(memory_spac...]
  transfers between devices with their start and end apart: 23 -> 25, of which waited for: 15 -> 14; matrix products, arithmetic and copies ran while one was open for 0% -> 0% of each run, Pallas kernels for 17% -> 18%
where the time goes in v12:
time: 66.8 us; the launch traced here: 66.7 us
  starting transfers between devices  29 us (43%)
  Pallas kernels  19.6 us (29%)
  waiting for transfers between devices  16.8 us (25%)
  between operations  1.18 us (2%)
    ppermute x23, starting transfers between devices, exchange(): lax.ppermute(values, axis, [(index, index ^ mask) for index in range(coun...  25.8 us
    pallas_call x15, Pallas kernels, local_call(): pl.pallas_call(kernel, out_shape=outs, in_specs=[pl.BlockSpec(memory_spac...  19.6 us
    ppermute x23, waiting for transfers between devices, exchange(): lax.ppermute(values, axis, [(index, index ^ mask) for index in range(coun...  13.9 us
    ppermute x2, starting transfers between devices, corner(): return lax.ppermute(values, ('dp', 'shard'), pairs)  3.25 us
    ppermute x2, waiting for transfers between devices, corner(): return lax.ppermute(values, ('dp', 'shard'), pairs)  2.88 us
  transfers between devices with their start and end apart: 25, of which 14 were waited for; matrix products, arithmetic and copies ran while one was open for 0% of the time, Pallas kernels for 18%

profile of v12, /device:TPU:0, one launch (start us, length us, event | category | flops | bytes accessed | tf_op | source)
XLA Modules:
  0.0 66.7 jit_solution(3126171614427865697)
XLA Ops:
  0.7 1.7 %pack_first.1.refs_2_.refs_3_.refs_12_ = bf16[208,256]{1,0:T(8,128)(2,1)} custom-call(f32[64,768]{1,0:T(8,128)} %refs_8_.1, f32[768]{0:T(1024)} %refs_20_.1), custom_call_target="tpu_custom_call" | custom-call | bytes 306176 | tf_op jit(solution)/shard_map/pack_first/pallas_call | solution.py:550
  2.4 3.0 %collective-permute-start = (bf16[208,256]{1,0:T(8,128)(2,1)}, bf16[208,256]{1,0:T(8,128)(2,1)S(1)}, u32[]{:S(2)}, u32[]{:S(2)}) collective-permute-start(bf16[208,256]{1,0:T(8,128)(2,1)} %pack_first.1.refs_2_.refs_3_.refs_12_), channel_id=1, source_target_pairs={{0,2},{1,3},{2,0},{3,1},{4,6},{5,7},{6,4},{7,5},{8,10},{9,11},{10,... | collective-permute-start | bytes 319496 | tf_op jit(solution)/shard_map/ppermute | solution.py:564
  5.4 1.8 %pack_second.1.refs_7_ = bf16[576,256]{1,0:T(8,128)(2,1)} custom-call(f32[64,256]{1,0:T(8,128)} %refs_11_.1, f32[64,1024]{1,0:T(8,128)} %refs_14_.1, f32[256,256]{1,0:T(8,128)} %refs_17_.1), custom_call_target="tpu_custom_call" | custom-call | bytes 884736 | tf_op jit(solution)/shard_map/pack_second/pallas_call | solution.py:550
  7.2 0.1 collective-permute-start.3
  7.3 0.1 collective-permute-start.1
  7.4 0.6 prepare.1
  8.1 0.5 collective-permute-done.refs_4_.refs_5_.refs_14_
  8.7 0.5 collective-permute-start.4
  9.1 0.8 %collective-permute-done.2.refs_5_.refs_6_.refs_15_ = bf16[208,256]{1,0:T(8,128)(2,1)S(1)} collective-permute-done((bf16[208,256]{1,0:T(8,128)(2,1)S(1)}, bf16[208,256]{1,0:T(8,128)(2,1)S(1)}, u32[]{:S(2)}, u32[]{:S(2)}) %collective-permute-start.2) | collective-permute-done | bytes 106528 | tf_op jit(solution)/shard_map/ppermute | solution.py:564
  9.9 3.0 %attend.1 = (bf16[512,768]{1,0:T(8,128)(2,1)S(1)}, bf16[512,256]{1,0:T(8,128)(2,1)S(1)}, f32[8,512]{1,0:T(8,128)S(1)}, f32[256,512]{1,0:T(8,128)S(1)}) custom-call(f32[512,256]{1,0:T(8,128)S(1)} %get-tuple-element.99.refs_0_.refs_8_, f32[512,512]{1,0:T(8,128)S(1)} %get-tuple-element.100.refs_1_.refs_3_, bf16[208,256]{1,0:T(8,128)(2,1)S(1)} %copy-done.13, ...), custom_call_target="tpu_custom_call" | custom-call | flops 1342177280 | bytes 3588096 | tf_op jit(solution)/shard_map/attend/pallas_call | solution.py:550
  12.9 3.0 %collective-permute-done.3.refs_9_ = bf16[576,256]{1,0:T(8,128)(2,1)S(1)} collective-permute-done((bf16[576,256]{1,0:T(8,128)(2,1)}, bf16[576,256]{1,0:T(8,128)(2,1)S(1)}, u32[]{:S(2)}, u32[]{:S(2)}) %collective-permute-start.3) | collective-permute-done | bytes 294944 | tf_op jit(solution)/shard_map/ppermute | solution.py:564
  16.0 1.6 %collective-permute-done.5.refs_10_ = bf16[576,256]{1,0:T(8,128)(2,1)S(1)} collective-permute-done((bf16[576,256]{1,0:T(8,128)(2,1)S(1)}, bf16[576,256]{1,0:T(8,128)(2,1)S(1)}, u32[]{:S(2)}, u32[]{:S(2)}) %collective-permute-start.5) | collective-permute-done | bytes 294944 | tf_op jit(solution)/shard_map/ppermute | solution.py:564
  17.6 3.9 %feed.1 = (bf16[512,256]{1,0:T(8,128)(2,1)}, f32[512,256]{1,0:T(8,128)S(1)}, bf16[512,256]{1,0:T(8,128)(2,1)S(1)}, f32[16,256]{1,0:T(8,128)S(1)}, f32[2,576,256]...) custom-call(bf16[512,256]{1,0:T(8,128)(2,1)S(1)} %copy-done.6, bf16[512,256]{1,0:T(8,128)(2,1)S(1)} %get-tuple-element.104.refs_1_, ...), custom_call_target="tpu_custom_call" | custom-call | flops 1811939328 | bytes 5226496 | tf_op jit(solution)/shard_map/feed/pallas_call | solution.py:550
  21.5 0.1 collective-permute-start.6
  21.6 1.7 %back_first.1 = (bf16[128,512]{1,0:T(8,128)(2,1)S(1)}, f32[512,128]{1,0:T(8,128)S(1)}, f32[512,128]{1,0:T(8,128)S(1)}) custom-call(bf16[512,768]{1,0:T(8,128)(2,1)S(1)} %get-tuple-element.108.refs_0_, bf16[512,256]{1,0:T(8,128)(2,1)S(1)} %get-tuple-element.109.refs_1_, f32[8,512]{1,0:T(8,128)S(1)} %get-tuple-element.110.refs_2_, ...), custom_call_target="tpu_custom_call" | custom-call | flops 1342177280 | bytes 3293184 | tf_op jit(solution)/shard_map/back_first/pallas_call | solution.py:550
  23.3 0.1 collective-permute-done.6.arrived
  23.5 0.2 quarter_ffn.1
  23.7 0.7 %collective-permute-start.7 = (bf16[4,72,256]{2,1,0:T(8,128)(2,1)S(1)}, bf16[4,72,256]{2,1,0:T(8,128)(2,1)S(1)}, u32[]{:S(2)}, u32[]{:S(2)}) collective-permute-start(bf16[4,72,256]{2,1,0:T(8,128)(2,1)S(1)} %get-tuple-element.129), channel_id=1, source_target_pairs={{0,2},{1,3},{2,0},{3,1},{4,6},{5,7},{6,4},{7,5},{8,10},{9,11},{10,... | collective-permute-start | bytes 442376 | tf_op jit(solution)/shard_map/ppermute | solution.py:564
  24.4 1.5 %collective-permute-start.8 = (bf16[4,72,256]{2,1,0:T(8,128)(2,1)S(1)}, bf16[4,72,256]{2,1,0:T(8,128)(2,1)S(1)}, u32[]{:S(2)}, u32[]{:S(2)}) collective-permute-start(bf16[4,72,256]{2,1,0:T(8,128)(2,1)S(1)} %get-tuple-element.130), channel_id=1, source_target_pairs={{0,4},{4,0},{8,12},{12,8},{16,20},{20,16},{24,28},{28,24},{1,5},{5... | collective-permute-start | bytes 442376 | tf_op jit(solution)/shard_map/ppermute | solution.py:564
  25.9 4.5 %back_last.1 = (f32[512,256]{1,0:T(8,128)}, f32[2,200,256]{2,1,0:T(8,128)S(1)}, bf16[2,200,256]{2,1,0:T(8,128)(2,1)S(1)}) custom-call(bf16[512,768]{1,0:T(8,128)(2,1)S(1)} %get-tuple-element.108.refs_0_, bf16[512,256]{1,0:T(8,128)(2,1)S(1)} %get-tuple-element.109.refs_1_, f32[8,512]{1,0:T(8,128)S(1)} %get-tuple-element.110.refs_2_, ...), custom_call_target="tpu_custom_call" | custom-call | flops 3221225472 | bytes 5924864 | tf_op jit(solution)/shard_map/back_last/pallas_call | solution.py:550
  30.6 0.1 collective-permute-start.12
  30.7 1.8 %collective-permute-start.9 = (bf16[4,72,256]{2,1,0:T(8,128)(2,1)S(1)}, bf16[4,72,256]{2,1,0:T(8,128)(2,1)S(1)}, u32[]{:S(2)}, u32[]{:S(2)}) collective-permute-start(bf16[4,72,256]{2,1,0:T(8,128)(2,1)S(1)} %get-tuple-element.133), channel_id=1, source_target_pairs={{0,6},{1,7},{2,4},{3,5},{4,2},{5,3},{6,0},{7,1},{8,14},{9,15},{10,... | collective-permute-start | bytes 442376 | tf_op jit(solution)/shard_map/ppermute | solution.py:590
  32.4 0.1 quarter_att.1
  32.5 1.1 %collective-permute-start.13 = (bf16[4,32,256]{2,1,0:T(8,128)(2,1)S(1)}, bf16[4,32,256]{2,1,0:T(8,128)(2,1)S(1)}, u32[]{:S(2)}, u32[]{:S(2)}) collective-permute-start(bf16[4,32,256]{2,1,0:T(8,128)(2,1)S(1)} %get-tuple-element.141), channel_id=1, source_target_pairs={{0,2},{1,3},{2,0},{3,1},{4,6},{5,7},{6,4},{7,5},{8,10},{9,11},{10,... | collective-permute-start | bytes 196616 | tf_op jit(solution)/shard_map/ppermute | solution.py:564
  33.6 1.0 %collective-permute-start.14 = (bf16[4,32,256]{2,1,0:T(8,128)(2,1)S(1)}, bf16[4,32,256]{2,1,0:T(8,128)(2,1)S(1)}, u32[]{:S(2)}, u32[]{:S(2)}) collective-permute-start(bf16[4,32,256]{2,1,0:T(8,128)(2,1)S(1)} %get-tuple-element.142), channel_id=1, source_target_pairs={{0,4},{4,0},{8,12},{12,8},{16,20},{20,16},{24,28},{28,24},{1,5},{5... | collective-permute-start | bytes 196616 | tf_op jit(solution)/shard_map/ppermute | solution.py:564
  34.6 1.5 %collective-permute-start.15 = (bf16[4,32,256]{2,1,0:T(8,128)(2,1)S(1)}, bf16[4,32,256]{2,1,0:T(8,128)(2,1)S(1)}, u32[]{:S(2)}, u32[]{:S(2)}) collective-permute-start(bf16[4,32,256]{2,1,0:T(8,128)(2,1)S(1)} %get-tuple-element.143), channel_id=1, source_target_pairs={{0,6},{1,7},{2,4},{3,5},{4,2},{5,3},{6,0},{7,1},{8,14},{9,15},{10,... | collective-permute-start | bytes 196616 | tf_op jit(solution)/shard_map/ppermute | solution.py:590
  36.1 2.2 %collective-permute-done.9.refs_2_ = bf16[4,72,256]{2,1,0:T(8,128)(2,1)S(1)} collective-permute-done((bf16[4,72,256]{2,1,0:T(8,128)(2,1)S(1)}, bf16[4,72,256]{2,1,0:T(8,128)(2,1)S(1)}, u32[]{:S(2)}, u32[]{:S(2)}) %collective-permute-start.9) | collective-permute-done | bytes 147488 | tf_op jit(solution)/shard_map/ppermute | solution.py:590
  38.3 0.1 halve_dp.4
  38.4 1.6 %collective-permute-start.10 = (bf16[2,72,256]{2,1,0:T(8,128)(2,1)S(1)}, bf16[2,72,256]{2,1,0:T(8,128)(2,1)S(1)}, u32[]{:S(2)}, u32[]{:S(2)}) collective-permute-start(bf16[2,72,256]{2,1,0:T(8,128)(2,1)S(1)} %get-tuple-element.135), channel_id=1, source_target_pairs={{0,8},{4,12},{8,0},{12,4},{16,24},{20,28},{24,16},{28,20},{1,9},{5... | collective-permute-start | bytes 221192 | tf_op jit(solution)/shard_map/ppermute | solution.py:564
  40.0 0.6 collective-permute-done.15.refs_2_
  40.7 1.6 %collective-permute-start.16 = (bf16[2,32,256]{2,1,0:T(8,128)(2,1)S(1)}, bf16[2,32,256]{2,1,0:T(8,128)(2,1)S(1)}, u32[]{:S(2)}, u32[]{:S(2)}) collective-permute-start(bf16[2,32,256]{2,1,0:T(8,128)(2,1)S(1)} %get-tuple-element.145), channel_id=1, source_target_pairs={{0,8},{4,12},{8,0},{12,4},{16,24},{20,28},{24,16},{28,20},{1,9},{5... | collective-permute-start | bytes 98312 | tf_op jit(solution)/shard_map/ppermute | solution.py:564
  42.4 0.5 collective-permute-done.10.refs_0_
  42.8 2.7 %collective-permute-start.11 = (bf16[1,72,256]{2,1,0:T(8,128)(2,1)S(1)}, bf16[1,72,256]{2,1,0:T(8,128)(2,1)S(1)}, u32[]{:S(2)}, u32[]{:S(2)}) collective-permute-start(bf16[1,72,256]{2,1,0:T(8,128)(2,1)S(1)} %get-tuple-element.137), channel_id=1, source_target_pairs={{0,16},{4,20},{8,24},{12,28},{16,0},{20,4},{24,8},{28,12},{1,17},{... | collective-permute-start | bytes 110600 | tf_op jit(solution)/shard_map/ppermute | solution.py:564
  45.5 1.8 %collective-permute-start.17 = (bf16[1,32,256]{2,1,0:T(8,128)(2,1)S(1)}, bf16[1,32,256]{2,1,0:T(8,128)(2,1)S(1)}, u32[]{:S(2)}, u32[]{:S(2)}) collective-permute-start(bf16[1,32,256]{2,1,0:T(8,128)(2,1)S(1)} %get-tuple-element.147), channel_id=1, source_target_pairs={{0,16},{4,20},{8,24},{12,28},{16,0},{20,4},{24,8},{28,12},{1,17},{... | collective-permute-start | bytes 49160 | tf_op jit(solution)/shard_map/ppermute | solution.py:564
  47.4 0.5 collective-permute-done.11.refs_1_
  47.9 2.3 %collective-permute-done.17.refs_3_ = bf16[1,32,256]{2,1,0:T(8,128)(2,1)S(1)} collective-permute-done((bf16[1,32,256]{2,1,0:T(8,128)(2,1)S(1)}, bf16[1,32,256]{2,1,0:T(8,128)(2,1)S(1)}, u32[]{:S(2)}, u32[]{:S(2)}) %collective-permute-start.17) | collective-permute-done | bytes 16416 | tf_op jit(solution)/shard_map/ppermute | solution.py:564
  50.2 1.0 %collective-permute-start.19 = (bf16[104,256]{1,0:T(8,128)(2,1)S(1)}, bf16[104,256]{1,0:T(8,128)(2,1)S(1)}, u32[]{:S(2)}, u32[]{:S(2)}) collective-permute-start(bf16[104,256]{1,0:T(8,128)(2,1)S(1)} %piece_sum.1.refs_0_), channel_id=1, source_target_pairs={{0,4},{4,0},{8,12},{12,8},{16,20},{20,16},{24,28},{28,24},{1,5},{5... | collective-permute-start | bytes 159752 | tf_op jit(solution)/shard_map/ppermute | solution.py:564
  51.2 1.9 %collective-permute-start.18 = (bf16[104,256]{1,0:T(8,128)(2,1)S(1)}, bf16[104,256]{1,0:T(8,128)(2,1)S(1)}, u32[]{:S(2)}, u32[]{:S(2)}) collective-permute-start(bf16[104,256]{1,0:T(8,128)(2,1)S(1)} %piece_sum.1.refs_0_), channel_id=1, source_target_pairs={{0,16},{4,20},{8,24},{12,28},{16,0},{20,4},{24,8},{28,12},{1,17},{... | collective-permute-start | bytes 159752 | tf_op jit(solution)/shard_map/ppermute | solution.py:564
  53.1 2.0 %collective-permute-start.20 = (bf16[104,256]{1,0:T(8,128)(2,1)S(1)}, bf16[104,256]{1,0:T(8,128)(2,1)S(1)}, u32[]{:S(2)}, u32[]{:S(2)}) collective-permute-start(bf16[104,256]{1,0:T(8,128)(2,1)S(1)} %piece_sum.1.refs_0_), channel_id=1, source_target_pairs={{0,8},{4,12},{8,0},{12,4},{16,24},{20,28},{24,16},{28,20},{1,9},{5... | collective-permute-start | bytes 159752 | tf_op jit(solution)/shard_map/ppermute | solution.py:564
  55.0 1.2 %collective-permute-done.18.refs_4_ = bf16[104,256]{1,0:T(8,128)(2,1)S(1)} collective-permute-done((bf16[104,256]{1,0:T(8,128)(2,1)S(1)}, bf16[104,256]{1,0:T(8,128)(2,1)S(1)}, u32[]{:S(2)}, u32[]{:S(2)}) %collective-permute-start.18) | collective-permute-done | bytes 53280 | tf_op jit(solution)/shard_map/ppermute | solution.py:564
  56.3 1.8 %collective-permute-start.23 = (bf16[104,256]{1,0:T(8,128)(2,1)S(1)}, bf16[104,256]{1,0:T(8,128)(2,1)S(1)}, u32[]{:S(2)}, u32[]{:S(2)}) collective-permute-start(bf16[104,256]{1,0:T(8,128)(2,1)S(1)} %collective-permute-done.18.refs_4_), channel_id=1, source_target_pairs={{0,8},{4,12},{8,0},{12,4},{16,24},{20,28},{24,16},{28,20},{1,9},{5... | collective-permute-start | bytes 159752 | tf_op jit(solution)/shard_map/ppermute | solution.py:564
  58.1 1.0 %collective-permute-start.22 = (bf16[104,256]{1,0:T(8,128)(2,1)S(1)}, bf16[104,256]{1,0:T(8,128)(2,1)S(1)}, u32[]{:S(2)}, u32[]{:S(2)}) collective-permute-start(bf16[104,256]{1,0:T(8,128)(2,1)S(1)} %collective-permute-done.18.refs_4_), channel_id=1, source_target_pairs={{0,4},{4,0},{8,12},{12,8},{16,20},{20,16},{24,28},{28,24},{1,5},{5... | collective-permute-start | bytes 159752 | tf_op jit(solution)/shard_map/ppermute | solution.py:564
  59.1 1.0 %collective-permute-start.21 = (bf16[104,256]{1,0:T(8,128)(2,1)S(1)}, bf16[104,256]{1,0:T(8,128)(2,1)S(1)}, u32[]{:S(2)}, u32[]{:S(2)}) collective-permute-start(bf16[104,256]{1,0:T(8,128)(2,1)S(1)} %collective-permute-done.20.refs_2_), channel_id=1, source_target_pairs={{0,4},{4,0},{8,12},{12,8},{16,20},{20,16},{24,28},{28,24},{1,5},{5... | collective-permute-start | bytes 159752 | tf_op jit(solution)/shard_map/ppermute | solution.py:564
  60.1 0.3 collective-permute-done.23.refs_6_
  60.4 1.1 %collective-permute-start.24 = (bf16[104,256]{1,0:T(8,128)(2,1)S(1)}, bf16[104,256]{1,0:T(8,128)(2,1)S(1)}, u32[]{:S(2)}, u32[]{:S(2)}) collective-permute-start(bf16[104,256]{1,0:T(8,128)(2,1)S(1)} %collective-permute-done.23.refs_6_), channel_id=1, source_target_pairs={{0,4},{4,0},{8,12},{12,8},{16,20},{20,16},{24,28},{28,24},{1,5},{5... | collective-permute-start | bytes 159752 | tf_op jit(solution)/shard_map/ppermute | solution.py:564
  61.5 1.7 %collective-permute-done.21.refs_3_ = bf16[104,256]{1,0:T(8,128)(2,1)S(1)} collective-permute-done((bf16[104,256]{1,0:T(8,128)(2,1)S(1)}, bf16[104,256]{1,0:T(8,128)(2,1)S(1)}, u32[]{:S(2)}, u32[]{:S(2)}) %collective-permute-start.21) | collective-permute-done | bytes 53280 | tf_op jit(solution)/shard_map/ppermute | solution.py:564
  63.2 1.3 %collective-permute-done.24.refs_7_ = bf16[104,256]{1,0:T(8,128)(2,1)S(1)} collective-permute-done((bf16[104,256]{1,0:T(8,128)(2,1)S(1)}, bf16[104,256]{1,0:T(8,128)(2,1)S(1)}, u32[]{:S(2)}, u32[]{:S(2)}) %collective-permute-start.24) | collective-permute-done | bytes 53280 | tf_op jit(solution)/shard_map/ppermute | solution.py:564
  64.7 1.8 %adam.1 = (f32[64,768]{1,0:T(8,128)}, f32[64,768]{1,0:T(8,128)}, f32[64,768]{1,0:T(8,128)}, f32[64,256]{1,0:T(8,128)}, f32[64,256]{1,0:T(8,128)}, /*index=5*/f32...) custom-call(bf16[104,256]{1,0:T(8,128)(2,1)S(1)} %piece_sum.1.refs_0, ...), custom_call_target="tpu_custom_call" | custom-call | bytes 5163008 | tf_op jit(solution)/shard_map/adam/pallas_call | solution.py:550
  (59 shorter events, 0.3 us)
Async XLA Ops:
  0.7 6.7 %copy-start.6 = (bf16[512,256]{1,0:T(8,128)(2,1)S(1)}, bf16[512,256]{1,0:T(8,128)(2,1)}, u32[]{:S(2)}) copy-start(bf16[512,256]{1,0:T(8,128)(2,1)} %refs_0_.1) | copy-start | bytes 786436
  0.7 6.7 %copy-start.20 = (s32[128]{0:T(128)S(1)}, s32[128]{0:T(128)}, u32[]{:S(2)}) copy-start(s32[128]{0:T(128)} %param.22) | copy-start | bytes 1540
  0.7 6.7 %copy-start.19 = (s32[128]{0:T(128)S(1)}, s32[128]{0:T(128)}, u32[]{:S(2)}) copy-start(s32[128]{0:T(128)} %param.21) | copy-start | bytes 1540
  0.7 6.7 %copy-start.5 = (bf16[512,256]{1,0:T(8,128)(2,1)S(1)}, bf16[512,256]{1,0:T(8,128)(2,1)}, u32[]{:S(2)}) copy-start(bf16[512,256]{1,0:T(8,128)(2,1)} %seed_ref.1) | copy-start | bytes 786436
  2.4 7.5 %copy-start.13 = (bf16[208,256]{1,0:T(8,128)(2,1)S(1)}, bf16[208,256]{1,0:T(8,128)(2,1)}, u32[]{:S(2)}) copy-start(bf16[208,256]{1,0:T(8,128)(2,1)} %pack_first.1.refs_2_.refs_3_.refs_12_) | copy-start | bytes 319492
  2.4 6.2 %collective-permute-start = (bf16[208,256]{1,0:T(8,128)(2,1)}, bf16[208,256]{1,0:T(8,128)(2,1)S(1)}, u32[]{:S(2)}, u32[]{:S(2)}) collective-permute-start(bf16[208,256]{1,0:T(8,128)(2,1)} %pack_first.1.refs_2_.refs_3_.refs_12_), channel_id=1, source_target_pairs={{0,2},{1,3},{2,0},{3,1},{4,6},{5,7},{6,4},{7,5},{8,10},{9,11},{10,... | collective-permute-start | bytes 319496 | tf_op jit(solution)/shard_map/ppermute | solution.py:564
  7.2 8.7 %collective-permute-start.3 = (bf16[576,256]{1,0:T(8,128)(2,1)}, bf16[576,256]{1,0:T(8,128)(2,1)S(1)}, u32[]{:S(2)}, u32[]{:S(2)}) collective-permute-start(bf16[576,256]{1,0:T(8,128)(2,1)} %pack_second.1.refs_7_), channel_id=1, source_target_pairs={{0,2},{1,3},{2,0},{3,1},{4,6},{5,7},{6,4},{7,5},{8,10},{9,11},{10,... | collective-permute-start | bytes 884744 | tf_op jit(solution)/shard_map/ppermute | solution.py:564
  7.3 1.8 %collective-permute-start.1 = (bf16[208,256]{1,0:T(8,128)(2,1)}, bf16[208,256]{1,0:T(8,128)(2,1)S(1)}, u32[]{:S(2)}, u32[]{:S(2)}) collective-permute-start(bf16[208,256]{1,0:T(8,128)(2,1)} %pack_first.1.refs_2_.refs_3_.refs_12_), channel_id=1, source_target_pairs={{0,1},{1,0},{2,3},{3,2},{4,5},{5,4},{6,7},{7,6},{8,9},{9,8},{10,11... | collective-permute-start | bytes 319496 | tf_op jit(solution)/shard_map/ppermute | solution.py:564
  8.6 9.0 %copy-start.3 = (bf16[576,256]{1,0:T(8,128)(2,1)S(1)}, bf16[576,256]{1,0:T(8,128)(2,1)}, u32[]{:S(2)}) copy-start(bf16[576,256]{1,0:T(8,128)(2,1)} %pack_second.1.refs_7_) | copy-start | bytes 884740
  8.6 1.3 %collective-permute-start.2 = (bf16[208,256]{1,0:T(8,128)(2,1)S(1)}, bf16[208,256]{1,0:T(8,128)(2,1)S(1)}, u32[]{:S(2)}, u32[]{:S(2)}) collective-permute-start(bf16[208,256]{1,0:T(8,128)(2,1)S(1)} %collective-permute-done.refs_4_.refs_5_.refs_14_), channel_id=1, source_target_pairs={{0,1},{1,0},{2,3},{3,2},{4,5},{5,4},{6,7},{7,6},{8,9},{9,8},{10,11... | collective-permute-start | bytes 319496 | tf_op jit(solution)/shard_map/ppermute | solution.py:564
  8.7 7.3 %collective-permute-start.4 = (bf16[576,256]{1,0:T(8,128)(2,1)}, bf16[576,256]{1,0:T(8,128)(2,1)S(1)}, u32[]{:S(2)}, u32[]{:S(2)}) collective-permute-start(bf16[576,256]{1,0:T(8,128)(2,1)} %pack_second.1.refs_7_), channel_id=1, source_target_pairs={{0,1},{1,0},{2,3},{3,2},{4,5},{5,4},{6,7},{7,6},{8,9},{9,8},{10,11... | collective-permute-start | bytes 884744 | tf_op jit(solution)/shard_map/ppermute | solution.py:564
  16.0 1.6 %collective-permute-start.5 = (bf16[576,256]{1,0:T(8,128)(2,1)S(1)}, bf16[576,256]{1,0:T(8,128)(2,1)S(1)}, u32[]{:S(2)}, u32[]{:S(2)}) collective-permute-start(bf16[576,256]{1,0:T(8,128)(2,1)S(1)} %collective-permute-done.3.refs_9_), channel_id=1, source_target_pairs={{0,1},{1,0},{2,3},{3,2},{4,5},{5,4},{6,7},{7,6},{8,9},{9,8},{10,11... | collective-permute-start | bytes 884744 | tf_op jit(solution)/shard_map/ppermute | solution.py:564
  21.5 2.0 %collective-permute-start.6 = (bf16[2,576,256]{2,1,0:T(8,128)(2,1)S(1)}, bf16[2,576,256]{2,1,0:T(8,128)(2,1)S(1)}, u32[]{:S(2)}, u32[]{:S(2)}) collective-permute-start(bf16[2,576,256]{2,1,0:T(8,128)(2,1)S(1)} %get-tuple-element.113), channel_id=1, source_target_pairs={{0,1},{1,0},{2,3},{3,2},{4,5},{5,4},{6,7},{7,6},{8,9},{9,8},{10,11... | collective-permute-start | bytes 1769480 | tf_op jit(solution)/shard_map/ppermute | solution.py:564
  23.7 6.9 %collective-permute-start.7 = (bf16[4,72,256]{2,1,0:T(8,128)(2,1)S(1)}, bf16[4,72,256]{2,1,0:T(8,128)(2,1)S(1)}, u32[]{:S(2)}, u32[]{:S(2)}) collective-permute-start(bf16[4,72,256]{2,1,0:T(8,128)(2,1)S(1)} %get-tuple-element.129), channel_id=1, source_target_pairs={{0,2},{1,3},{2,0},{3,1},{4,6},{5,7},{6,4},{7,5},{8,10},{9,11},{10,... | collective-permute-start | bytes 442376 | tf_op jit(solution)/shard_map/ppermute | solution.py:564
  24.4 6.2 %collective-permute-start.8 = (bf16[4,72,256]{2,1,0:T(8,128)(2,1)S(1)}, bf16[4,72,256]{2,1,0:T(8,128)(2,1)S(1)}, u32[]{:S(2)}, u32[]{:S(2)}) collective-permute-start(bf16[4,72,256]{2,1,0:T(8,128)(2,1)S(1)} %get-tuple-element.130), channel_id=1, source_target_pairs={{0,4},{4,0},{8,12},{12,8},{16,20},{20,16},{24,28},{28,24},{1,5},{5... | collective-permute-start | bytes 442376 | tf_op jit(solution)/shard_map/ppermute | solution.py:564
  25.9 38.6 %copy-start.14 = (f32[64,256]{1,0:T(8,128)S(1)}, f32[64,256]{1,0:T(8,128)}, u32[]{:S(2)}) copy-start(f32[64,256]{1,0:T(8,128)} %refs_12_.1) | copy-start | bytes 196612
  25.9 38.6 %copy-start.15 = (f32[64,256]{1,0:T(8,128)S(1)}, f32[64,256]{1,0:T(8,128)}, u32[]{:S(2)}) copy-start(f32[64,256]{1,0:T(8,128)} %refs_13_.1) | copy-start | bytes 196612
  30.4 34.1 %copy-start = (f32[64,1024]{1,0:T(8,128)S(1)}, f32[64,1024]{1,0:T(8,128)}, u32[]{:S(2)}) copy-start(f32[64,1024]{1,0:T(8,128)} %refs_14_.1) | copy-start | bytes 786436
  30.4 34.1 %copy-start.1 = (f32[256,256]{1,0:T(8,128)S(1)}, f32[256,256]{1,0:T(8,128)}, u32[]{:S(2)}) copy-start(f32[256,256]{1,0:T(8,128)} %refs_17_.1) | copy-start | bytes 786436
  30.4 34.1 %copy-start.2 = (f32[64,768]{1,0:T(8,128)S(1)}, f32[64,768]{1,0:T(8,128)}, u32[]{:S(2)}) copy-start(f32[64,768]{1,0:T(8,128)} %refs_8_.1) | copy-start | bytes 589828
  30.4 34.1 %copy-start.4 = (f32[64,256]{1,0:T(8,128)S(1)}, f32[64,256]{1,0:T(8,128)}, u32[]{:S(2)}) copy-start(f32[64,256]{1,0:T(8,128)} %refs_11_.1) | copy-start | bytes 196612
  30.4 34.1 %copy-start.7 = (f32[64,1024]{1,0:T(8,128)S(1)}, f32[64,1024]{1,0:T(8,128)}, u32[]{:S(2)}) copy-start(f32[64,1024]{1,0:T(8,128)} %refs_15_.1) | copy-start | bytes 786436
  30.5 34.1 %copy-start.8 = (f32[64,1024]{1,0:T(8,128)S(1)}, f32[64,1024]{1,0:T(8,128)}, u32[]{:S(2)}) copy-start(f32[64,1024]{1,0:T(8,128)} %refs_16_.1) | copy-start | bytes 786436
  30.5 34.1 %copy-start.9 = (f32[256,256]{1,0:T(8,128)S(1)}, f32[256,256]{1,0:T(8,128)}, u32[]{:S(2)}) copy-start(f32[256,256]{1,0:T(8,128)} %refs_18_.1) | copy-start | bytes 786436
  30.5 34.1 %copy-start.10 = (f32[256,256]{1,0:T(8,128)S(1)}, f32[256,256]{1,0:T(8,128)}, u32[]{:S(2)}) copy-start(f32[256,256]{1,0:T(8,128)} %refs_19_.1) | copy-start | bytes 786436
  30.5 34.1 %copy-start.11 = (f32[64,768]{1,0:T(8,128)S(1)}, f32[64,768]{1,0:T(8,128)}, u32[]{:S(2)}) copy-start(f32[64,768]{1,0:T(8,128)} %refs_9_.1) | copy-start | bytes 589828
  30.5 34.1 %copy-start.12 = (f32[64,768]{1,0:T(8,128)S(1)}, f32[64,768]{1,0:T(8,128)}, u32[]{:S(2)}) copy-start(f32[64,768]{1,0:T(8,128)} %refs_10_.1) | copy-start | bytes 589828
  30.5 34.1 %copy-start.16 = (f32[768]{0:T(1024)S(1)}, f32[768]{0:T(1024)}, u32[]{:S(2)}) copy-start(f32[768]{0:T(1024)} %refs_20_.1) | copy-start | bytes 9220
  30.5 34.1 %copy-start.17 = (f32[768]{0:T(1024)S(1)}, f32[768]{0:T(1024)}, u32[]{:S(2)}) copy-start(f32[768]{0:T(1024)} %refs_21_.1) | copy-start | bytes 9220
  30.5 34.1 %copy-start.18 = (f32[768]{0:T(1024)S(1)}, f32[768]{0:T(1024)}, u32[]{:S(2)}) copy-start(f32[768]{0:T(1024)} %refs_22_.1) | copy-start | bytes 9220
  30.6 1.9 %collective-permute-start.12 = (bf16[2,200,256]{2,1,0:T(8,128)(2,1)S(1)}, bf16[2,200,256]{2,1,0:T(8,128)(2,1)S(1)}, u32[]{:S(2)}, u32[]{:S(2)}) collective-permute-start(bf16[2,200,256]{2,1,0:T(8,128)(2,1)S(1)} %get-tuple-element.139), channel_id=1, source_target_pairs={{0,1},{1,0},{2,3},{3,2},{4,5},{5,4},{6,7},{7,6},{8,9},{9,8},{10,11... | collective-permute-start | bytes 614408 | tf_op jit(solution)/shard_map/ppermute | solution.py:564
  30.7 7.7 %collective-permute-start.9 = (bf16[4,72,256]{2,1,0:T(8,128)(2,1)S(1)}, bf16[4,72,256]{2,1,0:T(8,128)(2,1)S(1)}, u32[]{:S(2)}, u32[]{:S(2)}) collective-permute-start(bf16[4,72,256]{2,1,0:T(8,128)(2,1)S(1)} %get-tuple-element.133), channel_id=1, source_target_pairs={{0,6},{1,7},{2,4},{3,5},{4,2},{5,3},{6,0},{7,1},{8,14},{9,15},{10,... | collective-permute-start | bytes 442376 | tf_op jit(solution)/shard_map/ppermute | solution.py:590
  32.5 7.5 %collective-permute-start.13 = (bf16[4,32,256]{2,1,0:T(8,128)(2,1)S(1)}, bf16[4,32,256]{2,1,0:T(8,128)(2,1)S(1)}, u32[]{:S(2)}, u32[]{:S(2)}) collective-permute-start(bf16[4,32,256]{2,1,0:T(8,128)(2,1)S(1)} %get-tuple-element.141), channel_id=1, source_target_pairs={{0,2},{1,3},{2,0},{3,1},{4,6},{5,7},{6,4},{7,5},{8,10},{9,11},{10,... | collective-permute-start | bytes 196616 | tf_op jit(solution)/shard_map/ppermute | solution.py:564
  33.6 6.4 %collective-permute-start.14 = (bf16[4,32,256]{2,1,0:T(8,128)(2,1)S(1)}, bf16[4,32,256]{2,1,0:T(8,128)(2,1)S(1)}, u32[]{:S(2)}, u32[]{:S(2)}) collective-permute-start(bf16[4,32,256]{2,1,0:T(8,128)(2,1)S(1)} %get-tuple-element.142), channel_id=1, source_target_pairs={{0,4},{4,0},{8,12},{12,8},{16,20},{20,16},{24,28},{28,24},{1,5},{5... | collective-permute-start | bytes 196616 | tf_op jit(solution)/shard_map/ppermute | solution.py:564
  34.6 6.1 %collective-permute-start.15 = (bf16[4,32,256]{2,1,0:T(8,128)(2,1)S(1)}, bf16[4,32,256]{2,1,0:T(8,128)(2,1)S(1)}, u32[]{:S(2)}, u32[]{:S(2)}) collective-permute-start(bf16[4,32,256]{2,1,0:T(8,128)(2,1)S(1)} %get-tuple-element.143), channel_id=1, source_target_pairs={{0,6},{1,7},{2,4},{3,5},{4,2},{5,3},{6,0},{7,1},{8,14},{9,15},{10,... | collective-permute-start | bytes 196616 | tf_op jit(solution)/shard_map/ppermute | solution.py:590
  38.4 4.4 %collective-permute-start.10 = (bf16[2,72,256]{2,1,0:T(8,128)(2,1)S(1)}, bf16[2,72,256]{2,1,0:T(8,128)(2,1)S(1)}, u32[]{:S(2)}, u32[]{:S(2)}) collective-permute-start(bf16[2,72,256]{2,1,0:T(8,128)(2,1)S(1)} %get-tuple-element.135), channel_id=1, source_target_pairs={{0,8},{4,12},{8,0},{12,4},{16,24},{20,28},{24,16},{28,20},{1,9},{5... | collective-permute-start | bytes 221192 | tf_op jit(solution)/shard_map/ppermute | solution.py:564
  40.7 4.8 %collective-permute-start.16 = (bf16[2,32,256]{2,1,0:T(8,128)(2,1)S(1)}, bf16[2,32,256]{2,1,0:T(8,128)(2,1)S(1)}, u32[]{:S(2)}, u32[]{:S(2)}) collective-permute-start(bf16[2,32,256]{2,1,0:T(8,128)(2,1)S(1)} %get-tuple-element.145), channel_id=1, source_target_pairs={{0,8},{4,12},{8,0},{12,4},{16,24},{20,28},{24,16},{28,20},{1,9},{5... | collective-permute-start | bytes 98312 | tf_op jit(solution)/shard_map/ppermute | solution.py:564
  42.8 5.1 %collective-permute-start.11 = (bf16[1,72,256]{2,1,0:T(8,128)(2,1)S(1)}, bf16[1,72,256]{2,1,0:T(8,128)(2,1)S(1)}, u32[]{:S(2)}, u32[]{:S(2)}) collective-permute-start(bf16[1,72,256]{2,1,0:T(8,128)(2,1)S(1)} %get-tuple-element.137), channel_id=1, source_target_pairs={{0,16},{4,20},{8,24},{12,28},{16,0},{20,4},{24,8},{28,12},{1,17},{... | collective-permute-start | bytes 110600 | tf_op jit(solution)/shard_map/ppermute | solution.py:564
  45.5 4.7 %collective-permute-start.17 = (bf16[1,32,256]{2,1,0:T(8,128)(2,1)S(1)}, bf16[1,32,256]{2,1,0:T(8,128)(2,1)S(1)}, u32[]{:S(2)}, u32[]{:S(2)}) collective-permute-start(bf16[1,32,256]{2,1,0:T(8,128)(2,1)S(1)} %get-tuple-element.147), channel_id=1, source_target_pairs={{0,16},{4,20},{8,24},{12,28},{16,0},{20,4},{24,8},{28,12},{1,17},{... | collective-permute-start | bytes 49160 | tf_op jit(solution)/shard_map/ppermute | solution.py:564
  50.2 4.8 %collective-permute-start.19 = (bf16[104,256]{1,0:T(8,128)(2,1)S(1)}, bf16[104,256]{1,0:T(8,128)(2,1)S(1)}, u32[]{:S(2)}, u32[]{:S(2)}) collective-permute-start(bf16[104,256]{1,0:T(8,128)(2,1)S(1)} %piece_sum.1.refs_0_), channel_id=1, source_target_pairs={{0,4},{4,0},{8,12},{12,8},{16,20},{20,16},{24,28},{28,24},{1,5},{5... | collective-permute-start | bytes 159752 | tf_op jit(solution)/shard_map/ppermute | solution.py:564
  51.2 5.1 %collective-permute-start.18 = (bf16[104,256]{1,0:T(8,128)(2,1)S(1)}, bf16[104,256]{1,0:T(8,128)(2,1)S(1)}, u32[]{:S(2)}, u32[]{:S(2)}) collective-permute-start(bf16[104,256]{1,0:T(8,128)(2,1)S(1)} %piece_sum.1.refs_0_), channel_id=1, source_target_pairs={{0,16},{4,20},{8,24},{12,28},{16,0},{20,4},{24,8},{28,12},{1,17},{... | collective-permute-start | bytes 159752 | tf_op jit(solution)/shard_map/ppermute | solution.py:564
  53.1 6.0 %collective-permute-start.20 = (bf16[104,256]{1,0:T(8,128)(2,1)S(1)}, bf16[104,256]{1,0:T(8,128)(2,1)S(1)}, u32[]{:S(2)}, u32[]{:S(2)}) collective-permute-start(bf16[104,256]{1,0:T(8,128)(2,1)S(1)} %piece_sum.1.refs_0_), channel_id=1, source_target_pairs={{0,8},{4,12},{8,0},{12,4},{16,24},{20,28},{24,16},{28,20},{1,9},{5... | collective-permute-start | bytes 159752 | tf_op jit(solution)/shard_map/ppermute | solution.py:564
  56.3 4.1 %collective-permute-start.23 = (bf16[104,256]{1,0:T(8,128)(2,1)S(1)}, bf16[104,256]{1,0:T(8,128)(2,1)S(1)}, u32[]{:S(2)}, u32[]{:S(2)}) collective-permute-start(bf16[104,256]{1,0:T(8,128)(2,1)S(1)} %collective-permute-done.18.refs_4_), channel_id=1, source_target_pairs={{0,8},{4,12},{8,0},{12,4},{16,24},{20,28},{24,16},{28,20},{1,9},{5... | collective-permute-start | bytes 159752 | tf_op jit(solution)/shard_map/ppermute | solution.py:564
  58.1 5.1 %collective-permute-start.22 = (bf16[104,256]{1,0:T(8,128)(2,1)S(1)}, bf16[104,256]{1,0:T(8,128)(2,1)S(1)}, u32[]{:S(2)}, u32[]{:S(2)}) collective-permute-start(bf16[104,256]{1,0:T(8,128)(2,1)S(1)} %collective-permute-done.18.refs_4_), channel_id=1, source_target_pairs={{0,4},{4,0},{8,12},{12,8},{16,20},{20,16},{24,28},{28,24},{1,5},{5... | collective-permute-start | bytes 159752 | tf_op jit(solution)/shard_map/ppermute | solution.py:564
  59.1 4.1 %collective-permute-start.21 = (bf16[104,256]{1,0:T(8,128)(2,1)S(1)}, bf16[104,256]{1,0:T(8,128)(2,1)S(1)}, u32[]{:S(2)}, u32[]{:S(2)}) collective-permute-start(bf16[104,256]{1,0:T(8,128)(2,1)S(1)} %collective-permute-done.20.refs_2_), channel_id=1, source_target_pairs={{0,4},{4,0},{8,12},{12,8},{16,20},{20,16},{24,28},{28,24},{1,5},{5... | collective-permute-start | bytes 159752 | tf_op jit(solution)/shard_map/ppermute | solution.py:564
  60.4 4.1 %collective-permute-start.24 = (bf16[104,256]{1,0:T(8,128)(2,1)S(1)}, bf16[104,256]{1,0:T(8,128)(2,1)S(1)}, u32[]{:S(2)}, u32[]{:S(2)}) collective-permute-start(bf16[104,256]{1,0:T(8,128)(2,1)S(1)} %collective-permute-done.23.refs_6_), channel_id=1, source_target_pairs={{0,4},{4,0},{8,12},{12,8},{16,20},{20,16},{24,28},{28,24},{1,5},{5... | collective-permute-start | bytes 159752 | tf_op jit(solution)/shard_map/ppermute | solution.py:564

commit v13 on v12

--- a/solution.py
+++ b/solution.py
@@ -566,17 +566,19 @@
 
 def gather_pieces(value, group):
     found = {0: value}
-    found[1] = exchange(value, "dp", 1)
-    far = group // 2
-    while far > 1:
+    near = min(group, 4)
+    far = near
+    while far < group:
         for offset in sorted(found):
-            if offset & 1 == 0:
-                found[offset ^ far] = exchange(found[offset], "dp", far)
-        if far == group // 2:
-            found[far], found[1] = lax.optimization_barrier((found[far], found[1]))
-        far //= 2
-    for offset in range(2, group, 2):
-        found[offset ^ 1] = exchange(found[offset], "dp", 1)
+            found[offset ^ far] = exchange(found[offset], "dp", far)
+        far *= 2
+    for offset in range(1, near):
+        found[offset] = exchange(value, "dp", offset)
+    if near < group:
+        found[near], found[1] = lax.optimization_barrier((found[near], found[1]))
+    for base in range(near, group, near):
+        for offset in range(near - 1, 0, -1):
+            found[base ^ offset] = exchange(found[base], "dp", offset)
     return [found[offset] for offset in range(group)]
 
 
@@ -796,9 +798,7 @@
         flops=heads * rows * rows * 256 * 6,
         name="back_last",
     )
-    send_att, arrived_ffn[0], arrived_ffn[1] = lax.optimization_barrier(
-        (send_att, arrived_ffn[0], arrived_ffn[1])
-    )
+    send_att, arrived_ffn = lax.optimization_barrier((send_att, arrived_ffn))
     arrived_att = exchange(send_att, "shard", 1)
     keep_att, *sends_att = quarter_call(kept_att, arrived_att, tail, group, "quarter_att")
     arrived_att = spread(*sends_att)

time: 66.8 us -> 67.1 us (level)
  waiting for transfers between devices: 16.8 us -> 17.8 us
    ppermute x2, waiting for transfers between devices: 2.88 us -> 4.38 us  [corner(): return lax.ppermute(values, ('dp', 'shard'), pairs)]
where the time goes in v13:
time: 67.1 us; the launch traced here: 67 us
  starting transfers between devices  28.5 us (42%)
  Pallas kernels  19.5 us (29%)
  waiting for transfers between devices  17.8 us (27%)
  between operations  1.17 us (2%)
    ppermute x23, starting transfers between devices, exchange(): lax.ppermute(values, axis, [(index, index ^ mask) for index in range(coun...  25.8 us
    pallas_call x15, Pallas kernels, local_call(): pl.pallas_call(kernel, out_shape=outs, in_specs=[pl.BlockSpec(memory_spac...  19.5 us
    ppermute x23, waiting for transfers between devices, exchange(): lax.ppermute(values, axis, [(index, index ^ mask) for index in range(coun...  13.4 us
    ppermute x2, waiting for transfers between devices, corner(): return lax.ppermute(values, ('dp', 'shard'), pairs)  4.38 us
    ppermute x2, starting transfers between devices, corner(): return lax.ppermute(values, ('dp', 'shard'), pairs)  2.66 us
  transfers between devices with their start and end apart: 25, of which 14 were waited for; matrix products, arithmetic and copies ran while one was open for 0% of the time, Pallas kernels for 18%

profile of v13, /device:TPU:0, one launch (start us, length us, event | category | flops | bytes accessed | tf_op | source)
XLA Modules:
  0.0 67.0 jit_solution(17454467509084974474)
XLA Ops:
  0.7 1.7 %pack_first.1.refs_2_.refs_3_.refs_12_ = bf16[208,256]{1,0:T(8,128)(2,1)} custom-call(f32[64,768]{1,0:T(8,128)} %refs_8_.1, f32[768]{0:T(1024)} %refs_20_.1), custom_call_target="tpu_custom_call" | custom-call | bytes 306176 | tf_op jit(solution)/shard_map/pack_first/pallas_call | solution.py:550
  2.4 3.0 %collective-permute-start = (bf16[208,256]{1,0:T(8,128)(2,1)}, bf16[208,256]{1,0:T(8,128)(2,1)S(1)}, u32[]{:S(2)}, u32[]{:S(2)}) collective-permute-start(bf16[208,256]{1,0:T(8,128)(2,1)} %pack_first.1.refs_2_.refs_3_.refs_12_), channel_id=1, source_target_pairs={{0,2},{1,3},{2,0},{3,1},{4,6},{5,7},{6,4},{7,5},{8,10},{9,11},{10,... | collective-permute-start | bytes 319496 | tf_op jit(solution)/shard_map/ppermute | solution.py:564
  5.4 1.8 %pack_second.1.refs_7_ = bf16[576,256]{1,0:T(8,128)(2,1)} custom-call(f32[64,256]{1,0:T(8,128)} %refs_11_.1, f32[64,1024]{1,0:T(8,128)} %refs_14_.1, f32[256,256]{1,0:T(8,128)} %refs_17_.1), custom_call_target="tpu_custom_call" | custom-call | bytes 884736 | tf_op jit(solution)/shard_map/pack_second/pallas_call | solution.py:550
  7.2 0.1 collective-permute-start.3
  7.3 0.1 collective-permute-start.1
  7.4 0.6 prepare.1
  8.1 0.5 collective-permute-done.refs_4_.refs_5_.refs_14_
  8.6 0.1 collective-permute-start.2
  8.7 0.5 collective-permute-start.4
  9.1 0.8 %collective-permute-done.2.refs_5_.refs_6_.refs_15_ = bf16[208,256]{1,0:T(8,128)(2,1)S(1)} collective-permute-done((bf16[208,256]{1,0:T(8,128)(2,1)S(1)}, bf16[208,256]{1,0:T(8,128)(2,1)S(1)}, u32[]{:S(2)}, u32[]{:S(2)}) %collective-permute-start.2) | collective-permute-done | bytes 106528 | tf_op jit(solution)/shard_map/ppermute | solution.py:564
  9.9 3.0 %attend.1 = (bf16[512,768]{1,0:T(8,128)(2,1)S(1)}, bf16[512,256]{1,0:T(8,128)(2,1)S(1)}, f32[8,512]{1,0:T(8,128)S(1)}, f32[256,512]{1,0:T(8,128)S(1)}) custom-call(f32[512,256]{1,0:T(8,128)S(1)} %get-tuple-element.100.refs_0_.refs_8_, f32[512,512]{1,0:T(8,128)S(1)} %get-tuple-element.101.refs_1_.refs_3_, bf16[208,256]{1,0:T(8,128)(2,1)S(1)} %copy-done.13, ...), custom_call_target="tpu_custom_call" | custom-call | flops 1342177280 | bytes 3588096 | tf_op jit(solution)/shard_map/attend/pallas_call | solution.py:550
  12.9 3.1 %collective-permute-done.3.refs_9_ = bf16[576,256]{1,0:T(8,128)(2,1)S(1)} collective-permute-done((bf16[576,256]{1,0:T(8,128)(2,1)}, bf16[576,256]{1,0:T(8,128)(2,1)S(1)}, u32[]{:S(2)}, u32[]{:S(2)}) %collective-permute-start.3) | collective-permute-done | bytes 294944 | tf_op jit(solution)/shard_map/ppermute | solution.py:564
  16.0 1.6 %collective-permute-done.5.refs_10_ = bf16[576,256]{1,0:T(8,128)(2,1)S(1)} collective-permute-done((bf16[576,256]{1,0:T(8,128)(2,1)S(1)}, bf16[576,256]{1,0:T(8,128)(2,1)S(1)}, u32[]{:S(2)}, u32[]{:S(2)}) %collective-permute-start.5) | collective-permute-done | bytes 294944 | tf_op jit(solution)/shard_map/ppermute | solution.py:564
  17.6 3.9 %feed.1 = (bf16[512,256]{1,0:T(8,128)(2,1)}, f32[512,256]{1,0:T(8,128)S(1)}, bf16[512,256]{1,0:T(8,128)(2,1)S(1)}, f32[16,256]{1,0:T(8,128)S(1)}, f32[2,576,256]...) custom-call(bf16[512,256]{1,0:T(8,128)(2,1)S(1)} %copy-done.6, bf16[512,256]{1,0:T(8,128)(2,1)S(1)} %get-tuple-element.105.refs_1_, ...), custom_call_target="tpu_custom_call" | custom-call | flops 1811939328 | bytes 5226496 | tf_op jit(solution)/shard_map/feed/pallas_call | solution.py:550
  21.5 0.1 collective-permute-start.6
  21.6 1.7 %back_first.1 = (bf16[128,512]{1,0:T(8,128)(2,1)S(1)}, f32[512,128]{1,0:T(8,128)S(1)}, f32[512,128]{1,0:T(8,128)S(1)}) custom-call(bf16[512,768]{1,0:T(8,128)(2,1)S(1)} %get-tuple-element.109.refs_0_, bf16[512,256]{1,0:T(8,128)(2,1)S(1)} %get-tuple-element.110.refs_1_, f32[8,512]{1,0:T(8,128)S(1)} %get-tuple-element.111.refs_2_, ...), custom_call_target="tpu_custom_call" | custom-call | flops 1342177280 | bytes 3293184 | tf_op jit(solution)/shard_map/back_first/pallas_call | solution.py:550
  23.3 0.1 collective-permute-done.6.arrived
  23.5 0.2 quarter_ffn.1
  23.7 0.7 %collective-permute-start.7 = (bf16[4,72,256]{2,1,0:T(8,128)(2,1)S(1)}, bf16[4,72,256]{2,1,0:T(8,128)(2,1)S(1)}, u32[]{:S(2)}, u32[]{:S(2)}) collective-permute-start(bf16[4,72,256]{2,1,0:T(8,128)(2,1)S(1)} %get-tuple-element.130), channel_id=1, source_target_pairs={{0,2},{1,3},{2,0},{3,1},{4,6},{5,7},{6,4},{7,5},{8,10},{9,11},{10,... | collective-permute-start | bytes 442376 | tf_op jit(solution)/shard_map/ppermute | solution.py:564
  24.4 1.5 %collective-permute-start.8 = (bf16[4,72,256]{2,1,0:T(8,128)(2,1)S(1)}, bf16[4,72,256]{2,1,0:T(8,128)(2,1)S(1)}, u32[]{:S(2)}, u32[]{:S(2)}) collective-permute-start(bf16[4,72,256]{2,1,0:T(8,128)(2,1)S(1)} %get-tuple-element.131), channel_id=1, source_target_pairs={{0,4},{4,0},{8,12},{12,8},{16,20},{20,16},{24,28},{28,24},{1,5},{5... | collective-permute-start | bytes 442376 | tf_op jit(solution)/shard_map/ppermute | solution.py:564
  25.9 1.3 %collective-permute-start.9 = (bf16[4,72,256]{2,1,0:T(8,128)(2,1)S(1)}, bf16[4,72,256]{2,1,0:T(8,128)(2,1)S(1)}, u32[]{:S(2)}, u32[]{:S(2)}) collective-permute-start(bf16[4,72,256]{2,1,0:T(8,128)(2,1)S(1)} %get-tuple-element.132), channel_id=1, source_target_pairs={{0,6},{1,7},{2,4},{3,5},{4,2},{5,3},{6,0},{7,1},{8,14},{9,15},{10,... | collective-permute-start | bytes 442376 | tf_op jit(solution)/shard_map/ppermute | solution.py:592
  27.2 4.5 %back_last.1 = (f32[512,256]{1,0:T(8,128)}, f32[2,200,256]{2,1,0:T(8,128)S(1)}, bf16[2,200,256]{2,1,0:T(8,128)(2,1)S(1)}) custom-call(bf16[512,768]{1,0:T(8,128)(2,1)S(1)} %get-tuple-element.109.refs_0_, bf16[512,256]{1,0:T(8,128)(2,1)S(1)} %get-tuple-element.110.refs_1_, f32[8,512]{1,0:T(8,128)S(1)} %get-tuple-element.111.refs_2_, ...), custom_call_target="tpu_custom_call" | custom-call | flops 3221225472 | bytes 5924864 | tf_op jit(solution)/shard_map/back_last/pallas_call | solution.py:550
  31.8 2.3 %collective-permute-done.9.refs_2_ = bf16[4,72,256]{2,1,0:T(8,128)(2,1)S(1)} collective-permute-done((bf16[4,72,256]{2,1,0:T(8,128)(2,1)S(1)}, bf16[4,72,256]{2,1,0:T(8,128)(2,1)S(1)}, u32[]{:S(2)}, u32[]{:S(2)}) %collective-permute-start.9) | collective-permute-done | bytes 147488 | tf_op jit(solution)/shard_map/ppermute | solution.py:592
  34.1 1.5 %collective-permute-done.12.arrived = bf16[2,200,256]{2,1,0:T(8,128)(2,1)S(1)} collective-permute-done((bf16[2,200,256]{2,1,0:T(8,128)(2,1)S(1)}, bf16[2,200,256]{2,1,0:T(8,128)(2,1)S(1)}, u32[]{:S(2)}, u32[]{:S(2)}) %collective-permute-start.12) | collective-permute-done | bytes 204832 | tf_op jit(solution)/shard_map/ppermute | solution.py:564
  35.5 0.1 quarter_att.1
  35.6 0.7 %collective-permute-start.13 = (bf16[4,32,256]{2,1,0:T(8,128)(2,1)S(1)}, bf16[4,32,256]{2,1,0:T(8,128)(2,1)S(1)}, u32[]{:S(2)}, u32[]{:S(2)}) collective-permute-start(bf16[4,32,256]{2,1,0:T(8,128)(2,1)S(1)} %get-tuple-element.143), channel_id=1, source_target_pairs={{0,2},{1,3},{2,0},{3,1},{4,6},{5,7},{6,4},{7,5},{8,10},{9,11},{10,... | collective-permute-start | bytes 196616 | tf_op jit(solution)/shard_map/ppermute | solution.py:564
  36.4 1.5 %collective-permute-start.14 = (bf16[4,32,256]{2,1,0:T(8,128)(2,1)S(1)}, bf16[4,32,256]{2,1,0:T(8,128)(2,1)S(1)}, u32[]{:S(2)}, u32[]{:S(2)}) collective-permute-start(bf16[4,32,256]{2,1,0:T(8,128)(2,1)S(1)} %get-tuple-element.144), channel_id=1, source_target_pairs={{0,4},{4,0},{8,12},{12,8},{16,20},{20,16},{24,28},{28,24},{1,5},{5... | collective-permute-start | bytes 196616 | tf_op jit(solution)/shard_map/ppermute | solution.py:564
  37.8 1.3 %collective-permute-start.15 = (bf16[4,32,256]{2,1,0:T(8,128)(2,1)S(1)}, bf16[4,32,256]{2,1,0:T(8,128)(2,1)S(1)}, u32[]{:S(2)}, u32[]{:S(2)}) collective-permute-start(bf16[4,32,256]{2,1,0:T(8,128)(2,1)S(1)} %get-tuple-element.145), channel_id=1, source_target_pairs={{0,6},{1,7},{2,4},{3,5},{4,2},{5,3},{6,0},{7,1},{8,14},{9,15},{10,... | collective-permute-start | bytes 196616 | tf_op jit(solution)/shard_map/ppermute | solution.py:592
  39.2 0.1 halve_dp.4
  39.3 1.6 %collective-permute-start.10 = (bf16[2,72,256]{2,1,0:T(8,128)(2,1)S(1)}, bf16[2,72,256]{2,1,0:T(8,128)(2,1)S(1)}, u32[]{:S(2)}, u32[]{:S(2)}) collective-permute-start(bf16[2,72,256]{2,1,0:T(8,128)(2,1)S(1)} %get-tuple-element.137), channel_id=1, source_target_pairs={{0,8},{4,12},{8,0},{12,4},{16,24},{20,28},{24,16},{28,20},{1,9},{5... | collective-permute-start | bytes 221192 | tf_op jit(solution)/shard_map/ppermute | solution.py:564
  40.9 2.1 %collective-permute-done.15.refs_2_ = bf16[4,32,256]{2,1,0:T(8,128)(2,1)S(1)} collective-permute-done((bf16[4,32,256]{2,1,0:T(8,128)(2,1)S(1)}, bf16[4,32,256]{2,1,0:T(8,128)(2,1)S(1)}, u32[]{:S(2)}, u32[]{:S(2)}) %collective-permute-start.15) | collective-permute-done | bytes 65568 | tf_op jit(solution)/shard_map/ppermute | solution.py:592
  43.1 1.6 %collective-permute-start.16 = (bf16[2,32,256]{2,1,0:T(8,128)(2,1)S(1)}, bf16[2,32,256]{2,1,0:T(8,128)(2,1)S(1)}, u32[]{:S(2)}, u32[]{:S(2)}) collective-permute-start(bf16[2,32,256]{2,1,0:T(8,128)(2,1)S(1)} %get-tuple-element.147), channel_id=1, source_target_pairs={{0,8},{4,12},{8,0},{12,4},{16,24},{20,28},{24,16},{28,20},{1,9},{5... | collective-permute-start | bytes 98312 | tf_op jit(solution)/shard_map/ppermute | solution.py:564
  44.7 2.7 %collective-permute-start.11 = (bf16[1,72,256]{2,1,0:T(8,128)(2,1)S(1)}, bf16[1,72,256]{2,1,0:T(8,128)(2,1)S(1)}, u32[]{:S(2)}, u32[]{:S(2)}) collective-permute-start(bf16[1,72,256]{2,1,0:T(8,128)(2,1)S(1)} %get-tuple-element.139), channel_id=1, source_target_pairs={{0,16},{4,20},{8,24},{12,28},{16,0},{20,4},{24,8},{28,12},{1,17},{... | collective-permute-start | bytes 110600 | tf_op jit(solution)/shard_map/ppermute | solution.py:564
  47.4 2.3 %collective-permute-start.17 = (bf16[1,32,256]{2,1,0:T(8,128)(2,1)S(1)}, bf16[1,32,256]{2,1,0:T(8,128)(2,1)S(1)}, u32[]{:S(2)}, u32[]{:S(2)}) collective-permute-start(bf16[1,32,256]{2,1,0:T(8,128)(2,1)S(1)} %get-tuple-element.149), channel_id=1, source_target_pairs={{0,16},{4,20},{8,24},{12,28},{16,0},{20,4},{24,8},{28,12},{1,17},{... | collective-permute-start | bytes 49160 | tf_op jit(solution)/shard_map/ppermute | solution.py:564
  49.7 0.7 collective-permute-done.11.refs_1_
  50.4 1.7 %collective-permute-done.17.refs_3_ = bf16[1,32,256]{2,1,0:T(8,128)(2,1)S(1)} collective-permute-done((bf16[1,32,256]{2,1,0:T(8,128)(2,1)S(1)}, bf16[1,32,256]{2,1,0:T(8,128)(2,1)S(1)}, u32[]{:S(2)}, u32[]{:S(2)}) %collective-permute-start.17) | collective-permute-done | bytes 16416 | tf_op jit(solution)/shard_map/ppermute | solution.py:564
  52.1 1.0 %collective-permute-start.19 = (bf16[104,256]{1,0:T(8,128)(2,1)S(1)}, bf16[104,256]{1,0:T(8,128)(2,1)S(1)}, u32[]{:S(2)}, u32[]{:S(2)}) collective-permute-start(bf16[104,256]{1,0:T(8,128)(2,1)S(1)} %piece_sum.1.refs_0_), channel_id=1, source_target_pairs={{0,4},{4,0},{8,12},{12,8},{16,20},{20,16},{24,28},{28,24},{1,5},{5... | collective-permute-start | bytes 159752 | tf_op jit(solution)/shard_map/ppermute | solution.py:564
  53.1 2.2 %collective-permute-start.18 = (bf16[104,256]{1,0:T(8,128)(2,1)S(1)}, bf16[104,256]{1,0:T(8,128)(2,1)S(1)}, u32[]{:S(2)}, u32[]{:S(2)}) collective-permute-start(bf16[104,256]{1,0:T(8,128)(2,1)S(1)} %piece_sum.1.refs_0_), channel_id=1, source_target_pairs={{0,16},{4,20},{8,24},{12,28},{16,0},{20,4},{24,8},{28,12},{1,17},{... | collective-permute-start | bytes 159752 | tf_op jit(solution)/shard_map/ppermute | solution.py:564
  55.3 2.2 %collective-permute-start.21 = (bf16[104,256]{1,0:T(8,128)(2,1)S(1)}, bf16[104,256]{1,0:T(8,128)(2,1)S(1)}, u32[]{:S(2)}, u32[]{:S(2)}) collective-permute-start(bf16[104,256]{1,0:T(8,128)(2,1)S(1)} %piece_sum.1.refs_0_), channel_id=1, source_target_pairs={{0,12},{4,8},{8,4},{12,0},{16,28},{20,24},{24,20},{28,16},{1,13},{... | collective-permute-start | bytes 159752 | tf_op jit(solution)/shard_map/ppermute | solution.py:564
  57.5 0.4 collective-permute-start.20
  57.9 0.2 collective-permute-done.18.refs_4_
  58.1 2.2 %collective-permute-start.24 = (bf16[104,256]{1,0:T(8,128)(2,1)S(1)}, bf16[104,256]{1,0:T(8,128)(2,1)S(1)}, u32[]{:S(2)}, u32[]{:S(2)}) collective-permute-start(bf16[104,256]{1,0:T(8,128)(2,1)S(1)} %collective-permute-done.18.refs_4_), channel_id=1, source_target_pairs={{0,12},{4,8},{8,4},{12,0},{16,28},{20,24},{24,20},{28,16},{1,13},{... | collective-permute-start | bytes 159752 | tf_op jit(solution)/shard_map/ppermute | solution.py:564
  60.4 0.3 collective-permute-start.23
  60.7 0.9 %collective-permute-start.22 = (bf16[104,256]{1,0:T(8,128)(2,1)S(1)}, bf16[104,256]{1,0:T(8,128)(2,1)S(1)}, u32[]{:S(2)}, u32[]{:S(2)}) collective-permute-start(bf16[104,256]{1,0:T(8,128)(2,1)S(1)} %collective-permute-done.18.refs_4_), channel_id=1, source_target_pairs={{0,4},{4,0},{8,12},{12,8},{16,20},{20,16},{24,28},{28,24},{1,5},{5... | collective-permute-start | bytes 159752 | tf_op jit(solution)/shard_map/ppermute | solution.py:564
  61.7 1.5 %collective-permute-done.24.refs_7_ = bf16[104,256]{1,0:T(8,128)(2,1)S(1)} collective-permute-done((bf16[104,256]{1,0:T(8,128)(2,1)S(1)}, bf16[104,256]{1,0:T(8,128)(2,1)S(1)}, u32[]{:S(2)}, u32[]{:S(2)}) %collective-permute-start.24) | collective-permute-done | bytes 53280 | tf_op jit(solution)/shard_map/ppermute | solution.py:564
  63.2 1.3 %collective-permute-done.23.refs_6_ = bf16[104,256]{1,0:T(8,128)(2,1)S(1)} collective-permute-done((bf16[104,256]{1,0:T(8,128)(2,1)S(1)}, bf16[104,256]{1,0:T(8,128)(2,1)S(1)}, u32[]{:S(2)}, u32[]{:S(2)}) %collective-permute-start.23) | collective-permute-done | bytes 53280 | tf_op jit(solution)/shard_map/ppermute | solution.py:564
  64.5 0.3 collective-permute-done.22.refs_5_
  65.0 1.8 %adam.1 = (f32[64,768]{1,0:T(8,128)}, f32[64,768]{1,0:T(8,128)}, f32[64,768]{1,0:T(8,128)}, f32[64,256]{1,0:T(8,128)}, f32[64,256]{1,0:T(8,128)}, /*index=5*/f32...) custom-call(bf16[104,256]{1,0:T(8,128)(2,1)S(1)} %piece_sum.1.refs_0, ...), custom_call_target="tpu_custom_call" | custom-call | bytes 5163008 | tf_op jit(solution)/shard_map/adam/pallas_call | solution.py:550
  (59 shorter events, 0.2 us)
Async XLA Ops:
  0.7 6.7 %copy-start.6 = (bf16[512,256]{1,0:T(8,128)(2,1)S(1)}, bf16[512,256]{1,0:T(8,128)(2,1)}, u32[]{:S(2)}) copy-start(bf16[512,256]{1,0:T(8,128)(2,1)} %refs_0_.1) | copy-start | bytes 786436
  0.7 6.7 %copy-start.20 = (s32[128]{0:T(128)S(1)}, s32[128]{0:T(128)}, u32[]{:S(2)}) copy-start(s32[128]{0:T(128)} %param.22) | copy-start | bytes 1540
  0.7 6.7 %copy-start.19 = (s32[128]{0:T(128)S(1)}, s32[128]{0:T(128)}, u32[]{:S(2)}) copy-start(s32[128]{0:T(128)} %param.21) | copy-start | bytes 1540
  0.7 6.7 %copy-start.5 = (bf16[512,256]{1,0:T(8,128)(2,1)S(1)}, bf16[512,256]{1,0:T(8,128)(2,1)}, u32[]{:S(2)}) copy-start(bf16[512,256]{1,0:T(8,128)(2,1)} %seed_ref.1) | copy-start | bytes 786436
  2.4 7.5 %copy-start.13 = (bf16[208,256]{1,0:T(8,128)(2,1)S(1)}, bf16[208,256]{1,0:T(8,128)(2,1)}, u32[]{:S(2)}) copy-start(bf16[208,256]{1,0:T(8,128)(2,1)} %pack_first.1.refs_2_.refs_3_.refs_12_) | copy-start | bytes 319492
  2.4 6.2 %collective-permute-start = (bf16[208,256]{1,0:T(8,128)(2,1)}, bf16[208,256]{1,0:T(8,128)(2,1)S(1)}, u32[]{:S(2)}, u32[]{:S(2)}) collective-permute-start(bf16[208,256]{1,0:T(8,128)(2,1)} %pack_first.1.refs_2_.refs_3_.refs_12_), channel_id=1, source_target_pairs={{0,2},{1,3},{2,0},{3,1},{4,6},{5,7},{6,4},{7,5},{8,10},{9,11},{10,... | collective-permute-start | bytes 319496 | tf_op jit(solution)/shard_map/ppermute | solution.py:564
  7.2 8.7 %collective-permute-start.3 = (bf16[576,256]{1,0:T(8,128)(2,1)}, bf16[576,256]{1,0:T(8,128)(2,1)S(1)}, u32[]{:S(2)}, u32[]{:S(2)}) collective-permute-start(bf16[576,256]{1,0:T(8,128)(2,1)} %pack_second.1.refs_7_), channel_id=1, source_target_pairs={{0,2},{1,3},{2,0},{3,1},{4,6},{5,7},{6,4},{7,5},{8,10},{9,11},{10,... | collective-permute-start | bytes 884744 | tf_op jit(solution)/shard_map/ppermute | solution.py:564
  7.3 1.8 %collective-permute-start.1 = (bf16[208,256]{1,0:T(8,128)(2,1)}, bf16[208,256]{1,0:T(8,128)(2,1)S(1)}, u32[]{:S(2)}, u32[]{:S(2)}) collective-permute-start(bf16[208,256]{1,0:T(8,128)(2,1)} %pack_first.1.refs_2_.refs_3_.refs_12_), channel_id=1, source_target_pairs={{0,1},{1,0},{2,3},{3,2},{4,5},{5,4},{6,7},{7,6},{8,9},{9,8},{10,11... | collective-permute-start | bytes 319496 | tf_op jit(solution)/shard_map/ppermute | solution.py:564
  8.6 9.0 %copy-start.3 = (bf16[576,256]{1,0:T(8,128)(2,1)S(1)}, bf16[576,256]{1,0:T(8,128)(2,1)}, u32[]{:S(2)}) copy-start(bf16[576,256]{1,0:T(8,128)(2,1)} %pack_second.1.refs_7_) | copy-start | bytes 884740
  8.6 1.3 %collective-permute-start.2 = (bf16[208,256]{1,0:T(8,128)(2,1)S(1)}, bf16[208,256]{1,0:T(8,128)(2,1)S(1)}, u32[]{:S(2)}, u32[]{:S(2)}) collective-permute-start(bf16[208,256]{1,0:T(8,128)(2,1)S(1)} %collective-permute-done.refs_4_.refs_5_.refs_14_), channel_id=1, source_target_pairs={{0,1},{1,0},{2,3},{3,2},{4,5},{5,4},{6,7},{7,6},{8,9},{9,8},{10,11... | collective-permute-start | bytes 319496 | tf_op jit(solution)/shard_map/ppermute | solution.py:564
  8.7 7.3 %collective-permute-start.4 = (bf16[576,256]{1,0:T(8,128)(2,1)}, bf16[576,256]{1,0:T(8,128)(2,1)S(1)}, u32[]{:S(2)}, u32[]{:S(2)}) collective-permute-start(bf16[576,256]{1,0:T(8,128)(2,1)} %pack_second.1.refs_7_), channel_id=1, source_target_pairs={{0,1},{1,0},{2,3},{3,2},{4,5},{5,4},{6,7},{7,6},{8,9},{9,8},{10,11... | collective-permute-start | bytes 884744 | tf_op jit(solution)/shard_map/ppermute | solution.py:564
  16.0 1.6 %collective-permute-start.5 = (bf16[576,256]{1,0:T(8,128)(2,1)S(1)}, bf16[576,256]{1,0:T(8,128)(2,1)S(1)}, u32[]{:S(2)}, u32[]{:S(2)}) collective-permute-start(bf16[576,256]{1,0:T(8,128)(2,1)S(1)} %collective-permute-done.3.refs_9_), channel_id=1, source_target_pairs={{0,1},{1,0},{2,3},{3,2},{4,5},{5,4},{6,7},{7,6},{8,9},{9,8},{10,11... | collective-permute-start | bytes 884744 | tf_op jit(solution)/shard_map/ppermute | solution.py:564
  21.5 2.0 %collective-permute-start.6 = (bf16[2,576,256]{2,1,0:T(8,128)(2,1)S(1)}, bf16[2,576,256]{2,1,0:T(8,128)(2,1)S(1)}, u32[]{:S(2)}, u32[]{:S(2)}) collective-permute-start(bf16[2,576,256]{2,1,0:T(8,128)(2,1)S(1)} %get-tuple-element.114), channel_id=1, source_target_pairs={{0,1},{1,0},{2,3},{3,2},{4,5},{5,4},{6,7},{7,6},{8,9},{9,8},{10,11... | collective-permute-start | bytes 1769480 | tf_op jit(solution)/shard_map/ppermute | solution.py:564
  23.7 8.1 %collective-permute-start.7 = (bf16[4,72,256]{2,1,0:T(8,128)(2,1)S(1)}, bf16[4,72,256]{2,1,0:T(8,128)(2,1)S(1)}, u32[]{:S(2)}, u32[]{:S(2)}) collective-permute-start(bf16[4,72,256]{2,1,0:T(8,128)(2,1)S(1)} %get-tuple-element.130), channel_id=1, source_target_pairs={{0,2},{1,3},{2,0},{3,1},{4,6},{5,7},{6,4},{7,5},{8,10},{9,11},{10,... | collective-permute-start | bytes 442376 | tf_op jit(solution)/shard_map/ppermute | solution.py:564
  24.4 7.4 %collective-permute-start.8 = (bf16[4,72,256]{2,1,0:T(8,128)(2,1)S(1)}, bf16[4,72,256]{2,1,0:T(8,128)(2,1)S(1)}, u32[]{:S(2)}, u32[]{:S(2)}) collective-permute-start(bf16[4,72,256]{2,1,0:T(8,128)(2,1)S(1)} %get-tuple-element.131), channel_id=1, source_target_pairs={{0,4},{4,0},{8,12},{12,8},{16,20},{20,16},{24,28},{28,24},{1,5},{5... | collective-permute-start | bytes 442376 | tf_op jit(solution)/shard_map/ppermute | solution.py:564
  25.9 8.2 %collective-permute-start.9 = (bf16[4,72,256]{2,1,0:T(8,128)(2,1)S(1)}, bf16[4,72,256]{2,1,0:T(8,128)(2,1)S(1)}, u32[]{:S(2)}, u32[]{:S(2)}) collective-permute-start(bf16[4,72,256]{2,1,0:T(8,128)(2,1)S(1)} %get-tuple-element.132), channel_id=1, source_target_pairs={{0,6},{1,7},{2,4},{3,5},{4,2},{5,3},{6,0},{7,1},{8,14},{9,15},{10,... | collective-permute-start | bytes 442376 | tf_op jit(solution)/shard_map/ppermute | solution.py:592
  27.2 37.6 %copy-start.14 = (f32[64,256]{1,0:T(8,128)S(1)}, f32[64,256]{1,0:T(8,128)}, u32[]{:S(2)}) copy-start(f32[64,256]{1,0:T(8,128)} %refs_12_.1) | copy-start | bytes 196612
  27.2 37.6 %copy-start.15 = (f32[64,256]{1,0:T(8,128)S(1)}, f32[64,256]{1,0:T(8,128)}, u32[]{:S(2)}) copy-start(f32[64,256]{1,0:T(8,128)} %refs_13_.1) | copy-start | bytes 196612
  31.7 33.2 %copy-start = (f32[64,1024]{1,0:T(8,128)S(1)}, f32[64,1024]{1,0:T(8,128)}, u32[]{:S(2)}) copy-start(f32[64,1024]{1,0:T(8,128)} %refs_14_.1) | copy-start | bytes 786436
  31.7 33.2 %copy-start.1 = (f32[256,256]{1,0:T(8,128)S(1)}, f32[256,256]{1,0:T(8,128)}, u32[]{:S(2)}) copy-start(f32[256,256]{1,0:T(8,128)} %refs_17_.1) | copy-start | bytes 786436
  31.7 33.2 %copy-start.2 = (f32[64,768]{1,0:T(8,128)S(1)}, f32[64,768]{1,0:T(8,128)}, u32[]{:S(2)}) copy-start(f32[64,768]{1,0:T(8,128)} %refs_8_.1) | copy-start | bytes 589828
  31.7 33.2 %copy-start.4 = (f32[64,256]{1,0:T(8,128)S(1)}, f32[64,256]{1,0:T(8,128)}, u32[]{:S(2)}) copy-start(f32[64,256]{1,0:T(8,128)} %refs_11_.1) | copy-start | bytes 196612
  31.7 33.2 %copy-start.7 = (f32[64,1024]{1,0:T(8,128)S(1)}, f32[64,1024]{1,0:T(8,128)}, u32[]{:S(2)}) copy-start(f32[64,1024]{1,0:T(8,128)} %refs_15_.1) | copy-start | bytes 786436
  31.7 33.2 %copy-start.8 = (f32[64,1024]{1,0:T(8,128)S(1)}, f32[64,1024]{1,0:T(8,128)}, u32[]{:S(2)}) copy-start(f32[64,1024]{1,0:T(8,128)} %refs_16_.1) | copy-start | bytes 786436
  31.7 33.2 %copy-start.9 = (f32[256,256]{1,0:T(8,128)S(1)}, f32[256,256]{1,0:T(8,128)}, u32[]{:S(2)}) copy-start(f32[256,256]{1,0:T(8,128)} %refs_18_.1) | copy-start | bytes 786436
  31.7 33.2 %copy-start.10 = (f32[256,256]{1,0:T(8,128)S(1)}, f32[256,256]{1,0:T(8,128)}, u32[]{:S(2)}) copy-start(f32[256,256]{1,0:T(8,128)} %refs_19_.1) | copy-start | bytes 786436
  31.7 33.2 %copy-start.11 = (f32[64,768]{1,0:T(8,128)S(1)}, f32[64,768]{1,0:T(8,128)}, u32[]{:S(2)}) copy-start(f32[64,768]{1,0:T(8,128)} %refs_9_.1) | copy-start | bytes 589828
  31.8 33.2 %copy-start.12 = (f32[64,768]{1,0:T(8,128)S(1)}, f32[64,768]{1,0:T(8,128)}, u32[]{:S(2)}) copy-start(f32[64,768]{1,0:T(8,128)} %refs_10_.1) | copy-start | bytes 589828
  31.8 33.2 %copy-start.16 = (f32[768]{0:T(1024)S(1)}, f32[768]{0:T(1024)}, u32[]{:S(2)}) copy-start(f32[768]{0:T(1024)} %refs_20_.1) | copy-start | bytes 9220
  31.8 33.2 %copy-start.17 = (f32[768]{0:T(1024)S(1)}, f32[768]{0:T(1024)}, u32[]{:S(2)}) copy-start(f32[768]{0:T(1024)} %refs_21_.1) | copy-start | bytes 9220
  31.8 33.2 %copy-start.18 = (f32[768]{0:T(1024)S(1)}, f32[768]{0:T(1024)}, u32[]{:S(2)}) copy-start(f32[768]{0:T(1024)} %refs_22_.1) | copy-start | bytes 9220
  34.1 1.5 %collective-permute-start.12 = (bf16[2,200,256]{2,1,0:T(8,128)(2,1)S(1)}, bf16[2,200,256]{2,1,0:T(8,128)(2,1)S(1)}, u32[]{:S(2)}, u32[]{:S(2)}) collective-permute-start(bf16[2,200,256]{2,1,0:T(8,128)(2,1)S(1)} %get-tuple-element.141), channel_id=1, source_target_pairs={{0,1},{1,0},{2,3},{3,2},{4,5},{5,4},{6,7},{7,6},{8,9},{9,8},{10,11... | collective-permute-start | bytes 614408 | tf_op jit(solution)/shard_map/ppermute | solution.py:564
  35.6 5.3 %collective-permute-start.13 = (bf16[4,32,256]{2,1,0:T(8,128)(2,1)S(1)}, bf16[4,32,256]{2,1,0:T(8,128)(2,1)S(1)}, u32[]{:S(2)}, u32[]{:S(2)}) collective-permute-start(bf16[4,32,256]{2,1,0:T(8,128)(2,1)S(1)} %get-tuple-element.143), channel_id=1, source_target_pairs={{0,2},{1,3},{2,0},{3,1},{4,6},{5,7},{6,4},{7,5},{8,10},{9,11},{10,... | collective-permute-start | bytes 196616 | tf_op jit(solution)/shard_map/ppermute | solution.py:564
  36.4 4.5 %collective-permute-start.14 = (bf16[4,32,256]{2,1,0:T(8,128)(2,1)S(1)}, bf16[4,32,256]{2,1,0:T(8,128)(2,1)S(1)}, u32[]{:S(2)}, u32[]{:S(2)}) collective-permute-start(bf16[4,32,256]{2,1,0:T(8,128)(2,1)S(1)} %get-tuple-element.144), channel_id=1, source_target_pairs={{0,4},{4,0},{8,12},{12,8},{16,20},{20,16},{24,28},{28,24},{1,5},{5... | collective-permute-start | bytes 196616 | tf_op jit(solution)/shard_map/ppermute | solution.py:564
  37.8 5.2 %collective-permute-start.15 = (bf16[4,32,256]{2,1,0:T(8,128)(2,1)S(1)}, bf16[4,32,256]{2,1,0:T(8,128)(2,1)S(1)}, u32[]{:S(2)}, u32[]{:S(2)}) collective-permute-start(bf16[4,32,256]{2,1,0:T(8,128)(2,1)S(1)} %get-tuple-element.145), channel_id=1, source_target_pairs={{0,6},{1,7},{2,4},{3,5},{4,2},{5,3},{6,0},{7,1},{8,14},{9,15},{10,... | collective-permute-start | bytes 196616 | tf_op jit(solution)/shard_map/ppermute | solution.py:592
  39.3 5.4 %collective-permute-start.10 = (bf16[2,72,256]{2,1,0:T(8,128)(2,1)S(1)}, bf16[2,72,256]{2,1,0:T(8,128)(2,1)S(1)}, u32[]{:S(2)}, u32[]{:S(2)}) collective-permute-start(bf16[2,72,256]{2,1,0:T(8,128)(2,1)S(1)} %get-tuple-element.137), channel_id=1, source_target_pairs={{0,8},{4,12},{8,0},{12,4},{16,24},{20,28},{24,16},{28,20},{1,9},{5... | collective-permute-start | bytes 221192 | tf_op jit(solution)/shard_map/ppermute | solution.py:564
  43.1 4.3 %collective-permute-start.16 = (bf16[2,32,256]{2,1,0:T(8,128)(2,1)S(1)}, bf16[2,32,256]{2,1,0:T(8,128)(2,1)S(1)}, u32[]{:S(2)}, u32[]{:S(2)}) collective-permute-start(bf16[2,32,256]{2,1,0:T(8,128)(2,1)S(1)} %get-tuple-element.147), channel_id=1, source_target_pairs={{0,8},{4,12},{8,0},{12,4},{16,24},{20,28},{24,16},{28,20},{1,9},{5... | collective-permute-start | bytes 98312 | tf_op jit(solution)/shard_map/ppermute | solution.py:564
  44.7 5.6 %collective-permute-start.11 = (bf16[1,72,256]{2,1,0:T(8,128)(2,1)S(1)}, bf16[1,72,256]{2,1,0:T(8,128)(2,1)S(1)}, u32[]{:S(2)}, u32[]{:S(2)}) collective-permute-start(bf16[1,72,256]{2,1,0:T(8,128)(2,1)S(1)} %get-tuple-element.139), channel_id=1, source_target_pairs={{0,16},{4,20},{8,24},{12,28},{16,0},{20,4},{24,8},{28,12},{1,17},{... | collective-permute-start | bytes 110600 | tf_op jit(solution)/shard_map/ppermute | solution.py:564
  47.4 4.7 %collective-permute-start.17 = (bf16[1,32,256]{2,1,0:T(8,128)(2,1)S(1)}, bf16[1,32,256]{2,1,0:T(8,128)(2,1)S(1)}, u32[]{:S(2)}, u32[]{:S(2)}) collective-permute-start(bf16[1,32,256]{2,1,0:T(8,128)(2,1)S(1)} %get-tuple-element.149), channel_id=1, source_target_pairs={{0,16},{4,20},{8,24},{12,28},{16,0},{20,4},{24,8},{28,12},{1,17},{... | collective-permute-start | bytes 49160 | tf_op jit(solution)/shard_map/ppermute | solution.py:564
  52.1 5.8 %collective-permute-start.19 = (bf16[104,256]{1,0:T(8,128)(2,1)S(1)}, bf16[104,256]{1,0:T(8,128)(2,1)S(1)}, u32[]{:S(2)}, u32[]{:S(2)}) collective-permute-start(bf16[104,256]{1,0:T(8,128)(2,1)S(1)} %piece_sum.1.refs_0_), channel_id=1, source_target_pairs={{0,4},{4,0},{8,12},{12,8},{16,20},{20,16},{24,28},{28,24},{1,5},{5... | collective-permute-start | bytes 159752 | tf_op jit(solution)/shard_map/ppermute | solution.py:564
  53.1 5.0 %collective-permute-start.18 = (bf16[104,256]{1,0:T(8,128)(2,1)S(1)}, bf16[104,256]{1,0:T(8,128)(2,1)S(1)}, u32[]{:S(2)}, u32[]{:S(2)}) collective-permute-start(bf16[104,256]{1,0:T(8,128)(2,1)S(1)} %piece_sum.1.refs_0_), channel_id=1, source_target_pairs={{0,16},{4,20},{8,24},{12,28},{16,0},{20,4},{24,8},{28,12},{1,17},{... | collective-permute-start | bytes 159752 | tf_op jit(solution)/shard_map/ppermute | solution.py:564
  55.3 6.3 %collective-permute-start.21 = (bf16[104,256]{1,0:T(8,128)(2,1)S(1)}, bf16[104,256]{1,0:T(8,128)(2,1)S(1)}, u32[]{:S(2)}, u32[]{:S(2)}) collective-permute-start(bf16[104,256]{1,0:T(8,128)(2,1)S(1)} %piece_sum.1.refs_0_), channel_id=1, source_target_pairs={{0,12},{4,8},{8,4},{12,0},{16,28},{20,24},{24,20},{28,16},{1,13},{... | collective-permute-start | bytes 159752 | tf_op jit(solution)/shard_map/ppermute | solution.py:564
  57.5 4.1 %collective-permute-start.20 = (bf16[104,256]{1,0:T(8,128)(2,1)S(1)}, bf16[104,256]{1,0:T(8,128)(2,1)S(1)}, u32[]{:S(2)}, u32[]{:S(2)}) collective-permute-start(bf16[104,256]{1,0:T(8,128)(2,1)S(1)} %piece_sum.1.refs_0_), channel_id=1, source_target_pairs={{0,8},{4,12},{8,0},{12,4},{16,24},{20,28},{24,16},{28,20},{1,9},{5... | collective-permute-start | bytes 159752 | tf_op jit(solution)/shard_map/ppermute | solution.py:564
  58.1 5.0 %collective-permute-start.24 = (bf16[104,256]{1,0:T(8,128)(2,1)S(1)}, bf16[104,256]{1,0:T(8,128)(2,1)S(1)}, u32[]{:S(2)}, u32[]{:S(2)}) collective-permute-start(bf16[104,256]{1,0:T(8,128)(2,1)S(1)} %collective-permute-done.18.refs_4_), channel_id=1, source_target_pairs={{0,12},{4,8},{8,4},{12,0},{16,28},{20,24},{24,20},{28,16},{1,13},{... | collective-permute-start | bytes 159752 | tf_op jit(solution)/shard_map/ppermute | solution.py:564
  60.4 4.1 %collective-permute-start.23 = (bf16[104,256]{1,0:T(8,128)(2,1)S(1)}, bf16[104,256]{1,0:T(8,128)(2,1)S(1)}, u32[]{:S(2)}, u32[]{:S(2)}) collective-permute-start(bf16[104,256]{1,0:T(8,128)(2,1)S(1)} %collective-permute-done.18.refs_4_), channel_id=1, source_target_pairs={{0,8},{4,12},{8,0},{12,4},{16,24},{20,28},{24,16},{28,20},{1,9},{5... | collective-permute-start | bytes 159752 | tf_op jit(solution)/shard_map/ppermute | solution.py:564
  60.7 4.1 %collective-permute-start.22 = (bf16[104,256]{1,0:T(8,128)(2,1)S(1)}, bf16[104,256]{1,0:T(8,128)(2,1)S(1)}, u32[]{:S(2)}, u32[]{:S(2)}) collective-permute-start(bf16[104,256]{1,0:T(8,128)(2,1)S(1)} %collective-permute-done.18.refs_4_), channel_id=1, source_target_pairs={{0,4},{4,0},{8,12},{12,8},{16,20},{20,16},{24,28},{28,24},{1,5},{5... | collective-permute-start | bytes 159752 | tf_op jit(solution)/shard_map/ppermute | solution.py:564

commit v14 on v13

--- a/solution.py
+++ b/solution.py
@@ -798,7 +798,9 @@
         flops=heads * rows * rows * 256 * 6,
         name="back_last",
     )
-    send_att, arrived_ffn = lax.optimization_barrier((send_att, arrived_ffn))
+    send_att, arrived_ffn[0], arrived_ffn[1] = lax.optimization_barrier(
+        (send_att, arrived_ffn[0], arrived_ffn[1])
+    )
     arrived_att = exchange(send_att, "shard", 1)
     keep_att, *sends_att = quarter_call(kept_att, arrived_att, tail, group, "quarter_att")
     arrived_att = spread(*sends_att)

time: 67.1 us -> 65.3 us (0.973)
  waiting for transfers between devices: 17.8 us -> 16.2 us
    ppermute x2, waiting for transfers between devices: 4.38 us -> 2.88 us  [corner(): return lax.ppermute(values, ('dp', 'shard'), pairs)]
    ppermute x23, starting transfers between devices: 25.8 us -> 24.8 us  [exchange(): lax.ppermute(values, axis, [(index, index ^ mask) for index in range(coun...]
where the time goes in v14:
time: 65.3 us; the launch traced here: 65.1 us
  starting transfers between devices  28.1 us (43%)
  Pallas kernels  19.6 us (30%)
  waiting for transfers between devices  16.2 us (25%)
  between operations  1.18 us (2%)
    ppermute x23, starting transfers between devices, exchange(): lax.ppermute(values, axis, [(index, index ^ mask) for index in range(coun...  24.8 us
    pallas_call x15, Pallas kernels, local_call(): pl.pallas_call(kernel, out_shape=outs, in_specs=[pl.BlockSpec(memory_spac...  19.6 us
    ppermute x23, waiting for transfers between devices, exchange(): lax.ppermute(values, axis, [(index, index ^ mask) for index in range(coun...  13.3 us
    ppermute x2, starting transfers between devices, corner(): return lax.ppermute(values, ('dp', 'shard'), pairs)  3.25 us
    ppermute x2, waiting for transfers between devices, corner(): return lax.ppermute(values, ('dp', 'shard'), pairs)  2.88 us
  transfers between devices with their start and end apart: 25, of which 14 were waited for; matrix products, arithmetic and copies ran while one was open for 0% of the time, Pallas kernels for 18%

profile of v14, /device:TPU:0, one launch (start us, length us, event | category | flops | bytes accessed | tf_op | source)
XLA Modules:
  0.0 65.1 jit_solution(1498451150869858090)
XLA Ops:
  0.7 1.7 %pack_first.1.refs_2_.refs_3_.refs_12_ = bf16[208,256]{1,0:T(8,128)(2,1)} custom-call(f32[64,768]{1,0:T(8,128)} %refs_8_.1, f32[768]{0:T(1024)} %refs_20_.1), custom_call_target="tpu_custom_call" | custom-call | bytes 306176 | tf_op jit(solution)/shard_map/pack_first/pallas_call | solution.py:550
  2.4 3.0 %collective-permute-start = (bf16[208,256]{1,0:T(8,128)(2,1)}, bf16[208,256]{1,0:T(8,128)(2,1)S(1)}, u32[]{:S(2)}, u32[]{:S(2)}) collective-permute-start(bf16[208,256]{1,0:T(8,128)(2,1)} %pack_first.1.refs_2_.refs_3_.refs_12_), channel_id=1, source_target_pairs={{0,2},{1,3},{2,0},{3,1},{4,6},{5,7},{6,4},{7,5},{8,10},{9,11},{10,... | collective-permute-start | bytes 319496 | tf_op jit(solution)/shard_map/ppermute | solution.py:564
  5.4 1.8 %pack_second.1.refs_7_ = bf16[576,256]{1,0:T(8,128)(2,1)} custom-call(f32[64,256]{1,0:T(8,128)} %refs_11_.1, f32[64,1024]{1,0:T(8,128)} %refs_14_.1, f32[256,256]{1,0:T(8,128)} %refs_17_.1), custom_call_target="tpu_custom_call" | custom-call | bytes 884736 | tf_op jit(solution)/shard_map/pack_second/pallas_call | solution.py:550
  7.2 0.1 collective-permute-start.3
  7.3 0.1 collective-permute-start.1
  7.4 0.6 prepare.1
  8.1 0.5 collective-permute-done.refs_4_.refs_5_.refs_14_
  8.6 0.1 collective-permute-start.2
  8.7 0.5 collective-permute-start.4
  9.1 0.8 %collective-permute-done.2.refs_5_.refs_6_.refs_15_ = bf16[208,256]{1,0:T(8,128)(2,1)S(1)} collective-permute-done((bf16[208,256]{1,0:T(8,128)(2,1)S(1)}, bf16[208,256]{1,0:T(8,128)(2,1)S(1)}, u32[]{:S(2)}, u32[]{:S(2)}) %collective-permute-start.2) | collective-permute-done | bytes 106528 | tf_op jit(solution)/shard_map/ppermute | solution.py:564
  9.9 3.0 %attend.1 = (bf16[512,768]{1,0:T(8,128)(2,1)S(1)}, bf16[512,256]{1,0:T(8,128)(2,1)S(1)}, f32[8,512]{1,0:T(8,128)S(1)}, f32[256,512]{1,0:T(8,128)S(1)}) custom-call(f32[512,256]{1,0:T(8,128)S(1)} %get-tuple-element.99.refs_0_.refs_8_, f32[512,512]{1,0:T(8,128)S(1)} %get-tuple-element.100.refs_1_.refs_3_, bf16[208,256]{1,0:T(8,128)(2,1)S(1)} %copy-done.13, ...), custom_call_target="tpu_custom_call" | custom-call | flops 1342177280 | bytes 3588096 | tf_op jit(solution)/shard_map/attend/pallas_call | solution.py:550
  12.9 3.0 %collective-permute-done.3.refs_9_ = bf16[576,256]{1,0:T(8,128)(2,1)S(1)} collective-permute-done((bf16[576,256]{1,0:T(8,128)(2,1)}, bf16[576,256]{1,0:T(8,128)(2,1)S(1)}, u32[]{:S(2)}, u32[]{:S(2)}) %collective-permute-start.3) | collective-permute-done | bytes 294944 | tf_op jit(solution)/shard_map/ppermute | solution.py:564
  16.0 1.6 %collective-permute-done.5.refs_10_ = bf16[576,256]{1,0:T(8,128)(2,1)S(1)} collective-permute-done((bf16[576,256]{1,0:T(8,128)(2,1)S(1)}, bf16[576,256]{1,0:T(8,128)(2,1)S(1)}, u32[]{:S(2)}, u32[]{:S(2)}) %collective-permute-start.5) | collective-permute-done | bytes 294944 | tf_op jit(solution)/shard_map/ppermute | solution.py:564
  17.6 3.9 %feed.1 = (bf16[512,256]{1,0:T(8,128)(2,1)}, f32[512,256]{1,0:T(8,128)S(1)}, bf16[512,256]{1,0:T(8,128)(2,1)S(1)}, f32[16,256]{1,0:T(8,128)S(1)}, f32[2,576,256]...) custom-call(bf16[512,256]{1,0:T(8,128)(2,1)S(1)} %copy-done.6, bf16[512,256]{1,0:T(8,128)(2,1)S(1)} %get-tuple-element.104.refs_1_, ...), custom_call_target="tpu_custom_call" | custom-call | flops 1811939328 | bytes 5226496 | tf_op jit(solution)/shard_map/feed/pallas_call | solution.py:550
  21.5 0.1 collective-permute-start.6
  21.6 1.7 %back_first.1 = (bf16[128,512]{1,0:T(8,128)(2,1)S(1)}, f32[512,128]{1,0:T(8,128)S(1)}, f32[512,128]{1,0:T(8,128)S(1)}) custom-call(bf16[512,768]{1,0:T(8,128)(2,1)S(1)} %get-tuple-element.108.refs_0_, bf16[512,256]{1,0:T(8,128)(2,1)S(1)} %get-tuple-element.109.refs_1_, f32[8,512]{1,0:T(8,128)S(1)} %get-tuple-element.110.refs_2_, ...), custom_call_target="tpu_custom_call" | custom-call | flops 1342177280 | bytes 3293184 | tf_op jit(solution)/shard_map/back_first/pallas_call | solution.py:550
  23.3 0.1 collective-permute-done.6.arrived
  23.5 0.2 quarter_ffn.1
  23.7 0.7 %collective-permute-start.7 = (bf16[4,72,256]{2,1,0:T(8,128)(2,1)S(1)}, bf16[4,72,256]{2,1,0:T(8,128)(2,1)S(1)}, u32[]{:S(2)}, u32[]{:S(2)}) collective-permute-start(bf16[4,72,256]{2,1,0:T(8,128)(2,1)S(1)} %get-tuple-element.129), channel_id=1, source_target_pairs={{0,2},{1,3},{2,0},{3,1},{4,6},{5,7},{6,4},{7,5},{8,10},{9,11},{10,... | collective-permute-start | bytes 442376 | tf_op jit(solution)/shard_map/ppermute | solution.py:564
  24.4 1.5 %collective-permute-start.8 = (bf16[4,72,256]{2,1,0:T(8,128)(2,1)S(1)}, bf16[4,72,256]{2,1,0:T(8,128)(2,1)S(1)}, u32[]{:S(2)}, u32[]{:S(2)}) collective-permute-start(bf16[4,72,256]{2,1,0:T(8,128)(2,1)S(1)} %get-tuple-element.130), channel_id=1, source_target_pairs={{0,4},{4,0},{8,12},{12,8},{16,20},{20,16},{24,28},{28,24},{1,5},{5... | collective-permute-start | bytes 442376 | tf_op jit(solution)/shard_map/ppermute | solution.py:564
  25.9 4.5 %back_last.1 = (f32[512,256]{1,0:T(8,128)}, f32[2,200,256]{2,1,0:T(8,128)S(1)}, bf16[2,200,256]{2,1,0:T(8,128)(2,1)S(1)}) custom-call(bf16[512,768]{1,0:T(8,128)(2,1)S(1)} %get-tuple-element.108.refs_0_, bf16[512,256]{1,0:T(8,128)(2,1)S(1)} %get-tuple-element.109.refs_1_, f32[8,512]{1,0:T(8,128)S(1)} %get-tuple-element.110.refs_2_, ...), custom_call_target="tpu_custom_call" | custom-call | flops 3221225472 | bytes 5924864 | tf_op jit(solution)/shard_map/back_last/pallas_call | solution.py:550
  30.6 0.1 collective-permute-start.12
  30.7 1.8 %collective-permute-start.9 = (bf16[4,72,256]{2,1,0:T(8,128)(2,1)S(1)}, bf16[4,72,256]{2,1,0:T(8,128)(2,1)S(1)}, u32[]{:S(2)}, u32[]{:S(2)}) collective-permute-start(bf16[4,72,256]{2,1,0:T(8,128)(2,1)S(1)} %get-tuple-element.133), channel_id=1, source_target_pairs={{0,6},{1,7},{2,4},{3,5},{4,2},{5,3},{6,0},{7,1},{8,14},{9,15},{10,... | collective-permute-start | bytes 442376 | tf_op jit(solution)/shard_map/ppermute | solution.py:592
  32.4 0.1 quarter_att.1
  32.5 1.1 %collective-permute-start.13 = (bf16[4,32,256]{2,1,0:T(8,128)(2,1)S(1)}, bf16[4,32,256]{2,1,0:T(8,128)(2,1)S(1)}, u32[]{:S(2)}, u32[]{:S(2)}) collective-permute-start(bf16[4,32,256]{2,1,0:T(8,128)(2,1)S(1)} %get-tuple-element.141), channel_id=1, source_target_pairs={{0,2},{1,3},{2,0},{3,1},{4,6},{5,7},{6,4},{7,5},{8,10},{9,11},{10,... | collective-permute-start | bytes 196616 | tf_op jit(solution)/shard_map/ppermute | solution.py:564
  33.6 1.0 %collective-permute-start.14 = (bf16[4,32,256]{2,1,0:T(8,128)(2,1)S(1)}, bf16[4,32,256]{2,1,0:T(8,128)(2,1)S(1)}, u32[]{:S(2)}, u32[]{:S(2)}) collective-permute-start(bf16[4,32,256]{2,1,0:T(8,128)(2,1)S(1)} %get-tuple-element.142), channel_id=1, source_target_pairs={{0,4},{4,0},{8,12},{12,8},{16,20},{20,16},{24,28},{28,24},{1,5},{5... | collective-permute-start | bytes 196616 | tf_op jit(solution)/shard_map/ppermute | solution.py:564
  34.6 1.5 %collective-permute-start.15 = (bf16[4,32,256]{2,1,0:T(8,128)(2,1)S(1)}, bf16[4,32,256]{2,1,0:T(8,128)(2,1)S(1)}, u32[]{:S(2)}, u32[]{:S(2)}) collective-permute-start(bf16[4,32,256]{2,1,0:T(8,128)(2,1)S(1)} %get-tuple-element.143), channel_id=1, source_target_pairs={{0,6},{1,7},{2,4},{3,5},{4,2},{5,3},{6,0},{7,1},{8,14},{9,15},{10,... | collective-permute-start | bytes 196616 | tf_op jit(solution)/shard_map/ppermute | solution.py:592
  36.1 2.2 %collective-permute-done.9.refs_2_ = bf16[4,72,256]{2,1,0:T(8,128)(2,1)S(1)} collective-permute-done((bf16[4,72,256]{2,1,0:T(8,128)(2,1)S(1)}, bf16[4,72,256]{2,1,0:T(8,128)(2,1)S(1)}, u32[]{:S(2)}, u32[]{:S(2)}) %collective-permute-start.9) | collective-permute-done | bytes 147488 | tf_op jit(solution)/shard_map/ppermute | solution.py:592
  38.3 0.1 halve_dp.4
  38.4 1.6 %collective-permute-start.10 = (bf16[2,72,256]{2,1,0:T(8,128)(2,1)S(1)}, bf16[2,72,256]{2,1,0:T(8,128)(2,1)S(1)}, u32[]{:S(2)}, u32[]{:S(2)}) collective-permute-start(bf16[2,72,256]{2,1,0:T(8,128)(2,1)S(1)} %get-tuple-element.135), channel_id=1, source_target_pairs={{0,8},{4,12},{8,0},{12,4},{16,24},{20,28},{24,16},{28,20},{1,9},{5... | collective-permute-start | bytes 221192 | tf_op jit(solution)/shard_map/ppermute | solution.py:564
  40.0 0.6 collective-permute-done.15.refs_2_
  40.7 1.6 %collective-permute-start.16 = (bf16[2,32,256]{2,1,0:T(8,128)(2,1)S(1)}, bf16[2,32,256]{2,1,0:T(8,128)(2,1)S(1)}, u32[]{:S(2)}, u32[]{:S(2)}) collective-permute-start(bf16[2,32,256]{2,1,0:T(8,128)(2,1)S(1)} %get-tuple-element.145), channel_id=1, source_target_pairs={{0,8},{4,12},{8,0},{12,4},{16,24},{20,28},{24,16},{28,20},{1,9},{5... | collective-permute-start | bytes 98312 | tf_op jit(solution)/shard_map/ppermute | solution.py:564
  42.4 0.5 collective-permute-done.10.refs_0_
  42.8 2.7 %collective-permute-start.11 = (bf16[1,72,256]{2,1,0:T(8,128)(2,1)S(1)}, bf16[1,72,256]{2,1,0:T(8,128)(2,1)S(1)}, u32[]{:S(2)}, u32[]{:S(2)}) collective-permute-start(bf16[1,72,256]{2,1,0:T(8,128)(2,1)S(1)} %get-tuple-element.137), channel_id=1, source_target_pairs={{0,16},{4,20},{8,24},{12,28},{16,0},{20,4},{24,8},{28,12},{1,17},{... | collective-permute-start | bytes 110600 | tf_op jit(solution)/shard_map/ppermute | solution.py:564
  45.5 1.8 %collective-permute-start.17 = (bf16[1,32,256]{2,1,0:T(8,128)(2,1)S(1)}, bf16[1,32,256]{2,1,0:T(8,128)(2,1)S(1)}, u32[]{:S(2)}, u32[]{:S(2)}) collective-permute-start(bf16[1,32,256]{2,1,0:T(8,128)(2,1)S(1)} %get-tuple-element.147), channel_id=1, source_target_pairs={{0,16},{4,20},{8,24},{12,28},{16,0},{20,4},{24,8},{28,12},{1,17},{... | collective-permute-start | bytes 49160 | tf_op jit(solution)/shard_map/ppermute | solution.py:564
  47.4 0.5 collective-permute-done.11.refs_1_
  47.9 2.3 %collective-permute-done.17.refs_3_ = bf16[1,32,256]{2,1,0:T(8,128)(2,1)S(1)} collective-permute-done((bf16[1,32,256]{2,1,0:T(8,128)(2,1)S(1)}, bf16[1,32,256]{2,1,0:T(8,128)(2,1)S(1)}, u32[]{:S(2)}, u32[]{:S(2)}) %collective-permute-start.17) | collective-permute-done | bytes 16416 | tf_op jit(solution)/shard_map/ppermute | solution.py:564
  50.2 1.0 %collective-permute-start.19 = (bf16[104,256]{1,0:T(8,128)(2,1)S(1)}, bf16[104,256]{1,0:T(8,128)(2,1)S(1)}, u32[]{:S(2)}, u32[]{:S(2)}) collective-permute-start(bf16[104,256]{1,0:T(8,128)(2,1)S(1)} %piece_sum.1.refs_0_), channel_id=1, source_target_pairs={{0,4},{4,0},{8,12},{12,8},{16,20},{20,16},{24,28},{28,24},{1,5},{5... | collective-permute-start | bytes 159752 | tf_op jit(solution)/shard_map/ppermute | solution.py:564
  51.2 1.9 %collective-permute-start.18 = (bf16[104,256]{1,0:T(8,128)(2,1)S(1)}, bf16[104,256]{1,0:T(8,128)(2,1)S(1)}, u32[]{:S(2)}, u32[]{:S(2)}) collective-permute-start(bf16[104,256]{1,0:T(8,128)(2,1)S(1)} %piece_sum.1.refs_0_), channel_id=1, source_target_pairs={{0,16},{4,20},{8,24},{12,28},{16,0},{20,4},{24,8},{28,12},{1,17},{... | collective-permute-start | bytes 159752 | tf_op jit(solution)/shard_map/ppermute | solution.py:564
  53.1 2.5 %collective-permute-start.21 = (bf16[104,256]{1,0:T(8,128)(2,1)S(1)}, bf16[104,256]{1,0:T(8,128)(2,1)S(1)}, u32[]{:S(2)}, u32[]{:S(2)}) collective-permute-start(bf16[104,256]{1,0:T(8,128)(2,1)S(1)} %piece_sum.1.refs_0_), channel_id=1, source_target_pairs={{0,12},{4,8},{8,4},{12,0},{16,28},{20,24},{24,20},{28,16},{1,13},{... | collective-permute-start | bytes 159752 | tf_op jit(solution)/shard_map/ppermute | solution.py:564
  55.6 0.7 %collective-permute-done.18.refs_4_ = bf16[104,256]{1,0:T(8,128)(2,1)S(1)} collective-permute-done((bf16[104,256]{1,0:T(8,128)(2,1)S(1)}, bf16[104,256]{1,0:T(8,128)(2,1)S(1)}, u32[]{:S(2)}, u32[]{:S(2)}) %collective-permute-start.18) | collective-permute-done | bytes 53280 | tf_op jit(solution)/shard_map/ppermute | solution.py:564
  56.2 2.5 %collective-permute-start.24 = (bf16[104,256]{1,0:T(8,128)(2,1)S(1)}, bf16[104,256]{1,0:T(8,128)(2,1)S(1)}, u32[]{:S(2)}, u32[]{:S(2)}) collective-permute-start(bf16[104,256]{1,0:T(8,128)(2,1)S(1)} %collective-permute-done.18.refs_4_), channel_id=1, source_target_pairs={{0,12},{4,8},{8,4},{12,0},{16,28},{20,24},{24,20},{28,16},{1,13},{... | collective-permute-start | bytes 159752 | tf_op jit(solution)/shard_map/ppermute | solution.py:564
  58.8 0.1 collective-permute-start.23
  58.8 0.9 %collective-permute-start.22 = (bf16[104,256]{1,0:T(8,128)(2,1)S(1)}, bf16[104,256]{1,0:T(8,128)(2,1)S(1)}, u32[]{:S(2)}, u32[]{:S(2)}) collective-permute-start(bf16[104,256]{1,0:T(8,128)(2,1)S(1)} %collective-permute-done.18.refs_4_), channel_id=1, source_target_pairs={{0,4},{4,0},{8,12},{12,8},{16,20},{20,16},{24,28},{28,24},{1,5},{5... | collective-permute-start | bytes 159752 | tf_op jit(solution)/shard_map/ppermute | solution.py:564
  59.8 1.5 %collective-permute-done.24.refs_7_ = bf16[104,256]{1,0:T(8,128)(2,1)S(1)} collective-permute-done((bf16[104,256]{1,0:T(8,128)(2,1)S(1)}, bf16[104,256]{1,0:T(8,128)(2,1)S(1)}, u32[]{:S(2)}, u32[]{:S(2)}) %collective-permute-start.24) | collective-permute-done | bytes 53280 | tf_op jit(solution)/shard_map/ppermute | solution.py:564
  61.3 1.6 %collective-permute-done.23.refs_6_ = bf16[104,256]{1,0:T(8,128)(2,1)S(1)} collective-permute-done((bf16[104,256]{1,0:T(8,128)(2,1)S(1)}, bf16[104,256]{1,0:T(8,128)(2,1)S(1)}, u32[]{:S(2)}, u32[]{:S(2)}) %collective-permute-start.23) | collective-permute-done | bytes 53280 | tf_op jit(solution)/shard_map/ppermute | solution.py:564
  62.9 0.1 collective-permute-done.22.refs_5_
  63.1 1.8 %adam.1 = (f32[64,768]{1,0:T(8,128)}, f32[64,768]{1,0:T(8,128)}, f32[64,768]{1,0:T(8,128)}, f32[64,256]{1,0:T(8,128)}, f32[64,256]{1,0:T(8,128)}, /*index=5*/f32...) custom-call(bf16[104,256]{1,0:T(8,128)(2,1)S(1)} %piece_sum.1.refs_0, ...), custom_call_target="tpu_custom_call" | custom-call | bytes 5163008 | tf_op jit(solution)/shard_map/adam/pallas_call | solution.py:550
  (59 shorter events, 0.3 us)
Async XLA Ops:
  0.7 6.7 %copy-start.6 = (bf16[512,256]{1,0:T(8,128)(2,1)S(1)}, bf16[512,256]{1,0:T(8,128)(2,1)}, u32[]{:S(2)}) copy-start(bf16[512,256]{1,0:T(8,128)(2,1)} %refs_0_.1) | copy-start | bytes 786436
  0.7 6.7 %copy-start.20 = (s32[128]{0:T(128)S(1)}, s32[128]{0:T(128)}, u32[]{:S(2)}) copy-start(s32[128]{0:T(128)} %param.22) | copy-start | bytes 1540
  0.7 6.7 %copy-start.19 = (s32[128]{0:T(128)S(1)}, s32[128]{0:T(128)}, u32[]{:S(2)}) copy-start(s32[128]{0:T(128)} %param.21) | copy-start | bytes 1540
  0.7 6.7 %copy-start.5 = (bf16[512,256]{1,0:T(8,128)(2,1)S(1)}, bf16[512,256]{1,0:T(8,128)(2,1)}, u32[]{:S(2)}) copy-start(bf16[512,256]{1,0:T(8,128)(2,1)} %seed_ref.1) | copy-start | bytes 786436
  2.4 7.5 %copy-start.13 = (bf16[208,256]{1,0:T(8,128)(2,1)S(1)}, bf16[208,256]{1,0:T(8,128)(2,1)}, u32[]{:S(2)}) copy-start(bf16[208,256]{1,0:T(8,128)(2,1)} %pack_first.1.refs_2_.refs_3_.refs_12_) | copy-start | bytes 319492
  2.4 6.2 %collective-permute-start = (bf16[208,256]{1,0:T(8,128)(2,1)}, bf16[208,256]{1,0:T(8,128)(2,1)S(1)}, u32[]{:S(2)}, u32[]{:S(2)}) collective-permute-start(bf16[208,256]{1,0:T(8,128)(2,1)} %pack_first.1.refs_2_.refs_3_.refs_12_), channel_id=1, source_target_pairs={{0,2},{1,3},{2,0},{3,1},{4,6},{5,7},{6,4},{7,5},{8,10},{9,11},{10,... | collective-permute-start | bytes 319496 | tf_op jit(solution)/shard_map/ppermute | solution.py:564
  7.2 8.7 %collective-permute-start.3 = (bf16[576,256]{1,0:T(8,128)(2,1)}, bf16[576,256]{1,0:T(8,128)(2,1)S(1)}, u32[]{:S(2)}, u32[]{:S(2)}) collective-permute-start(bf16[576,256]{1,0:T(8,128)(2,1)} %pack_second.1.refs_7_), channel_id=1, source_target_pairs={{0,2},{1,3},{2,0},{3,1},{4,6},{5,7},{6,4},{7,5},{8,10},{9,11},{10,... | collective-permute-start | bytes 884744 | tf_op jit(solution)/shard_map/ppermute | solution.py:564
  7.3 1.8 %collective-permute-start.1 = (bf16[208,256]{1,0:T(8,128)(2,1)}, bf16[208,256]{1,0:T(8,128)(2,1)S(1)}, u32[]{:S(2)}, u32[]{:S(2)}) collective-permute-start(bf16[208,256]{1,0:T(8,128)(2,1)} %pack_first.1.refs_2_.refs_3_.refs_12_), channel_id=1, source_target_pairs={{0,1},{1,0},{2,3},{3,2},{4,5},{5,4},{6,7},{7,6},{8,9},{9,8},{10,11... | collective-permute-start | bytes 319496 | tf_op jit(solution)/shard_map/ppermute | solution.py:564
  8.6 9.0 %copy-start.3 = (bf16[576,256]{1,0:T(8,128)(2,1)S(1)}, bf16[576,256]{1,0:T(8,128)(2,1)}, u32[]{:S(2)}) copy-start(bf16[576,256]{1,0:T(8,128)(2,1)} %pack_second.1.refs_7_) | copy-start | bytes 884740
  8.6 1.3 %collective-permute-start.2 = (bf16[208,256]{1,0:T(8,128)(2,1)S(1)}, bf16[208,256]{1,0:T(8,128)(2,1)S(1)}, u32[]{:S(2)}, u32[]{:S(2)}) collective-permute-start(bf16[208,256]{1,0:T(8,128)(2,1)S(1)} %collective-permute-done.refs_4_.refs_5_.refs_14_), channel_id=1, source_target_pairs={{0,1},{1,0},{2,3},{3,2},{4,5},{5,4},{6,7},{7,6},{8,9},{9,8},{10,11... | collective-permute-start | bytes 319496 | tf_op jit(solution)/shard_map/ppermute | solution.py:564
  8.7 7.3 %collective-permute-start.4 = (bf16[576,256]{1,0:T(8,128)(2,1)}, bf16[576,256]{1,0:T(8,128)(2,1)S(1)}, u32[]{:S(2)}, u32[]{:S(2)}) collective-permute-start(bf16[576,256]{1,0:T(8,128)(2,1)} %pack_second.1.refs_7_), channel_id=1, source_target_pairs={{0,1},{1,0},{2,3},{3,2},{4,5},{5,4},{6,7},{7,6},{8,9},{9,8},{10,11... | collective-permute-start | bytes 884744 | tf_op jit(solution)/shard_map/ppermute | solution.py:564
  16.0 1.6 %collective-permute-start.5 = (bf16[576,256]{1,0:T(8,128)(2,1)S(1)}, bf16[576,256]{1,0:T(8,128)(2,1)S(1)}, u32[]{:S(2)}, u32[]{:S(2)}) collective-permute-start(bf16[576,256]{1,0:T(8,128)(2,1)S(1)} %collective-permute-done.3.refs_9_), channel_id=1, source_target_pairs={{0,1},{1,0},{2,3},{3,2},{4,5},{5,4},{6,7},{7,6},{8,9},{9,8},{10,11... | collective-permute-start | bytes 884744 | tf_op jit(solution)/shard_map/ppermute | solution.py:564
  21.5 2.0 %collective-permute-start.6 = (bf16[2,576,256]{2,1,0:T(8,128)(2,1)S(1)}, bf16[2,576,256]{2,1,0:T(8,128)(2,1)S(1)}, u32[]{:S(2)}, u32[]{:S(2)}) collective-permute-start(bf16[2,576,256]{2,1,0:T(8,128)(2,1)S(1)} %get-tuple-element.113), channel_id=1, source_target_pairs={{0,1},{1,0},{2,3},{3,2},{4,5},{5,4},{6,7},{7,6},{8,9},{9,8},{10,11... | collective-permute-start | bytes 1769480 | tf_op jit(solution)/shard_map/ppermute | solution.py:564
  23.7 6.9 %collective-permute-start.7 = (bf16[4,72,256]{2,1,0:T(8,128)(2,1)S(1)}, bf16[4,72,256]{2,1,0:T(8,128)(2,1)S(1)}, u32[]{:S(2)}, u32[]{:S(2)}) collective-permute-start(bf16[4,72,256]{2,1,0:T(8,128)(2,1)S(1)} %get-tuple-element.129), channel_id=1, source_target_pairs={{0,2},{1,3},{2,0},{3,1},{4,6},{5,7},{6,4},{7,5},{8,10},{9,11},{10,... | collective-permute-start | bytes 442376 | tf_op jit(solution)/shard_map/ppermute | solution.py:564
  24.4 6.2 %collective-permute-start.8 = (bf16[4,72,256]{2,1,0:T(8,128)(2,1)S(1)}, bf16[4,72,256]{2,1,0:T(8,128)(2,1)S(1)}, u32[]{:S(2)}, u32[]{:S(2)}) collective-permute-start(bf16[4,72,256]{2,1,0:T(8,128)(2,1)S(1)} %get-tuple-element.130), channel_id=1, source_target_pairs={{0,4},{4,0},{8,12},{12,8},{16,20},{20,16},{24,28},{28,24},{1,5},{5... | collective-permute-start | bytes 442376 | tf_op jit(solution)/shard_map/ppermute | solution.py:564
  25.9 37.1 %copy-start.14 = (f32[64,256]{1,0:T(8,128)S(1)}, f32[64,256]{1,0:T(8,128)}, u32[]{:S(2)}) copy-start(f32[64,256]{1,0:T(8,128)} %refs_12_.1) | copy-start | bytes 196612
  25.9 37.1 %copy-start.15 = (f32[64,256]{1,0:T(8,128)S(1)}, f32[64,256]{1,0:T(8,128)}, u32[]{:S(2)}) copy-start(f32[64,256]{1,0:T(8,128)} %refs_13_.1) | copy-start | bytes 196612
  30.4 32.6 %copy-start = (f32[64,1024]{1,0:T(8,128)S(1)}, f32[64,1024]{1,0:T(8,128)}, u32[]{:S(2)}) copy-start(f32[64,1024]{1,0:T(8,128)} %refs_14_.1) | copy-start | bytes 786436
  30.4 32.6 %copy-start.1 = (f32[256,256]{1,0:T(8,128)S(1)}, f32[256,256]{1,0:T(8,128)}, u32[]{:S(2)}) copy-start(f32[256,256]{1,0:T(8,128)} %refs_17_.1) | copy-start | bytes 786436
  30.4 32.6 %copy-start.2 = (f32[64,768]{1,0:T(8,128)S(1)}, f32[64,768]{1,0:T(8,128)}, u32[]{:S(2)}) copy-start(f32[64,768]{1,0:T(8,128)} %refs_8_.1) | copy-start | bytes 589828
  30.4 32.6 %copy-start.4 = (f32[64,256]{1,0:T(8,128)S(1)}, f32[64,256]{1,0:T(8,128)}, u32[]{:S(2)}) copy-start(f32[64,256]{1,0:T(8,128)} %refs_11_.1) | copy-start | bytes 196612
  30.4 32.6 %copy-start.7 = (f32[64,1024]{1,0:T(8,128)S(1)}, f32[64,1024]{1,0:T(8,128)}, u32[]{:S(2)}) copy-start(f32[64,1024]{1,0:T(8,128)} %refs_15_.1) | copy-start | bytes 786436
  30.5 32.6 %copy-start.8 = (f32[64,1024]{1,0:T(8,128)S(1)}, f32[64,1024]{1,0:T(8,128)}, u32[]{:S(2)}) copy-start(f32[64,1024]{1,0:T(8,128)} %refs_16_.1) | copy-start | bytes 786436
  30.5 32.6 %copy-start.9 = (f32[256,256]{1,0:T(8,128)S(1)}, f32[256,256]{1,0:T(8,128)}, u32[]{:S(2)}) copy-start(f32[256,256]{1,0:T(8,128)} %refs_18_.1) | copy-start | bytes 786436
  30.5 32.6 %copy-start.10 = (f32[256,256]{1,0:T(8,128)S(1)}, f32[256,256]{1,0:T(8,128)}, u32[]{:S(2)}) copy-start(f32[256,256]{1,0:T(8,128)} %refs_19_.1) | copy-start | bytes 786436
  30.5 32.6 %copy-start.11 = (f32[64,768]{1,0:T(8,128)S(1)}, f32[64,768]{1,0:T(8,128)}, u32[]{:S(2)}) copy-start(f32[64,768]{1,0:T(8,128)} %refs_9_.1) | copy-start | bytes 589828
  30.5 32.6 %copy-start.12 = (f32[64,768]{1,0:T(8,128)S(1)}, f32[64,768]{1,0:T(8,128)}, u32[]{:S(2)}) copy-start(f32[64,768]{1,0:T(8,128)} %refs_10_.1) | copy-start | bytes 589828
  30.5 32.6 %copy-start.16 = (f32[768]{0:T(1024)S(1)}, f32[768]{0:T(1024)}, u32[]{:S(2)}) copy-start(f32[768]{0:T(1024)} %refs_20_.1) | copy-start | bytes 9220
  30.5 32.6 %copy-start.17 = (f32[768]{0:T(1024)S(1)}, f32[768]{0:T(1024)}, u32[]{:S(2)}) copy-start(f32[768]{0:T(1024)} %refs_21_.1) | copy-start | bytes 9220
  30.5 32.6 %copy-start.18 = (f32[768]{0:T(1024)S(1)}, f32[768]{0:T(1024)}, u32[]{:S(2)}) copy-start(f32[768]{0:T(1024)} %refs_22_.1) | copy-start | bytes 9220
  30.6 1.9 %collective-permute-start.12 = (bf16[2,200,256]{2,1,0:T(8,128)(2,1)S(1)}, bf16[2,200,256]{2,1,0:T(8,128)(2,1)S(1)}, u32[]{:S(2)}, u32[]{:S(2)}) collective-permute-start(bf16[2,200,256]{2,1,0:T(8,128)(2,1)S(1)} %get-tuple-element.139), channel_id=1, source_target_pairs={{0,1},{1,0},{2,3},{3,2},{4,5},{5,4},{6,7},{7,6},{8,9},{9,8},{10,11... | collective-permute-start | bytes 614408 | tf_op jit(solution)/shard_map/ppermute | solution.py:564
  30.7 7.7 %collective-permute-start.9 = (bf16[4,72,256]{2,1,0:T(8,128)(2,1)S(1)}, bf16[4,72,256]{2,1,0:T(8,128)(2,1)S(1)}, u32[]{:S(2)}, u32[]{:S(2)}) collective-permute-start(bf16[4,72,256]{2,1,0:T(8,128)(2,1)S(1)} %get-tuple-element.133), channel_id=1, source_target_pairs={{0,6},{1,7},{2,4},{3,5},{4,2},{5,3},{6,0},{7,1},{8,14},{9,15},{10,... | collective-permute-start | bytes 442376 | tf_op jit(solution)/shard_map/ppermute | solution.py:592
  32.5 7.5 %collective-permute-start.13 = (bf16[4,32,256]{2,1,0:T(8,128)(2,1)S(1)}, bf16[4,32,256]{2,1,0:T(8,128)(2,1)S(1)}, u32[]{:S(2)}, u32[]{:S(2)}) collective-permute-start(bf16[4,32,256]{2,1,0:T(8,128)(2,1)S(1)} %get-tuple-element.141), channel_id=1, source_target_pairs={{0,2},{1,3},{2,0},{3,1},{4,6},{5,7},{6,4},{7,5},{8,10},{9,11},{10,... | collective-permute-start | bytes 196616 | tf_op jit(solution)/shard_map/ppermute | solution.py:564
  33.6 6.4 %collective-permute-start.14 = (bf16[4,32,256]{2,1,0:T(8,128)(2,1)S(1)}, bf16[4,32,256]{2,1,0:T(8,128)(2,1)S(1)}, u32[]{:S(2)}, u32[]{:S(2)}) collective-permute-start(bf16[4,32,256]{2,1,0:T(8,128)(2,1)S(1)} %get-tuple-element.142), channel_id=1, source_target_pairs={{0,4},{4,0},{8,12},{12,8},{16,20},{20,16},{24,28},{28,24},{1,5},{5... | collective-permute-start | bytes 196616 | tf_op jit(solution)/shard_map/ppermute | solution.py:564
  34.6 6.1 %collective-permute-start.15 = (bf16[4,32,256]{2,1,0:T(8,128)(2,1)S(1)}, bf16[4,32,256]{2,1,0:T(8,128)(2,1)S(1)}, u32[]{:S(2)}, u32[]{:S(2)}) collective-permute-start(bf16[4,32,256]{2,1,0:T(8,128)(2,1)S(1)} %get-tuple-element.143), channel_id=1, source_target_pairs={{0,6},{1,7},{2,4},{3,5},{4,2},{5,3},{6,0},{7,1},{8,14},{9,15},{10,... | collective-permute-start | bytes 196616 | tf_op jit(solution)/shard_map/ppermute | solution.py:592
  38.4 4.4 %collective-permute-start.10 = (bf16[2,72,256]{2,1,0:T(8,128)(2,1)S(1)}, bf16[2,72,256]{2,1,0:T(8,128)(2,1)S(1)}, u32[]{:S(2)}, u32[]{:S(2)}) collective-permute-start(bf16[2,72,256]{2,1,0:T(8,128)(2,1)S(1)} %get-tuple-element.135), channel_id=1, source_target_pairs={{0,8},{4,12},{8,0},{12,4},{16,24},{20,28},{24,16},{28,20},{1,9},{5... | collective-permute-start | bytes 221192 | tf_op jit(solution)/shard_map/ppermute | solution.py:564
  40.7 4.8 %collective-permute-start.16 = (bf16[2,32,256]{2,1,0:T(8,128)(2,1)S(1)}, bf16[2,32,256]{2,1,0:T(8,128)(2,1)S(1)}, u32[]{:S(2)}, u32[]{:S(2)}) collective-permute-start(bf16[2,32,256]{2,1,0:T(8,128)(2,1)S(1)} %get-tuple-element.145), channel_id=1, source_target_pairs={{0,8},{4,12},{8,0},{12,4},{16,24},{20,28},{24,16},{28,20},{1,9},{5... | collective-permute-start | bytes 98312 | tf_op jit(solution)/shard_map/ppermute | solution.py:564
  42.8 5.1 %collective-permute-start.11 = (bf16[1,72,256]{2,1,0:T(8,128)(2,1)S(1)}, bf16[1,72,256]{2,1,0:T(8,128)(2,1)S(1)}, u32[]{:S(2)}, u32[]{:S(2)}) collective-permute-start(bf16[1,72,256]{2,1,0:T(8,128)(2,1)S(1)} %get-tuple-element.137), channel_id=1, source_target_pairs={{0,16},{4,20},{8,24},{12,28},{16,0},{20,4},{24,8},{28,12},{1,17},{... | collective-permute-start | bytes 110600 | tf_op jit(solution)/shard_map/ppermute | solution.py:564
  45.5 4.7 %collective-permute-start.17 = (bf16[1,32,256]{2,1,0:T(8,128)(2,1)S(1)}, bf16[1,32,256]{2,1,0:T(8,128)(2,1)S(1)}, u32[]{:S(2)}, u32[]{:S(2)}) collective-permute-start(bf16[1,32,256]{2,1,0:T(8,128)(2,1)S(1)} %get-tuple-element.147), channel_id=1, source_target_pairs={{0,16},{4,20},{8,24},{12,28},{16,0},{20,4},{24,8},{28,12},{1,17},{... | collective-permute-start | bytes 49160 | tf_op jit(solution)/shard_map/ppermute | solution.py:564
  50.2 5.3 %collective-permute-start.19 = (bf16[104,256]{1,0:T(8,128)(2,1)S(1)}, bf16[104,256]{1,0:T(8,128)(2,1)S(1)}, u32[]{:S(2)}, u32[]{:S(2)}) collective-permute-start(bf16[104,256]{1,0:T(8,128)(2,1)S(1)} %piece_sum.1.refs_0_), channel_id=1, source_target_pairs={{0,4},{4,0},{8,12},{12,8},{16,20},{20,16},{24,28},{28,24},{1,5},{5... | collective-permute-start | bytes 159752 | tf_op jit(solution)/shard_map/ppermute | solution.py:564
  51.2 5.0 %collective-permute-start.18 = (bf16[104,256]{1,0:T(8,128)(2,1)S(1)}, bf16[104,256]{1,0:T(8,128)(2,1)S(1)}, u32[]{:S(2)}, u32[]{:S(2)}) collective-permute-start(bf16[104,256]{1,0:T(8,128)(2,1)S(1)} %piece_sum.1.refs_0_), channel_id=1, source_target_pairs={{0,16},{4,20},{8,24},{12,28},{16,0},{20,4},{24,8},{28,12},{1,17},{... | collective-permute-start | bytes 159752 | tf_op jit(solution)/shard_map/ppermute | solution.py:564
  53.1 6.7 %collective-permute-start.21 = (bf16[104,256]{1,0:T(8,128)(2,1)S(1)}, bf16[104,256]{1,0:T(8,128)(2,1)S(1)}, u32[]{:S(2)}, u32[]{:S(2)}) collective-permute-start(bf16[104,256]{1,0:T(8,128)(2,1)S(1)} %piece_sum.1.refs_0_), channel_id=1, source_target_pairs={{0,12},{4,8},{8,4},{12,0},{16,28},{20,24},{24,20},{28,16},{1,13},{... | collective-permute-start | bytes 159752 | tf_op jit(solution)/shard_map/ppermute | solution.py:564
  55.5 4.2 %collective-permute-start.20 = (bf16[104,256]{1,0:T(8,128)(2,1)S(1)}, bf16[104,256]{1,0:T(8,128)(2,1)S(1)}, u32[]{:S(2)}, u32[]{:S(2)}) collective-permute-start(bf16[104,256]{1,0:T(8,128)(2,1)S(1)} %piece_sum.1.refs_0_), channel_id=1, source_target_pairs={{0,8},{4,12},{8,0},{12,4},{16,24},{20,28},{24,16},{28,20},{1,9},{5... | collective-permute-start | bytes 159752 | tf_op jit(solution)/shard_map/ppermute | solution.py:564
  56.2 5.0 %collective-permute-start.24 = (bf16[104,256]{1,0:T(8,128)(2,1)S(1)}, bf16[104,256]{1,0:T(8,128)(2,1)S(1)}, u32[]{:S(2)}, u32[]{:S(2)}) collective-permute-start(bf16[104,256]{1,0:T(8,128)(2,1)S(1)} %collective-permute-done.18.refs_4_), channel_id=1, source_target_pairs={{0,12},{4,8},{8,4},{12,0},{16,28},{20,24},{24,20},{28,16},{1,13},{... | collective-permute-start | bytes 159752 | tf_op jit(solution)/shard_map/ppermute | solution.py:564
  58.8 4.1 %collective-permute-start.23 = (bf16[104,256]{1,0:T(8,128)(2,1)S(1)}, bf16[104,256]{1,0:T(8,128)(2,1)S(1)}, u32[]{:S(2)}, u32[]{:S(2)}) collective-permute-start(bf16[104,256]{1,0:T(8,128)(2,1)S(1)} %collective-permute-done.18.refs_4_), channel_id=1, source_target_pairs={{0,8},{4,12},{8,0},{12,4},{16,24},{20,28},{24,16},{28,20},{1,9},{5... | collective-permute-start | bytes 159752 | tf_op jit(solution)/shard_map/ppermute | solution.py:564
  58.8 4.1 %collective-permute-start.22 = (bf16[104,256]{1,0:T(8,128)(2,1)S(1)}, bf16[104,256]{1,0:T(8,128)(2,1)S(1)}, u32[]{:S(2)}, u32[]{:S(2)}) collective-permute-start(bf16[104,256]{1,0:T(8,128)(2,1)S(1)} %collective-permute-done.18.refs_4_), channel_id=1, source_target_pairs={{0,4},{4,0},{8,12},{12,8},{16,20},{20,16},{24,28},{28,24},{1,5},{5... | collective-permute-start | bytes 159752 | tf_op jit(solution)/shard_map/ppermute | solution.py:564

commit v15 on v14

--- a/solution.py
+++ b/solution.py
@@ -301,7 +301,7 @@
             at = part + block * part
             grads_ref[target, at : at + part, :] = grad_up[target * part : (target + 1) * part, :]
         sums_ref[4 + block : 5 + block, :] = jnp.sum(dpre.astype(wide), axis=0, keepdims=True)
-    out_ref[...] = result.astype(low)
+    out_ref[...] = result
     through, gain_grad, shift_grad = norm_back(dhidden, normed, root, gain)
     dmiddle = seed + through
     middle_ref[...] = dmiddle
@@ -422,7 +422,7 @@
         if block != 1:
             bias_sums.append(jnp.sum(piece.astype(wide), axis=0, keepdims=True))
     through, gain_grad, shift_grad = norm_back(dhidden, normed, root, gain)
-    dx_ref[...] = middle_ref[...] + through
+    dx_ref[...] = through
     sums = [gain_grad, shift_grad, sums_in[0:1, :], sums_in[1:2, :]] + bias_sums
     sums += [sums_in[row : row + 1, :] for row in range(2, 8)]
     per_shard = len(sums) // shards
@@ -747,10 +747,10 @@
     seconds[3] = exchange(seconds[2], "shard", 1)
     seconds = [seconds[offset] for offset in range(shards)]
     pair = (shards // 2, second_rows, width)
-    output, middle_grad, attended_grad, sums, kept_ffn, send_ffn = local_call(
+    result, middle_grad, attended_grad, sums, kept_ffn, send_ffn = local_call(
         functools.partial(feed_kernel, shards),
         [
-            ((rows, width), low),
+            ((rows, width), wide),
             ((rows, width), wide),
             ((rows, width), low),
             ((SMALL_PAD, width), wide),
@@ -788,7 +788,7 @@
     arrived_ffn = spread(*sends_ffn)
     att_rows = 3 * part + tail
     pair = (shards // 2, att_rows, width)
-    input_grad, kept_att, send_att = local_call(
+    through, kept_att, send_att = local_call(
         functools.partial(back_last_kernel, shards, groups[1:]),
         [((rows, width), wide), (pair, wide), (pair, low)],
         shared + [first_query, first_key, first_value, normed, root, middle_grad, sums] + firsts,
@@ -826,7 +826,7 @@
             (second_rows + 3 * part, 1, 0.0),
         ],
     )
-    return (output, input_grad, *results)
+    return (result.astype(low), middle_grad + through, *results)
 
 
 def solution(mesh):

time: 65.3 us -> 64.2 us (0.983)
  waiting for transfers between devices: 16.2 us -> 14.3 us
  other arithmetic: 0 us -> 1.59 us
  Pallas kernels: 19.6 us -> 18.2 us
    pallas_call x15, Pallas kernels: 19.6 us -> 18.2 us  [local_call(): pl.pallas_call(kernel, out_shape=outs, in_specs=[pl.BlockSpec(memory_spac...]
    ppermute x23, waiting for transfers between devices: 13.3 us -> 11.9 us  [exchange(): lax.ppermute(values, axis, [(index, index ^ mask) for index in range(coun...]
    add x0 -> x1, other arithmetic: none -> 0.86 us  [shards_program(): return (result.astype(low), middle_grad + through, *results)]
    convert_element_type x0 -> x1, other arithmetic: none -> 0.73 us  [shards_program(): return (result.astype(low), middle_grad + through, *results)]
  transfers between devices with their start and end apart: 25 -> 25, of which waited for: 14 -> 15; matrix products, arithmetic and copies ran while one was open for 0% -> 2% of each run, Pallas kernels for 18% -> 17%
where the time goes in v15:
time: 64.2 us; the launch traced here: 64.1 us
  starting transfers between devices  28.7 us (45%)
  Pallas kernels  18.2 us (28%)
  waiting for transfers between devices  14.3 us (22%)
  other arithmetic  1.59 us (2%)
  between operations  1.16 us (2%)
    ppermute x23, starting transfers between devices, exchange(): lax.ppermute(values, axis, [(index, index ^ mask) for index in range(coun...  25 us
    pallas_call x15, Pallas kernels, local_call(): pl.pallas_call(kernel, out_shape=outs, in_specs=[pl.BlockSpec(memory_spac...  18.2 us
    ppermute x23, waiting for transfers between devices, exchange(): lax.ppermute(values, axis, [(index, index ^ mask) for index in range(coun...  11.9 us
    ppermute x2, starting transfers between devices, corner(): return lax.ppermute(values, ('dp', 'shard'), pairs)  3.76 us
    ppermute x2, waiting for transfers between devices, corner(): return lax.ppermute(values, ('dp', 'shard'), pairs)  2.33 us
  transfers between devices with their start and end apart: 25, of which 15 were waited for; matrix products, arithmetic and copies ran while one was open for 2% of the time, Pallas kernels for 17%

profile of v15, /device:TPU:0, one launch (start us, length us, event | category | flops | bytes accessed | tf_op | source)
XLA Modules:
  0.0 64.1 jit_solution(13879829165675327625)
XLA Ops:
  0.7 1.7 %pack_first.1.refs_2_.refs_3_.refs_12_ = bf16[208,256]{1,0:T(8,128)(2,1)} custom-call(f32[64,768]{1,0:T(8,128)} %refs_8_.1, f32[768]{0:T(1024)} %refs_20_.1), custom_call_target="tpu_custom_call" | custom-call | bytes 306176 | tf_op jit(solution)/shard_map/pack_first/pallas_call | solution.py:550
  2.4 3.0 %collective-permute-start = (bf16[208,256]{1,0:T(8,128)(2,1)}, bf16[208,256]{1,0:T(8,128)(2,1)S(1)}, u32[]{:S(2)}, u32[]{:S(2)}) collective-permute-start(bf16[208,256]{1,0:T(8,128)(2,1)} %pack_first.1.refs_2_.refs_3_.refs_12_), channel_id=1, source_target_pairs={{0,2},{1,3},{2,0},{3,1},{4,6},{5,7},{6,4},{7,5},{8,10},{9,11},{10,... | collective-permute-start | bytes 319496 | tf_op jit(solution)/shard_map/ppermute | solution.py:564
  5.4 1.8 %pack_second.1.refs_7_ = bf16[576,256]{1,0:T(8,128)(2,1)} custom-call(f32[64,256]{1,0:T(8,128)} %refs_11_.1, f32[64,1024]{1,0:T(8,128)} %refs_14_.1, f32[256,256]{1,0:T(8,128)} %refs_17_.1), custom_call_target="tpu_custom_call" | custom-call | bytes 884736 | tf_op jit(solution)/shard_map/pack_second/pallas_call | solution.py:550
  7.2 0.1 collective-permute-start.3
  7.4 0.6 %prepare.1 = (f32[512,512]{1,0:T(8,128)S(1)}, f32[512,256]{1,0:T(8,128)S(1)}, f32[512,1]{1,0:T(8,128)S(1)}, bf16[512,256]{1,0:T(8,128)(2,1)S(1)}) custom-call(bf16[512,256]{1,0:T(8,128)(2,1)S(1)} %copy-done.6, bf16[512,256]{1,0:T(8,128)(2,1)S(1)} %copy-done.5, s32[1,128]{1,0:T(1,128)S(1)} %bitcast.2, s32[1,128]{1,0:T(1,128)S(1)} %bitcast.3), custom_call_target="tpu_custom_call" | custom-call | bytes 2362368 | tf_op jit(solution)/shard_map/prepare/pallas_call | solution.py:550
  8.1 0.5 collective-permute-done.refs_4_.refs_5_.refs_14_
  8.7 0.5 collective-permute-start.4
  9.1 0.8 %collective-permute-done.2.refs_5_.refs_6_.refs_15_ = bf16[208,256]{1,0:T(8,128)(2,1)S(1)} collective-permute-done((bf16[208,256]{1,0:T(8,128)(2,1)S(1)}, bf16[208,256]{1,0:T(8,128)(2,1)S(1)}, u32[]{:S(2)}, u32[]{:S(2)}) %collective-permute-start.2) | collective-permute-done | bytes 106528 | tf_op jit(solution)/shard_map/ppermute | solution.py:564
  9.9 3.0 %attend.1 = (bf16[512,768]{1,0:T(8,128)(2,1)S(1)}, bf16[512,256]{1,0:T(8,128)(2,1)S(1)}, f32[8,512]{1,0:T(8,128)S(1)}, f32[256,512]{1,0:T(8,128)S(1)}) custom-call(f32[512,256]{1,0:T(8,128)S(1)} %get-tuple-element.99.refs_0_.refs_8_, f32[512,512]{1,0:T(8,128)S(1)} %get-tuple-element.100.refs_1_.refs_3_, bf16[208,256]{1,0:T(8,128)(2,1)S(1)} %copy-done.13, ...), custom_call_target="tpu_custom_call" | custom-call | flops 1342177280 | bytes 3588096 | tf_op jit(solution)/shard_map/attend/pallas_call | solution.py:550
  12.9 3.1 %collective-permute-done.3.refs_9_ = bf16[576,256]{1,0:T(8,128)(2,1)S(1)} collective-permute-done((bf16[576,256]{1,0:T(8,128)(2,1)}, bf16[576,256]{1,0:T(8,128)(2,1)S(1)}, u32[]{:S(2)}, u32[]{:S(2)}) %collective-permute-start.3) | collective-permute-done | bytes 294944 | tf_op jit(solution)/shard_map/ppermute | solution.py:564
  16.0 1.6 %collective-permute-done.5.refs_10_ = bf16[576,256]{1,0:T(8,128)(2,1)S(1)} collective-permute-done((bf16[576,256]{1,0:T(8,128)(2,1)S(1)}, bf16[576,256]{1,0:T(8,128)(2,1)S(1)}, u32[]{:S(2)}, u32[]{:S(2)}) %collective-permute-start.5) | collective-permute-done | bytes 294944 | tf_op jit(solution)/shard_map/ppermute | solution.py:564
  17.6 3.4 %feed.1 = (f32[512,256]{1,0:T(8,128)S(1)}, f32[512,256]{1,0:T(8,128)S(1)}, bf16[512,256]{1,0:T(8,128)(2,1)S(1)}, f32[16,256]{1,0:T(8,128)S(1)}, f32[2,576,256]{2...) custom-call(bf16[512,256]{1,0:T(8,128)(2,1)S(1)} %copy-done.6, bf16[512,256]{1,0:T(8,128)(2,1)S(1)} %get-tuple-element.104.refs_1_, ...), custom_call_target="tpu_custom_call" | custom-call | flops 1811939328 | bytes 5488640 | tf_op jit(solution)/shard_map/feed/pallas_call | solution.py:550
  21.0 0.2 collective-permute-start.6
  21.2 1.7 %back_first.1 = (bf16[128,512]{1,0:T(8,128)(2,1)S(1)}, f32[512,128]{1,0:T(8,128)S(1)}, f32[512,128]{1,0:T(8,128)S(1)}) custom-call(bf16[512,768]{1,0:T(8,128)(2,1)S(1)} %get-tuple-element.109.refs_0_, bf16[512,256]{1,0:T(8,128)(2,1)S(1)} %get-tuple-element.110.refs_1_, f32[8,512]{1,0:T(8,128)S(1)} %get-tuple-element.111.refs_2_, ...), custom_call_target="tpu_custom_call" | custom-call | flops 1342177280 | bytes 3293184 | tf_op jit(solution)/shard_map/back_first/pallas_call | solution.py:550
  22.9 0.1 collective-permute-done.6.arrived
  23.0 0.2 quarter_ffn.1
  23.3 0.7 %collective-permute-start.7 = (bf16[4,72,256]{2,1,0:T(8,128)(2,1)S(1)}, bf16[4,72,256]{2,1,0:T(8,128)(2,1)S(1)}, u32[]{:S(2)}, u32[]{:S(2)}) collective-permute-start(bf16[4,72,256]{2,1,0:T(8,128)(2,1)S(1)} %get-tuple-element.129), channel_id=1, source_target_pairs={{0,2},{1,3},{2,0},{3,1},{4,6},{5,7},{6,4},{7,5},{8,10},{9,11},{10,... | collective-permute-start | bytes 442376 | tf_op jit(solution)/shard_map/ppermute | solution.py:564
  24.0 1.5 %collective-permute-start.8 = (bf16[4,72,256]{2,1,0:T(8,128)(2,1)S(1)}, bf16[4,72,256]{2,1,0:T(8,128)(2,1)S(1)}, u32[]{:S(2)}, u32[]{:S(2)}) collective-permute-start(bf16[4,72,256]{2,1,0:T(8,128)(2,1)S(1)} %get-tuple-element.130), channel_id=1, source_target_pairs={{0,4},{4,0},{8,12},{12,8},{16,20},{20,16},{24,28},{28,24},{1,5},{5... | collective-permute-start | bytes 442376 | tf_op jit(solution)/shard_map/ppermute | solution.py:564
  25.5 3.7 %back_last.1 = (f32[512,256]{1,0:T(8,128)S(1)}, f32[2,200,256]{2,1,0:T(8,128)S(1)}, bf16[2,200,256]{2,1,0:T(8,128)(2,1)S(1)}) custom-call(bf16[512,768]{1,0:T(8,128)(2,1)S(1)} %get-tuple-element.109.refs_0_, bf16[512,256]{1,0:T(8,128)(2,1)S(1)} %get-tuple-element.110.refs_1_, f32[8,512]{1,0:T(8,128)S(1)} %get-tuple-element.111.refs_2_, ...), custom_call_target="tpu_custom_call" | custom-call | flops 3221225472 | bytes 5924864 | tf_op jit(solution)/shard_map/back_last/pallas_call | solution.py:550
  29.1 0.2 collective-permute-done.7.refs_0_
  29.3 0.4 collective-permute-done.8.refs_1_
  29.7 2.3 %collective-permute-start.9 = (bf16[4,72,256]{2,1,0:T(8,128)(2,1)S(1)}, bf16[4,72,256]{2,1,0:T(8,128)(2,1)S(1)}, u32[]{:S(2)}, u32[]{:S(2)}) collective-permute-start(bf16[4,72,256]{2,1,0:T(8,128)(2,1)S(1)} %get-tuple-element.133), channel_id=1, source_target_pairs={{0,6},{1,7},{2,4},{3,5},{4,2},{5,3},{6,0},{7,1},{8,14},{9,15},{10,... | collective-permute-start | bytes 442376 | tf_op jit(solution)/shard_map/ppermute | solution.py:592
  32.0 0.1 quarter_att.1
  32.1 0.7 %collective-permute-start.13 = (bf16[4,32,256]{2,1,0:T(8,128)(2,1)S(1)}, bf16[4,32,256]{2,1,0:T(8,128)(2,1)S(1)}, u32[]{:S(2)}, u32[]{:S(2)}) collective-permute-start(bf16[4,32,256]{2,1,0:T(8,128)(2,1)S(1)} %get-tuple-element.141), channel_id=1, source_target_pairs={{0,2},{1,3},{2,0},{3,1},{4,6},{5,7},{6,4},{7,5},{8,10},{9,11},{10,... | collective-permute-start | bytes 196616 | tf_op jit(solution)/shard_map/ppermute | solution.py:564
  32.8 1.3 %collective-permute-start.14 = (bf16[4,32,256]{2,1,0:T(8,128)(2,1)S(1)}, bf16[4,32,256]{2,1,0:T(8,128)(2,1)S(1)}, u32[]{:S(2)}, u32[]{:S(2)}) collective-permute-start(bf16[4,32,256]{2,1,0:T(8,128)(2,1)S(1)} %get-tuple-element.142), channel_id=1, source_target_pairs={{0,4},{4,0},{8,12},{12,8},{16,20},{20,16},{24,28},{28,24},{1,5},{5... | collective-permute-start | bytes 196616 | tf_op jit(solution)/shard_map/ppermute | solution.py:564
  34.2 1.5 %collective-permute-start.15 = (bf16[4,32,256]{2,1,0:T(8,128)(2,1)S(1)}, bf16[4,32,256]{2,1,0:T(8,128)(2,1)S(1)}, u32[]{:S(2)}, u32[]{:S(2)}) collective-permute-start(bf16[4,32,256]{2,1,0:T(8,128)(2,1)S(1)} %get-tuple-element.143), channel_id=1, source_target_pairs={{0,6},{1,7},{2,4},{3,5},{4,2},{5,3},{6,0},{7,1},{8,14},{9,15},{10,... | collective-permute-start | bytes 196616 | tf_op jit(solution)/shard_map/ppermute | solution.py:592
  35.6 1.6 %collective-permute-done.9.refs_2_ = bf16[4,72,256]{2,1,0:T(8,128)(2,1)S(1)} collective-permute-done((bf16[4,72,256]{2,1,0:T(8,128)(2,1)S(1)}, bf16[4,72,256]{2,1,0:T(8,128)(2,1)S(1)}, u32[]{:S(2)}, u32[]{:S(2)}) %collective-permute-start.9) | collective-permute-done | bytes 147488 | tf_op jit(solution)/shard_map/ppermute | solution.py:592
  37.3 0.1 halve_dp.4
  37.3 1.6 %collective-permute-start.10 = (bf16[2,72,256]{2,1,0:T(8,128)(2,1)S(1)}, bf16[2,72,256]{2,1,0:T(8,128)(2,1)S(1)}, u32[]{:S(2)}, u32[]{:S(2)}) collective-permute-start(bf16[2,72,256]{2,1,0:T(8,128)(2,1)S(1)} %get-tuple-element.135), channel_id=1, source_target_pairs={{0,8},{4,12},{8,0},{12,4},{16,24},{20,28},{24,16},{28,20},{1,9},{5... | collective-permute-start | bytes 221192 | tf_op jit(solution)/shard_map/ppermute | solution.py:564
  39.0 0.7 %collective-permute-done.15.refs_2_ = bf16[4,32,256]{2,1,0:T(8,128)(2,1)S(1)} collective-permute-done((bf16[4,32,256]{2,1,0:T(8,128)(2,1)S(1)}, bf16[4,32,256]{2,1,0:T(8,128)(2,1)S(1)}, u32[]{:S(2)}, u32[]{:S(2)}) %collective-permute-start.15) | collective-permute-done | bytes 65568 | tf_op jit(solution)/shard_map/ppermute | solution.py:592
  39.7 1.6 %collective-permute-start.16 = (bf16[2,32,256]{2,1,0:T(8,128)(2,1)S(1)}, bf16[2,32,256]{2,1,0:T(8,128)(2,1)S(1)}, u32[]{:S(2)}, u32[]{:S(2)}) collective-permute-start(bf16[2,32,256]{2,1,0:T(8,128)(2,1)S(1)} %get-tuple-element.145), channel_id=1, source_target_pairs={{0,8},{4,12},{8,0},{12,4},{16,24},{20,28},{24,16},{28,20},{1,9},{5... | collective-permute-start | bytes 98312 | tf_op jit(solution)/shard_map/ppermute | solution.py:564
  41.4 0.4 collective-permute-done.10.refs_0_
  41.8 2.7 %collective-permute-start.11 = (bf16[1,72,256]{2,1,0:T(8,128)(2,1)S(1)}, bf16[1,72,256]{2,1,0:T(8,128)(2,1)S(1)}, u32[]{:S(2)}, u32[]{:S(2)}) collective-permute-start(bf16[1,72,256]{2,1,0:T(8,128)(2,1)S(1)} %get-tuple-element.137), channel_id=1, source_target_pairs={{0,16},{4,20},{8,24},{12,28},{16,0},{20,4},{24,8},{28,12},{1,17},{... | collective-permute-start | bytes 110600 | tf_op jit(solution)/shard_map/ppermute | solution.py:564
  44.5 1.9 %collective-permute-start.17 = (bf16[1,32,256]{2,1,0:T(8,128)(2,1)S(1)}, bf16[1,32,256]{2,1,0:T(8,128)(2,1)S(1)}, u32[]{:S(2)}, u32[]{:S(2)}) collective-permute-start(bf16[1,32,256]{2,1,0:T(8,128)(2,1)S(1)} %get-tuple-element.147), channel_id=1, source_target_pairs={{0,16},{4,20},{8,24},{12,28},{16,0},{20,4},{24,8},{28,12},{1,17},{... | collective-permute-start | bytes 49160 | tf_op jit(solution)/shard_map/ppermute | solution.py:564
  46.4 0.3 collective-permute-done.11.refs_1_
  46.7 2.5 %collective-permute-done.17.refs_3_ = bf16[1,32,256]{2,1,0:T(8,128)(2,1)S(1)} collective-permute-done((bf16[1,32,256]{2,1,0:T(8,128)(2,1)S(1)}, bf16[1,32,256]{2,1,0:T(8,128)(2,1)S(1)}, u32[]{:S(2)}, u32[]{:S(2)}) %collective-permute-start.17) | collective-permute-done | bytes 16416 | tf_op jit(solution)/shard_map/ppermute | solution.py:564
  49.2 1.6 %collective-permute-start.19 = (bf16[104,256]{1,0:T(8,128)(2,1)S(1)}, bf16[104,256]{1,0:T(8,128)(2,1)S(1)}, u32[]{:S(2)}, u32[]{:S(2)}) collective-permute-start(bf16[104,256]{1,0:T(8,128)(2,1)S(1)} %piece_sum.1.refs_0_), channel_id=1, source_target_pairs={{0,4},{4,0},{8,12},{12,8},{16,20},{20,16},{24,28},{28,24},{1,5},{5... | collective-permute-start | bytes 159752 | tf_op jit(solution)/shard_map/ppermute | solution.py:564
  50.8 1.9 %collective-permute-start.18 = (bf16[104,256]{1,0:T(8,128)(2,1)S(1)}, bf16[104,256]{1,0:T(8,128)(2,1)S(1)}, u32[]{:S(2)}, u32[]{:S(2)}) collective-permute-start(bf16[104,256]{1,0:T(8,128)(2,1)S(1)} %piece_sum.1.refs_0_), channel_id=1, source_target_pairs={{0,16},{4,20},{8,24},{12,28},{16,0},{20,4},{24,8},{28,12},{1,17},{... | collective-permute-start | bytes 159752 | tf_op jit(solution)/shard_map/ppermute | solution.py:564
  52.6 1.9 %collective-permute-start.21 = (bf16[104,256]{1,0:T(8,128)(2,1)S(1)}, bf16[104,256]{1,0:T(8,128)(2,1)S(1)}, u32[]{:S(2)}, u32[]{:S(2)}) collective-permute-start(bf16[104,256]{1,0:T(8,128)(2,1)S(1)} %piece_sum.1.refs_0_), channel_id=1, source_target_pairs={{0,12},{4,8},{8,4},{12,0},{16,28},{20,24},{24,20},{28,16},{1,13},{... | collective-permute-start | bytes 159752 | tf_op jit(solution)/shard_map/ppermute | solution.py:564
  54.6 1.3 %collective-permute-done.18.refs_4_ = bf16[104,256]{1,0:T(8,128)(2,1)S(1)} collective-permute-done((bf16[104,256]{1,0:T(8,128)(2,1)S(1)}, bf16[104,256]{1,0:T(8,128)(2,1)S(1)}, u32[]{:S(2)}, u32[]{:S(2)}) %collective-permute-start.18) | collective-permute-done | bytes 53280 | tf_op jit(solution)/shard_map/ppermute | solution.py:564
  55.9 1.6 %collective-permute-start.24 = (bf16[104,256]{1,0:T(8,128)(2,1)S(1)}, bf16[104,256]{1,0:T(8,128)(2,1)S(1)}, u32[]{:S(2)}, u32[]{:S(2)}) collective-permute-start(bf16[104,256]{1,0:T(8,128)(2,1)S(1)} %collective-permute-done.18.refs_4_), channel_id=1, source_target_pairs={{0,12},{4,8},{8,4},{12,0},{16,28},{20,24},{24,20},{28,16},{1,13},{... | collective-permute-start | bytes 159752 | tf_op jit(solution)/shard_map/ppermute | solution.py:564
  57.5 0.3 collective-permute-start.23
  57.8 1.6 %collective-permute-start.22 = (bf16[104,256]{1,0:T(8,128)(2,1)S(1)}, bf16[104,256]{1,0:T(8,128)(2,1)S(1)}, u32[]{:S(2)}, u32[]{:S(2)}) collective-permute-start(bf16[104,256]{1,0:T(8,128)(2,1)S(1)} %collective-permute-done.18.refs_4_), channel_id=1, source_target_pairs={{0,4},{4,0},{8,12},{12,8},{16,20},{20,16},{24,28},{28,24},{1,5},{5... | collective-permute-start | bytes 159752 | tf_op jit(solution)/shard_map/ppermute | solution.py:564
  59.5 0.7 %convert_element_type.3 = bf16[512,256]{1,0:T(8,128)(2,1)} convert(f32[512,256]{1,0:T(8,128)S(1)} %get-tuple-element.107) | non-fusion elementwise | flops 131072 | bytes 786432 | tf_op jit(solution)/shard_map/convert_element_type | solution.py:829
  60.2 0.9 %add.3 = f32[512,256]{1,0:T(8,128)} add(f32[512,256]{1,0:T(8,128)S(1)} %get-tuple-element.108.refs_10_, f32[512,256]{1,0:T(8,128)S(1)} %get-tuple-element.126) | non-fusion elementwise | flops 131072 | bytes 1572864 | tf_op jit(solution)/shard_map/add | solution.py:829
  61.1 0.6 collective-permute-done.23.refs_6_
  61.7 0.3 collective-permute-done.22.refs_5_
  62.1 1.8 %adam.1 = (f32[64,768]{1,0:T(8,128)}, f32[64,768]{1,0:T(8,128)}, f32[64,768]{1,0:T(8,128)}, f32[64,256]{1,0:T(8,128)}, f32[64,256]{1,0:T(8,128)}, /*index=5*/f32...) custom-call(bf16[104,256]{1,0:T(8,128)(2,1)S(1)} %piece_sum.1.refs_0, ...), custom_call_target="tpu_custom_call" | custom-call | bytes 5163008 | tf_op jit(solution)/shard_map/adam/pallas_call | solution.py:550
  (61 shorter events, 0.4 us)
Async XLA Ops:
  0.7 6.7 %copy-start.6 = (bf16[512,256]{1,0:T(8,128)(2,1)S(1)}, bf16[512,256]{1,0:T(8,128)(2,1)}, u32[]{:S(2)}) copy-start(bf16[512,256]{1,0:T(8,128)(2,1)} %refs_0_.1) | copy-start | bytes 786436
  0.7 6.7 %copy-start.20 = (s32[128]{0:T(128)S(1)}, s32[128]{0:T(128)}, u32[]{:S(2)}) copy-start(s32[128]{0:T(128)} %param.22) | copy-start | bytes 1540
  0.7 6.7 %copy-start.19 = (s32[128]{0:T(128)S(1)}, s32[128]{0:T(128)}, u32[]{:S(2)}) copy-start(s32[128]{0:T(128)} %param.21) | copy-start | bytes 1540
  0.7 6.7 %copy-start.5 = (bf16[512,256]{1,0:T(8,128)(2,1)S(1)}, bf16[512,256]{1,0:T(8,128)(2,1)}, u32[]{:S(2)}) copy-start(bf16[512,256]{1,0:T(8,128)(2,1)} %seed_ref.1) | copy-start | bytes 786436
  2.4 7.5 %copy-start.13 = (bf16[208,256]{1,0:T(8,128)(2,1)S(1)}, bf16[208,256]{1,0:T(8,128)(2,1)}, u32[]{:S(2)}) copy-start(bf16[208,256]{1,0:T(8,128)(2,1)} %pack_first.1.refs_2_.refs_3_.refs_12_) | copy-start | bytes 319492
  2.4 6.2 %collective-permute-start = (bf16[208,256]{1,0:T(8,128)(2,1)}, bf16[208,256]{1,0:T(8,128)(2,1)S(1)}, u32[]{:S(2)}, u32[]{:S(2)}) collective-permute-start(bf16[208,256]{1,0:T(8,128)(2,1)} %pack_first.1.refs_2_.refs_3_.refs_12_), channel_id=1, source_target_pairs={{0,2},{1,3},{2,0},{3,1},{4,6},{5,7},{6,4},{7,5},{8,10},{9,11},{10,... | collective-permute-start | bytes 319496 | tf_op jit(solution)/shard_map/ppermute | solution.py:564
  7.2 8.7 %collective-permute-start.3 = (bf16[576,256]{1,0:T(8,128)(2,1)}, bf16[576,256]{1,0:T(8,128)(2,1)S(1)}, u32[]{:S(2)}, u32[]{:S(2)}) collective-permute-start(bf16[576,256]{1,0:T(8,128)(2,1)} %pack_second.1.refs_7_), channel_id=1, source_target_pairs={{0,2},{1,3},{2,0},{3,1},{4,6},{5,7},{6,4},{7,5},{8,10},{9,11},{10,... | collective-permute-start | bytes 884744 | tf_op jit(solution)/shard_map/ppermute | solution.py:564
  7.3 1.8 %collective-permute-start.1 = (bf16[208,256]{1,0:T(8,128)(2,1)}, bf16[208,256]{1,0:T(8,128)(2,1)S(1)}, u32[]{:S(2)}, u32[]{:S(2)}) collective-permute-start(bf16[208,256]{1,0:T(8,128)(2,1)} %pack_first.1.refs_2_.refs_3_.refs_12_), channel_id=1, source_target_pairs={{0,1},{1,0},{2,3},{3,2},{4,5},{5,4},{6,7},{7,6},{8,9},{9,8},{10,11... | collective-permute-start | bytes 319496 | tf_op jit(solution)/shard_map/ppermute | solution.py:564
  8.6 9.0 %copy-start.3 = (bf16[576,256]{1,0:T(8,128)(2,1)S(1)}, bf16[576,256]{1,0:T(8,128)(2,1)}, u32[]{:S(2)}) copy-start(bf16[576,256]{1,0:T(8,128)(2,1)} %pack_second.1.refs_7_) | copy-start | bytes 884740
  8.6 1.3 %collective-permute-start.2 = (bf16[208,256]{1,0:T(8,128)(2,1)S(1)}, bf16[208,256]{1,0:T(8,128)(2,1)S(1)}, u32[]{:S(2)}, u32[]{:S(2)}) collective-permute-start(bf16[208,256]{1,0:T(8,128)(2,1)S(1)} %collective-permute-done.refs_4_.refs_5_.refs_14_), channel_id=1, source_target_pairs={{0,1},{1,0},{2,3},{3,2},{4,5},{5,4},{6,7},{7,6},{8,9},{9,8},{10,11... | collective-permute-start | bytes 319496 | tf_op jit(solution)/shard_map/ppermute | solution.py:564
  8.7 7.3 %collective-permute-start.4 = (bf16[576,256]{1,0:T(8,128)(2,1)}, bf16[576,256]{1,0:T(8,128)(2,1)S(1)}, u32[]{:S(2)}, u32[]{:S(2)}) collective-permute-start(bf16[576,256]{1,0:T(8,128)(2,1)} %pack_second.1.refs_7_), channel_id=1, source_target_pairs={{0,1},{1,0},{2,3},{3,2},{4,5},{5,4},{6,7},{7,6},{8,9},{9,8},{10,11... | collective-permute-start | bytes 884744 | tf_op jit(solution)/shard_map/ppermute | solution.py:564
  16.0 1.6 %collective-permute-start.5 = (bf16[576,256]{1,0:T(8,128)(2,1)S(1)}, bf16[576,256]{1,0:T(8,128)(2,1)S(1)}, u32[]{:S(2)}, u32[]{:S(2)}) collective-permute-start(bf16[576,256]{1,0:T(8,128)(2,1)S(1)} %collective-permute-done.3.refs_9_), channel_id=1, source_target_pairs={{0,1},{1,0},{2,3},{3,2},{4,5},{5,4},{6,7},{7,6},{8,9},{9,8},{10,11... | collective-permute-start | bytes 884744 | tf_op jit(solution)/shard_map/ppermute | solution.py:564
  21.0 2.1 %collective-permute-start.6 = (bf16[2,576,256]{2,1,0:T(8,128)(2,1)S(1)}, bf16[2,576,256]{2,1,0:T(8,128)(2,1)S(1)}, u32[]{:S(2)}, u32[]{:S(2)}) collective-permute-start(bf16[2,576,256]{2,1,0:T(8,128)(2,1)S(1)} %get-tuple-element.114), channel_id=1, source_target_pairs={{0,1},{1,0},{2,3},{3,2},{4,5},{5,4},{6,7},{7,6},{8,9},{9,8},{10,11... | collective-permute-start | bytes 1769480 | tf_op jit(solution)/shard_map/ppermute | solution.py:564
  23.3 6.1 %collective-permute-start.7 = (bf16[4,72,256]{2,1,0:T(8,128)(2,1)S(1)}, bf16[4,72,256]{2,1,0:T(8,128)(2,1)S(1)}, u32[]{:S(2)}, u32[]{:S(2)}) collective-permute-start(bf16[4,72,256]{2,1,0:T(8,128)(2,1)S(1)} %get-tuple-element.129), channel_id=1, source_target_pairs={{0,2},{1,3},{2,0},{3,1},{4,6},{5,7},{6,4},{7,5},{8,10},{9,11},{10,... | collective-permute-start | bytes 442376 | tf_op jit(solution)/shard_map/ppermute | solution.py:564
  24.0 5.7 %collective-permute-start.8 = (bf16[4,72,256]{2,1,0:T(8,128)(2,1)S(1)}, bf16[4,72,256]{2,1,0:T(8,128)(2,1)S(1)}, u32[]{:S(2)}, u32[]{:S(2)}) collective-permute-start(bf16[4,72,256]{2,1,0:T(8,128)(2,1)S(1)} %get-tuple-element.130), channel_id=1, source_target_pairs={{0,4},{4,0},{8,12},{12,8},{16,20},{20,16},{24,28},{28,24},{1,5},{5... | collective-permute-start | bytes 442376 | tf_op jit(solution)/shard_map/ppermute | solution.py:564
  29.7 2.3 %collective-permute-start.12 = (bf16[2,200,256]{2,1,0:T(8,128)(2,1)S(1)}, bf16[2,200,256]{2,1,0:T(8,128)(2,1)S(1)}, u32[]{:S(2)}, u32[]{:S(2)}) collective-permute-start(bf16[2,200,256]{2,1,0:T(8,128)(2,1)S(1)} %get-tuple-element.139), channel_id=1, source_target_pairs={{0,1},{1,0},{2,3},{3,2},{4,5},{5,4},{6,7},{7,6},{8,9},{9,8},{10,11... | collective-permute-start | bytes 614408 | tf_op jit(solution)/shard_map/ppermute | solution.py:564
  29.7 7.5 %collective-permute-start.9 = (bf16[4,72,256]{2,1,0:T(8,128)(2,1)S(1)}, bf16[4,72,256]{2,1,0:T(8,128)(2,1)S(1)}, u32[]{:S(2)}, u32[]{:S(2)}) collective-permute-start(bf16[4,72,256]{2,1,0:T(8,128)(2,1)S(1)} %get-tuple-element.133), channel_id=1, source_target_pairs={{0,6},{1,7},{2,4},{3,5},{4,2},{5,3},{6,0},{7,1},{8,14},{9,15},{10,... | collective-permute-start | bytes 442376 | tf_op jit(solution)/shard_map/ppermute | solution.py:592
  32.1 6.9 %collective-permute-start.13 = (bf16[4,32,256]{2,1,0:T(8,128)(2,1)S(1)}, bf16[4,32,256]{2,1,0:T(8,128)(2,1)S(1)}, u32[]{:S(2)}, u32[]{:S(2)}) collective-permute-start(bf16[4,32,256]{2,1,0:T(8,128)(2,1)S(1)} %get-tuple-element.141), channel_id=1, source_target_pairs={{0,2},{1,3},{2,0},{3,1},{4,6},{5,7},{6,4},{7,5},{8,10},{9,11},{10,... | collective-permute-start | bytes 196616 | tf_op jit(solution)/shard_map/ppermute | solution.py:564
  32.8 6.2 %collective-permute-start.14 = (bf16[4,32,256]{2,1,0:T(8,128)(2,1)S(1)}, bf16[4,32,256]{2,1,0:T(8,128)(2,1)S(1)}, u32[]{:S(2)}, u32[]{:S(2)}) collective-permute-start(bf16[4,32,256]{2,1,0:T(8,128)(2,1)S(1)} %get-tuple-element.142), channel_id=1, source_target_pairs={{0,4},{4,0},{8,12},{12,8},{16,20},{20,16},{24,28},{28,24},{1,5},{5... | collective-permute-start | bytes 196616 | tf_op jit(solution)/shard_map/ppermute | solution.py:564
  34.2 5.5 %collective-permute-start.15 = (bf16[4,32,256]{2,1,0:T(8,128)(2,1)S(1)}, bf16[4,32,256]{2,1,0:T(8,128)(2,1)S(1)}, u32[]{:S(2)}, u32[]{:S(2)}) collective-permute-start(bf16[4,32,256]{2,1,0:T(8,128)(2,1)S(1)} %get-tuple-element.143), channel_id=1, source_target_pairs={{0,6},{1,7},{2,4},{3,5},{4,2},{5,3},{6,0},{7,1},{8,14},{9,15},{10,... | collective-permute-start | bytes 196616 | tf_op jit(solution)/shard_map/ppermute | solution.py:592
  37.3 4.4 %collective-permute-start.10 = (bf16[2,72,256]{2,1,0:T(8,128)(2,1)S(1)}, bf16[2,72,256]{2,1,0:T(8,128)(2,1)S(1)}, u32[]{:S(2)}, u32[]{:S(2)}) collective-permute-start(bf16[2,72,256]{2,1,0:T(8,128)(2,1)S(1)} %get-tuple-element.135), channel_id=1, source_target_pairs={{0,8},{4,12},{8,0},{12,4},{16,24},{20,28},{24,16},{28,20},{1,9},{5... | collective-permute-start | bytes 221192 | tf_op jit(solution)/shard_map/ppermute | solution.py:564
  39.7 4.7 %collective-permute-start.16 = (bf16[2,32,256]{2,1,0:T(8,128)(2,1)S(1)}, bf16[2,32,256]{2,1,0:T(8,128)(2,1)S(1)}, u32[]{:S(2)}, u32[]{:S(2)}) collective-permute-start(bf16[2,32,256]{2,1,0:T(8,128)(2,1)S(1)} %get-tuple-element.145), channel_id=1, source_target_pairs={{0,8},{4,12},{8,0},{12,4},{16,24},{20,28},{24,16},{28,20},{1,9},{5... | collective-permute-start | bytes 98312 | tf_op jit(solution)/shard_map/ppermute | solution.py:564
  41.8 20.2 %copy-start.16 = (f32[768]{0:T(1024)S(1)}, f32[768]{0:T(1024)}, u32[]{:S(2)}) copy-start(f32[768]{0:T(1024)} %refs_20_.1) | copy-start | bytes 9220
  41.8 20.2 %copy-start.17 = (f32[768]{0:T(1024)S(1)}, f32[768]{0:T(1024)}, u32[]{:S(2)}) copy-start(f32[768]{0:T(1024)} %refs_21_.1) | copy-start | bytes 9220
  41.8 20.2 %copy-start.18 = (f32[768]{0:T(1024)S(1)}, f32[768]{0:T(1024)}, u32[]{:S(2)}) copy-start(f32[768]{0:T(1024)} %refs_22_.1) | copy-start | bytes 9220
  41.8 4.9 %collective-permute-start.11 = (bf16[1,72,256]{2,1,0:T(8,128)(2,1)S(1)}, bf16[1,72,256]{2,1,0:T(8,128)(2,1)S(1)}, u32[]{:S(2)}, u32[]{:S(2)}) collective-permute-start(bf16[1,72,256]{2,1,0:T(8,128)(2,1)S(1)} %get-tuple-element.137), channel_id=1, source_target_pairs={{0,16},{4,20},{8,24},{12,28},{16,0},{20,4},{24,8},{28,12},{1,17},{... | collective-permute-start | bytes 110600 | tf_op jit(solution)/shard_map/ppermute | solution.py:564
  44.5 4.7 %collective-permute-start.17 = (bf16[1,32,256]{2,1,0:T(8,128)(2,1)S(1)}, bf16[1,32,256]{2,1,0:T(8,128)(2,1)S(1)}, u32[]{:S(2)}, u32[]{:S(2)}) collective-permute-start(bf16[1,32,256]{2,1,0:T(8,128)(2,1)S(1)} %get-tuple-element.147), channel_id=1, source_target_pairs={{0,16},{4,20},{8,24},{12,28},{16,0},{20,4},{24,8},{28,12},{1,17},{... | collective-permute-start | bytes 49160 | tf_op jit(solution)/shard_map/ppermute | solution.py:564
  49.2 5.4 %collective-permute-start.19 = (bf16[104,256]{1,0:T(8,128)(2,1)S(1)}, bf16[104,256]{1,0:T(8,128)(2,1)S(1)}, u32[]{:S(2)}, u32[]{:S(2)}) collective-permute-start(bf16[104,256]{1,0:T(8,128)(2,1)S(1)} %piece_sum.1.refs_0_), channel_id=1, source_target_pairs={{0,4},{4,0},{8,12},{12,8},{16,20},{20,16},{24,28},{28,24},{1,5},{5... | collective-permute-start | bytes 159752 | tf_op jit(solution)/shard_map/ppermute | solution.py:564
  50.8 5.1 %collective-permute-start.18 = (bf16[104,256]{1,0:T(8,128)(2,1)S(1)}, bf16[104,256]{1,0:T(8,128)(2,1)S(1)}, u32[]{:S(2)}, u32[]{:S(2)}) collective-permute-start(bf16[104,256]{1,0:T(8,128)(2,1)S(1)} %piece_sum.1.refs_0_), channel_id=1, source_target_pairs={{0,16},{4,20},{8,24},{12,28},{16,0},{20,4},{24,8},{28,12},{1,17},{... | collective-permute-start | bytes 159752 | tf_op jit(solution)/shard_map/ppermute | solution.py:564
  52.6 8.5 %collective-permute-start.21 = (bf16[104,256]{1,0:T(8,128)(2,1)S(1)}, bf16[104,256]{1,0:T(8,128)(2,1)S(1)}, u32[]{:S(2)}, u32[]{:S(2)}) collective-permute-start(bf16[104,256]{1,0:T(8,128)(2,1)S(1)} %piece_sum.1.refs_0_), channel_id=1, source_target_pairs={{0,12},{4,8},{8,4},{12,0},{16,28},{20,24},{24,20},{28,16},{1,13},{... | collective-permute-start | bytes 159752 | tf_op jit(solution)/shard_map/ppermute | solution.py:564
  54.5 6.6 %collective-permute-start.20 = (bf16[104,256]{1,0:T(8,128)(2,1)S(1)}, bf16[104,256]{1,0:T(8,128)(2,1)S(1)}, u32[]{:S(2)}, u32[]{:S(2)}) collective-permute-start(bf16[104,256]{1,0:T(8,128)(2,1)S(1)} %piece_sum.1.refs_0_), channel_id=1, source_target_pairs={{0,8},{4,12},{8,0},{12,4},{16,24},{20,28},{24,16},{28,20},{1,9},{5... | collective-permute-start | bytes 159752 | tf_op jit(solution)/shard_map/ppermute | solution.py:564
  55.9 5.2 %collective-permute-start.24 = (bf16[104,256]{1,0:T(8,128)(2,1)S(1)}, bf16[104,256]{1,0:T(8,128)(2,1)S(1)}, u32[]{:S(2)}, u32[]{:S(2)}) collective-permute-start(bf16[104,256]{1,0:T(8,128)(2,1)S(1)} %collective-permute-done.18.refs_4_), channel_id=1, source_target_pairs={{0,12},{4,8},{8,4},{12,0},{16,28},{20,24},{24,20},{28,16},{1,13},{... | collective-permute-start | bytes 159752 | tf_op jit(solution)/shard_map/ppermute | solution.py:564
  57.5 4.1 %collective-permute-start.23 = (bf16[104,256]{1,0:T(8,128)(2,1)S(1)}, bf16[104,256]{1,0:T(8,128)(2,1)S(1)}, u32[]{:S(2)}, u32[]{:S(2)}) collective-permute-start(bf16[104,256]{1,0:T(8,128)(2,1)S(1)} %collective-permute-done.18.refs_4_), channel_id=1, source_target_pairs={{0,8},{4,12},{8,0},{12,4},{16,24},{20,28},{24,16},{28,20},{1,9},{5... | collective-permute-start | bytes 159752 | tf_op jit(solution)/shard_map/ppermute | solution.py:564
  57.8 4.1 %collective-permute-start.22 = (bf16[104,256]{1,0:T(8,128)(2,1)S(1)}, bf16[104,256]{1,0:T(8,128)(2,1)S(1)}, u32[]{:S(2)}, u32[]{:S(2)}) collective-permute-start(bf16[104,256]{1,0:T(8,128)(2,1)S(1)} %collective-permute-done.18.refs_4_), channel_id=1, source_target_pairs={{0,4},{4,0},{8,12},{12,8},{16,20},{20,16},{24,28},{28,24},{1,5},{5... | collective-permute-start | bytes 159752 | tf_op jit(solution)/shard_map/ppermute | solution.py:564
  59.4 2.5 %copy-start = (f32[64,1024]{1,0:T(8,128)S(1)}, f32[64,1024]{1,0:T(8,128)}, u32[]{:S(2)}) copy-start(f32[64,1024]{1,0:T(8,128)} %refs_14_.1) | copy-start | bytes 786436
  59.4 2.6 %copy-start.1 = (f32[256,256]{1,0:T(8,128)S(1)}, f32[256,256]{1,0:T(8,128)}, u32[]{:S(2)}) copy-start(f32[256,256]{1,0:T(8,128)} %refs_17_.1) | copy-start | bytes 786436
  59.4 2.6 %copy-start.2 = (f32[64,768]{1,0:T(8,128)S(1)}, f32[64,768]{1,0:T(8,128)}, u32[]{:S(2)}) copy-start(f32[64,768]{1,0:T(8,128)} %refs_8_.1) | copy-start | bytes 589828
  59.4 2.6 %copy-start.4 = (f32[64,256]{1,0:T(8,128)S(1)}, f32[64,256]{1,0:T(8,128)}, u32[]{:S(2)}) copy-start(f32[64,256]{1,0:T(8,128)} %refs_11_.1) | copy-start | bytes 196612
  59.4 2.6 %copy-start.7 = (f32[64,1024]{1,0:T(8,128)S(1)}, f32[64,1024]{1,0:T(8,128)}, u32[]{:S(2)}) copy-start(f32[64,1024]{1,0:T(8,128)} %refs_15_.1) | copy-start | bytes 786436
  59.4 2.6 %copy-start.8 = (f32[64,1024]{1,0:T(8,128)S(1)}, f32[64,1024]{1,0:T(8,128)}, u32[]{:S(2)}) copy-start(f32[64,1024]{1,0:T(8,128)} %refs_16_.1) | copy-start | bytes 786436
  59.4 2.6 %copy-start.9 = (f32[256,256]{1,0:T(8,128)S(1)}, f32[256,256]{1,0:T(8,128)}, u32[]{:S(2)}) copy-start(f32[256,256]{1,0:T(8,128)} %refs_18_.1) | copy-start | bytes 786436
  59.5 2.6 %copy-start.10 = (f32[256,256]{1,0:T(8,128)S(1)}, f32[256,256]{1,0:T(8,128)}, u32[]{:S(2)}) copy-start(f32[256,256]{1,0:T(8,128)} %refs_19_.1) | copy-start | bytes 786436
  59.5 2.6 %copy-start.11 = (f32[64,768]{1,0:T(8,128)S(1)}, f32[64,768]{1,0:T(8,128)}, u32[]{:S(2)}) copy-start(f32[64,768]{1,0:T(8,128)} %refs_9_.1) | copy-start | bytes 589828
  59.5 2.6 %copy-start.12 = (f32[64,768]{1,0:T(8,128)S(1)}, f32[64,768]{1,0:T(8,128)}, u32[]{:S(2)}) copy-start(f32[64,768]{1,0:T(8,128)} %refs_10_.1) | copy-start | bytes 589828
  59.5 2.6 %copy-start.14 = (f32[64,256]{1,0:T(8,128)S(1)}, f32[64,256]{1,0:T(8,128)}, u32[]{:S(2)}) copy-start(f32[64,256]{1,0:T(8,128)} %refs_12_.1) | copy-start | bytes 196612
  59.5 2.6 %copy-start.15 = (f32[64,256]{1,0:T(8,128)S(1)}, f32[64,256]{1,0:T(8,128)}, u32[]{:S(2)}) copy-start(f32[64,256]{1,0:T(8,128)} %refs_13_.1) | copy-start | bytes 196612

commit v16 on v15

--- a/solution.py
+++ b/solution.py
@@ -608,6 +608,10 @@
     return [exchange(beside, "shard", 2), exchange(across, "dp", 1), corner(far)]
 
 
+def spread_far_first(beside, across, far):
+    return [corner(far), exchange(beside, "shard", 2), exchange(across, "dp", 1)]
+
+
 def near_sum(flat):
     half = flat[0].shape[0]
     bit = 1
@@ -803,7 +807,7 @@
     )
     arrived_att = exchange(send_att, "shard", 1)
     keep_att, *sends_att = quarter_call(kept_att, arrived_att, tail, group, "quarter_att")
-    arrived_att = spread(*sends_att)
+    arrived_att = spread_far_first(*sends_att)
     tails = (0, tail)
     pieces = finish_sum([[keep_ffn] + arrived_ffn, [keep_att] + arrived_att], group)
     blocks = hidden_count // width

time: 64.2 us -> 64.3 us (level)
    ppermute x23, waiting for transfers between devices: 11.9 us -> 12.9 us  [exchange(): lax.ppermute(values, axis, [(index, index ^ mask) for index in range(coun...]
where the time goes in v16:
time: 64.3 us; the launch traced here: 64.2 us
  starting transfers between devices  28.5 us (44%)
  Pallas kernels  18.2 us (28%)
  waiting for transfers between devices  14.6 us (23%)
  other arithmetic  1.59 us (2%)
  between operations  1.16 us (2%)
    ppermute x23, starting transfers between devices, exchange(): lax.ppermute(values, axis, [(index, index ^ mask) for index in range(coun...  24.8 us
    pallas_call x15, Pallas kernels, local_call(): pl.pallas_call(kernel, out_shape=outs, in_specs=[pl.BlockSpec(memory_spac...  18.2 us
    ppermute x23, waiting for transfers between devices, exchange(): lax.ppermute(values, axis, [(index, index ^ mask) for index in range(coun...  12.9 us
    ppermute x2, starting transfers between devices, corner(): return lax.ppermute(values, ('dp', 'shard'), pairs)  3.79 us
    ppermute x2, waiting for transfers between devices, corner(): return lax.ppermute(values, ('dp', 'shard'), pairs)  1.72 us
  transfers between devices with their start and end apart: 25, of which 15 were waited for; matrix products, arithmetic and copies ran while one was open for 2% of the time, Pallas kernels for 17%

profile of v16, /device:TPU:0, one launch (start us, length us, event | category | flops | bytes accessed | tf_op | source)
XLA Modules:
  0.0 64.2 jit_solution(17751701394595305438)
XLA Ops:
  0.7 1.7 %pack_first.1.refs_2_.refs_3_.refs_12_ = bf16[208,256]{1,0:T(8,128)(2,1)} custom-call(f32[64,768]{1,0:T(8,128)} %refs_8_.1, f32[768]{0:T(1024)} %refs_20_.1), custom_call_target="tpu_custom_call" | custom-call | bytes 306176 | tf_op jit(solution)/shard_map/pack_first/pallas_call | solution.py:550
  2.4 3.0 %collective-permute-start = (bf16[208,256]{1,0:T(8,128)(2,1)}, bf16[208,256]{1,0:T(8,128)(2,1)S(1)}, u32[]{:S(2)}, u32[]{:S(2)}) collective-permute-start(bf16[208,256]{1,0:T(8,128)(2,1)} %pack_first.1.refs_2_.refs_3_.refs_12_), channel_id=1, source_target_pairs={{0,2},{1,3},{2,0},{3,1},{4,6},{5,7},{6,4},{7,5},{8,10},{9,11},{10,... | collective-permute-start | bytes 319496 | tf_op jit(solution)/shard_map/ppermute | solution.py:564
  5.4 1.8 %pack_second.1.refs_7_ = bf16[576,256]{1,0:T(8,128)(2,1)} custom-call(f32[64,256]{1,0:T(8,128)} %refs_11_.1, f32[64,1024]{1,0:T(8,128)} %refs_14_.1, f32[256,256]{1,0:T(8,128)} %refs_17_.1), custom_call_target="tpu_custom_call" | custom-call | bytes 884736 | tf_op jit(solution)/shard_map/pack_second/pallas_call | solution.py:550
  7.2 0.1 collective-permute-start.3
  7.4 0.6 %prepare.1 = (f32[512,512]{1,0:T(8,128)S(1)}, f32[512,256]{1,0:T(8,128)S(1)}, f32[512,1]{1,0:T(8,128)S(1)}, bf16[512,256]{1,0:T(8,128)(2,1)S(1)}) custom-call(bf16[512,256]{1,0:T(8,128)(2,1)S(1)} %copy-done.6, bf16[512,256]{1,0:T(8,128)(2,1)S(1)} %copy-done.5, s32[1,128]{1,0:T(1,128)S(1)} %bitcast.2, s32[1,128]{1,0:T(1,128)S(1)} %bitcast.3), custom_call_target="tpu_custom_call" | custom-call | bytes 2362368 | tf_op jit(solution)/shard_map/prepare/pallas_call | solution.py:550
  8.1 0.5 collective-permute-done.refs_4_.refs_5_.refs_14_
  8.7 0.5 collective-permute-start.4
  9.1 0.8 %collective-permute-done.2.refs_5_.refs_6_.refs_15_ = bf16[208,256]{1,0:T(8,128)(2,1)S(1)} collective-permute-done((bf16[208,256]{1,0:T(8,128)(2,1)S(1)}, bf16[208,256]{1,0:T(8,128)(2,1)S(1)}, u32[]{:S(2)}, u32[]{:S(2)}) %collective-permute-start.2) | collective-permute-done | bytes 106528 | tf_op jit(solution)/shard_map/ppermute | solution.py:564
  9.9 3.0 %attend.1 = (bf16[512,768]{1,0:T(8,128)(2,1)S(1)}, bf16[512,256]{1,0:T(8,128)(2,1)S(1)}, f32[8,512]{1,0:T(8,128)S(1)}, f32[256,512]{1,0:T(8,128)S(1)}) custom-call(f32[512,256]{1,0:T(8,128)S(1)} %get-tuple-element.99.refs_0_.refs_8_, f32[512,512]{1,0:T(8,128)S(1)} %get-tuple-element.100.refs_1_.refs_3_, bf16[208,256]{1,0:T(8,128)(2,1)S(1)} %copy-done.13, ...), custom_call_target="tpu_custom_call" | custom-call | flops 1342177280 | bytes 3588096 | tf_op jit(solution)/shard_map/attend/pallas_call | solution.py:550
  12.9 3.1 %collective-permute-done.3.refs_9_ = bf16[576,256]{1,0:T(8,128)(2,1)S(1)} collective-permute-done((bf16[576,256]{1,0:T(8,128)(2,1)}, bf16[576,256]{1,0:T(8,128)(2,1)S(1)}, u32[]{:S(2)}, u32[]{:S(2)}) %collective-permute-start.3) | collective-permute-done | bytes 294944 | tf_op jit(solution)/shard_map/ppermute | solution.py:564
  16.0 1.6 %collective-permute-done.5.refs_10_ = bf16[576,256]{1,0:T(8,128)(2,1)S(1)} collective-permute-done((bf16[576,256]{1,0:T(8,128)(2,1)S(1)}, bf16[576,256]{1,0:T(8,128)(2,1)S(1)}, u32[]{:S(2)}, u32[]{:S(2)}) %collective-permute-start.5) | collective-permute-done | bytes 294944 | tf_op jit(solution)/shard_map/ppermute | solution.py:564
  17.6 3.4 %feed.1 = (f32[512,256]{1,0:T(8,128)S(1)}, f32[512,256]{1,0:T(8,128)S(1)}, bf16[512,256]{1,0:T(8,128)(2,1)S(1)}, f32[16,256]{1,0:T(8,128)S(1)}, f32[2,576,256]{2...) custom-call(bf16[512,256]{1,0:T(8,128)(2,1)S(1)} %copy-done.6, bf16[512,256]{1,0:T(8,128)(2,1)S(1)} %get-tuple-element.104.refs_1_, ...), custom_call_target="tpu_custom_call" | custom-call | flops 1811939328 | bytes 5488640 | tf_op jit(solution)/shard_map/feed/pallas_call | solution.py:550
  21.0 0.2 collective-permute-start.6
  21.2 1.7 %back_first.1 = (bf16[128,512]{1,0:T(8,128)(2,1)S(1)}, f32[512,128]{1,0:T(8,128)S(1)}, f32[512,128]{1,0:T(8,128)S(1)}) custom-call(bf16[512,768]{1,0:T(8,128)(2,1)S(1)} %get-tuple-element.109.refs_0_, bf16[512,256]{1,0:T(8,128)(2,1)S(1)} %get-tuple-element.110.refs_1_, f32[8,512]{1,0:T(8,128)S(1)} %get-tuple-element.111.refs_2_, ...), custom_call_target="tpu_custom_call" | custom-call | flops 1342177280 | bytes 3293184 | tf_op jit(solution)/shard_map/back_first/pallas_call | solution.py:550
  22.9 0.1 collective-permute-done.6.arrived
  23.0 0.2 quarter_ffn.1
  23.3 0.7 %collective-permute-start.7 = (bf16[4,72,256]{2,1,0:T(8,128)(2,1)S(1)}, bf16[4,72,256]{2,1,0:T(8,128)(2,1)S(1)}, u32[]{:S(2)}, u32[]{:S(2)}) collective-permute-start(bf16[4,72,256]{2,1,0:T(8,128)(2,1)S(1)} %get-tuple-element.129), channel_id=1, source_target_pairs={{0,2},{1,3},{2,0},{3,1},{4,6},{5,7},{6,4},{7,5},{8,10},{9,11},{10,... | collective-permute-start | bytes 442376 | tf_op jit(solution)/shard_map/ppermute | solution.py:564
  24.0 1.5 %collective-permute-start.8 = (bf16[4,72,256]{2,1,0:T(8,128)(2,1)S(1)}, bf16[4,72,256]{2,1,0:T(8,128)(2,1)S(1)}, u32[]{:S(2)}, u32[]{:S(2)}) collective-permute-start(bf16[4,72,256]{2,1,0:T(8,128)(2,1)S(1)} %get-tuple-element.130), channel_id=1, source_target_pairs={{0,4},{4,0},{8,12},{12,8},{16,20},{20,16},{24,28},{28,24},{1,5},{5... | collective-permute-start | bytes 442376 | tf_op jit(solution)/shard_map/ppermute | solution.py:564
  25.5 3.7 %back_last.1 = (f32[512,256]{1,0:T(8,128)S(1)}, f32[2,200,256]{2,1,0:T(8,128)S(1)}, bf16[2,200,256]{2,1,0:T(8,128)(2,1)S(1)}) custom-call(bf16[512,768]{1,0:T(8,128)(2,1)S(1)} %get-tuple-element.109.refs_0_, bf16[512,256]{1,0:T(8,128)(2,1)S(1)} %get-tuple-element.110.refs_1_, f32[8,512]{1,0:T(8,128)S(1)} %get-tuple-element.111.refs_2_, ...), custom_call_target="tpu_custom_call" | custom-call | flops 3221225472 | bytes 5924864 | tf_op jit(solution)/shard_map/back_last/pallas_call | solution.py:550
  29.1 0.2 collective-permute-done.7.refs_0_
  29.3 0.4 collective-permute-done.8.refs_1_
  29.7 2.3 %collective-permute-start.9 = (bf16[4,72,256]{2,1,0:T(8,128)(2,1)S(1)}, bf16[4,72,256]{2,1,0:T(8,128)(2,1)S(1)}, u32[]{:S(2)}, u32[]{:S(2)}) collective-permute-start(bf16[4,72,256]{2,1,0:T(8,128)(2,1)S(1)} %get-tuple-element.133), channel_id=1, source_target_pairs={{0,6},{1,7},{2,4},{3,5},{4,2},{5,3},{6,0},{7,1},{8,14},{9,15},{10,... | collective-permute-start | bytes 442376 | tf_op jit(solution)/shard_map/ppermute | solution.py:592
  32.0 0.1 quarter_att.1
  32.1 1.5 %collective-permute-start.13 = (bf16[4,32,256]{2,1,0:T(8,128)(2,1)S(1)}, bf16[4,32,256]{2,1,0:T(8,128)(2,1)S(1)}, u32[]{:S(2)}, u32[]{:S(2)}) collective-permute-start(bf16[4,32,256]{2,1,0:T(8,128)(2,1)S(1)} %get-tuple-element.141), channel_id=1, source_target_pairs={{0,6},{1,7},{2,4},{3,5},{4,2},{5,3},{6,0},{7,1},{8,14},{9,15},{10,... | collective-permute-start | bytes 196616 | tf_op jit(solution)/shard_map/ppermute | solution.py:592
  33.6 0.7 %collective-permute-start.14 = (bf16[4,32,256]{2,1,0:T(8,128)(2,1)S(1)}, bf16[4,32,256]{2,1,0:T(8,128)(2,1)S(1)}, u32[]{:S(2)}, u32[]{:S(2)}) collective-permute-start(bf16[4,32,256]{2,1,0:T(8,128)(2,1)S(1)} %get-tuple-element.142), channel_id=1, source_target_pairs={{0,2},{1,3},{2,0},{3,1},{4,6},{5,7},{6,4},{7,5},{8,10},{9,11},{10,... | collective-permute-start | bytes 196616 | tf_op jit(solution)/shard_map/ppermute | solution.py:564
  34.3 1.4 %collective-permute-start.15 = (bf16[4,32,256]{2,1,0:T(8,128)(2,1)S(1)}, bf16[4,32,256]{2,1,0:T(8,128)(2,1)S(1)}, u32[]{:S(2)}, u32[]{:S(2)}) collective-permute-start(bf16[4,32,256]{2,1,0:T(8,128)(2,1)S(1)} %get-tuple-element.143), channel_id=1, source_target_pairs={{0,4},{4,0},{8,12},{12,8},{16,20},{20,16},{24,28},{28,24},{1,5},{5... | collective-permute-start | bytes 196616 | tf_op jit(solution)/shard_map/ppermute | solution.py:564
  35.6 1.7 %collective-permute-done.9.refs_2_ = bf16[4,72,256]{2,1,0:T(8,128)(2,1)S(1)} collective-permute-done((bf16[4,72,256]{2,1,0:T(8,128)(2,1)S(1)}, bf16[4,72,256]{2,1,0:T(8,128)(2,1)S(1)}, u32[]{:S(2)}, u32[]{:S(2)}) %collective-permute-start.9) | collective-permute-done | bytes 147488 | tf_op jit(solution)/shard_map/ppermute | solution.py:592
  37.4 0.1 halve_dp.4
  37.4 1.6 %collective-permute-start.10 = (bf16[2,72,256]{2,1,0:T(8,128)(2,1)S(1)}, bf16[2,72,256]{2,1,0:T(8,128)(2,1)S(1)}, u32[]{:S(2)}, u32[]{:S(2)}) collective-permute-start(bf16[2,72,256]{2,1,0:T(8,128)(2,1)S(1)} %get-tuple-element.135), channel_id=1, source_target_pairs={{0,8},{4,12},{8,0},{12,4},{16,24},{20,28},{24,16},{28,20},{1,9},{5... | collective-permute-start | bytes 221192 | tf_op jit(solution)/shard_map/ppermute | solution.py:564
  39.1 0.6 collective-permute-done.14.refs_1_
  39.7 1.6 %collective-permute-start.16 = (bf16[2,32,256]{2,1,0:T(8,128)(2,1)S(1)}, bf16[2,32,256]{2,1,0:T(8,128)(2,1)S(1)}, u32[]{:S(2)}, u32[]{:S(2)}) collective-permute-start(bf16[2,32,256]{2,1,0:T(8,128)(2,1)S(1)} %get-tuple-element.145), channel_id=1, source_target_pairs={{0,8},{4,12},{8,0},{12,4},{16,24},{20,28},{24,16},{28,20},{1,9},{5... | collective-permute-start | bytes 98312 | tf_op jit(solution)/shard_map/ppermute | solution.py:564
  41.4 0.5 collective-permute-done.10.refs_0_
  41.9 2.7 %collective-permute-start.11 = (bf16[1,72,256]{2,1,0:T(8,128)(2,1)S(1)}, bf16[1,72,256]{2,1,0:T(8,128)(2,1)S(1)}, u32[]{:S(2)}, u32[]{:S(2)}) collective-permute-start(bf16[1,72,256]{2,1,0:T(8,128)(2,1)S(1)} %get-tuple-element.137), channel_id=1, source_target_pairs={{0,16},{4,20},{8,24},{12,28},{16,0},{20,4},{24,8},{28,12},{1,17},{... | collective-permute-start | bytes 110600 | tf_op jit(solution)/shard_map/ppermute | solution.py:564
  44.6 1.8 %collective-permute-start.17 = (bf16[1,32,256]{2,1,0:T(8,128)(2,1)S(1)}, bf16[1,32,256]{2,1,0:T(8,128)(2,1)S(1)}, u32[]{:S(2)}, u32[]{:S(2)}) collective-permute-start(bf16[1,32,256]{2,1,0:T(8,128)(2,1)S(1)} %get-tuple-element.147), channel_id=1, source_target_pairs={{0,16},{4,20},{8,24},{12,28},{16,0},{20,4},{24,8},{28,12},{1,17},{... | collective-permute-start | bytes 49160 | tf_op jit(solution)/shard_map/ppermute | solution.py:564
  46.4 0.4 collective-permute-done.11.refs_1_
  46.8 2.5 %collective-permute-done.17.refs_3_ = bf16[1,32,256]{2,1,0:T(8,128)(2,1)S(1)} collective-permute-done((bf16[1,32,256]{2,1,0:T(8,128)(2,1)S(1)}, bf16[1,32,256]{2,1,0:T(8,128)(2,1)S(1)}, u32[]{:S(2)}, u32[]{:S(2)}) %collective-permute-start.17) | collective-permute-done | bytes 16416 | tf_op jit(solution)/shard_map/ppermute | solution.py:564
  49.3 1.6 %collective-permute-start.19 = (bf16[104,256]{1,0:T(8,128)(2,1)S(1)}, bf16[104,256]{1,0:T(8,128)(2,1)S(1)}, u32[]{:S(2)}, u32[]{:S(2)}) collective-permute-start(bf16[104,256]{1,0:T(8,128)(2,1)S(1)} %piece_sum.1.refs_0_), channel_id=1, source_target_pairs={{0,4},{4,0},{8,12},{12,8},{16,20},{20,16},{24,28},{28,24},{1,5},{5... | collective-permute-start | bytes 159752 | tf_op jit(solution)/shard_map/ppermute | solution.py:564
  50.8 1.8 %collective-permute-start.18 = (bf16[104,256]{1,0:T(8,128)(2,1)S(1)}, bf16[104,256]{1,0:T(8,128)(2,1)S(1)}, u32[]{:S(2)}, u32[]{:S(2)}) collective-permute-start(bf16[104,256]{1,0:T(8,128)(2,1)S(1)} %piece_sum.1.refs_0_), channel_id=1, source_target_pairs={{0,16},{4,20},{8,24},{12,28},{16,0},{20,4},{24,8},{28,12},{1,17},{... | collective-permute-start | bytes 159752 | tf_op jit(solution)/shard_map/ppermute | solution.py:564
  52.6 1.9 %collective-permute-start.21 = (bf16[104,256]{1,0:T(8,128)(2,1)S(1)}, bf16[104,256]{1,0:T(8,128)(2,1)S(1)}, u32[]{:S(2)}, u32[]{:S(2)}) collective-permute-start(bf16[104,256]{1,0:T(8,128)(2,1)S(1)} %piece_sum.1.refs_0_), channel_id=1, source_target_pairs={{0,12},{4,8},{8,4},{12,0},{16,28},{20,24},{24,20},{28,16},{1,13},{... | collective-permute-start | bytes 159752 | tf_op jit(solution)/shard_map/ppermute | solution.py:564
  54.6 1.3 %collective-permute-done.18.refs_4_ = bf16[104,256]{1,0:T(8,128)(2,1)S(1)} collective-permute-done((bf16[104,256]{1,0:T(8,128)(2,1)S(1)}, bf16[104,256]{1,0:T(8,128)(2,1)S(1)}, u32[]{:S(2)}, u32[]{:S(2)}) %collective-permute-start.18) | collective-permute-done | bytes 53280 | tf_op jit(solution)/shard_map/ppermute | solution.py:564
  55.9 1.6 %collective-permute-start.24 = (bf16[104,256]{1,0:T(8,128)(2,1)S(1)}, bf16[104,256]{1,0:T(8,128)(2,1)S(1)}, u32[]{:S(2)}, u32[]{:S(2)}) collective-permute-start(bf16[104,256]{1,0:T(8,128)(2,1)S(1)} %collective-permute-done.18.refs_4_), channel_id=1, source_target_pairs={{0,12},{4,8},{8,4},{12,0},{16,28},{20,24},{24,20},{28,16},{1,13},{... | collective-permute-start | bytes 159752 | tf_op jit(solution)/shard_map/ppermute | solution.py:564
  57.5 0.4 collective-permute-start.23
  57.9 1.4 %collective-permute-start.22 = (bf16[104,256]{1,0:T(8,128)(2,1)S(1)}, bf16[104,256]{1,0:T(8,128)(2,1)S(1)}, u32[]{:S(2)}, u32[]{:S(2)}) collective-permute-start(bf16[104,256]{1,0:T(8,128)(2,1)S(1)} %collective-permute-done.18.refs_4_), channel_id=1, source_target_pairs={{0,4},{4,0},{8,12},{12,8},{16,20},{20,16},{24,28},{28,24},{1,5},{5... | collective-permute-start | bytes 159752 | tf_op jit(solution)/shard_map/ppermute | solution.py:564
  59.5 0.7 %convert_element_type.3 = bf16[512,256]{1,0:T(8,128)(2,1)} convert(f32[512,256]{1,0:T(8,128)S(1)} %get-tuple-element.107) | non-fusion elementwise | flops 131072 | bytes 786432 | tf_op jit(solution)/shard_map/convert_element_type | solution.py:833
  60.2 0.9 %add.3 = f32[512,256]{1,0:T(8,128)} add(f32[512,256]{1,0:T(8,128)S(1)} %get-tuple-element.108.refs_10_, f32[512,256]{1,0:T(8,128)S(1)} %get-tuple-element.126) | non-fusion elementwise | flops 131072 | bytes 1572864 | tf_op jit(solution)/shard_map/add | solution.py:833
  61.1 0.6 collective-permute-done.23.refs_6_
  61.6 0.4 collective-permute-done.22.refs_5_
  62.2 1.8 %adam.1 = (f32[64,768]{1,0:T(8,128)}, f32[64,768]{1,0:T(8,128)}, f32[64,768]{1,0:T(8,128)}, f32[64,256]{1,0:T(8,128)}, f32[64,256]{1,0:T(8,128)}, /*index=5*/f32...) custom-call(bf16[104,256]{1,0:T(8,128)(2,1)S(1)} %piece_sum.1.refs_0, ...), custom_call_target="tpu_custom_call" | custom-call | bytes 5163008 | tf_op jit(solution)/shard_map/adam/pallas_call | solution.py:550
  (61 shorter events, 0.4 us)
Async XLA Ops:
  0.7 6.7 %copy-start.6 = (bf16[512,256]{1,0:T(8,128)(2,1)S(1)}, bf16[512,256]{1,0:T(8,128)(2,1)}, u32[]{:S(2)}) copy-start(bf16[512,256]{1,0:T(8,128)(2,1)} %refs_0_.1) | copy-start | bytes 786436
  0.7 6.7 %copy-start.20 = (s32[128]{0:T(128)S(1)}, s32[128]{0:T(128)}, u32[]{:S(2)}) copy-start(s32[128]{0:T(128)} %param.22) | copy-start | bytes 1540
  0.7 6.7 %copy-start.19 = (s32[128]{0:T(128)S(1)}, s32[128]{0:T(128)}, u32[]{:S(2)}) copy-start(s32[128]{0:T(128)} %param.21) | copy-start | bytes 1540
  0.7 6.7 %copy-start.5 = (bf16[512,256]{1,0:T(8,128)(2,1)S(1)}, bf16[512,256]{1,0:T(8,128)(2,1)}, u32[]{:S(2)}) copy-start(bf16[512,256]{1,0:T(8,128)(2,1)} %seed_ref.1) | copy-start | bytes 786436
  2.4 7.5 %copy-start.13 = (bf16[208,256]{1,0:T(8,128)(2,1)S(1)}, bf16[208,256]{1,0:T(8,128)(2,1)}, u32[]{:S(2)}) copy-start(bf16[208,256]{1,0:T(8,128)(2,1)} %pack_first.1.refs_2_.refs_3_.refs_12_) | copy-start | bytes 319492
  2.4 6.2 %collective-permute-start = (bf16[208,256]{1,0:T(8,128)(2,1)}, bf16[208,256]{1,0:T(8,128)(2,1)S(1)}, u32[]{:S(2)}, u32[]{:S(2)}) collective-permute-start(bf16[208,256]{1,0:T(8,128)(2,1)} %pack_first.1.refs_2_.refs_3_.refs_12_), channel_id=1, source_target_pairs={{0,2},{1,3},{2,0},{3,1},{4,6},{5,7},{6,4},{7,5},{8,10},{9,11},{10,... | collective-permute-start | bytes 319496 | tf_op jit(solution)/shard_map/ppermute | solution.py:564
  7.2 8.7 %collective-permute-start.3 = (bf16[576,256]{1,0:T(8,128)(2,1)}, bf16[576,256]{1,0:T(8,128)(2,1)S(1)}, u32[]{:S(2)}, u32[]{:S(2)}) collective-permute-start(bf16[576,256]{1,0:T(8,128)(2,1)} %pack_second.1.refs_7_), channel_id=1, source_target_pairs={{0,2},{1,3},{2,0},{3,1},{4,6},{5,7},{6,4},{7,5},{8,10},{9,11},{10,... | collective-permute-start | bytes 884744 | tf_op jit(solution)/shard_map/ppermute | solution.py:564
  7.3 1.8 %collective-permute-start.1 = (bf16[208,256]{1,0:T(8,128)(2,1)}, bf16[208,256]{1,0:T(8,128)(2,1)S(1)}, u32[]{:S(2)}, u32[]{:S(2)}) collective-permute-start(bf16[208,256]{1,0:T(8,128)(2,1)} %pack_first.1.refs_2_.refs_3_.refs_12_), channel_id=1, source_target_pairs={{0,1},{1,0},{2,3},{3,2},{4,5},{5,4},{6,7},{7,6},{8,9},{9,8},{10,11... | collective-permute-start | bytes 319496 | tf_op jit(solution)/shard_map/ppermute | solution.py:564
  8.6 9.0 %copy-start.3 = (bf16[576,256]{1,0:T(8,128)(2,1)S(1)}, bf16[576,256]{1,0:T(8,128)(2,1)}, u32[]{:S(2)}) copy-start(bf16[576,256]{1,0:T(8,128)(2,1)} %pack_second.1.refs_7_) | copy-start | bytes 884740
  8.6 1.3 %collective-permute-start.2 = (bf16[208,256]{1,0:T(8,128)(2,1)S(1)}, bf16[208,256]{1,0:T(8,128)(2,1)S(1)}, u32[]{:S(2)}, u32[]{:S(2)}) collective-permute-start(bf16[208,256]{1,0:T(8,128)(2,1)S(1)} %collective-permute-done.refs_4_.refs_5_.refs_14_), channel_id=1, source_target_pairs={{0,1},{1,0},{2,3},{3,2},{4,5},{5,4},{6,7},{7,6},{8,9},{9,8},{10,11... | collective-permute-start | bytes 319496 | tf_op jit(solution)/shard_map/ppermute | solution.py:564
  8.7 7.3 %collective-permute-start.4 = (bf16[576,256]{1,0:T(8,128)(2,1)}, bf16[576,256]{1,0:T(8,128)(2,1)S(1)}, u32[]{:S(2)}, u32[]{:S(2)}) collective-permute-start(bf16[576,256]{1,0:T(8,128)(2,1)} %pack_second.1.refs_7_), channel_id=1, source_target_pairs={{0,1},{1,0},{2,3},{3,2},{4,5},{5,4},{6,7},{7,6},{8,9},{9,8},{10,11... | collective-permute-start | bytes 884744 | tf_op jit(solution)/shard_map/ppermute | solution.py:564
  16.0 1.6 %collective-permute-start.5 = (bf16[576,256]{1,0:T(8,128)(2,1)S(1)}, bf16[576,256]{1,0:T(8,128)(2,1)S(1)}, u32[]{:S(2)}, u32[]{:S(2)}) collective-permute-start(bf16[576,256]{1,0:T(8,128)(2,1)S(1)} %collective-permute-done.3.refs_9_), channel_id=1, source_target_pairs={{0,1},{1,0},{2,3},{3,2},{4,5},{5,4},{6,7},{7,6},{8,9},{9,8},{10,11... | collective-permute-start | bytes 884744 | tf_op jit(solution)/shard_map/ppermute | solution.py:564
  21.0 2.1 %collective-permute-start.6 = (bf16[2,576,256]{2,1,0:T(8,128)(2,1)S(1)}, bf16[2,576,256]{2,1,0:T(8,128)(2,1)S(1)}, u32[]{:S(2)}, u32[]{:S(2)}) collective-permute-start(bf16[2,576,256]{2,1,0:T(8,128)(2,1)S(1)} %get-tuple-element.114), channel_id=1, source_target_pairs={{0,1},{1,0},{2,3},{3,2},{4,5},{5,4},{6,7},{7,6},{8,9},{9,8},{10,11... | collective-permute-start | bytes 1769480 | tf_op jit(solution)/shard_map/ppermute | solution.py:564
  23.3 6.1 %collective-permute-start.7 = (bf16[4,72,256]{2,1,0:T(8,128)(2,1)S(1)}, bf16[4,72,256]{2,1,0:T(8,128)(2,1)S(1)}, u32[]{:S(2)}, u32[]{:S(2)}) collective-permute-start(bf16[4,72,256]{2,1,0:T(8,128)(2,1)S(1)} %get-tuple-element.129), channel_id=1, source_target_pairs={{0,2},{1,3},{2,0},{3,1},{4,6},{5,7},{6,4},{7,5},{8,10},{9,11},{10,... | collective-permute-start | bytes 442376 | tf_op jit(solution)/shard_map/ppermute | solution.py:564
  24.0 5.7 %collective-permute-start.8 = (bf16[4,72,256]{2,1,0:T(8,128)(2,1)S(1)}, bf16[4,72,256]{2,1,0:T(8,128)(2,1)S(1)}, u32[]{:S(2)}, u32[]{:S(2)}) collective-permute-start(bf16[4,72,256]{2,1,0:T(8,128)(2,1)S(1)} %get-tuple-element.130), channel_id=1, source_target_pairs={{0,4},{4,0},{8,12},{12,8},{16,20},{20,16},{24,28},{28,24},{1,5},{5... | collective-permute-start | bytes 442376 | tf_op jit(solution)/shard_map/ppermute | solution.py:564
  29.7 2.3 %collective-permute-start.12 = (bf16[2,200,256]{2,1,0:T(8,128)(2,1)S(1)}, bf16[2,200,256]{2,1,0:T(8,128)(2,1)S(1)}, u32[]{:S(2)}, u32[]{:S(2)}) collective-permute-start(bf16[2,200,256]{2,1,0:T(8,128)(2,1)S(1)} %get-tuple-element.139), channel_id=1, source_target_pairs={{0,1},{1,0},{2,3},{3,2},{4,5},{5,4},{6,7},{7,6},{8,9},{9,8},{10,11... | collective-permute-start | bytes 614408 | tf_op jit(solution)/shard_map/ppermute | solution.py:564
  29.7 7.6 %collective-permute-start.9 = (bf16[4,72,256]{2,1,0:T(8,128)(2,1)S(1)}, bf16[4,72,256]{2,1,0:T(8,128)(2,1)S(1)}, u32[]{:S(2)}, u32[]{:S(2)}) collective-permute-start(bf16[4,72,256]{2,1,0:T(8,128)(2,1)S(1)} %get-tuple-element.133), channel_id=1, source_target_pairs={{0,6},{1,7},{2,4},{3,5},{4,2},{5,3},{6,0},{7,1},{8,14},{9,15},{10,... | collective-permute-start | bytes 442376 | tf_op jit(solution)/shard_map/ppermute | solution.py:592
  32.1 7.0 %collective-permute-start.13 = (bf16[4,32,256]{2,1,0:T(8,128)(2,1)S(1)}, bf16[4,32,256]{2,1,0:T(8,128)(2,1)S(1)}, u32[]{:S(2)}, u32[]{:S(2)}) collective-permute-start(bf16[4,32,256]{2,1,0:T(8,128)(2,1)S(1)} %get-tuple-element.141), channel_id=1, source_target_pairs={{0,6},{1,7},{2,4},{3,5},{4,2},{5,3},{6,0},{7,1},{8,14},{9,15},{10,... | collective-permute-start | bytes 196616 | tf_op jit(solution)/shard_map/ppermute | solution.py:592
  33.6 6.1 %collective-permute-start.14 = (bf16[4,32,256]{2,1,0:T(8,128)(2,1)S(1)}, bf16[4,32,256]{2,1,0:T(8,128)(2,1)S(1)}, u32[]{:S(2)}, u32[]{:S(2)}) collective-permute-start(bf16[4,32,256]{2,1,0:T(8,128)(2,1)S(1)} %get-tuple-element.142), channel_id=1, source_target_pairs={{0,2},{1,3},{2,0},{3,1},{4,6},{5,7},{6,4},{7,5},{8,10},{9,11},{10,... | collective-permute-start | bytes 196616 | tf_op jit(solution)/shard_map/ppermute | solution.py:564
  34.3 5.4 %collective-permute-start.15 = (bf16[4,32,256]{2,1,0:T(8,128)(2,1)S(1)}, bf16[4,32,256]{2,1,0:T(8,128)(2,1)S(1)}, u32[]{:S(2)}, u32[]{:S(2)}) collective-permute-start(bf16[4,32,256]{2,1,0:T(8,128)(2,1)S(1)} %get-tuple-element.143), channel_id=1, source_target_pairs={{0,4},{4,0},{8,12},{12,8},{16,20},{20,16},{24,28},{28,24},{1,5},{5... | collective-permute-start | bytes 196616 | tf_op jit(solution)/shard_map/ppermute | solution.py:564
  37.4 4.4 %collective-permute-start.10 = (bf16[2,72,256]{2,1,0:T(8,128)(2,1)S(1)}, bf16[2,72,256]{2,1,0:T(8,128)(2,1)S(1)}, u32[]{:S(2)}, u32[]{:S(2)}) collective-permute-start(bf16[2,72,256]{2,1,0:T(8,128)(2,1)S(1)} %get-tuple-element.135), channel_id=1, source_target_pairs={{0,8},{4,12},{8,0},{12,4},{16,24},{20,28},{24,16},{28,20},{1,9},{5... | collective-permute-start | bytes 221192 | tf_op jit(solution)/shard_map/ppermute | solution.py:564
  39.7 4.8 %collective-permute-start.16 = (bf16[2,32,256]{2,1,0:T(8,128)(2,1)S(1)}, bf16[2,32,256]{2,1,0:T(8,128)(2,1)S(1)}, u32[]{:S(2)}, u32[]{:S(2)}) collective-permute-start(bf16[2,32,256]{2,1,0:T(8,128)(2,1)S(1)} %get-tuple-element.145), channel_id=1, source_target_pairs={{0,8},{4,12},{8,0},{12,4},{16,24},{20,28},{24,16},{28,20},{1,9},{5... | collective-permute-start | bytes 98312 | tf_op jit(solution)/shard_map/ppermute | solution.py:564
  41.9 20.2 %copy-start.16 = (f32[768]{0:T(1024)S(1)}, f32[768]{0:T(1024)}, u32[]{:S(2)}) copy-start(f32[768]{0:T(1024)} %refs_20_.1) | copy-start | bytes 9220
  41.9 20.2 %copy-start.17 = (f32[768]{0:T(1024)S(1)}, f32[768]{0:T(1024)}, u32[]{:S(2)}) copy-start(f32[768]{0:T(1024)} %refs_21_.1) | copy-start | bytes 9220
  41.9 20.2 %copy-start.18 = (f32[768]{0:T(1024)S(1)}, f32[768]{0:T(1024)}, u32[]{:S(2)}) copy-start(f32[768]{0:T(1024)} %refs_22_.1) | copy-start | bytes 9220
  41.9 4.9 %collective-permute-start.11 = (bf16[1,72,256]{2,1,0:T(8,128)(2,1)S(1)}, bf16[1,72,256]{2,1,0:T(8,128)(2,1)S(1)}, u32[]{:S(2)}, u32[]{:S(2)}) collective-permute-start(bf16[1,72,256]{2,1,0:T(8,128)(2,1)S(1)} %get-tuple-element.137), channel_id=1, source_target_pairs={{0,16},{4,20},{8,24},{12,28},{16,0},{20,4},{24,8},{28,12},{1,17},{... | collective-permute-start | bytes 110600 | tf_op jit(solution)/shard_map/ppermute | solution.py:564
  44.6 4.7 %collective-permute-start.17 = (bf16[1,32,256]{2,1,0:T(8,128)(2,1)S(1)}, bf16[1,32,256]{2,1,0:T(8,128)(2,1)S(1)}, u32[]{:S(2)}, u32[]{:S(2)}) collective-permute-start(bf16[1,32,256]{2,1,0:T(8,128)(2,1)S(1)} %get-tuple-element.147), channel_id=1, source_target_pairs={{0,16},{4,20},{8,24},{12,28},{16,0},{20,4},{24,8},{28,12},{1,17},{... | collective-permute-start | bytes 49160 | tf_op jit(solution)/shard_map/ppermute | solution.py:564
  49.3 5.3 %collective-permute-start.19 = (bf16[104,256]{1,0:T(8,128)(2,1)S(1)}, bf16[104,256]{1,0:T(8,128)(2,1)S(1)}, u32[]{:S(2)}, u32[]{:S(2)}) collective-permute-start(bf16[104,256]{1,0:T(8,128)(2,1)S(1)} %piece_sum.1.refs_0_), channel_id=1, source_target_pairs={{0,4},{4,0},{8,12},{12,8},{16,20},{20,16},{24,28},{28,24},{1,5},{5... | collective-permute-start | bytes 159752 | tf_op jit(solution)/shard_map/ppermute | solution.py:564
  50.8 5.0 %collective-permute-start.18 = (bf16[104,256]{1,0:T(8,128)(2,1)S(1)}, bf16[104,256]{1,0:T(8,128)(2,1)S(1)}, u32[]{:S(2)}, u32[]{:S(2)}) collective-permute-start(bf16[104,256]{1,0:T(8,128)(2,1)S(1)} %piece_sum.1.refs_0_), channel_id=1, source_target_pairs={{0,16},{4,20},{8,24},{12,28},{16,0},{20,4},{24,8},{28,12},{1,17},{... | collective-permute-start | bytes 159752 | tf_op jit(solution)/shard_map/ppermute | solution.py:564
  52.6 8.5 %collective-permute-start.21 = (bf16[104,256]{1,0:T(8,128)(2,1)S(1)}, bf16[104,256]{1,0:T(8,128)(2,1)S(1)}, u32[]{:S(2)}, u32[]{:S(2)}) collective-permute-start(bf16[104,256]{1,0:T(8,128)(2,1)S(1)} %piece_sum.1.refs_0_), channel_id=1, source_target_pairs={{0,12},{4,8},{8,4},{12,0},{16,28},{20,24},{24,20},{28,16},{1,13},{... | collective-permute-start | bytes 159752 | tf_op jit(solution)/shard_map/ppermute | solution.py:564
  54.5 6.5 %collective-permute-start.20 = (bf16[104,256]{1,0:T(8,128)(2,1)S(1)}, bf16[104,256]{1,0:T(8,128)(2,1)S(1)}, u32[]{:S(2)}, u32[]{:S(2)}) collective-permute-start(bf16[104,256]{1,0:T(8,128)(2,1)S(1)} %piece_sum.1.refs_0_), channel_id=1, source_target_pairs={{0,8},{4,12},{8,0},{12,4},{16,24},{20,28},{24,16},{28,20},{1,9},{5... | collective-permute-start | bytes 159752 | tf_op jit(solution)/shard_map/ppermute | solution.py:564
  55.9 5.2 %collective-permute-start.24 = (bf16[104,256]{1,0:T(8,128)(2,1)S(1)}, bf16[104,256]{1,0:T(8,128)(2,1)S(1)}, u32[]{:S(2)}, u32[]{:S(2)}) collective-permute-start(bf16[104,256]{1,0:T(8,128)(2,1)S(1)} %collective-permute-done.18.refs_4_), channel_id=1, source_target_pairs={{0,12},{4,8},{8,4},{12,0},{16,28},{20,24},{24,20},{28,16},{1,13},{... | collective-permute-start | bytes 159752 | tf_op jit(solution)/shard_map/ppermute | solution.py:564
  57.5 4.1 %collective-permute-start.23 = (bf16[104,256]{1,0:T(8,128)(2,1)S(1)}, bf16[104,256]{1,0:T(8,128)(2,1)S(1)}, u32[]{:S(2)}, u32[]{:S(2)}) collective-permute-start(bf16[104,256]{1,0:T(8,128)(2,1)S(1)} %collective-permute-done.18.refs_4_), channel_id=1, source_target_pairs={{0,8},{4,12},{8,0},{12,4},{16,24},{20,28},{24,16},{28,20},{1,9},{5... | collective-permute-start | bytes 159752 | tf_op jit(solution)/shard_map/ppermute | solution.py:564
  57.9 4.1 %collective-permute-start.22 = (bf16[104,256]{1,0:T(8,128)(2,1)S(1)}, bf16[104,256]{1,0:T(8,128)(2,1)S(1)}, u32[]{:S(2)}, u32[]{:S(2)}) collective-permute-start(bf16[104,256]{1,0:T(8,128)(2,1)S(1)} %collective-permute-done.18.refs_4_), channel_id=1, source_target_pairs={{0,4},{4,0},{8,12},{12,8},{16,20},{20,16},{24,28},{28,24},{1,5},{5... | collective-permute-start | bytes 159752 | tf_op jit(solution)/shard_map/ppermute | solution.py:564
  59.4 2.7 %copy-start = (f32[64,1024]{1,0:T(8,128)S(1)}, f32[64,1024]{1,0:T(8,128)}, u32[]{:S(2)}) copy-start(f32[64,1024]{1,0:T(8,128)} %refs_14_.1) | copy-start | bytes 786436
  59.4 2.7 %copy-start.1 = (f32[256,256]{1,0:T(8,128)S(1)}, f32[256,256]{1,0:T(8,128)}, u32[]{:S(2)}) copy-start(f32[256,256]{1,0:T(8,128)} %refs_17_.1) | copy-start | bytes 786436
  59.4 2.7 %copy-start.2 = (f32[64,768]{1,0:T(8,128)S(1)}, f32[64,768]{1,0:T(8,128)}, u32[]{:S(2)}) copy-start(f32[64,768]{1,0:T(8,128)} %refs_8_.1) | copy-start | bytes 589828
  59.4 2.7 %copy-start.4 = (f32[64,256]{1,0:T(8,128)S(1)}, f32[64,256]{1,0:T(8,128)}, u32[]{:S(2)}) copy-start(f32[64,256]{1,0:T(8,128)} %refs_11_.1) | copy-start | bytes 196612
  59.4 2.7 %copy-start.7 = (f32[64,1024]{1,0:T(8,128)S(1)}, f32[64,1024]{1,0:T(8,128)}, u32[]{:S(2)}) copy-start(f32[64,1024]{1,0:T(8,128)} %refs_15_.1) | copy-start | bytes 786436
  59.4 2.7 %copy-start.8 = (f32[64,1024]{1,0:T(8,128)S(1)}, f32[64,1024]{1,0:T(8,128)}, u32[]{:S(2)}) copy-start(f32[64,1024]{1,0:T(8,128)} %refs_16_.1) | copy-start | bytes 786436
  59.4 2.7 %copy-start.9 = (f32[256,256]{1,0:T(8,128)S(1)}, f32[256,256]{1,0:T(8,128)}, u32[]{:S(2)}) copy-start(f32[256,256]{1,0:T(8,128)} %refs_18_.1) | copy-start | bytes 786436
  59.4 2.7 %copy-start.10 = (f32[256,256]{1,0:T(8,128)S(1)}, f32[256,256]{1,0:T(8,128)}, u32[]{:S(2)}) copy-start(f32[256,256]{1,0:T(8,128)} %refs_19_.1) | copy-start | bytes 786436
  59.4 2.7 %copy-start.11 = (f32[64,768]{1,0:T(8,128)S(1)}, f32[64,768]{1,0:T(8,128)}, u32[]{:S(2)}) copy-start(f32[64,768]{1,0:T(8,128)} %refs_9_.1) | copy-start | bytes 589828
  59.4 2.7 %copy-start.12 = (f32[64,768]{1,0:T(8,128)S(1)}, f32[64,768]{1,0:T(8,128)}, u32[]{:S(2)}) copy-start(f32[64,768]{1,0:T(8,128)} %refs_10_.1) | copy-start | bytes 589828
  59.4 2.7 %copy-start.14 = (f32[64,256]{1,0:T(8,128)S(1)}, f32[64,256]{1,0:T(8,128)}, u32[]{:S(2)}) copy-start(f32[64,256]{1,0:T(8,128)} %refs_12_.1) | copy-start | bytes 196612
  59.5 2.7 %copy-start.15 = (f32[64,256]{1,0:T(8,128)S(1)}, f32[64,256]{1,0:T(8,128)}, u32[]{:S(2)}) copy-start(f32[64,256]{1,0:T(8,128)} %refs_13_.1) | copy-start | bytes 196612

commit v17 on v15

--- a/solution.py
+++ b/solution.py
@@ -14,7 +14,7 @@
 GROUP = 8
 SMALL_PAD = 16
 TILE_ROWS = 8
-CHUNK = 64
+CHUNK = 32
 
 norm_eps = 1e-05
 beta_one = 0.9

time: 64.2 us -> 64.2 us (level)
  no operation moved by 1% of the time
where the time goes in v17:
time: 64.2 us; the launch traced here: 64.1 us
  starting transfers between devices  28.7 us (45%)
  Pallas kernels  18.2 us (28%)
  waiting for transfers between devices  14.2 us (22%)
  other arithmetic  1.59 us (2%)
  between operations  1.16 us (2%)
    ppermute x23, starting transfers between devices, exchange(): lax.ppermute(values, axis, [(index, index ^ mask) for index in range(coun...  25 us
    pallas_call x15, Pallas kernels, local_call(): pl.pallas_call(kernel, out_shape=outs, in_specs=[pl.BlockSpec(memory_spac...  18.2 us
    ppermute x23, waiting for transfers between devices, exchange(): lax.ppermute(values, axis, [(index, index ^ mask) for index in range(coun...  11.9 us
    ppermute x2, starting transfers between devices, corner(): return lax.ppermute(values, ('dp', 'shard'), pairs)  3.76 us
    ppermute x2, waiting for transfers between devices, corner(): return lax.ppermute(values, ('dp', 'shard'), pairs)  2.33 us
  transfers between devices with their start and end apart: 25, of which 15 were waited for; matrix products, arithmetic and copies ran while one was open for 2% of the time, Pallas kernels for 17%

profile of v17, /device:TPU:0, one launch (start us, length us, event | category | flops | bytes accessed | tf_op | source)
XLA Modules:
  0.0 64.1 jit_solution(16476144604034628659)
XLA Ops:
  0.7 1.7 %pack_first.1.refs_2_.refs_3_.refs_12_ = bf16[208,256]{1,0:T(8,128)(2,1)} custom-call(f32[64,768]{1,0:T(8,128)} %refs_8_.1, f32[768]{0:T(1024)} %refs_20_.1), custom_call_target="tpu_custom_call" | custom-call | bytes 306176 | tf_op jit(solution)/shard_map/pack_first/pallas_call | solution.py:550
  2.4 3.0 %collective-permute-start = (bf16[208,256]{1,0:T(8,128)(2,1)}, bf16[208,256]{1,0:T(8,128)(2,1)S(1)}, u32[]{:S(2)}, u32[]{:S(2)}) collective-permute-start(bf16[208,256]{1,0:T(8,128)(2,1)} %pack_first.1.refs_2_.refs_3_.refs_12_), channel_id=1, source_target_pairs={{0,2},{1,3},{2,0},{3,1},{4,6},{5,7},{6,4},{7,5},{8,10},{9,11},{10,... | collective-permute-start | bytes 319496 | tf_op jit(solution)/shard_map/ppermute | solution.py:564
  5.4 1.8 %pack_second.1.refs_7_ = bf16[576,256]{1,0:T(8,128)(2,1)} custom-call(f32[64,256]{1,0:T(8,128)} %refs_11_.1, f32[64,1024]{1,0:T(8,128)} %refs_14_.1, f32[256,256]{1,0:T(8,128)} %refs_17_.1), custom_call_target="tpu_custom_call" | custom-call | bytes 884736 | tf_op jit(solution)/shard_map/pack_second/pallas_call | solution.py:550
  7.2 0.1 collective-permute-start.3
  7.4 0.6 %prepare.1 = (f32[512,512]{1,0:T(8,128)S(1)}, f32[512,256]{1,0:T(8,128)S(1)}, f32[512,1]{1,0:T(8,128)S(1)}, bf16[512,256]{1,0:T(8,128)(2,1)S(1)}) custom-call(bf16[512,256]{1,0:T(8,128)(2,1)S(1)} %copy-done.6, bf16[512,256]{1,0:T(8,128)(2,1)S(1)} %copy-done.5, s32[1,128]{1,0:T(1,128)S(1)} %bitcast.2, s32[1,128]{1,0:T(1,128)S(1)} %bitcast.3), custom_call_target="tpu_custom_call" | custom-call | bytes 2362368 | tf_op jit(solution)/shard_map/prepare/pallas_call | solution.py:550
  8.1 0.5 collective-permute-done.refs_4_.refs_5_.refs_14_
  8.7 0.5 collective-permute-start.4
  9.1 0.8 %collective-permute-done.2.refs_5_.refs_6_.refs_15_ = bf16[208,256]{1,0:T(8,128)(2,1)S(1)} collective-permute-done((bf16[208,256]{1,0:T(8,128)(2,1)S(1)}, bf16[208,256]{1,0:T(8,128)(2,1)S(1)}, u32[]{:S(2)}, u32[]{:S(2)}) %collective-permute-start.2) | collective-permute-done | bytes 106528 | tf_op jit(solution)/shard_map/ppermute | solution.py:564
  9.9 3.0 %attend.1 = (bf16[512,768]{1,0:T(8,128)(2,1)S(1)}, bf16[512,256]{1,0:T(8,128)(2,1)S(1)}, f32[8,512]{1,0:T(8,128)S(1)}, f32[256,512]{1,0:T(8,128)S(1)}) custom-call(f32[512,256]{1,0:T(8,128)S(1)} %get-tuple-element.99.refs_0_.refs_8_, f32[512,512]{1,0:T(8,128)S(1)} %get-tuple-element.100.refs_1_.refs_3_, bf16[208,256]{1,0:T(8,128)(2,1)S(1)} %copy-done.13, ...), custom_call_target="tpu_custom_call" | custom-call | flops 1342177280 | bytes 3588096 | tf_op jit(solution)/shard_map/attend/pallas_call | solution.py:550
  13.0 3.0 %collective-permute-done.3.refs_9_ = bf16[576,256]{1,0:T(8,128)(2,1)S(1)} collective-permute-done((bf16[576,256]{1,0:T(8,128)(2,1)}, bf16[576,256]{1,0:T(8,128)(2,1)S(1)}, u32[]{:S(2)}, u32[]{:S(2)}) %collective-permute-start.3) | collective-permute-done | bytes 294944 | tf_op jit(solution)/shard_map/ppermute | solution.py:564
  16.0 1.6 %collective-permute-done.5.refs_10_ = bf16[576,256]{1,0:T(8,128)(2,1)S(1)} collective-permute-done((bf16[576,256]{1,0:T(8,128)(2,1)S(1)}, bf16[576,256]{1,0:T(8,128)(2,1)S(1)}, u32[]{:S(2)}, u32[]{:S(2)}) %collective-permute-start.5) | collective-permute-done | bytes 294944 | tf_op jit(solution)/shard_map/ppermute | solution.py:564
  17.6 3.4 %feed.1 = (f32[512,256]{1,0:T(8,128)S(1)}, f32[512,256]{1,0:T(8,128)S(1)}, bf16[512,256]{1,0:T(8,128)(2,1)S(1)}, f32[16,256]{1,0:T(8,128)S(1)}, f32[2,576,256]{2...) custom-call(bf16[512,256]{1,0:T(8,128)(2,1)S(1)} %copy-done.6, bf16[512,256]{1,0:T(8,128)(2,1)S(1)} %get-tuple-element.104.refs_1_, ...), custom_call_target="tpu_custom_call" | custom-call | flops 1811939328 | bytes 5488640 | tf_op jit(solution)/shard_map/feed/pallas_call | solution.py:550
  21.0 0.2 collective-permute-start.6
  21.2 1.7 %back_first.1 = (bf16[128,512]{1,0:T(8,128)(2,1)S(1)}, f32[512,128]{1,0:T(8,128)S(1)}, f32[512,128]{1,0:T(8,128)S(1)}) custom-call(bf16[512,768]{1,0:T(8,128)(2,1)S(1)} %get-tuple-element.109.refs_0_, bf16[512,256]{1,0:T(8,128)(2,1)S(1)} %get-tuple-element.110.refs_1_, f32[8,512]{1,0:T(8,128)S(1)} %get-tuple-element.111.refs_2_, ...), custom_call_target="tpu_custom_call" | custom-call | flops 1342177280 | bytes 3293184 | tf_op jit(solution)/shard_map/back_first/pallas_call | solution.py:550
  22.9 0.1 collective-permute-done.6.arrived
  23.0 0.2 quarter_ffn.1
  23.3 0.7 %collective-permute-start.7 = (bf16[4,72,256]{2,1,0:T(8,128)(2,1)S(1)}, bf16[4,72,256]{2,1,0:T(8,128)(2,1)S(1)}, u32[]{:S(2)}, u32[]{:S(2)}) collective-permute-start(bf16[4,72,256]{2,1,0:T(8,128)(2,1)S(1)} %get-tuple-element.129), channel_id=1, source_target_pairs={{0,2},{1,3},{2,0},{3,1},{4,6},{5,7},{6,4},{7,5},{8,10},{9,11},{10,... | collective-permute-start | bytes 442376 | tf_op jit(solution)/shard_map/ppermute | solution.py:564
  24.0 1.5 %collective-permute-start.8 = (bf16[4,72,256]{2,1,0:T(8,128)(2,1)S(1)}, bf16[4,72,256]{2,1,0:T(8,128)(2,1)S(1)}, u32[]{:S(2)}, u32[]{:S(2)}) collective-permute-start(bf16[4,72,256]{2,1,0:T(8,128)(2,1)S(1)} %get-tuple-element.130), channel_id=1, source_target_pairs={{0,4},{4,0},{8,12},{12,8},{16,20},{20,16},{24,28},{28,24},{1,5},{5... | collective-permute-start | bytes 442376 | tf_op jit(solution)/shard_map/ppermute | solution.py:564
  25.5 3.7 %back_last.1 = (f32[512,256]{1,0:T(8,128)S(1)}, f32[2,200,256]{2,1,0:T(8,128)S(1)}, bf16[2,200,256]{2,1,0:T(8,128)(2,1)S(1)}) custom-call(bf16[512,768]{1,0:T(8,128)(2,1)S(1)} %get-tuple-element.109.refs_0_, bf16[512,256]{1,0:T(8,128)(2,1)S(1)} %get-tuple-element.110.refs_1_, f32[8,512]{1,0:T(8,128)S(1)} %get-tuple-element.111.refs_2_, ...), custom_call_target="tpu_custom_call" | custom-call | flops 3221225472 | bytes 5924864 | tf_op jit(solution)/shard_map/back_last/pallas_call | solution.py:550
  29.2 0.2 collective-permute-done.7.refs_0_
  29.3 0.4 collective-permute-done.8.refs_1_
  29.7 2.3 %collective-permute-start.9 = (bf16[4,72,256]{2,1,0:T(8,128)(2,1)S(1)}, bf16[4,72,256]{2,1,0:T(8,128)(2,1)S(1)}, u32[]{:S(2)}, u32[]{:S(2)}) collective-permute-start(bf16[4,72,256]{2,1,0:T(8,128)(2,1)S(1)} %get-tuple-element.133), channel_id=1, source_target_pairs={{0,6},{1,7},{2,4},{3,5},{4,2},{5,3},{6,0},{7,1},{8,14},{9,15},{10,... | collective-permute-start | bytes 442376 | tf_op jit(solution)/shard_map/ppermute | solution.py:592
  32.0 0.1 quarter_att.1
  32.1 0.7 %collective-permute-start.13 = (bf16[4,32,256]{2,1,0:T(8,128)(2,1)S(1)}, bf16[4,32,256]{2,1,0:T(8,128)(2,1)S(1)}, u32[]{:S(2)}, u32[]{:S(2)}) collective-permute-start(bf16[4,32,256]{2,1,0:T(8,128)(2,1)S(1)} %get-tuple-element.141), channel_id=1, source_target_pairs={{0,2},{1,3},{2,0},{3,1},{4,6},{5,7},{6,4},{7,5},{8,10},{9,11},{10,... | collective-permute-start | bytes 196616 | tf_op jit(solution)/shard_map/ppermute | solution.py:564
  32.8 1.3 %collective-permute-start.14 = (bf16[4,32,256]{2,1,0:T(8,128)(2,1)S(1)}, bf16[4,32,256]{2,1,0:T(8,128)(2,1)S(1)}, u32[]{:S(2)}, u32[]{:S(2)}) collective-permute-start(bf16[4,32,256]{2,1,0:T(8,128)(2,1)S(1)} %get-tuple-element.142), channel_id=1, source_target_pairs={{0,4},{4,0},{8,12},{12,8},{16,20},{20,16},{24,28},{28,24},{1,5},{5... | collective-permute-start | bytes 196616 | tf_op jit(solution)/shard_map/ppermute | solution.py:564
  34.2 1.5 %collective-permute-start.15 = (bf16[4,32,256]{2,1,0:T(8,128)(2,1)S(1)}, bf16[4,32,256]{2,1,0:T(8,128)(2,1)S(1)}, u32[]{:S(2)}, u32[]{:S(2)}) collective-permute-start(bf16[4,32,256]{2,1,0:T(8,128)(2,1)S(1)} %get-tuple-element.143), channel_id=1, source_target_pairs={{0,6},{1,7},{2,4},{3,5},{4,2},{5,3},{6,0},{7,1},{8,14},{9,15},{10,... | collective-permute-start | bytes 196616 | tf_op jit(solution)/shard_map/ppermute | solution.py:592
  35.6 1.6 %collective-permute-done.9.refs_2_ = bf16[4,72,256]{2,1,0:T(8,128)(2,1)S(1)} collective-permute-done((bf16[4,72,256]{2,1,0:T(8,128)(2,1)S(1)}, bf16[4,72,256]{2,1,0:T(8,128)(2,1)S(1)}, u32[]{:S(2)}, u32[]{:S(2)}) %collective-permute-start.9) | collective-permute-done | bytes 147488 | tf_op jit(solution)/shard_map/ppermute | solution.py:592
  37.3 0.1 halve_dp.4
  37.3 1.6 %collective-permute-start.10 = (bf16[2,72,256]{2,1,0:T(8,128)(2,1)S(1)}, bf16[2,72,256]{2,1,0:T(8,128)(2,1)S(1)}, u32[]{:S(2)}, u32[]{:S(2)}) collective-permute-start(bf16[2,72,256]{2,1,0:T(8,128)(2,1)S(1)} %get-tuple-element.135), channel_id=1, source_target_pairs={{0,8},{4,12},{8,0},{12,4},{16,24},{20,28},{24,16},{28,20},{1,9},{5... | collective-permute-start | bytes 221192 | tf_op jit(solution)/shard_map/ppermute | solution.py:564
  39.0 0.7 %collective-permute-done.15.refs_2_ = bf16[4,32,256]{2,1,0:T(8,128)(2,1)S(1)} collective-permute-done((bf16[4,32,256]{2,1,0:T(8,128)(2,1)S(1)}, bf16[4,32,256]{2,1,0:T(8,128)(2,1)S(1)}, u32[]{:S(2)}, u32[]{:S(2)}) %collective-permute-start.15) | collective-permute-done | bytes 65568 | tf_op jit(solution)/shard_map/ppermute | solution.py:592
  39.7 1.6 %collective-permute-start.16 = (bf16[2,32,256]{2,1,0:T(8,128)(2,1)S(1)}, bf16[2,32,256]{2,1,0:T(8,128)(2,1)S(1)}, u32[]{:S(2)}, u32[]{:S(2)}) collective-permute-start(bf16[2,32,256]{2,1,0:T(8,128)(2,1)S(1)} %get-tuple-element.145), channel_id=1, source_target_pairs={{0,8},{4,12},{8,0},{12,4},{16,24},{20,28},{24,16},{28,20},{1,9},{5... | collective-permute-start | bytes 98312 | tf_op jit(solution)/shard_map/ppermute | solution.py:564
  41.4 0.4 collective-permute-done.10.refs_0_
  41.8 2.7 %collective-permute-start.11 = (bf16[1,72,256]{2,1,0:T(8,128)(2,1)S(1)}, bf16[1,72,256]{2,1,0:T(8,128)(2,1)S(1)}, u32[]{:S(2)}, u32[]{:S(2)}) collective-permute-start(bf16[1,72,256]{2,1,0:T(8,128)(2,1)S(1)} %get-tuple-element.137), channel_id=1, source_target_pairs={{0,16},{4,20},{8,24},{12,28},{16,0},{20,4},{24,8},{28,12},{1,17},{... | collective-permute-start | bytes 110600 | tf_op jit(solution)/shard_map/ppermute | solution.py:564
  44.5 1.9 %collective-permute-start.17 = (bf16[1,32,256]{2,1,0:T(8,128)(2,1)S(1)}, bf16[1,32,256]{2,1,0:T(8,128)(2,1)S(1)}, u32[]{:S(2)}, u32[]{:S(2)}) collective-permute-start(bf16[1,32,256]{2,1,0:T(8,128)(2,1)S(1)} %get-tuple-element.147), channel_id=1, source_target_pairs={{0,16},{4,20},{8,24},{12,28},{16,0},{20,4},{24,8},{28,12},{1,17},{... | collective-permute-start | bytes 49160 | tf_op jit(solution)/shard_map/ppermute | solution.py:564
  46.4 0.3 collective-permute-done.11.refs_1_
  46.7 2.5 %collective-permute-done.17.refs_3_ = bf16[1,32,256]{2,1,0:T(8,128)(2,1)S(1)} collective-permute-done((bf16[1,32,256]{2,1,0:T(8,128)(2,1)S(1)}, bf16[1,32,256]{2,1,0:T(8,128)(2,1)S(1)}, u32[]{:S(2)}, u32[]{:S(2)}) %collective-permute-start.17) | collective-permute-done | bytes 16416 | tf_op jit(solution)/shard_map/ppermute | solution.py:564
  49.2 1.6 %collective-permute-start.19 = (bf16[104,256]{1,0:T(8,128)(2,1)S(1)}, bf16[104,256]{1,0:T(8,128)(2,1)S(1)}, u32[]{:S(2)}, u32[]{:S(2)}) collective-permute-start(bf16[104,256]{1,0:T(8,128)(2,1)S(1)} %piece_sum.1.refs_0_), channel_id=1, source_target_pairs={{0,4},{4,0},{8,12},{12,8},{16,20},{20,16},{24,28},{28,24},{1,5},{5... | collective-permute-start | bytes 159752 | tf_op jit(solution)/shard_map/ppermute | solution.py:564
  50.8 1.9 %collective-permute-start.18 = (bf16[104,256]{1,0:T(8,128)(2,1)S(1)}, bf16[104,256]{1,0:T(8,128)(2,1)S(1)}, u32[]{:S(2)}, u32[]{:S(2)}) collective-permute-start(bf16[104,256]{1,0:T(8,128)(2,1)S(1)} %piece_sum.1.refs_0_), channel_id=1, source_target_pairs={{0,16},{4,20},{8,24},{12,28},{16,0},{20,4},{24,8},{28,12},{1,17},{... | collective-permute-start | bytes 159752 | tf_op jit(solution)/shard_map/ppermute | solution.py:564
  52.6 1.9 %collective-permute-start.21 = (bf16[104,256]{1,0:T(8,128)(2,1)S(1)}, bf16[104,256]{1,0:T(8,128)(2,1)S(1)}, u32[]{:S(2)}, u32[]{:S(2)}) collective-permute-start(bf16[104,256]{1,0:T(8,128)(2,1)S(1)} %piece_sum.1.refs_0_), channel_id=1, source_target_pairs={{0,12},{4,8},{8,4},{12,0},{16,28},{20,24},{24,20},{28,16},{1,13},{... | collective-permute-start | bytes 159752 | tf_op jit(solution)/shard_map/ppermute | solution.py:564
  54.6 1.3 %collective-permute-done.18.refs_4_ = bf16[104,256]{1,0:T(8,128)(2,1)S(1)} collective-permute-done((bf16[104,256]{1,0:T(8,128)(2,1)S(1)}, bf16[104,256]{1,0:T(8,128)(2,1)S(1)}, u32[]{:S(2)}, u32[]{:S(2)}) %collective-permute-start.18) | collective-permute-done | bytes 53280 | tf_op jit(solution)/shard_map/ppermute | solution.py:564
  55.9 1.6 %collective-permute-start.24 = (bf16[104,256]{1,0:T(8,128)(2,1)S(1)}, bf16[104,256]{1,0:T(8,128)(2,1)S(1)}, u32[]{:S(2)}, u32[]{:S(2)}) collective-permute-start(bf16[104,256]{1,0:T(8,128)(2,1)S(1)} %collective-permute-done.18.refs_4_), channel_id=1, source_target_pairs={{0,12},{4,8},{8,4},{12,0},{16,28},{20,24},{24,20},{28,16},{1,13},{... | collective-permute-start | bytes 159752 | tf_op jit(solution)/shard_map/ppermute | solution.py:564
  57.5 0.3 collective-permute-start.23
  57.8 1.6 %collective-permute-start.22 = (bf16[104,256]{1,0:T(8,128)(2,1)S(1)}, bf16[104,256]{1,0:T(8,128)(2,1)S(1)}, u32[]{:S(2)}, u32[]{:S(2)}) collective-permute-start(bf16[104,256]{1,0:T(8,128)(2,1)S(1)} %collective-permute-done.18.refs_4_), channel_id=1, source_target_pairs={{0,4},{4,0},{8,12},{12,8},{16,20},{20,16},{24,28},{28,24},{1,5},{5... | collective-permute-start | bytes 159752 | tf_op jit(solution)/shard_map/ppermute | solution.py:564
  59.5 0.7 %convert_element_type.3 = bf16[512,256]{1,0:T(8,128)(2,1)} convert(f32[512,256]{1,0:T(8,128)S(1)} %get-tuple-element.107) | non-fusion elementwise | flops 131072 | bytes 786432 | tf_op jit(solution)/shard_map/convert_element_type | solution.py:829
  60.2 0.9 %add.3 = f32[512,256]{1,0:T(8,128)} add(f32[512,256]{1,0:T(8,128)S(1)} %get-tuple-element.108.refs_10_, f32[512,256]{1,0:T(8,128)S(1)} %get-tuple-element.126) | non-fusion elementwise | flops 131072 | bytes 1572864 | tf_op jit(solution)/shard_map/add | solution.py:829
  61.1 0.6 collective-permute-done.23.refs_6_
  61.7 0.3 collective-permute-done.22.refs_5_
  62.1 1.8 %adam.1 = (f32[64,768]{1,0:T(8,128)}, f32[64,768]{1,0:T(8,128)}, f32[64,768]{1,0:T(8,128)}, f32[64,256]{1,0:T(8,128)}, f32[64,256]{1,0:T(8,128)}, /*index=5*/f32...) custom-call(bf16[104,256]{1,0:T(8,128)(2,1)S(1)} %piece_sum.1.refs_0, ...), custom_call_target="tpu_custom_call" | custom-call | bytes 5163008 | tf_op jit(solution)/shard_map/adam/pallas_call | solution.py:550
  (61 shorter events, 0.4 us)
Async XLA Ops:
  0.7 6.7 %copy-start.6 = (bf16[512,256]{1,0:T(8,128)(2,1)S(1)}, bf16[512,256]{1,0:T(8,128)(2,1)}, u32[]{:S(2)}) copy-start(bf16[512,256]{1,0:T(8,128)(2,1)} %refs_0_.1) | copy-start | bytes 786436
  0.7 6.7 %copy-start.20 = (s32[128]{0:T(128)S(1)}, s32[128]{0:T(128)}, u32[]{:S(2)}) copy-start(s32[128]{0:T(128)} %param.22) | copy-start | bytes 1540
  0.7 6.7 %copy-start.19 = (s32[128]{0:T(128)S(1)}, s32[128]{0:T(128)}, u32[]{:S(2)}) copy-start(s32[128]{0:T(128)} %param.21) | copy-start | bytes 1540
  0.7 6.7 %copy-start.5 = (bf16[512,256]{1,0:T(8,128)(2,1)S(1)}, bf16[512,256]{1,0:T(8,128)(2,1)}, u32[]{:S(2)}) copy-start(bf16[512,256]{1,0:T(8,128)(2,1)} %seed_ref.1) | copy-start | bytes 786436
  2.4 7.5 %copy-start.13 = (bf16[208,256]{1,0:T(8,128)(2,1)S(1)}, bf16[208,256]{1,0:T(8,128)(2,1)}, u32[]{:S(2)}) copy-start(bf16[208,256]{1,0:T(8,128)(2,1)} %pack_first.1.refs_2_.refs_3_.refs_12_) | copy-start | bytes 319492
  2.4 6.2 %collective-permute-start = (bf16[208,256]{1,0:T(8,128)(2,1)}, bf16[208,256]{1,0:T(8,128)(2,1)S(1)}, u32[]{:S(2)}, u32[]{:S(2)}) collective-permute-start(bf16[208,256]{1,0:T(8,128)(2,1)} %pack_first.1.refs_2_.refs_3_.refs_12_), channel_id=1, source_target_pairs={{0,2},{1,3},{2,0},{3,1},{4,6},{5,7},{6,4},{7,5},{8,10},{9,11},{10,... | collective-permute-start | bytes 319496 | tf_op jit(solution)/shard_map/ppermute | solution.py:564
  7.2 8.7 %collective-permute-start.3 = (bf16[576,256]{1,0:T(8,128)(2,1)}, bf16[576,256]{1,0:T(8,128)(2,1)S(1)}, u32[]{:S(2)}, u32[]{:S(2)}) collective-permute-start(bf16[576,256]{1,0:T(8,128)(2,1)} %pack_second.1.refs_7_), channel_id=1, source_target_pairs={{0,2},{1,3},{2,0},{3,1},{4,6},{5,7},{6,4},{7,5},{8,10},{9,11},{10,... | collective-permute-start | bytes 884744 | tf_op jit(solution)/shard_map/ppermute | solution.py:564
  7.3 1.8 %collective-permute-start.1 = (bf16[208,256]{1,0:T(8,128)(2,1)}, bf16[208,256]{1,0:T(8,128)(2,1)S(1)}, u32[]{:S(2)}, u32[]{:S(2)}) collective-permute-start(bf16[208,256]{1,0:T(8,128)(2,1)} %pack_first.1.refs_2_.refs_3_.refs_12_), channel_id=1, source_target_pairs={{0,1},{1,0},{2,3},{3,2},{4,5},{5,4},{6,7},{7,6},{8,9},{9,8},{10,11... | collective-permute-start | bytes 319496 | tf_op jit(solution)/shard_map/ppermute | solution.py:564
  8.6 9.0 %copy-start.3 = (bf16[576,256]{1,0:T(8,128)(2,1)S(1)}, bf16[576,256]{1,0:T(8,128)(2,1)}, u32[]{:S(2)}) copy-start(bf16[576,256]{1,0:T(8,128)(2,1)} %pack_second.1.refs_7_) | copy-start | bytes 884740
  8.6 1.3 %collective-permute-start.2 = (bf16[208,256]{1,0:T(8,128)(2,1)S(1)}, bf16[208,256]{1,0:T(8,128)(2,1)S(1)}, u32[]{:S(2)}, u32[]{:S(2)}) collective-permute-start(bf16[208,256]{1,0:T(8,128)(2,1)S(1)} %collective-permute-done.refs_4_.refs_5_.refs_14_), channel_id=1, source_target_pairs={{0,1},{1,0},{2,3},{3,2},{4,5},{5,4},{6,7},{7,6},{8,9},{9,8},{10,11... | collective-permute-start | bytes 319496 | tf_op jit(solution)/shard_map/ppermute | solution.py:564
  8.7 7.3 %collective-permute-start.4 = (bf16[576,256]{1,0:T(8,128)(2,1)}, bf16[576,256]{1,0:T(8,128)(2,1)S(1)}, u32[]{:S(2)}, u32[]{:S(2)}) collective-permute-start(bf16[576,256]{1,0:T(8,128)(2,1)} %pack_second.1.refs_7_), channel_id=1, source_target_pairs={{0,1},{1,0},{2,3},{3,2},{4,5},{5,4},{6,7},{7,6},{8,9},{9,8},{10,11... | collective-permute-start | bytes 884744 | tf_op jit(solution)/shard_map/ppermute | solution.py:564
  16.0 1.6 %collective-permute-start.5 = (bf16[576,256]{1,0:T(8,128)(2,1)S(1)}, bf16[576,256]{1,0:T(8,128)(2,1)S(1)}, u32[]{:S(2)}, u32[]{:S(2)}) collective-permute-start(bf16[576,256]{1,0:T(8,128)(2,1)S(1)} %collective-permute-done.3.refs_9_), channel_id=1, source_target_pairs={{0,1},{1,0},{2,3},{3,2},{4,5},{5,4},{6,7},{7,6},{8,9},{9,8},{10,11... | collective-permute-start | bytes 884744 | tf_op jit(solution)/shard_map/ppermute | solution.py:564
  21.0 2.1 %collective-permute-start.6 = (bf16[2,576,256]{2,1,0:T(8,128)(2,1)S(1)}, bf16[2,576,256]{2,1,0:T(8,128)(2,1)S(1)}, u32[]{:S(2)}, u32[]{:S(2)}) collective-permute-start(bf16[2,576,256]{2,1,0:T(8,128)(2,1)S(1)} %get-tuple-element.114), channel_id=1, source_target_pairs={{0,1},{1,0},{2,3},{3,2},{4,5},{5,4},{6,7},{7,6},{8,9},{9,8},{10,11... | collective-permute-start | bytes 1769480 | tf_op jit(solution)/shard_map/ppermute | solution.py:564
  23.3 6.1 %collective-permute-start.7 = (bf16[4,72,256]{2,1,0:T(8,128)(2,1)S(1)}, bf16[4,72,256]{2,1,0:T(8,128)(2,1)S(1)}, u32[]{:S(2)}, u32[]{:S(2)}) collective-permute-start(bf16[4,72,256]{2,1,0:T(8,128)(2,1)S(1)} %get-tuple-element.129), channel_id=1, source_target_pairs={{0,2},{1,3},{2,0},{3,1},{4,6},{5,7},{6,4},{7,5},{8,10},{9,11},{10,... | collective-permute-start | bytes 442376 | tf_op jit(solution)/shard_map/ppermute | solution.py:564
  24.0 5.7 %collective-permute-start.8 = (bf16[4,72,256]{2,1,0:T(8,128)(2,1)S(1)}, bf16[4,72,256]{2,1,0:T(8,128)(2,1)S(1)}, u32[]{:S(2)}, u32[]{:S(2)}) collective-permute-start(bf16[4,72,256]{2,1,0:T(8,128)(2,1)S(1)} %get-tuple-element.130), channel_id=1, source_target_pairs={{0,4},{4,0},{8,12},{12,8},{16,20},{20,16},{24,28},{28,24},{1,5},{5... | collective-permute-start | bytes 442376 | tf_op jit(solution)/shard_map/ppermute | solution.py:564
  29.7 2.3 %collective-permute-start.12 = (bf16[2,200,256]{2,1,0:T(8,128)(2,1)S(1)}, bf16[2,200,256]{2,1,0:T(8,128)(2,1)S(1)}, u32[]{:S(2)}, u32[]{:S(2)}) collective-permute-start(bf16[2,200,256]{2,1,0:T(8,128)(2,1)S(1)} %get-tuple-element.139), channel_id=1, source_target_pairs={{0,1},{1,0},{2,3},{3,2},{4,5},{5,4},{6,7},{7,6},{8,9},{9,8},{10,11... | collective-permute-start | bytes 614408 | tf_op jit(solution)/shard_map/ppermute | solution.py:564
  29.7 7.5 %collective-permute-start.9 = (bf16[4,72,256]{2,1,0:T(8,128)(2,1)S(1)}, bf16[4,72,256]{2,1,0:T(8,128)(2,1)S(1)}, u32[]{:S(2)}, u32[]{:S(2)}) collective-permute-start(bf16[4,72,256]{2,1,0:T(8,128)(2,1)S(1)} %get-tuple-element.133), channel_id=1, source_target_pairs={{0,6},{1,7},{2,4},{3,5},{4,2},{5,3},{6,0},{7,1},{8,14},{9,15},{10,... | collective-permute-start | bytes 442376 | tf_op jit(solution)/shard_map/ppermute | solution.py:592
  32.1 6.9 %collective-permute-start.13 = (bf16[4,32,256]{2,1,0:T(8,128)(2,1)S(1)}, bf16[4,32,256]{2,1,0:T(8,128)(2,1)S(1)}, u32[]{:S(2)}, u32[]{:S(2)}) collective-permute-start(bf16[4,32,256]{2,1,0:T(8,128)(2,1)S(1)} %get-tuple-element.141), channel_id=1, source_target_pairs={{0,2},{1,3},{2,0},{3,1},{4,6},{5,7},{6,4},{7,5},{8,10},{9,11},{10,... | collective-permute-start | bytes 196616 | tf_op jit(solution)/shard_map/ppermute | solution.py:564
  32.8 6.2 %collective-permute-start.14 = (bf16[4,32,256]{2,1,0:T(8,128)(2,1)S(1)}, bf16[4,32,256]{2,1,0:T(8,128)(2,1)S(1)}, u32[]{:S(2)}, u32[]{:S(2)}) collective-permute-start(bf16[4,32,256]{2,1,0:T(8,128)(2,1)S(1)} %get-tuple-element.142), channel_id=1, source_target_pairs={{0,4},{4,0},{8,12},{12,8},{16,20},{20,16},{24,28},{28,24},{1,5},{5... | collective-permute-start | bytes 196616 | tf_op jit(solution)/shard_map/ppermute | solution.py:564
  34.2 5.5 %collective-permute-start.15 = (bf16[4,32,256]{2,1,0:T(8,128)(2,1)S(1)}, bf16[4,32,256]{2,1,0:T(8,128)(2,1)S(1)}, u32[]{:S(2)}, u32[]{:S(2)}) collective-permute-start(bf16[4,32,256]{2,1,0:T(8,128)(2,1)S(1)} %get-tuple-element.143), channel_id=1, source_target_pairs={{0,6},{1,7},{2,4},{3,5},{4,2},{5,3},{6,0},{7,1},{8,14},{9,15},{10,... | collective-permute-start | bytes 196616 | tf_op jit(solution)/shard_map/ppermute | solution.py:592
  37.3 4.4 %collective-permute-start.10 = (bf16[2,72,256]{2,1,0:T(8,128)(2,1)S(1)}, bf16[2,72,256]{2,1,0:T(8,128)(2,1)S(1)}, u32[]{:S(2)}, u32[]{:S(2)}) collective-permute-start(bf16[2,72,256]{2,1,0:T(8,128)(2,1)S(1)} %get-tuple-element.135), channel_id=1, source_target_pairs={{0,8},{4,12},{8,0},{12,4},{16,24},{20,28},{24,16},{28,20},{1,9},{5... | collective-permute-start | bytes 221192 | tf_op jit(solution)/shard_map/ppermute | solution.py:564
  39.7 4.7 %collective-permute-start.16 = (bf16[2,32,256]{2,1,0:T(8,128)(2,1)S(1)}, bf16[2,32,256]{2,1,0:T(8,128)(2,1)S(1)}, u32[]{:S(2)}, u32[]{:S(2)}) collective-permute-start(bf16[2,32,256]{2,1,0:T(8,128)(2,1)S(1)} %get-tuple-element.145), channel_id=1, source_target_pairs={{0,8},{4,12},{8,0},{12,4},{16,24},{20,28},{24,16},{28,20},{1,9},{5... | collective-permute-start | bytes 98312 | tf_op jit(solution)/shard_map/ppermute | solution.py:564
  41.8 20.2 %copy-start.16 = (f32[768]{0:T(1024)S(1)}, f32[768]{0:T(1024)}, u32[]{:S(2)}) copy-start(f32[768]{0:T(1024)} %refs_20_.1) | copy-start | bytes 9220
  41.8 20.2 %copy-start.17 = (f32[768]{0:T(1024)S(1)}, f32[768]{0:T(1024)}, u32[]{:S(2)}) copy-start(f32[768]{0:T(1024)} %refs_21_.1) | copy-start | bytes 9220
  41.8 20.2 %copy-start.18 = (f32[768]{0:T(1024)S(1)}, f32[768]{0:T(1024)}, u32[]{:S(2)}) copy-start(f32[768]{0:T(1024)} %refs_22_.1) | copy-start | bytes 9220
  41.8 4.9 %collective-permute-start.11 = (bf16[1,72,256]{2,1,0:T(8,128)(2,1)S(1)}, bf16[1,72,256]{2,1,0:T(8,128)(2,1)S(1)}, u32[]{:S(2)}, u32[]{:S(2)}) collective-permute-start(bf16[1,72,256]{2,1,0:T(8,128)(2,1)S(1)} %get-tuple-element.137), channel_id=1, source_target_pairs={{0,16},{4,20},{8,24},{12,28},{16,0},{20,4},{24,8},{28,12},{1,17},{... | collective-permute-start | bytes 110600 | tf_op jit(solution)/shard_map/ppermute | solution.py:564
  44.5 4.7 %collective-permute-start.17 = (bf16[1,32,256]{2,1,0:T(8,128)(2,1)S(1)}, bf16[1,32,256]{2,1,0:T(8,128)(2,1)S(1)}, u32[]{:S(2)}, u32[]{:S(2)}) collective-permute-start(bf16[1,32,256]{2,1,0:T(8,128)(2,1)S(1)} %get-tuple-element.147), channel_id=1, source_target_pairs={{0,16},{4,20},{8,24},{12,28},{16,0},{20,4},{24,8},{28,12},{1,17},{... | collective-permute-start | bytes 49160 | tf_op jit(solution)/shard_map/ppermute | solution.py:564
  49.2 5.4 %collective-permute-start.19 = (bf16[104,256]{1,0:T(8,128)(2,1)S(1)}, bf16[104,256]{1,0:T(8,128)(2,1)S(1)}, u32[]{:S(2)}, u32[]{:S(2)}) collective-permute-start(bf16[104,256]{1,0:T(8,128)(2,1)S(1)} %piece_sum.1.refs_0_), channel_id=1, source_target_pairs={{0,4},{4,0},{8,12},{12,8},{16,20},{20,16},{24,28},{28,24},{1,5},{5... | collective-permute-start | bytes 159752 | tf_op jit(solution)/shard_map/ppermute | solution.py:564
  50.8 5.1 %collective-permute-start.18 = (bf16[104,256]{1,0:T(8,128)(2,1)S(1)}, bf16[104,256]{1,0:T(8,128)(2,1)S(1)}, u32[]{:S(2)}, u32[]{:S(2)}) collective-permute-start(bf16[104,256]{1,0:T(8,128)(2,1)S(1)} %piece_sum.1.refs_0_), channel_id=1, source_target_pairs={{0,16},{4,20},{8,24},{12,28},{16,0},{20,4},{24,8},{28,12},{1,17},{... | collective-permute-start | bytes 159752 | tf_op jit(solution)/shard_map/ppermute | solution.py:564
  52.6 8.5 %collective-permute-start.21 = (bf16[104,256]{1,0:T(8,128)(2,1)S(1)}, bf16[104,256]{1,0:T(8,128)(2,1)S(1)}, u32[]{:S(2)}, u32[]{:S(2)}) collective-permute-start(bf16[104,256]{1,0:T(8,128)(2,1)S(1)} %piece_sum.1.refs_0_), channel_id=1, source_target_pairs={{0,12},{4,8},{8,4},{12,0},{16,28},{20,24},{24,20},{28,16},{1,13},{... | collective-permute-start | bytes 159752 | tf_op jit(solution)/shard_map/ppermute | solution.py:564
  54.5 6.6 %collective-permute-start.20 = (bf16[104,256]{1,0:T(8,128)(2,1)S(1)}, bf16[104,256]{1,0:T(8,128)(2,1)S(1)}, u32[]{:S(2)}, u32[]{:S(2)}) collective-permute-start(bf16[104,256]{1,0:T(8,128)(2,1)S(1)} %piece_sum.1.refs_0_), channel_id=1, source_target_pairs={{0,8},{4,12},{8,0},{12,4},{16,24},{20,28},{24,16},{28,20},{1,9},{5... | collective-permute-start | bytes 159752 | tf_op jit(solution)/shard_map/ppermute | solution.py:564
  55.9 5.2 %collective-permute-start.24 = (bf16[104,256]{1,0:T(8,128)(2,1)S(1)}, bf16[104,256]{1,0:T(8,128)(2,1)S(1)}, u32[]{:S(2)}, u32[]{:S(2)}) collective-permute-start(bf16[104,256]{1,0:T(8,128)(2,1)S(1)} %collective-permute-done.18.refs_4_), channel_id=1, source_target_pairs={{0,12},{4,8},{8,4},{12,0},{16,28},{20,24},{24,20},{28,16},{1,13},{... | collective-permute-start | bytes 159752 | tf_op jit(solution)/shard_map/ppermute | solution.py:564
  57.5 4.1 %collective-permute-start.23 = (bf16[104,256]{1,0:T(8,128)(2,1)S(1)}, bf16[104,256]{1,0:T(8,128)(2,1)S(1)}, u32[]{:S(2)}, u32[]{:S(2)}) collective-permute-start(bf16[104,256]{1,0:T(8,128)(2,1)S(1)} %collective-permute-done.18.refs_4_), channel_id=1, source_target_pairs={{0,8},{4,12},{8,0},{12,4},{16,24},{20,28},{24,16},{28,20},{1,9},{5... | collective-permute-start | bytes 159752 | tf_op jit(solution)/shard_map/ppermute | solution.py:564
  57.8 4.1 %collective-permute-start.22 = (bf16[104,256]{1,0:T(8,128)(2,1)S(1)}, bf16[104,256]{1,0:T(8,128)(2,1)S(1)}, u32[]{:S(2)}, u32[]{:S(2)}) collective-permute-start(bf16[104,256]{1,0:T(8,128)(2,1)S(1)} %collective-permute-done.18.refs_4_), channel_id=1, source_target_pairs={{0,4},{4,0},{8,12},{12,8},{16,20},{20,16},{24,28},{28,24},{1,5},{5... | collective-permute-start | bytes 159752 | tf_op jit(solution)/shard_map/ppermute | solution.py:564
  59.4 2.5 %copy-start = (f32[64,1024]{1,0:T(8,128)S(1)}, f32[64,1024]{1,0:T(8,128)}, u32[]{:S(2)}) copy-start(f32[64,1024]{1,0:T(8,128)} %refs_14_.1) | copy-start | bytes 786436
  59.4 2.6 %copy-start.1 = (f32[256,256]{1,0:T(8,128)S(1)}, f32[256,256]{1,0:T(8,128)}, u32[]{:S(2)}) copy-start(f32[256,256]{1,0:T(8,128)} %refs_17_.1) | copy-start | bytes 786436
  59.4 2.6 %copy-start.2 = (f32[64,768]{1,0:T(8,128)S(1)}, f32[64,768]{1,0:T(8,128)}, u32[]{:S(2)}) copy-start(f32[64,768]{1,0:T(8,128)} %refs_8_.1) | copy-start | bytes 589828
  59.4 2.6 %copy-start.4 = (f32[64,256]{1,0:T(8,128)S(1)}, f32[64,256]{1,0:T(8,128)}, u32[]{:S(2)}) copy-start(f32[64,256]{1,0:T(8,128)} %refs_11_.1) | copy-start | bytes 196612
  59.4 2.6 %copy-start.7 = (f32[64,1024]{1,0:T(8,128)S(1)}, f32[64,1024]{1,0:T(8,128)}, u32[]{:S(2)}) copy-start(f32[64,1024]{1,0:T(8,128)} %refs_15_.1) | copy-start | bytes 786436
  59.4 2.6 %copy-start.8 = (f32[64,1024]{1,0:T(8,128)S(1)}, f32[64,1024]{1,0:T(8,128)}, u32[]{:S(2)}) copy-start(f32[64,1024]{1,0:T(8,128)} %refs_16_.1) | copy-start | bytes 786436
  59.4 2.6 %copy-start.9 = (f32[256,256]{1,0:T(8,128)S(1)}, f32[256,256]{1,0:T(8,128)}, u32[]{:S(2)}) copy-start(f32[256,256]{1,0:T(8,128)} %refs_18_.1) | copy-start | bytes 786436
  59.5 2.6 %copy-start.10 = (f32[256,256]{1,0:T(8,128)S(1)}, f32[256,256]{1,0:T(8,128)}, u32[]{:S(2)}) copy-start(f32[256,256]{1,0:T(8,128)} %refs_19_.1) | copy-start | bytes 786436
  59.5 2.6 %copy-start.11 = (f32[64,768]{1,0:T(8,128)S(1)}, f32[64,768]{1,0:T(8,128)}, u32[]{:S(2)}) copy-start(f32[64,768]{1,0:T(8,128)} %refs_9_.1) | copy-start | bytes 589828
  59.5 2.6 %copy-start.12 = (f32[64,768]{1,0:T(8,128)S(1)}, f32[64,768]{1,0:T(8,128)}, u32[]{:S(2)}) copy-start(f32[64,768]{1,0:T(8,128)} %refs_10_.1) | copy-start | bytes 589828
  59.5 2.6 %copy-start.14 = (f32[64,256]{1,0:T(8,128)S(1)}, f32[64,256]{1,0:T(8,128)}, u32[]{:S(2)}) copy-start(f32[64,256]{1,0:T(8,128)} %refs_12_.1) | copy-start | bytes 196612
  59.5 2.6 %copy-start.15 = (f32[64,256]{1,0:T(8,128)S(1)}, f32[64,256]{1,0:T(8,128)}, u32[]{:S(2)}) copy-start(f32[64,256]{1,0:T(8,128)} %refs_13_.1) | copy-start | bytes 196612
